TPU v7x, 32 devices: a whole 2x2x4 slice. The times are simulated.
32 devices in a mesh: section: 4 (over y, core), dp: 8 (over z, x).
Axes of the slice: x: 2, y: 2, z: 4, core: 2. Of those that a mesh axis runs over, the one named last changes fastest.
Arguments:
- hidden: bfloat16 [4, 384, 8192], P('section', None, 'dp'), may hold values from -6 to 6
- norm_gain: bfloat16 [8192], P('dp'), may hold values from 0.25 to 1.75
- head: bfloat16 [8192, 8192], P(None, ('section', 'dp')), may hold values from -0.13258252 to 0.13258252
- reward_head: bfloat16 [8192], P('dp'), may hold values from -0.5 to 0.5
- tokens: int32 [4, 384], replicated, may hold values from 0 to 8191
- lengths: int32 [4], replicated, may hold values from 1 to 384, 1152 in all
Outputs:
- logprobs: float32 [4, 384], P('section')
- scores: float32 [4], P('section')
Inputs may be any that keep to these rules, and one draw needn't show every extreme that they name: `lengths`: some span has length exactly 384.
All inputs are finite; a program needn't handle non-finite values.
Results may differ from a plain program's by a relative error of at most 0.0028.
Values may be sent and summed in bfloat16 or wider, within the bound.
No kernel may reach another device: no remote copies, remote signals or barrier semaphores. Data moves between devices by JAX's collectives and lax.ppermute only.
A program may use at most 128 MiB of HBM per device.

v0:
```python
import jax
import jax.numpy as jnp
from jax import lax
from jax.sharding import PartitionSpec as P


def joined(value, axis, join):
    pieces = jax.tree.map(lambda part: lax.all_gather(part, axis), value)
    head = jax.tree.map(lambda part: part[0], pieces)
    tail = jax.tree.map(lambda part: part[1:], pieces)
    so_far, _ = lax.scan(lambda so_far, piece: (join(so_far, piece), None), head, tail)
    return so_far


def combine(first, second):
    top = jnp.maximum(first[0], second[0])
    total = first[1] * jnp.exp(first[0] - top) + second[1] * jnp.exp(second[0] - top)
    return (top, total, first[2] + second[2])


def summary(logits, vocab_ids, token_ids):
    top = jnp.max(logits, axis=-1)
    total = jnp.sum(jnp.exp(logits - top[..., None]), axis=-1)
    target = jnp.sum(
        jnp.where(vocab_ids == token_ids[..., None], logits, jnp.float32(0.0)), axis=-1
    )
    return (top, total, target)


def per_device(hidden, norm_gain, head, reward_head, tokens, lengths):
    section = lax.axis_index("section")
    dp_index = lax.axis_index("dp")
    groups = lax.axis_size("dp")
    block = head.shape[1]
    width = head.shape[0]
    widened = hidden[0].astype(jnp.float32)
    positions = widened.shape[0]
    scaled = (widened * norm_gain.astype(jnp.float32)).astype(jnp.bfloat16)
    square_part = jnp.sum(widened * widened, axis=1)
    reward_part = jnp.dot(scaled, reward_head, preferred_element_type=jnp.float32)
    square_sum, reward_sum = lax.psum((square_part, reward_part), "dp")
    inverse_rms = lax.rsqrt(square_sum / width + 1e-05)
    features_all = lax.all_gather(scaled, "dp", axis=1, tiled=True)
    own_length = lax.dynamic_slice_in_dim(lengths, section, 1, 0)[0]
    spans_all = lax.all_gather(features_all[None], "section", axis=0, tiled=True)
    scales_all = lax.all_gather(inverse_rms[None], "section", axis=0, tiled=True)
    logits = scales_all[:, :, None] * jnp.einsum(
        "ctd,dv->ctv", spans_all, head, preferred_element_type=jnp.float32
    )
    vocab_ids = (section * groups + dp_index) * block + jnp.arange(block, dtype=jnp.int32)
    stats = summary(logits, vocab_ids[None, None, :], tokens)
    merged = joined(stats, ("section", "dp"), combine)
    top = lax.dynamic_slice_in_dim(merged[0], section, 1, 0)[0]
    total = lax.dynamic_slice_in_dim(merged[1], section, 1, 0)[0]
    target = lax.dynamic_slice_in_dim(merged[2], section, 1, 0)[0]
    inside = jnp.arange(positions, dtype=jnp.int32) < own_length
    logprob = jnp.where(inside, target - (top + jnp.log(total)), jnp.float32(0.0))
    reward = inverse_rms * reward_sum
    score = jnp.sum(jnp.where(inside, reward, jnp.float32(0.0))) / own_length.astype(jnp.float32)
    return (logprob[None], score[None])


def solution(mesh):
    return jax.shard_map(
        per_device,
        mesh=mesh,
        in_specs=(P("section", None, "dp"), P("dp"), P(None, ("section", "dp")), P("dp"), P(), P()),
        out_specs=(P("section", None), P("section")),
        check_vma=False,
    )
```

profile of v0, /device:TPU:0, one launch (start us, length us, event | category | flops | bytes accessed | tf_op | source)
XLA Modules:
  0.0 491.3 jit_solution(6481459973357438872)
XLA Ops:
  7.2 0.0 all-gather.12.cloned.1.call-start
  7.2 0.7 convert_element_type.17
  7.9 2.2 fusion.4
  10.1 0.0 all-gather.12.cloned.1.call-update
  10.2 0.0 all-gather.14.cloned.1.call-start
  10.2 101.8 %all-gather.12.cloned.1.call-done = bf16[384,8192]{1,0:T(8,128)(2,1)} async-done(((bf16[384,1024]{1,0:T(8,128)(2,1)}), bf16[384,8192]{1,0:T(8,128)(2,1)}) %all-gather.12.cloned.1.call-update) | async-done | bytes 6291472 | tf_op jit(solution)/shard_map/all_gather | solution.py:43
  112.0 0.0 copy-start.3
  112.0 0.0 copy-start.2
  112.0 0.0 copy-start
  112.0 0.0 all-gather.14.cloned.1.call-update
  112.1 0.6 copy-done.3
  112.7 0.6 dynamic_slice.22
  113.9 0.0 copy-done.2
  113.9 0.0 copy-done
  113.9 0.3 convolution_reduce_fusion
  114.3 18.6 %all-reduce = (f32[384]{0:T(512)S(1)}, f32[384]{0:T(512)S(1)}) all-reduce(f32[384]{0:T(512)S(1)} %get-tuple-element.65, f32[384]{0:T(512)S(1)} %convolution_reduce_fusion), channel_id=1, replica_groups=mesh['section'=4,'dp'=8] {'dp'}, use_global_device_ids=true, to_apply=%region_1.0 | all-reduce | flops 768 | bytes 6144 | tf_op jit(solution)/shard_map/psum | solution.py:41
  132.8 1.2 select_reduce_fusion.1
  134.1 5.1 %all-gather.5 = f32[4,1,384]{2,1,0:T(1,128)S(1)} all-gather(f32[1,1,384]{2,1,0:T(1,128)S(1)} %reshape.36), channel_id=2, replica_groups=mesh['section'=4,'dp'=8] {'section'}, dimensions={0}, use_global_device_ids=true | all-gather | bytes 7680 | tf_op jit(solution)/shard_map/all_gather | solution.py:46
  139.9 126.8 %all-gather.14.cloned.1.call-done = bf16[1536,8192]{1,0:T(8,128)(2,1)} async-done(((bf16[384,8192]{1,0:T(8,128)(2,1)}), bf16[1536,8192]{1,0:T(8,128)(2,1)}) %all-gather.14.cloned.1.call-update) | async-done | bytes 25165840 | tf_op jit(solution)/shard_map/all_gather | solution.py:45
  266.7 0.0 copy-start.1
  266.7 14.1 %fusion.9 = (f32[4,384]{1,0:T(4,128)S(1)}, f32[4,384,256]{1,2,0:T(8,128)S(1)}) fusion(bf16[4,384,8192]{2,1,0:T(8,128)(2,1)} %bitcast.49, bf16[8192,256]{1,0:T(8,128)(2,1)} %param.10, f32[4,384]{1,0:T(4,128)S(1)} %bitcast.48), kind=kOutput, calls=%fused_computation.25 | convolution fusion | flops 6443235840 | bytes 30945280 | tf_op jit(solution)/shard_map/ctd,dv->ctv/dot_general | solution.py:47
  280.8 68.4 %all-gather.6 = f32[32,4,384]{2,1,0:T(4,128)S(1)} all-gather(f32[1,4,384]{2,1,0:T(4,128)S(1)} %bitcast.45), channel_id=4, replica_groups=mesh['section'=4,'dp'=8] {'section','dp'}, dimensions={0}, use_global_device_ids=true | all-gather | bytes 202752 | tf_op jit(solution)/shard_map/all_gather | solution.py:8
  349.2 0.0 copy-done.1
  349.2 0.4 select_reduce_fusion
  349.6 64.4 %all-gather.7 = f32[32,4,384]{2,1,0:T(4,128)S(1)} all-gather(f32[1,4,384]{2,1,0:T(4,128)S(1)} %bitcast.47), channel_id=5, replica_groups=mesh['section'=4,'dp'=8] {'section','dp'}, dimensions={0}, use_global_device_ids=true | all-gather | bytes 202752 | tf_op jit(solution)/shard_map/all_gather | solution.py:8
  414.0 66.6 %all-gather.8 = f32[32,4,384]{2,1,0:T(4,128)S(1)} all-gather(f32[1,4,384]{2,1,0:T(4,128)S(1)} %bitcast.46), channel_id=6, replica_groups=mesh['section'=4,'dp'=8] {'section','dp'}, dimensions={0}, use_global_device_ids=true | all-gather | bytes 202752 | tf_op jit(solution)/shard_map/all_gather | solution.py:8
  480.6 1.5 while.14
  482.2 1.2 compare_select_fusion
  (41 shorter events, 1.1 us)
Async XLA Ops:
  7.2 104.9 %all-gather.12.cloned.1.call-start = ((), (), s32[]{:S(2)}) async-start(), calls=%async_computation | async-start | bytes 7077888 | tf_op jit(solution)/shard_map/all_gather | solution.py:43
  10.2 256.5 %all-gather.14.cloned.1.call-start = ((), (), s32[]{:S(2)}) async-start(), calls=%async_computation.1 | async-start | bytes 31457280 | tf_op jit(solution)/shard_map/all_gather | solution.py:45
  112.0 0.7 copy-start.3
  112.0 1.9 copy-start.2
  112.0 1.9 copy-start
  266.7 82.5 %copy-start.1 = (s32[4,384]{1,0:T(4,128)S(1)}, s32[4,384]{1,0:T(4,128)}, u32[]{:S(2)}) copy-start(s32[4,384]{1,0:T(4,128)} %param.12) | copy-start | bytes 18436
Sparse Core Ops, SparseCore 0:
  10.3 101.7 all-gather.11
  113.6 153.0 all-gather.13
where the time goes:
time: 492 us; the launch traced here: 491 us
  waiting for transfers between devices  229 us (47%)
  blocking collectives  223 us (45%)
  between operations  16.5 us (3%)
  matrix products  14.4 us (3%)
  other arithmetic  6.76 us (1%)
    all_gather x3, blocking collectives, joined(): pieces = jax.tree.map(lambda part: lax.all_gather(part, axis), value)  199 us
    all_gather x1, waiting for transfers between devices, per_device(): lax.all_gather(features_all[None], 'section', axis=0, tiled=True)  127 us
    all_gather x1, waiting for transfers between devices, per_device(): features_all = lax.all_gather(scaled, 'dp', axis=1, tiled=True)  102 us
    psum x1, blocking collectives, per_device(): square_sum, reward_sum = lax.psum((square_part, reward_part), 'dp')  18.6 us
    dot_general x1, matrix products, per_device(): jnp.einsum('ctd,dv->ctv', spans_all, head, preferred_element_type=jnp.flo...  14.1 us
  transfers between devices with their start and end apart: 2, of which 2 were waited for; matrix products, arithmetic and copies ran while one was open for 0% of the time, Pallas kernels for 0%

commit v1 on v0

v1 whole, which is shorter than its diff:
```python
import jax
import jax.numpy as jnp
from jax import lax
from jax.sharding import PartitionSpec as P

AXES = ("section", "dp")
F32 = jnp.float32
BF16 = jnp.bfloat16


def combine(parts):
    top = parts[0][0]
    for part in parts[1:]:
        top = jnp.maximum(top, part[0])
    total = sum(part[1] * jnp.exp(part[0] - top) for part in parts)
    target = sum(part[2] for part in parts)
    return jnp.stack([top, total, target])


def summary(logits, vocab_ids, token_ids):
    top = jnp.max(logits, axis=-1)
    total = jnp.sum(jnp.exp(logits - top[:, None]), axis=-1)
    target = jnp.sum(jnp.where(vocab_ids[None, :] == token_ids[:, None], logits, F32(0.0)), axis=-1)
    return jnp.stack([top, total, target])


def row_map(lengths, section, count, half):
    pair, core = section // 2, section % 2
    first, second = lengths[2 * pair], lengths[2 * pair + 1]
    other_first = lengths[2 - 2 * pair]
    j = core * count + jnp.arange(count, dtype=jnp.int32)
    in_first = j < first
    in_second = j < first + second
    span = jnp.where(in_first, 2 * pair, jnp.where(in_second, 2 * pair + 1, 3 - 2 * pair))
    place = jnp.where(
        in_first, j, jnp.where(in_second, j - first, 2 * count - other_first + j - first - second)
    )
    return span, place


def per_device(groups, hidden, norm_gain, head, reward_head, tokens, lengths):
    section = lax.axis_index("section")
    dp_index = lax.axis_index("dp")
    core, pair = section % 2, section // 2
    sections = lax.axis_size("section")
    spans, positions = tokens.shape
    block, width, part = head.shape[1], head.shape[0], hidden.shape[2]
    count = 3 * spans * positions // 4 // sections
    half = positions // 2
    rows = hidden[0]

    swap = [(s, s ^ 1) for s in range(sections)]
    sibling = lax.ppermute(rows, "section", swap)
    extra = lax.ppermute(rows[half:], "section", [(1, 3), (3, 1)])
    head_sibling = lax.ppermute(head, "section", swap)

    span, place = row_map(lengths, section, count, half)
    own = (span == section)
    sib = (span == section + 1 - 2 * core)
    away = ~(own | sib)
    ids = jnp.arange(positions, dtype=jnp.int32)[None, :]
    pick_own = (own[:, None] & (ids == place[:, None])).astype(BF16)
    pick_sib = (sib[:, None] & (ids == place[:, None])).astype(BF16)
    pick_away = (away[:, None] & (ids[:, half:] == place[:, None])).astype(BF16)
    picked = (
        jnp.dot(pick_own, rows, preferred_element_type=F32)
        + jnp.dot(pick_sib, sibling, preferred_element_type=F32)
        + jnp.dot(pick_away, extra, preferred_element_type=F32)
    )
    mine = (picked * norm_gain.astype(F32)).astype(BF16)
    square_part = jnp.sum(picked * picked, axis=1)
    reward_part = jnp.sum(mine.astype(F32) * reward_head.astype(F32), axis=1)
    partial = jnp.stack([square_part, reward_part])
    slot = (jnp.arange(sections) == section)[:, None, None]
    sums = lax.psum(jnp.where(slot, partial[None], F32(0.0)), AXES)
    scales = lax.rsqrt(sums[:, 0] / width + 1e-05)
    rewards = scales * sums[:, 1]

    def mesh_perm(move):
        pairs = []
        for s in range(sections):
            for d in range(groups):
                s2, d2 = move(s, d)
                pairs.append((s * groups + d, s2 * groups + d2))
        return pairs

    if groups == 8:
        perm_a = mesh_perm(lambda s, d: (s, d ^ 1) if s % 2 == 0 else (s ^ 2, d))
        perm_b = mesh_perm(lambda s, d: (s ^ 2, d) if s % 2 == 0 else (s, d ^ 1))
        perm_z1 = mesh_perm(lambda s, d: (s, d ^ 2))
        perm_z3 = mesh_perm(lambda s, d: (s, d ^ 6))
        send = lambda value, perm: lax.ppermute(value, AXES, perm)
        big = (count * 7 // 9) // 16 * 16
        g, small = mine[:big], mine[big:]
        zero = core == 0

        a3 = send(small, perm_a)
        z1 = send(g, perm_z1)
        z3 = send(g, perm_z3)
        a0 = send(g, perm_a)
        b3 = send(jnp.concatenate([small, a3]), perm_b)
        b0 = send(g, perm_b)
        c0 = send(a0, perm_b)
        n3 = small.shape[0]
        wide = jnp.concatenate(
            [small, jnp.where(zero, b3[:n3], a3), jnp.where(zero, a3, b3[:n3]), b3[n3:]]
        )
        z2 = send(z3, perm_z1)
        a1 = send(z1, perm_a)
        b1 = send(z1, perm_b)
        c1 = send(a1, perm_b)
        w1 = send(wide, perm_z1)
        w3 = send(wide, perm_z3)
        a_3 = send(z3, perm_a)
        b_3 = send(z3, perm_b)
        c_3 = send(a_3, perm_b)
        a_2 = send(z2, perm_a)
        b_2 = send(z2, perm_b)
        c_2 = send(a_2, perm_b)
        w2 = send(w3, perm_z1)

        def times(value, where):
            start = where * part
            return jnp.concatenate(
                [
                    jnp.dot(value, lax.dynamic_slice_in_dim(h, start, part, 0), preferred_element_type=F32)
                    for h in (head, head_sibling)
                ],
                axis=1,
            )

        acc = [0.0, 0.0, 0.0, 0.0, 0.0, 0.0]
        order = [
            (0, g, a0, b0, c0, wide), (1, z1, a1, b1, c1, w1), (3, z3, a_3, b_3, c_3, w3), (2, z2, a_2, b_2, c_2, w2)
        ]
        for k, z_k, a_k, b_k, c_k, w_k in order:
            near = dp_index ^ (2 * k)
            far = near ^ 1
            acc[0] += times(z_k, near)
            acc[1] += times(a_k, jnp.where(zero, far, near))
            acc[2] += times(b_k, jnp.where(zero, near, far))
            acc[3] += times(c_k, far)
            acc[4] += times(w_k[: 2 * n3], near)
            acc[5] += times(w_k[2 * n3 :], far)
        low = acc[4] + acc[5]
        here = jnp.concatenate([acc[0] + jnp.where(zero, acc[1], acc[2]), low[:n3]])
        there = jnp.concatenate([acc[3] + jnp.where(zero, acc[2], acc[1]), low[n3:]])
    else:
        across = lax.ppermute(mine, "section", [(s, s ^ 2) for s in range(sections)])
        everything = lax.all_gather(jnp.concatenate([mine, across]), "dp", axis=1, tiled=True)
        both = jnp.concatenate(
            [jnp.dot(everything, h, preferred_element_type=F32) for h in (head, head_sibling)], axis=1
        )
        here, there = both[:count], both[count:]

    top_pair = pair == 0
    logits = jnp.concatenate([jnp.where(top_pair, here, there), jnp.where(top_pair, there, here)])
    flat_tokens = tokens.reshape(-1)
    all_ids = jnp.arange(spans * positions, dtype=jnp.int32)[None, :]
    token_ids, row_scales = [], []
    for p in range(2):
        s_, t_ = row_map(lengths, 2 * p + core, count, half)
        flat = s_ * positions + t_
        token_ids.append(jnp.sum(jnp.where(all_ids == flat[:, None], flat_tokens[None, :], 0), axis=1))
        row_scales.append(lax.dynamic_index_in_dim(scales, 2 * p + core, 0, keepdims=False))
    token_ids = jnp.concatenate(token_ids)
    logits = logits * jnp.concatenate(row_scales)[:, None]
    lane = jnp.arange(block, dtype=jnp.int32)
    vocab_ids = jnp.concatenate(
        [(section * groups + dp_index) * block + lane, ((section + 1 - 2 * core) * groups + dp_index) * block + lane]
    )
    stats = summary(logits, vocab_ids, token_ids)
    if groups == 8:
        stats = combine([stats] + [send(stats, mesh_perm(lambda s, d, k=k: (s, d ^ (2 * k)))) for k in (1, 2, 3)])
        stats = combine(
            [stats]
            + [send(stats, mesh_perm(lambda s, d, m=m: (s ^ m[0], d ^ m[1]))) for m in ((0, 1), (2, 0), (2, 1))]
        )
    else:
        gathered = lax.all_gather(stats, "dp")
        stats = combine([gathered[i] for i in range(groups)])
        stats = combine([stats, lax.ppermute(stats, "section", [(s, s ^ 2) for s in range(sections)])])
    logprob_list = stats[2] - (stats[0] + jnp.log(stats[1]))
    other_list = lax.ppermute(logprob_list, "section", swap)
    by_core = jnp.stack([jnp.where(core == 0, logprob_list, other_list), jnp.where(core == 0, other_list, logprob_list)])
    span_all, place_all = [], []
    for c in range(2):
        for p in range(2):
            s_, t_ = row_map(lengths, 2 * p + c, count, half)
            span_all.append(s_)
            place_all.append(t_)
    span_all, place_all = jnp.concatenate(span_all), jnp.concatenate(place_all)
    hit = (span_all == section)[None, :] & (place_all[None, :] == jnp.arange(positions, dtype=jnp.int32)[:, None])
    logprob = jnp.sum(jnp.where(hit, by_core.reshape(-1)[None, :], F32(0.0)), axis=1)
    span_sec = jnp.stack([row_map(lengths, s, count, half)[0] for s in range(sections)])
    score = jnp.sum(jnp.where(span_sec == section, rewards, F32(0.0))) / lengths[section].astype(F32)
    return (logprob[None], score[None])


def solution(mesh):
    groups = mesh.shape["dp"]
    return jax.shard_map(
        lambda *args: per_device(groups, *args),
        mesh=mesh,
        in_specs=(P("section", None, "dp"), P("dp"), P(None, ("section", "dp")), P("dp"), P(), P()),
        out_specs=(P("section", None), P("section")),
        check_vma=False,
    )
```

time: 492 us -> 219 us (0.45)
  blocking collectives: 223 us -> 41.4 us
  waiting for transfers between devices: 229 us -> 66 us
  starting transfers between devices: 0.08 us -> 31.6 us
  matrix products: 14.4 us -> 44.1 us
  other arithmetic: 6.76 us -> 15.2 us
    all_gather x2 -> x0, waiting for transfers between devices: 229 us -> none  [the longest x1 127 us: per_device(): lax.all_gather(features_all[None], 'section', axis=0, tiled=True)]
    all_gather x4 -> x0, blocking collectives: 205 us -> none  [the longest x3 199 us: joined(): pieces = jax.tree.map(lambda part: lax.all_gather(part, axis), value)]
    ppermute x0 -> x30, waiting for transfers between devices: none -> 66 us  [the longest x26 66 us: per_device(): send = lambda value, perm: lax.ppermute(value, AXES, perm)]
    ppermute x0 -> x30, starting transfers between devices: none -> 31.6 us  [the longest x26 30.2 us: per_device(): send = lambda value, perm: lax.ppermute(value, AXES, perm)]
    dot_general x2 -> x51, matrix products: 14.4 us -> 44.1 us  [the longest x48 41.3 us: times(): jnp.dot(value, lax.dynamic_slice_in_dim(h, start, part, 0), preferred_ele...]
    psum x1, blocking collectives: 18.6 us -> 41.4 us  [per_device(): sums = lax.psum(jnp.where(slot, partial[None], F32(0.0)), AXES)]
    select_n x1 -> x11, other arithmetic: 1.2 us -> 7.14 us  [the longest x4 4.97 us: row_map(): jnp.where(in_first, j, jnp.where(in_second, j - first, 2 * count - other_...]
  transfers between devices with their start and end apart: 2 -> 30, of which waited for: 2 -> 14; matrix products, arithmetic and copies ran while one was open for 0% -> 14% of each run, Pallas kernels for 0% -> 0%
where the time goes in v1:
time: 219 us; the launch traced here: 217 us
  waiting for transfers between devices  66 us (30%)
  matrix products  44.1 us (20%)
  blocking collectives  41.4 us (19%)
  starting transfers between devices  31.6 us (14%)
  other arithmetic  15.2 us (7%)
  between operations  13.6 us (6%)
  local copies, waits for them, and re-layouts  4.64 us (2%)
    ppermute x26, waiting for transfers between devices, per_device(): send = lambda value, perm: lax.ppermute(value, AXES, perm)  66 us
    psum x1, blocking collectives, per_device(): sums = lax.psum(jnp.where(slot, partial[None], F32(0.0)), AXES)  41.4 us
    dot_general x48, matrix products, times(): jnp.dot(value, lax.dynamic_slice_in_dim(h, start, part, 0), preferred_ele...  41.3 us
    ppermute x26, starting transfers between devices, per_device(): send = lambda value, perm: lax.ppermute(value, AXES, perm)  30.2 us
    select_n x4, other arithmetic, row_map(): jnp.where(in_first, j, jnp.where(in_second, j - first, 2 * count - other_...  4.97 us
  transfers between devices with their start and end apart: 30, of which 14 were waited for; matrix products, arithmetic and copies ran while one was open for 14% of the time, Pallas kernels for 0%

profile of v1, /device:TPU:0, one launch (start us, length us, event | category | flops | bytes accessed | tf_op | source)
XLA Modules:
  0.0 216.6 jit_solution(4771803869656182779)
XLA Ops:
  3.2 1.9 fusion.217
  23.6 2.5 %fusion.195 = (s32[288]{0:T(512)S(1)}, s32[288]{0:T(512)S(1)}) fusion(s32[]{:T(128)} %bitcast.5, s32[]{:T(128)} %bitcast.6, s32[]{:T(128)S(6)} %sub.254, s32[]{:T(128)S(6)} %add.507, s32[]{:T(128)S(6)} %add.509, s32[]{:T(128)S(6)} %mul.194, s32[]{:T(128)} %bitcast.4, s32[]{:T(128)S(6)} %mul.193, s32[]{:T(128)} %bitcast.8, s32[]{:T(128)} %bitcast.9, ...), kind=kLoop, calls=%fused_computation.267 | loop fusion | flops 7488 | bytes 2368 | tf_op jit(solution)/shard_map/add | solution.py:163
  26.8 1.7 fusion.112
  29.7 3.0 %collective-permute-start.6 = (bf16[224,1024]{1,0:T(8,128)(2,1)S(1)}, bf16[224,1024]{1,0:T(8,128)(2,1)S(1)}, u32[]{:S(2)}, u32[]{:S(2)}) collective-permute-start(bf16[224,1024]{1,0:T(8,128)(2,1)S(1)} %slice.183), channel_id=1, source_target_pairs={{0,1},{1,0},{2,3},{3,2},{4,5},{5,4},{6,7},{7,6},{8,24},{9,25},{10,... | collective-permute-start | bytes 1376264 | tf_op jit(solution)/shard_map/ppermute | solution.py:92
  32.7 1.6 collective-permute-start.3
  34.3 2.5 %collective-permute-start.4 = (bf16[224,1024]{1,0:T(8,128)(2,1)S(1)}, bf16[224,1024]{1,0:T(8,128)(2,1)S(1)}, u32[]{:S(2)}, u32[]{:S(2)}) collective-permute-start(bf16[224,1024]{1,0:T(8,128)(2,1)S(1)} %slice.183), channel_id=1, source_target_pairs={{0,6},{1,7},{2,4},{3,5},{4,2},{5,3},{6,0},{7,1},{8,14},{9,15},{10,... | collective-permute-start | bytes 1376264 | tf_op jit(solution)/shard_map/ppermute | solution.py:92
  37.4 41.4 %psum.7 = f32[4,2,288]{2,0,1:T(4,128)S(1)} all-reduce(f32[4,2,288]{2,0,1:T(4,128)S(1)} %broadcast_select_fusion.2), channel_id=1, replica_groups=mesh['section'=4,'dp'=8] {'section','dp'}, use_global_device_ids=true, to_apply=%region_4.5 | all-reduce | flops 2304 | bytes 18432 | tf_op jit(solution)/shard_map/psum | solution.py:75
  78.9 2.5 %collective-permute-start.15 = (bf16[128,1024]{1,0:T(8,128)(2,1)S(1)}, bf16[128,1024]{1,0:T(8,128)(2,1)S(1)}, u32[]{:S(2)}, u32[]{:S(2)}) collective-permute-start(bf16[128,1024]{1,0:T(8,128)(2,1)S(1)} %pad_maximum_fusion.3), channel_id=1, source_target_pairs={{0,16},{1,17},{2,18},{3,19},{4,20},{5,21},{6,22},{7,23},{8,9},{9,8... | collective-permute-start | bytes 786440 | tf_op jit(solution)/shard_map/ppermute | solution.py:92
  81.5 1.3 fusion.98
  82.8 2.9 %collective-permute-done.15 = bf16[128,1024]{1,0:T(8,128)(2,1)S(1)} collective-permute-done((bf16[128,1024]{1,0:T(8,128)(2,1)S(1)}, bf16[128,1024]{1,0:T(8,128)(2,1)S(1)}, u32[]{:S(2)}, u32[]{:S(2)}) %collective-permute-start.15) | collective-permute-done | bytes 262176 | tf_op jit(solution)/shard_map/ppermute | solution.py:92
  85.8 2.0 collective-permute-start.10
  87.8 1.3 fusion.96
  90.9 1.6 collective-permute-start.17
  94.6 7.4 %collective-permute-done.19 = bf16[224,1024]{1,0:T(8,128)(2,1)S(1)} collective-permute-done((bf16[224,1024]{1,0:T(8,128)(2,1)S(1)}, bf16[224,1024]{1,0:T(8,128)(2,1)S(1)}, u32[]{:S(2)}, u32[]{:S(2)}) %collective-permute-start.19) | collective-permute-done | bytes 458784 | tf_op jit(solution)/shard_map/ppermute | solution.py:92
  101.9 2.6 %collective-permute-start.8 = (bf16[224,1024]{1,0:T(8,128)(2,1)S(1)}, bf16[224,1024]{1,0:T(8,128)(2,1)S(1)}, u32[]{:S(2)}, u32[]{:S(2)}) collective-permute-start(bf16[224,1024]{1,0:T(8,128)(2,1)S(1)} %collective-permute-done.4), channel_id=1, source_target_pairs={{0,1},{1,0},{2,3},{3,2},{4,5},{5,4},{6,7},{7,6},{8,24},{9,25},{10,... | collective-permute-start | bytes 1376264 | tf_op jit(solution)/shard_map/ppermute | solution.py:92
  104.8 18.4 %collective-permute-done.5 = bf16[224,1024]{1,0:T(8,128)(2,1)S(1)} collective-permute-done((bf16[224,1024]{1,0:T(8,128)(2,1)S(1)}, bf16[224,1024]{1,0:T(8,128)(2,1)S(1)}, u32[]{:S(2)}, u32[]{:S(2)}) %collective-permute-start.5) | collective-permute-done | bytes 458784 | tf_op jit(solution)/shard_map/ppermute | solution.py:92
  123.8 1.9 collective-permute-start.12
  126.3 10.4 %collective-permute-done.7 = bf16[224,1024]{1,0:T(8,128)(2,1)S(1)} collective-permute-done((bf16[224,1024]{1,0:T(8,128)(2,1)S(1)}, bf16[224,1024]{1,0:T(8,128)(2,1)S(1)}, u32[]{:S(2)}, u32[]{:S(2)}) %collective-permute-start.7) | collective-permute-done | bytes 458784 | tf_op jit(solution)/shard_map/ppermute | solution.py:92
  138.3 1.7 collective-permute-start.21
  141.5 9.1 %collective-permute-done.20 = bf16[224,1024]{1,0:T(8,128)(2,1)S(1)} collective-permute-done((bf16[224,1024]{1,0:T(8,128)(2,1)S(1)}, bf16[224,1024]{1,0:T(8,128)(2,1)S(1)}, u32[]{:S(2)}, u32[]{:S(2)}) %collective-permute-start.20) | collective-permute-done | bytes 458784 | tf_op jit(solution)/shard_map/ppermute | solution.py:92
  151.4 4.1 %collective-permute-done.21 = bf16[224,1024]{1,0:T(8,128)(2,1)S(1)} collective-permute-done((bf16[224,1024]{1,0:T(8,128)(2,1)S(1)}, bf16[224,1024]{1,0:T(8,128)(2,1)S(1)}, u32[]{:S(2)}, u32[]{:S(2)}) %collective-permute-start.21) | collective-permute-done | bytes 458784 | tf_op jit(solution)/shard_map/ppermute | solution.py:92
  157.0 3.4 %collective-permute-done.13 = bf16[224,1024]{1,0:T(8,128)(2,1)S(1)} collective-permute-done((bf16[224,1024]{1,0:T(8,128)(2,1)S(1)}, bf16[224,1024]{1,0:T(8,128)(2,1)S(1)}, u32[]{:S(2)}, u32[]{:S(2)}) %collective-permute-start.13) | collective-permute-done | bytes 458784 | tf_op jit(solution)/shard_map/ppermute | solution.py:92
  161.2 4.1 %collective-permute-done.22 = bf16[224,1024]{1,0:T(8,128)(2,1)S(1)} collective-permute-done((bf16[224,1024]{1,0:T(8,128)(2,1)S(1)}, bf16[224,1024]{1,0:T(8,128)(2,1)S(1)}, u32[]{:S(2)}, u32[]{:S(2)}) %collective-permute-start.22) | collective-permute-done | bytes 458784 | tf_op jit(solution)/shard_map/ppermute | solution.py:92
  165.6 1.3 fusion.92
  166.9 1.3 fusion.84
  168.2 1.3 fusion.76
  172.1 1.3 fusion.54
  176.1 1.3 fusion.94
  177.4 1.3 fusion.86
  178.8 1.3 fusion.78
  180.1 1.3 fusion.70
  181.5 1.3 fusion.18
  182.8 1.3 fusion.22
  184.1 1.3 fusion.26
  185.5 1.3 fusion.30
  186.8 1.3 fusion.2
  188.2 1.3 fusion.6
  189.5 1.3 fusion.10
  190.8 1.3 fusion.14
  192.6 1.3 fusion.60
  193.9 1.3 fusion.52
  195.3 1.3 fusion.44
  196.6 1.3 fusion.36
  199.9 1.5 collective-permute-start.25
  201.4 1.4 collective-permute-start.24
  206.1 1.5 collective-permute-start.28
  207.6 1.7 collective-permute-start.27
  211.3 1.7 collective-permute-done.26
  (127 shorter events, 39.7 us)
Async XLA Ops:
  0.6 165.0 %collective-permute-start.2 = (bf16[8192,256]{1,0:T(8,128)(2,1)}, bf16[8192,256]{1,0:T(8,128)(2,1)}, u32[]{:S(2)}, u32[]{:S(2)}) collective-permute-start(bf16[8192,256]{1,0:T(8,128)(2,1)} %param.8), channel_id=1, source_target_pairs={{0,8},{8,0},{16,24},{24,16},{1,9},{9,1},{17,25},{25,17},{2,10},{10... | collective-permute-start | bytes 12582920 | tf_op jit(solution)/shard_map/ppermute | solution.py:55
  1.1 27.4 %collective-permute-start = (bf16[384,1024]{1,0:T(8,128)(2,1)}, bf16[384,1024]{1,0:T(8,128)(2,1)S(1)}, u32[]{:S(2)}, u32[]{:S(2)}) collective-permute-start(bf16[384,1024]{1,0:T(8,128)(2,1)} %bitcast.59), channel_id=1, source_target_pairs={{0,8},{8,0},{16,24},{24,16},{1,9},{9,1},{17,25},{25,17},{2,10},{10... | collective-permute-start | bytes 2359304 | tf_op jit(solution)/shard_map/ppermute | solution.py:53
  2.3 26.8 %collective-permute-start.1 = (bf16[192,1024]{1,0:T(8,128)(2,1)S(1)}, bf16[192,1024]{1,0:T(8,128)(2,1)S(1)}, u32[]{:S(2)}, u32[]{:S(2)}) collective-permute-start(bf16[192,1024]{1,0:T(8,128)(2,1)S(1)} %slice_bitcast_fusion), channel_id=1, source_target_pairs={{8,24},{24,8},{9,25},{25,9},{10,26},{26,10},{11,27},{27,11},{12,28... | collective-permute-start | bytes 1179656 | tf_op jit(solution)/shard_map/ppermute | solution.py:54
  29.7 61.1 %collective-permute-start.6 = (bf16[224,1024]{1,0:T(8,128)(2,1)S(1)}, bf16[224,1024]{1,0:T(8,128)(2,1)S(1)}, u32[]{:S(2)}, u32[]{:S(2)}) collective-permute-start(bf16[224,1024]{1,0:T(8,128)(2,1)S(1)} %slice.183), channel_id=1, source_target_pairs={{0,1},{1,0},{2,3},{3,2},{4,5},{5,4},{6,7},{7,6},{8,24},{9,25},{10,... | collective-permute-start | bytes 1376264 | tf_op jit(solution)/shard_map/ppermute | solution.py:92
  32.7 57.7 %collective-permute-start.3 = (bf16[224,1024]{1,0:T(8,128)(2,1)S(1)}, bf16[224,1024]{1,0:T(8,128)(2,1)S(1)}, u32[]{:S(2)}, u32[]{:S(2)}) collective-permute-start(bf16[224,1024]{1,0:T(8,128)(2,1)S(1)} %slice.183), channel_id=1, source_target_pairs={{0,2},{1,3},{2,0},{3,1},{4,6},{5,7},{6,4},{7,5},{8,10},{9,11},{10,... | collective-permute-start | bytes 1376264 | tf_op jit(solution)/shard_map/ppermute | solution.py:92
  34.3 58.4 %collective-permute-start.4 = (bf16[224,1024]{1,0:T(8,128)(2,1)S(1)}, bf16[224,1024]{1,0:T(8,128)(2,1)S(1)}, u32[]{:S(2)}, u32[]{:S(2)}) collective-permute-start(bf16[224,1024]{1,0:T(8,128)(2,1)S(1)} %slice.183), channel_id=1, source_target_pairs={{0,6},{1,7},{2,4},{3,5},{4,2},{5,3},{6,0},{7,1},{8,14},{9,15},{10,... | collective-permute-start | bytes 1376264 | tf_op jit(solution)/shard_map/ppermute | solution.py:92
  36.8 42.1 %collective-permute-start.14 = (bf16[64,1024]{1,0:T(8,128)(2,1)S(1)}, bf16[64,1024]{1,0:T(8,128)(2,1)S(1)}, u32[]{:S(2)}, u32[]{:S(2)}) collective-permute-start(bf16[64,1024]{1,0:T(8,128)(2,1)S(1)} %slice.184), channel_id=1, source_target_pairs={{0,1},{1,0},{2,3},{3,2},{4,5},{5,4},{6,7},{7,6},{8,24},{9,25},{10,... | collective-permute-start | bytes 393224 | tf_op jit(solution)/shard_map/ppermute | solution.py:92
  78.8 11.7 %copy-start = (bf16[8192,256]{1,0:T(8,128)(2,1)S(1)}, bf16[8192,256]{1,0:T(8,128)(2,1)}, u32[]{:S(2)}) copy-start(bf16[8192,256]{1,0:T(8,128)(2,1)} %param.8) | copy-start | bytes 12582916
  78.9 6.8 %collective-permute-start.15 = (bf16[128,1024]{1,0:T(8,128)(2,1)S(1)}, bf16[128,1024]{1,0:T(8,128)(2,1)S(1)}, u32[]{:S(2)}, u32[]{:S(2)}) collective-permute-start(bf16[128,1024]{1,0:T(8,128)(2,1)S(1)} %pad_maximum_fusion.3), channel_id=1, source_target_pairs={{0,16},{1,17},{2,18},{3,19},{4,20},{5,21},{6,22},{7,23},{8,9},{9,8... | collective-permute-start | bytes 786440 | tf_op jit(solution)/shard_map/ppermute | solution.py:92
  85.8 8.5 %collective-permute-start.10 = (bf16[224,1024]{1,0:T(8,128)(2,1)S(1)}, bf16[224,1024]{1,0:T(8,128)(2,1)S(1)}, u32[]{:S(2)}, u32[]{:S(2)}) collective-permute-start(bf16[224,1024]{1,0:T(8,128)(2,1)S(1)} %slice.183), channel_id=1, source_target_pairs={{0,16},{1,17},{2,18},{3,19},{4,20},{5,21},{6,22},{7,23},{8,9},{9,8... | collective-permute-start | bytes 1376264 | tf_op jit(solution)/shard_map/ppermute | solution.py:92
  90.5 47.1 %collective-permute-start.16 = (bf16[256,1024]{1,0:T(8,128)(2,1)S(1)}, bf16[256,1024]{1,0:T(8,128)(2,1)S(1)}, u32[]{:S(2)}, u32[]{:S(2)}) collective-permute-start(bf16[256,1024]{1,0:T(8,128)(2,1)S(1)} %pad_maximum_fusion.2), channel_id=1, source_target_pairs={{0,2},{1,3},{2,0},{3,1},{4,6},{5,7},{6,4},{7,5},{8,10},{9,11},{10,... | collective-permute-start | bytes 1572872 | tf_op jit(solution)/shard_map/ppermute | solution.py:92
  90.9 35.2 %collective-permute-start.17 = (bf16[256,1024]{1,0:T(8,128)(2,1)S(1)}, bf16[256,1024]{1,0:T(8,128)(2,1)S(1)}, u32[]{:S(2)}, u32[]{:S(2)}) collective-permute-start(bf16[256,1024]{1,0:T(8,128)(2,1)S(1)} %pad_maximum_fusion.2), channel_id=1, source_target_pairs={{0,6},{1,7},{2,4},{3,5},{4,2},{5,3},{6,0},{7,1},{8,14},{9,15},{10,... | collective-permute-start | bytes 1572872 | tf_op jit(solution)/shard_map/ppermute | solution.py:92
  92.7 9.2 %collective-permute-start.19 = (bf16[224,1024]{1,0:T(8,128)(2,1)S(1)}, bf16[224,1024]{1,0:T(8,128)(2,1)S(1)}, u32[]{:S(2)}, u32[]{:S(2)}) collective-permute-start(bf16[224,1024]{1,0:T(8,128)(2,1)S(1)} %collective-permute-done.6), channel_id=1, source_target_pairs={{0,16},{1,17},{2,18},{3,19},{4,20},{5,21},{6,22},{7,23},{8,9},{9,8... | collective-permute-start | bytes 1376264 | tf_op jit(solution)/shard_map/ppermute | solution.py:92
  94.3 29.0 %collective-permute-start.5 = (bf16[224,1024]{1,0:T(8,128)(2,1)S(1)}, bf16[224,1024]{1,0:T(8,128)(2,1)S(1)}, u32[]{:S(2)}, u32[]{:S(2)}) collective-permute-start(bf16[224,1024]{1,0:T(8,128)(2,1)S(1)} %collective-permute-done.4), channel_id=1, source_target_pairs={{0,2},{1,3},{2,0},{3,1},{4,6},{5,7},{6,4},{7,5},{8,10},{9,11},{10,... | collective-permute-start | bytes 1376264 | tf_op jit(solution)/shard_map/ppermute | solution.py:92
  101.9 21.9 %collective-permute-start.8 = (bf16[224,1024]{1,0:T(8,128)(2,1)S(1)}, bf16[224,1024]{1,0:T(8,128)(2,1)S(1)}, u32[]{:S(2)}, u32[]{:S(2)}) collective-permute-start(bf16[224,1024]{1,0:T(8,128)(2,1)S(1)} %collective-permute-done.4), channel_id=1, source_target_pairs={{0,1},{1,0},{2,3},{3,2},{4,5},{5,4},{6,7},{7,6},{8,24},{9,25},{10,... | collective-permute-start | bytes 1376264 | tf_op jit(solution)/shard_map/ppermute | solution.py:92
  123.2 13.5 %collective-permute-start.7 = (bf16[224,1024]{1,0:T(8,128)(2,1)S(1)}, bf16[224,1024]{1,0:T(8,128)(2,1)S(1)}, u32[]{:S(2)}, u32[]{:S(2)}) collective-permute-start(bf16[224,1024]{1,0:T(8,128)(2,1)S(1)} %collective-permute-done.3), channel_id=1, source_target_pairs={{0,1},{1,0},{2,3},{3,2},{4,5},{5,4},{6,7},{7,6},{8,24},{9,25},{10,... | collective-permute-start | bytes 1376264 | tf_op jit(solution)/shard_map/ppermute | solution.py:92
  123.8 14.5 %collective-permute-start.12 = (bf16[224,1024]{1,0:T(8,128)(2,1)S(1)}, bf16[224,1024]{1,0:T(8,128)(2,1)S(1)}, u32[]{:S(2)}, u32[]{:S(2)}) collective-permute-start(bf16[224,1024]{1,0:T(8,128)(2,1)S(1)} %collective-permute-done.4), channel_id=1, source_target_pairs={{0,16},{1,17},{2,18},{3,19},{4,20},{5,21},{6,22},{7,23},{8,9},{9,8... | collective-permute-start | bytes 1376264 | tf_op jit(solution)/shard_map/ppermute | solution.py:92
  126.0 14.3 %collective-permute-start.11 = (bf16[224,1024]{1,0:T(8,128)(2,1)S(1)}, bf16[224,1024]{1,0:T(8,128)(2,1)S(1)}, u32[]{:S(2)}, u32[]{:S(2)}) collective-permute-start(bf16[224,1024]{1,0:T(8,128)(2,1)S(1)} %collective-permute-done.3), channel_id=1, source_target_pairs={{0,16},{1,17},{2,18},{3,19},{4,20},{5,21},{6,22},{7,23},{8,9},{9,8... | collective-permute-start | bytes 1376264 | tf_op jit(solution)/shard_map/ppermute | solution.py:92
  136.7 24.0 %collective-permute-start.18 = (bf16[256,1024]{1,0:T(8,128)(2,1)S(1)}, bf16[256,1024]{1,0:T(8,128)(2,1)S(1)}, u32[]{:S(2)}, u32[]{:S(2)}) collective-permute-start(bf16[256,1024]{1,0:T(8,128)(2,1)S(1)} %collective-permute-done.17), channel_id=1, source_target_pairs={{0,2},{1,3},{2,0},{3,1},{4,6},{5,7},{6,4},{7,5},{8,10},{9,11},{10,... | collective-permute-start | bytes 1572872 | tf_op jit(solution)/shard_map/ppermute | solution.py:92
  137.6 13.0 %collective-permute-start.20 = (bf16[224,1024]{1,0:T(8,128)(2,1)S(1)}, bf16[224,1024]{1,0:T(8,128)(2,1)S(1)}, u32[]{:S(2)}, u32[]{:S(2)}) collective-permute-start(bf16[224,1024]{1,0:T(8,128)(2,1)S(1)} %collective-permute-done.7), channel_id=1, source_target_pairs={{0,16},{1,17},{2,18},{3,19},{4,20},{5,21},{6,22},{7,23},{8,9},{9,8... | collective-permute-start | bytes 1376264 | tf_op jit(solution)/shard_map/ppermute | solution.py:92
  138.3 17.2 %collective-permute-start.21 = (bf16[224,1024]{1,0:T(8,128)(2,1)S(1)}, bf16[224,1024]{1,0:T(8,128)(2,1)S(1)}, u32[]{:S(2)}, u32[]{:S(2)}) collective-permute-start(bf16[224,1024]{1,0:T(8,128)(2,1)S(1)} %collective-permute-done.8), channel_id=1, source_target_pairs={{0,16},{1,17},{2,18},{3,19},{4,20},{5,21},{6,22},{7,23},{8,9},{9,8... | collective-permute-start | bytes 1376264 | tf_op jit(solution)/shard_map/ppermute | solution.py:92
  140.3 15.5 %collective-permute-start.9 = (bf16[224,1024]{1,0:T(8,128)(2,1)S(1)}, bf16[224,1024]{1,0:T(8,128)(2,1)S(1)}, u32[]{:S(2)}, u32[]{:S(2)}) collective-permute-start(bf16[224,1024]{1,0:T(8,128)(2,1)S(1)} %collective-permute-done.5), channel_id=1, source_target_pairs={{0,1},{1,0},{2,3},{3,2},{4,5},{5,4},{6,7},{7,6},{8,24},{9,25},{10,... | collective-permute-start | bytes 1376264 | tf_op jit(solution)/shard_map/ppermute | solution.py:92
  150.6 9.8 %collective-permute-start.13 = (bf16[224,1024]{1,0:T(8,128)(2,1)S(1)}, bf16[224,1024]{1,0:T(8,128)(2,1)S(1)}, u32[]{:S(2)}, u32[]{:S(2)}) collective-permute-start(bf16[224,1024]{1,0:T(8,128)(2,1)S(1)} %collective-permute-done.5), channel_id=1, source_target_pairs={{0,16},{1,17},{2,18},{3,19},{4,20},{5,21},{6,22},{7,23},{8,9},{9,8... | collective-permute-start | bytes 1376264 | tf_op jit(solution)/shard_map/ppermute | solution.py:92
  155.8 9.5 %collective-permute-start.22 = (bf16[224,1024]{1,0:T(8,128)(2,1)S(1)}, bf16[224,1024]{1,0:T(8,128)(2,1)S(1)}, u32[]{:S(2)}, u32[]{:S(2)}) collective-permute-start(bf16[224,1024]{1,0:T(8,128)(2,1)S(1)} %collective-permute-done.9), channel_id=1, source_target_pairs={{0,16},{1,17},{2,18},{3,19},{4,20},{5,21},{6,22},{7,23},{8,9},{9,8... | collective-permute-start | bytes 1376264 | tf_op jit(solution)/shard_map/ppermute | solution.py:92
  199.2 4.9 %collective-permute-start.23 = (f32[3,576]{1,0:T(4,128)S(1)}, f32[3,576]{1,0:T(4,128)S(1)}, u32[]{:S(2)}, u32[]{:S(2)}) collective-permute-start(f32[3,576]{1,0:T(4,128)S(1)} %pad_maximum_fusion.10), channel_id=1, source_target_pairs={{0,2},{1,3},{2,0},{3,1},{4,6},{5,7},{6,4},{7,5},{8,10},{9,11},{10,... | collective-permute-start | bytes 20744 | tf_op jit(solution)/shard_map/ppermute | solution.py:92
  199.9 5.5 %collective-permute-start.25 = (f32[3,576]{1,0:T(4,128)S(1)}, f32[3,576]{1,0:T(4,128)S(1)}, u32[]{:S(2)}, u32[]{:S(2)}) collective-permute-start(f32[3,576]{1,0:T(4,128)S(1)} %pad_maximum_fusion.10), channel_id=1, source_target_pairs={{0,6},{1,7},{2,4},{3,5},{4,2},{5,3},{6,0},{7,1},{8,14},{9,15},{10,... | collective-permute-start | bytes 20744 | tf_op jit(solution)/shard_map/ppermute | solution.py:92
  201.4 4.6 %collective-permute-start.24 = (f32[3,576]{1,0:T(4,128)S(1)}, f32[3,576]{1,0:T(4,128)S(1)}, u32[]{:S(2)}, u32[]{:S(2)}) collective-permute-start(f32[3,576]{1,0:T(4,128)S(1)} %pad_maximum_fusion.10), channel_id=1, source_target_pairs={{0,4},{1,5},{2,6},{3,7},{4,0},{5,1},{6,2},{7,3},{8,12},{9,13},{10,... | collective-permute-start | bytes 20744 | tf_op jit(solution)/shard_map/ppermute | solution.py:92
  206.1 4.6 %collective-permute-start.28 = (f32[3,576]{1,0:T(4,128)S(1)}, f32[3,576]{1,0:T(4,128)S(1)}, u32[]{:S(2)}, u32[]{:S(2)}) collective-permute-start(f32[3,576]{1,0:T(4,128)S(1)} %pad_maximum_fusion.11), channel_id=1, source_target_pairs={{0,17},{1,16},{2,19},{3,18},{4,21},{5,20},{6,23},{7,22},{8,25},{9,... | collective-permute-start | bytes 20744 | tf_op jit(solution)/shard_map/ppermute | solution.py:92
  207.6 3.7 %collective-permute-start.27 = (f32[3,576]{1,0:T(4,128)S(1)}, f32[3,576]{1,0:T(4,128)S(1)}, u32[]{:S(2)}, u32[]{:S(2)}) collective-permute-start(f32[3,576]{1,0:T(4,128)S(1)} %pad_maximum_fusion.11), channel_id=1, source_target_pairs={{0,16},{1,17},{2,18},{3,19},{4,20},{5,21},{6,22},{7,23},{8,24},{9,... | collective-permute-start | bytes 20744 | tf_op jit(solution)/shard_map/ppermute | solution.py:92
  209.2 3.7 %collective-permute-start.26 = (f32[3,576]{1,0:T(4,128)S(1)}, f32[3,576]{1,0:T(4,128)S(1)}, u32[]{:S(2)}, u32[]{:S(2)}) collective-permute-start(f32[3,576]{1,0:T(4,128)S(1)} %pad_maximum_fusion.11), channel_id=1, source_target_pairs={{0,1},{1,0},{2,3},{3,2},{4,5},{5,4},{6,7},{7,6},{8,9},{9,8},{10,11... | collective-permute-start | bytes 20744 | tf_op jit(solution)/shard_map/ppermute | solution.py:92
  213.0 1.4 collective-permute-start.29

commit v2 on v0

v2 whole, which is shorter than its diff:
```python
import functools

import jax
import jax.numpy as jnp
from jax import lax
from jax.experimental import pallas as pl
from jax.experimental.pallas import tpu as pltpu
from jax.sharding import PartitionSpec as P

AXES = ("section", "dp")
F32 = jnp.float32
BF16 = jnp.bfloat16
I32 = jnp.int32
LANES = 128
VMEM = pl.BlockSpec(memory_space=pltpu.VMEM)
SMEM = pl.BlockSpec(memory_space=pltpu.SMEM)


def row_map(lengths, pair, core, index, count):
    first, second = lengths[2 * pair], lengths[2 * pair + 1]
    other_first = lengths[2 - 2 * pair]
    j = core * count + index
    in_first = j < first
    in_second = j < first + second
    span = jnp.where(in_first, 2 * pair, jnp.where(in_second, 2 * pair + 1, 3 - 2 * pair))
    place = jnp.where(
        in_first, j, jnp.where(in_second, j - first, 2 * count - other_first + j - first - second)
    )
    return span, place


def as_rows(columns, count):
    lane = lax.broadcasted_iota(I32, (count, LANES), 1)
    wide = jnp.zeros((count, LANES), F32)
    for i, column in enumerate(columns):
        wide = jnp.where(lane == i, column, wide)
    return jnp.transpose(wide)[:8]


def as_column(rows, which):
    full = jnp.concatenate([rows, jnp.zeros((LANES - 8, rows.shape[1]), F32)], axis=0)
    return jnp.transpose(full)[:, which : which + 1]


def pick_kernel(count, lengths, rows, sibling, extra, gain, reward, big, small, partial):
    section = lax.axis_index("section")
    core, pair = lax.rem(section, 2), lax.div(section, 2)
    positions, half = rows.shape[0], extra.shape[0]
    index = lax.broadcasted_iota(I32, (count, 1), 0)
    span, place = row_map(lengths, pair, core, index, count)
    source = jnp.where(span == section, place, place + positions)
    source = jnp.where(span // 2 == pair, source, place + (2 * positions - (positions - half)))
    lane = lax.broadcasted_iota(I32, (count, 2 * positions + half), 1)
    pick = jnp.where(lane == source, F32(1.0), F32(0.0)).astype(BF16)
    picked = jnp.dot(pick[:, :positions], rows[...], preferred_element_type=F32)
    picked += jnp.dot(pick[:, positions : 2 * positions], sibling[...], preferred_element_type=F32)
    picked += jnp.dot(pick[:, 2 * positions :], extra[...], preferred_element_type=F32)
    scaled = (picked * gain[...].astype(F32)).astype(BF16)
    n = big.shape[0]
    big[...] = scaled[:n]
    small[...] = scaled[n:]
    squares = jnp.sum(picked * picked, axis=1, keepdims=True)
    rewards = jnp.sum(scaled.astype(F32) * reward[...].astype(F32), axis=1, keepdims=True)
    padded = partial.shape[1]
    zeros = jnp.zeros((padded - count, 1), F32)
    partial[...] = as_rows(
        [jnp.concatenate([squares, zeros]), jnp.concatenate([rewards, zeros])], padded
    )


def token_kernel(count, n, lengths, tokens, out):
    core = lax.rem(lax.axis_index("section"), 2)
    spans, positions = tokens.shape
    for pair in range(2):
        index = lax.broadcasted_iota(I32, (count, 1), 0)
        span, place = row_map(lengths, pair, core, index, count)
        lane = lax.broadcasted_iota(I32, (count, positions), 1)
        ids = jnp.zeros((count, 1), F32)
        for s in range(spans):
            hit = (lane == place) & (span == s)
            ids += jnp.sum(jnp.where(hit, tokens[s : s + 1, :].astype(F32), F32(0.0)), axis=1, keepdims=True)
        ids = ids.astype(I32)
        m = count - n
        out[pair * n : pair * n + n, :] = ids[:n]
        out[2 * n + pair * m : 2 * n + pair * m + m, :] = ids[n:]


def offsets(k, n, m):
    section, dp_index = lax.axis_index("section"), lax.axis_index("dp")
    core, pair = lax.rem(section, 2), lax.div(section, 2)
    near = jnp.bitwise_xor(dp_index, 2 * k)
    far = jnp.bitwise_xor(near, 1)
    mine = pl.ds(pl.multiple_of(pair * n, n), n)
    others = pl.ds(pl.multiple_of((1 - pair) * n, n), n)
    small_mine = pl.ds(pl.multiple_of(2 * n + pair * m, 16), m)
    small_others = pl.ds(pl.multiple_of(2 * n + (1 - pair) * m, 16), m)
    return core, near, far, mine, others, small_mine, small_others


def add(acc, rows, value, first):
    for i, part in enumerate(value):
        w = part.shape[1]
        if first:
            acc[rows, i * w : (i + 1) * w] = part
        else:
            acc[rows, i * w : (i + 1) * w] = acc[rows, i * w : (i + 1) * w] + part


def mm_kernel(k, first, parts, *refs):
    refs = list(refs)
    head, sibling = refs.pop(0), refs.pop(0)
    acc_in = None if first else refs.pop(0)
    acc = refs.pop()
    named = dict(zip(parts, refs))
    depth = refs[0].shape[1]
    m = 64 if "w" not in named else named["w"].shape[0] // 4
    n = acc.shape[0] // 2 - m
    core, near, far, mine, others, small_mine, small_others = offsets(k, n, m)

    def times(value, where):
        rows = pl.ds(pl.multiple_of(where * depth, depth), depth)
        return [jnp.dot(value, h[rows, :], preferred_element_type=F32) for h in (head, sibling)]

    def plus(x, y):
        return [i + j for i, j in zip(x, y)]

    if not first:
        acc[...] = acc_in[...]
    if "a" in named:

        @pl.when(core == 0)
        def _():
            add(acc, mine, plus(times(named["z"][...], near), times(named["a"][...], far)), first)
            value = times(named["b"][...], near)
            if "c" in named:
                value = plus(value, times(named["c"][...], far))
            add(acc, others, value, first)

        @pl.when(core == 1)
        def _():
            add(acc, mine, plus(times(named["z"][...], near), times(named["b"][...], far)), first)
            value = times(named["a"][...], near)
            if "c" in named:
                value = plus(value, times(named["c"][...], far))
            add(acc, others, value, first)

    if "w" in named:
        w = named["w"]
        value = plus(times(w[: 2 * m, :], near), times(w[2 * m :, :], far))
        add(acc, small_mine, [v[:m] for v in value], first)
        add(acc, small_others, [v[m:] for v in value], first)


def summarize(logits, squares, token_ids, bases, block, width, out):
    scale = lax.rsqrt(squares / width + 1e-05)
    logits = logits * scale
    top = jnp.max(logits, axis=1, keepdims=True)
    total = jnp.sum(jnp.exp(logits - top), axis=1, keepdims=True)
    lane = lax.broadcasted_iota(I32, (1, block), 1)
    target = jnp.zeros(top.shape, F32)
    for i, base in enumerate(bases):
        hit = (lane + base) == token_ids
        target += jnp.sum(
            jnp.where(hit, logits[:, i * block : (i + 1) * block], F32(0.0)), axis=1, keepdims=True
        )
    count, padded = logits.shape[0], out.shape[1]
    zeros = jnp.zeros((padded - count, 1), F32)
    out[...] = as_rows([jnp.concatenate([v, zeros]) for v in (top, total, target)], padded)


def last_kernel(k, n, width, head, sibling, acc_in, c, sums, token_ids, out, acc):
    count = acc_in.shape[0] // 2
    m = count - n
    block = head.shape[1]
    section, dp_index = lax.axis_index("section"), lax.axis_index("dp")
    groups = lax.axis_size("dp")
    bases = [(section * groups + dp_index) * block, ((section + 1 - 2 * lax.rem(section, 2)) * groups + dp_index) * block]
    acc[...] = acc_in[...]
    if c is not None:
        _, near, far, mine, others, _, _ = offsets(k, n, m)
        depth = c.shape[1]
        rows = pl.ds(pl.multiple_of(far * depth, depth), depth)
        for i, h in enumerate((head, sibling)):
            cols = slice(i * block, (i + 1) * block)
            acc[others, cols] = acc[others, cols] + jnp.dot(c[...], h[rows, :], preferred_element_type=F32)
    squares = [as_column(sums[p], 0) for p in range(2)]
    column = jnp.concatenate([squares[0][:n], squares[1][:n], squares[0][n:count], squares[1][n:count]])
    summarize(acc[...], column, token_ids[...], bases, block, width, out)


def final_kernel(count, n, width, lengths, sums, stats, out_ref, score_ref):
    section = lax.axis_index("section")
    m = count - n
    positions = out_ref.shape[1]
    where = lax.broadcasted_iota(I32, (1, positions), 1)
    logprob = jnp.zeros((1, positions), F32)
    score = jnp.zeros((1, 1), F32)
    index = lax.broadcasted_iota(I32, (count, 1), 0)
    for core in range(2):
        s = stats[core]
        lp = as_column(s, 0)
        for pair in range(2):
            value = jnp.concatenate([lp[pair * n : pair * n + n], lp[2 * n + pair * m : 2 * n + pair * m + m]])
            span, place = row_map(lengths, pair, core, index, count)
            hit = (place == where) & (span == section)
            logprob += jnp.sum(jnp.where(hit, value, F32(0.0)), axis=0, keepdims=True)
            columns = jnp.transpose(
                jnp.concatenate([sums[core, pair], jnp.zeros((LANES - 8, sums.shape[3]), F32)], axis=0)
            )[:count]
            reward = columns[:, 1:2] * lax.rsqrt(columns[:, 0:1] / width + 1e-05)
            score += jnp.sum(jnp.where(span == section, reward, F32(0.0)), axis=0, keepdims=True)
    out_ref[...] = logprob
    score_ref[...] = score / lengths[section].astype(F32)


def combine(parts):
    top = parts[0][0]
    for part in parts[1:]:
        top = jnp.maximum(top, part[0])
    total = sum(part[1] * jnp.exp(part[0] - top) for part in parts)
    target = sum(part[2] for part in parts)
    return jnp.concatenate([jnp.stack([top, total, target]), jnp.zeros((5,) + top.shape, F32)])


def call(body, outs, in_specs, args, flops=0, moved=0, alias=None, limit=32):
    many = isinstance(outs, (list, tuple))
    return pl.pallas_call(
        body,
        out_shape=outs,
        in_specs=in_specs,
        out_specs=[VMEM] * len(outs) if many else VMEM,
        input_output_aliases=alias or {},
        compiler_params=pltpu.CompilerParams(vmem_limit_bytes=limit << 20),
        cost_estimate=pl.CostEstimate(flops=flops, bytes_accessed=moved, transcendentals=0),
    )(*args)


def up(value):
    return -(-value // LANES) * LANES


def per_device(groups, hidden, norm_gain, head, reward_head, tokens, lengths):
    section = lax.axis_index("section")
    core, pair = section % 2, section // 2
    sections = lax.axis_size("section")
    spans, positions = tokens.shape
    block, width, part = head.shape[1], head.shape[0], hidden.shape[2]
    count = 3 * spans * positions // 4 // sections
    half = positions // 2
    big = (count * 7 // 9) // 16 * 16
    small = count - big
    rows = hidden[0]

    swap = [(s, s ^ 1) for s in range(sections)]
    over = [(s, s ^ 2) for s in range(sections)]
    sibling = lax.ppermute(rows, "section", swap)
    extra = lax.ppermute(rows[half:], "section", [(1, 3), (3, 1)])
    head_sibling = lax.ppermute(head, "section", swap)

    g, s0, partial = call(
        functools.partial(pick_kernel, count),
        [
            jax.ShapeDtypeStruct((big, part), BF16),
            jax.ShapeDtypeStruct((small, part), BF16),
            jax.ShapeDtypeStruct((8, up(count)), F32),
        ],
        [SMEM] + [VMEM] * 5,
        (lengths, rows, sibling, extra, norm_gain[None], reward_head[None]),
        flops=2 * count * 960 * part,
    )
    token_ids = call(
        functools.partial(token_kernel, count, big),
        jax.ShapeDtypeStruct((2 * count, 1), I32),
        [SMEM, VMEM],
        (lengths, tokens),
        flops=10**6,
    )

    def mesh_perm(move):
        pairs = []
        for s in range(sections):
            for d in range(groups):
                s2, d2 = move(s, d)
                pairs.append((s * groups + d, s2 * groups + d2))
        return pairs

    send = lambda value, perm: lax.ppermute(value, AXES, perm)
    acc_shape = jax.ShapeDtypeStruct((2 * count, 2 * block), F32)
    if groups == 8:
        perm_a = mesh_perm(lambda s, d: (s, d ^ 1) if s % 2 == 0 else (s ^ 2, d))
        perm_b = mesh_perm(lambda s, d: (s ^ 2, d) if s % 2 == 0 else (s, d ^ 1))
        perm_x = mesh_perm(lambda s, d: (s, d ^ 1))
        perm_z = {k: mesh_perm(lambda s, d, k=k: (s, d ^ (2 * k))) for k in (1, 2, 3)}
        zero = core == 0

        z = {0: g}
        a, b, c, w = {}, {}, {}, {}
        z[3] = send(g, perm_z[3])
        a3 = send(s0, perm_a)
        z[1] = send(g, perm_z[1])
        a[0] = send(g, perm_a)
        b3 = send(jnp.concatenate([s0, a3]), perm_b)
        b[0] = send(g, perm_b)
        c[0] = send(a[0], perm_b)
        w[0] = jnp.concatenate(
            [s0, jnp.where(zero, b3[:small], a3), jnp.where(zero, a3, b3[:small]), b3[small:]]
        )
        z[2] = send(z[3], perm_z[1])
        w[3] = send(w[0], perm_z[3])
        w[1] = send(w[0], perm_z[1])
        w[2] = send(w[3], perm_z[1])
        for k in (1, 3, 2):
            a[k] = send(z[k], perm_a)
            b[k] = send(z[k], perm_b)
            c[k] = send(a[k], perm_b)

        for perm in (perm_z[1], perm_z[2], perm_x):
            partial = partial + send(partial, perm)
        acc = None
        for k, parts in ((0, "zabcw"), (1, "zabcw"), (3, "zabcw"), (2, "zabw")):
            pieces = {"z": z, "a": a, "b": b, "c": c, "w": w}
            values = [pieces[p][k] for p in parts]
            first = acc is None
            acc = call(
                functools.partial(mm_kernel, k, first, parts),
                acc_shape,
                [VMEM] * (2 + (not first) + len(values)),
                (head, head_sibling) + (() if first else (acc,)) + tuple(values),
                flops=2 * 4 * count * part * 2 * block,
                alias={} if first else {2: 0},
            )
        last_c = c[2]
    else:
        partial = lax.psum(partial, "dp")
        mine = jnp.concatenate([g, s0])
        across = lax.ppermute(mine, "section", over)
        first_pair = jnp.where(pair == 0, mine, across)
        second_pair = jnp.where(pair == 0, across, mine)
        ordered = jnp.concatenate([first_pair[:big], second_pair[:big], first_pair[big:], second_pair[big:]])
        everything = lax.all_gather(ordered, "dp", axis=1, tiled=True)
        acc = jnp.concatenate(
            [jnp.dot(everything, h, preferred_element_type=F32) for h in (head, head_sibling)], axis=1
        )
        last_c = None

    other = lax.ppermute(partial, "section", over)
    sums = jnp.stack([jnp.where(pair == 0, partial, other), jnp.where(pair == 0, other, partial)])
    stats_shape = jax.ShapeDtypeStruct((8, up(2 * count)), F32)
    if last_c is not None:
        stats, _ = call(
            functools.partial(last_kernel, 2, big, width),
            [stats_shape, acc_shape],
            [VMEM] * 6,
            (head, head_sibling, acc, last_c, sums, token_ids),
            flops=2 * count * part * 2 * block,
            alias={2: 1},
        )
        stats = combine([stats] + [send(stats, perm_z[k]) for k in (1, 2, 3)])
        stats = combine(
            [stats]
            + [send(stats, mesh_perm(lambda s, d, v=v: (s ^ v[0], d ^ v[1]))) for v in ((0, 1), (2, 0), (2, 1))]
        )
    else:
        def body(head, sibling, acc_in, sums, token_ids, out, acc):
            last_kernel(2, big, width, head, sibling, acc_in, None, sums, token_ids, out, acc)

        stats, _ = call(
            body, [stats_shape, acc_shape], [VMEM] * 5, (head, head_sibling, acc, sums, token_ids), alias={2: 1}
        )
        gathered = lax.all_gather(stats, "dp")
        stats = combine([gathered[i] for i in range(groups)])
        stats = combine([stats, lax.ppermute(stats, "section", over)])
    lp = stats[2:3] - (stats[0:1] + jnp.log(stats[1:2]))
    lp = jnp.concatenate([lp, jnp.zeros((7, lp.shape[1]), F32)])
    both = lambda v, u: jnp.stack([jnp.where(core == 0, v, u), jnp.where(core == 0, u, v)])
    sums = both(sums, lax.ppermute(sums, "section", swap))
    stats = both(lp, lax.ppermute(lp, "section", swap))
    logprob, score = call(
        functools.partial(final_kernel, count, big, width),
        [jax.ShapeDtypeStruct((1, positions), F32), jax.ShapeDtypeStruct((1, 1), F32)],
        [SMEM, VMEM, VMEM],
        (lengths, sums, stats),
    )
    return (logprob, score[0])


def solution(mesh):
    groups = mesh.shape["dp"]
    return jax.shard_map(
        lambda *args: per_device(groups, *args),
        mesh=mesh,
        in_specs=(P("section", None, "dp"), P("dp"), P(None, ("section", "dp")), P("dp"), P(), P()),
        out_specs=(P("section", None), P("section")),
        check_vma=False,
    )
```

time: 492 us -> 148 us (0.30)
  blocking collectives: 223 us -> 0 us
  waiting for transfers between devices: 229 us -> 55.1 us
  starting transfers between devices: 0.08 us -> 56.4 us
  Pallas kernels: 0 us -> 25.2 us
  between operations: 16.5 us -> 0.84 us
  matrix products: 14.4 us -> 0 us
  local copies, waits for them, and re-layouts: 1.3 us -> 9.88 us
  other arithmetic: 6.76 us -> 0.29 us
    all_gather x2 -> x0, waiting for transfers between devices: 229 us -> none  [the longest x1 127 us: per_device(): lax.all_gather(features_all[None], 'section', axis=0, tiled=True)]
    all_gather x4 -> x0, blocking collectives: 205 us -> none  [the longest x3 199 us: joined(): pieces = jax.tree.map(lambda part: lax.all_gather(part, axis), value)]
    ppermute x0 -> x35, starting transfers between devices: none -> 56.4 us  [the longest x29 53.2 us: per_device(): send = lambda value, perm: lax.ppermute(value, AXES, perm)]
    ppermute x0 -> x35, waiting for transfers between devices: none -> 55.1 us  [the longest x29 47.6 us: per_device(): send = lambda value, perm: lax.ppermute(value, AXES, perm)]
    pallas_call x0 -> x8, Pallas kernels: none -> 25.2 us  [call(): pl.pallas_call(body, out_shape=outs, in_specs=in_specs, out_specs=[VMEM]...]
    psum x1 -> x0, blocking collectives: 18.6 us -> none  [per_device(): square_sum, reward_sum = lax.psum((square_part, reward_part), 'dp')]
    dot_general x2 -> x0, matrix products: 14.4 us -> none  [the longest x1 14.1 us: per_device(): jnp.einsum('ctd,dv->ctv', spans_all, head, preferred_element_type=jnp.flo...]
    unnamed x11 -> x24, local copies, waits for them, and re-layouts: 0.64 us -> 7.4 us
  transfers between devices with their start and end apart: 2 -> 35, of which waited for: 2 -> 17; matrix products, arithmetic and copies ran while one was open for 0% -> 2% of each run, Pallas kernels for 0% -> 13%
where the time goes in v2:
time: 148 us
  starting transfers between devices  56.4 us (38%)
  waiting for transfers between devices  55.1 us (37%)
  Pallas kernels  25.2 us (17%)
  local copies, waits for them, and re-layouts  9.88 us (7%)
    ppermute x29, starting transfers between devices, per_device(): send = lambda value, perm: lax.ppermute(value, AXES, perm)  53.2 us
    ppermute x29, waiting for transfers between devices, per_device(): send = lambda value, perm: lax.ppermute(value, AXES, perm)  47.6 us
    pallas_call x8, Pallas kernels, call(): pl.pallas_call(body, out_shape=outs, in_specs=in_specs, out_specs=[VMEM]...  25.2 us
    unnamed x24, local copies, waits for them, and re-layouts  7.4 us
    ppermute x1, waiting for transfers between devices, per_device(): sibling = lax.ppermute(rows, 'section', swap)  4.52 us
  transfers between devices with their start and end apart: 35, of which 17 were waited for; matrix products, arithmetic and copies ran while one was open for 2% of the time, Pallas kernels for 13%

profile of v2, /device:TPU:0, one launch (start us, length us, event | category | flops | bytes accessed | tf_op | source)
XLA Modules:
  0.0 147.7 jit_solution(12101571445349977533)
XLA Ops:
  4.3 4.5 %collective-permute-done.sibling = bf16[384,1024]{1,0:T(8,128)(2,1)S(1)} collective-permute-done((bf16[384,1024]{1,0:T(8,128)(2,1)}, bf16[384,1024]{1,0:T(8,128)(2,1)S(1)}, u32[]{:S(2)}, u32[]{:S(2)}) %collective-permute-start) | collective-permute-done | bytes 786464 | tf_op jit(solution)/shard_map/ppermute | solution.py:256
  10.6 1.9 %shard_map.77 = (bf16[224,1024]{1,0:T(8,128)(2,1)S(1)}, bf16[64,1024]{1,0:T(8,128)(2,1)S(1)}, f32[8,384]{1,0:T(8,128)S(1)}) custom-call(s32[4]{0:T(128)S(1)} %copy-done.10, bf16[384,1024]{1,0:T(8,128)(2,1)S(1)} %bitcast.17, bf16[384,1024]{1,0:T(8,128)(2,1)S(1)} %collective-permute-done.sibling, bf16[192,1024]{1,0:T(8,128)(2,1)S(1)} %collective-permute-done.1.extra, ...), custom_call_target="tpu_custom_call" | custom-call | flops 566231040 | tf_op jit(solution)/shard_map/pallas_call | solution.py:227
  12.6 2.9 %collective-permute-start.11 = (bf16[64,1024]{1,0:T(8,128)(2,1)S(1)}, bf16[64,1024]{1,0:T(8,128)(2,1)S(1)}, u32[]{:S(2)}, u32[]{:S(2)}) collective-permute-start(bf16[64,1024]{1,0:T(8,128)(2,1)S(1)} %get-tuple-element.10), channel_id=1, source_target_pairs={{0,1},{1,0},{2,3},{3,2},{4,5},{5,4},{6,7},{7,6},{8,24},{9,25},{10,... | collective-permute-start | bytes 393224 | tf_op jit(solution)/shard_map/ppermute | solution.py:287
  15.6 2.8 %collective-permute-done.11 = bf16[64,1024]{1,0:T(8,128)(2,1)S(1)} collective-permute-done((bf16[64,1024]{1,0:T(8,128)(2,1)S(1)}, bf16[64,1024]{1,0:T(8,128)(2,1)S(1)}, u32[]{:S(2)}, u32[]{:S(2)}) %collective-permute-start.11) | collective-permute-done | bytes 131104 | tf_op jit(solution)/shard_map/ppermute | solution.py:287
  18.5 2.1 %collective-permute-start.12 = (bf16[128,1024]{1,0:T(8,128)(2,1)S(1)}, bf16[128,1024]{1,0:T(8,128)(2,1)S(1)}, u32[]{:S(2)}, u32[]{:S(2)}) collective-permute-start(bf16[128,1024]{1,0:T(8,128)(2,1)S(1)} %pad_maximum_fusion.1), channel_id=1, source_target_pairs={{0,16},{1,17},{2,18},{3,19},{4,20},{5,21},{6,22},{7,23},{8,9},{9,8... | collective-permute-start | bytes 786440 | tf_op jit(solution)/shard_map/ppermute | solution.py:287
  20.7 2.0 %collective-permute-start.2 = (f32[8,384]{1,0:T(8,128)S(1)}, f32[8,384]{1,0:T(8,128)S(1)}, u32[]{:S(2)}, u32[]{:S(2)}) collective-permute-start(f32[8,384]{1,0:T(8,128)S(1)} %get-tuple-element.8), channel_id=1, source_target_pairs={{0,2},{1,3},{2,0},{3,1},{4,6},{5,7},{6,4},{7,5},{8,10},{9,11},{10,... | collective-permute-start | bytes 36872 | tf_op jit(solution)/shard_map/ppermute | solution.py:287
  22.7 1.7 %collective-permute-done.2 = f32[8,384]{1,0:T(8,128)S(1)} collective-permute-done((f32[8,384]{1,0:T(8,128)S(1)}, f32[8,384]{1,0:T(8,128)S(1)}, u32[]{:S(2)}, u32[]{:S(2)}) %collective-permute-start.2) | collective-permute-done | bytes 12320 | tf_op jit(solution)/shard_map/ppermute | solution.py:287
  24.4 3.0 %collective-permute-start.3 = (f32[8,384]{1,0:T(8,128)S(1)}, f32[8,384]{1,0:T(8,128)S(1)}, u32[]{:S(2)}, u32[]{:S(2)}) collective-permute-start(f32[8,384]{1,0:T(8,128)S(1)} %add.76), channel_id=1, source_target_pairs={{0,4},{1,5},{2,6},{3,7},{4,0},{5,1},{6,2},{7,3},{8,12},{9,13},{10,... | collective-permute-start | bytes 36872 | tf_op jit(solution)/shard_map/ppermute | solution.py:287
  27.4 1.7 %collective-permute-done.3 = f32[8,384]{1,0:T(8,128)S(1)} collective-permute-done((f32[8,384]{1,0:T(8,128)S(1)}, f32[8,384]{1,0:T(8,128)S(1)}, u32[]{:S(2)}, u32[]{:S(2)}) %collective-permute-start.3) | collective-permute-done | bytes 12320 | tf_op jit(solution)/shard_map/ppermute | solution.py:287
  29.1 1.8 %collective-permute-start.4 = (f32[8,384]{1,0:T(8,128)S(1)}, f32[8,384]{1,0:T(8,128)S(1)}, u32[]{:S(2)}, u32[]{:S(2)}) collective-permute-start(f32[8,384]{1,0:T(8,128)S(1)} %add.77), channel_id=1, source_target_pairs={{0,1},{1,0},{2,3},{3,2},{4,5},{5,4},{6,7},{7,6},{8,9},{9,8},{10,11... | collective-permute-start | bytes 36872 | tf_op jit(solution)/shard_map/ppermute | solution.py:287
  30.9 1.9 %collective-permute-done.4 = f32[8,384]{1,0:T(8,128)S(1)} collective-permute-done((f32[8,384]{1,0:T(8,128)S(1)}, f32[8,384]{1,0:T(8,128)S(1)}, u32[]{:S(2)}, u32[]{:S(2)}) %collective-permute-start.4) | collective-permute-done | bytes 12320 | tf_op jit(solution)/shard_map/ppermute | solution.py:287
  32.8 1.8 %collective-permute-start.5 = (f32[8,384]{1,0:T(8,128)S(1)}, f32[8,384]{1,0:T(8,128)S(1)}, u32[]{:S(2)}, u32[]{:S(2)}) collective-permute-start(f32[8,384]{1,0:T(8,128)S(1)} %add.78), channel_id=1, source_target_pairs={{0,16},{8,24},{16,0},{24,8},{1,17},{9,25},{17,1},{25,9},{2,18},{10... | collective-permute-start | bytes 36872 | tf_op jit(solution)/shard_map/ppermute | solution.py:346
  34.6 1.9 %collective-permute-done.5 = f32[8,384]{1,0:T(8,128)S(1)} collective-permute-done((f32[8,384]{1,0:T(8,128)S(1)}, f32[8,384]{1,0:T(8,128)S(1)}, u32[]{:S(2)}, u32[]{:S(2)}) %collective-permute-start.5) | collective-permute-done | bytes 12320 | tf_op jit(solution)/shard_map/ppermute | solution.py:346
  36.5 1.9 %collective-permute-start.13 = (bf16[224,1024]{1,0:T(8,128)(2,1)S(1)}, bf16[224,1024]{1,0:T(8,128)(2,1)S(1)}, u32[]{:S(2)}, u32[]{:S(2)}) collective-permute-start(bf16[224,1024]{1,0:T(8,128)(2,1)S(1)} %get-tuple-element.9.refs_2_), channel_id=1, source_target_pairs={{0,2},{1,3},{2,0},{3,1},{4,6},{5,7},{6,4},{7,5},{8,10},{9,11},{10,... | collective-permute-start | bytes 1376264 | tf_op jit(solution)/shard_map/ppermute | solution.py:287
  38.4 2.5 %collective-permute-start.18 = (bf16[224,1024]{1,0:T(8,128)(2,1)S(1)}, bf16[224,1024]{1,0:T(8,128)(2,1)S(1)}, u32[]{:S(2)}, u32[]{:S(2)}) collective-permute-start(bf16[224,1024]{1,0:T(8,128)(2,1)S(1)} %get-tuple-element.9.refs_2_), channel_id=1, source_target_pairs={{0,6},{1,7},{2,4},{3,5},{4,2},{5,3},{6,0},{7,1},{8,14},{9,15},{10,... | collective-permute-start | bytes 1376264 | tf_op jit(solution)/shard_map/ppermute | solution.py:287
  40.9 1.5 %collective-permute-start.10 = (bf16[224,1024]{1,0:T(8,128)(2,1)S(1)}, bf16[224,1024]{1,0:T(8,128)(2,1)S(1)}, u32[]{:S(2)}, u32[]{:S(2)}) collective-permute-start(bf16[224,1024]{1,0:T(8,128)(2,1)S(1)} %collective-permute-done.8.refs_3_), channel_id=1, source_target_pairs={{0,16},{1,17},{2,18},{3,19},{4,20},{5,21},{6,22},{7,23},{8,9},{9,8... | collective-permute-start | bytes 1376264 | tf_op jit(solution)/shard_map/ppermute | solution.py:287
  43.2 14.1 %collective-permute-done.13.refs_3_ = bf16[224,1024]{1,0:T(8,128)(2,1)S(1)} collective-permute-done((bf16[224,1024]{1,0:T(8,128)(2,1)S(1)}, bf16[224,1024]{1,0:T(8,128)(2,1)S(1)}, u32[]{:S(2)}, u32[]{:S(2)}) %collective-permute-start.13) | collective-permute-done | bytes 458784 | tf_op jit(solution)/shard_map/ppermute | solution.py:287
  57.3 2.2 %collective-permute-start.14 = (bf16[224,1024]{1,0:T(8,128)(2,1)S(1)}, bf16[224,1024]{1,0:T(8,128)(2,1)}, u32[]{:S(2)}, u32[]{:S(2)}) collective-permute-start(bf16[224,1024]{1,0:T(8,128)(2,1)S(1)} %collective-permute-done.13.refs_3_), channel_id=1, source_target_pairs={{0,1},{1,0},{2,3},{3,2},{4,5},{5,4},{6,7},{7,6},{8,24},{9,25},{10,... | collective-permute-start | bytes 1376264 | tf_op jit(solution)/shard_map/ppermute | solution.py:287
  59.5 2.7 %collective-permute-done.18.refs_3_ = bf16[224,1024]{1,0:T(8,128)(2,1)S(1)} collective-permute-done((bf16[224,1024]{1,0:T(8,128)(2,1)S(1)}, bf16[224,1024]{1,0:T(8,128)(2,1)S(1)}, u32[]{:S(2)}, u32[]{:S(2)}) %collective-permute-start.18) | collective-permute-done | bytes 458784 | tf_op jit(solution)/shard_map/ppermute | solution.py:287
  62.2 1.5 %collective-permute-start.15 = (bf16[224,1024]{1,0:T(8,128)(2,1)S(1)}, bf16[224,1024]{1,0:T(8,128)(2,1)S(1)}, u32[]{:S(2)}, u32[]{:S(2)}) collective-permute-start(bf16[224,1024]{1,0:T(8,128)(2,1)S(1)} %collective-permute-done.13.refs_3_), channel_id=1, source_target_pairs={{0,16},{1,17},{2,18},{3,19},{4,20},{5,21},{6,22},{7,23},{8,9},{9,8... | collective-permute-start | bytes 1376264 | tf_op jit(solution)/shard_map/ppermute | solution.py:287
  65.3 5.7 %collective-permute-done.17.refs_7_ = bf16[256,1024]{1,0:T(8,128)(2,1)S(1)} collective-permute-done((bf16[256,1024]{1,0:T(8,128)(2,1)S(1)}, bf16[256,1024]{1,0:T(8,128)(2,1)S(1)}, u32[]{:S(2)}, u32[]{:S(2)}) %collective-permute-start.17) | collective-permute-done | bytes 524320 | tf_op jit(solution)/shard_map/ppermute | solution.py:287
  71.0 3.9 %collective-permute-start.22 = (bf16[256,1024]{1,0:T(8,128)(2,1)S(1)}, bf16[256,1024]{1,0:T(8,128)(2,1)S(1)}, u32[]{:S(2)}, u32[]{:S(2)}) collective-permute-start(bf16[256,1024]{1,0:T(8,128)(2,1)S(1)} %pad_maximum_fusion.refs_6_), channel_id=1, source_target_pairs={{0,6},{1,7},{2,4},{3,5},{4,2},{5,3},{6,0},{7,1},{8,14},{9,15},{10,... | collective-permute-start | bytes 1572872 | tf_op jit(solution)/shard_map/ppermute | solution.py:287
  74.9 1.5 %collective-permute-start.19 = (bf16[224,1024]{1,0:T(8,128)(2,1)S(1)}, bf16[224,1024]{1,0:T(8,128)(2,1)}, u32[]{:S(2)}, u32[]{:S(2)}) collective-permute-start(bf16[224,1024]{1,0:T(8,128)(2,1)S(1)} %collective-permute-done.18.refs_3_), channel_id=1, source_target_pairs={{0,1},{1,0},{2,3},{3,2},{4,5},{5,4},{6,7},{7,6},{8,24},{9,25},{10,... | collective-permute-start | bytes 1376264 | tf_op jit(solution)/shard_map/ppermute | solution.py:287
  77.3 1.5 %collective-permute-start.16 = (bf16[224,1024]{1,0:T(8,128)(2,1)}, bf16[224,1024]{1,0:T(8,128)(2,1)}, u32[]{:S(2)}, u32[]{:S(2)}) collective-permute-start(bf16[224,1024]{1,0:T(8,128)(2,1)} %collective-permute-done.14.refs_4_), channel_id=1, source_target_pairs={{0,16},{1,17},{2,18},{3,19},{4,20},{5,21},{6,22},{7,23},{8,9},{9,8... | collective-permute-start | bytes 1376264 | tf_op jit(solution)/shard_map/ppermute | solution.py:287
  78.8 1.5 %collective-permute-done.23.refs_3_ = bf16[224,1024]{1,0:T(8,128)(2,1)} collective-permute-done((bf16[224,1024]{1,0:T(8,128)(2,1)S(1)}, bf16[224,1024]{1,0:T(8,128)(2,1)}, u32[]{:S(2)}, u32[]{:S(2)}) %collective-permute-start.23) | collective-permute-done | bytes 458784 | tf_op jit(solution)/shard_map/ppermute | solution.py:287
  80.3 1.5 %collective-permute-start.24 = (bf16[224,1024]{1,0:T(8,128)(2,1)}, bf16[224,1024]{1,0:T(8,128)(2,1)}, u32[]{:S(2)}, u32[]{:S(2)}) collective-permute-start(bf16[224,1024]{1,0:T(8,128)(2,1)} %collective-permute-done.23.refs_3_), channel_id=1, source_target_pairs={{0,1},{1,0},{2,3},{3,2},{4,5},{5,4},{6,7},{7,6},{8,24},{9,25},{10,... | collective-permute-start | bytes 1376264 | tf_op jit(solution)/shard_map/ppermute | solution.py:287
  81.8 1.3 shard_map.82.token_ids
  83.1 8.2 %collective-permute-done.22.refs_7_ = bf16[256,1024]{1,0:T(8,128)(2,1)S(1)} collective-permute-done((bf16[256,1024]{1,0:T(8,128)(2,1)S(1)}, bf16[256,1024]{1,0:T(8,128)(2,1)S(1)}, u32[]{:S(2)}, u32[]{:S(2)}) %collective-permute-start.22) | collective-permute-done | bytes 524320 | tf_op jit(solution)/shard_map/ppermute | solution.py:287
  91.3 1.5 %collective-permute-start.20 = (bf16[224,1024]{1,0:T(8,128)(2,1)S(1)}, bf16[224,1024]{1,0:T(8,128)(2,1)S(1)}, u32[]{:S(2)}, u32[]{:S(2)}) collective-permute-start(bf16[224,1024]{1,0:T(8,128)(2,1)S(1)} %collective-permute-done.18.refs_3_), channel_id=1, source_target_pairs={{0,16},{1,17},{2,18},{3,19},{4,20},{5,21},{6,22},{7,23},{8,9},{9,8... | collective-permute-start | bytes 1376264 | tf_op jit(solution)/shard_map/ppermute | solution.py:287
  93.3 1.5 %collective-permute-start.21 = (bf16[224,1024]{1,0:T(8,128)(2,1)}, bf16[224,1024]{1,0:T(8,128)(2,1)S(1)}, u32[]{:S(2)}, u32[]{:S(2)}) collective-permute-start(bf16[224,1024]{1,0:T(8,128)(2,1)} %collective-permute-done.19.refs_4_), channel_id=1, source_target_pairs={{0,16},{1,17},{2,18},{3,19},{4,20},{5,21},{6,22},{7,23},{8,9},{9,8... | collective-permute-start | bytes 1376264 | tf_op jit(solution)/shard_map/ppermute | solution.py:287
  94.8 2.1 %collective-permute-start.26 = (bf16[256,1024]{1,0:T(8,128)(2,1)S(1)}, bf16[256,1024]{1,0:T(8,128)(2,1)S(1)}, u32[]{:S(2)}, u32[]{:S(2)}) collective-permute-start(bf16[256,1024]{1,0:T(8,128)(2,1)S(1)} %collective-permute-done.22.refs_7_), channel_id=1, source_target_pairs={{0,2},{1,3},{2,0},{3,1},{4,6},{5,7},{6,4},{7,5},{8,10},{9,11},{10,... | collective-permute-start | bytes 1572872 | tf_op jit(solution)/shard_map/ppermute | solution.py:287
  96.9 1.3 collective-permute-start.27
  98.3 2.2 %copy-done = bf16[8192,256]{1,0:T(8,128)(2,1)S(1)} copy-done((bf16[8192,256]{1,0:T(8,128)(2,1)S(1)}, bf16[8192,256]{1,0:T(8,128)(2,1)}, u32[]{:S(2)}) %copy-start) | copy-done | bytes 4194328
  101.5 3.9 %shard_map.78.refs_2_ = f32[576,512]{1,0:T(8,128)S(1)} custom-call(bf16[8192,256]{1,0:T(8,128)(2,1)S(1)} %copy-done, bf16[8192,256]{1,0:T(8,128)(2,1)} %collective-permute-done.7.refs_1_.sibling, bf16[224,1024]{1,0:T(8,128)(2,1)S(1)} %get-tuple-element.9.refs_2_, bf16[224,1024]{1,0:T(8,128)(2,1)S(1)} %collective-permute-done.8.refs_3_, ...), custom_call_target="tpu_custom_call" | custom-call | flops 1207959552 | tf_op jit(solution)/shard_map/pallas_call | solution.py:227
  105.4 4.1 %shard_map.79.refs_2_ = f32[576,512]{1,0:T(8,128)S(1)} custom-call(bf16[8192,256]{1,0:T(8,128)(2,1)S(1)} %copy-done.1, bf16[8192,256]{1,0:T(8,128)(2,1)} %collective-permute-done.7.refs_1_.sibling, f32[576,512]{1,0:T(8,128)S(1)} %shard_map.78.refs_2_, bf16[224,1024]{1,0:T(8,128)(2,1)S(1)} %copy-done.3, ...), custom_call_target="tpu_custom_call", output_to_operand_aliasing={{}: (2, {})} | custom-call | flops 1207959552 | tf_op jit(solution)/shard_map/pallas_call | solution.py:227
  109.6 4.0 %shard_map.80.refs_2_ = f32[576,512]{1,0:T(8,128)S(1)} custom-call(bf16[8192,256]{1,0:T(8,128)(2,1)S(1)} %copy-done.1, bf16[8192,256]{1,0:T(8,128)(2,1)} %collective-permute-done.7.refs_1_.sibling, f32[576,512]{1,0:T(8,128)S(1)} %shard_map.79.refs_2_, bf16[224,1024]{1,0:T(8,128)(2,1)S(1)} %collective-permute-done.18.refs_3_, ...), custom_call_target="tpu_custom_call", output_to_operand_aliasing={{}: (2, {})} | custom-call | flops 1207959552 | tf_op jit(solution)/shard_map/pallas_call | solution.py:227
  113.6 4.1 %shard_map.81.acc_in = f32[576,512]{1,0:T(8,128)S(1)} custom-call(bf16[8192,256]{1,0:T(8,128)(2,1)S(1)} %copy-done.1, bf16[8192,256]{1,0:T(8,128)(2,1)} %collective-permute-done.7.refs_1_.sibling, f32[576,512]{1,0:T(8,128)S(1)} %shard_map.80.refs_2_, bf16[224,1024]{1,0:T(8,128)(2,1)} %collective-permute-done.23.refs_3_, ...), custom_call_target="tpu_custom_call", output_to_operand_aliasing={{}: (2, {})} | custom-call | flops 1207959552 | tf_op jit(solution)/shard_map/pallas_call | solution.py:227
  117.7 3.7 %shard_map.83 = (f32[8,640]{1,0:T(8,128)S(1)}, f32[576,512]{1,0:T(8,128)S(1)}) custom-call(bf16[8192,256]{1,0:T(8,128)(2,1)S(1)} %copy-done.1, bf16[8192,256]{1,0:T(8,128)(2,1)} %collective-permute-done.7.refs_1_.sibling, f32[576,512]{1,0:T(8,128)S(1)} %shard_map.81.acc_in, ...), custom_call_target="tpu_custom_call", output_to_operand_aliasing={{1}: (2, {})} | custom-call | flops 301989888 | tf_op jit(solution)/shard_map/pallas_call | solution.py:227
  121.4 2.1 %collective-permute-start.28 = (f32[8,640]{1,0:T(8,128)S(1)}, f32[8,640]{1,0:T(8,128)S(1)}, u32[]{:S(2)}, u32[]{:S(2)}) collective-permute-start(f32[8,640]{1,0:T(8,128)S(1)} %get-tuple-element.11), channel_id=1, source_target_pairs={{0,2},{1,3},{2,0},{3,1},{4,6},{5,7},{6,4},{7,5},{8,10},{9,11},{10,... | collective-permute-start | bytes 61448 | tf_op jit(solution)/shard_map/ppermute | solution.py:287
  123.5 8.4 %collective-permute-start.29 = (f32[8,640]{1,0:T(8,128)S(1)}, f32[8,640]{1,0:T(8,128)S(1)}, u32[]{:S(2)}, u32[]{:S(2)}) collective-permute-start(f32[8,640]{1,0:T(8,128)S(1)} %get-tuple-element.11), channel_id=1, source_target_pairs={{0,4},{1,5},{2,6},{3,7},{4,0},{5,1},{6,2},{7,3},{8,12},{9,13},{10,... | collective-permute-start | bytes 61448 | tf_op jit(solution)/shard_map/ppermute | solution.py:287
  131.9 1.4 collective-permute-start.30
  133.7 3.8 %collective-permute-done.30 = f32[8,640]{1,0:T(8,128)S(1)} collective-permute-done((f32[8,640]{1,0:T(8,128)S(1)}, f32[8,640]{1,0:T(8,128)S(1)}, u32[]{:S(2)}, u32[]{:S(2)}) %collective-permute-start.30) | collective-permute-done | bytes 20512 | tf_op jit(solution)/shard_map/ppermute | solution.py:287
  137.6 1.4 collective-permute-start.31
  139.5 1.6 %collective-permute-start.33 = (f32[8,640]{1,0:T(8,128)S(1)}, f32[8,640]{1,0:T(8,128)S(1)}, u32[]{:S(2)}, u32[]{:S(2)}) collective-permute-start(f32[8,640]{1,0:T(8,128)S(1)} %maximum_maximum_fusion), channel_id=1, source_target_pairs={{0,17},{1,16},{2,19},{3,18},{4,21},{5,20},{6,23},{7,22},{8,25},{9,... | collective-permute-start | bytes 61448 | tf_op jit(solution)/shard_map/ppermute | solution.py:287
  141.4 1.4 collective-permute-done.32
  142.8 1.4 collective-permute-done.33
  144.3 1.2 collective-permute-done.34
  145.5 2.2 %shard_map.84 = (f32[1,384]{1,0:T(1,128)}, f32[1,1]{1,0:T(1,128)}) custom-call(s32[4]{0:T(128)S(1)} %copy-done.11, f32[2,2,8,384]{3,2,1,0:T(8,128)S(1)} %pad_maximum_fusion.2.sums, f32[2,8,640]{2,1,0:T(8,128)S(1)} %pad_maximum_fusion.3.stats), custom_call_target="tpu_custom_call" | custom-call | tf_op jit(solution)/shard_map/pallas_call | solution.py:227
  (75 shorter events, 11.9 us)
Async XLA Ops:
  0.6 96.3 %collective-permute-start.7 = (bf16[8192,256]{1,0:T(8,128)(2,1)}, bf16[8192,256]{1,0:T(8,128)(2,1)}, u32[]{:S(2)}, u32[]{:S(2)}) collective-permute-start(bf16[8192,256]{1,0:T(8,128)(2,1)} %head.1), channel_id=1, source_target_pairs={{0,8},{8,0},{16,24},{24,16},{1,9},{9,1},{17,25},{25,17},{2,10},{10... | collective-permute-start | bytes 12582920 | tf_op jit(solution)/shard_map/ppermute | solution.py:258
  1.1 7.7 %collective-permute-start = (bf16[384,1024]{1,0:T(8,128)(2,1)}, bf16[384,1024]{1,0:T(8,128)(2,1)S(1)}, u32[]{:S(2)}, u32[]{:S(2)}) collective-permute-start(bf16[384,1024]{1,0:T(8,128)(2,1)} %bitcast.16), channel_id=1, source_target_pairs={{0,8},{8,0},{16,24},{24,16},{1,9},{9,1},{17,25},{25,17},{2,10},{10... | collective-permute-start | bytes 2359304 | tf_op jit(solution)/shard_map/ppermute | solution.py:256
  2.3 2.1 %collective-permute-start.1 = (bf16[192,1024]{1,0:T(8,128)(2,1)S(1)}, bf16[192,1024]{1,0:T(8,128)(2,1)S(1)}, u32[]{:S(2)}, u32[]{:S(2)}) collective-permute-start(bf16[192,1024]{1,0:T(8,128)(2,1)S(1)} %slice_bitcast_fusion), channel_id=1, source_target_pairs={{8,24},{24,8},{9,25},{25,9},{10,26},{26,10},{11,27},{27,11},{12,28... | collective-permute-start | bytes 1179656 | tf_op jit(solution)/shard_map/ppermute | solution.py:257
  8.8 1.1 copy-start.8
  10.0 0.7 copy-start.10
  12.6 5.9 %collective-permute-start.11 = (bf16[64,1024]{1,0:T(8,128)(2,1)S(1)}, bf16[64,1024]{1,0:T(8,128)(2,1)S(1)}, u32[]{:S(2)}, u32[]{:S(2)}) collective-permute-start(bf16[64,1024]{1,0:T(8,128)(2,1)S(1)} %get-tuple-element.10), channel_id=1, source_target_pairs={{0,1},{1,0},{2,3},{3,2},{4,5},{5,4},{6,7},{7,6},{8,24},{9,25},{10,... | collective-permute-start | bytes 393224 | tf_op jit(solution)/shard_map/ppermute | solution.py:287
  15.5 66.3 %copy-start.9 = (s32[4,384]{1,0:T(4,128)S(1)}, s32[4,384]{1,0:T(4,128)}, u32[]{:S(2)}) copy-start(s32[4,384]{1,0:T(4,128)} %tokens.1) | copy-start | bytes 18436
  15.5 66.3 %copy-start.11 = (s32[4]{0:T(128)S(1)}, s32[4]{0:T(128)}, u32[]{:S(2)}) copy-start(s32[4]{0:T(128)} %lengths.5) | copy-start | bytes 52
  15.5 25.4 %collective-permute-start.8 = (bf16[224,1024]{1,0:T(8,128)(2,1)S(1)}, bf16[224,1024]{1,0:T(8,128)(2,1)S(1)}, u32[]{:S(2)}, u32[]{:S(2)}) collective-permute-start(bf16[224,1024]{1,0:T(8,128)(2,1)S(1)} %get-tuple-element.9.refs_2_), channel_id=1, source_target_pairs={{0,1},{1,0},{2,3},{3,2},{4,5},{5,4},{6,7},{7,6},{8,24},{9,25},{10,... | collective-permute-start | bytes 1376264 | tf_op jit(solution)/shard_map/ppermute | solution.py:287
  18.5 19.9 %collective-permute-start.12 = (bf16[128,1024]{1,0:T(8,128)(2,1)S(1)}, bf16[128,1024]{1,0:T(8,128)(2,1)S(1)}, u32[]{:S(2)}, u32[]{:S(2)}) collective-permute-start(bf16[128,1024]{1,0:T(8,128)(2,1)S(1)} %pad_maximum_fusion.1), channel_id=1, source_target_pairs={{0,16},{1,17},{2,18},{3,19},{4,20},{5,21},{6,22},{7,23},{8,9},{9,8... | collective-permute-start | bytes 786440 | tf_op jit(solution)/shard_map/ppermute | solution.py:287
  20.6 21.9 %collective-permute-start.9 = (bf16[224,1024]{1,0:T(8,128)(2,1)S(1)}, bf16[224,1024]{1,0:T(8,128)(2,1)S(1)}, u32[]{:S(2)}, u32[]{:S(2)}) collective-permute-start(bf16[224,1024]{1,0:T(8,128)(2,1)S(1)} %get-tuple-element.9.refs_2_), channel_id=1, source_target_pairs={{0,16},{1,17},{2,18},{3,19},{4,20},{5,21},{6,22},{7,23},{8,9},{9,8... | collective-permute-start | bytes 1376264 | tf_op jit(solution)/shard_map/ppermute | solution.py:287
  20.7 3.7 %collective-permute-start.2 = (f32[8,384]{1,0:T(8,128)S(1)}, f32[8,384]{1,0:T(8,128)S(1)}, u32[]{:S(2)}, u32[]{:S(2)}) collective-permute-start(f32[8,384]{1,0:T(8,128)S(1)} %get-tuple-element.8), channel_id=1, source_target_pairs={{0,2},{1,3},{2,0},{3,1},{4,6},{5,7},{6,4},{7,5},{8,10},{9,11},{10,... | collective-permute-start | bytes 36872 | tf_op jit(solution)/shard_map/ppermute | solution.py:287
  24.4 4.7 %collective-permute-start.3 = (f32[8,384]{1,0:T(8,128)S(1)}, f32[8,384]{1,0:T(8,128)S(1)}, u32[]{:S(2)}, u32[]{:S(2)}) collective-permute-start(f32[8,384]{1,0:T(8,128)S(1)} %add.76), channel_id=1, source_target_pairs={{0,4},{1,5},{2,6},{3,7},{4,0},{5,1},{6,2},{7,3},{8,12},{9,13},{10,... | collective-permute-start | bytes 36872 | tf_op jit(solution)/shard_map/ppermute | solution.py:287
  29.1 3.7 %collective-permute-start.4 = (f32[8,384]{1,0:T(8,128)S(1)}, f32[8,384]{1,0:T(8,128)S(1)}, u32[]{:S(2)}, u32[]{:S(2)}) collective-permute-start(f32[8,384]{1,0:T(8,128)S(1)} %add.77), channel_id=1, source_target_pairs={{0,1},{1,0},{2,3},{3,2},{4,5},{5,4},{6,7},{7,6},{8,9},{9,8},{10,11... | collective-permute-start | bytes 36872 | tf_op jit(solution)/shard_map/ppermute | solution.py:287
  32.8 3.7 %collective-permute-start.5 = (f32[8,384]{1,0:T(8,128)S(1)}, f32[8,384]{1,0:T(8,128)S(1)}, u32[]{:S(2)}, u32[]{:S(2)}) collective-permute-start(f32[8,384]{1,0:T(8,128)S(1)} %add.78), channel_id=1, source_target_pairs={{0,16},{8,24},{16,0},{24,8},{1,17},{9,25},{17,1},{25,9},{2,18},{10... | collective-permute-start | bytes 36872 | tf_op jit(solution)/shard_map/ppermute | solution.py:346
  36.5 20.9 %collective-permute-start.13 = (bf16[224,1024]{1,0:T(8,128)(2,1)S(1)}, bf16[224,1024]{1,0:T(8,128)(2,1)S(1)}, u32[]{:S(2)}, u32[]{:S(2)}) collective-permute-start(bf16[224,1024]{1,0:T(8,128)(2,1)S(1)} %get-tuple-element.9.refs_2_), channel_id=1, source_target_pairs={{0,2},{1,3},{2,0},{3,1},{4,6},{5,7},{6,4},{7,5},{8,10},{9,11},{10,... | collective-permute-start | bytes 1376264 | tf_op jit(solution)/shard_map/ppermute | solution.py:287
  38.4 23.8 %collective-permute-start.18 = (bf16[224,1024]{1,0:T(8,128)(2,1)S(1)}, bf16[224,1024]{1,0:T(8,128)(2,1)S(1)}, u32[]{:S(2)}, u32[]{:S(2)}) collective-permute-start(bf16[224,1024]{1,0:T(8,128)(2,1)S(1)} %get-tuple-element.9.refs_2_), channel_id=1, source_target_pairs={{0,6},{1,7},{2,4},{3,5},{4,2},{5,3},{6,0},{7,1},{8,14},{9,15},{10,... | collective-permute-start | bytes 1376264 | tf_op jit(solution)/shard_map/ppermute | solution.py:287
  40.9 23.6 %collective-permute-start.10 = (bf16[224,1024]{1,0:T(8,128)(2,1)S(1)}, bf16[224,1024]{1,0:T(8,128)(2,1)S(1)}, u32[]{:S(2)}, u32[]{:S(2)}) collective-permute-start(bf16[224,1024]{1,0:T(8,128)(2,1)S(1)} %collective-permute-done.8.refs_3_), channel_id=1, source_target_pairs={{0,16},{1,17},{2,18},{3,19},{4,20},{5,21},{6,22},{7,23},{8,9},{9,8... | collective-permute-start | bytes 1376264 | tf_op jit(solution)/shard_map/ppermute | solution.py:287
  42.5 28.5 %collective-permute-start.17 = (bf16[256,1024]{1,0:T(8,128)(2,1)S(1)}, bf16[256,1024]{1,0:T(8,128)(2,1)S(1)}, u32[]{:S(2)}, u32[]{:S(2)}) collective-permute-start(bf16[256,1024]{1,0:T(8,128)(2,1)S(1)} %pad_maximum_fusion.refs_6_), channel_id=1, source_target_pairs={{0,2},{1,3},{2,0},{3,1},{4,6},{5,7},{6,4},{7,5},{8,10},{9,11},{10,... | collective-permute-start | bytes 1572872 | tf_op jit(solution)/shard_map/ppermute | solution.py:287
  57.3 17.6 %collective-permute-start.14 = (bf16[224,1024]{1,0:T(8,128)(2,1)S(1)}, bf16[224,1024]{1,0:T(8,128)(2,1)}, u32[]{:S(2)}, u32[]{:S(2)}) collective-permute-start(bf16[224,1024]{1,0:T(8,128)(2,1)S(1)} %collective-permute-done.13.refs_3_), channel_id=1, source_target_pairs={{0,1},{1,0},{2,3},{3,2},{4,5},{5,4},{6,7},{7,6},{8,24},{9,25},{10,... | collective-permute-start | bytes 1376264 | tf_op jit(solution)/shard_map/ppermute | solution.py:287
  62.2 14.3 %collective-permute-start.15 = (bf16[224,1024]{1,0:T(8,128)(2,1)S(1)}, bf16[224,1024]{1,0:T(8,128)(2,1)S(1)}, u32[]{:S(2)}, u32[]{:S(2)}) collective-permute-start(bf16[224,1024]{1,0:T(8,128)(2,1)S(1)} %collective-permute-done.13.refs_3_), channel_id=1, source_target_pairs={{0,16},{1,17},{2,18},{3,19},{4,20},{5,21},{6,22},{7,23},{8,9},{9,8... | collective-permute-start | bytes 1376264 | tf_op jit(solution)/shard_map/ppermute | solution.py:287
  63.7 0.8 copy-start.2
  64.5 0.8 copy-start.4
  65.3 15.0 %collective-permute-start.23 = (bf16[224,1024]{1,0:T(8,128)(2,1)S(1)}, bf16[224,1024]{1,0:T(8,128)(2,1)}, u32[]{:S(2)}, u32[]{:S(2)}) collective-permute-start(bf16[224,1024]{1,0:T(8,128)(2,1)S(1)} %collective-permute-done.18.refs_3_), channel_id=1, source_target_pairs={{0,2},{1,3},{2,0},{3,1},{4,6},{5,7},{6,4},{7,5},{8,10},{9,11},{10,... | collective-permute-start | bytes 1376264 | tf_op jit(solution)/shard_map/ppermute | solution.py:287
  71.0 20.3 %collective-permute-start.22 = (bf16[256,1024]{1,0:T(8,128)(2,1)S(1)}, bf16[256,1024]{1,0:T(8,128)(2,1)S(1)}, u32[]{:S(2)}, u32[]{:S(2)}) collective-permute-start(bf16[256,1024]{1,0:T(8,128)(2,1)S(1)} %pad_maximum_fusion.refs_6_), channel_id=1, source_target_pairs={{0,6},{1,7},{2,4},{3,5},{4,2},{5,3},{6,0},{7,1},{8,14},{9,15},{10,... | collective-permute-start | bytes 1572872 | tf_op jit(solution)/shard_map/ppermute | solution.py:287
  74.9 17.8 %collective-permute-start.19 = (bf16[224,1024]{1,0:T(8,128)(2,1)S(1)}, bf16[224,1024]{1,0:T(8,128)(2,1)}, u32[]{:S(2)}, u32[]{:S(2)}) collective-permute-start(bf16[224,1024]{1,0:T(8,128)(2,1)S(1)} %collective-permute-done.18.refs_3_), channel_id=1, source_target_pairs={{0,1},{1,0},{2,3},{3,2},{4,5},{5,4},{6,7},{7,6},{8,24},{9,25},{10,... | collective-permute-start | bytes 1376264 | tf_op jit(solution)/shard_map/ppermute | solution.py:287
  76.4 0.8 copy-start.6
  77.3 16.0 %collective-permute-start.16 = (bf16[224,1024]{1,0:T(8,128)(2,1)}, bf16[224,1024]{1,0:T(8,128)(2,1)}, u32[]{:S(2)}, u32[]{:S(2)}) collective-permute-start(bf16[224,1024]{1,0:T(8,128)(2,1)} %collective-permute-done.14.refs_4_), channel_id=1, source_target_pairs={{0,16},{1,17},{2,18},{3,19},{4,20},{5,21},{6,22},{7,23},{8,9},{9,8... | collective-permute-start | bytes 1376264 | tf_op jit(solution)/shard_map/ppermute | solution.py:287
  80.3 14.5 %collective-permute-start.24 = (bf16[224,1024]{1,0:T(8,128)(2,1)}, bf16[224,1024]{1,0:T(8,128)(2,1)}, u32[]{:S(2)}, u32[]{:S(2)}) collective-permute-start(bf16[224,1024]{1,0:T(8,128)(2,1)} %collective-permute-done.23.refs_3_), channel_id=1, source_target_pairs={{0,1},{1,0},{2,3},{3,2},{4,5},{5,4},{6,7},{7,6},{8,24},{9,25},{10,... | collective-permute-start | bytes 1376264 | tf_op jit(solution)/shard_map/ppermute | solution.py:287
  91.3 18.3 %collective-permute-start.20 = (bf16[224,1024]{1,0:T(8,128)(2,1)S(1)}, bf16[224,1024]{1,0:T(8,128)(2,1)S(1)}, u32[]{:S(2)}, u32[]{:S(2)}) collective-permute-start(bf16[224,1024]{1,0:T(8,128)(2,1)S(1)} %collective-permute-done.18.refs_3_), channel_id=1, source_target_pairs={{0,16},{1,17},{2,18},{3,19},{4,20},{5,21},{6,22},{7,23},{8,9},{9,8... | collective-permute-start | bytes 1376264 | tf_op jit(solution)/shard_map/ppermute | solution.py:287
  92.8 20.8 %collective-permute-start.25 = (bf16[224,1024]{1,0:T(8,128)(2,1)}, bf16[224,1024]{1,0:T(8,128)(2,1)S(1)}, u32[]{:S(2)}, u32[]{:S(2)}) collective-permute-start(bf16[224,1024]{1,0:T(8,128)(2,1)} %collective-permute-done.23.refs_3_), channel_id=1, source_target_pairs={{0,16},{1,17},{2,18},{3,19},{4,20},{5,21},{6,22},{7,23},{8,9},{9,8... | collective-permute-start | bytes 1376264 | tf_op jit(solution)/shard_map/ppermute | solution.py:287
  93.3 16.3 %collective-permute-start.21 = (bf16[224,1024]{1,0:T(8,128)(2,1)}, bf16[224,1024]{1,0:T(8,128)(2,1)S(1)}, u32[]{:S(2)}, u32[]{:S(2)}) collective-permute-start(bf16[224,1024]{1,0:T(8,128)(2,1)} %collective-permute-done.19.refs_4_), channel_id=1, source_target_pairs={{0,16},{1,17},{2,18},{3,19},{4,20},{5,21},{6,22},{7,23},{8,9},{9,8... | collective-permute-start | bytes 1376264 | tf_op jit(solution)/shard_map/ppermute | solution.py:287
  94.8 18.8 %collective-permute-start.26 = (bf16[256,1024]{1,0:T(8,128)(2,1)S(1)}, bf16[256,1024]{1,0:T(8,128)(2,1)S(1)}, u32[]{:S(2)}, u32[]{:S(2)}) collective-permute-start(bf16[256,1024]{1,0:T(8,128)(2,1)S(1)} %collective-permute-done.22.refs_7_), channel_id=1, source_target_pairs={{0,2},{1,3},{2,0},{3,1},{4,6},{5,7},{6,4},{7,5},{8,10},{9,11},{10,... | collective-permute-start | bytes 1572872 | tf_op jit(solution)/shard_map/ppermute | solution.py:287
  96.9 20.7 %collective-permute-start.27 = (bf16[224,1024]{1,0:T(8,128)(2,1)}, bf16[224,1024]{1,0:T(8,128)(2,1)S(1)}, u32[]{:S(2)}, u32[]{:S(2)}) collective-permute-start(bf16[224,1024]{1,0:T(8,128)(2,1)} %collective-permute-done.24.refs_4_), channel_id=1, source_target_pairs={{0,16},{1,17},{2,18},{3,19},{4,20},{5,21},{6,22},{7,23},{8,9},{9,8... | collective-permute-start | bytes 1376264 | tf_op jit(solution)/shard_map/ppermute | solution.py:287
  98.2 2.2 %copy-start = (bf16[8192,256]{1,0:T(8,128)(2,1)S(1)}, bf16[8192,256]{1,0:T(8,128)(2,1)}, u32[]{:S(2)}) copy-start(bf16[8192,256]{1,0:T(8,128)(2,1)} %head.1) | copy-start | bytes 12582916
  100.4 1.0 copy-start.5
  101.5 3.9 %copy-start.1 = (bf16[8192,256]{1,0:T(8,128)(2,1)S(1)}, bf16[8192,256]{1,0:T(8,128)(2,1)}, u32[]{:S(2)}) copy-start(bf16[8192,256]{1,0:T(8,128)(2,1)} %head.1) | copy-start | bytes 12582916
  101.5 3.9 %copy-start.3 = (bf16[224,1024]{1,0:T(8,128)(2,1)S(1)}, bf16[224,1024]{1,0:T(8,128)(2,1)}, u32[]{:S(2)}) copy-start(bf16[224,1024]{1,0:T(8,128)(2,1)} %copy-done.2) | copy-start | bytes 1376260
  101.5 3.9 %copy-start.7 = (bf16[224,1024]{1,0:T(8,128)(2,1)S(1)}, bf16[224,1024]{1,0:T(8,128)(2,1)}, u32[]{:S(2)}) copy-start(bf16[224,1024]{1,0:T(8,128)(2,1)} %copy-done.6) | copy-start | bytes 1376260
  121.4 12.0 %collective-permute-start.28 = (f32[8,640]{1,0:T(8,128)S(1)}, f32[8,640]{1,0:T(8,128)S(1)}, u32[]{:S(2)}, u32[]{:S(2)}) collective-permute-start(f32[8,640]{1,0:T(8,128)S(1)} %get-tuple-element.11), channel_id=1, source_target_pairs={{0,2},{1,3},{2,0},{3,1},{4,6},{5,7},{6,4},{7,5},{8,10},{9,11},{10,... | collective-permute-start | bytes 61448 | tf_op jit(solution)/shard_map/ppermute | solution.py:287
  123.5 10.2 %collective-permute-start.29 = (f32[8,640]{1,0:T(8,128)S(1)}, f32[8,640]{1,0:T(8,128)S(1)}, u32[]{:S(2)}, u32[]{:S(2)}) collective-permute-start(f32[8,640]{1,0:T(8,128)S(1)} %get-tuple-element.11), channel_id=1, source_target_pairs={{0,4},{1,5},{2,6},{3,7},{4,0},{5,1},{6,2},{7,3},{8,12},{9,13},{10,... | collective-permute-start | bytes 61448 | tf_op jit(solution)/shard_map/ppermute | solution.py:287
  131.9 5.6 %collective-permute-start.30 = (f32[8,640]{1,0:T(8,128)S(1)}, f32[8,640]{1,0:T(8,128)S(1)}, u32[]{:S(2)}, u32[]{:S(2)}) collective-permute-start(f32[8,640]{1,0:T(8,128)S(1)} %get-tuple-element.11), channel_id=1, source_target_pairs={{0,6},{1,7},{2,4},{3,5},{4,2},{5,3},{6,0},{7,1},{8,14},{9,15},{10,... | collective-permute-start | bytes 61448 | tf_op jit(solution)/shard_map/ppermute | solution.py:287
  133.4 7.7 %collective-permute-start.6 = (f32[2,8,384]{2,1,0:T(8,128)S(1)}, f32[2,8,384]{2,1,0:T(8,128)S(1)}, u32[]{:S(2)}, u32[]{:S(2)}) collective-permute-start(f32[2,8,384]{2,1,0:T(8,128)S(1)} %pad_maximum_fusion.4.sums), channel_id=1, source_target_pairs={{0,8},{8,0},{16,24},{24,16},{1,9},{9,1},{17,25},{25,17},{2,10},{10... | collective-permute-start | bytes 73736 | tf_op jit(solution)/shard_map/ppermute | solution.py:376
  137.6 3.8 %collective-permute-start.31 = (f32[8,640]{1,0:T(8,128)S(1)}, f32[8,640]{1,0:T(8,128)S(1)}, u32[]{:S(2)}, u32[]{:S(2)}) collective-permute-start(f32[8,640]{1,0:T(8,128)S(1)} %maximum_maximum_fusion), channel_id=1, source_target_pairs={{0,1},{1,0},{2,3},{3,2},{4,5},{5,4},{6,7},{7,6},{8,9},{9,8},{10,11... | collective-permute-start | bytes 61448 | tf_op jit(solution)/shard_map/ppermute | solution.py:287
  139.0 3.8 %collective-permute-start.32 = (f32[8,640]{1,0:T(8,128)S(1)}, f32[8,640]{1,0:T(8,128)S(1)}, u32[]{:S(2)}, u32[]{:S(2)}) collective-permute-start(f32[8,640]{1,0:T(8,128)S(1)} %maximum_maximum_fusion), channel_id=1, source_target_pairs={{0,16},{1,17},{2,18},{3,19},{4,20},{5,21},{6,22},{7,23},{8,24},{9,... | collective-permute-start | bytes 61448 | tf_op jit(solution)/shard_map/ppermute | solution.py:287
  139.5 4.7 %collective-permute-start.33 = (f32[8,640]{1,0:T(8,128)S(1)}, f32[8,640]{1,0:T(8,128)S(1)}, u32[]{:S(2)}, u32[]{:S(2)}) collective-permute-start(f32[8,640]{1,0:T(8,128)S(1)} %maximum_maximum_fusion), channel_id=1, source_target_pairs={{0,17},{1,16},{2,19},{3,18},{4,21},{5,20},{6,23},{7,22},{8,25},{9,... | collective-permute-start | bytes 61448 | tf_op jit(solution)/shard_map/ppermute | solution.py:287
  144.3 1.3 collective-permute-start.34

commit v3 on v2

--- a/solution.py
+++ b/solution.py
@@ -14,6 +14,7 @@
 LANES = 128
 VMEM = pl.BlockSpec(memory_space=pltpu.VMEM)
 SMEM = pl.BlockSpec(memory_space=pltpu.SMEM)
+ANY = pl.BlockSpec(memory_space=pl.ANY)
 
 
 def row_map(lengths, pair, core, index, count):
@@ -42,7 +43,9 @@
     return jnp.transpose(full)[:, which : which + 1]
 
 
-def pick_kernel(count, lengths, rows, sibling, extra, gain, reward, big, small, partial):
+def pick_kernel(count, lengths, rows, sibling, extra, gain, reward, head, big, small, partial, head_out, sem):
+    copy = pltpu.make_async_copy(head, head_out, sem)
+    copy.start()
     section = lax.axis_index("section")
     core, pair = lax.rem(section, 2), lax.div(section, 2)
     positions, half = rows.shape[0], extra.shape[0]
@@ -66,6 +69,7 @@
     partial[...] = as_rows(
         [jnp.concatenate([squares, zeros]), jnp.concatenate([rewards, zeros])], padded
     )
+    copy.wait()
 
 
 def token_kernel(count, n, lengths, tokens, out):
@@ -106,49 +110,74 @@
             acc[rows, i * w : (i + 1) * w] = acc[rows, i * w : (i + 1) * w] + part
 
 
-def mm_kernel(k, first, parts, *refs):
+def stage_kernel(stage, names, n, m, n_pass, *refs):
     refs = list(refs)
-    head, sibling = refs.pop(0), refs.pop(0)
-    acc_in = None if first else refs.pop(0)
-    acc = refs.pop()
-    named = dict(zip(parts, refs))
-    depth = refs[0].shape[1]
-    m = 64 if "w" not in named else named["w"].shape[0] // 4
-    n = acc.shape[0] // 2 - m
-    core, near, far, mine, others, small_mine, small_others = offsets(k, n, m)
-
-    def times(value, where):
+    head, sibling = refs[0], refs[1]
+    first = stage == 0
+    at = 2
+    acc_in = None
+    if not first:
+        acc_in = refs[at]
+        at += 1
+    pieces = dict(zip(names, refs[at : at + len(names)]))
+    at += len(names)
+    sums = refs[at]
+    at += 1
+    if not first:
+        received = refs[at]
+        at += 1
+    at += n_pass
+    acc, sums_out = refs[at], refs[at + 1]
+    depth = refs[2 if first else 3].shape[1]
+
+    def times(name, k, far):
+        _, near, other, _, _, _, _ = offsets(k, n, m)
+        where = other if far else near
         rows = pl.ds(pl.multiple_of(where * depth, depth), depth)
+        value = pieces[name][...]
         return [jnp.dot(value, h[rows, :], preferred_element_type=F32) for h in (head, sibling)]
 
     def plus(x, y):
         return [i + j for i, j in zip(x, y)]
 
-    if not first:
+    core, _, _, mine, others, small_mine, small_others = offsets(0, n, m)
+    if first:
+        sums_out[...] = sums[...]
+        acc[2 * n :, :] = jnp.zeros((2 * m, acc.shape[1]), F32)
+    else:
+        sums_out[...] = sums[...] + received[...]
         acc[...] = acc_in[...]
-    if "a" in named:
-
-        @pl.when(core == 0)
+    k = (0, 1, 3, 2)[stage]
+    before = (0, 0, 1, 3)[stage]
+    for c in range(2):
+
+        @pl.when(core == c)
         def _():
-            add(acc, mine, plus(times(named["z"][...], near), times(named["a"][...], far)), first)
-            value = times(named["b"][...], near)
-            if "c" in named:
-                value = plus(value, times(named["c"][...], far))
+            same, cross = ("a", "b") if c == 0 else ("b", "a")
+            add(acc, mine, plus(times("z", k, False), times(same, k, True)), first)
+            value = times(cross, k, False)
+            if "c" in pieces:
+                value = plus(value, times("c", before, True))
             add(acc, others, value, first)
 
-        @pl.when(core == 1)
-        def _():
-            add(acc, mine, plus(times(named["z"][...], near), times(named["b"][...], far)), first)
-            value = times(named["a"][...], near)
-            if "c" in named:
-                value = plus(value, times(named["c"][...], far))
-            add(acc, others, value, first)
-
-    if "w" in named:
-        w = named["w"]
-        value = plus(times(w[: 2 * m, :], near), times(w[2 * m :, :], far))
-        add(acc, small_mine, [v[:m] for v in value], first)
-        add(acc, small_others, [v[m:] for v in value], first)
+    for name, w_k in (("w0", 0), ("w1", 1), ("w3", 3)):
+        if name in pieces:
+            small(acc, pieces[name], head, sibling, w_k, n, m)
+
+
+def small(acc, w, head, sibling, k, n, m):
+    _, near, far, _, _, mine, others = offsets(k, n, m)
+    depth = w.shape[1]
+    value = None
+    for i, where in enumerate((near, far)):
+        rows = pl.ds(pl.multiple_of(where * depth, depth), depth)
+        part = [
+            jnp.dot(w[2 * m * i : 2 * m * (i + 1), :], h[rows, :], preferred_element_type=F32)
+            for h in (head, sibling)
+        ]
+        value = part if value is None else [x + y for x, y in zip(value, part)]
+    add(acc, mine, [v[:m] for v in value], False)
+    add(acc, others, [v[m:] for v in value], False)
 
 
 def summarize(logits, squares, token_ids, bases, block, width, out):
@@ -168,7 +197,7 @@
     out[...] = as_rows([jnp.concatenate([v, zeros]) for v in (top, total, target)], padded)
 
 
-def last_kernel(k, n, width, head, sibling, acc_in, c, sums, token_ids, out, acc):
+def last_kernel(k, n, width, head, sibling, acc_in, c, w, sums, across, token_ids, out, acc):
     count = acc_in.shape[0] // 2
     m = count - n
     block = head.shape[1]
@@ -183,7 +212,12 @@
         for i, h in enumerate((head, sibling)):
             cols = slice(i * block, (i + 1) * block)
             acc[others, cols] = acc[others, cols] + jnp.dot(c[...], h[rows, :], preferred_element_type=F32)
-    squares = [as_column(sums[p], 0) for p in range(2)]
+        small(acc, w, head, sibling, k, n, m)
+    swapped = lax.div(section, 2) == 1
+    squares = [
+        as_column(jnp.where(swapped, across[...], sums[...]), 0),
+        as_column(jnp.where(swapped, sums[...], across[...]), 0),
+    ]
     column = jnp.concatenate([squares[0][:n], squares[1][:n], squares[0][n:count], squares[1][n:count]])
     summarize(acc[...], column, token_ids[...], bases, block, width, out)
 
@@ -222,14 +256,15 @@
     return jnp.concatenate([jnp.stack([top, total, target]), jnp.zeros((5,) + top.shape, F32)])
 
 
-def call(body, outs, in_specs, args, flops=0, moved=0, alias=None, limit=32):
+def call(body, outs, in_specs, args, flops=0, moved=0, alias=None, limit=32, out_specs=None, scratch=()):
     many = isinstance(outs, (list, tuple))
     return pl.pallas_call(
         body,
         out_shape=outs,
         in_specs=in_specs,
-        out_specs=[VMEM] * len(outs) if many else VMEM,
+        out_specs=out_specs or ([VMEM] * len(outs) if many else VMEM),
         input_output_aliases=alias or {},
+        scratch_shapes=scratch,
         compiler_params=pltpu.CompilerParams(vmem_limit_bytes=limit << 20),
         cost_estimate=pl.CostEstimate(flops=flops, bytes_accessed=moved, transcendentals=0),
     )(*args)
@@ -255,19 +290,21 @@
     over = [(s, s ^ 2) for s in range(sections)]
     sibling = lax.ppermute(rows, "section", swap)
     extra = lax.ppermute(rows[half:], "section", [(1, 3), (3, 1)])
-    head_sibling = lax.ppermute(head, "section", swap)
-
-    g, s0, partial = call(
+
+    g, s0, partial, head = call(
         functools.partial(pick_kernel, count),
         [
             jax.ShapeDtypeStruct((big, part), BF16),
             jax.ShapeDtypeStruct((small, part), BF16),
             jax.ShapeDtypeStruct((8, up(count)), F32),
+            jax.ShapeDtypeStruct(head.shape, BF16),
         ],
-        [SMEM] + [VMEM] * 5,
-        (lengths, rows, sibling, extra, norm_gain[None], reward_head[None]),
+        [SMEM] + [VMEM] * 5 + [ANY],
+        (lengths, rows, sibling, extra, norm_gain[None], reward_head[None], head),
         flops=2 * count * 960 * part,
-    )
+        scratch=[pltpu.SemaphoreType.DMA],
+    )
+    head_sibling = lax.ppermute(head, "section", swap)
     token_ids = call(
         functools.partial(token_kernel, count, big),
         jax.ShapeDtypeStruct((2 * count, 1), I32),
@@ -293,43 +330,60 @@
         perm_z = {k: mesh_perm(lambda s, d, k=k: (s, d ^ (2 * k))) for k in (1, 2, 3)}
         zero = core == 0
 
-        z = {0: g}
-        a, b, c, w = {}, {}, {}, {}
-        z[3] = send(g, perm_z[3])
+        z1 = send(g, perm_z[1])
+        z3 = send(g, perm_z[3])
         a3 = send(s0, perm_a)
-        z[1] = send(g, perm_z[1])
-        a[0] = send(g, perm_a)
+        a0 = send(g, perm_a)
+        b0 = send(g, perm_b)
         b3 = send(jnp.concatenate([s0, a3]), perm_b)
-        b[0] = send(g, perm_b)
-        c[0] = send(a[0], perm_b)
-        w[0] = jnp.concatenate(
+        c0 = send(a0, perm_b)
+        w0 = jnp.concatenate(
             [s0, jnp.where(zero, b3[:small], a3), jnp.where(zero, a3, b3[:small]), b3[small:]]
         )
-        z[2] = send(z[3], perm_z[1])
-        w[3] = send(w[0], perm_z[3])
-        w[1] = send(w[0], perm_z[1])
-        w[2] = send(w[3], perm_z[1])
-        for k in (1, 3, 2):
-            a[k] = send(z[k], perm_a)
-            b[k] = send(z[k], perm_b)
-            c[k] = send(a[k], perm_b)
-
-        for perm in (perm_z[1], perm_z[2], perm_x):
-            partial = partial + send(partial, perm)
-        acc = None
-        for k, parts in ((0, "zabcw"), (1, "zabcw"), (3, "zabcw"), (2, "zabw")):
-            pieces = {"z": z, "a": a, "b": b, "c": c, "w": w}
-            values = [pieces[p][k] for p in parts]
+        z2 = send(z3, perm_z[1])
+
+        def run(stage, acc, pieces, sums, received, passed):
             first = acc is None
-            acc = call(
-                functools.partial(mm_kernel, k, first, parts),
-                acc_shape,
-                [VMEM] * (2 + (not first) + len(values)),
-                (head, head_sibling) + (() if first else (acc,)) + tuple(values),
-                flops=2 * 4 * count * part * 2 * block,
-                alias={} if first else {2: 0},
+            args = (head, head_sibling) + (() if first else (acc,)) + tuple(pieces.values())
+            args = args + (sums,) + (() if first else (received,))
+            alias = {len(args) + i: 2 + i for i in range(len(passed))}
+            if not first:
+                alias[2] = 0
+            return call(
+                functools.partial(stage_kernel, stage, tuple(pieces), big, small, len(passed)),
+                [acc_shape, jax.ShapeDtypeStruct(partial.shape, F32)]
+                + [jax.ShapeDtypeStruct(p.shape, p.dtype) for p in passed],
+                [VMEM] * len(args) + [ANY] * len(passed),
+                args + tuple(passed),
+                flops=2 * len(pieces) * big * part * 2 * block,
+                alias=alias,
+                out_specs=[VMEM] * 2 + [ANY] * len(passed),
             )
-        last_c = c[2]
+
+        acc, sums, z1, w0 = run(0, None, {"z": g, "a": a0, "b": b0}, partial, None, (z1, w0))
+        received = send(sums, perm_z[1])
+        w1 = send(w0, perm_z[1])
+        a1 = send(z1, perm_a)
+        b1 = send(z1, perm_b)
+        c1 = send(a1, perm_b)
+        acc, sums, z3, w0 = run(1, acc, {"z": z1, "a": a1, "b": b1, "c": c0}, sums, received, (z3, w0))
+        received = send(sums, perm_z[2])
+        w3 = send(w0, perm_z[3])
+        a_3 = send(z3, perm_a)
+        b_3 = send(z3, perm_b)
+        c_3 = send(a_3, perm_b)
+        acc, sums, z2 = run(
+            2, acc, {"z": z3, "a": a_3, "b": b_3, "c": c1, "w0": w0, "w1": w1}, sums, received, (z2,)
+        )
+        received = send(sums, perm_x)
+        a_2 = send(z2, perm_a)
+        b_2 = send(z2, perm_b)
+        c_2 = send(a_2, perm_b)
+        w2 = send(w3, perm_z[1])
+        acc, partial = run(
+            3, acc, {"z": z2, "a": a_2, "b": b_2, "c": c_3, "w3": w3}, sums, received, ()
+        )
+        last_c = c_2
     else:
         partial = lax.psum(partial, "dp")
         mine = jnp.concatenate([g, s0])
@@ -350,8 +404,8 @@
         stats, _ = call(
             functools.partial(last_kernel, 2, big, width),
             [stats_shape, acc_shape],
-            [VMEM] * 6,
-            (head, head_sibling, acc, last_c, sums, token_ids),
+            [VMEM] * 8,
+            (head, head_sibling, acc, last_c, w2, partial, other, token_ids),
             flops=2 * count * part * 2 * block,
             alias={2: 1},
         )
@@ -361,11 +415,15 @@
             + [send(stats, mesh_perm(lambda s, d, v=v: (s ^ v[0], d ^ v[1]))) for v in ((0, 1), (2, 0), (2, 1))]
         )
     else:
-        def body(head, sibling, acc_in, sums, token_ids, out, acc):
-            last_kernel(2, big, width, head, sibling, acc_in, None, sums, token_ids, out, acc)
+        def body(head, sibling, acc_in, sums, across, token_ids, out, acc):
+            last_kernel(2, big, width, head, sibling, acc_in, None, None, sums, across, token_ids, out, acc)
 
         stats, _ = call(
-            body, [stats_shape, acc_shape], [VMEM] * 5, (head, head_sibling, acc, sums, token_ids), alias={2: 1}
+            body,
+            [stats_shape, acc_shape],
+            [VMEM] * 6,
+            (head, head_sibling, acc, partial, other, token_ids),
+            alias={2: 1},
         )
         gathered = lax.all_gather(stats, "dp")
         stats = combine([gathered[i] for i in range(groups)])

time: 148 us -> 149 us (level)
  starting transfers between devices: 56.4 us -> 46.9 us
  Pallas kernels: 25.2 us -> 32.8 us
  waiting for transfers between devices: 55.1 us -> 62.6 us
  local copies, waits for them, and re-layouts: 9.88 us -> 5.33 us
    ppermute x29, starting transfers between devices: 53.2 us -> 37.3 us  [per_device(): send = lambda value, perm: lax.ppermute(value, AXES, perm)]
    ppermute x29, waiting for transfers between devices: 47.6 us -> 59.6 us  [per_device(): send = lambda value, perm: lax.ppermute(value, AXES, perm)]
    pallas_call x8, Pallas kernels: 25.2 us -> 32.8 us  [call(): pl.pallas_call(body, out_shape=outs, in_specs=in_specs, out_specs=out_spe...]
    ppermute x1, starting transfers between devices: 0.52 us -> 7.8 us  [per_device(): head_sibling = lax.ppermute(head, 'section', swap)]
    unnamed x24 -> x10, local copies, waits for them, and re-layouts: 7.4 us -> 2.85 us
    ppermute x1, waiting for transfers between devices: 4.52 us -> 0.01 us  [per_device(): sibling = lax.ppermute(rows, 'section', swap)]
  transfers between devices with their start and end apart: 35 -> 35, of which waited for: 17 -> 20; matrix products, arithmetic and copies ran while one was open for 2% -> 2% of each run, Pallas kernels for 13% -> 14%
where the time goes in v3:
time: 149 us
  waiting for transfers between devices  62.6 us (42%)
  starting transfers between devices  46.9 us (31%)
  Pallas kernels  32.8 us (22%)
  local copies, waits for them, and re-layouts  5.33 us (4%)
    ppermute x29, waiting for transfers between devices, per_device(): send = lambda value, perm: lax.ppermute(value, AXES, perm)  59.6 us
    ppermute x29, starting transfers between devices, per_device(): send = lambda value, perm: lax.ppermute(value, AXES, perm)  37.3 us
    pallas_call x8, Pallas kernels, call(): pl.pallas_call(body, out_shape=outs, in_specs=in_specs, out_specs=out_spe...  32.8 us
    ppermute x1, starting transfers between devices, per_device(): head_sibling = lax.ppermute(head, 'section', swap)  7.8 us
  transfers between devices with their start and end apart: 35, of which 20 were waited for; matrix products, arithmetic and copies ran while one was open for 2% of the time, Pallas kernels for 14%

profile of v3, /device:TPU:0, one launch (start us, length us, event | category | flops | bytes accessed | tf_op | source)
XLA Modules:
  0.0 148.8 jit_solution(14685602729415341061)
XLA Ops:
  1.2 1.0 slice_bitcast_fusion
  2.2 0.7 collective-permute-start.1
  2.9 0.7 broadcast_in_dim.10.gain
  3.6 0.7 broadcast_in_dim.11.reward
  4.3 2.2 %copy-done = bf16[8192,256]{1,0:T(8,128)(2,1)S(1)} copy-done((bf16[8192,256]{1,0:T(8,128)(2,1)S(1)}, bf16[8192,256]{1,0:T(8,128)(2,1)}, u32[]{:S(2)}) %copy-start) | copy-done | bytes 4194328
  6.5 0.7 copy-done.3
  7.1 4.2 %shard_map.77 = (bf16[224,1024]{1,0:T(8,128)(2,1)S(1)}, bf16[64,1024]{1,0:T(8,128)(2,1)S(1)}, f32[8,384]{1,0:T(8,128)S(1)}, bf16[8192,256]{1,0:T(8,128)(2,1)}) custom-call(s32[4]{0:T(128)S(1)} %copy-done.3, bf16[384,1024]{1,0:T(8,128)(2,1)S(1)} %bitcast.17, bf16[384,1024]{1,0:T(8,128)(2,1)S(1)} %collective-permute-done.sibling, ...), custom_call_target="tpu_custom_call" | custom-call | flops 566231040 | tf_op jit(solution)/shard_map/pallas_call | solution.py:261
  11.3 7.8 %collective-permute-start.2 = (bf16[8192,256]{1,0:T(8,128)(2,1)}, bf16[8192,256]{1,0:T(8,128)(2,1)}, u32[]{:S(2)}, u32[]{:S(2)}) collective-permute-start(bf16[8192,256]{1,0:T(8,128)(2,1)} %get-tuple-element.22.refs_0_.head), channel_id=1, source_target_pairs={{0,8},{8,0},{16,24},{24,16},{1,9},{9,1},{17,25},{25,17},{2,10},{10... | collective-permute-start | bytes 12582920 | tf_op jit(solution)/shard_map/ppermute | solution.py:307
  19.1 1.7 %collective-permute-start.6 = (bf16[64,1024]{1,0:T(8,128)(2,1)S(1)}, bf16[64,1024]{1,0:T(8,128)(2,1)S(1)}, u32[]{:S(2)}, u32[]{:S(2)}) collective-permute-start(bf16[64,1024]{1,0:T(8,128)(2,1)S(1)} %get-tuple-element.25), channel_id=1, source_target_pairs={{0,1},{1,0},{2,3},{3,2},{4,5},{5,4},{6,7},{7,6},{8,24},{9,25},{10,... | collective-permute-start | bytes 393224 | tf_op jit(solution)/shard_map/ppermute | solution.py:324
  20.8 3.3 %collective-permute-done.6 = bf16[64,1024]{1,0:T(8,128)(2,1)S(1)} collective-permute-done((bf16[64,1024]{1,0:T(8,128)(2,1)S(1)}, bf16[64,1024]{1,0:T(8,128)(2,1)S(1)}, u32[]{:S(2)}, u32[]{:S(2)}) %collective-permute-start.6) | collective-permute-done | bytes 131104 | tf_op jit(solution)/shard_map/ppermute | solution.py:324
  24.1 1.8 %collective-permute-start.7 = (bf16[128,1024]{1,0:T(8,128)(2,1)S(1)}, bf16[128,1024]{1,0:T(8,128)(2,1)S(1)}, u32[]{:S(2)}, u32[]{:S(2)}) collective-permute-start(bf16[128,1024]{1,0:T(8,128)(2,1)S(1)} %pad_maximum_fusion.1), channel_id=1, source_target_pairs={{0,16},{1,17},{2,18},{3,19},{4,20},{5,21},{6,22},{7,23},{8,9},{9,8... | collective-permute-start | bytes 786440 | tf_op jit(solution)/shard_map/ppermute | solution.py:324
  25.9 1.5 %collective-permute-start.3 = (bf16[224,1024]{1,0:T(8,128)(2,1)S(1)}, bf16[224,1024]{1,0:T(8,128)(2,1)S(1)}, u32[]{:S(2)}, u32[]{:S(2)}) collective-permute-start(bf16[224,1024]{1,0:T(8,128)(2,1)S(1)} %get-tuple-element.23.refs_2_), channel_id=1, source_target_pairs={{0,1},{1,0},{2,3},{3,2},{4,5},{5,4},{6,7},{7,6},{8,24},{9,25},{10,... | collective-permute-start | bytes 1376264 | tf_op jit(solution)/shard_map/ppermute | solution.py:324
  27.9 1.6 %collective-permute-start.5 = (bf16[224,1024]{1,0:T(8,128)(2,1)S(1)}, bf16[224,1024]{1,0:T(8,128)(2,1)S(1)}, u32[]{:S(2)}, u32[]{:S(2)}) collective-permute-start(bf16[224,1024]{1,0:T(8,128)(2,1)S(1)} %get-tuple-element.23.refs_2_), channel_id=1, source_target_pairs={{0,2},{1,3},{2,0},{3,1},{4,6},{5,7},{6,4},{7,5},{8,10},{9,11},{10,... | collective-permute-start | bytes 1376264 | tf_op jit(solution)/shard_map/ppermute | solution.py:324
  29.5 3.9 %collective-permute-done.7 = bf16[128,1024]{1,0:T(8,128)(2,1)S(1)} collective-permute-done((bf16[128,1024]{1,0:T(8,128)(2,1)S(1)}, bf16[128,1024]{1,0:T(8,128)(2,1)S(1)}, u32[]{:S(2)}, u32[]{:S(2)}) %collective-permute-start.7) | collective-permute-done | bytes 262176 | tf_op jit(solution)/shard_map/ppermute | solution.py:324
  33.4 3.8 %collective-permute-start.12 = (bf16[224,1024]{1,0:T(8,128)(2,1)S(1)}, bf16[224,1024]{1,0:T(8,128)(2,1)S(1)}, u32[]{:S(2)}, u32[]{:S(2)}) collective-permute-start(bf16[224,1024]{1,0:T(8,128)(2,1)S(1)} %get-tuple-element.23.refs_2_), channel_id=1, source_target_pairs={{0,6},{1,7},{2,4},{3,5},{4,2},{5,3},{6,0},{7,1},{8,14},{9,15},{10,... | collective-permute-start | bytes 1376264 | tf_op jit(solution)/shard_map/ppermute | solution.py:324
  37.2 1.4 collective-permute-done.3.refs_3_
  38.6 1.4 collective-permute-done.4.refs_4_
  40.5 4.4 %shard_map.78 = (f32[576,512]{1,0:T(8,128)S(1)}, f32[8,384]{1,0:T(8,128)S(1)}, bf16[224,1024]{1,0:T(8,128)(2,1)S(1)}, bf16[256,1024]{1,0:T(8,128)(2,1)S(1)}) custom-call(bf16[8192,256]{1,0:T(8,128)(2,1)} %get-tuple-element.22.refs_0_.head, bf16[8192,256]{1,0:T(8,128)(2,1)} %collective-permute-done.2.refs_1_.sibling, ...), custom_call_target="tpu_custom_call", output_to_operand_aliasing={{2}: (6, {}), {3}: (7, {})} | custom-call | flops 704643072 | tf_op jit(solution)/shard_map/pallas_call | solution.py:261
  44.8 2.5 %collective-permute-start.16 = (bf16[256,1024]{1,0:T(8,128)(2,1)S(1)}, bf16[256,1024]{1,0:T(8,128)(2,1)S(1)}, u32[]{:S(2)}, u32[]{:S(2)}) collective-permute-start(bf16[256,1024]{1,0:T(8,128)(2,1)S(1)} %get-tuple-element.29.refs_10_), channel_id=1, source_target_pairs={{0,2},{1,3},{2,0},{3,1},{4,6},{5,7},{6,4},{7,5},{8,10},{9,11},{10,... | collective-permute-start | bytes 1572872 | tf_op jit(solution)/shard_map/ppermute | solution.py:324
  47.4 1.3 collective-permute-start.10
  48.7 0.7 collective-permute-start.8
  49.4 3.9 %collective-permute-done.12.refs_9_ = bf16[224,1024]{1,0:T(8,128)(2,1)S(1)} collective-permute-done((bf16[224,1024]{1,0:T(8,128)(2,1)S(1)}, bf16[224,1024]{1,0:T(8,128)(2,1)S(1)}, u32[]{:S(2)}, u32[]{:S(2)}) %collective-permute-start.12) | collective-permute-done | bytes 458784 | tf_op jit(solution)/shard_map/ppermute | solution.py:324
  53.3 1.7 %collective-permute-start.9 = (bf16[224,1024]{1,0:T(8,128)(2,1)S(1)}, bf16[224,1024]{1,0:T(8,128)(2,1)S(1)}, u32[]{:S(2)}, u32[]{:S(2)}) collective-permute-start(bf16[224,1024]{1,0:T(8,128)(2,1)S(1)} %get-tuple-element.27.refs_3_), channel_id=1, source_target_pairs={{0,16},{1,17},{2,18},{3,19},{4,20},{5,21},{6,22},{7,23},{8,9},{9,8... | collective-permute-start | bytes 1376264 | tf_op jit(solution)/shard_map/ppermute | solution.py:324
  55.0 3.1 %collective-permute-done.10.refs_6_ = bf16[224,1024]{1,0:T(8,128)(2,1)S(1)} collective-permute-done((bf16[224,1024]{1,0:T(8,128)(2,1)S(1)}, bf16[224,1024]{1,0:T(8,128)(2,1)S(1)}, u32[]{:S(2)}, u32[]{:S(2)}) %collective-permute-start.10) | collective-permute-done | bytes 458784 | tf_op jit(solution)/shard_map/ppermute | solution.py:324
  58.6 3.6 %collective-permute-done.8.refs_4_ = bf16[224,1024]{1,0:T(8,128)(2,1)S(1)} collective-permute-done((bf16[224,1024]{1,0:T(8,128)(2,1)S(1)}, bf16[224,1024]{1,0:T(8,128)(2,1)S(1)}, u32[]{:S(2)}, u32[]{:S(2)}) %collective-permute-start.8) | collective-permute-done | bytes 458784 | tf_op jit(solution)/shard_map/ppermute | solution.py:324
  62.2 0.7 collective-permute-start.15
  62.9 9.0 %collective-permute-done.18.refs_11_ = bf16[224,1024]{1,0:T(8,128)(2,1)S(1)} collective-permute-done((bf16[224,1024]{1,0:T(8,128)(2,1)S(1)}, bf16[224,1024]{1,0:T(8,128)(2,1)S(1)}, u32[]{:S(2)}, u32[]{:S(2)}) %collective-permute-start.18) | collective-permute-done | bytes 458784 | tf_op jit(solution)/shard_map/ppermute | solution.py:324
  72.0 4.7 %shard_map.79 = (f32[576,512]{1,0:T(8,128)S(1)}, f32[8,384]{1,0:T(8,128)S(1)}, bf16[224,1024]{1,0:T(8,128)(2,1)S(1)}, bf16[256,1024]{1,0:T(8,128)(2,1)S(1)}) custom-call(bf16[8192,256]{1,0:T(8,128)(2,1)} %get-tuple-element.22.refs_0_.head, ...), custom_call_target="tpu_custom_call", output_to_operand_aliasing={{2}: (9, {}), {3}: (10, {}), {0}: (2, {})} | custom-call | flops 939524096 | tf_op jit(solution)/shard_map/pallas_call | solution.py:261
  76.8 1.6 %collective-permute-start.13 = (bf16[224,1024]{1,0:T(8,128)(2,1)S(1)}, bf16[224,1024]{1,0:T(8,128)(2,1)S(1)}, u32[]{:S(2)}, u32[]{:S(2)}) collective-permute-start(bf16[224,1024]{1,0:T(8,128)(2,1)S(1)} %get-tuple-element.31.refs_3_), channel_id=1, source_target_pairs={{0,1},{1,0},{2,3},{3,2},{4,5},{5,4},{6,7},{7,6},{8,24},{9,25},{10,... | collective-permute-start | bytes 1376264 | tf_op jit(solution)/shard_map/ppermute | solution.py:324
  79.4 1.4 collective-permute-start.22
  80.8 13.6 %collective-permute-done.17.refs_10_ = f32[8,384]{1,0:T(8,128)S(1)} collective-permute-done((f32[8,384]{1,0:T(8,128)S(1)}, f32[8,384]{1,0:T(8,128)S(1)}, u32[]{:S(2)}, u32[]{:S(2)}) %collective-permute-start.17) | collective-permute-done | bytes 12320 | tf_op jit(solution)/shard_map/ppermute | solution.py:324
  94.3 5.5 %shard_map.80 = (f32[576,512]{1,0:T(8,128)S(1)}, f32[8,384]{1,0:T(8,128)S(1)}, bf16[224,1024]{1,0:T(8,128)(2,1)S(1)}) custom-call(bf16[8192,256]{1,0:T(8,128)(2,1)} %get-tuple-element.22.refs_0_.head, bf16[8192,256]{1,0:T(8,128)(2,1)} %collective-permute-done.2.refs_1_.sibling, ...), custom_call_target="tpu_custom_call", output_to_operand_aliasing={{2}: (11, {}), {0}: (2, {})} | custom-call | flops 1409286144 | tf_op jit(solution)/shard_map/pallas_call | solution.py:261
  100.3 1.5 collective-permute-start.20
  102.3 2.9 %collective-permute-start.27 = (bf16[256,1024]{1,0:T(8,128)(2,1)S(1)}, bf16[256,1024]{1,0:T(8,128)(2,1)S(1)}, u32[]{:S(2)}, u32[]{:S(2)}) collective-permute-start(bf16[256,1024]{1,0:T(8,128)(2,1)S(1)} %collective-permute-done.22.refs_7_), channel_id=1, source_target_pairs={{0,2},{1,3},{2,0},{3,1},{4,6},{5,7},{6,4},{7,5},{8,10},{9,11},{10,... | collective-permute-start | bytes 1572872 | tf_op jit(solution)/shard_map/ppermute | solution.py:324
  105.2 8.1 %collective-permute-done.19.refs_4_ = bf16[224,1024]{1,0:T(8,128)(2,1)S(1)} collective-permute-done((bf16[224,1024]{1,0:T(8,128)(2,1)S(1)}, bf16[224,1024]{1,0:T(8,128)(2,1)S(1)}, u32[]{:S(2)}, u32[]{:S(2)}) %collective-permute-start.19) | collective-permute-done | bytes 458784 | tf_op jit(solution)/shard_map/ppermute | solution.py:324
  113.4 1.5 %collective-permute-start.26 = (bf16[224,1024]{1,0:T(8,128)(2,1)S(1)}, bf16[224,1024]{1,0:T(8,128)(2,1)S(1)}, u32[]{:S(2)}, u32[]{:S(2)}) collective-permute-start(bf16[224,1024]{1,0:T(8,128)(2,1)S(1)} %collective-permute-done.19.refs_4_), channel_id=1, source_target_pairs={{0,16},{1,17},{2,18},{3,19},{4,20},{5,21},{6,22},{7,23},{8,9},{9,8... | collective-permute-start | bytes 1376264 | tf_op jit(solution)/shard_map/ppermute | solution.py:324
  115.2 3.5 %collective-permute-done.23.refs_9_ = f32[8,384]{1,0:T(8,128)S(1)} collective-permute-done((f32[8,384]{1,0:T(8,128)S(1)}, f32[8,384]{1,0:T(8,128)S(1)}, u32[]{:S(2)}, u32[]{:S(2)}) %collective-permute-start.23) | collective-permute-done | bytes 12320 | tf_op jit(solution)/shard_map/ppermute | solution.py:324
  118.7 5.4 %shard_map.81 = (f32[576,512]{1,0:T(8,128)S(1)}, f32[8,384]{1,0:T(8,128)S(1)}) custom-call(bf16[8192,256]{1,0:T(8,128)(2,1)} %get-tuple-element.22.refs_0_.head, bf16[8192,256]{1,0:T(8,128)(2,1)} %collective-permute-done.2.refs_1_.sibling, f32[576,512]{1,0:T(8,128)S(1)} %get-tuple-element.34.refs_2_, ...), custom_call_target="tpu_custom_call", output_to_operand_aliasing={{0}: (2, {})} | custom-call | flops 1174405120 | tf_op jit(solution)/shard_map/pallas_call | solution.py:261
  124.7 1.3 shard_map.82.token_ids
  126.0 1.9 %collective-permute-done.24.across = f32[8,384]{1,0:T(8,128)S(1)} collective-permute-done((f32[8,384]{1,0:T(8,128)S(1)}, f32[8,384]{1,0:T(8,128)S(1)}, u32[]{:S(2)}, u32[]{:S(2)}) %collective-permute-start.24) | collective-permute-done | bytes 12320 | tf_op jit(solution)/shard_map/ppermute | solution.py:400
  127.9 5.1 %shard_map.83 = (f32[8,640]{1,0:T(8,128)S(1)}, f32[576,512]{1,0:T(8,128)S(1)}) custom-call(bf16[8192,256]{1,0:T(8,128)(2,1)} %get-tuple-element.22.refs_0_.head, bf16[8192,256]{1,0:T(8,128)(2,1)} %collective-permute-done.2.refs_1_.sibling, f32[576,512]{1,0:T(8,128)S(1)} %get-tuple-element.38.acc_in, ...), custom_call_target="tpu_custom_call", output_to_operand_aliasing={{1}: (2, {})} | custom-call | flops 301989888 | tf_op jit(solution)/shard_map/pallas_call | solution.py:261
  133.2 4.3 %collective-permute-start.30 = (f32[8,640]{1,0:T(8,128)S(1)}, f32[8,640]{1,0:T(8,128)S(1)}, u32[]{:S(2)}, u32[]{:S(2)}) collective-permute-start(f32[8,640]{1,0:T(8,128)S(1)} %get-tuple-element.39), channel_id=1, source_target_pairs={{0,6},{1,7},{2,4},{3,5},{4,2},{5,3},{6,0},{7,1},{8,14},{9,15},{10,... | collective-permute-start | bytes 61448 | tf_op jit(solution)/shard_map/ppermute | solution.py:324
  137.9 1.6 %collective-permute-done.30 = f32[8,640]{1,0:T(8,128)S(1)} collective-permute-done((f32[8,640]{1,0:T(8,128)S(1)}, f32[8,640]{1,0:T(8,128)S(1)}, u32[]{:S(2)}, u32[]{:S(2)}) %collective-permute-start.30) | collective-permute-done | bytes 20512 | tf_op jit(solution)/shard_map/ppermute | solution.py:324
  140.0 0.6 collective-permute-start.32
  140.6 2.5 %collective-permute-start.33 = (f32[8,640]{1,0:T(8,128)S(1)}, f32[8,640]{1,0:T(8,128)S(1)}, u32[]{:S(2)}, u32[]{:S(2)}) collective-permute-start(f32[8,640]{1,0:T(8,128)S(1)} %maximum_maximum_fusion), channel_id=1, source_target_pairs={{0,17},{1,16},{2,19},{3,18},{4,21},{5,20},{6,23},{7,22},{8,25},{9,... | collective-permute-start | bytes 61448 | tf_op jit(solution)/shard_map/ppermute | solution.py:324
  143.8 1.5 %collective-permute-done.33 = f32[8,640]{1,0:T(8,128)S(1)} collective-permute-done((f32[8,640]{1,0:T(8,128)S(1)}, f32[8,640]{1,0:T(8,128)S(1)}, u32[]{:S(2)}, u32[]{:S(2)}) %collective-permute-start.33) | collective-permute-done | bytes 20512 | tf_op jit(solution)/shard_map/ppermute | solution.py:324
  145.5 1.2 collective-permute-done.34
  146.6 2.2 %shard_map.84 = (f32[1,384]{1,0:T(1,128)}, f32[1,1]{1,0:T(1,128)}) custom-call(s32[4]{0:T(128)S(1)} %copy-done.4, f32[2,2,8,384]{3,2,1,0:T(8,128)S(1)} %pad_maximum_fusion.2.sums, f32[2,8,640]{2,1,0:T(8,128)S(1)} %pad_maximum_fusion.3.stats), custom_call_target="tpu_custom_call" | custom-call | tf_op jit(solution)/shard_map/pallas_call | solution.py:261
  (58 shorter events, 6.8 us)
Async XLA Ops:
  0.6 3.6 %copy-start.1 = (bf16[1,384,1024]{2,1,0:T(8,128)(2,1)S(1)}, bf16[1,384,1024]{2,1,0:T(8,128)(2,1)}, u32[]{:S(2)}) copy-start(bf16[1,384,1024]{2,1,0:T(8,128)(2,1)} %param.6) | copy-start | bytes 2359300
  0.6 3.6 %collective-permute-start = (bf16[384,1024]{1,0:T(8,128)(2,1)}, bf16[384,1024]{1,0:T(8,128)(2,1)S(1)}, u32[]{:S(2)}, u32[]{:S(2)}) collective-permute-start(bf16[384,1024]{1,0:T(8,128)(2,1)} %bitcast.16), channel_id=1, source_target_pairs={{0,8},{8,0},{16,24},{24,16},{1,9},{9,1},{17,25},{25,17},{2,10},{10... | collective-permute-start | bytes 2359304 | tf_op jit(solution)/shard_map/ppermute | solution.py:291
  2.2 2.1 %collective-permute-start.1 = (bf16[192,1024]{1,0:T(8,128)(2,1)S(1)}, bf16[192,1024]{1,0:T(8,128)(2,1)S(1)}, u32[]{:S(2)}, u32[]{:S(2)}) collective-permute-start(bf16[192,1024]{1,0:T(8,128)(2,1)S(1)} %slice_bitcast_fusion), channel_id=1, source_target_pairs={{8,24},{24,8},{9,25},{25,9},{10,26},{26,10},{11,27},{27,11},{12,28... | collective-permute-start | bytes 1179656 | tf_op jit(solution)/shard_map/ppermute | solution.py:292
  4.3 2.2 %copy-start = (bf16[8192,256]{1,0:T(8,128)(2,1)S(1)}, bf16[8192,256]{1,0:T(8,128)(2,1)}, u32[]{:S(2)}) copy-start(bf16[8192,256]{1,0:T(8,128)(2,1)} %head.1) | copy-start | bytes 12582916
  6.5 0.7 copy-start.3
  11.3 29.1 %collective-permute-start.2 = (bf16[8192,256]{1,0:T(8,128)(2,1)}, bf16[8192,256]{1,0:T(8,128)(2,1)}, u32[]{:S(2)}, u32[]{:S(2)}) collective-permute-start(bf16[8192,256]{1,0:T(8,128)(2,1)} %get-tuple-element.22.refs_0_.head), channel_id=1, source_target_pairs={{0,8},{8,0},{16,24},{24,16},{1,9},{9,1},{17,25},{25,17},{2,10},{10... | collective-permute-start | bytes 12582920 | tf_op jit(solution)/shard_map/ppermute | solution.py:307
  19.1 5.0 %collective-permute-start.6 = (bf16[64,1024]{1,0:T(8,128)(2,1)S(1)}, bf16[64,1024]{1,0:T(8,128)(2,1)S(1)}, u32[]{:S(2)}, u32[]{:S(2)}) collective-permute-start(bf16[64,1024]{1,0:T(8,128)(2,1)S(1)} %get-tuple-element.25), channel_id=1, source_target_pairs={{0,1},{1,0},{2,3},{3,2},{4,5},{5,4},{6,7},{7,6},{8,24},{9,25},{10,... | collective-permute-start | bytes 393224 | tf_op jit(solution)/shard_map/ppermute | solution.py:324
  24.1 9.2 %collective-permute-start.7 = (bf16[128,1024]{1,0:T(8,128)(2,1)S(1)}, bf16[128,1024]{1,0:T(8,128)(2,1)S(1)}, u32[]{:S(2)}, u32[]{:S(2)}) collective-permute-start(bf16[128,1024]{1,0:T(8,128)(2,1)S(1)} %pad_maximum_fusion.1), channel_id=1, source_target_pairs={{0,16},{1,17},{2,18},{3,19},{4,20},{5,21},{6,22},{7,23},{8,9},{9,8... | collective-permute-start | bytes 786440 | tf_op jit(solution)/shard_map/ppermute | solution.py:324
  25.9 12.7 %collective-permute-start.3 = (bf16[224,1024]{1,0:T(8,128)(2,1)S(1)}, bf16[224,1024]{1,0:T(8,128)(2,1)S(1)}, u32[]{:S(2)}, u32[]{:S(2)}) collective-permute-start(bf16[224,1024]{1,0:T(8,128)(2,1)S(1)} %get-tuple-element.23.refs_2_), channel_id=1, source_target_pairs={{0,1},{1,0},{2,3},{3,2},{4,5},{5,4},{6,7},{7,6},{8,24},{9,25},{10,... | collective-permute-start | bytes 1376264 | tf_op jit(solution)/shard_map/ppermute | solution.py:324
  27.4 12.7 %collective-permute-start.4 = (bf16[224,1024]{1,0:T(8,128)(2,1)S(1)}, bf16[224,1024]{1,0:T(8,128)(2,1)S(1)}, u32[]{:S(2)}, u32[]{:S(2)}) collective-permute-start(bf16[224,1024]{1,0:T(8,128)(2,1)S(1)} %get-tuple-element.23.refs_2_), channel_id=1, source_target_pairs={{0,16},{1,17},{2,18},{3,19},{4,20},{5,21},{6,22},{7,23},{8,9},{9,8... | collective-permute-start | bytes 1376264 | tf_op jit(solution)/shard_map/ppermute | solution.py:324
  27.9 12.5 %collective-permute-start.5 = (bf16[224,1024]{1,0:T(8,128)(2,1)S(1)}, bf16[224,1024]{1,0:T(8,128)(2,1)S(1)}, u32[]{:S(2)}, u32[]{:S(2)}) collective-permute-start(bf16[224,1024]{1,0:T(8,128)(2,1)S(1)} %get-tuple-element.23.refs_2_), channel_id=1, source_target_pairs={{0,2},{1,3},{2,0},{3,1},{4,6},{5,7},{6,4},{7,5},{8,10},{9,11},{10,... | collective-permute-start | bytes 1376264 | tf_op jit(solution)/shard_map/ppermute | solution.py:324
  33.4 19.9 %collective-permute-start.12 = (bf16[224,1024]{1,0:T(8,128)(2,1)S(1)}, bf16[224,1024]{1,0:T(8,128)(2,1)S(1)}, u32[]{:S(2)}, u32[]{:S(2)}) collective-permute-start(bf16[224,1024]{1,0:T(8,128)(2,1)S(1)} %get-tuple-element.23.refs_2_), channel_id=1, source_target_pairs={{0,6},{1,7},{2,4},{3,5},{4,2},{5,3},{6,0},{7,1},{8,14},{9,15},{10,... | collective-permute-start | bytes 1376264 | tf_op jit(solution)/shard_map/ppermute | solution.py:324
  44.8 27.2 %collective-permute-start.16 = (bf16[256,1024]{1,0:T(8,128)(2,1)S(1)}, bf16[256,1024]{1,0:T(8,128)(2,1)S(1)}, u32[]{:S(2)}, u32[]{:S(2)}) collective-permute-start(bf16[256,1024]{1,0:T(8,128)(2,1)S(1)} %get-tuple-element.29.refs_10_), channel_id=1, source_target_pairs={{0,2},{1,3},{2,0},{3,1},{4,6},{5,7},{6,4},{7,5},{8,10},{9,11},{10,... | collective-permute-start | bytes 1572872 | tf_op jit(solution)/shard_map/ppermute | solution.py:324
  47.4 10.7 %collective-permute-start.10 = (bf16[224,1024]{1,0:T(8,128)(2,1)S(1)}, bf16[224,1024]{1,0:T(8,128)(2,1)S(1)}, u32[]{:S(2)}, u32[]{:S(2)}) collective-permute-start(bf16[224,1024]{1,0:T(8,128)(2,1)S(1)} %collective-permute-done.3.refs_3_), channel_id=1, source_target_pairs={{0,16},{1,17},{2,18},{3,19},{4,20},{5,21},{6,22},{7,23},{8,9},{9,8... | collective-permute-start | bytes 1376264 | tf_op jit(solution)/shard_map/ppermute | solution.py:324
  48.7 13.5 %collective-permute-start.8 = (bf16[224,1024]{1,0:T(8,128)(2,1)S(1)}, bf16[224,1024]{1,0:T(8,128)(2,1)S(1)}, u32[]{:S(2)}, u32[]{:S(2)}) collective-permute-start(bf16[224,1024]{1,0:T(8,128)(2,1)S(1)} %get-tuple-element.27.refs_3_), channel_id=1, source_target_pairs={{0,1},{1,0},{2,3},{3,2},{4,5},{5,4},{6,7},{7,6},{8,24},{9,25},{10,... | collective-permute-start | bytes 1376264 | tf_op jit(solution)/shard_map/ppermute | solution.py:324
  53.3 18.6 %collective-permute-start.18 = (bf16[224,1024]{1,0:T(8,128)(2,1)S(1)}, bf16[224,1024]{1,0:T(8,128)(2,1)S(1)}, u32[]{:S(2)}, u32[]{:S(2)}) collective-permute-start(bf16[224,1024]{1,0:T(8,128)(2,1)S(1)} %collective-permute-done.12.refs_9_), channel_id=1, source_target_pairs={{0,2},{1,3},{2,0},{3,1},{4,6},{5,7},{6,4},{7,5},{8,10},{9,11},{10,... | collective-permute-start | bytes 1376264 | tf_op jit(solution)/shard_map/ppermute | solution.py:324
  53.3 18.7 %collective-permute-start.9 = (bf16[224,1024]{1,0:T(8,128)(2,1)S(1)}, bf16[224,1024]{1,0:T(8,128)(2,1)S(1)}, u32[]{:S(2)}, u32[]{:S(2)}) collective-permute-start(bf16[224,1024]{1,0:T(8,128)(2,1)S(1)} %get-tuple-element.27.refs_3_), channel_id=1, source_target_pairs={{0,16},{1,17},{2,18},{3,19},{4,20},{5,21},{6,22},{7,23},{8,9},{9,8... | collective-permute-start | bytes 1376264 | tf_op jit(solution)/shard_map/ppermute | solution.py:324
  58.1 13.9 %collective-permute-start.11 = (f32[8,384]{1,0:T(8,128)S(1)}, f32[8,384]{1,0:T(8,128)S(1)}, u32[]{:S(2)}, u32[]{:S(2)}) collective-permute-start(f32[8,384]{1,0:T(8,128)S(1)} %get-tuple-element.28.refs_7_), channel_id=1, source_target_pairs={{0,2},{1,3},{2,0},{3,1},{4,6},{5,7},{6,4},{7,5},{8,10},{9,11},{10,... | collective-permute-start | bytes 36872 | tf_op jit(solution)/shard_map/ppermute | solution.py:324
  62.2 32.2 %collective-permute-start.15 = (bf16[224,1024]{1,0:T(8,128)(2,1)S(1)}, bf16[224,1024]{1,0:T(8,128)(2,1)S(1)}, u32[]{:S(2)}, u32[]{:S(2)}) collective-permute-start(bf16[224,1024]{1,0:T(8,128)(2,1)S(1)} %collective-permute-done.8.refs_4_), channel_id=1, source_target_pairs={{0,16},{1,17},{2,18},{3,19},{4,20},{5,21},{6,22},{7,23},{8,9},{9,8... | collective-permute-start | bytes 1376264 | tf_op jit(solution)/shard_map/ppermute | solution.py:324
  76.8 17.5 %collective-permute-start.13 = (bf16[224,1024]{1,0:T(8,128)(2,1)S(1)}, bf16[224,1024]{1,0:T(8,128)(2,1)S(1)}, u32[]{:S(2)}, u32[]{:S(2)}) collective-permute-start(bf16[224,1024]{1,0:T(8,128)(2,1)S(1)} %get-tuple-element.31.refs_3_), channel_id=1, source_target_pairs={{0,1},{1,0},{2,3},{3,2},{4,5},{5,4},{6,7},{7,6},{8,24},{9,25},{10,... | collective-permute-start | bytes 1376264 | tf_op jit(solution)/shard_map/ppermute | solution.py:324
  78.3 16.0 %collective-permute-start.14 = (bf16[224,1024]{1,0:T(8,128)(2,1)S(1)}, bf16[224,1024]{1,0:T(8,128)(2,1)S(1)}, u32[]{:S(2)}, u32[]{:S(2)}) collective-permute-start(bf16[224,1024]{1,0:T(8,128)(2,1)S(1)} %get-tuple-element.31.refs_3_), channel_id=1, source_target_pairs={{0,16},{1,17},{2,18},{3,19},{4,20},{5,21},{6,22},{7,23},{8,9},{9,8... | collective-permute-start | bytes 1376264 | tf_op jit(solution)/shard_map/ppermute | solution.py:324
  78.9 15.5 %collective-permute-start.17 = (f32[8,384]{1,0:T(8,128)S(1)}, f32[8,384]{1,0:T(8,128)S(1)}, u32[]{:S(2)}, u32[]{:S(2)}) collective-permute-start(f32[8,384]{1,0:T(8,128)S(1)} %get-tuple-element.33.refs_9_), channel_id=1, source_target_pairs={{0,4},{1,5},{2,6},{3,7},{4,0},{5,1},{6,2},{7,3},{8,12},{9,13},{10,... | collective-permute-start | bytes 36872 | tf_op jit(solution)/shard_map/ppermute | solution.py:324
  79.4 22.9 %collective-permute-start.22 = (bf16[256,1024]{1,0:T(8,128)(2,1)S(1)}, bf16[256,1024]{1,0:T(8,128)(2,1)S(1)}, u32[]{:S(2)}, u32[]{:S(2)}) collective-permute-start(bf16[256,1024]{1,0:T(8,128)(2,1)S(1)} %get-tuple-element.32.refs_7_), channel_id=1, source_target_pairs={{0,6},{1,7},{2,4},{3,5},{4,2},{5,3},{6,0},{7,1},{8,14},{9,15},{10,... | collective-permute-start | bytes 1572872 | tf_op jit(solution)/shard_map/ppermute | solution.py:324
  99.9 13.5 %collective-permute-start.19 = (bf16[224,1024]{1,0:T(8,128)(2,1)S(1)}, bf16[224,1024]{1,0:T(8,128)(2,1)S(1)}, u32[]{:S(2)}, u32[]{:S(2)}) collective-permute-start(bf16[224,1024]{1,0:T(8,128)(2,1)S(1)} %get-tuple-element.35.refs_3_), channel_id=1, source_target_pairs={{0,1},{1,0},{2,3},{3,2},{4,5},{5,4},{6,7},{7,6},{8,24},{9,25},{10,... | collective-permute-start | bytes 1376264 | tf_op jit(solution)/shard_map/ppermute | solution.py:324
  100.3 18.4 %collective-permute-start.20 = (bf16[224,1024]{1,0:T(8,128)(2,1)S(1)}, bf16[224,1024]{1,0:T(8,128)(2,1)S(1)}, u32[]{:S(2)}, u32[]{:S(2)}) collective-permute-start(bf16[224,1024]{1,0:T(8,128)(2,1)S(1)} %get-tuple-element.35.refs_3_), channel_id=1, source_target_pairs={{0,16},{1,17},{2,18},{3,19},{4,20},{5,21},{6,22},{7,23},{8,9},{9,8... | collective-permute-start | bytes 1376264 | tf_op jit(solution)/shard_map/ppermute | solution.py:324
  101.8 17.0 %collective-permute-start.21 = (bf16[224,1024]{1,0:T(8,128)(2,1)S(1)}, bf16[224,1024]{1,0:T(8,128)(2,1)S(1)}, u32[]{:S(2)}, u32[]{:S(2)}) collective-permute-start(bf16[224,1024]{1,0:T(8,128)(2,1)S(1)} %collective-permute-done.13.refs_4_), channel_id=1, source_target_pairs={{0,16},{1,17},{2,18},{3,19},{4,20},{5,21},{6,22},{7,23},{8,9},{9,8... | collective-permute-start | bytes 1376264 | tf_op jit(solution)/shard_map/ppermute | solution.py:324
  102.3 25.6 %collective-permute-start.27 = (bf16[256,1024]{1,0:T(8,128)(2,1)S(1)}, bf16[256,1024]{1,0:T(8,128)(2,1)S(1)}, u32[]{:S(2)}, u32[]{:S(2)}) collective-permute-start(bf16[256,1024]{1,0:T(8,128)(2,1)S(1)} %collective-permute-done.22.refs_7_), channel_id=1, source_target_pairs={{0,2},{1,3},{2,0},{3,1},{4,6},{5,7},{6,4},{7,5},{8,10},{9,11},{10,... | collective-permute-start | bytes 1572872 | tf_op jit(solution)/shard_map/ppermute | solution.py:324
  113.4 14.5 %collective-permute-start.26 = (bf16[224,1024]{1,0:T(8,128)(2,1)S(1)}, bf16[224,1024]{1,0:T(8,128)(2,1)S(1)}, u32[]{:S(2)}, u32[]{:S(2)}) collective-permute-start(bf16[224,1024]{1,0:T(8,128)(2,1)S(1)} %collective-permute-done.19.refs_4_), channel_id=1, source_target_pairs={{0,16},{1,17},{2,18},{3,19},{4,20},{5,21},{6,22},{7,23},{8,9},{9,8... | collective-permute-start | bytes 1376264 | tf_op jit(solution)/shard_map/ppermute | solution.py:324
  114.9 3.8 %collective-permute-start.23 = (f32[8,384]{1,0:T(8,128)S(1)}, f32[8,384]{1,0:T(8,128)S(1)}, u32[]{:S(2)}, u32[]{:S(2)}) collective-permute-start(f32[8,384]{1,0:T(8,128)S(1)} %get-tuple-element.36.refs_8_), channel_id=1, source_target_pairs={{0,1},{1,0},{2,3},{3,2},{4,5},{5,4},{6,7},{7,6},{8,9},{9,8},{10,11... | collective-permute-start | bytes 36872 | tf_op jit(solution)/shard_map/ppermute | solution.py:324
  118.7 6.0 %copy-start.2 = (s32[4,384]{1,0:T(4,128)S(1)}, s32[4,384]{1,0:T(4,128)}, u32[]{:S(2)}) copy-start(s32[4,384]{1,0:T(4,128)} %tokens.1) | copy-start | bytes 18436
  118.7 6.0 %copy-start.4 = (s32[4]{0:T(128)S(1)}, s32[4]{0:T(128)}, u32[]{:S(2)}) copy-start(s32[4]{0:T(128)} %lengths.5) | copy-start | bytes 52
  124.1 3.8 %collective-permute-start.24 = (f32[8,384]{1,0:T(8,128)S(1)}, f32[8,384]{1,0:T(8,128)S(1)}, u32[]{:S(2)}, u32[]{:S(2)}) collective-permute-start(f32[8,384]{1,0:T(8,128)S(1)} %get-tuple-element.37.sums), channel_id=1, source_target_pairs={{0,16},{8,24},{16,0},{24,8},{1,17},{9,25},{17,1},{25,9},{2,18},{10... | collective-permute-start | bytes 36872 | tf_op jit(solution)/shard_map/ppermute | solution.py:400
  133.1 4.4 %collective-permute-start.28 = (f32[8,640]{1,0:T(8,128)S(1)}, f32[8,640]{1,0:T(8,128)S(1)}, u32[]{:S(2)}, u32[]{:S(2)}) collective-permute-start(f32[8,640]{1,0:T(8,128)S(1)} %get-tuple-element.39), channel_id=1, source_target_pairs={{0,2},{1,3},{2,0},{3,1},{4,6},{5,7},{6,4},{7,5},{8,10},{9,11},{10,... | collective-permute-start | bytes 61448 | tf_op jit(solution)/shard_map/ppermute | solution.py:324
  133.1 4.7 %collective-permute-start.29 = (f32[8,640]{1,0:T(8,128)S(1)}, f32[8,640]{1,0:T(8,128)S(1)}, u32[]{:S(2)}, u32[]{:S(2)}) collective-permute-start(f32[8,640]{1,0:T(8,128)S(1)} %get-tuple-element.39), channel_id=1, source_target_pairs={{0,4},{1,5},{2,6},{3,7},{4,0},{5,1},{6,2},{7,3},{8,12},{9,13},{10,... | collective-permute-start | bytes 61448 | tf_op jit(solution)/shard_map/ppermute | solution.py:324
  133.2 6.3 %collective-permute-start.30 = (f32[8,640]{1,0:T(8,128)S(1)}, f32[8,640]{1,0:T(8,128)S(1)}, u32[]{:S(2)}, u32[]{:S(2)}) collective-permute-start(f32[8,640]{1,0:T(8,128)S(1)} %get-tuple-element.39), channel_id=1, source_target_pairs={{0,6},{1,7},{2,4},{3,5},{4,2},{5,3},{6,0},{7,1},{8,14},{9,15},{10,... | collective-permute-start | bytes 61448 | tf_op jit(solution)/shard_map/ppermute | solution.py:324
  137.5 5.6 %collective-permute-start.25 = (f32[2,8,384]{2,1,0:T(8,128)S(1)}, f32[2,8,384]{2,1,0:T(8,128)S(1)}, u32[]{:S(2)}, u32[]{:S(2)}) collective-permute-start(f32[2,8,384]{2,1,0:T(8,128)S(1)} %pad_maximum_fusion.4), channel_id=1, source_target_pairs={{0,8},{8,0},{16,24},{24,16},{1,9},{9,1},{17,25},{25,17},{2,10},{10... | collective-permute-start | bytes 73736 | tf_op jit(solution)/shard_map/ppermute | solution.py:434
  139.6 3.8 %collective-permute-start.31 = (f32[8,640]{1,0:T(8,128)S(1)}, f32[8,640]{1,0:T(8,128)S(1)}, u32[]{:S(2)}, u32[]{:S(2)}) collective-permute-start(f32[8,640]{1,0:T(8,128)S(1)} %maximum_maximum_fusion), channel_id=1, source_target_pairs={{0,1},{1,0},{2,3},{3,2},{4,5},{5,4},{6,7},{7,6},{8,9},{9,8},{10,11... | collective-permute-start | bytes 61448 | tf_op jit(solution)/shard_map/ppermute | solution.py:324
  140.0 3.8 %collective-permute-start.32 = (f32[8,640]{1,0:T(8,128)S(1)}, f32[8,640]{1,0:T(8,128)S(1)}, u32[]{:S(2)}, u32[]{:S(2)}) collective-permute-start(f32[8,640]{1,0:T(8,128)S(1)} %maximum_maximum_fusion), channel_id=1, source_target_pairs={{0,16},{1,17},{2,18},{3,19},{4,20},{5,21},{6,22},{7,23},{8,24},{9,... | collective-permute-start | bytes 61448 | tf_op jit(solution)/shard_map/ppermute | solution.py:324
  140.6 4.7 %collective-permute-start.33 = (f32[8,640]{1,0:T(8,128)S(1)}, f32[8,640]{1,0:T(8,128)S(1)}, u32[]{:S(2)}, u32[]{:S(2)}) collective-permute-start(f32[8,640]{1,0:T(8,128)S(1)} %maximum_maximum_fusion), channel_id=1, source_target_pairs={{0,17},{1,16},{2,19},{3,18},{4,21},{5,20},{6,23},{7,22},{8,25},{9,... | collective-permute-start | bytes 61448 | tf_op jit(solution)/shard_map/ppermute | solution.py:324
  145.4 1.3 collective-permute-start.34

commit v4 on v2

v4 whole, which is shorter than its diff:
```python
import functools

import jax
import jax.numpy as jnp
from jax import lax
from jax.experimental import pallas as pl
from jax.experimental.pallas import tpu as pltpu
from jax.sharding import PartitionSpec as P

AXES = ("section", "dp")
F32 = jnp.float32
BF16 = jnp.bfloat16
I32 = jnp.int32
LANES = 128
VMEM = pl.BlockSpec(memory_space=pltpu.VMEM)
SMEM = pl.BlockSpec(memory_space=pltpu.SMEM)
ANY = pl.BlockSpec(memory_space=pl.ANY)
HBM = pl.BlockSpec(memory_space=pltpu.HBM)


def row_map(lengths, pair, core, index, count):
    first, second = lengths[2 * pair], lengths[2 * pair + 1]
    other_first = lengths[2 - 2 * pair]
    j = core * count + index
    in_first = j < first
    in_second = j < first + second
    span = jnp.where(in_first, 2 * pair, jnp.where(in_second, 2 * pair + 1, 3 - 2 * pair))
    place = jnp.where(
        in_first, j, jnp.where(in_second, j - first, 2 * count - other_first + j - first - second)
    )
    return span, place


def as_rows(columns, count):
    lane = lax.broadcasted_iota(I32, (count, LANES), 1)
    wide = jnp.zeros((count, LANES), F32)
    for i, column in enumerate(columns):
        wide = jnp.where(lane == i, column, wide)
    return jnp.transpose(wide)[:8]


def as_column(rows, which):
    full = jnp.concatenate([rows, jnp.zeros((LANES - 8, rows.shape[1]), F32)], axis=0)
    return jnp.transpose(full)[:, which : which + 1]


def pick_kernel(count, lengths, rows, sibling, extra, gain, reward, head, full, big, partial, head_out, sem):
    copy = pltpu.make_async_copy(head, head_out, sem)
    copy.start()
    section = lax.axis_index("section")
    core, pair = lax.rem(section, 2), lax.div(section, 2)
    positions, half = rows.shape[0], extra.shape[0]
    index = lax.broadcasted_iota(I32, (count, 1), 0)
    span, place = row_map(lengths, pair, core, index, count)
    source = jnp.where(span == section, place, place + positions)
    source = jnp.where(span // 2 == pair, source, place + (2 * positions - (positions - half)))
    lane = lax.broadcasted_iota(I32, (count, 2 * positions + half), 1)
    pick = jnp.where(lane == source, F32(1.0), F32(0.0)).astype(BF16)
    picked = jnp.dot(pick[:, :positions], rows[...], preferred_element_type=F32)
    picked += jnp.dot(pick[:, positions : 2 * positions], sibling[...], preferred_element_type=F32)
    picked += jnp.dot(pick[:, 2 * positions :], extra[...], preferred_element_type=F32)
    scaled = (picked * gain[...].astype(F32)).astype(BF16)
    full[...] = scaled
    big[...] = scaled[: big.shape[0]]
    squares = jnp.sum(picked * picked, axis=1, keepdims=True)
    rewards = jnp.sum(scaled.astype(F32) * reward[...].astype(F32), axis=1, keepdims=True)
    padded = partial.shape[1]
    zeros = jnp.zeros((padded - count, 1), F32)
    partial[...] = as_rows(
        [jnp.concatenate([squares, zeros]), jnp.concatenate([rewards, zeros])], padded
    )
    copy.wait()


def token_kernel(count, lengths, tokens, out):
    core = lax.rem(lax.axis_index("section"), 2)
    spans, positions = tokens.shape
    for pair in range(2):
        index = lax.broadcasted_iota(I32, (count, 1), 0)
        span, place = row_map(lengths, pair, core, index, count)
        lane = lax.broadcasted_iota(I32, (count, positions), 1)
        ids = jnp.zeros((count, 1), F32)
        for s in range(spans):
            hit = (lane == place) & (span == s)
            ids += jnp.sum(jnp.where(hit, tokens[s : s + 1, :].astype(F32), F32(0.0)), axis=1, keepdims=True)
        out[pair * count : pair * count + count, :] = ids.astype(I32)


def here():
    section = lax.axis_index("section")
    return section, lax.rem(section, 2), lax.div(section, 2)


def blocks(count):
    _, _, pair = here()
    return pl.multiple_of(pair * count, 16), pl.multiple_of((1 - pair) * count, 16)


def weights(head, sibling, depth, k, far):
    dp_index = lax.axis_index("dp")
    where = jnp.bitwise_xor(dp_index, 2 * k + (1 if far else 0))
    rows = pl.ds(pl.multiple_of(where * depth, depth), depth)
    return head[rows, :], sibling[rows, :]


def products(terms):
    value = jnp.concatenate([t[0] for t in terms], axis=1) if len(terms) > 1 else terms[0][0]
    out = []
    for side in range(2):
        w = [t[1][side] for t in terms]
        w = jnp.concatenate(w, axis=0) if len(w) > 1 else w[0]
        out.append(jnp.dot(value, w, preferred_element_type=F32))
    return jnp.concatenate(out, axis=1)


def small_terms(w, head, sibling, k):
    m2 = w.shape[0] // 2
    depth = w.shape[1]
    return products(
        [(w[:m2, :], weights(head, sibling, depth, k, False)), (w[m2:, :], weights(head, sibling, depth, k, True))]
    )


def first_kernel(n, head, sibling, z, a, b, c, sums, z1, z3, acc, sums_out, w0, z1_out, z3_out):
    count, depth = z.shape
    m = count - n
    _, core, _ = here()
    mine, others = blocks(count)
    near = weights(head, sibling, depth, 0, False)
    far = weights(head, sibling, depth, 0, True)
    w0[:m, :] = z[n:, :]
    w0[3 * m :, :] = c[n:, :]
    for which, same, cross in ((0, a, b), (1, b, a)):

        @pl.when(core == which)
        def _():
            acc[pl.ds(mine, count), :] = products([(z[...], near), (same[...], far)])
            acc[pl.ds(others, count), :] = products([(cross[...], near), (c[...], far)])
            w0[m : 2 * m, :] = cross[n:, :]
            w0[2 * m : 3 * m, :] = same[n:, :]

    sums_out[...] = sums[...]
    z1_out[...] = z1[...]
    z3_out[...] = z3[...]


def stage_kernel(k, n_small, n_pass, *refs):
    refs = list(refs)
    head, sibling, acc_in, z, a, b, c, sums, received = refs[:9]
    smalls = refs[9 : 9 + n_small]
    passed = refs[9 + n_small : 9 + n_small + n_pass]
    acc, sums_out = refs[9 + n_small + n_pass : 11 + n_small + n_pass]
    outs = refs[11 + n_small + n_pass :]
    n, depth = z.shape
    count = acc.shape[0] // 2
    m = count - n
    _, core, _ = here()
    mine, others = blocks(count)
    near = weights(head, sibling, depth, k, False)
    far = weights(head, sibling, depth, k, True)
    for which, same, cross in ((0, a, b), (1, b, a)):

        @pl.when(core == which)
        def _():
            rows = pl.ds(mine, n)
            acc[rows, :] = acc_in[rows, :] + products([(z[...], near), (same[...], far)])
            rows = pl.ds(others, n)
            acc[rows, :] = acc_in[rows, :] + products([(cross[...], near), (c[...], far)])

    for i, base in enumerate((mine, others)):
        rows = pl.ds(pl.multiple_of(base + n, 16), m)
        value = acc_in[rows, :]
        acc[rows, :] = value
    for w, w_k in zip(smalls, (1, 3)):
        value = small_terms(w, head, sibling, w_k)
        for i, base in enumerate((mine, others)):
            rows = pl.ds(pl.multiple_of(base + n, 16), m)
            acc[rows, :] = acc[rows, :] + value[i * m : (i + 1) * m]
    sums_out[...] = sums[...] + received[...]
    for out, value in zip(outs, passed):
        out[...] = value[...]


def gate_kernel(value, after, out):
    out[...] = value[...]


def column_ids(block):
    section, core, _ = here()
    dp_index, groups = lax.axis_index("dp"), lax.axis_size("dp")
    lane = lax.broadcasted_iota(I32, (1, block), 1)
    own = (section * groups + dp_index) * block
    other = ((section + 1 - 2 * core) * groups + dp_index) * block
    return jnp.concatenate([lane + own, lane + other], axis=1)


def summary(logits, squares, token_ids, ids, width):
    logits = logits * lax.rsqrt(squares / width + 1e-05)
    top = jnp.max(logits, axis=1, keepdims=True)
    total = jnp.sum(jnp.exp(logits - top), axis=1, keepdims=True)
    target = jnp.sum(jnp.where(ids == token_ids, logits, F32(0.0)), axis=1, keepdims=True)
    lane = lax.broadcasted_iota(I32, (logits.shape[0], LANES), 1)
    return jnp.where(lane == 0, top, jnp.where(lane == 1, total, jnp.where(lane == 2, target, F32(0.0))))


def own_kernel(k, width, head, sibling, acc_in, z, a, b, w, sums, received, token_ids, acc, sums_out, own):
    n, depth = z.shape
    count = acc_in.shape[0] // 2
    m = count - n
    _, core, _ = here()
    mine, others = blocks(count)
    near = weights(head, sibling, depth, k, False)
    far = weights(head, sibling, depth, k, True)
    total = sums[...] + received[...]
    sums_out[...] = total
    scale = as_column(total, 0)
    ids = column_ids(head.shape[1])
    for which, same, cross in ((0, a, b), (1, b, a)):

        @pl.when(core == which)
        def _():
            rows = pl.ds(mine, n)
            logits = acc_in[rows, :] + products([(z[...], near), (same[...], far)])
            own[...] = summary(logits, scale[:n], token_ids[rows, :], ids, width)
            acc[:n, :] = acc_in[pl.ds(others, n), :] + products([(cross[...], near)])

    value = small_terms(w, head, sibling, 3)
    for i, base in enumerate((mine, others)):
        rows = pl.ds(pl.multiple_of(base + n, 16), m)
        acc[n + i * m : n + (i + 1) * m, :] = acc_in[rows, :] + value[i * m : (i + 1) * m]


def last_kernel(k, width, head, sibling, acc, c, w, own, sums, across, token_ids, out, wide):
    n, depth = c.shape
    count = token_ids.shape[0] // 2
    m = count - n
    mine, others = blocks(count)
    ids = column_ids(head.shape[1])
    scale, scale_across = as_column(sums[...], 0), as_column(across[...], 0)
    wide[2 * count :, :] = jnp.zeros((wide.shape[0] - 2 * count, LANES), F32)
    wide[pl.ds(mine, n), :] = own[...]
    logits = acc[:n, :] + products([(c[...], weights(head, sibling, depth, k, True))])
    rows = pl.ds(others, n)
    wide[rows, :] = summary(logits, scale_across[:n], token_ids[rows, :], ids, width)
    value = acc[n:, :] + small_terms(w, head, sibling, k)
    for i, (base, squares) in enumerate(((mine, scale), (others, scale_across))):
        rows = pl.ds(pl.multiple_of(base + n, 16), m)
        wide[rows, :] = summary(value[i * m : (i + 1) * m], squares[n:count], token_ids[rows, :], ids, width)
    out[...] = jnp.transpose(wide[...])[:8]


def whole_kernel(width, acc, sums, token_ids, out):
    count = acc.shape[0] // 2
    ids = column_ids(acc.shape[1] // 2)
    squares = jnp.concatenate([as_column(sums[0], 0)[:count], as_column(sums[1], 0)[:count]])
    wide = summary(acc[...], squares, token_ids[...], ids, width)
    wide = jnp.concatenate([wide, jnp.zeros((out.shape[1] - 2 * count, LANES), F32)])
    out[...] = jnp.transpose(wide)[:8]


def final_kernel(count, width, lengths, sums, stats, out_ref, score_ref):
    section = lax.axis_index("section")
    positions = out_ref.shape[1]
    where = lax.broadcasted_iota(I32, (1, positions), 1)
    logprob = jnp.zeros((1, positions), F32)
    score = jnp.zeros((1, 1), F32)
    index = lax.broadcasted_iota(I32, (count, 1), 0)
    for core in range(2):
        s = stats[core]
        lp = as_column(s, 0)
        for pair in range(2):
            value = lp[pair * count : pair * count + count]
            span, place = row_map(lengths, pair, core, index, count)
            hit = (place == where) & (span == section)
            logprob += jnp.sum(jnp.where(hit, value, F32(0.0)), axis=0, keepdims=True)
            columns = jnp.transpose(
                jnp.concatenate([sums[core, pair], jnp.zeros((LANES - 8, sums.shape[3]), F32)], axis=0)
            )[:count]
            reward = columns[:, 1:2] * lax.rsqrt(columns[:, 0:1] / width + 1e-05)
            score += jnp.sum(jnp.where(span == section, reward, F32(0.0)), axis=0, keepdims=True)
    out_ref[...] = logprob
    score_ref[...] = score / lengths[section].astype(F32)


def combine(parts):
    top = parts[0][0]
    for part in parts[1:]:
        top = jnp.maximum(top, part[0])
    total = sum(part[1] * jnp.exp(part[0] - top) for part in parts)
    target = sum(part[2] for part in parts)
    return jnp.concatenate([jnp.stack([top, total, target]), jnp.zeros((5,) + top.shape, F32)])


def call(body, outs, in_specs, args, limit=16, scratch=()):
    many = isinstance(outs, (list, tuple))
    return pl.pallas_call(
        body,
        out_shape=outs,
        in_specs=in_specs,
        out_specs=[VMEM] * len(outs) if many else VMEM,
        scratch_shapes=scratch,
        compiler_params=pltpu.CompilerParams(vmem_limit_bytes=limit << 20),
    )(*args)


def up(value):
    return -(-value // LANES) * LANES


def per_device(groups, hidden, norm_gain, head, reward_head, tokens, lengths):
    section = lax.axis_index("section")
    core, pair = section % 2, section // 2
    sections = lax.axis_size("section")
    spans, positions = tokens.shape
    block, width, part = head.shape[1], head.shape[0], hidden.shape[2]
    count = 3 * spans * positions // 4 // sections
    half = positions // 2
    big = (count * 7 // 9) // 16 * 16
    small = count - big
    rows = hidden[0]

    swap = [(s, s ^ 1) for s in range(sections)]
    over = [(s, s ^ 2) for s in range(sections)]
    sibling = lax.ppermute(rows, "section", swap)
    extra = lax.ppermute(rows[half:], "section", [(1, 3), (3, 1)])

    full, g, partial, head = call(
        functools.partial(pick_kernel, count),
        [
            jax.ShapeDtypeStruct((count, part), BF16),
            jax.ShapeDtypeStruct((big, part), BF16),
            jax.ShapeDtypeStruct((8, up(count)), F32),
            jax.ShapeDtypeStruct(head.shape, BF16),
        ],
        [SMEM] + [VMEM] * 5 + [HBM],
        (lengths, rows, sibling, extra, norm_gain[None], reward_head[None], head),
        scratch=[pltpu.SemaphoreType.DMA],
    )
    head_sibling = lax.ppermute(head, "section", swap)
    token_ids = call(
        functools.partial(token_kernel, count), jax.ShapeDtypeStruct((2 * count, 1), I32), [SMEM, VMEM], (lengths, tokens)
    )

    def mesh_perm(move):
        pairs = []
        for s in range(sections):
            for d in range(groups):
                s2, d2 = move(s, d)
                pairs.append((s * groups + d, s2 * groups + d2))
        return pairs

    send = lambda value, perm: lax.ppermute(value, AXES, perm)
    like = lambda v: jax.ShapeDtypeStruct(v.shape, v.dtype)
    acc_shape = jax.ShapeDtypeStruct((2 * count, 2 * block), F32)
    stats_shape = jax.ShapeDtypeStruct((8, up(2 * count)), F32)
    if groups == 8:
        perm_a = mesh_perm(lambda s, d: (s, d ^ 1) if s % 2 == 0 else (s ^ 2, d))
        perm_b = mesh_perm(lambda s, d: (s ^ 2, d) if s % 2 == 0 else (s, d ^ 1))
        perm_x = mesh_perm(lambda s, d: (s, d ^ 1))
        perm_z = {k: mesh_perm(lambda s, d, k=k: (s, d ^ (2 * k))) for k in (1, 2, 3)}

        def gate(value, after):
            return call(gate_kernel, like(value), [VMEM, ANY], (value, after))

        def stage(k, acc, pieces, sums, received, smalls, passed):
            args = (head, head_sibling, acc) + pieces + (sums, received) + smalls + passed
            return call(
                functools.partial(stage_kernel, k, len(smalls), len(passed)),
                [acc_shape, like(sums)] + [like(p) for p in passed],
                [VMEM] * len(args),
                args,
            )

        z1 = send(g, perm_z[1])
        z3 = send(g, perm_z[3])
        a0 = send(full, perm_a)
        b0 = send(full, perm_b)
        c0 = send(a0, perm_b)
        z1 = gate(z1, b0)
        a1 = send(z1, perm_a)
        acc, sums, w0, z1, z3 = call(
            functools.partial(first_kernel, big),
            [acc_shape, like(partial), jax.ShapeDtypeStruct((4 * small, part), BF16), like(z1), like(z3)],
            [VMEM] * 9,
            (head, head_sibling, full, a0, b0, c0, partial, z1, z3),
        )
        received = send(sums, perm_z[1])
        b1 = send(z1, perm_b)
        z2 = send(z3, perm_z[1])
        w3 = send(w0, perm_z[3])
        c1 = send(a1, perm_b)
        z3 = gate(z3, b1)
        a3 = send(z3, perm_a)
        acc, sums, z3, w0 = stage(1, acc, (z1, a1, b1, c1), sums, received, (), (z3, w0))
        received = send(sums, perm_z[2])
        b3 = send(z3, perm_b)
        w1 = send(w0, perm_z[1])
        c3 = send(a3, perm_b)
        z2 = gate(z2, b3)
        a2 = send(z2, perm_a)
        acc, sums, z2, w3 = stage(3, acc, (z3, a3, b3, c3), sums, received, (w1,), (z2, w3))
        received = send(sums, perm_x)
        b2 = send(z2, perm_b)
        w2 = send(w3, perm_z[1])
        c2 = send(a2, perm_b)
        acc, sums, own = call(
            functools.partial(own_kernel, 2, width),
            [jax.ShapeDtypeStruct((big + 2 * small, 2 * block), F32), like(sums), jax.ShapeDtypeStruct((big, LANES), F32)],
            [VMEM] * 10,
            (head, head_sibling, acc, z2, a2, b2, w3, sums, received, token_ids),
        )
        across = lax.ppermute(sums, "section", over)
        stats = call(
            functools.partial(last_kernel, 2, width),
            stats_shape,
            [VMEM] * 9,
            (head, head_sibling, acc, c2, w2, own, sums, across, token_ids),
            scratch=[pltpu.VMEM((up(2 * count), LANES), F32)],
        )
        stats = combine([stats] + [send(stats, perm_z[k]) for k in (1, 2, 3)])
        stats = combine(
            [stats]
            + [send(stats, mesh_perm(lambda s, d, v=v: (s ^ v[0], d ^ v[1]))) for v in ((0, 1), (2, 0), (2, 1))]
        )
    else:
        sums = lax.psum(partial, "dp")
        across = lax.ppermute(sums, "section", over)
    all_sums = jnp.stack([jnp.where(pair == 0, sums, across), jnp.where(pair == 0, across, sums)])
    if groups != 8:
        other = lax.ppermute(full, "section", over)
        ordered = jnp.concatenate([jnp.where(pair == 0, full, other), jnp.where(pair == 0, other, full)])
        everything = lax.all_gather(ordered, "dp", axis=1, tiled=True)
        acc = jnp.concatenate(
            [jnp.dot(everything, h, preferred_element_type=F32) for h in (head, head_sibling)], axis=1
        )
        stats = call(functools.partial(whole_kernel, width), stats_shape, [VMEM] * 3, (acc, all_sums, token_ids))
        gathered = lax.all_gather(stats, "dp")
        stats = combine([gathered[i] for i in range(groups)])
        stats = combine([stats, lax.ppermute(stats, "section", over)])
    lp = stats[2:3] - (stats[0:1] + jnp.log(stats[1:2]))
    lp = jnp.concatenate([lp, jnp.zeros((7, lp.shape[1]), F32)])
    both = lambda v, u: jnp.stack([jnp.where(core == 0, v, u), jnp.where(core == 0, u, v)])
    all_sums = both(all_sums, lax.ppermute(all_sums, "section", swap))
    stats = both(lp, lax.ppermute(lp, "section", swap))
    logprob, score = call(
        functools.partial(final_kernel, count, width),
        [jax.ShapeDtypeStruct((1, positions), F32), jax.ShapeDtypeStruct((1, 1), F32)],
        [SMEM, VMEM, VMEM],
        (lengths, all_sums, stats),
    )
    return (logprob, score[0])


def solution(mesh):
    groups = mesh.shape["dp"]
    return jax.shard_map(
        lambda *args: per_device(groups, *args),
        mesh=mesh,
        in_specs=(P("section", None, "dp"), P("dp"), P(None, ("section", "dp")), P("dp"), P(), P()),
        out_specs=(P("section", None), P("section")),
        check_vma=False,
    )
```

time: 148 us -> 141 us (0.953)
  Pallas kernels: 25.2 us -> 13.3 us
  waiting for transfers between devices: 55.1 us -> 58.3 us
    pallas_call x8 -> x11, Pallas kernels: 25.2 us -> 13.3 us  [call(): pl.pallas_call(body, out_shape=outs, in_specs=in_specs, out_specs=[VMEM]...]
    ppermute x1, starting transfers between devices: 0.52 us -> 7.8 us  [per_device(): head_sibling = lax.ppermute(head, 'section', swap)]
    ppermute x29 -> x27, waiting for transfers between devices: 47.6 us -> 53.9 us  [per_device(): send = lambda value, perm: lax.ppermute(value, AXES, perm)]
    ppermute x29 -> x27, starting transfers between devices: 53.2 us -> 47.3 us  [per_device(): send = lambda value, perm: lax.ppermute(value, AXES, perm)]
    ppermute x1, waiting for transfers between devices: 4.52 us -> 0.01 us  [per_device(): sibling = lax.ppermute(rows, 'section', swap)]
    unnamed x24 -> x18, local copies, waits for them, and re-layouts: 7.4 us -> 8.35 us
  transfers between devices with their start and end apart: 35 -> 33, of which waited for: 17 -> 17; matrix products, arithmetic and copies ran while one was open for 2% -> 2% of each run, Pallas kernels for 13% -> 6%
where the time goes in v4:
time: 141 us
  waiting for transfers between devices  58.3 us (41%)
  starting transfers between devices  57.4 us (41%)
  Pallas kernels  13.3 us (9%)
  local copies, waits for them, and re-layouts  10.8 us (8%)
    ppermute x27, waiting for transfers between devices, per_device(): send = lambda value, perm: lax.ppermute(value, AXES, perm)  53.9 us
    ppermute x27, starting transfers between devices, per_device(): send = lambda value, perm: lax.ppermute(value, AXES, perm)  47.3 us
    pallas_call x11, Pallas kernels, call(): pl.pallas_call(body, out_shape=outs, in_specs=in_specs, out_specs=[VMEM]...  13.3 us
    unnamed x18, local copies, waits for them, and re-layouts  8.35 us
    ppermute x1, starting transfers between devices, per_device(): head_sibling = lax.ppermute(head, 'section', swap)  7.8 us
    ppermute x1, waiting for transfers between devices, per_device(): across = lax.ppermute(sums, 'section', over)  3.23 us
  transfers between devices with their start and end apart: 33, of which 17 were waited for; matrix products, arithmetic and copies ran while one was open for 2% of the time, Pallas kernels for 6%

profile of v4, /device:TPU:0, one launch (start us, length us, event | category | flops | bytes accessed | tf_op | source)
XLA Modules:
  0.0 140.8 jit_solution(3208079146409112555)
XLA Ops:
  1.1 1.0 slice_bitcast_fusion
  2.2 0.7 collective-permute-start.1
  2.9 0.7 broadcast_in_dim.10.gain
  4.3 2.2 %copy-done.4 = bf16[8192,256]{1,0:T(8,128)(2,1)S(1)} copy-done((bf16[8192,256]{1,0:T(8,128)(2,1)S(1)}, bf16[8192,256]{1,0:T(8,128)(2,1)}, u32[]{:S(2)}) %copy-start.4) | copy-done | bytes 4194328
  6.4 1.1 copy-done.5
  8.2 2.2 %shard_map.77 = (bf16[288,1024]{1,0:T(8,128)(2,1)S(1)}, bf16[224,1024]{1,0:T(8,128)(2,1)S(1)}, f32[8,384]{1,0:T(8,128)S(1)}, bf16[8192,256]{1,0:T(8,128)(2,1)S(1)}) custom-call(s32[4]{0:T(128)S(1)} %copy-done.7, bf16[384,1024]{1,0:T(8,128)(2,1)S(1)} %bitcast.17, bf16[384,1024]{1,0:T(8,128)(2,1)S(1)} %collective-permute-done.sibling, ...), custom_call_target="tpu_custom_call" | custom-call | tf_op jit(solution)/shard_map/pallas_call | solution.py:296
  10.5 7.8 %collective-permute-start.2 = (bf16[8192,256]{1,0:T(8,128)(2,1)S(1)}, bf16[8192,256]{1,0:T(8,128)(2,1)S(1)}, u32[]{:S(2)}, u32[]{:S(2)}) collective-permute-start(bf16[8192,256]{1,0:T(8,128)(2,1)S(1)} %get-tuple-element.24.head.refs_0_), channel_id=1, source_target_pairs={{0,8},{8,0},{16,24},{24,16},{1,9},{9,1},{17,25},{25,17},{2,10},{10... | collective-permute-start | bytes 12582920 | tf_op jit(solution)/shard_map/ppermute | solution.py:339
  18.3 1.7 %collective-permute-start.3 = (bf16[288,1024]{1,0:T(8,128)(2,1)S(1)}, bf16[288,1024]{1,0:T(8,128)(2,1)S(1)}, u32[]{:S(2)}, u32[]{:S(2)}) collective-permute-start(bf16[288,1024]{1,0:T(8,128)(2,1)S(1)} %get-tuple-element.25.z), channel_id=1, source_target_pairs={{0,1},{1,0},{2,3},{3,2},{4,5},{5,4},{6,7},{7,6},{8,24},{9,25},{10,... | collective-permute-start | bytes 1769480 | tf_op jit(solution)/shard_map/ppermute | solution.py:352
  20.0 1.5 %collective-permute-start.4 = (bf16[288,1024]{1,0:T(8,128)(2,1)S(1)}, bf16[288,1024]{1,0:T(8,128)(2,1)S(1)}, u32[]{:S(2)}, u32[]{:S(2)}) collective-permute-start(bf16[288,1024]{1,0:T(8,128)(2,1)S(1)} %get-tuple-element.25.z), channel_id=1, source_target_pairs={{0,16},{1,17},{2,18},{3,19},{4,20},{5,21},{6,22},{7,23},{8,9},{9,8... | collective-permute-start | bytes 1769480 | tf_op jit(solution)/shard_map/ppermute | solution.py:352
  21.5 1.6 %collective-permute-start.6 = (bf16[224,1024]{1,0:T(8,128)(2,1)S(1)}, bf16[224,1024]{1,0:T(8,128)(2,1)S(1)}, u32[]{:S(2)}, u32[]{:S(2)}) collective-permute-start(bf16[224,1024]{1,0:T(8,128)(2,1)S(1)} %get-tuple-element.27), channel_id=1, source_target_pairs={{0,2},{1,3},{2,0},{3,1},{4,6},{5,7},{6,4},{7,5},{8,10},{9,11},{10,... | collective-permute-start | bytes 1376264 | tf_op jit(solution)/shard_map/ppermute | solution.py:352
  23.1 10.9 %collective-permute-done.3.a = bf16[288,1024]{1,0:T(8,128)(2,1)S(1)} collective-permute-done((bf16[288,1024]{1,0:T(8,128)(2,1)S(1)}, bf16[288,1024]{1,0:T(8,128)(2,1)S(1)}, u32[]{:S(2)}, u32[]{:S(2)}) %collective-permute-start.3) | collective-permute-done | bytes 589856 | tf_op jit(solution)/shard_map/ppermute | solution.py:352
  34.0 1.4 collective-permute-start.5
  35.4 3.8 %collective-permute-start.7 = (bf16[224,1024]{1,0:T(8,128)(2,1)S(1)}, bf16[224,1024]{1,0:T(8,128)(2,1)S(1)}, u32[]{:S(2)}, u32[]{:S(2)}) collective-permute-start(bf16[224,1024]{1,0:T(8,128)(2,1)S(1)} %get-tuple-element.27), channel_id=1, source_target_pairs={{0,6},{1,7},{2,4},{3,5},{4,2},{5,3},{6,0},{7,1},{8,14},{9,15},{10,... | collective-permute-start | bytes 1376264 | tf_op jit(solution)/shard_map/ppermute | solution.py:352
  39.2 1.5 %collective-permute-start.8 = (bf16[224,1024]{1,0:T(8,128)(2,1)S(1)}, bf16[224,1024]{1,0:T(8,128)(2,1)S(1)}, u32[]{:S(2)}, u32[]{:S(2)}) collective-permute-start(bf16[224,1024]{1,0:T(8,128)(2,1)S(1)} %shard_map.78.z1), channel_id=1, source_target_pairs={{0,1},{1,0},{2,3},{3,2},{4,5},{5,4},{6,7},{7,6},{8,24},{9,25},{10,... | collective-permute-start | bytes 1376264 | tf_op jit(solution)/shard_map/ppermute | solution.py:352
  40.8 7.5 %collective-permute-done.7.z3 = bf16[224,1024]{1,0:T(8,128)(2,1)S(1)} collective-permute-done((bf16[224,1024]{1,0:T(8,128)(2,1)S(1)}, bf16[224,1024]{1,0:T(8,128)(2,1)S(1)}, u32[]{:S(2)}, u32[]{:S(2)}) %collective-permute-start.7) | collective-permute-done | bytes 458784 | tf_op jit(solution)/shard_map/ppermute | solution.py:352
  48.2 1.6 %shard_map.79 = (f32[576,512]{1,0:T(8,128)S(1)}, f32[8,384]{1,0:T(8,128)S(1)}, bf16[256,1024]{1,0:T(8,128)(2,1)S(1)}, bf16[224,1024]{1,0:T(8,128)(2,1)S(1)}, bf16[224,1024]{1,0:T(8,128)(2,1)S(1)}) custom-call(bf16[8192,256]{1,0:T(8,128)(2,1)S(1)} %get-tuple-element.24.head.refs_0_, bf16[8192,256]{1,0:T(8,128)(2,1)S(1)} %collective-permute-done.2.sibling.refs_1_, ...), custom_call_target="tpu_custom_call" | custom-call | tf_op jit(solution)/shard_map/pallas_call | solution.py:296
  49.9 1.4 collective-permute-start.9
  51.3 0.7 collective-permute-start.10
  52.0 6.8 %collective-permute-done.9.after.refs_5_ = bf16[224,1024]{1,0:T(8,128)(2,1)S(1)} collective-permute-done((bf16[224,1024]{1,0:T(8,128)(2,1)S(1)}, bf16[224,1024]{1,0:T(8,128)(2,1)S(1)}, u32[]{:S(2)}, u32[]{:S(2)}) %collective-permute-start.9) | collective-permute-done | bytes 458784 | tf_op jit(solution)/shard_map/ppermute | solution.py:352
  58.8 4.8 %collective-permute-start.12 = (bf16[224,1024]{1,0:T(8,128)(2,1)S(1)}, bf16[224,1024]{1,0:T(8,128)(2,1)S(1)}, u32[]{:S(2)}, u32[]{:S(2)}) collective-permute-start(bf16[224,1024]{1,0:T(8,128)(2,1)S(1)} %shard_map.80.refs_9_), channel_id=1, source_target_pairs={{0,1},{1,0},{2,3},{3,2},{4,5},{5,4},{6,7},{7,6},{8,24},{9,25},{10,... | collective-permute-start | bytes 1376264 | tf_op jit(solution)/shard_map/ppermute | solution.py:352
  63.6 4.5 %collective-permute-start.11 = (f32[8,384]{1,0:T(8,128)S(1)}, f32[8,384]{1,0:T(8,128)S(1)}, u32[]{:S(2)}, u32[]{:S(2)}) collective-permute-start(f32[8,384]{1,0:T(8,128)S(1)} %get-tuple-element.30.refs_7_), channel_id=1, source_target_pairs={{0,2},{1,3},{2,0},{3,1},{4,6},{5,7},{6,4},{7,5},{8,10},{9,11},{10,... | collective-permute-start | bytes 36872 | tf_op jit(solution)/shard_map/ppermute | solution.py:352
  68.2 1.6 %collective-permute-done.11.refs_8_ = f32[8,384]{1,0:T(8,128)S(1)} collective-permute-done((f32[8,384]{1,0:T(8,128)S(1)}, f32[8,384]{1,0:T(8,128)S(1)}, u32[]{:S(2)}, u32[]{:S(2)}) %collective-permute-start.11) | collective-permute-done | bytes 12320 | tf_op jit(solution)/shard_map/ppermute | solution.py:352
  69.8 1.4 shard_map.81
  71.2 1.6 %collective-permute-start.13 = (bf16[224,1024]{1,0:T(8,128)(2,1)S(1)}, bf16[224,1024]{1,0:T(8,128)(2,1)S(1)}, u32[]{:S(2)}, u32[]{:S(2)}) collective-permute-start(bf16[224,1024]{1,0:T(8,128)(2,1)S(1)} %get-tuple-element.34.refs_3_), channel_id=1, source_target_pairs={{0,16},{1,17},{2,18},{3,19},{4,20},{5,21},{6,22},{7,23},{8,9},{9,8... | collective-permute-start | bytes 1376264 | tf_op jit(solution)/shard_map/ppermute | solution.py:352
  72.8 2.5 %collective-permute-start.18 = (bf16[256,1024]{1,0:T(8,128)(2,1)S(1)}, bf16[256,1024]{1,0:T(8,128)(2,1)S(1)}, u32[]{:S(2)}, u32[]{:S(2)}) collective-permute-start(bf16[256,1024]{1,0:T(8,128)(2,1)S(1)} %get-tuple-element.32.refs_10_), channel_id=1, source_target_pairs={{0,6},{1,7},{2,4},{3,5},{4,2},{5,3},{6,0},{7,1},{8,14},{9,15},{10,... | collective-permute-start | bytes 1572872 | tf_op jit(solution)/shard_map/ppermute | solution.py:352
  75.4 6.6 %collective-permute-start.16 = (bf16[256,1024]{1,0:T(8,128)(2,1)S(1)}, bf16[256,1024]{1,0:T(8,128)(2,1)S(1)}, u32[]{:S(2)}, u32[]{:S(2)}) collective-permute-start(bf16[256,1024]{1,0:T(8,128)(2,1)S(1)} %get-tuple-element.36), channel_id=1, source_target_pairs={{0,2},{1,3},{2,0},{3,1},{4,6},{5,7},{6,4},{7,5},{8,10},{9,11},{10,... | collective-permute-start | bytes 1572872 | tf_op jit(solution)/shard_map/ppermute | solution.py:352
  82.5 9.7 %collective-permute-done.17.value = bf16[224,1024]{1,0:T(8,128)(2,1)S(1)} collective-permute-done((bf16[224,1024]{1,0:T(8,128)(2,1)S(1)}, bf16[224,1024]{1,0:T(8,128)(2,1)S(1)}, u32[]{:S(2)}, u32[]{:S(2)}) %collective-permute-start.17) | collective-permute-done | bytes 458784 | tf_op jit(solution)/shard_map/ppermute | solution.py:352
  92.2 2.4 %collective-permute-start.19 = (bf16[224,1024]{1,0:T(8,128)(2,1)S(1)}, bf16[224,1024]{1,0:T(8,128)(2,1)S(1)}, u32[]{:S(2)}, u32[]{:S(2)}) collective-permute-start(bf16[224,1024]{1,0:T(8,128)(2,1)S(1)} %shard_map.82.refs_10_), channel_id=1, source_target_pairs={{0,1},{1,0},{2,3},{3,2},{4,5},{5,4},{6,7},{7,6},{8,24},{9,25},{10,... | collective-permute-start | bytes 1376264 | tf_op jit(solution)/shard_map/ppermute | solution.py:352
  94.6 5.7 %collective-permute-done.15.refs_8_ = f32[8,384]{1,0:T(8,128)S(1)} collective-permute-done((f32[8,384]{1,0:T(8,128)S(1)}, f32[8,384]{1,0:T(8,128)S(1)}, u32[]{:S(2)}, u32[]{:S(2)}) %collective-permute-start.15) | collective-permute-done | bytes 12320 | tf_op jit(solution)/shard_map/ppermute | solution.py:352
  100.3 2.0 %collective-permute-done.16.refs_9_ = bf16[256,1024]{1,0:T(8,128)(2,1)S(1)} collective-permute-done((bf16[256,1024]{1,0:T(8,128)(2,1)S(1)}, bf16[256,1024]{1,0:T(8,128)(2,1)S(1)}, u32[]{:S(2)}, u32[]{:S(2)}) %collective-permute-start.16) | collective-permute-done | bytes 524320 | tf_op jit(solution)/shard_map/ppermute | solution.py:352
  102.3 1.8 %shard_map.83 = (f32[576,512]{1,0:T(8,128)S(1)}, f32[8,384]{1,0:T(8,128)S(1)}, bf16[224,1024]{1,0:T(8,128)(2,1)S(1)}, bf16[256,1024]{1,0:T(8,128)(2,1)S(1)}) custom-call(bf16[8192,256]{1,0:T(8,128)(2,1)S(1)} %get-tuple-element.24.head.refs_0_, bf16[8192,256]{1,0:T(8,128)(2,1)S(1)} %collective-permute-done.2.sibling.refs_1_, ...), custom_call_target="tpu_custom_call" | custom-call | tf_op jit(solution)/shard_map/pallas_call | solution.py:296
  105.1 1.5 %collective-permute-start.24 = (bf16[224,1024]{1,0:T(8,128)(2,1)S(1)}, bf16[224,1024]{1,0:T(8,128)(2,1)S(1)}, u32[]{:S(2)}, u32[]{:S(2)}) collective-permute-start(bf16[224,1024]{1,0:T(8,128)(2,1)S(1)} %collective-permute-done.19.a), channel_id=1, source_target_pairs={{0,16},{1,17},{2,18},{3,19},{4,20},{5,21},{6,22},{7,23},{8,9},{9,8... | collective-permute-start | bytes 1376264 | tf_op jit(solution)/shard_map/ppermute | solution.py:352
  106.9 1.3 shard_map.84.token_ids
  108.2 2.3 %collective-permute-done.21.received = f32[8,384]{1,0:T(8,128)S(1)} collective-permute-done((f32[8,384]{1,0:T(8,128)S(1)}, f32[8,384]{1,0:T(8,128)S(1)}, u32[]{:S(2)}, u32[]{:S(2)}) %collective-permute-start.21) | collective-permute-done | bytes 12320 | tf_op jit(solution)/shard_map/ppermute | solution.py:352
  110.5 2.1 %collective-permute-done.20.b = bf16[224,1024]{1,0:T(8,128)(2,1)S(1)} collective-permute-done((bf16[224,1024]{1,0:T(8,128)(2,1)S(1)}, bf16[224,1024]{1,0:T(8,128)(2,1)S(1)}, u32[]{:S(2)}, u32[]{:S(2)}) %collective-permute-start.20) | collective-permute-done | bytes 458784 | tf_op jit(solution)/shard_map/ppermute | solution.py:352
  112.6 1.7 %shard_map.85 = (f32[352,512]{1,0:T(8,128)S(1)}, f32[8,384]{1,0:T(8,128)S(1)}, f32[224,128]{1,0:T(8,128)S(1)}) custom-call(bf16[8192,256]{1,0:T(8,128)(2,1)S(1)} %get-tuple-element.24.head.refs_0_, bf16[8192,256]{1,0:T(8,128)(2,1)S(1)} %collective-permute-done.2.sibling.refs_1_, f32[576,512]{1,0:T(8,128)S(1)} %get-tuple-element.37.acc_in, ...), custom_call_target="tpu_custom_call" | custom-call | tf_op jit(solution)/shard_map/pallas_call | solution.py:296
  114.9 3.2 %collective-permute-done.22.across = f32[8,384]{1,0:T(8,128)S(1)} collective-permute-done((f32[8,384]{1,0:T(8,128)S(1)}, f32[8,384]{1,0:T(8,128)S(1)}, u32[]{:S(2)}, u32[]{:S(2)}) %collective-permute-start.22) | collective-permute-done | bytes 12320 | tf_op jit(solution)/shard_map/ppermute | solution.py:412
  118.1 2.2 %copy-done.1 = bf16[8192,256]{1,0:T(8,128)(2,1)S(1)} copy-done((bf16[8192,256]{1,0:T(8,128)(2,1)S(1)}, bf16[8192,256]{1,0:T(8,128)(2,1)}, u32[]{:S(2)}) %copy-start.1) | copy-done | bytes 4194328
  120.3 2.2 %copy-done.3 = bf16[8192,256]{1,0:T(8,128)(2,1)S(1)} copy-done((bf16[8192,256]{1,0:T(8,128)(2,1)S(1)}, bf16[8192,256]{1,0:T(8,128)(2,1)}, u32[]{:S(2)}) %copy-start.3) | copy-done | bytes 4194328
  122.5 1.0 shard_map.86
  124.0 1.5 %collective-permute-start.27 = (f32[8,640]{1,0:T(8,128)S(1)}, f32[8,640]{1,0:T(8,128)S(1)}, u32[]{:S(2)}, u32[]{:S(2)}) collective-permute-start(f32[8,640]{1,0:T(8,128)S(1)} %shard_map.86), channel_id=1, source_target_pairs={{0,4},{1,5},{2,6},{3,7},{4,0},{5,1},{6,2},{7,3},{8,12},{9,13},{10,... | collective-permute-start | bytes 61448 | tf_op jit(solution)/shard_map/ppermute | solution.py:352
  125.5 2.4 %collective-permute-start.28 = (f32[8,640]{1,0:T(8,128)S(1)}, f32[8,640]{1,0:T(8,128)S(1)}, u32[]{:S(2)}, u32[]{:S(2)}) collective-permute-start(f32[8,640]{1,0:T(8,128)S(1)} %shard_map.86), channel_id=1, source_target_pairs={{0,6},{1,7},{2,4},{3,5},{4,2},{5,3},{6,0},{7,1},{8,14},{9,15},{10,... | collective-permute-start | bytes 61448 | tf_op jit(solution)/shard_map/ppermute | solution.py:352
  128.8 2.3 %collective-permute-done.28 = f32[8,640]{1,0:T(8,128)S(1)} collective-permute-done((f32[8,640]{1,0:T(8,128)S(1)}, f32[8,640]{1,0:T(8,128)S(1)}, u32[]{:S(2)}, u32[]{:S(2)}) %collective-permute-start.28) | collective-permute-done | bytes 20512 | tf_op jit(solution)/shard_map/ppermute | solution.py:352
  131.5 1.1 collective-permute-start.30
  132.6 2.1 %collective-permute-start.31 = (f32[8,640]{1,0:T(8,128)S(1)}, f32[8,640]{1,0:T(8,128)S(1)}, u32[]{:S(2)}, u32[]{:S(2)}) collective-permute-start(f32[8,640]{1,0:T(8,128)S(1)} %maximum_maximum_fusion), channel_id=1, source_target_pairs={{0,17},{1,16},{2,19},{3,18},{4,21},{5,20},{6,23},{7,22},{8,25},{9,... | collective-permute-start | bytes 61448 | tf_op jit(solution)/shard_map/ppermute | solution.py:352
  135.3 2.0 %collective-permute-done.31 = f32[8,640]{1,0:T(8,128)S(1)} collective-permute-done((f32[8,640]{1,0:T(8,128)S(1)}, f32[8,640]{1,0:T(8,128)S(1)}, u32[]{:S(2)}, u32[]{:S(2)}) %collective-permute-start.31) | collective-permute-done | bytes 20512 | tf_op jit(solution)/shard_map/ppermute | solution.py:352
  137.4 1.2 collective-permute-done.32
  138.6 2.2 %shard_map.87 = (f32[1,384]{1,0:T(1,128)}, f32[1,1]{1,0:T(1,128)}) custom-call(s32[4]{0:T(128)S(1)} %copy-done.8, f32[2,2,8,384]{3,2,1,0:T(8,128)S(1)} %pad_maximum_fusion.sums, f32[2,8,640]{2,1,0:T(8,128)S(1)} %pad_maximum_fusion.1.stats), custom_call_target="tpu_custom_call" | custom-call | tf_op jit(solution)/shard_map/pallas_call | solution.py:296
  (62 shorter events, 7.0 us)
Async XLA Ops:
  0.6 3.6 %collective-permute-start = (bf16[384,1024]{1,0:T(8,128)(2,1)}, bf16[384,1024]{1,0:T(8,128)(2,1)S(1)}, u32[]{:S(2)}, u32[]{:S(2)}) collective-permute-start(bf16[384,1024]{1,0:T(8,128)(2,1)} %bitcast.16), channel_id=1, source_target_pairs={{0,8},{8,0},{16,24},{24,16},{1,9},{9,1},{17,25},{25,17},{2,10},{10... | collective-permute-start | bytes 2359304 | tf_op jit(solution)/shard_map/ppermute | solution.py:324
  2.2 2.1 %collective-permute-start.1 = (bf16[192,1024]{1,0:T(8,128)(2,1)S(1)}, bf16[192,1024]{1,0:T(8,128)(2,1)S(1)}, u32[]{:S(2)}, u32[]{:S(2)}) collective-permute-start(bf16[192,1024]{1,0:T(8,128)(2,1)S(1)} %slice_bitcast_fusion), channel_id=1, source_target_pairs={{8,24},{24,8},{9,25},{25,9},{10,26},{26,10},{11,27},{27,11},{12,28... | collective-permute-start | bytes 1179656 | tf_op jit(solution)/shard_map/ppermute | solution.py:325
  4.2 2.2 %copy-start.4 = (bf16[8192,256]{1,0:T(8,128)(2,1)S(1)}, bf16[8192,256]{1,0:T(8,128)(2,1)}, u32[]{:S(2)}) copy-start(bf16[8192,256]{1,0:T(8,128)(2,1)} %head.1) | copy-start | bytes 12582916
  6.4 1.1 copy-start.5
  7.6 0.7 copy-start.7
  10.5 102.1 %copy-start = (bf16[8192,256]{1,0:T(8,128)(2,1)}, bf16[8192,256]{1,0:T(8,128)(2,1)S(1)}, u32[]{:S(2)}) copy-start(bf16[8192,256]{1,0:T(8,128)(2,1)S(1)} %get-tuple-element.24.head.refs_0_) | copy-start | bytes 12582916
  10.5 37.7 %collective-permute-start.2 = (bf16[8192,256]{1,0:T(8,128)(2,1)S(1)}, bf16[8192,256]{1,0:T(8,128)(2,1)S(1)}, u32[]{:S(2)}, u32[]{:S(2)}) collective-permute-start(bf16[8192,256]{1,0:T(8,128)(2,1)S(1)} %get-tuple-element.24.head.refs_0_), channel_id=1, source_target_pairs={{0,8},{8,0},{16,24},{24,16},{1,9},{9,1},{17,25},{25,17},{2,10},{10... | collective-permute-start | bytes 12582920 | tf_op jit(solution)/shard_map/ppermute | solution.py:339
  18.3 15.7 %collective-permute-start.3 = (bf16[288,1024]{1,0:T(8,128)(2,1)S(1)}, bf16[288,1024]{1,0:T(8,128)(2,1)S(1)}, u32[]{:S(2)}, u32[]{:S(2)}) collective-permute-start(bf16[288,1024]{1,0:T(8,128)(2,1)S(1)} %get-tuple-element.25.z), channel_id=1, source_target_pairs={{0,1},{1,0},{2,3},{3,2},{4,5},{5,4},{6,7},{7,6},{8,24},{9,25},{10,... | collective-permute-start | bytes 1769480 | tf_op jit(solution)/shard_map/ppermute | solution.py:352
  20.0 19.2 %collective-permute-start.4 = (bf16[288,1024]{1,0:T(8,128)(2,1)S(1)}, bf16[288,1024]{1,0:T(8,128)(2,1)S(1)}, u32[]{:S(2)}, u32[]{:S(2)}) collective-permute-start(bf16[288,1024]{1,0:T(8,128)(2,1)S(1)} %get-tuple-element.25.z), channel_id=1, source_target_pairs={{0,16},{1,17},{2,18},{3,19},{4,20},{5,21},{6,22},{7,23},{8,9},{9,8... | collective-permute-start | bytes 1769480 | tf_op jit(solution)/shard_map/ppermute | solution.py:352
  21.5 17.7 %collective-permute-start.6 = (bf16[224,1024]{1,0:T(8,128)(2,1)S(1)}, bf16[224,1024]{1,0:T(8,128)(2,1)S(1)}, u32[]{:S(2)}, u32[]{:S(2)}) collective-permute-start(bf16[224,1024]{1,0:T(8,128)(2,1)S(1)} %get-tuple-element.27), channel_id=1, source_target_pairs={{0,2},{1,3},{2,0},{3,1},{4,6},{5,7},{6,4},{7,5},{8,10},{9,11},{10,... | collective-permute-start | bytes 1376264 | tf_op jit(solution)/shard_map/ppermute | solution.py:352
  34.0 14.2 %collective-permute-start.5 = (bf16[288,1024]{1,0:T(8,128)(2,1)S(1)}, bf16[288,1024]{1,0:T(8,128)(2,1)S(1)}, u32[]{:S(2)}, u32[]{:S(2)}) collective-permute-start(bf16[288,1024]{1,0:T(8,128)(2,1)S(1)} %collective-permute-done.3.a), channel_id=1, source_target_pairs={{0,16},{1,17},{2,18},{3,19},{4,20},{5,21},{6,22},{7,23},{8,9},{9,8... | collective-permute-start | bytes 1769480 | tf_op jit(solution)/shard_map/ppermute | solution.py:352
  35.4 12.8 %collective-permute-start.7 = (bf16[224,1024]{1,0:T(8,128)(2,1)S(1)}, bf16[224,1024]{1,0:T(8,128)(2,1)S(1)}, u32[]{:S(2)}, u32[]{:S(2)}) collective-permute-start(bf16[224,1024]{1,0:T(8,128)(2,1)S(1)} %get-tuple-element.27), channel_id=1, source_target_pairs={{0,6},{1,7},{2,4},{3,5},{4,2},{5,3},{6,0},{7,1},{8,14},{9,15},{10,... | collective-permute-start | bytes 1376264 | tf_op jit(solution)/shard_map/ppermute | solution.py:352
  39.2 12.1 %collective-permute-start.8 = (bf16[224,1024]{1,0:T(8,128)(2,1)S(1)}, bf16[224,1024]{1,0:T(8,128)(2,1)S(1)}, u32[]{:S(2)}, u32[]{:S(2)}) collective-permute-start(bf16[224,1024]{1,0:T(8,128)(2,1)S(1)} %shard_map.78.z1), channel_id=1, source_target_pairs={{0,1},{1,0},{2,3},{3,2},{4,5},{5,4},{6,7},{7,6},{8,24},{9,25},{10,... | collective-permute-start | bytes 1376264 | tf_op jit(solution)/shard_map/ppermute | solution.py:352
  48.2 64.4 %copy-start.2 = (bf16[8192,256]{1,0:T(8,128)(2,1)}, bf16[8192,256]{1,0:T(8,128)(2,1)S(1)}, u32[]{:S(2)}) copy-start(bf16[8192,256]{1,0:T(8,128)(2,1)S(1)} %collective-permute-done.2.sibling.refs_1_) | copy-start | bytes 12582916
  49.9 8.9 %collective-permute-start.9 = (bf16[224,1024]{1,0:T(8,128)(2,1)S(1)}, bf16[224,1024]{1,0:T(8,128)(2,1)S(1)}, u32[]{:S(2)}, u32[]{:S(2)}) collective-permute-start(bf16[224,1024]{1,0:T(8,128)(2,1)S(1)} %get-tuple-element.29.refs_3_), channel_id=1, source_target_pairs={{0,16},{1,17},{2,18},{3,19},{4,20},{5,21},{6,22},{7,23},{8,9},{9,8... | collective-permute-start | bytes 1376264 | tf_op jit(solution)/shard_map/ppermute | solution.py:352
  51.3 17.0 %collective-permute-start.10 = (bf16[224,1024]{1,0:T(8,128)(2,1)S(1)}, bf16[224,1024]{1,0:T(8,128)(2,1)S(1)}, u32[]{:S(2)}, u32[]{:S(2)}) collective-permute-start(bf16[224,1024]{1,0:T(8,128)(2,1)S(1)} %collective-permute-done.8.refs_4_), channel_id=1, source_target_pairs={{0,16},{1,17},{2,18},{3,19},{4,20},{5,21},{6,22},{7,23},{8,9},{9,8... | collective-permute-start | bytes 1376264 | tf_op jit(solution)/shard_map/ppermute | solution.py:352
  58.8 23.2 %collective-permute-start.12 = (bf16[224,1024]{1,0:T(8,128)(2,1)S(1)}, bf16[224,1024]{1,0:T(8,128)(2,1)S(1)}, u32[]{:S(2)}, u32[]{:S(2)}) collective-permute-start(bf16[224,1024]{1,0:T(8,128)(2,1)S(1)} %shard_map.80.refs_9_), channel_id=1, source_target_pairs={{0,1},{1,0},{2,3},{3,2},{4,5},{5,4},{6,7},{7,6},{8,24},{9,25},{10,... | collective-permute-start | bytes 1376264 | tf_op jit(solution)/shard_map/ppermute | solution.py:352
  63.6 6.2 %collective-permute-start.11 = (f32[8,384]{1,0:T(8,128)S(1)}, f32[8,384]{1,0:T(8,128)S(1)}, u32[]{:S(2)}, u32[]{:S(2)}) collective-permute-start(f32[8,384]{1,0:T(8,128)S(1)} %get-tuple-element.30.refs_7_), channel_id=1, source_target_pairs={{0,2},{1,3},{2,0},{3,1},{4,6},{5,7},{6,4},{7,5},{8,10},{9,11},{10,... | collective-permute-start | bytes 36872 | tf_op jit(solution)/shard_map/ppermute | solution.py:352
  68.0 24.2 %collective-permute-start.17 = (bf16[224,1024]{1,0:T(8,128)(2,1)S(1)}, bf16[224,1024]{1,0:T(8,128)(2,1)S(1)}, u32[]{:S(2)}, u32[]{:S(2)}) collective-permute-start(bf16[224,1024]{1,0:T(8,128)(2,1)S(1)} %get-tuple-element.31.value), channel_id=1, source_target_pairs={{0,2},{1,3},{2,0},{3,1},{4,6},{5,7},{6,4},{7,5},{8,10},{9,11},{10,... | collective-permute-start | bytes 1376264 | tf_op jit(solution)/shard_map/ppermute | solution.py:352
  71.2 21.0 %collective-permute-start.13 = (bf16[224,1024]{1,0:T(8,128)(2,1)S(1)}, bf16[224,1024]{1,0:T(8,128)(2,1)S(1)}, u32[]{:S(2)}, u32[]{:S(2)}) collective-permute-start(bf16[224,1024]{1,0:T(8,128)(2,1)S(1)} %get-tuple-element.34.refs_3_), channel_id=1, source_target_pairs={{0,16},{1,17},{2,18},{3,19},{4,20},{5,21},{6,22},{7,23},{8,9},{9,8... | collective-permute-start | bytes 1376264 | tf_op jit(solution)/shard_map/ppermute | solution.py:352
  72.8 27.5 %collective-permute-start.18 = (bf16[256,1024]{1,0:T(8,128)(2,1)S(1)}, bf16[256,1024]{1,0:T(8,128)(2,1)S(1)}, u32[]{:S(2)}, u32[]{:S(2)}) collective-permute-start(bf16[256,1024]{1,0:T(8,128)(2,1)S(1)} %get-tuple-element.32.refs_10_), channel_id=1, source_target_pairs={{0,6},{1,7},{2,4},{3,5},{4,2},{5,3},{6,0},{7,1},{8,14},{9,15},{10,... | collective-permute-start | bytes 1572872 | tf_op jit(solution)/shard_map/ppermute | solution.py:352
  75.4 26.9 %collective-permute-start.16 = (bf16[256,1024]{1,0:T(8,128)(2,1)S(1)}, bf16[256,1024]{1,0:T(8,128)(2,1)S(1)}, u32[]{:S(2)}, u32[]{:S(2)}) collective-permute-start(bf16[256,1024]{1,0:T(8,128)(2,1)S(1)} %get-tuple-element.36), channel_id=1, source_target_pairs={{0,2},{1,3},{2,0},{3,1},{4,6},{5,7},{6,4},{7,5},{8,10},{9,11},{10,... | collective-permute-start | bytes 1572872 | tf_op jit(solution)/shard_map/ppermute | solution.py:352
  82.0 20.3 %collective-permute-start.14 = (bf16[224,1024]{1,0:T(8,128)(2,1)S(1)}, bf16[224,1024]{1,0:T(8,128)(2,1)S(1)}, u32[]{:S(2)}, u32[]{:S(2)}) collective-permute-start(bf16[224,1024]{1,0:T(8,128)(2,1)S(1)} %collective-permute-done.12.refs_4_), channel_id=1, source_target_pairs={{0,16},{1,17},{2,18},{3,19},{4,20},{5,21},{6,22},{7,23},{8,9},{9,8... | collective-permute-start | bytes 1376264 | tf_op jit(solution)/shard_map/ppermute | solution.py:352
  92.2 12.8 %collective-permute-start.19 = (bf16[224,1024]{1,0:T(8,128)(2,1)S(1)}, bf16[224,1024]{1,0:T(8,128)(2,1)S(1)}, u32[]{:S(2)}, u32[]{:S(2)}) collective-permute-start(bf16[224,1024]{1,0:T(8,128)(2,1)S(1)} %shard_map.82.refs_10_), channel_id=1, source_target_pairs={{0,1},{1,0},{2,3},{3,2},{4,5},{5,4},{6,7},{7,6},{8,24},{9,25},{10,... | collective-permute-start | bytes 1376264 | tf_op jit(solution)/shard_map/ppermute | solution.py:352
  94.6 5.7 %collective-permute-start.15 = (f32[8,384]{1,0:T(8,128)S(1)}, f32[8,384]{1,0:T(8,128)S(1)}, u32[]{:S(2)}, u32[]{:S(2)}) collective-permute-start(f32[8,384]{1,0:T(8,128)S(1)} %get-tuple-element.35.refs_7_), channel_id=1, source_target_pairs={{0,4},{1,5},{2,6},{3,7},{4,0},{5,1},{6,2},{7,3},{8,12},{9,13},{10,... | collective-permute-start | bytes 36872 | tf_op jit(solution)/shard_map/ppermute | solution.py:352
  102.3 4.6 %copy-start.6 = (s32[4,384]{1,0:T(4,128)S(1)}, s32[4,384]{1,0:T(4,128)}, u32[]{:S(2)}) copy-start(s32[4,384]{1,0:T(4,128)} %tokens.1) | copy-start | bytes 18436
  102.3 4.6 %copy-start.8 = (s32[4]{0:T(128)S(1)}, s32[4]{0:T(128)}, u32[]{:S(2)}) copy-start(s32[4]{0:T(128)} %lengths.5) | copy-start | bytes 52
  104.1 8.5 %collective-permute-start.20 = (bf16[224,1024]{1,0:T(8,128)(2,1)S(1)}, bf16[224,1024]{1,0:T(8,128)(2,1)S(1)}, u32[]{:S(2)}, u32[]{:S(2)}) collective-permute-start(bf16[224,1024]{1,0:T(8,128)(2,1)S(1)} %get-tuple-element.38.z), channel_id=1, source_target_pairs={{0,16},{1,17},{2,18},{3,19},{4,20},{5,21},{6,22},{7,23},{8,9},{9,8... | collective-permute-start | bytes 1376264 | tf_op jit(solution)/shard_map/ppermute | solution.py:352
  104.5 13.6 %collective-permute-start.25 = (bf16[256,1024]{1,0:T(8,128)(2,1)S(1)}, bf16[256,1024]{1,0:T(8,128)(2,1)S(1)}, u32[]{:S(2)}, u32[]{:S(2)}) collective-permute-start(bf16[256,1024]{1,0:T(8,128)(2,1)S(1)} %get-tuple-element.39.w), channel_id=1, source_target_pairs={{0,2},{1,3},{2,0},{3,1},{4,6},{5,7},{6,4},{7,5},{8,10},{9,11},{10,... | collective-permute-start | bytes 1572872 | tf_op jit(solution)/shard_map/ppermute | solution.py:352
  105.1 13.0 %collective-permute-start.24 = (bf16[224,1024]{1,0:T(8,128)(2,1)S(1)}, bf16[224,1024]{1,0:T(8,128)(2,1)S(1)}, u32[]{:S(2)}, u32[]{:S(2)}) collective-permute-start(bf16[224,1024]{1,0:T(8,128)(2,1)S(1)} %collective-permute-done.19.a), channel_id=1, source_target_pairs={{0,16},{1,17},{2,18},{3,19},{4,20},{5,21},{6,22},{7,23},{8,9},{9,8... | collective-permute-start | bytes 1376264 | tf_op jit(solution)/shard_map/ppermute | solution.py:352
  106.6 3.9 %collective-permute-start.21 = (f32[8,384]{1,0:T(8,128)S(1)}, f32[8,384]{1,0:T(8,128)S(1)}, u32[]{:S(2)}, u32[]{:S(2)}) collective-permute-start(f32[8,384]{1,0:T(8,128)S(1)} %get-tuple-element.40.sums), channel_id=1, source_target_pairs={{0,1},{1,0},{2,3},{3,2},{4,5},{5,4},{6,7},{7,6},{8,9},{9,8},{10,11... | collective-permute-start | bytes 36872 | tf_op jit(solution)/shard_map/ppermute | solution.py:352
  114.3 3.8 %collective-permute-start.22 = (f32[8,384]{1,0:T(8,128)S(1)}, f32[8,384]{1,0:T(8,128)S(1)}, u32[]{:S(2)}, u32[]{:S(2)}) collective-permute-start(f32[8,384]{1,0:T(8,128)S(1)} %get-tuple-element.41.sums), channel_id=1, source_target_pairs={{0,16},{8,24},{16,0},{24,8},{1,17},{9,25},{17,1},{25,9},{2,18},{10... | collective-permute-start | bytes 36872 | tf_op jit(solution)/shard_map/ppermute | solution.py:412
  118.1 2.2 %copy-start.1 = (bf16[8192,256]{1,0:T(8,128)(2,1)S(1)}, bf16[8192,256]{1,0:T(8,128)(2,1)}, u32[]{:S(2)}) copy-start(bf16[8192,256]{1,0:T(8,128)(2,1)} %copy-done) | copy-start | bytes 12582916
  120.3 2.2 %copy-start.3 = (bf16[8192,256]{1,0:T(8,128)(2,1)S(1)}, bf16[8192,256]{1,0:T(8,128)(2,1)}, u32[]{:S(2)}) copy-start(bf16[8192,256]{1,0:T(8,128)(2,1)} %copy-done.2) | copy-start | bytes 12582916
  123.5 5.0 %collective-permute-start.26 = (f32[8,640]{1,0:T(8,128)S(1)}, f32[8,640]{1,0:T(8,128)S(1)}, u32[]{:S(2)}, u32[]{:S(2)}) collective-permute-start(f32[8,640]{1,0:T(8,128)S(1)} %shard_map.86), channel_id=1, source_target_pairs={{0,2},{1,3},{2,0},{3,1},{4,6},{5,7},{6,4},{7,5},{8,10},{9,11},{10,... | collective-permute-start | bytes 61448 | tf_op jit(solution)/shard_map/ppermute | solution.py:352
  124.0 4.8 %collective-permute-start.27 = (f32[8,640]{1,0:T(8,128)S(1)}, f32[8,640]{1,0:T(8,128)S(1)}, u32[]{:S(2)}, u32[]{:S(2)}) collective-permute-start(f32[8,640]{1,0:T(8,128)S(1)} %shard_map.86), channel_id=1, source_target_pairs={{0,4},{1,5},{2,6},{3,7},{4,0},{5,1},{6,2},{7,3},{8,12},{9,13},{10,... | collective-permute-start | bytes 61448 | tf_op jit(solution)/shard_map/ppermute | solution.py:352
  125.5 5.6 %collective-permute-start.28 = (f32[8,640]{1,0:T(8,128)S(1)}, f32[8,640]{1,0:T(8,128)S(1)}, u32[]{:S(2)}, u32[]{:S(2)}) collective-permute-start(f32[8,640]{1,0:T(8,128)S(1)} %shard_map.86), channel_id=1, source_target_pairs={{0,6},{1,7},{2,4},{3,5},{4,2},{5,3},{6,0},{7,1},{8,14},{9,15},{10,... | collective-permute-start | bytes 61448 | tf_op jit(solution)/shard_map/ppermute | solution.py:352
  127.9 6.8 %collective-permute-start.23 = (f32[2,8,384]{2,1,0:T(8,128)S(1)}, f32[2,8,384]{2,1,0:T(8,128)S(1)}, u32[]{:S(2)}, u32[]{:S(2)}) collective-permute-start(f32[2,8,384]{2,1,0:T(8,128)S(1)} %pad_maximum_fusion.2), channel_id=1, source_target_pairs={{0,8},{8,0},{16,24},{24,16},{1,9},{9,1},{17,25},{25,17},{2,10},{10... | collective-permute-start | bytes 73736 | tf_op jit(solution)/shard_map/ppermute | solution.py:443
  131.2 3.8 %collective-permute-start.29 = (f32[8,640]{1,0:T(8,128)S(1)}, f32[8,640]{1,0:T(8,128)S(1)}, u32[]{:S(2)}, u32[]{:S(2)}) collective-permute-start(f32[8,640]{1,0:T(8,128)S(1)} %maximum_maximum_fusion), channel_id=1, source_target_pairs={{0,1},{1,0},{2,3},{3,2},{4,5},{5,4},{6,7},{7,6},{8,9},{9,8},{10,11... | collective-permute-start | bytes 61448 | tf_op jit(solution)/shard_map/ppermute | solution.py:352
  131.5 3.8 %collective-permute-start.30 = (f32[8,640]{1,0:T(8,128)S(1)}, f32[8,640]{1,0:T(8,128)S(1)}, u32[]{:S(2)}, u32[]{:S(2)}) collective-permute-start(f32[8,640]{1,0:T(8,128)S(1)} %maximum_maximum_fusion), channel_id=1, source_target_pairs={{0,16},{1,17},{2,18},{3,19},{4,20},{5,21},{6,22},{7,23},{8,24},{9,... | collective-permute-start | bytes 61448 | tf_op jit(solution)/shard_map/ppermute | solution.py:352
  132.6 4.7 %collective-permute-start.31 = (f32[8,640]{1,0:T(8,128)S(1)}, f32[8,640]{1,0:T(8,128)S(1)}, u32[]{:S(2)}, u32[]{:S(2)}) collective-permute-start(f32[8,640]{1,0:T(8,128)S(1)} %maximum_maximum_fusion), channel_id=1, source_target_pairs={{0,17},{1,16},{2,19},{3,18},{4,21},{5,20},{6,23},{7,22},{8,25},{9,... | collective-permute-start | bytes 61448 | tf_op jit(solution)/shard_map/ppermute | solution.py:352
  137.3 1.3 collective-permute-start.32

commit v5 on v4

v5 whole, which is shorter than its diff:
```python
import functools

import jax
import jax.numpy as jnp
from jax import lax
from jax.experimental import pallas as pl
from jax.experimental.pallas import tpu as pltpu
from jax.sharding import PartitionSpec as P

AXES = ("section", "dp")
F32 = jnp.float32
BF16 = jnp.bfloat16
I32 = jnp.int32
LANES = 128
VMEM = pl.BlockSpec(memory_space=pltpu.VMEM)
SMEM = pl.BlockSpec(memory_space=pltpu.SMEM)
ANY = pl.BlockSpec(memory_space=pl.ANY)
HBM = pl.BlockSpec(memory_space=pltpu.HBM)


def row_map(lengths, pair, core, index, count):
    first, second = lengths[2 * pair], lengths[2 * pair + 1]
    other_first = lengths[2 - 2 * pair]
    j = core * count + index
    in_first = j < first
    in_second = j < first + second
    span = jnp.where(in_first, 2 * pair, jnp.where(in_second, 2 * pair + 1, 3 - 2 * pair))
    place = jnp.where(
        in_first, j, jnp.where(in_second, j - first, 2 * count - other_first + j - first - second)
    )
    return span, place


def as_rows(columns, count):
    lane = lax.broadcasted_iota(I32, (count, LANES), 1)
    wide = jnp.zeros((count, LANES), F32)
    for i, column in enumerate(columns):
        wide = jnp.where(lane == i, column, wide)
    return jnp.transpose(wide)[:8]


def as_column(rows, which):
    full = jnp.concatenate([rows, jnp.zeros((LANES - 8, rows.shape[1]), F32)], axis=0)
    return jnp.transpose(full)[:, which : which + 1]


def sum_kernel(rows, gain, reward, lengths, out):
    value = rows[...].astype(F32)
    scaled = (value * gain[...].astype(F32)).astype(BF16).astype(F32)
    squares = jnp.sum(value * value, axis=1, keepdims=True)
    rewards = jnp.sum(scaled * reward[...].astype(F32), axis=1, keepdims=True)
    out[...] = as_rows([squares, rewards], rows.shape[0])


def pick_kernel(count, lengths, rows, sibling, extra, gain, sums, received, full, big, sums_out):
    section = lax.axis_index("section")
    core, pair = lax.rem(section, 2), lax.div(section, 2)
    positions, half = rows.shape[0], extra.shape[0]
    index = lax.broadcasted_iota(I32, (count, 1), 0)
    span, place = row_map(lengths, pair, core, index, count)
    source = jnp.where(span == section, place, place + positions)
    source = jnp.where(span // 2 == pair, source, place + (2 * positions - (positions - half)))
    lane = lax.broadcasted_iota(I32, (count, 2 * positions + half), 1)
    pick = jnp.where(lane == source, F32(1.0), F32(0.0)).astype(BF16)
    picked = jnp.dot(pick[:, :positions], rows[...], preferred_element_type=F32)
    picked += jnp.dot(pick[:, positions : 2 * positions], sibling[...], preferred_element_type=F32)
    picked += jnp.dot(pick[:, 2 * positions :], extra[...], preferred_element_type=F32)
    scaled = (picked * gain[...].astype(F32)).astype(BF16)
    full[...] = scaled
    big[...] = scaled[: big.shape[0]]
    sums_out[...] = sums[...] + received[...]


def row_kernel(count, width, lengths, tokens, s0, s1, s2, s3, ids, scales):
    section, core, _ = here()
    spans, positions = tokens.shape
    by_move = (s0, s1, s2, s3)
    for pair in range(2):
        index = lax.broadcasted_iota(I32, (count, 1), 0)
        span, place = row_map(lengths, pair, core, index, count)
        lane = lax.broadcasted_iota(I32, (count, positions), 1)
        found = jnp.zeros((count, positions), F32)
        squares = jnp.zeros((count, positions), F32)
        for s in range(spans):
            found = jnp.where(span == s, tokens[s : s + 1, :].astype(F32), found)
        for move in range(spans):
            squares = jnp.where(span == jnp.bitwise_xor(section, move), by_move[move][0:1, :], squares)
        hit = lane == place
        found = jnp.sum(jnp.where(hit, found, F32(0.0)), axis=1, keepdims=True)
        squares = jnp.sum(jnp.where(hit, squares, F32(0.0)), axis=1, keepdims=True)
        ids[pair * count : pair * count + count, :] = found.astype(I32)
        scales[pair * count : pair * count + count, :] = lax.rsqrt(squares / width + 1e-05)


def here():
    section = lax.axis_index("section")
    return section, lax.rem(section, 2), lax.div(section, 2)


def blocks(count):
    _, _, pair = here()
    return pl.multiple_of(pair * count, 16), pl.multiple_of((1 - pair) * count, 16)


def weights(head, sibling, depth, k, far):
    dp_index = lax.axis_index("dp")
    where = jnp.bitwise_xor(dp_index, 2 * k + (1 if far else 0))
    rows = pl.ds(pl.multiple_of(where * depth, depth), depth)
    return head[rows, :], sibling[rows, :]


def products(terms):
    value = jnp.concatenate([t[0] for t in terms], axis=1) if len(terms) > 1 else terms[0][0]
    out = []
    for side in range(2):
        w = [t[1][side] for t in terms]
        w = jnp.concatenate(w, axis=0) if len(w) > 1 else w[0]
        out.append(jnp.dot(value, w, preferred_element_type=F32))
    return jnp.concatenate(out, axis=1)


def small_terms(w, head, sibling, k):
    m2 = w.shape[0] // 2
    depth = w.shape[1]
    return products(
        [(w[:m2, :], weights(head, sibling, depth, k, False)), (w[m2:, :], weights(head, sibling, depth, k, True))]
    )


def first_kernel(n, head, sibling, z, a, b, c, ids, scales, z1, z3, acc, ids_out, scales_out, w0, z1_out, z3_out):
    count, depth = z.shape
    m = count - n
    _, core, _ = here()
    mine, others = blocks(count)
    near = weights(head, sibling, depth, 0, False)
    far = weights(head, sibling, depth, 0, True)
    w0[:m, :] = z[n:, :]
    w0[3 * m :, :] = c[n:, :]
    for which, same, cross in ((0, a, b), (1, b, a)):

        @pl.when(core == which)
        def _():
            acc[pl.ds(mine, count), :] = products([(z[...], near), (same[...], far)])
            acc[pl.ds(others, count), :] = products([(cross[...], near), (c[...], far)])
            w0[m : 2 * m, :] = cross[n:, :]
            w0[2 * m : 3 * m, :] = same[n:, :]

    ids_out[...] = ids[...]
    scales_out[...] = scales[...]
    z1_out[...] = z1[...]
    z3_out[...] = z3[...]


def stage_kernel(k, small_k, n_pass, *refs):
    refs = list(refs)
    n_small = len(small_k)
    head, sibling, acc_in, z, a, b, c = refs[:7]
    smalls = refs[7 : 7 + n_small]
    passed = refs[7 + n_small : 7 + n_small + n_pass]
    acc = refs[7 + n_small + n_pass]
    outs = refs[8 + n_small + n_pass :]
    n, depth = z.shape
    count = acc.shape[0] // 2
    m = count - n
    _, core, _ = here()
    mine, others = blocks(count)
    near = weights(head, sibling, depth, k, False)
    far = weights(head, sibling, depth, k, True)
    for which, same, cross in ((0, a, b), (1, b, a)):

        @pl.when(core == which)
        def _():
            rows = pl.ds(mine, n)
            acc[rows, :] = acc_in[rows, :] + products([(z[...], near), (same[...], far)])
            rows = pl.ds(others, n)
            acc[rows, :] = acc_in[rows, :] + products([(cross[...], near), (c[...], far)])

    values = [small_terms(w, head, sibling, w_k) for w, w_k in zip(smalls, small_k)]
    for i, base in enumerate((mine, others)):
        rows = pl.ds(pl.multiple_of(base + n, 16), m)
        value = acc_in[rows, :]
        for v in values:
            value = value + v[i * m : (i + 1) * m]
        acc[rows, :] = value
    for out, value in zip(outs, passed):
        out[...] = value[...]


def gate_kernel(value, *refs):
    refs[-1][...] = value[...]


def column_ids(block):
    section, core, _ = here()
    dp_index, groups = lax.axis_index("dp"), lax.axis_size("dp")
    lane = lax.broadcasted_iota(I32, (1, block), 1)
    own = (section * groups + dp_index) * block
    other = ((section + 1 - 2 * core) * groups + dp_index) * block
    return jnp.concatenate([lane + own, lane + other], axis=1)


def summary(logits, scale, token_ids, ids):
    logits = logits * scale
    top = jnp.max(logits, axis=1, keepdims=True)
    total = jnp.sum(jnp.exp(logits - top), axis=1, keepdims=True)
    target = jnp.sum(jnp.where(ids == token_ids, logits, F32(0.0)), axis=1, keepdims=True)
    lane = lax.broadcasted_iota(I32, (logits.shape[0], LANES), 1)
    return jnp.where(lane == 0, top, jnp.where(lane == 1, total, jnp.where(lane == 2, target, F32(0.0))))


def own_kernel(k, head, sibling, acc_in, z, a, b, w, token_ids, scales, left, far_out, wide):
    n, depth = z.shape
    count = acc_in.shape[0] // 2
    m = count - n
    _, core, _ = here()
    mine, others = blocks(count)
    near = weights(head, sibling, depth, k, False)
    far = weights(head, sibling, depth, k, True)
    block = head.shape[1]
    far_out[:, :block] = far[0]
    far_out[:, block:] = far[1]
    ids = column_ids(block)
    wide[...] = jnp.zeros(wide.shape, F32)
    for which, same, cross in ((0, a, b), (1, b, a)):

        @pl.when(core == which)
        def _():
            rows = pl.ds(mine, n)
            logits = acc_in[rows, :] + products([(z[...], near), (same[...], far)])
            wide[rows, :] = summary(logits, scales[rows, :], token_ids[rows, :], ids)
            left[...] = acc_in[pl.ds(others, n), :] + products([(cross[...], near)])

    value = small_terms(w, head, sibling, k)
    for i, base in enumerate((mine, others)):
        rows = pl.ds(pl.multiple_of(base + n, 16), m)
        logits = acc_in[rows, :] + value[i * m : (i + 1) * m]
        wide[rows, :] = summary(logits, scales[rows, :], token_ids[rows, :], ids)


def last_kernel(far, left, c, wide_in, token_ids, scales, out, wide):
    n = c.shape[0]
    count = token_ids.shape[0] // 2
    _, others = blocks(count)
    ids = column_ids(far.shape[1] // 2)
    wide[...] = wide_in[...]
    logits = left[...] + jnp.dot(c[...], far[...], preferred_element_type=F32)
    rows = pl.ds(others, n)
    wide[rows, :] = summary(logits, scales[rows, :], token_ids[rows, :], ids)
    out[...] = jnp.transpose(wide[...])[:8]


def whole_kernel(acc, token_ids, scales, out):
    count = acc.shape[0] // 2
    ids = column_ids(acc.shape[1] // 2)
    wide = summary(acc[...], scales[...], token_ids[...], ids)
    wide = jnp.concatenate([wide, jnp.zeros((out.shape[1] - 2 * count, LANES), F32)])
    out[...] = jnp.transpose(wide)[:8]


def final_kernel(count, width, lengths, sums, stats, out_ref, score_ref):
    section = lax.axis_index("section")
    positions = out_ref.shape[1]
    where = lax.broadcasted_iota(I32, (1, positions), 1)
    logprob = jnp.zeros((1, positions), F32)
    index = lax.broadcasted_iota(I32, (count, 1), 0)
    for core in range(2):
        lp = as_column(stats[core], 0)
        for pair in range(2):
            value = lp[pair * count : pair * count + count]
            span, place = row_map(lengths, pair, core, index, count)
            hit = (place == where) & (span == section)
            logprob += jnp.sum(jnp.where(hit, value, F32(0.0)), axis=0, keepdims=True)
    out_ref[...] = logprob
    length = lengths[section]
    reward = sums[1:2, :] * lax.rsqrt(sums[0:1, :] / width + 1e-05)
    score = jnp.sum(jnp.where(where < length, reward, F32(0.0)), axis=1, keepdims=True)
    score_ref[...] = score / length.astype(F32)


def combine(parts):
    top = parts[0][0]
    for part in parts[1:]:
        top = jnp.maximum(top, part[0])
    total = sum(part[1] * jnp.exp(part[0] - top) for part in parts)
    target = sum(part[2] for part in parts)
    return jnp.concatenate([jnp.stack([top, total, target]), jnp.zeros((5,) + top.shape, F32)])


def call(body, outs, in_specs, args, limit=16, scratch=()):
    many = isinstance(outs, (list, tuple))
    return pl.pallas_call(
        body,
        out_shape=outs,
        in_specs=in_specs,
        out_specs=[VMEM] * len(outs) if many else VMEM,
        scratch_shapes=scratch,
        compiler_params=pltpu.CompilerParams(vmem_limit_bytes=limit << 20),
    )(*args)


def up(value):
    return -(-value // LANES) * LANES


def per_device(groups, hidden, norm_gain, head, reward_head, tokens, lengths):
    section = lax.axis_index("section")
    core, pair = section % 2, section // 2
    sections = lax.axis_size("section")
    spans, positions = tokens.shape
    block, width, part = head.shape[1], head.shape[0], hidden.shape[2]
    count = 3 * spans * positions // 4 // sections
    half = positions // 2
    big = (count * 8 // 9) // 16 * 16
    small = count - big
    rows = hidden[0]
    gain = norm_gain[None]

    def mesh_perm(move):
        pairs = []
        for s in range(sections):
            for d in range(groups):
                s2, d2 = move(s, d)
                pairs.append((s * groups + d, s2 * groups + d2))
        return pairs

    send = lambda value, perm: lax.ppermute(value, AXES, perm)
    like = lambda v: jax.ShapeDtypeStruct(v.shape, v.dtype)
    acc_shape = jax.ShapeDtypeStruct((2 * count, 2 * block), F32)
    stats_shape = jax.ShapeDtypeStruct((8, up(2 * count)), F32)
    ids_shape = jax.ShapeDtypeStruct((2 * count, 1), I32)
    scales_shape = jax.ShapeDtypeStruct((2 * count, 1), F32)
    perm_z = {k: mesh_perm(lambda s, d, k=k: (s, d ^ (2 * k))) for k in (1, 2, 3)}
    perm_x = mesh_perm(lambda s, d: (s, d ^ 1))

    swap = [(s, s ^ 1) for s in range(sections)]
    over = [(s, s ^ 2) for s in range(sections)]
    across = [(s, s ^ 3) for s in range(sections)]
    extra = lax.ppermute(rows[half:], "section", [(1, 3), (3, 1)])
    sibling = lax.ppermute(rows, "section", swap)
    head_sibling = lax.ppermute(head, "section", swap)

    sums = call(
        sum_kernel,
        jax.ShapeDtypeStruct((8, positions), F32),
        [VMEM] * 3 + [SMEM],
        (rows, gain, reward_head[None], lengths),
    )
    if groups == 8:
        sums = sums + send(sums, perm_z[1])
        received = send(sums, perm_z[2])
    else:
        sums = lax.psum(sums, "dp")
        received = jnp.zeros_like(sums)
    full, g, sums = call(
        functools.partial(pick_kernel, count),
        [
            jax.ShapeDtypeStruct((count, part), BF16),
            jax.ShapeDtypeStruct((big, part), BF16),
            like(sums),
        ],
        [SMEM] + [VMEM] * 6,
        (lengths, rows, sibling, extra, gain, sums, received),
    )
    if groups == 8:
        sums = sums + send(sums, perm_x)
    token_ids, scales = call(
        functools.partial(row_kernel, count, width),
        [ids_shape, scales_shape],
        [SMEM] + [VMEM] * 5,
        (lengths, tokens, sums) + tuple(lax.ppermute(sums, "section", p) for p in (swap, over, across)),
    )

    if groups == 8:
        perm_a = mesh_perm(lambda s, d: (s, d ^ 1) if s % 2 == 0 else (s ^ 2, d))
        perm_b = mesh_perm(lambda s, d: (s ^ 2, d) if s % 2 == 0 else (s, d ^ 1))

        def gate(value, *after):
            return call(gate_kernel, like(value), [VMEM] + [ANY] * len(after), (value,) + after)

        def stage(k, acc, pieces, smalls, passed):
            args = (head, head_sibling, acc) + pieces + tuple(smalls.values()) + passed
            return call(
                functools.partial(stage_kernel, k, tuple(smalls), len(passed)),
                [acc_shape] + [like(p) for p in passed],
                [VMEM] * len(args),
                args,
            )

        z1 = send(g, perm_z[1])
        z3 = send(full, perm_z[3])[:big]
        a0 = send(full, perm_a)
        b0 = send(full, perm_b)
        c0 = send(a0, perm_b)
        z1 = gate(z1, b0)
        a1 = send(z1, perm_a)
        acc, token_ids, scales, w0, z1, z3 = call(
            functools.partial(first_kernel, big),
            [acc_shape, ids_shape, scales_shape, jax.ShapeDtypeStruct((4 * small, part), BF16), like(z1), like(z3)],
            [VMEM] * 10,
            (head, head_sibling, full, a0, b0, c0, token_ids, scales, z1, z3),
        )
        b1 = send(z1, perm_b)
        z2 = send(z3, perm_z[1])
        c1 = send(a1, perm_b)
        z3 = gate(z3, b1, z2)
        a3 = send(z3, perm_a)
        acc, z3, w0 = stage(1, acc, (z1, a1, b1, c1), {}, (z3, w0))
        b3 = send(z3, perm_b)
        w3 = send(w0, perm_z[3])
        w1 = send(w0, perm_z[1])
        c3 = send(a3, perm_b)
        z2 = gate(z2, b3)
        a2 = send(z2, perm_a)
        acc, z2, w3 = stage(3, acc, (z3, a3, b3, c3), {1: w1, 3: w3}, (z2, w3))
        b2 = send(z2, perm_b)
        w2 = send(w3, perm_z[1])
        c2 = send(a2, perm_b)
        left, far, wide = call(
            functools.partial(own_kernel, 2),
            [
                jax.ShapeDtypeStruct((big, 2 * block), F32),
                jax.ShapeDtypeStruct((part, 2 * block), BF16),
                jax.ShapeDtypeStruct((up(2 * count), LANES), F32),
            ],
            [VMEM] * 9,
            (head, head_sibling, acc, z2, a2, b2, w2, token_ids, scales),
        )
        stats = call(
            last_kernel,
            stats_shape,
            [VMEM] * 6,
            (far, left, c2, wide, token_ids, scales),
            scratch=[pltpu.VMEM((up(2 * count), LANES), F32)],
        )
        stats = combine([stats] + [send(stats, perm_z[k]) for k in (1, 2, 3)])
        stats = combine(
            [stats]
            + [send(stats, mesh_perm(lambda s, d, v=v: (s ^ v[0], d ^ v[1]))) for v in ((0, 1), (2, 0), (2, 1))]
        )
    else:
        other = lax.ppermute(full, "section", over)
        ordered = jnp.concatenate([jnp.where(pair == 0, full, other), jnp.where(pair == 0, other, full)])
        everything = lax.all_gather(ordered, "dp", axis=1, tiled=True)
        acc = jnp.concatenate(
            [jnp.dot(everything, h, preferred_element_type=F32) for h in (head, head_sibling)], axis=1
        )
        stats = call(whole_kernel, stats_shape, [VMEM] * 3, (acc, token_ids, scales))
        gathered = lax.all_gather(stats, "dp")
        stats = combine([gathered[i] for i in range(groups)])
        stats = combine([stats, lax.ppermute(stats, "section", over)])
    lp = stats[2:3] - (stats[0:1] + jnp.log(stats[1:2]))
    lp = jnp.concatenate([lp, jnp.zeros((7, lp.shape[1]), F32)])
    both = lambda v, u: jnp.stack([jnp.where(core == 0, v, u), jnp.where(core == 0, u, v)])
    stats = both(lp, lax.ppermute(lp, "section", swap))
    logprob, score = call(
        functools.partial(final_kernel, count, width),
        [jax.ShapeDtypeStruct((1, positions), F32), jax.ShapeDtypeStruct((1, 1), F32)],
        [SMEM, VMEM, VMEM],
        (lengths, sums, stats),
    )
    return (logprob, score[0])


def solution(mesh):
    groups = mesh.shape["dp"]
    return jax.shard_map(
        lambda *args: per_device(groups, *args),
        mesh=mesh,
        in_specs=(P("section", None, "dp"), P("dp"), P(None, ("section", "dp")), P("dp"), P(), P()),
        out_specs=(P("section", None), P("section")),
        check_vma=False,
    )
```

time: 141 us -> 148 us (1.050)
  waiting for transfers between devices: 58.3 us -> 80.1 us
  starting transfers between devices: 57.4 us -> 49.7 us
  local copies, waits for them, and re-layouts: 10.8 us -> 3.19 us
    ppermute x27, waiting for transfers between devices: 53.9 us -> 71.2 us  [per_device(): send = lambda value, perm: lax.ppermute(value, AXES, perm)]
    unnamed x18 -> x10, local copies, waits for them, and re-layouts: 8.35 us -> 0.67 us
    ppermute x1, starting transfers between devices: 7.8 us -> 0.52 us  [per_device(): head_sibling = lax.ppermute(head, 'section', swap)]
    ppermute x2 -> x3, waiting for transfers between devices: 3.23 us -> 7.77 us  [per_device(): lax.ppermute(sums, 'section', p)]
    pallas_call x11 -> x12, Pallas kernels: 13.3 us -> 14 us  [call(): pl.pallas_call(body, out_shape=outs, in_specs=in_specs, out_specs=[VMEM]...]
  transfers between devices with their start and end apart: 33 -> 34, of which waited for: 17 -> 20; matrix products, arithmetic and copies ran while one was open for 2% -> 2% of each run, Pallas kernels for 6% -> 8%
where the time goes in v5:
time: 148 us
  waiting for transfers between devices  80.1 us (54%)
  starting transfers between devices  49.7 us (34%)
  Pallas kernels  14 us (9%)
  local copies, waits for them, and re-layouts  3.19 us (2%)
    ppermute x27, waiting for transfers between devices, per_device(): send = lambda value, perm: lax.ppermute(value, AXES, perm)  71.2 us
    ppermute x27, starting transfers between devices, per_device(): send = lambda value, perm: lax.ppermute(value, AXES, perm)  48.1 us
    pallas_call x12, Pallas kernels, call(): pl.pallas_call(body, out_shape=outs, in_specs=in_specs, out_specs=[VMEM]...  14 us
    ppermute x3, waiting for transfers between devices, per_device(): lax.ppermute(sums, 'section', p)  7.77 us
  transfers between devices with their start and end apart: 34, of which 20 were waited for; matrix products, arithmetic and copies ran while one was open for 2% of the time, Pallas kernels for 8%

profile of v5, /device:TPU:0, one launch (start us, length us, event | category | flops | bytes accessed | tf_op | source)
XLA Modules:
  0.0 148.0 jit_solution(16500397048060719497)
XLA Ops:
  1.2 1.0 slice_bitcast_fusion
  5.0 1.0 shard_map.77
  6.0 3.0 %collective-permute-start.2 = (f32[8,384]{1,0:T(8,128)S(1)}, f32[8,384]{1,0:T(8,128)S(1)}, u32[]{:S(2)}, u32[]{:S(2)}) collective-permute-start(f32[8,384]{1,0:T(8,128)S(1)} %shard_map.77), channel_id=1, source_target_pairs={{0,2},{1,3},{2,0},{3,1},{4,6},{5,7},{6,4},{7,5},{8,10},{9,11},{10,... | collective-permute-start | bytes 36872 | tf_op jit(solution)/shard_map/ppermute | solution.py:326
  9.1 1.7 %collective-permute-done.2 = f32[8,384]{1,0:T(8,128)S(1)} collective-permute-done((f32[8,384]{1,0:T(8,128)S(1)}, f32[8,384]{1,0:T(8,128)S(1)}, u32[]{:S(2)}, u32[]{:S(2)}) %collective-permute-start.2) | collective-permute-done | bytes 12320 | tf_op jit(solution)/shard_map/ppermute | solution.py:326
  10.7 3.0 %collective-permute-start.3 = (f32[8,384]{1,0:T(8,128)S(1)}, f32[8,384]{1,0:T(8,128)S(1)}, u32[]{:S(2)}, u32[]{:S(2)}) collective-permute-start(f32[8,384]{1,0:T(8,128)S(1)} %add.71.sums), channel_id=1, source_target_pairs={{0,4},{1,5},{2,6},{3,7},{4,0},{5,1},{6,2},{7,3},{8,12},{9,13},{10,... | collective-permute-start | bytes 36872 | tf_op jit(solution)/shard_map/ppermute | solution.py:326
  13.8 1.7 %collective-permute-done.3.received = f32[8,384]{1,0:T(8,128)S(1)} collective-permute-done((f32[8,384]{1,0:T(8,128)S(1)}, f32[8,384]{1,0:T(8,128)S(1)}, u32[]{:S(2)}, u32[]{:S(2)}) %collective-permute-start.3) | collective-permute-done | bytes 12320 | tf_op jit(solution)/shard_map/ppermute | solution.py:326
  15.5 1.6 %shard_map.78 = (bf16[288,1024]{1,0:T(8,128)(2,1)S(1)}, bf16[256,1024]{1,0:T(8,128)(2,1)S(1)}, f32[8,384]{1,0:T(8,128)S(1)}) custom-call(s32[4]{0:T(128)S(1)} %copy-done.3, bf16[384,1024]{1,0:T(8,128)(2,1)S(1)} %bitcast.10, bf16[384,1024]{1,0:T(8,128)(2,1)S(1)} %collective-permute-done.sibling, bf16[192,1024]{1,0:T(8,128)(2,1)S(1)} %collective-permute-done.1.extra, ...), custom_call_target="tpu_custom_call" | custom-call | tf_op jit(solution)/shard_map/pallas_call | solution.py:291
  17.1 1.9 %collective-permute-start.6 = (bf16[288,1024]{1,0:T(8,128)(2,1)S(1)}, bf16[288,1024]{1,0:T(8,128)(2,1)S(1)}, u32[]{:S(2)}, u32[]{:S(2)}) collective-permute-start(bf16[288,1024]{1,0:T(8,128)(2,1)S(1)} %get-tuple-element.25.z), channel_id=1, source_target_pairs={{0,1},{1,0},{2,3},{3,2},{4,5},{5,4},{6,7},{7,6},{8,24},{9,25},{10,... | collective-permute-start | bytes 1769480 | tf_op jit(solution)/shard_map/ppermute | solution.py:326
  19.0 1.5 %collective-permute-start.7 = (bf16[288,1024]{1,0:T(8,128)(2,1)S(1)}, bf16[288,1024]{1,0:T(8,128)(2,1)S(1)}, u32[]{:S(2)}, u32[]{:S(2)}) collective-permute-start(bf16[288,1024]{1,0:T(8,128)(2,1)S(1)} %get-tuple-element.25.z), channel_id=1, source_target_pairs={{0,16},{1,17},{2,18},{3,19},{4,20},{5,21},{6,22},{7,23},{8,9},{9,8... | collective-permute-start | bytes 1769480 | tf_op jit(solution)/shard_map/ppermute | solution.py:326
  20.5 1.6 %collective-permute-start.12 = (bf16[256,1024]{1,0:T(8,128)(2,1)S(1)}, bf16[256,1024]{1,0:T(8,128)(2,1)S(1)}, u32[]{:S(2)}, u32[]{:S(2)}) collective-permute-start(bf16[256,1024]{1,0:T(8,128)(2,1)S(1)} %get-tuple-element.28), channel_id=1, source_target_pairs={{0,2},{1,3},{2,0},{3,1},{4,6},{5,7},{6,4},{7,5},{8,10},{9,11},{10,... | collective-permute-start | bytes 1572872 | tf_op jit(solution)/shard_map/ppermute | solution.py:326
  22.1 2.5 %collective-permute-start.13 = (bf16[288,1024]{1,0:T(8,128)(2,1)S(1)}, bf16[288,1024]{1,0:T(8,128)(2,1)S(1)}, u32[]{:S(2)}, u32[]{:S(2)}) collective-permute-start(bf16[288,1024]{1,0:T(8,128)(2,1)S(1)} %get-tuple-element.25.z), channel_id=1, source_target_pairs={{0,6},{1,7},{2,4},{3,5},{4,2},{5,3},{6,0},{7,1},{8,14},{9,15},{10,... | collective-permute-start | bytes 1769480 | tf_op jit(solution)/shard_map/ppermute | solution.py:326
  24.6 8.6 %collective-permute-done.6.a = bf16[288,1024]{1,0:T(8,128)(2,1)S(1)} collective-permute-done((bf16[288,1024]{1,0:T(8,128)(2,1)S(1)}, bf16[288,1024]{1,0:T(8,128)(2,1)S(1)}, u32[]{:S(2)}, u32[]{:S(2)}) %collective-permute-start.6) | collective-permute-done | bytes 589856 | tf_op jit(solution)/shard_map/ppermute | solution.py:326
  33.1 2.0 %collective-permute-start.8 = (bf16[288,1024]{1,0:T(8,128)(2,1)S(1)}, bf16[288,1024]{1,0:T(8,128)(2,1)S(1)}, u32[]{:S(2)}, u32[]{:S(2)}) collective-permute-start(bf16[288,1024]{1,0:T(8,128)(2,1)S(1)} %collective-permute-done.6.a), channel_id=1, source_target_pairs={{0,16},{1,17},{2,18},{3,19},{4,20},{5,21},{6,22},{7,23},{8,9},{9,8... | collective-permute-start | bytes 1769480 | tf_op jit(solution)/shard_map/ppermute | solution.py:326
  35.2 1.5 collective-permute-start.14
  37.3 9.4 %collective-permute-done.4 = f32[8,384]{1,0:T(8,128)S(1)} collective-permute-done((f32[8,384]{1,0:T(8,128)S(1)}, f32[8,384]{1,0:T(8,128)S(1)}, u32[]{:S(2)}, u32[]{:S(2)}) %collective-permute-start.4) | collective-permute-done | bytes 12320 | tf_op jit(solution)/shard_map/ppermute | solution.py:326
  46.9 3.5 %collective-permute-done.10.s2 = f32[8,384]{1,0:T(8,128)S(1)} collective-permute-done((f32[8,384]{1,0:T(8,128)S(1)}, f32[8,384]{1,0:T(8,128)S(1)}, u32[]{:S(2)}, u32[]{:S(2)}) %collective-permute-start.10) | collective-permute-done | bytes 12320 | tf_op jit(solution)/shard_map/ppermute | solution.py:370
  50.4 3.1 %collective-permute-done.11.s3 = f32[8,384]{1,0:T(8,128)S(1)} collective-permute-done((f32[8,384]{1,0:T(8,128)S(1)}, f32[8,384]{1,0:T(8,128)S(1)}, u32[]{:S(2)}, u32[]{:S(2)}) %collective-permute-start.11) | collective-permute-done | bytes 12320 | tf_op jit(solution)/shard_map/ppermute | solution.py:370
  53.5 1.2 collective-permute-done.9.s1
  54.7 1.3 shard_map.79
  56.1 1.6 %shard_map.81 = (f32[576,512]{1,0:T(8,128)S(1)}, s32[576,1]{1,0:T(8,128)S(1)}, f32[576,1]{1,0:T(8,128)S(1)}, bf16[128,1024]{1,0:T(8,128)(2,1)S(1)}, bf16[256,102...) custom-call(bf16[8192,256]{1,0:T(8,128)(2,1)S(1)} %copy-done, ...), custom_call_target="tpu_custom_call" | custom-call | tf_op jit(solution)/shard_map/pallas_call | solution.py:291
  58.0 1.7 %collective-permute-start.17 = (bf16[256,1024]{1,0:T(8,128)(2,1)S(1)}, bf16[256,1024]{1,0:T(8,128)(2,1)S(1)}, u32[]{:S(2)}, u32[]{:S(2)}) collective-permute-start(bf16[256,1024]{1,0:T(8,128)(2,1)S(1)} %get-tuple-element.31.value), channel_id=1, source_target_pairs={{0,2},{1,3},{2,0},{3,1},{4,6},{5,7},{6,4},{7,5},{8,10},{9,11},{10,... | collective-permute-start | bytes 1572872 | tf_op jit(solution)/shard_map/ppermute | solution.py:326
  59.7 1.3 collective-permute-start.16
  61.0 6.0 %collective-permute-done.15.refs_0_.refs_5_ = bf16[256,1024]{1,0:T(8,128)(2,1)S(1)} collective-permute-done((bf16[256,1024]{1,0:T(8,128)(2,1)S(1)}, bf16[256,1024]{1,0:T(8,128)(2,1)S(1)}, u32[]{:S(2)}, u32[]{:S(2)}) %collective-permute-start.15) | collective-permute-done | bytes 524320 | tf_op jit(solution)/shard_map/ppermute | solution.py:326
  67.0 5.5 %collective-permute-done.17.refs_1_.value = bf16[256,1024]{1,0:T(8,128)(2,1)S(1)} collective-permute-done((bf16[256,1024]{1,0:T(8,128)(2,1)S(1)}, bf16[256,1024]{1,0:T(8,128)(2,1)S(1)}, u32[]{:S(2)}, u32[]{:S(2)}) %collective-permute-start.17) | collective-permute-done | bytes 524320 | tf_op jit(solution)/shard_map/ppermute | solution.py:326
  72.5 1.2 collective-permute-start.18
  73.7 1.4 shard_map.83
  75.5 11.1 %collective-permute-done.18.refs_4_ = bf16[256,1024]{1,0:T(8,128)(2,1)S(1)} collective-permute-done((bf16[256,1024]{1,0:T(8,128)(2,1)S(1)}, bf16[256,1024]{1,0:T(8,128)(2,1)S(1)}, u32[]{:S(2)}, u32[]{:S(2)}) %collective-permute-start.18) | collective-permute-done | bytes 524320 | tf_op jit(solution)/shard_map/ppermute | solution.py:326
  86.8 1.4 collective-permute-start.23
  88.2 1.1 collective-permute-start.21
  89.3 12.3 %collective-permute-start.22 = (bf16[128,1024]{1,0:T(8,128)(2,1)S(1)}, bf16[128,1024]{1,0:T(8,128)(2,1)S(1)}, u32[]{:S(2)}, u32[]{:S(2)}) collective-permute-start(bf16[128,1024]{1,0:T(8,128)(2,1)S(1)} %get-tuple-element.35), channel_id=1, source_target_pairs={{0,6},{1,7},{2,4},{3,5},{4,2},{5,3},{6,0},{7,1},{8,14},{9,15},{10,... | collective-permute-start | bytes 786440 | tf_op jit(solution)/shard_map/ppermute | solution.py:326
  101.5 10.8 %collective-permute-done.22.refs_8_.refs_10_ = bf16[128,1024]{1,0:T(8,128)(2,1)S(1)} collective-permute-done((bf16[128,1024]{1,0:T(8,128)(2,1)S(1)}, bf16[128,1024]{1,0:T(8,128)(2,1)S(1)}, u32[]{:S(2)}, u32[]{:S(2)}) %collective-permute-start.22) | collective-permute-done | bytes 262176 | tf_op jit(solution)/shard_map/ppermute | solution.py:326
  112.4 2.2 %shard_map.85 = (f32[576,512]{1,0:T(8,128)S(1)}, bf16[256,1024]{1,0:T(8,128)(2,1)S(1)}, bf16[128,1024]{1,0:T(8,128)(2,1)S(1)}) custom-call(bf16[8192,256]{1,0:T(8,128)(2,1)S(1)} %copy-done, bf16[8192,256]{1,0:T(8,128)(2,1)S(1)} %collective-permute-done.5.sibling.refs_1_, f32[576,512]{1,0:T(8,128)S(1)} %get-tuple-element.33.refs_2_, ...), custom_call_target="tpu_custom_call" | custom-call | tf_op jit(solution)/shard_map/pallas_call | solution.py:291
  115.1 1.6 %collective-permute-start.26 = (bf16[256,1024]{1,0:T(8,128)(2,1)S(1)}, bf16[256,1024]{1,0:T(8,128)(2,1)S(1)}, u32[]{:S(2)}, u32[]{:S(2)}) collective-permute-start(bf16[256,1024]{1,0:T(8,128)(2,1)S(1)} %collective-permute-done.23.a), channel_id=1, source_target_pairs={{0,16},{1,17},{2,18},{3,19},{4,20},{5,21},{6,22},{7,23},{8,9},{9,8... | collective-permute-start | bytes 1572872 | tf_op jit(solution)/shard_map/ppermute | solution.py:326
  117.3 5.8 %collective-permute-done.25.w = bf16[128,1024]{1,0:T(8,128)(2,1)S(1)} collective-permute-done((bf16[128,1024]{1,0:T(8,128)(2,1)S(1)}, bf16[128,1024]{1,0:T(8,128)(2,1)S(1)}, u32[]{:S(2)}, u32[]{:S(2)}) %collective-permute-start.25) | collective-permute-done | bytes 262176 | tf_op jit(solution)/shard_map/ppermute | solution.py:326
  123.1 0.8 collective-permute-done.24.b
  123.9 2.1 %shard_map.86 = (f32[256,512]{1,0:T(8,128)S(1)}, bf16[1024,512]{1,0:T(8,128)(2,1)S(1)}, f32[640,128]{1,0:T(8,128)S(1)}) custom-call(bf16[8192,256]{1,0:T(8,128)(2,1)S(1)} %copy-done, bf16[8192,256]{1,0:T(8,128)(2,1)S(1)} %collective-permute-done.5.sibling.refs_1_, f32[576,512]{1,0:T(8,128)S(1)} %get-tuple-element.36.acc_in, ...), custom_call_target="tpu_custom_call" | custom-call | tf_op jit(solution)/shard_map/pallas_call | solution.py:291
  125.9 3.6 %collective-permute-done.26.c = bf16[256,1024]{1,0:T(8,128)(2,1)S(1)} collective-permute-done((bf16[256,1024]{1,0:T(8,128)(2,1)S(1)}, bf16[256,1024]{1,0:T(8,128)(2,1)S(1)}, u32[]{:S(2)}, u32[]{:S(2)}) %collective-permute-start.26) | collective-permute-done | bytes 524320 | tf_op jit(solution)/shard_map/ppermute | solution.py:326
  129.5 0.7 shard_map.87
  130.9 1.5 collective-permute-start.28
  132.4 2.3 %collective-permute-start.29 = (f32[8,640]{1,0:T(8,128)S(1)}, f32[8,640]{1,0:T(8,128)S(1)}, u32[]{:S(2)}, u32[]{:S(2)}) collective-permute-start(f32[8,640]{1,0:T(8,128)S(1)} %shard_map.87), channel_id=1, source_target_pairs={{0,6},{1,7},{2,4},{3,5},{4,2},{5,3},{6,0},{7,1},{8,14},{9,15},{10,... | collective-permute-start | bytes 61448 | tf_op jit(solution)/shard_map/ppermute | solution.py:326
  134.7 0.8 collective-permute-done.28
  135.6 2.4 %collective-permute-done.29 = f32[8,640]{1,0:T(8,128)S(1)} collective-permute-done((f32[8,640]{1,0:T(8,128)S(1)}, f32[8,640]{1,0:T(8,128)S(1)}, u32[]{:S(2)}, u32[]{:S(2)}) %collective-permute-start.29) | collective-permute-done | bytes 20512 | tf_op jit(solution)/shard_map/ppermute | solution.py:326
  138.0 1.5 %collective-permute-start.30 = (f32[8,640]{1,0:T(8,128)S(1)}, f32[8,640]{1,0:T(8,128)S(1)}, u32[]{:S(2)}, u32[]{:S(2)}) collective-permute-start(f32[8,640]{1,0:T(8,128)S(1)} %maximum_maximum_fusion), channel_id=1, source_target_pairs={{0,1},{1,0},{2,3},{3,2},{4,5},{5,4},{6,7},{7,6},{8,9},{9,8},{10,11... | collective-permute-start | bytes 61448 | tf_op jit(solution)/shard_map/ppermute | solution.py:326
  140.1 1.4 collective-permute-start.32
  141.8 1.5 %collective-permute-done.31 = f32[8,640]{1,0:T(8,128)S(1)} collective-permute-done((f32[8,640]{1,0:T(8,128)S(1)}, f32[8,640]{1,0:T(8,128)S(1)}, u32[]{:S(2)}, u32[]{:S(2)}) %collective-permute-start.31) | collective-permute-done | bytes 20512 | tf_op jit(solution)/shard_map/ppermute | solution.py:326
  143.4 1.4 collective-permute-done.32
  144.9 1.2 collective-permute-done.33
  146.1 1.9 %shard_map.88 = (f32[1,384]{1,0:T(1,128)}, f32[1,1]{1,0:T(1,128)}) custom-call(s32[4]{0:T(128)S(1)} %copy-done.3, f32[8,384]{1,0:T(8,128)S(1)} %add.72.s0.sums, f32[2,8,640]{2,1,0:T(8,128)S(1)} %pad_maximum_fusion.stats), custom_call_target="tpu_custom_call" | custom-call | tf_op jit(solution)/shard_map/pallas_call | solution.py:291
  (56 shorter events, 8.2 us)
Async XLA Ops:
  0.6 3.7 %copy-start.1 = (bf16[1,384,1024]{2,1,0:T(8,128)(2,1)S(1)}, bf16[1,384,1024]{2,1,0:T(8,128)(2,1)}, u32[]{:S(2)}) copy-start(bf16[1,384,1024]{2,1,0:T(8,128)(2,1)} %param.6) | copy-start | bytes 2359300
  0.6 14.8 %copy-start.3 = (s32[4]{0:T(128)S(1)}, s32[4]{0:T(128)}, u32[]{:S(2)}) copy-start(s32[4]{0:T(128)} %lengths.7) | copy-start | bytes 52
  0.7 55.4 %collective-permute-start.5 = (bf16[8192,256]{1,0:T(8,128)(2,1)}, bf16[8192,256]{1,0:T(8,128)(2,1)S(1)}, u32[]{:S(2)}, u32[]{:S(2)}) collective-permute-start(bf16[8192,256]{1,0:T(8,128)(2,1)} %head.3), channel_id=1, source_target_pairs={{0,8},{8,0},{16,24},{24,16},{1,9},{9,1},{17,25},{25,17},{2,10},{10... | collective-permute-start | bytes 12582920 | tf_op jit(solution)/shard_map/ppermute | solution.py:340
  1.2 14.3 %collective-permute-start = (bf16[384,1024]{1,0:T(8,128)(2,1)}, bf16[384,1024]{1,0:T(8,128)(2,1)S(1)}, u32[]{:S(2)}, u32[]{:S(2)}) collective-permute-start(bf16[384,1024]{1,0:T(8,128)(2,1)} %bitcast.8), channel_id=1, source_target_pairs={{0,8},{8,0},{16,24},{24,16},{1,9},{9,1},{17,25},{25,17},{2,10},{10... | collective-permute-start | bytes 2359304 | tf_op jit(solution)/shard_map/ppermute | solution.py:339
  2.3 13.2 %collective-permute-start.1 = (bf16[192,1024]{1,0:T(8,128)(2,1)S(1)}, bf16[192,1024]{1,0:T(8,128)(2,1)S(1)}, u32[]{:S(2)}, u32[]{:S(2)}) collective-permute-start(bf16[192,1024]{1,0:T(8,128)(2,1)S(1)} %slice_bitcast_fusion), channel_id=1, source_target_pairs={{8,24},{24,8},{9,25},{25,9},{10,26},{26,10},{11,27},{27,11},{12,28... | collective-permute-start | bytes 1179656 | tf_op jit(solution)/shard_map/ppermute | solution.py:338
  4.3 0.7 copy-start.2
  6.0 4.7 %collective-permute-start.2 = (f32[8,384]{1,0:T(8,128)S(1)}, f32[8,384]{1,0:T(8,128)S(1)}, u32[]{:S(2)}, u32[]{:S(2)}) collective-permute-start(f32[8,384]{1,0:T(8,128)S(1)} %shard_map.77), channel_id=1, source_target_pairs={{0,2},{1,3},{2,0},{3,1},{4,6},{5,7},{6,4},{7,5},{8,10},{9,11},{10,... | collective-permute-start | bytes 36872 | tf_op jit(solution)/shard_map/ppermute | solution.py:326
  10.7 4.7 %collective-permute-start.3 = (f32[8,384]{1,0:T(8,128)S(1)}, f32[8,384]{1,0:T(8,128)S(1)}, u32[]{:S(2)}, u32[]{:S(2)}) collective-permute-start(f32[8,384]{1,0:T(8,128)S(1)} %add.71.sums), channel_id=1, source_target_pairs={{0,4},{1,5},{2,6},{3,7},{4,0},{5,1},{6,2},{7,3},{8,12},{9,13},{10,... | collective-permute-start | bytes 36872 | tf_op jit(solution)/shard_map/ppermute | solution.py:326
  15.5 39.2 %copy-start.4 = (s32[4,384]{1,0:T(4,128)S(1)}, s32[4,384]{1,0:T(4,128)}, u32[]{:S(2)}) copy-start(s32[4,384]{1,0:T(4,128)} %tokens.1) | copy-start | bytes 18436
  15.5 40.6 %copy-start = (bf16[8192,256]{1,0:T(8,128)(2,1)S(1)}, bf16[8192,256]{1,0:T(8,128)(2,1)}, u32[]{:S(2)}) copy-start(bf16[8192,256]{1,0:T(8,128)(2,1)} %head.3) | copy-start | bytes 12582916
  17.1 16.0 %collective-permute-start.6 = (bf16[288,1024]{1,0:T(8,128)(2,1)S(1)}, bf16[288,1024]{1,0:T(8,128)(2,1)S(1)}, u32[]{:S(2)}, u32[]{:S(2)}) collective-permute-start(bf16[288,1024]{1,0:T(8,128)(2,1)S(1)} %get-tuple-element.25.z), channel_id=1, source_target_pairs={{0,1},{1,0},{2,3},{3,2},{4,5},{5,4},{6,7},{7,6},{8,24},{9,25},{10,... | collective-permute-start | bytes 1769480 | tf_op jit(solution)/shard_map/ppermute | solution.py:326
  19.0 16.2 %collective-permute-start.7 = (bf16[288,1024]{1,0:T(8,128)(2,1)S(1)}, bf16[288,1024]{1,0:T(8,128)(2,1)S(1)}, u32[]{:S(2)}, u32[]{:S(2)}) collective-permute-start(bf16[288,1024]{1,0:T(8,128)(2,1)S(1)} %get-tuple-element.25.z), channel_id=1, source_target_pairs={{0,16},{1,17},{2,18},{3,19},{4,20},{5,21},{6,22},{7,23},{8,9},{9,8... | collective-permute-start | bytes 1769480 | tf_op jit(solution)/shard_map/ppermute | solution.py:326
  20.5 14.6 %collective-permute-start.12 = (bf16[256,1024]{1,0:T(8,128)(2,1)S(1)}, bf16[256,1024]{1,0:T(8,128)(2,1)S(1)}, u32[]{:S(2)}, u32[]{:S(2)}) collective-permute-start(bf16[256,1024]{1,0:T(8,128)(2,1)S(1)} %get-tuple-element.28), channel_id=1, source_target_pairs={{0,2},{1,3},{2,0},{3,1},{4,6},{5,7},{6,4},{7,5},{8,10},{9,11},{10,... | collective-permute-start | bytes 1572872 | tf_op jit(solution)/shard_map/ppermute | solution.py:326
  22.1 33.9 %collective-permute-start.13 = (bf16[288,1024]{1,0:T(8,128)(2,1)S(1)}, bf16[288,1024]{1,0:T(8,128)(2,1)S(1)}, u32[]{:S(2)}, u32[]{:S(2)}) collective-permute-start(bf16[288,1024]{1,0:T(8,128)(2,1)S(1)} %get-tuple-element.25.z), channel_id=1, source_target_pairs={{0,6},{1,7},{2,4},{3,5},{4,2},{5,3},{6,0},{7,1},{8,14},{9,15},{10,... | collective-permute-start | bytes 1769480 | tf_op jit(solution)/shard_map/ppermute | solution.py:326
  33.1 22.9 %collective-permute-start.8 = (bf16[288,1024]{1,0:T(8,128)(2,1)S(1)}, bf16[288,1024]{1,0:T(8,128)(2,1)S(1)}, u32[]{:S(2)}, u32[]{:S(2)}) collective-permute-start(bf16[288,1024]{1,0:T(8,128)(2,1)S(1)} %collective-permute-done.6.a), channel_id=1, source_target_pairs={{0,16},{1,17},{2,18},{3,19},{4,20},{5,21},{6,22},{7,23},{8,9},{9,8... | collective-permute-start | bytes 1769480 | tf_op jit(solution)/shard_map/ppermute | solution.py:326
  35.2 24.5 %collective-permute-start.14 = (bf16[256,1024]{1,0:T(8,128)(2,1)S(1)}, bf16[256,1024]{1,0:T(8,128)(2,1)S(1)}, u32[]{:S(2)}, u32[]{:S(2)}) collective-permute-start(bf16[256,1024]{1,0:T(8,128)(2,1)S(1)} %shard_map.80.z1), channel_id=1, source_target_pairs={{0,1},{1,0},{2,3},{3,2},{4,5},{5,4},{6,7},{7,6},{8,24},{9,25},{10,... | collective-permute-start | bytes 1572872 | tf_op jit(solution)/shard_map/ppermute | solution.py:326
  36.7 10.0 %collective-permute-start.4 = (f32[8,384]{1,0:T(8,128)S(1)}, f32[8,384]{1,0:T(8,128)S(1)}, u32[]{:S(2)}, u32[]{:S(2)}) collective-permute-start(f32[8,384]{1,0:T(8,128)S(1)} %get-tuple-element.24), channel_id=1, source_target_pairs={{0,1},{1,0},{2,3},{3,2},{4,5},{5,4},{6,7},{7,6},{8,9},{9,8},{10,11... | collective-permute-start | bytes 36872 | tf_op jit(solution)/shard_map/ppermute | solution.py:326
  46.7 3.7 %collective-permute-start.10 = (f32[8,384]{1,0:T(8,128)S(1)}, f32[8,384]{1,0:T(8,128)S(1)}, u32[]{:S(2)}, u32[]{:S(2)}) collective-permute-start(f32[8,384]{1,0:T(8,128)S(1)} %add.72.s0.sums), channel_id=1, source_target_pairs={{0,16},{8,24},{16,0},{24,8},{1,17},{9,25},{17,1},{25,9},{2,18},{10... | collective-permute-start | bytes 36872 | tf_op jit(solution)/shard_map/ppermute | solution.py:370
  50.4 3.1 %collective-permute-start.11 = (f32[8,384]{1,0:T(8,128)S(1)}, f32[8,384]{1,0:T(8,128)S(1)}, u32[]{:S(2)}, u32[]{:S(2)}) collective-permute-start(f32[8,384]{1,0:T(8,128)S(1)} %add.72.s0.sums), channel_id=1, source_target_pairs={{0,24},{8,16},{16,8},{24,0},{1,25},{9,17},{17,9},{25,1},{2,26},{10... | collective-permute-start | bytes 36872 | tf_op jit(solution)/shard_map/ppermute | solution.py:370
  53.5 1.2 collective-permute-start.9
  57.7 9.2 %collective-permute-start.15 = (bf16[256,1024]{1,0:T(8,128)(2,1)S(1)}, bf16[256,1024]{1,0:T(8,128)(2,1)S(1)}, u32[]{:S(2)}, u32[]{:S(2)}) collective-permute-start(bf16[256,1024]{1,0:T(8,128)(2,1)S(1)} %get-tuple-element.30.refs_3_), channel_id=1, source_target_pairs={{0,16},{1,17},{2,18},{3,19},{4,20},{5,21},{6,22},{7,23},{8,9},{9,8... | collective-permute-start | bytes 1572872 | tf_op jit(solution)/shard_map/ppermute | solution.py:326
  58.0 14.4 %collective-permute-start.17 = (bf16[256,1024]{1,0:T(8,128)(2,1)S(1)}, bf16[256,1024]{1,0:T(8,128)(2,1)S(1)}, u32[]{:S(2)}, u32[]{:S(2)}) collective-permute-start(bf16[256,1024]{1,0:T(8,128)(2,1)S(1)} %get-tuple-element.31.value), channel_id=1, source_target_pairs={{0,2},{1,3},{2,0},{3,1},{4,6},{5,7},{6,4},{7,5},{8,10},{9,11},{10,... | collective-permute-start | bytes 1572872 | tf_op jit(solution)/shard_map/ppermute | solution.py:326
  59.7 14.0 %collective-permute-start.16 = (bf16[256,1024]{1,0:T(8,128)(2,1)S(1)}, bf16[256,1024]{1,0:T(8,128)(2,1)S(1)}, u32[]{:S(2)}, u32[]{:S(2)}) collective-permute-start(bf16[256,1024]{1,0:T(8,128)(2,1)S(1)} %collective-permute-done.14.refs_4_), channel_id=1, source_target_pairs={{0,16},{1,17},{2,18},{3,19},{4,20},{5,21},{6,22},{7,23},{8,9},{9,8... | collective-permute-start | bytes 1572872 | tf_op jit(solution)/shard_map/ppermute | solution.py:326
  72.5 14.0 %collective-permute-start.18 = (bf16[256,1024]{1,0:T(8,128)(2,1)S(1)}, bf16[256,1024]{1,0:T(8,128)(2,1)S(1)}, u32[]{:S(2)}, u32[]{:S(2)}) collective-permute-start(bf16[256,1024]{1,0:T(8,128)(2,1)S(1)} %shard_map.82.refs_7_), channel_id=1, source_target_pairs={{0,1},{1,0},{2,3},{3,2},{4,5},{5,4},{6,7},{7,6},{8,24},{9,25},{10,... | collective-permute-start | bytes 1572872 | tf_op jit(solution)/shard_map/ppermute | solution.py:326
  75.2 11.6 %collective-permute-start.19 = (bf16[256,1024]{1,0:T(8,128)(2,1)S(1)}, bf16[256,1024]{1,0:T(8,128)(2,1)S(1)}, u32[]{:S(2)}, u32[]{:S(2)}) collective-permute-start(bf16[256,1024]{1,0:T(8,128)(2,1)S(1)} %get-tuple-element.34.refs_3_), channel_id=1, source_target_pairs={{0,16},{1,17},{2,18},{3,19},{4,20},{5,21},{6,22},{7,23},{8,9},{9,8... | collective-permute-start | bytes 1572872 | tf_op jit(solution)/shard_map/ppermute | solution.py:326
  86.5 25.9 %collective-permute-start.20 = (bf16[256,1024]{1,0:T(8,128)(2,1)S(1)}, bf16[256,1024]{1,0:T(8,128)(2,1)S(1)}, u32[]{:S(2)}, u32[]{:S(2)}) collective-permute-start(bf16[256,1024]{1,0:T(8,128)(2,1)S(1)} %collective-permute-done.18.refs_4_), channel_id=1, source_target_pairs={{0,16},{1,17},{2,18},{3,19},{4,20},{5,21},{6,22},{7,23},{8,9},{9,8... | collective-permute-start | bytes 1572872 | tf_op jit(solution)/shard_map/ppermute | solution.py:326
  86.8 28.3 %collective-permute-start.23 = (bf16[256,1024]{1,0:T(8,128)(2,1)S(1)}, bf16[256,1024]{1,0:T(8,128)(2,1)S(1)}, u32[]{:S(2)}, u32[]{:S(2)}) collective-permute-start(bf16[256,1024]{1,0:T(8,128)(2,1)S(1)} %shard_map.84.refs_9_), channel_id=1, source_target_pairs={{0,1},{1,0},{2,3},{3,2},{4,5},{5,4},{6,7},{7,6},{8,24},{9,25},{10,... | collective-permute-start | bytes 1572872 | tf_op jit(solution)/shard_map/ppermute | solution.py:326
  88.2 13.3 %collective-permute-start.21 = (bf16[128,1024]{1,0:T(8,128)(2,1)S(1)}, bf16[128,1024]{1,0:T(8,128)(2,1)S(1)}, u32[]{:S(2)}, u32[]{:S(2)}) collective-permute-start(bf16[128,1024]{1,0:T(8,128)(2,1)S(1)} %get-tuple-element.35), channel_id=1, source_target_pairs={{0,2},{1,3},{2,0},{3,1},{4,6},{5,7},{6,4},{7,5},{8,10},{9,11},{10,... | collective-permute-start | bytes 786440 | tf_op jit(solution)/shard_map/ppermute | solution.py:326
  89.3 23.1 %collective-permute-start.22 = (bf16[128,1024]{1,0:T(8,128)(2,1)S(1)}, bf16[128,1024]{1,0:T(8,128)(2,1)S(1)}, u32[]{:S(2)}, u32[]{:S(2)}) collective-permute-start(bf16[128,1024]{1,0:T(8,128)(2,1)S(1)} %get-tuple-element.35), channel_id=1, source_target_pairs={{0,6},{1,7},{2,4},{3,5},{4,2},{5,3},{6,0},{7,1},{8,14},{9,15},{10,... | collective-permute-start | bytes 786440 | tf_op jit(solution)/shard_map/ppermute | solution.py:326
  114.6 9.2 %collective-permute-start.24 = (bf16[256,1024]{1,0:T(8,128)(2,1)S(1)}, bf16[256,1024]{1,0:T(8,128)(2,1)S(1)}, u32[]{:S(2)}, u32[]{:S(2)}) collective-permute-start(bf16[256,1024]{1,0:T(8,128)(2,1)S(1)} %get-tuple-element.37.z), channel_id=1, source_target_pairs={{0,16},{1,17},{2,18},{3,19},{4,20},{5,21},{6,22},{7,23},{8,9},{9,8... | collective-permute-start | bytes 1572872 | tf_op jit(solution)/shard_map/ppermute | solution.py:326
  115.1 14.4 %collective-permute-start.26 = (bf16[256,1024]{1,0:T(8,128)(2,1)S(1)}, bf16[256,1024]{1,0:T(8,128)(2,1)S(1)}, u32[]{:S(2)}, u32[]{:S(2)}) collective-permute-start(bf16[256,1024]{1,0:T(8,128)(2,1)S(1)} %collective-permute-done.23.a), channel_id=1, source_target_pairs={{0,16},{1,17},{2,18},{3,19},{4,20},{5,21},{6,22},{7,23},{8,9},{9,8... | collective-permute-start | bytes 1572872 | tf_op jit(solution)/shard_map/ppermute | solution.py:326
  116.7 6.4 %collective-permute-start.25 = (bf16[128,1024]{1,0:T(8,128)(2,1)S(1)}, bf16[128,1024]{1,0:T(8,128)(2,1)S(1)}, u32[]{:S(2)}, u32[]{:S(2)}) collective-permute-start(bf16[128,1024]{1,0:T(8,128)(2,1)S(1)} %get-tuple-element.38), channel_id=1, source_target_pairs={{0,2},{1,3},{2,0},{3,1},{4,6},{5,7},{6,4},{7,5},{8,10},{9,11},{10,... | collective-permute-start | bytes 786440 | tf_op jit(solution)/shard_map/ppermute | solution.py:326
  130.2 4.5 %collective-permute-start.27 = (f32[8,640]{1,0:T(8,128)S(1)}, f32[8,640]{1,0:T(8,128)S(1)}, u32[]{:S(2)}, u32[]{:S(2)}) collective-permute-start(f32[8,640]{1,0:T(8,128)S(1)} %shard_map.87), channel_id=1, source_target_pairs={{0,2},{1,3},{2,0},{3,1},{4,6},{5,7},{6,4},{7,5},{8,10},{9,11},{10,... | collective-permute-start | bytes 61448 | tf_op jit(solution)/shard_map/ppermute | solution.py:326
  130.9 4.7 %collective-permute-start.28 = (f32[8,640]{1,0:T(8,128)S(1)}, f32[8,640]{1,0:T(8,128)S(1)}, u32[]{:S(2)}, u32[]{:S(2)}) collective-permute-start(f32[8,640]{1,0:T(8,128)S(1)} %shard_map.87), channel_id=1, source_target_pairs={{0,4},{1,5},{2,6},{3,7},{4,0},{5,1},{6,2},{7,3},{8,12},{9,13},{10,... | collective-permute-start | bytes 61448 | tf_op jit(solution)/shard_map/ppermute | solution.py:326
  132.4 5.6 %collective-permute-start.29 = (f32[8,640]{1,0:T(8,128)S(1)}, f32[8,640]{1,0:T(8,128)S(1)}, u32[]{:S(2)}, u32[]{:S(2)}) collective-permute-start(f32[8,640]{1,0:T(8,128)S(1)} %shard_map.87), channel_id=1, source_target_pairs={{0,6},{1,7},{2,4},{3,5},{4,2},{5,3},{6,0},{7,1},{8,14},{9,15},{10,... | collective-permute-start | bytes 61448 | tf_op jit(solution)/shard_map/ppermute | solution.py:326
  138.0 3.8 %collective-permute-start.30 = (f32[8,640]{1,0:T(8,128)S(1)}, f32[8,640]{1,0:T(8,128)S(1)}, u32[]{:S(2)}, u32[]{:S(2)}) collective-permute-start(f32[8,640]{1,0:T(8,128)S(1)} %maximum_maximum_fusion), channel_id=1, source_target_pairs={{0,1},{1,0},{2,3},{3,2},{4,5},{5,4},{6,7},{7,6},{8,9},{9,8},{10,11... | collective-permute-start | bytes 61448 | tf_op jit(solution)/shard_map/ppermute | solution.py:326
  139.6 3.8 %collective-permute-start.31 = (f32[8,640]{1,0:T(8,128)S(1)}, f32[8,640]{1,0:T(8,128)S(1)}, u32[]{:S(2)}, u32[]{:S(2)}) collective-permute-start(f32[8,640]{1,0:T(8,128)S(1)} %maximum_maximum_fusion), channel_id=1, source_target_pairs={{0,16},{1,17},{2,18},{3,19},{4,20},{5,21},{6,22},{7,23},{8,24},{9,... | collective-permute-start | bytes 61448 | tf_op jit(solution)/shard_map/ppermute | solution.py:326
  140.1 4.7 %collective-permute-start.32 = (f32[8,640]{1,0:T(8,128)S(1)}, f32[8,640]{1,0:T(8,128)S(1)}, u32[]{:S(2)}, u32[]{:S(2)}) collective-permute-start(f32[8,640]{1,0:T(8,128)S(1)} %maximum_maximum_fusion), channel_id=1, source_target_pairs={{0,17},{1,16},{2,19},{3,18},{4,21},{5,20},{6,23},{7,22},{8,25},{9,... | collective-permute-start | bytes 61448 | tf_op jit(solution)/shard_map/ppermute | solution.py:326
  144.9 1.3 collective-permute-start.33

commit v6 on v5

--- a/solution.py
+++ b/solution.py
@@ -15,7 +15,6 @@
 VMEM = pl.BlockSpec(memory_space=pltpu.VMEM)
 SMEM = pl.BlockSpec(memory_space=pltpu.SMEM)
 ANY = pl.BlockSpec(memory_space=pl.ANY)
-HBM = pl.BlockSpec(memory_space=pltpu.HBM)
 
 
 def row_map(lengths, pair, core, index, count):
@@ -45,14 +44,23 @@
 
 
 def sum_kernel(rows, gain, reward, lengths, out):
+    _, core, _ = here()
     value = rows[...].astype(F32)
     scaled = (value * gain[...].astype(F32)).astype(BF16).astype(F32)
     squares = jnp.sum(value * value, axis=1, keepdims=True)
     rewards = jnp.sum(scaled * reward[...].astype(F32), axis=1, keepdims=True)
-    out[...] = as_rows([squares, rewards], rows.shape[0])
-
-
-def pick_kernel(count, lengths, rows, sibling, extra, gain, sums, received, full, big, sums_out):
+    zero = jnp.zeros(squares.shape, F32)
+    first = core == 0
+    columns = [
+        jnp.where(first, squares, zero),
+        jnp.where(first, zero, squares),
+        jnp.where(first, rewards, zero),
+        jnp.where(first, zero, rewards),
+    ]
+    out[...] = as_rows(columns, rows.shape[0])
+
+
+def pick_kernel(count, lengths, rows, sibling, extra, gain, s0, s1, s2, s3, full, sums_out):
     section = lax.axis_index("section")
     core, pair = lax.rem(section, 2), lax.div(section, 2)
     positions, half = rows.shape[0], extra.shape[0]
@@ -67,14 +75,12 @@
     picked += jnp.dot(pick[:, 2 * positions :], extra[...], preferred_element_type=F32)
     scaled = (picked * gain[...].astype(F32)).astype(BF16)
     full[...] = scaled
-    big[...] = scaled[: big.shape[0]]
-    sums_out[...] = sums[...] + received[...]
-
-
-def row_kernel(count, width, lengths, tokens, s0, s1, s2, s3, ids, scales):
-    section, core, _ = here()
+    sums_out[...] = s0[...] + s1[...] + s2[...] + s3[...]
+
+
+def row_kernel(count, width, lengths, tokens, near, across, ids, scales):
+    _, core, own_pair = here()
     spans, positions = tokens.shape
-    by_move = (s0, s1, s2, s3)
     for pair in range(2):
         index = lax.broadcasted_iota(I32, (count, 1), 0)
         span, place = row_map(lengths, pair, core, index, count)
@@ -83,8 +89,9 @@
         squares = jnp.zeros((count, positions), F32)
         for s in range(spans):
             found = jnp.where(span == s, tokens[s : s + 1, :].astype(F32), found)
-        for move in range(spans):
-            squares = jnp.where(span == jnp.bitwise_xor(section, move), by_move[move][0:1, :], squares)
+            row = s % 2
+            value = jnp.where(own_pair == s // 2, near[row : row + 1, :], across[row : row + 1, :])
+            squares = jnp.where(span == s, value, squares)
         hit = lane == place
         found = jnp.sum(jnp.where(hit, found, F32(0.0)), axis=1, keepdims=True)
         squares = jnp.sum(jnp.where(hit, squares, F32(0.0)), axis=1, keepdims=True)
@@ -119,31 +126,18 @@
     return jnp.concatenate(out, axis=1)
 
 
-def small_terms(w, head, sibling, k):
-    m2 = w.shape[0] // 2
-    depth = w.shape[1]
-    return products(
-        [(w[:m2, :], weights(head, sibling, depth, k, False)), (w[m2:, :], weights(head, sibling, depth, k, True))]
-    )
-
-
-def first_kernel(n, head, sibling, z, a, b, c, ids, scales, z1, z3, acc, ids_out, scales_out, w0, z1_out, z3_out):
+def first_kernel(head, sibling, z, a, b, c, ids, scales, z1, z3, after, acc, ids_out, scales_out, z1_out, z3_out):
     count, depth = z.shape
-    m = count - n
     _, core, _ = here()
     mine, others = blocks(count)
     near = weights(head, sibling, depth, 0, False)
     far = weights(head, sibling, depth, 0, True)
-    w0[:m, :] = z[n:, :]
-    w0[3 * m :, :] = c[n:, :]
     for which, same, cross in ((0, a, b), (1, b, a)):
 
         @pl.when(core == which)
         def _():
             acc[pl.ds(mine, count), :] = products([(z[...], near), (same[...], far)])
             acc[pl.ds(others, count), :] = products([(cross[...], near), (c[...], far)])
-            w0[m : 2 * m, :] = cross[n:, :]
-            w0[2 * m : 3 * m, :] = same[n:, :]
 
     ids_out[...] = ids[...]
     scales_out[...] = scales[...]
@@ -151,17 +145,8 @@
     z3_out[...] = z3[...]
 
 
-def stage_kernel(k, small_k, n_pass, *refs):
-    refs = list(refs)
-    n_small = len(small_k)
-    head, sibling, acc_in, z, a, b, c = refs[:7]
-    smalls = refs[7 : 7 + n_small]
-    passed = refs[7 + n_small : 7 + n_small + n_pass]
-    acc = refs[7 + n_small + n_pass]
-    outs = refs[8 + n_small + n_pass :]
-    n, depth = z.shape
-    count = acc.shape[0] // 2
-    m = count - n
+def stage_kernel(k, head, sibling, acc_in, z, a, b, passed, acc, out):
+    count, depth = z.shape
     _, core, _ = here()
     mine, others = blocks(count)
     near = weights(head, sibling, depth, k, False)
@@ -170,20 +155,12 @@
 
         @pl.when(core == which)
         def _():
-            rows = pl.ds(mine, n)
+            rows = pl.ds(mine, count)
             acc[rows, :] = acc_in[rows, :] + products([(z[...], near), (same[...], far)])
-            rows = pl.ds(others, n)
-            acc[rows, :] = acc_in[rows, :] + products([(cross[...], near), (c[...], far)])
-
-    values = [small_terms(w, head, sibling, w_k) for w, w_k in zip(smalls, small_k)]
-    for i, base in enumerate((mine, others)):
-        rows = pl.ds(pl.multiple_of(base + n, 16), m)
-        value = acc_in[rows, :]
-        for v in values:
-            value = value + v[i * m : (i + 1) * m]
-        acc[rows, :] = value
-    for out, value in zip(outs, passed):
-        out[...] = value[...]
+            rows = pl.ds(others, count)
+            acc[rows, :] = acc_in[rows, :] + products([(cross[...], near)])
+
+    out[...] = passed[...]
 
 
 def gate_kernel(value, *refs):
@@ -208,43 +185,38 @@
     return jnp.where(lane == 0, top, jnp.where(lane == 1, total, jnp.where(lane == 2, target, F32(0.0))))
 
 
-def own_kernel(k, head, sibling, acc_in, z, a, b, w, token_ids, scales, left, far_out, wide):
-    n, depth = z.shape
-    count = acc_in.shape[0] // 2
-    m = count - n
+def own_kernel(head, sibling, acc_in, z, a, b, c1, c3, token_ids, scales, left, far_out, wide):
+    count, depth = z.shape
     _, core, _ = here()
     mine, others = blocks(count)
-    near = weights(head, sibling, depth, k, False)
-    far = weights(head, sibling, depth, k, True)
+    near = weights(head, sibling, depth, 2, False)
+    far = weights(head, sibling, depth, 2, True)
     block = head.shape[1]
     far_out[:, :block] = far[0]
     far_out[:, block:] = far[1]
     ids = column_ids(block)
+    far1 = weights(head, sibling, depth, 1, True)
+    far3 = weights(head, sibling, depth, 3, True)
     wide[...] = jnp.zeros(wide.shape, F32)
     for which, same, cross in ((0, a, b), (1, b, a)):
 
         @pl.when(core == which)
         def _():
-            rows = pl.ds(mine, n)
+            rows = pl.ds(mine, count)
             logits = acc_in[rows, :] + products([(z[...], near), (same[...], far)])
             wide[rows, :] = summary(logits, scales[rows, :], token_ids[rows, :], ids)
-            left[...] = acc_in[pl.ds(others, n), :] + products([(cross[...], near)])
-
-    value = small_terms(w, head, sibling, k)
-    for i, base in enumerate((mine, others)):
-        rows = pl.ds(pl.multiple_of(base + n, 16), m)
-        logits = acc_in[rows, :] + value[i * m : (i + 1) * m]
-        wide[rows, :] = summary(logits, scales[rows, :], token_ids[rows, :], ids)
+            left[...] = acc_in[pl.ds(others, count), :] + products(
+                [(cross[...], near), (c1[...], far1), (c3[...], far3)]
+            )
 
 
 def last_kernel(far, left, c, wide_in, token_ids, scales, out, wide):
-    n = c.shape[0]
-    count = token_ids.shape[0] // 2
+    count = c.shape[0]
     _, others = blocks(count)
     ids = column_ids(far.shape[1] // 2)
     wide[...] = wide_in[...]
     logits = left[...] + jnp.dot(c[...], far[...], preferred_element_type=F32)
-    rows = pl.ds(others, n)
+    rows = pl.ds(others, count)
     wide[rows, :] = summary(logits, scales[rows, :], token_ids[rows, :], ids)
     out[...] = jnp.transpose(wide[...])[:8]
 
@@ -272,7 +244,9 @@
             logprob += jnp.sum(jnp.where(hit, value, F32(0.0)), axis=0, keepdims=True)
     out_ref[...] = logprob
     length = lengths[section]
-    reward = sums[1:2, :] * lax.rsqrt(sums[0:1, :] / width + 1e-05)
+    first = lax.rem(section, 2) == 0
+    squares = jnp.where(first, sums[0:1, :], sums[1:2, :])
+    reward = jnp.where(first, sums[2:3, :], sums[3:4, :]) * lax.rsqrt(squares / width + 1e-05)
     score = jnp.sum(jnp.where(where < length, reward, F32(0.0)), axis=1, keepdims=True)
     score_ref[...] = score / length.astype(F32)
 
@@ -310,8 +284,6 @@
     block, width, part = head.shape[1], head.shape[0], hidden.shape[2]
     count = 3 * spans * positions // 4 // sections
     half = positions // 2
-    big = (count * 8 // 9) // 16 * 16
-    small = count - big
     rows = hidden[0]
     gain = norm_gain[None]
 
@@ -334,7 +306,6 @@
 
     swap = [(s, s ^ 1) for s in range(sections)]
     over = [(s, s ^ 2) for s in range(sections)]
-    across = [(s, s ^ 3) for s in range(sections)]
     extra = lax.ppermute(rows[half:], "section", [(1, 3), (3, 1)])
     sibling = lax.ppermute(rows, "section", swap)
     head_sibling = lax.ppermute(head, "section", swap)
@@ -345,29 +316,25 @@
         [VMEM] * 3 + [SMEM],
         (rows, gain, reward_head[None], lengths),
     )
+    sums = sums + lax.ppermute(sums, "section", swap)
     if groups == 8:
-        sums = sums + send(sums, perm_z[1])
-        received = send(sums, perm_z[2])
+        parts = (sums,) + tuple(send(sums, perm_z[k]) for k in (1, 2, 3))
     else:
         sums = lax.psum(sums, "dp")
-        received = jnp.zeros_like(sums)
-    full, g, sums = call(
+        parts = (sums,) + (jnp.zeros_like(sums),) * 3
+    full, sums = call(
         functools.partial(pick_kernel, count),
-        [
-            jax.ShapeDtypeStruct((count, part), BF16),
-            jax.ShapeDtypeStruct((big, part), BF16),
-            like(sums),
-        ],
-        [SMEM] + [VMEM] * 6,
-        (lengths, rows, sibling, extra, gain, sums, received),
+        [jax.ShapeDtypeStruct((count, part), BF16), like(sums)],
+        [SMEM] + [VMEM] * 8,
+        (lengths, rows, sibling, extra, gain) + parts,
     )
     if groups == 8:
         sums = sums + send(sums, perm_x)
     token_ids, scales = call(
         functools.partial(row_kernel, count, width),
         [ids_shape, scales_shape],
-        [SMEM] + [VMEM] * 5,
-        (lengths, tokens, sums) + tuple(lax.ppermute(sums, "section", p) for p in (swap, over, across)),
+        [SMEM] + [VMEM] * 3,
+        (lengths, tokens, sums, lax.ppermute(sums, "section", over)),
     )
 
     if groups == 8:
@@ -377,53 +344,45 @@
         def gate(value, *after):
             return call(gate_kernel, like(value), [VMEM] + [ANY] * len(after), (value,) + after)
 
-        def stage(k, acc, pieces, smalls, passed):
-            args = (head, head_sibling, acc) + pieces + tuple(smalls.values()) + passed
-            return call(
-                functools.partial(stage_kernel, k, tuple(smalls), len(passed)),
-                [acc_shape] + [like(p) for p in passed],
-                [VMEM] * len(args),
-                args,
-            )
-
-        z1 = send(g, perm_z[1])
-        z3 = send(full, perm_z[3])[:big]
+        def stage(k, acc, pieces, passed):
+            args = (head, head_sibling, acc) + pieces + (passed,)
+            return call(functools.partial(stage_kernel, k), [acc_shape, like(passed)], [VMEM] * len(args), args)
+
+        z1 = send(full, perm_z[1])
+        z3 = send(full, perm_z[3])
         a0 = send(full, perm_a)
         b0 = send(full, perm_b)
         c0 = send(a0, perm_b)
         z1 = gate(z1, b0)
         a1 = send(z1, perm_a)
-        acc, token_ids, scales, w0, z1, z3 = call(
-            functools.partial(first_kernel, big),
-            [acc_shape, ids_shape, scales_shape, jax.ShapeDtypeStruct((4 * small, part), BF16), like(z1), like(z3)],
-            [VMEM] * 10,
-            (head, head_sibling, full, a0, b0, c0, token_ids, scales, z1, z3),
+        acc, token_ids, scales, z1, z3 = call(
+            first_kernel,
+            [acc_shape, ids_shape, scales_shape, like(z1), like(z3)],
+            [VMEM] * 10 + [ANY],
+            (head, head_sibling, full, a0, b0, c0, token_ids, scales, z1, z3, a1),
         )
         b1 = send(z1, perm_b)
+        a3 = send(z3, perm_a)
         z2 = send(z3, perm_z[1])
-        c1 = send(a1, perm_b)
-        z3 = gate(z3, b1, z2)
-        a3 = send(z3, perm_a)
-        acc, z3, w0 = stage(1, acc, (z1, a1, b1, c1), {}, (z3, w0))
+        acc, z3 = stage(1, acc, (z1, a1, b1), z3)
         b3 = send(z3, perm_b)
-        w3 = send(w0, perm_z[3])
-        w1 = send(w0, perm_z[1])
+        z2 = gate(z2, a3)
+        a2 = send(z2, perm_a)
+        acc, a3 = stage(3, acc, (z3, a3, b3), a3)
         c3 = send(a3, perm_b)
-        z2 = gate(z2, b3)
-        a2 = send(z2, perm_a)
-        acc, z2, w3 = stage(3, acc, (z3, a3, b3, c3), {1: w1, 3: w3}, (z2, w3))
+        c1 = send(c0, perm_z[1])
+        z2 = gate(z2, a2)
         b2 = send(z2, perm_b)
-        w2 = send(w3, perm_z[1])
         c2 = send(a2, perm_b)
         left, far, wide = call(
-            functools.partial(own_kernel, 2),
+            own_kernel,
             [
-                jax.ShapeDtypeStruct((big, 2 * block), F32),
+                jax.ShapeDtypeStruct((count, 2 * block), F32),
                 jax.ShapeDtypeStruct((part, 2 * block), BF16),
                 jax.ShapeDtypeStruct((up(2 * count), LANES), F32),
             ],
-            [VMEM] * 9,
-            (head, head_sibling, acc, z2, a2, b2, w2, token_ids, scales),
+            [VMEM] * 10,
+            (head, head_sibling, acc, z2, a2, b2, c1, c3, token_ids, scales),
         )
         stats = call(
             last_kernel,

time: 148 us -> 146 us (0.986)
  waiting for transfers between devices: 80.1 us -> 65.4 us
  starting transfers between devices: 49.7 us -> 63.5 us
    ppermute x27 -> x25, waiting for transfers between devices: 71.2 us -> 60.6 us  [per_device(): send = lambda value, perm: lax.ppermute(value, AXES, perm)]
    ppermute x27 -> x25, starting transfers between devices: 48.1 us -> 57.1 us  [per_device(): send = lambda value, perm: lax.ppermute(value, AXES, perm)]
    ppermute x3 -> x2, starting transfers between devices: 0.22 us -> 5.09 us  [the longest x1 4.01 us: per_device(): sums = sums + lax.ppermute(sums, 'section', swap)]
    ppermute x3 -> x2, waiting for transfers between devices: 7.77 us -> 3.62 us  [the longest x1 2.79 us: per_device(): lax.ppermute(sums, 'section', over)]
  transfers between devices with their start and end apart: 34 -> 31, of which waited for: 20 -> 20; matrix products, arithmetic and copies ran while one was open for 2% -> 2% of each run, Pallas kernels for 8% -> 6%
where the time goes in v6:
time: 146 us
  waiting for transfers between devices  65.4 us (45%)
  starting transfers between devices  63.5 us (43%)
  Pallas kernels  13.2 us (9%)
  local copies, waits for them, and re-layouts  3.15 us (2%)
    ppermute x25, waiting for transfers between devices, per_device(): send = lambda value, perm: lax.ppermute(value, AXES, perm)  60.6 us
    ppermute x25, starting transfers between devices, per_device(): send = lambda value, perm: lax.ppermute(value, AXES, perm)  57.1 us
    pallas_call x12, Pallas kernels, call(): pl.pallas_call(body, out_shape=outs, in_specs=in_specs, out_specs=[VMEM]...  13.2 us
    ppermute x1, starting transfers between devices, per_device(): sums = sums + lax.ppermute(sums, 'section', swap)  4.01 us
  transfers between devices with their start and end apart: 31, of which 20 were waited for; matrix products, arithmetic and copies ran while one was open for 2% of the time, Pallas kernels for 6%

profile of v6, /device:TPU:0, one launch (start us, length us, event | category | flops | bytes accessed | tf_op | source)
XLA Modules:
  0.0 146.3 jit_solution(15999549019825945999)
XLA Ops:
  1.2 1.0 slice_bitcast_fusion
  5.0 1.0 shard_map.77
  6.0 4.0 %collective-permute-start.2 = (f32[8,384]{1,0:T(8,128)S(1)}, f32[8,384]{1,0:T(8,128)S(1)}, u32[]{:S(2)}, u32[]{:S(2)}) collective-permute-start(f32[8,384]{1,0:T(8,128)S(1)} %shard_map.77), channel_id=1, source_target_pairs={{0,8},{8,0},{16,24},{24,16},{1,9},{9,1},{17,25},{25,17},{2,10},{10... | collective-permute-start | bytes 36872 | tf_op jit(solution)/shard_map/ppermute | solution.py:319
  10.1 0.8 collective-permute-done.2
  10.9 1.6 %collective-permute-start.3 = (f32[8,384]{1,0:T(8,128)S(1)}, f32[8,384]{1,0:T(8,128)S(1)}, u32[]{:S(2)}, u32[]{:S(2)}) collective-permute-start(f32[8,384]{1,0:T(8,128)S(1)} %add.71.s0), channel_id=1, source_target_pairs={{0,2},{1,3},{2,0},{3,1},{4,6},{5,7},{6,4},{7,5},{8,10},{9,11},{10,... | collective-permute-start | bytes 36872 | tf_op jit(solution)/shard_map/ppermute | solution.py:298
  12.5 2.6 %collective-permute-start.4 = (f32[8,384]{1,0:T(8,128)S(1)}, f32[8,384]{1,0:T(8,128)S(1)}, u32[]{:S(2)}, u32[]{:S(2)}) collective-permute-start(f32[8,384]{1,0:T(8,128)S(1)} %add.71.s0), channel_id=1, source_target_pairs={{0,4},{1,5},{2,6},{3,7},{4,0},{5,1},{6,2},{7,3},{8,12},{9,13},{10,... | collective-permute-start | bytes 36872 | tf_op jit(solution)/shard_map/ppermute | solution.py:298
  15.1 3.1 %collective-permute-start.5 = (f32[8,384]{1,0:T(8,128)S(1)}, f32[8,384]{1,0:T(8,128)S(1)}, u32[]{:S(2)}, u32[]{:S(2)}) collective-permute-start(f32[8,384]{1,0:T(8,128)S(1)} %add.71.s0), channel_id=1, source_target_pairs={{0,6},{1,7},{2,4},{3,5},{4,2},{5,3},{6,0},{7,1},{8,14},{9,15},{10,... | collective-permute-start | bytes 36872 | tf_op jit(solution)/shard_map/ppermute | solution.py:298
  18.2 2.4 %collective-permute-done.5.s3 = f32[8,384]{1,0:T(8,128)S(1)} collective-permute-done((f32[8,384]{1,0:T(8,128)S(1)}, f32[8,384]{1,0:T(8,128)S(1)}, u32[]{:S(2)}, u32[]{:S(2)}) %collective-permute-start.5) | collective-permute-done | bytes 12320 | tf_op jit(solution)/shard_map/ppermute | solution.py:298
  20.6 1.6 %shard_map.78 = (bf16[288,1024]{1,0:T(8,128)(2,1)S(1)}, f32[8,384]{1,0:T(8,128)S(1)}) custom-call(s32[4]{0:T(128)S(1)} %copy-done.3, bf16[384,1024]{1,0:T(8,128)(2,1)S(1)} %bitcast.10, bf16[384,1024]{1,0:T(8,128)(2,1)S(1)} %collective-permute-done.sibling, bf16[192,1024]{1,0:T(8,128)(2,1)S(1)} %collective-permute-done.1.extra, ...), custom_call_target="tpu_custom_call" | custom-call | tf_op jit(solution)/shard_map/pallas_call | solution.py:265
  22.2 1.6 %collective-permute-start.8 = (bf16[288,1024]{1,0:T(8,128)(2,1)S(1)}, bf16[288,1024]{1,0:T(8,128)(2,1)S(1)}, u32[]{:S(2)}, u32[]{:S(2)}) collective-permute-start(bf16[288,1024]{1,0:T(8,128)(2,1)S(1)} %get-tuple-element.21.z), channel_id=1, source_target_pairs={{0,1},{1,0},{2,3},{3,2},{4,5},{5,4},{6,7},{7,6},{8,24},{9,25},{10,... | collective-permute-start | bytes 1769480 | tf_op jit(solution)/shard_map/ppermute | solution.py:298
  23.7 1.1 collective-permute-start.9
  24.8 3.1 %collective-permute-start.13 = (bf16[288,1024]{1,0:T(8,128)(2,1)S(1)}, bf16[288,1024]{1,0:T(8,128)(2,1)S(1)}, u32[]{:S(2)}, u32[]{:S(2)}) collective-permute-start(bf16[288,1024]{1,0:T(8,128)(2,1)S(1)} %get-tuple-element.21.z), channel_id=1, source_target_pairs={{0,6},{1,7},{2,4},{3,5},{4,2},{5,3},{6,0},{7,1},{8,14},{9,15},{10,... | collective-permute-start | bytes 1769480 | tf_op jit(solution)/shard_map/ppermute | solution.py:298
  28.0 9.6 %collective-permute-done.8.a = bf16[288,1024]{1,0:T(8,128)(2,1)S(1)} collective-permute-done((bf16[288,1024]{1,0:T(8,128)(2,1)S(1)}, bf16[288,1024]{1,0:T(8,128)(2,1)S(1)}, u32[]{:S(2)}, u32[]{:S(2)}) %collective-permute-start.8) | collective-permute-done | bytes 589856 | tf_op jit(solution)/shard_map/ppermute | solution.py:298
  37.6 1.9 %collective-permute-start.10 = (bf16[288,1024]{1,0:T(8,128)(2,1)S(1)}, bf16[288,1024]{1,0:T(8,128)(2,1)S(1)}, u32[]{:S(2)}, u32[]{:S(2)}) collective-permute-start(bf16[288,1024]{1,0:T(8,128)(2,1)S(1)} %collective-permute-done.8.a), channel_id=1, source_target_pairs={{0,16},{1,17},{2,18},{3,19},{4,20},{5,21},{6,22},{7,23},{8,9},{9,8... | collective-permute-start | bytes 1769480 | tf_op jit(solution)/shard_map/ppermute | solution.py:298
  39.5 1.1 collective-permute-done.12.value
  41.3 1.5 %collective-permute-start.6 = (f32[8,384]{1,0:T(8,128)S(1)}, f32[8,384]{1,0:T(8,128)S(1)}, u32[]{:S(2)}, u32[]{:S(2)}) collective-permute-start(f32[8,384]{1,0:T(8,128)S(1)} %get-tuple-element.20), channel_id=1, source_target_pairs={{0,1},{1,0},{2,3},{3,2},{4,5},{5,4},{6,7},{7,6},{8,9},{9,8},{10,11... | collective-permute-start | bytes 36872 | tf_op jit(solution)/shard_map/ppermute | solution.py:298
  42.7 8.0 %collective-permute-done.6 = f32[8,384]{1,0:T(8,128)S(1)} collective-permute-done((f32[8,384]{1,0:T(8,128)S(1)}, f32[8,384]{1,0:T(8,128)S(1)}, u32[]{:S(2)}, u32[]{:S(2)}) %collective-permute-start.6) | collective-permute-done | bytes 12320 | tf_op jit(solution)/shard_map/ppermute | solution.py:298
  50.7 1.1 collective-permute-start.11
  51.8 2.8 %collective-permute-done.11.across = f32[8,384]{1,0:T(8,128)S(1)} collective-permute-done((f32[8,384]{1,0:T(8,128)S(1)}, f32[8,384]{1,0:T(8,128)S(1)}, u32[]{:S(2)}, u32[]{:S(2)}) %collective-permute-start.11) | collective-permute-done | bytes 12320 | tf_op jit(solution)/shard_map/ppermute | solution.py:337
  54.6 1.3 shard_map.79
  56.0 1.6 %shard_map.81 = (f32[576,512]{1,0:T(8,128)S(1)}, s32[576,1]{1,0:T(8,128)S(1)}, f32[576,1]{1,0:T(8,128)S(1)}, bf16[288,1024]{1,0:T(8,128)(2,1)S(1)}, bf16[288,1024]{1,0:T(8,128)(2,1)S(1)}) custom-call(bf16[8192,256]{1,0:T(8,128)(2,1)S(1)} %copy-done, bf16[8192,256]{1,0:T(8,128)(2,1)S(1)} %collective-permute-done.7.sibling, ...), custom_call_target="tpu_custom_call" | custom-call | tf_op jit(solution)/shard_map/pallas_call | solution.py:265
  58.7 0.9 collective-permute-start.15
  59.6 10.3 %collective-permute-done.16.a.passed.refs_0_ = bf16[288,1024]{1,0:T(8,128)(2,1)S(1)} collective-permute-done((bf16[288,1024]{1,0:T(8,128)(2,1)S(1)}, bf16[288,1024]{1,0:T(8,128)(2,1)S(1)}, u32[]{:S(2)}, u32[]{:S(2)}) %collective-permute-start.16) | collective-permute-done | bytes 589856 | tf_op jit(solution)/shard_map/ppermute | solution.py:298
  69.9 2.0 %collective-permute-start.19 = (bf16[288,1024]{1,0:T(8,128)(2,1)S(1)}, bf16[288,1024]{1,0:T(8,128)(2,1)S(1)}, u32[]{:S(2)}, u32[]{:S(2)}) collective-permute-start(bf16[288,1024]{1,0:T(8,128)(2,1)S(1)} %shard_map.84.value), channel_id=1, source_target_pairs={{0,1},{1,0},{2,3},{3,2},{4,5},{5,4},{6,7},{7,6},{8,24},{9,25},{10,... | collective-permute-start | bytes 1769480 | tf_op jit(solution)/shard_map/ppermute | solution.py:298
  71.9 2.8 %collective-permute-done.15.b = bf16[288,1024]{1,0:T(8,128)(2,1)S(1)} collective-permute-done((bf16[288,1024]{1,0:T(8,128)(2,1)S(1)}, bf16[288,1024]{1,0:T(8,128)(2,1)S(1)}, u32[]{:S(2)}, u32[]{:S(2)}) %collective-permute-start.15) | collective-permute-done | bytes 589856 | tf_op jit(solution)/shard_map/ppermute | solution.py:298
  74.7 1.3 shard_map.82
  76.0 0.8 collective-permute-start.17
  76.8 1.8 %collective-permute-start.21 = (bf16[288,1024]{1,0:T(8,128)(2,1)S(1)}, bf16[288,1024]{1,0:T(8,128)(2,1)S(1)}, u32[]{:S(2)}, u32[]{:S(2)}) collective-permute-start(bf16[288,1024]{1,0:T(8,128)(2,1)S(1)} %collective-permute-done.10.c), channel_id=1, source_target_pairs={{0,2},{1,3},{2,0},{3,1},{4,6},{5,7},{6,4},{7,5},{8,10},{9,11},{10,... | collective-permute-start | bytes 1769480 | tf_op jit(solution)/shard_map/ppermute | solution.py:298
  78.6 4.4 %collective-permute-done.19.refs_0_.a = bf16[288,1024]{1,0:T(8,128)(2,1)S(1)} collective-permute-done((bf16[288,1024]{1,0:T(8,128)(2,1)S(1)}, bf16[288,1024]{1,0:T(8,128)(2,1)S(1)}, u32[]{:S(2)}, u32[]{:S(2)}) %collective-permute-start.19) | collective-permute-done | bytes 589856 | tf_op jit(solution)/shard_map/ppermute | solution.py:298
  83.0 1.3 collective-permute-start.20
  84.3 1.6 %collective-permute-done.17.b = bf16[288,1024]{1,0:T(8,128)(2,1)S(1)} collective-permute-done((bf16[288,1024]{1,0:T(8,128)(2,1)S(1)}, bf16[288,1024]{1,0:T(8,128)(2,1)S(1)}, u32[]{:S(2)}, u32[]{:S(2)}) %collective-permute-start.17) | collective-permute-done | bytes 589856 | tf_op jit(solution)/shard_map/ppermute | solution.py:298
  85.9 1.3 shard_map.83
  87.2 0.8 collective-permute-start.22
  88.0 1.3 collective-permute-start.23
  89.3 3.7 %collective-permute-done.20.b = bf16[288,1024]{1,0:T(8,128)(2,1)S(1)} collective-permute-done((bf16[288,1024]{1,0:T(8,128)(2,1)S(1)}, bf16[288,1024]{1,0:T(8,128)(2,1)S(1)}, u32[]{:S(2)}, u32[]{:S(2)}) %collective-permute-start.20) | collective-permute-done | bytes 589856 | tf_op jit(solution)/shard_map/ppermute | solution.py:298
  92.9 6.3 %collective-permute-done.22.c3 = bf16[288,1024]{1,0:T(8,128)(2,1)S(1)} collective-permute-done((bf16[288,1024]{1,0:T(8,128)(2,1)S(1)}, bf16[288,1024]{1,0:T(8,128)(2,1)S(1)}, u32[]{:S(2)}, u32[]{:S(2)}) %collective-permute-start.22) | collective-permute-done | bytes 589856 | tf_op jit(solution)/shard_map/ppermute | solution.py:298
  99.2 2.3 %shard_map.86 = (f32[288,512]{1,0:T(8,128)S(1)}, bf16[1024,512]{1,0:T(8,128)(2,1)S(1)}, f32[640,128]{1,0:T(8,128)S(1)}) custom-call(bf16[8192,256]{1,0:T(8,128)(2,1)S(1)} %copy-done, bf16[8192,256]{1,0:T(8,128)(2,1)S(1)} %collective-permute-done.7.sibling, f32[576,512]{1,0:T(8,128)S(1)} %get-tuple-element.29.acc_in, bf16[288,1024]{1,0:T(8,128)(2,1)S(1)} %shard_map.85.z, ...), custom_call_target="tpu_custom_call" | custom-call | tf_op jit(solution)/shard_map/pallas_call | solution.py:265
  101.5 4.0 %collective-permute-done.23.c = bf16[288,1024]{1,0:T(8,128)(2,1)S(1)} collective-permute-done((bf16[288,1024]{1,0:T(8,128)(2,1)S(1)}, bf16[288,1024]{1,0:T(8,128)(2,1)S(1)}, u32[]{:S(2)}, u32[]{:S(2)}) %collective-permute-start.23) | collective-permute-done | bytes 589856 | tf_op jit(solution)/shard_map/ppermute | solution.py:298
  106.3 25.9 %collective-permute-start.26 = (f32[8,640]{1,0:T(8,128)S(1)}, f32[8,640]{1,0:T(8,128)S(1)}, u32[]{:S(2)}, u32[]{:S(2)}) collective-permute-start(f32[8,640]{1,0:T(8,128)S(1)} %shard_map.87), channel_id=1, source_target_pairs={{0,6},{1,7},{2,4},{3,5},{4,2},{5,3},{6,0},{7,1},{8,14},{9,15},{10,... | collective-permute-start | bytes 61448 | tf_op jit(solution)/shard_map/ppermute | solution.py:298
  133.0 1.0 collective-permute-done.26
  134.0 2.9 %collective-permute-done.25 = f32[8,640]{1,0:T(8,128)S(1)} collective-permute-done((f32[8,640]{1,0:T(8,128)S(1)}, f32[8,640]{1,0:T(8,128)S(1)}, u32[]{:S(2)}, u32[]{:S(2)}) %collective-permute-start.25) | collective-permute-done | bytes 20512 | tf_op jit(solution)/shard_map/ppermute | solution.py:298
  137.1 1.1 collective-permute-start.29
  138.1 1.1 collective-permute-start.28
  139.3 1.3 collective-permute-start.27
  140.6 1.2 collective-permute-done.29
  142.0 1.1 collective-permute-done.27
  143.2 1.2 collective-permute-done.30
  144.4 1.9 %shard_map.88 = (f32[1,384]{1,0:T(1,128)}, f32[1,1]{1,0:T(1,128)}) custom-call(s32[4]{0:T(128)S(1)} %copy-done.3, f32[8,384]{1,0:T(8,128)S(1)} %add.72.near.sums, f32[2,8,640]{2,1,0:T(8,128)S(1)} %pad_maximum_fusion.stats), custom_call_target="tpu_custom_call" | custom-call | tf_op jit(solution)/shard_map/pallas_call | solution.py:265
  (49 shorter events, 7.2 us)
Async XLA Ops:
  0.6 3.7 %copy-start.1 = (bf16[1,384,1024]{2,1,0:T(8,128)(2,1)S(1)}, bf16[1,384,1024]{2,1,0:T(8,128)(2,1)}, u32[]{:S(2)}) copy-start(bf16[1,384,1024]{2,1,0:T(8,128)(2,1)} %param.6) | copy-start | bytes 2359300
  0.6 19.9 %copy-start.3 = (s32[4]{0:T(128)S(1)}, s32[4]{0:T(128)}, u32[]{:S(2)}) copy-start(s32[4]{0:T(128)} %lengths.7) | copy-start | bytes 52
  0.7 55.3 %collective-permute-start.7 = (bf16[8192,256]{1,0:T(8,128)(2,1)}, bf16[8192,256]{1,0:T(8,128)(2,1)S(1)}, u32[]{:S(2)}, u32[]{:S(2)}) collective-permute-start(bf16[8192,256]{1,0:T(8,128)(2,1)} %head.7), channel_id=1, source_target_pairs={{0,8},{8,0},{16,24},{24,16},{1,9},{9,1},{17,25},{25,17},{2,10},{10... | collective-permute-start | bytes 12582920 | tf_op jit(solution)/shard_map/ppermute | solution.py:311
  1.2 19.4 %collective-permute-start = (bf16[384,1024]{1,0:T(8,128)(2,1)}, bf16[384,1024]{1,0:T(8,128)(2,1)S(1)}, u32[]{:S(2)}, u32[]{:S(2)}) collective-permute-start(bf16[384,1024]{1,0:T(8,128)(2,1)} %bitcast.8), channel_id=1, source_target_pairs={{0,8},{8,0},{16,24},{24,16},{1,9},{9,1},{17,25},{25,17},{2,10},{10... | collective-permute-start | bytes 2359304 | tf_op jit(solution)/shard_map/ppermute | solution.py:310
  2.3 18.3 %collective-permute-start.1 = (bf16[192,1024]{1,0:T(8,128)(2,1)S(1)}, bf16[192,1024]{1,0:T(8,128)(2,1)S(1)}, u32[]{:S(2)}, u32[]{:S(2)}) collective-permute-start(bf16[192,1024]{1,0:T(8,128)(2,1)S(1)} %slice_bitcast_fusion), channel_id=1, source_target_pairs={{8,24},{24,8},{9,25},{25,9},{10,26},{26,10},{11,27},{27,11},{12,28... | collective-permute-start | bytes 1179656 | tf_op jit(solution)/shard_map/ppermute | solution.py:309
  4.3 0.7 copy-start.2
  5.0 50.9 %copy-start = (bf16[8192,256]{1,0:T(8,128)(2,1)S(1)}, bf16[8192,256]{1,0:T(8,128)(2,1)}, u32[]{:S(2)}) copy-start(bf16[8192,256]{1,0:T(8,128)(2,1)} %head.7) | copy-start | bytes 12582916
  6.0 4.8 %collective-permute-start.2 = (f32[8,384]{1,0:T(8,128)S(1)}, f32[8,384]{1,0:T(8,128)S(1)}, u32[]{:S(2)}, u32[]{:S(2)}) collective-permute-start(f32[8,384]{1,0:T(8,128)S(1)} %shard_map.77), channel_id=1, source_target_pairs={{0,8},{8,0},{16,24},{24,16},{1,9},{9,1},{17,25},{25,17},{2,10},{10... | collective-permute-start | bytes 36872 | tf_op jit(solution)/shard_map/ppermute | solution.py:319
  10.9 4.2 %collective-permute-start.3 = (f32[8,384]{1,0:T(8,128)S(1)}, f32[8,384]{1,0:T(8,128)S(1)}, u32[]{:S(2)}, u32[]{:S(2)}) collective-permute-start(f32[8,384]{1,0:T(8,128)S(1)} %add.71.s0), channel_id=1, source_target_pairs={{0,2},{1,3},{2,0},{3,1},{4,6},{5,7},{6,4},{7,5},{8,10},{9,11},{10,... | collective-permute-start | bytes 36872 | tf_op jit(solution)/shard_map/ppermute | solution.py:298
  12.5 5.7 %collective-permute-start.4 = (f32[8,384]{1,0:T(8,128)S(1)}, f32[8,384]{1,0:T(8,128)S(1)}, u32[]{:S(2)}, u32[]{:S(2)}) collective-permute-start(f32[8,384]{1,0:T(8,128)S(1)} %add.71.s0), channel_id=1, source_target_pairs={{0,4},{1,5},{2,6},{3,7},{4,0},{5,1},{6,2},{7,3},{8,12},{9,13},{10,... | collective-permute-start | bytes 36872 | tf_op jit(solution)/shard_map/ppermute | solution.py:298
  15.1 5.5 %collective-permute-start.5 = (f32[8,384]{1,0:T(8,128)S(1)}, f32[8,384]{1,0:T(8,128)S(1)}, u32[]{:S(2)}, u32[]{:S(2)}) collective-permute-start(f32[8,384]{1,0:T(8,128)S(1)} %add.71.s0), channel_id=1, source_target_pairs={{0,6},{1,7},{2,4},{3,5},{4,2},{5,3},{6,0},{7,1},{8,14},{9,15},{10,... | collective-permute-start | bytes 36872 | tf_op jit(solution)/shard_map/ppermute | solution.py:298
  22.2 32.4 %copy-start.4 = (s32[4,384]{1,0:T(4,128)S(1)}, s32[4,384]{1,0:T(4,128)}, u32[]{:S(2)}) copy-start(s32[4,384]{1,0:T(4,128)} %tokens.1) | copy-start | bytes 18436
  22.2 15.4 %collective-permute-start.8 = (bf16[288,1024]{1,0:T(8,128)(2,1)S(1)}, bf16[288,1024]{1,0:T(8,128)(2,1)S(1)}, u32[]{:S(2)}, u32[]{:S(2)}) collective-permute-start(bf16[288,1024]{1,0:T(8,128)(2,1)S(1)} %get-tuple-element.21.z), channel_id=1, source_target_pairs={{0,1},{1,0},{2,3},{3,2},{4,5},{5,4},{6,7},{7,6},{8,24},{9,25},{10,... | collective-permute-start | bytes 1769480 | tf_op jit(solution)/shard_map/ppermute | solution.py:298
  23.7 15.7 %collective-permute-start.9 = (bf16[288,1024]{1,0:T(8,128)(2,1)S(1)}, bf16[288,1024]{1,0:T(8,128)(2,1)S(1)}, u32[]{:S(2)}, u32[]{:S(2)}) collective-permute-start(bf16[288,1024]{1,0:T(8,128)(2,1)S(1)} %get-tuple-element.21.z), channel_id=1, source_target_pairs={{0,16},{1,17},{2,18},{3,19},{4,20},{5,21},{6,22},{7,23},{8,9},{9,8... | collective-permute-start | bytes 1769480 | tf_op jit(solution)/shard_map/ppermute | solution.py:298
  24.8 15.8 %collective-permute-start.12 = (bf16[288,1024]{1,0:T(8,128)(2,1)S(1)}, bf16[288,1024]{1,0:T(8,128)(2,1)S(1)}, u32[]{:S(2)}, u32[]{:S(2)}) collective-permute-start(bf16[288,1024]{1,0:T(8,128)(2,1)S(1)} %get-tuple-element.21.z), channel_id=1, source_target_pairs={{0,2},{1,3},{2,0},{3,1},{4,6},{5,7},{6,4},{7,5},{8,10},{9,11},{10,... | collective-permute-start | bytes 1769480 | tf_op jit(solution)/shard_map/ppermute | solution.py:298
  24.8 31.1 %collective-permute-start.13 = (bf16[288,1024]{1,0:T(8,128)(2,1)S(1)}, bf16[288,1024]{1,0:T(8,128)(2,1)S(1)}, u32[]{:S(2)}, u32[]{:S(2)}) collective-permute-start(bf16[288,1024]{1,0:T(8,128)(2,1)S(1)} %get-tuple-element.21.z), channel_id=1, source_target_pairs={{0,6},{1,7},{2,4},{3,5},{4,2},{5,3},{6,0},{7,1},{8,14},{9,15},{10,... | collective-permute-start | bytes 1769480 | tf_op jit(solution)/shard_map/ppermute | solution.py:298
  37.6 18.3 %collective-permute-start.10 = (bf16[288,1024]{1,0:T(8,128)(2,1)S(1)}, bf16[288,1024]{1,0:T(8,128)(2,1)S(1)}, u32[]{:S(2)}, u32[]{:S(2)}) collective-permute-start(bf16[288,1024]{1,0:T(8,128)(2,1)S(1)} %collective-permute-done.8.a), channel_id=1, source_target_pairs={{0,16},{1,17},{2,18},{3,19},{4,20},{5,21},{6,22},{7,23},{8,9},{9,8... | collective-permute-start | bytes 1769480 | tf_op jit(solution)/shard_map/ppermute | solution.py:298
  40.6 15.3 %collective-permute-start.14 = (bf16[288,1024]{1,0:T(8,128)(2,1)S(1)}, bf16[288,1024]{1,0:T(8,128)(2,1)S(1)}, u32[]{:S(2)}, u32[]{:S(2)}) collective-permute-start(bf16[288,1024]{1,0:T(8,128)(2,1)S(1)} %shard_map.80.z1), channel_id=1, source_target_pairs={{0,1},{1,0},{2,3},{3,2},{4,5},{5,4},{6,7},{7,6},{8,24},{9,25},{10,... | collective-permute-start | bytes 1769480 | tf_op jit(solution)/shard_map/ppermute | solution.py:298
  41.3 9.5 %collective-permute-start.6 = (f32[8,384]{1,0:T(8,128)S(1)}, f32[8,384]{1,0:T(8,128)S(1)}, u32[]{:S(2)}, u32[]{:S(2)}) collective-permute-start(f32[8,384]{1,0:T(8,128)S(1)} %get-tuple-element.20), channel_id=1, source_target_pairs={{0,1},{1,0},{2,3},{3,2},{4,5},{5,4},{6,7},{7,6},{8,9},{9,8},{10,11... | collective-permute-start | bytes 36872 | tf_op jit(solution)/shard_map/ppermute | solution.py:298
  50.7 3.9 %collective-permute-start.11 = (f32[8,384]{1,0:T(8,128)S(1)}, f32[8,384]{1,0:T(8,128)S(1)}, u32[]{:S(2)}, u32[]{:S(2)}) collective-permute-start(f32[8,384]{1,0:T(8,128)S(1)} %add.72.near.sums), channel_id=1, source_target_pairs={{0,16},{8,24},{16,0},{24,8},{1,17},{9,25},{17,1},{25,9},{2,18},{10... | collective-permute-start | bytes 36872 | tf_op jit(solution)/shard_map/ppermute | solution.py:337
  57.6 12.2 %collective-permute-start.16 = (bf16[288,1024]{1,0:T(8,128)(2,1)S(1)}, bf16[288,1024]{1,0:T(8,128)(2,1)S(1)}, u32[]{:S(2)}, u32[]{:S(2)}) collective-permute-start(bf16[288,1024]{1,0:T(8,128)(2,1)S(1)} %get-tuple-element.26.passed), channel_id=1, source_target_pairs={{0,1},{1,0},{2,3},{3,2},{4,5},{5,4},{6,7},{7,6},{8,24},{9,25},{10,... | collective-permute-start | bytes 1769480 | tf_op jit(solution)/shard_map/ppermute | solution.py:298
  58.2 11.7 %collective-permute-start.18 = (bf16[288,1024]{1,0:T(8,128)(2,1)S(1)}, bf16[288,1024]{1,0:T(8,128)(2,1)S(1)}, u32[]{:S(2)}, u32[]{:S(2)}) collective-permute-start(bf16[288,1024]{1,0:T(8,128)(2,1)S(1)} %get-tuple-element.26.passed), channel_id=1, source_target_pairs={{0,2},{1,3},{2,0},{3,1},{4,6},{5,7},{6,4},{7,5},{8,10},{9,11},{10,... | collective-permute-start | bytes 1769480 | tf_op jit(solution)/shard_map/ppermute | solution.py:298
  58.7 16.0 %collective-permute-start.15 = (bf16[288,1024]{1,0:T(8,128)(2,1)S(1)}, bf16[288,1024]{1,0:T(8,128)(2,1)S(1)}, u32[]{:S(2)}, u32[]{:S(2)}) collective-permute-start(bf16[288,1024]{1,0:T(8,128)(2,1)S(1)} %get-tuple-element.25.z), channel_id=1, source_target_pairs={{0,16},{1,17},{2,18},{3,19},{4,20},{5,21},{6,22},{7,23},{8,9},{9,8... | collective-permute-start | bytes 1769480 | tf_op jit(solution)/shard_map/ppermute | solution.py:298
  69.9 13.0 %collective-permute-start.19 = (bf16[288,1024]{1,0:T(8,128)(2,1)S(1)}, bf16[288,1024]{1,0:T(8,128)(2,1)S(1)}, u32[]{:S(2)}, u32[]{:S(2)}) collective-permute-start(bf16[288,1024]{1,0:T(8,128)(2,1)S(1)} %shard_map.84.value), channel_id=1, source_target_pairs={{0,1},{1,0},{2,3},{3,2},{4,5},{5,4},{6,7},{7,6},{8,24},{9,25},{10,... | collective-permute-start | bytes 1769480 | tf_op jit(solution)/shard_map/ppermute | solution.py:298
  76.0 9.9 %collective-permute-start.17 = (bf16[288,1024]{1,0:T(8,128)(2,1)S(1)}, bf16[288,1024]{1,0:T(8,128)(2,1)S(1)}, u32[]{:S(2)}, u32[]{:S(2)}) collective-permute-start(bf16[288,1024]{1,0:T(8,128)(2,1)S(1)} %get-tuple-element.28.z), channel_id=1, source_target_pairs={{0,16},{1,17},{2,18},{3,19},{4,20},{5,21},{6,22},{7,23},{8,9},{9,8... | collective-permute-start | bytes 1769480 | tf_op jit(solution)/shard_map/ppermute | solution.py:298
  76.8 12.5 %collective-permute-start.21 = (bf16[288,1024]{1,0:T(8,128)(2,1)S(1)}, bf16[288,1024]{1,0:T(8,128)(2,1)S(1)}, u32[]{:S(2)}, u32[]{:S(2)}) collective-permute-start(bf16[288,1024]{1,0:T(8,128)(2,1)S(1)} %collective-permute-done.10.c), channel_id=1, source_target_pairs={{0,2},{1,3},{2,0},{3,1},{4,6},{5,7},{6,4},{7,5},{8,10},{9,11},{10,... | collective-permute-start | bytes 1769480 | tf_op jit(solution)/shard_map/ppermute | solution.py:298
  83.0 9.9 %collective-permute-start.20 = (bf16[288,1024]{1,0:T(8,128)(2,1)S(1)}, bf16[288,1024]{1,0:T(8,128)(2,1)S(1)}, u32[]{:S(2)}, u32[]{:S(2)}) collective-permute-start(bf16[288,1024]{1,0:T(8,128)(2,1)S(1)} %shard_map.85.z), channel_id=1, source_target_pairs={{0,16},{1,17},{2,18},{3,19},{4,20},{5,21},{6,22},{7,23},{8,9},{9,8... | collective-permute-start | bytes 1769480 | tf_op jit(solution)/shard_map/ppermute | solution.py:298
  87.2 12.1 %collective-permute-start.22 = (bf16[288,1024]{1,0:T(8,128)(2,1)S(1)}, bf16[288,1024]{1,0:T(8,128)(2,1)S(1)}, u32[]{:S(2)}, u32[]{:S(2)}) collective-permute-start(bf16[288,1024]{1,0:T(8,128)(2,1)S(1)} %get-tuple-element.30), channel_id=1, source_target_pairs={{0,16},{1,17},{2,18},{3,19},{4,20},{5,21},{6,22},{7,23},{8,9},{9,8... | collective-permute-start | bytes 1769480 | tf_op jit(solution)/shard_map/ppermute | solution.py:298
  88.0 17.6 %collective-permute-start.23 = (bf16[288,1024]{1,0:T(8,128)(2,1)S(1)}, bf16[288,1024]{1,0:T(8,128)(2,1)S(1)}, u32[]{:S(2)}, u32[]{:S(2)}) collective-permute-start(bf16[288,1024]{1,0:T(8,128)(2,1)S(1)} %collective-permute-done.19.refs_0_.a), channel_id=1, source_target_pairs={{0,16},{1,17},{2,18},{3,19},{4,20},{5,21},{6,22},{7,23},{8,9},{9,8... | collective-permute-start | bytes 1769480 | tf_op jit(solution)/shard_map/ppermute | solution.py:298
  106.3 27.7 %collective-permute-start.26 = (f32[8,640]{1,0:T(8,128)S(1)}, f32[8,640]{1,0:T(8,128)S(1)}, u32[]{:S(2)}, u32[]{:S(2)}) collective-permute-start(f32[8,640]{1,0:T(8,128)S(1)} %shard_map.87), channel_id=1, source_target_pairs={{0,6},{1,7},{2,4},{3,5},{4,2},{5,3},{6,0},{7,1},{8,14},{9,15},{10,... | collective-permute-start | bytes 61448 | tf_op jit(solution)/shard_map/ppermute | solution.py:298
  132.3 4.7 %collective-permute-start.25 = (f32[8,640]{1,0:T(8,128)S(1)}, f32[8,640]{1,0:T(8,128)S(1)}, u32[]{:S(2)}, u32[]{:S(2)}) collective-permute-start(f32[8,640]{1,0:T(8,128)S(1)} %shard_map.87), channel_id=1, source_target_pairs={{0,4},{1,5},{2,6},{3,7},{4,0},{5,1},{6,2},{7,3},{8,12},{9,13},{10,... | collective-permute-start | bytes 61448 | tf_op jit(solution)/shard_map/ppermute | solution.py:298
  132.3 4.7 %collective-permute-start.24 = (f32[8,640]{1,0:T(8,128)S(1)}, f32[8,640]{1,0:T(8,128)S(1)}, u32[]{:S(2)}, u32[]{:S(2)}) collective-permute-start(f32[8,640]{1,0:T(8,128)S(1)} %shard_map.87), channel_id=1, source_target_pairs={{0,2},{1,3},{2,0},{3,1},{4,6},{5,7},{6,4},{7,5},{8,10},{9,11},{10,... | collective-permute-start | bytes 61448 | tf_op jit(solution)/shard_map/ppermute | solution.py:298
  137.1 4.7 %collective-permute-start.29 = (f32[8,640]{1,0:T(8,128)S(1)}, f32[8,640]{1,0:T(8,128)S(1)}, u32[]{:S(2)}, u32[]{:S(2)}) collective-permute-start(f32[8,640]{1,0:T(8,128)S(1)} %maximum_maximum_fusion), channel_id=1, source_target_pairs={{0,17},{1,16},{2,19},{3,18},{4,21},{5,20},{6,23},{7,22},{8,25},{9,... | collective-permute-start | bytes 61448 | tf_op jit(solution)/shard_map/ppermute | solution.py:298
  138.1 3.8 %collective-permute-start.28 = (f32[8,640]{1,0:T(8,128)S(1)}, f32[8,640]{1,0:T(8,128)S(1)}, u32[]{:S(2)}, u32[]{:S(2)}) collective-permute-start(f32[8,640]{1,0:T(8,128)S(1)} %maximum_maximum_fusion), channel_id=1, source_target_pairs={{0,16},{1,17},{2,18},{3,19},{4,20},{5,21},{6,22},{7,23},{8,24},{9,... | collective-permute-start | bytes 61448 | tf_op jit(solution)/shard_map/ppermute | solution.py:298
  139.3 3.8 %collective-permute-start.27 = (f32[8,640]{1,0:T(8,128)S(1)}, f32[8,640]{1,0:T(8,128)S(1)}, u32[]{:S(2)}, u32[]{:S(2)}) collective-permute-start(f32[8,640]{1,0:T(8,128)S(1)} %maximum_maximum_fusion), channel_id=1, source_target_pairs={{0,1},{1,0},{2,3},{3,2},{4,5},{5,4},{6,7},{7,6},{8,9},{9,8},{10,11... | collective-permute-start | bytes 61448 | tf_op jit(solution)/shard_map/ppermute | solution.py:298
  143.1 1.3 collective-permute-start.30

commit v7 on v6

v7 whole, which is shorter than its diff:
```python
import functools

import jax
import jax.numpy as jnp
from jax import lax
from jax.experimental import pallas as pl
from jax.experimental.pallas import tpu as pltpu
from jax.sharding import PartitionSpec as P

AXES = ("section", "dp")
F32 = jnp.float32
BF16 = jnp.bfloat16
I32 = jnp.int32
LANES = 128
VMEM = pl.BlockSpec(memory_space=pltpu.VMEM)
SMEM = pl.BlockSpec(memory_space=pltpu.SMEM)
ANY = pl.BlockSpec(memory_space=pl.ANY)


def row_map(lengths, pair, core, index, count):
    first, second = lengths[2 * pair], lengths[2 * pair + 1]
    other_first = lengths[2 - 2 * pair]
    j = core * count + index
    in_first = j < first
    in_second = j < first + second
    span = jnp.where(in_first, 2 * pair, jnp.where(in_second, 2 * pair + 1, 3 - 2 * pair))
    place = jnp.where(
        in_first, j, jnp.where(in_second, j - first, 2 * count - other_first + j - first - second)
    )
    return span, place


def as_rows(columns, count):
    lane = lax.broadcasted_iota(I32, (count, LANES), 1)
    wide = jnp.zeros((count, LANES), F32)
    for i, column in enumerate(columns):
        wide = jnp.where(lane == i, column, wide)
    return jnp.transpose(wide)[:8]


def as_column(rows, which):
    full = jnp.concatenate([rows, jnp.zeros((LANES - 8, rows.shape[1]), F32)], axis=0)
    return jnp.transpose(full)[:, which : which + 1]


def pick_kernel(count, lengths, rows, sibling, extra, near, far, full, near_out, far_out):
    section = lax.axis_index("section")
    core, pair = lax.rem(section, 2), lax.div(section, 2)
    positions, half = rows.shape[0], extra.shape[0]
    index = lax.broadcasted_iota(I32, (count, 1), 0)
    span, place = row_map(lengths, pair, core, index, count)
    source = jnp.where(span == section, place, place + positions)
    source = jnp.where(span // 2 == pair, source, place + (2 * positions - (positions - half)))
    lane = lax.broadcasted_iota(I32, (count, 2 * positions + half), 1)
    pick = jnp.where(lane == source, F32(1.0), F32(0.0)).astype(BF16)
    picked = jnp.dot(pick[:, :positions], rows[...], preferred_element_type=F32)
    picked += jnp.dot(pick[:, positions : 2 * positions], sibling[...], preferred_element_type=F32)
    picked += jnp.dot(pick[:, 2 * positions :], extra[...], preferred_element_type=F32)
    full[...] = (picked * near[0:1, :]).astype(BF16)
    near_out[...] = near[...]
    far_out[...] = far[...]


def token_kernel(count, lengths, tokens, out):
    core = lax.rem(lax.axis_index("section"), 2)
    spans, positions = tokens.shape
    for pair in range(2):
        index = lax.broadcasted_iota(I32, (count, 1), 0)
        span, place = row_map(lengths, pair, core, index, count)
        lane = lax.broadcasted_iota(I32, (count, positions), 1)
        found = jnp.zeros((count, positions), F32)
        for s in range(spans):
            found = jnp.where(span == s, tokens[s : s + 1, :].astype(F32), found)
        found = jnp.sum(jnp.where(lane == place, found, F32(0.0)), axis=1, keepdims=True)
        out[pair * count : pair * count + count, :] = found.astype(I32)


def here():
    section = lax.axis_index("section")
    return section, lax.rem(section, 2), lax.div(section, 2)


def blocks(count):
    _, _, pair = here()
    return pl.multiple_of(pair * count, 16), pl.multiple_of((1 - pair) * count, 16)


def weights(head, sibling, depth, k, far):
    dp_index = lax.axis_index("dp")
    where = jnp.bitwise_xor(dp_index, 2 * k + (1 if far else 0))
    rows = pl.ds(pl.multiple_of(where * depth, depth), depth)
    return head[rows, :], sibling[rows, :]


def products(terms):
    value = jnp.concatenate([t[0] for t in terms], axis=1) if len(terms) > 1 else terms[0][0]
    out = []
    for side in range(2):
        w = [t[1][side] for t in terms]
        w = jnp.concatenate(w, axis=0) if len(w) > 1 else w[0]
        out.append(jnp.dot(value, w, preferred_element_type=F32))
    return jnp.concatenate(out, axis=1)


def sides(terms):
    square, reward = None, None
    for value, table, k in terms:
        value = value.astype(F32)
        gain, weight = table[k : k + 1, :], table[k + 4 : k + 5, :]
        s = value * value * (1.0 / (gain * gain))
        r = value * weight
        for i in range(value.shape[1] // LANES):
            cols = slice(i * LANES, (i + 1) * LANES)
            square = s[:, cols] if square is None else square + s[:, cols]
            reward = r[:, cols] if reward is None else reward + r[:, cols]
    return jnp.concatenate([square, reward], axis=1)


def begin_kernel(head, sibling, near, far, z, a, b, c, z1, a1, b1, ids, z2, acc, side, ids_out, z2_out):
    count, depth = z.shape
    _, core, _ = here()
    mine, others = blocks(count)
    near0, far0 = weights(head, sibling, depth, 0, False), weights(head, sibling, depth, 0, True)
    near1, far1 = weights(head, sibling, depth, 1, False), weights(head, sibling, depth, 1, True)
    for which, same, cross, same1, cross1 in ((0, a, b, a1, b1), (1, b, a, b1, a1)):

        @pl.when(core == which)
        def _():
            rows = pl.ds(mine, count)
            acc[rows, :] = products([(z[...], near0), (same[...], far0), (z1[...], near1), (same1[...], far1)])
            side[rows, :] = sides([(z[...], near, 0), (same[...], far, 0), (z1[...], near, 1), (same1[...], far, 1)])
            rows = pl.ds(others, count)
            acc[rows, :] = products([(cross[...], near0), (c[...], far0), (cross1[...], near1)])
            side[rows, :] = sides([(cross[...], near, 0), (c[...], far, 0), (cross1[...], near, 1)])

    ids_out[...] = ids[...]
    z2_out[...] = z2[...]


def middle_kernel(head, sibling, near, far, acc_in, side_in, z, a, b, c, a2, acc, side, a2_out):
    count, depth = z.shape
    _, core, _ = here()
    mine, others = blocks(count)
    near3, far3 = weights(head, sibling, depth, 3, False), weights(head, sibling, depth, 3, True)
    for which, same, cross in ((0, a, b), (1, b, a)):

        @pl.when(core == which)
        def _():
            rows = pl.ds(mine, count)
            acc[rows, :] = acc_in[rows, :] + products([(z[...], near3), (same[...], far3)])
            side[rows, :] = side_in[rows, :] + sides([(z[...], near, 3), (same[...], far, 3)])
            rows = pl.ds(others, count)
            acc[rows, :] = acc_in[rows, :] + products([(cross[...], near3), (c[...], far3)])
            side[rows, :] = side_in[rows, :] + sides([(cross[...], near, 3), (c[...], far, 3)])

    a2_out[...] = a2[...]


def gate_kernel(value, *refs):
    refs[-1][...] = value[...]


def column_ids(block):
    section, core, _ = here()
    dp_index, groups = lax.axis_index("dp"), lax.axis_size("dp")
    lane = lax.broadcasted_iota(I32, (1, block), 1)
    own = (section * groups + dp_index) * block
    other = ((section + 1 - 2 * core) * groups + dp_index) * block
    return jnp.concatenate([lane + own, lane + other], axis=1)


def summary(logits, square, reward, token_ids, ids, width):
    scale = lax.rsqrt(square / width + 1e-05)
    logits = logits * scale
    top = jnp.max(logits, axis=1, keepdims=True)
    total = jnp.sum(jnp.exp(logits - top), axis=1, keepdims=True)
    target = jnp.sum(jnp.where(ids == token_ids, logits, F32(0.0)), axis=1, keepdims=True)
    lane = lax.broadcasted_iota(I32, (logits.shape[0], LANES), 1)
    wide = jnp.where(lane == 2, target, jnp.where(lane == 3, reward * scale, F32(0.0)))
    return jnp.where(lane == 0, top, jnp.where(lane == 1, total, wide))


def added(side):
    return jnp.sum(side[:, :LANES], axis=1, keepdims=True), jnp.sum(side[:, LANES:], axis=1, keepdims=True)


def own_kernel(width, head, sibling, near, far, acc_in, side_in, z, a, b, c1, token_ids, left, left_side, far_out, wide):
    count, depth = z.shape
    _, core, _ = here()
    mine, others = blocks(count)
    near2, far2 = weights(head, sibling, depth, 2, False), weights(head, sibling, depth, 2, True)
    far1 = weights(head, sibling, depth, 1, True)
    block = head.shape[1]
    far_out[:, :block] = far2[0]
    far_out[:, block:] = far2[1]
    ids = column_ids(block)
    wide[...] = jnp.zeros(wide.shape, F32)
    for which, same, cross in ((0, a, b), (1, b, a)):

        @pl.when(core == which)
        def _():
            rows = pl.ds(mine, count)
            logits = acc_in[rows, :] + products([(z[...], near2), (same[...], far2)])
            square, reward = added(side_in[rows, :] + sides([(z[...], near, 2), (same[...], far, 2)]))
            wide[rows, :] = summary(logits, square, reward, token_ids[rows, :], ids, width)
            rows = pl.ds(others, count)
            left[...] = acc_in[rows, :] + products([(cross[...], near2), (c1[...], far1)])
            left_side[...] = side_in[rows, :] + sides([(cross[...], near, 2), (c1[...], far, 1)])


def last_kernel(width, far_weights, far, left, left_side, c, wide_in, token_ids, out, wide):
    count = c.shape[0]
    _, others = blocks(count)
    ids = column_ids(far_weights.shape[1] // 2)
    wide[...] = wide_in[...]
    logits = left[...] + jnp.dot(c[...], far_weights[...], preferred_element_type=F32)
    square, reward = added(left_side[...] + sides([(c[...], far, 2)]))
    rows = pl.ds(others, count)
    wide[rows, :] = summary(logits, square, reward, token_ids[rows, :], ids, width)
    out[...] = jnp.transpose(wide[...])[:8]


def whole_kernel(width, acc, square, reward, token_ids, out):
    count = acc.shape[0] // 2
    ids = column_ids(acc.shape[1] // 2)
    wide = summary(acc[...], square[...], reward[...], token_ids[...], ids, width)
    wide = jnp.concatenate([wide, jnp.zeros((out.shape[1] - 2 * count, LANES), F32)])
    out[...] = jnp.transpose(wide)[:8]


def final_kernel(count, lengths, stats, out_ref, score_ref):
    section = lax.axis_index("section")
    positions = out_ref.shape[1]
    where = lax.broadcasted_iota(I32, (1, positions), 1)
    logprob = jnp.zeros((1, positions), F32)
    score = jnp.zeros((1, 1), F32)
    index = lax.broadcasted_iota(I32, (count, 1), 0)
    for core in range(2):
        columns = jnp.transpose(
            jnp.concatenate([stats[core], jnp.zeros((LANES - 8, stats.shape[2]), F32)], axis=0)
        )
        for pair in range(2):
            value = columns[pair * count : pair * count + count]
            span, place = row_map(lengths, pair, core, index, count)
            own = span == section
            logprob += jnp.sum(jnp.where((place == where) & own, value[:, 0:1], F32(0.0)), axis=0, keepdims=True)
            score += jnp.sum(jnp.where(own, value[:, 1:2], F32(0.0)), axis=0, keepdims=True)
    out_ref[...] = logprob
    score_ref[...] = score / lengths[section].astype(F32)


def combine(parts):
    top = parts[0][0]
    for part in parts[1:]:
        top = jnp.maximum(top, part[0])
    total = sum(part[1] * jnp.exp(part[0] - top) for part in parts)
    target = sum(part[2] for part in parts)
    return jnp.concatenate([jnp.stack([top, total, target, parts[0][3]]), jnp.zeros((4,) + top.shape, F32)])


def call(body, outs, in_specs, args, limit=16, scratch=()):
    many = isinstance(outs, (list, tuple))
    return pl.pallas_call(
        body,
        out_shape=outs,
        in_specs=in_specs,
        out_specs=[VMEM] * len(outs) if many else VMEM,
        scratch_shapes=scratch,
        compiler_params=pltpu.CompilerParams(vmem_limit_bytes=limit << 20),
    )(*args)


def up(value):
    return -(-value // LANES) * LANES


def per_device(groups, hidden, norm_gain, head, reward_head, tokens, lengths):
    section = lax.axis_index("section")
    core, pair = section % 2, section // 2
    sections = lax.axis_size("section")
    spans, positions = tokens.shape
    block, width, part = head.shape[1], head.shape[0], hidden.shape[2]
    count = 3 * spans * positions // 4 // sections
    half = positions // 2
    rows = hidden[0]

    def mesh_perm(move):
        pairs = []
        for s in range(sections):
            for d in range(groups):
                s2, d2 = move(s, d)
                pairs.append((s * groups + d, s2 * groups + d2))
        return pairs

    send = lambda value, perm: lax.ppermute(value, AXES, perm)
    like = lambda v: jax.ShapeDtypeStruct(v.shape, v.dtype)
    acc_shape = jax.ShapeDtypeStruct((2 * count, 2 * block), F32)
    stats_shape = jax.ShapeDtypeStruct((8, up(2 * count)), F32)
    ids_shape = jax.ShapeDtypeStruct((2 * count, 1), I32)
    perm_z = {k: mesh_perm(lambda s, d, k=k: (s, d ^ (2 * k))) for k in (1, 2, 3)}
    perm_x = mesh_perm(lambda s, d: (s, d ^ 1))
    table = jnp.stack([norm_gain, reward_head]).astype(F32)

    swap = [(s, s ^ 1) for s in range(sections)]
    over = [(s, s ^ 2) for s in range(sections)]
    extra = lax.ppermute(rows[half:], "section", [(1, 3), (3, 1)])
    sibling = lax.ppermute(rows, "section", swap)
    head_sibling = lax.ppermute(head, "section", swap)

    if groups == 8:
        tables = [table] + [send(table, perm_z[k]) for k in (1, 2, 3)]
        near = jnp.concatenate([t[i : i + 1] for i in range(2) for t in tables])
        far = send(near, perm_x)
    else:
        near = jnp.concatenate([jnp.broadcast_to(table[i : i + 1], (4, part)) for i in range(2)])
        far = near
    full, near, far = call(
        functools.partial(pick_kernel, count),
        [jax.ShapeDtypeStruct((count, part), BF16), like(near), like(far)],
        [SMEM] + [VMEM] * 5,
        (lengths, rows, sibling, extra, near, far),
    )
    token_ids = call(functools.partial(token_kernel, count), ids_shape, [SMEM, VMEM], (lengths, tokens))

    if groups == 8:
        perm_a = mesh_perm(lambda s, d: (s, d ^ 1) if s % 2 == 0 else (s ^ 2, d))
        perm_b = mesh_perm(lambda s, d: (s ^ 2, d) if s % 2 == 0 else (s, d ^ 1))

        def gate(value, *after):
            return call(gate_kernel, like(value), [VMEM] + [ANY] * len(after), (value,) + after)

        side_shape = jax.ShapeDtypeStruct((2 * count, 2 * LANES), F32)
        z1 = send(full, perm_z[1])
        z3 = send(full, perm_z[3])
        a0 = send(full, perm_a)
        b0 = send(full, perm_b)
        c0 = send(a0, perm_b)
        z1 = gate(z1, b0)
        a1 = send(z1, perm_a)
        b1 = send(z1, perm_b)
        z3 = gate(z3, a1, b1, c0)
        a3 = send(z3, perm_a)
        b3 = send(z3, perm_b)
        z2 = send(z3, perm_z[1])
        c3 = send(a3, perm_b)
        acc, side, token_ids, z2 = call(
            begin_kernel,
            [acc_shape, side_shape, ids_shape, like(z2)],
            [VMEM] * 13,
            (head, head_sibling, near, far, full, a0, b0, c0, z1, a1, b1, token_ids, z2),
        )
        a2 = send(z2, perm_a)
        b2 = send(z2, perm_b)
        c1 = send(c0, perm_z[1])
        acc, side, a2 = call(
            middle_kernel,
            [acc_shape, side_shape, like(a2)],
            [VMEM] * 11,
            (head, head_sibling, near, far, acc, side, z3, a3, b3, c3, a2),
        )
        c2 = send(a2, perm_b)
        left, left_side, far_weights, wide = call(
            functools.partial(own_kernel, width),
            [
                jax.ShapeDtypeStruct((count, 2 * block), F32),
                jax.ShapeDtypeStruct((count, 2 * LANES), F32),
                jax.ShapeDtypeStruct((part, 2 * block), BF16),
                jax.ShapeDtypeStruct((up(2 * count), LANES), F32),
            ],
            [VMEM] * 11,
            (head, head_sibling, near, far, acc, side, z2, a2, b2, c1, token_ids),
        )
        stats = call(
            functools.partial(last_kernel, width),
            stats_shape,
            [VMEM] * 7,
            (far_weights, far, left, left_side, c2, wide, token_ids),
            scratch=[pltpu.VMEM((up(2 * count), LANES), F32)],
        )
        stats = combine([stats] + [send(stats, perm_z[k]) for k in (1, 2, 3)])
        stats = combine(
            [stats]
            + [send(stats, mesh_perm(lambda s, d, v=v: (s ^ v[0], d ^ v[1]))) for v in ((0, 1), (2, 0), (2, 1))]
        )
    else:
        other = lax.ppermute(full, "section", over)
        ordered = jnp.concatenate([jnp.where(pair == 0, full, other), jnp.where(pair == 0, other, full)])
        everything = lax.all_gather(ordered, "dp", axis=1, tiled=True)
        acc = jnp.concatenate(
            [jnp.dot(everything, h, preferred_element_type=F32) for h in (head, head_sibling)], axis=1
        )
        gains, weights_all = (lax.all_gather(t, "dp", axis=0, tiled=True) for t in table)
        wide = everything.astype(F32)
        square = jnp.sum((wide / gains) ** 2, axis=1, keepdims=True)
        reward = jnp.sum(wide * weights_all, axis=1, keepdims=True)
        stats = call(
            functools.partial(whole_kernel, width), stats_shape, [VMEM] * 4, (acc, square, reward, token_ids)
        )
        gathered = lax.all_gather(stats, "dp")
        stats = combine([gathered[i] for i in range(groups)])
        stats = combine([stats, lax.ppermute(stats, "section", over)])
    lp = stats[2:3] - (stats[0:1] + jnp.log(stats[1:2]))
    lp = jnp.concatenate([lp, stats[3:4], jnp.zeros((6, lp.shape[1]), F32)])
    both = lambda v, u: jnp.stack([jnp.where(core == 0, v, u), jnp.where(core == 0, u, v)])
    stats = both(lp, lax.ppermute(lp, "section", swap))
    logprob, score = call(
        functools.partial(final_kernel, count),
        [jax.ShapeDtypeStruct((1, positions), F32), jax.ShapeDtypeStruct((1, 1), F32)],
        [SMEM, VMEM],
        (lengths, stats),
    )
    return (logprob, score[0])


def solution(mesh):
    groups = mesh.shape["dp"]
    return jax.shard_map(
        lambda *args: per_device(groups, *args),
        mesh=mesh,
        in_specs=(P("section", None, "dp"), P("dp"), P(None, ("section", "dp")), P("dp"), P(), P()),
        out_specs=(P("section", None), P("section")),
        check_vma=False,
    )
```

time: 146 us -> 134 us (0.918)
  starting transfers between devices: 63.5 us -> 33.3 us
  Pallas kernels: 13.2 us -> 24.5 us
  waiting for transfers between devices: 65.4 us -> 70.7 us
    ppermute x25, starting transfers between devices: 57.1 us -> 32.1 us  [per_device(): send = lambda value, perm: lax.ppermute(value, AXES, perm)]
    pallas_call x12 -> x9, Pallas kernels: 13.2 us -> 24.5 us  [call(): pl.pallas_call(body, out_shape=outs, in_specs=in_specs, out_specs=[VMEM]...]
    ppermute x25, waiting for transfers between devices: 60.6 us -> 69.5 us  [per_device(): send = lambda value, perm: lax.ppermute(value, AXES, perm)]
    ppermute x2 -> x0, starting transfers between devices: 5.09 us -> none  [the longest x1 4.01 us: per_device(): sums = sums + lax.ppermute(sums, 'section', swap)]
    ppermute x2 -> x0, waiting for transfers between devices: 3.62 us -> none  [the longest x1 2.79 us: per_device(): lax.ppermute(sums, 'section', over)]
  transfers between devices with their start and end apart: 31 -> 29, of which waited for: 20 -> 17; matrix products, arithmetic and copies ran while one was open for 2% -> 2% of each run, Pallas kernels for 6% -> 16%
where the time goes in v7:
time: 134 us
  waiting for transfers between devices  70.7 us (53%)
  starting transfers between devices  33.3 us (25%)
  Pallas kernels  24.5 us (18%)
  local copies, waits for them, and re-layouts  4.4 us (3%)
    ppermute x25, waiting for transfers between devices, per_device(): send = lambda value, perm: lax.ppermute(value, AXES, perm)  69.5 us
    ppermute x25, starting transfers between devices, per_device(): send = lambda value, perm: lax.ppermute(value, AXES, perm)  32.1 us
    pallas_call x9, Pallas kernels, call(): pl.pallas_call(body, out_shape=outs, in_specs=in_specs, out_specs=[VMEM]...  24.5 us
  transfers between devices with their start and end apart: 29, of which 17 were waited for; matrix products, arithmetic and copies ran while one was open for 2% of the time, Pallas kernels for 16%

profile of v7, /device:TPU:0, one launch (start us, length us, event | category | flops | bytes accessed | tf_op | source)
XLA Modules:
  0.0 134.0 jit_solution(17205730550255287788)
XLA Ops:
  0.6 0.5 collective-permute-start
  1.2 0.7 stack.24
  1.8 0.7 stack.25
  2.5 4.7 %collective-permute-start.5 = (f32[2,1024]{1,0:T(2,128)S(1)}, f32[2,1024]{1,0:T(2,128)S(1)}, u32[]{:S(2)}, u32[]{:S(2)}) collective-permute-start(f32[2,1024]{1,0:T(2,128)S(1)} %maximum_convert_fusion), channel_id=1, source_target_pairs={{0,6},{1,7},{2,4},{3,5},{4,2},{5,3},{6,0},{7,1},{8,14},{9,15},{10,... | collective-permute-start | bytes 24584 | tf_op jit(solution)/shard_map/ppermute | solution.py:295
  7.2 0.6 collective-permute-start.3
  7.9 1.0 slice_bitcast_fusion
  8.9 0.7 collective-permute-start.2
  9.6 2.1 %collective-permute-done.4 = f32[2,1024]{1,0:T(2,128)S(1)} collective-permute-done((f32[2,1024]{1,0:T(2,128)S(1)}, f32[2,1024]{1,0:T(2,128)S(1)}, u32[]{:S(2)}, u32[]{:S(2)}) %collective-permute-start.4) | collective-permute-done | bytes 8224 | tf_op jit(solution)/shard_map/ppermute | solution.py:295
  11.9 1.6 %collective-permute-start.6 = (f32[8,1024]{1,0:T(8,128)S(1)}, f32[8,1024]{1,0:T(8,128)S(1)}, u32[]{:S(2)}, u32[]{:S(2)}) collective-permute-start(f32[8,1024]{1,0:T(8,128)S(1)} %concatenate.9.near), channel_id=1, source_target_pairs={{0,1},{1,0},{2,3},{3,2},{4,5},{5,4},{6,7},{7,6},{8,9},{9,8},{10,11... | collective-permute-start | bytes 98312 | tf_op jit(solution)/shard_map/ppermute | solution.py:295
  13.4 2.8 %collective-permute-done.6.far = f32[8,1024]{1,0:T(8,128)S(1)} collective-permute-done((f32[8,1024]{1,0:T(8,128)S(1)}, f32[8,1024]{1,0:T(8,128)S(1)}, u32[]{:S(2)}, u32[]{:S(2)}) %collective-permute-start.6) | collective-permute-done | bytes 32800 | tf_op jit(solution)/shard_map/ppermute | solution.py:295
  16.2 1.1 copy-done.1
  17.4 0.7 copy-done.3
  18.0 1.6 %shard_map.77 = (bf16[288,1024]{1,0:T(8,128)(2,1)S(1)}, f32[8,1024]{1,0:T(8,128)S(1)}, f32[8,1024]{1,0:T(8,128)S(1)}) custom-call(s32[4]{0:T(128)S(1)} %copy-done.3, bf16[384,1024]{1,0:T(8,128)(2,1)S(1)} %bitcast.9, bf16[384,1024]{1,0:T(8,128)(2,1)S(1)} %collective-permute-done.1.sibling, bf16[192,1024]{1,0:T(8,128)(2,1)S(1)} %collective-permute-done.2.extra, ...), custom_call_target="tpu_custom_call" | custom-call | tf_op jit(solution)/shard_map/pallas_call | solution.py:263
  19.6 1.2 collective-permute-start.8
  20.9 1.5 %collective-permute-start.7 = (bf16[288,1024]{1,0:T(8,128)(2,1)S(1)}, bf16[288,1024]{1,0:T(8,128)(2,1)S(1)}, u32[]{:S(2)}, u32[]{:S(2)}) collective-permute-start(bf16[288,1024]{1,0:T(8,128)(2,1)S(1)} %get-tuple-element.20.z), channel_id=1, source_target_pairs={{0,1},{1,0},{2,3},{3,2},{4,5},{5,4},{6,7},{7,6},{8,24},{9,25},{10,... | collective-permute-start | bytes 1769480 | tf_op jit(solution)/shard_map/ppermute | solution.py:295
  22.3 3.5 %collective-permute-start.13 = (bf16[288,1024]{1,0:T(8,128)(2,1)S(1)}, bf16[288,1024]{1,0:T(8,128)(2,1)S(1)}, u32[]{:S(2)}, u32[]{:S(2)}) collective-permute-start(bf16[288,1024]{1,0:T(8,128)(2,1)S(1)} %get-tuple-element.20.z), channel_id=1, source_target_pairs={{0,6},{1,7},{2,4},{3,5},{4,2},{5,3},{6,0},{7,1},{8,14},{9,15},{10,... | collective-permute-start | bytes 1769480 | tf_op jit(solution)/shard_map/ppermute | solution.py:295
  25.8 6.9 %collective-permute-done.8.refs_0_.b = bf16[288,1024]{1,0:T(8,128)(2,1)S(1)} collective-permute-done((bf16[288,1024]{1,0:T(8,128)(2,1)S(1)}, bf16[288,1024]{1,0:T(8,128)(2,1)S(1)}, u32[]{:S(2)}, u32[]{:S(2)}) %collective-permute-start.8) | collective-permute-done | bytes 589856 | tf_op jit(solution)/shard_map/ppermute | solution.py:295
  32.7 3.4 %collective-permute-done.10.value = bf16[288,1024]{1,0:T(8,128)(2,1)S(1)} collective-permute-done((bf16[288,1024]{1,0:T(8,128)(2,1)S(1)}, bf16[288,1024]{1,0:T(8,128)(2,1)S(1)}, u32[]{:S(2)}, u32[]{:S(2)}) %collective-permute-start.10) | collective-permute-done | bytes 589856 | tf_op jit(solution)/shard_map/ppermute | solution.py:295
  36.2 2.3 %collective-permute-start.11 = (bf16[288,1024]{1,0:T(8,128)(2,1)S(1)}, bf16[288,1024]{1,0:T(8,128)(2,1)S(1)}, u32[]{:S(2)}, u32[]{:S(2)}) collective-permute-start(bf16[288,1024]{1,0:T(8,128)(2,1)S(1)} %shard_map.78.z1), channel_id=1, source_target_pairs={{0,1},{1,0},{2,3},{3,2},{4,5},{5,4},{6,7},{7,6},{8,24},{9,25},{10,... | collective-permute-start | bytes 1769480 | tf_op jit(solution)/shard_map/ppermute | solution.py:295
  38.9 1.6 %collective-permute-start.9 = (bf16[288,1024]{1,0:T(8,128)(2,1)S(1)}, bf16[288,1024]{1,0:T(8,128)(2,1)S(1)}, u32[]{:S(2)}, u32[]{:S(2)}) collective-permute-start(bf16[288,1024]{1,0:T(8,128)(2,1)S(1)} %collective-permute-done.7.a), channel_id=1, source_target_pairs={{0,16},{1,17},{2,18},{3,19},{4,20},{5,21},{6,22},{7,23},{8,9},{9,8... | collective-permute-start | bytes 1769480 | tf_op jit(solution)/shard_map/ppermute | solution.py:295
  40.5 9.3 %collective-permute-done.13.value = bf16[288,1024]{1,0:T(8,128)(2,1)S(1)} collective-permute-done((bf16[288,1024]{1,0:T(8,128)(2,1)S(1)}, bf16[288,1024]{1,0:T(8,128)(2,1)S(1)}, u32[]{:S(2)}, u32[]{:S(2)}) %collective-permute-start.13) | collective-permute-done | bytes 589856 | tf_op jit(solution)/shard_map/ppermute | solution.py:295
  49.8 2.3 %collective-permute-done.11.refs_0_.a1 = bf16[288,1024]{1,0:T(8,128)(2,1)S(1)} collective-permute-done((bf16[288,1024]{1,0:T(8,128)(2,1)S(1)}, bf16[288,1024]{1,0:T(8,128)(2,1)S(1)}, u32[]{:S(2)}, u32[]{:S(2)}) %collective-permute-start.11) | collective-permute-done | bytes 589856 | tf_op jit(solution)/shard_map/ppermute | solution.py:295
  52.6 6.3 %collective-permute-done.9.refs_2_.c = bf16[288,1024]{1,0:T(8,128)(2,1)S(1)} collective-permute-done((bf16[288,1024]{1,0:T(8,128)(2,1)S(1)}, bf16[288,1024]{1,0:T(8,128)(2,1)S(1)}, u32[]{:S(2)}, u32[]{:S(2)}) %collective-permute-start.9) | collective-permute-done | bytes 589856 | tf_op jit(solution)/shard_map/ppermute | solution.py:295
  58.9 1.2 collective-permute-start.15
  60.1 0.6 collective-permute-start.14
  60.8 1.0 shard_map.79.ids
  62.2 12.7 %collective-permute-done.15.a = bf16[288,1024]{1,0:T(8,128)(2,1)S(1)} collective-permute-done((bf16[288,1024]{1,0:T(8,128)(2,1)S(1)}, bf16[288,1024]{1,0:T(8,128)(2,1)S(1)}, u32[]{:S(2)}, u32[]{:S(2)}) %collective-permute-start.15) | collective-permute-done | bytes 589856 | tf_op jit(solution)/shard_map/ppermute | solution.py:295
  74.9 1.9 %collective-permute-start.17 = (bf16[288,1024]{1,0:T(8,128)(2,1)S(1)}, bf16[288,1024]{1,0:T(8,128)(2,1)S(1)}, u32[]{:S(2)}, u32[]{:S(2)}) collective-permute-start(bf16[288,1024]{1,0:T(8,128)(2,1)S(1)} %collective-permute-done.15.a), channel_id=1, source_target_pairs={{0,16},{1,17},{2,18},{3,19},{4,20},{5,21},{6,22},{7,23},{8,9},{9,8... | collective-permute-start | bytes 1769480 | tf_op jit(solution)/shard_map/ppermute | solution.py:295
  76.7 8.2 %shard_map.81 = (f32[576,512]{1,0:T(8,128)S(1)}, f32[576,256]{1,0:T(8,128)S(1)}, s32[576,1]{1,0:T(8,128)S(1)}, bf16[288,1024]{1,0:T(8,128)(2,1)S(1)}) custom-call(bf16[8192,256]{1,0:T(8,128)(2,1)S(1)} %copy-done, bf16[8192,256]{1,0:T(8,128)(2,1)} %collective-permute-done.sibling, f32[8,1024]{1,0:T(8,128)S(1)} %get-tuple-element.18.near, ...), custom_call_target="tpu_custom_call" | custom-call | tf_op jit(solution)/shard_map/pallas_call | solution.py:263
  85.1 1.8 %collective-permute-start.19 = (bf16[288,1024]{1,0:T(8,128)(2,1)S(1)}, bf16[288,1024]{1,0:T(8,128)(2,1)S(1)}, u32[]{:S(2)}, u32[]{:S(2)}) collective-permute-start(bf16[288,1024]{1,0:T(8,128)(2,1)S(1)} %get-tuple-element.23.z), channel_id=1, source_target_pairs={{0,16},{1,17},{2,18},{3,19},{4,20},{5,21},{6,22},{7,23},{8,9},{9,8... | collective-permute-start | bytes 1769480 | tf_op jit(solution)/shard_map/ppermute | solution.py:295
  86.9 11.6 %collective-permute-done.18.a2 = bf16[288,1024]{1,0:T(8,128)(2,1)S(1)} collective-permute-done((bf16[288,1024]{1,0:T(8,128)(2,1)S(1)}, bf16[288,1024]{1,0:T(8,128)(2,1)S(1)}, u32[]{:S(2)}, u32[]{:S(2)}) %collective-permute-start.18) | collective-permute-done | bytes 589856 | tf_op jit(solution)/shard_map/ppermute | solution.py:295
  98.5 5.7 %shard_map.82 = (f32[576,512]{1,0:T(8,128)S(1)}, f32[576,256]{1,0:T(8,128)S(1)}, bf16[288,1024]{1,0:T(8,128)(2,1)S(1)}) custom-call(bf16[8192,256]{1,0:T(8,128)(2,1)S(1)} %copy-done, bf16[8192,256]{1,0:T(8,128)(2,1)} %collective-permute-done.sibling, f32[8,1024]{1,0:T(8,128)S(1)} %get-tuple-element.18.near, f32[8,1024]{1,0:T(8,128)S(1)} %get-tuple-element.19.far, ...), custom_call_target="tpu_custom_call" | custom-call | tf_op jit(solution)/shard_map/pallas_call | solution.py:263
  104.2 0.6 collective-permute-start.21
  104.8 5.2 %shard_map.83 = (f32[288,512]{1,0:T(8,128)S(1)}, f32[288,256]{1,0:T(8,128)S(1)}, bf16[1024,512]{1,0:T(8,128)(2,1)S(1)}, f32[640,128]{1,0:T(8,128)S(1)}) custom-call(bf16[8192,256]{1,0:T(8,128)(2,1)S(1)} %copy-done, bf16[8192,256]{1,0:T(8,128)(2,1)} %collective-permute-done.sibling, f32[8,1024]{1,0:T(8,128)S(1)} %get-tuple-element.18.near, ...), custom_call_target="tpu_custom_call" | custom-call | tf_op jit(solution)/shard_map/pallas_call | solution.py:263
  110.0 4.1 %collective-permute-done.21.c = bf16[288,1024]{1,0:T(8,128)(2,1)S(1)} collective-permute-done((bf16[288,1024]{1,0:T(8,128)(2,1)S(1)}, bf16[288,1024]{1,0:T(8,128)(2,1)S(1)}, u32[]{:S(2)}, u32[]{:S(2)}) %collective-permute-start.21) | collective-permute-done | bytes 589856 | tf_op jit(solution)/shard_map/ppermute | solution.py:295
  114.1 0.9 shard_map.84
  115.0 1.6 %collective-permute-start.22 = (f32[8,640]{1,0:T(8,128)S(1)}, f32[8,640]{1,0:T(8,128)S(1)}, u32[]{:S(2)}, u32[]{:S(2)}) collective-permute-start(f32[8,640]{1,0:T(8,128)S(1)} %shard_map.84), channel_id=1, source_target_pairs={{0,2},{1,3},{2,0},{3,1},{4,6},{5,7},{6,4},{7,5},{8,10},{9,11},{10,... | collective-permute-start | bytes 61448 | tf_op jit(solution)/shard_map/ppermute | solution.py:295
  116.6 1.8 %collective-permute-start.23 = (f32[8,640]{1,0:T(8,128)S(1)}, f32[8,640]{1,0:T(8,128)S(1)}, u32[]{:S(2)}, u32[]{:S(2)}) collective-permute-start(f32[8,640]{1,0:T(8,128)S(1)} %shard_map.84), channel_id=1, source_target_pairs={{0,4},{1,5},{2,6},{3,7},{4,0},{5,1},{6,2},{7,3},{8,12},{9,13},{10,... | collective-permute-start | bytes 61448 | tf_op jit(solution)/shard_map/ppermute | solution.py:295
  118.4 1.0 collective-permute-start.24
  119.4 2.0 %collective-permute-done.23 = f32[8,640]{1,0:T(8,128)S(1)} collective-permute-done((f32[8,640]{1,0:T(8,128)S(1)}, f32[8,640]{1,0:T(8,128)S(1)}, u32[]{:S(2)}, u32[]{:S(2)}) %collective-permute-start.23) | collective-permute-done | bytes 20512 | tf_op jit(solution)/shard_map/ppermute | solution.py:295
  121.4 2.6 %collective-permute-done.24 = f32[8,640]{1,0:T(8,128)S(1)} collective-permute-done((f32[8,640]{1,0:T(8,128)S(1)}, f32[8,640]{1,0:T(8,128)S(1)}, u32[]{:S(2)}, u32[]{:S(2)}) %collective-permute-start.24) | collective-permute-done | bytes 20512 | tf_op jit(solution)/shard_map/ppermute | solution.py:295
  124.1 0.7 collective-permute-start.25
  124.8 1.2 collective-permute-start.26
  126.0 1.7 %collective-permute-start.27 = (f32[8,640]{1,0:T(8,128)S(1)}, f32[8,640]{1,0:T(8,128)S(1)}, u32[]{:S(2)}, u32[]{:S(2)}) collective-permute-start(f32[8,640]{1,0:T(8,128)S(1)} %concatenate.10), channel_id=1, source_target_pairs={{0,17},{1,16},{2,19},{3,18},{4,21},{5,20},{6,23},{7,22},{8,25},{9,... | collective-permute-start | bytes 61448 | tf_op jit(solution)/shard_map/ppermute | solution.py:295
  127.9 0.6 collective-permute-done.26
  128.6 2.1 %collective-permute-done.27 = f32[8,640]{1,0:T(8,128)S(1)} collective-permute-done((f32[8,640]{1,0:T(8,128)S(1)}, f32[8,640]{1,0:T(8,128)S(1)}, u32[]{:S(2)}, u32[]{:S(2)}) %collective-permute-start.27) | collective-permute-done | bytes 20512 | tf_op jit(solution)/shard_map/ppermute | solution.py:295
  130.8 1.2 collective-permute-done.28
  132.1 1.9 %shard_map.85 = (f32[1,384]{1,0:T(1,128)}, f32[1,1]{1,0:T(1,128)}) custom-call(s32[4]{0:T(128)S(1)} %copy-done.4, f32[2,8,640]{2,1,0:T(8,128)S(1)} %pad_maximum_fusion.stats), custom_call_target="tpu_custom_call" | custom-call | tf_op jit(solution)/shard_map/pallas_call | solution.py:263
  (47 shorter events, 2.2 us)
Async XLA Ops:
  0.6 60.1 %copy-start.2 = (s32[4,384]{1,0:T(4,128)S(1)}, s32[4,384]{1,0:T(4,128)}, u32[]{:S(2)}) copy-start(s32[4,384]{1,0:T(4,128)} %tokens.1) | copy-start | bytes 18436
  0.6 76.1 %collective-permute-start = (bf16[8192,256]{1,0:T(8,128)(2,1)}, bf16[8192,256]{1,0:T(8,128)(2,1)}, u32[]{:S(2)}, u32[]{:S(2)}) collective-permute-start(bf16[8192,256]{1,0:T(8,128)(2,1)} %head.5), channel_id=1, source_target_pairs={{0,8},{8,0},{16,24},{24,16},{1,9},{9,1},{17,25},{25,17},{2,10},{10... | collective-permute-start | bytes 12582920 | tf_op jit(solution)/shard_map/ppermute | solution.py:308
  2.5 6.4 %collective-permute-start.5 = (f32[2,1024]{1,0:T(2,128)S(1)}, f32[2,1024]{1,0:T(2,128)S(1)}, u32[]{:S(2)}, u32[]{:S(2)}) collective-permute-start(f32[2,1024]{1,0:T(2,128)S(1)} %maximum_convert_fusion), channel_id=1, source_target_pairs={{0,6},{1,7},{2,4},{3,5},{4,2},{5,3},{6,0},{7,1},{8,14},{9,15},{10,... | collective-permute-start | bytes 24584 | tf_op jit(solution)/shard_map/ppermute | solution.py:295
  7.2 4.5 %collective-permute-start.4 = (f32[2,1024]{1,0:T(2,128)S(1)}, f32[2,1024]{1,0:T(2,128)S(1)}, u32[]{:S(2)}, u32[]{:S(2)}) collective-permute-start(f32[2,1024]{1,0:T(2,128)S(1)} %maximum_convert_fusion), channel_id=1, source_target_pairs={{0,4},{1,5},{2,6},{3,7},{4,0},{5,1},{6,2},{7,3},{8,12},{9,13},{10,... | collective-permute-start | bytes 24584 | tf_op jit(solution)/shard_map/ppermute | solution.py:295
  7.2 4.6 %collective-permute-start.3 = (f32[2,1024]{1,0:T(2,128)S(1)}, f32[2,1024]{1,0:T(2,128)S(1)}, u32[]{:S(2)}, u32[]{:S(2)}) collective-permute-start(f32[2,1024]{1,0:T(2,128)S(1)} %maximum_convert_fusion), channel_id=1, source_target_pairs={{0,2},{1,3},{2,0},{3,1},{4,6},{5,7},{6,4},{7,5},{8,10},{9,11},{10,... | collective-permute-start | bytes 24584 | tf_op jit(solution)/shard_map/ppermute | solution.py:295
  7.9 8.3 %collective-permute-start.1 = (bf16[384,1024]{1,0:T(8,128)(2,1)}, bf16[384,1024]{1,0:T(8,128)(2,1)S(1)}, u32[]{:S(2)}, u32[]{:S(2)}) collective-permute-start(bf16[384,1024]{1,0:T(8,128)(2,1)} %bitcast.8), channel_id=1, source_target_pairs={{0,8},{8,0},{16,24},{24,16},{1,9},{9,1},{17,25},{25,17},{2,10},{10... | collective-permute-start | bytes 2359304 | tf_op jit(solution)/shard_map/ppermute | solution.py:307
  8.9 7.3 %collective-permute-start.2 = (bf16[192,1024]{1,0:T(8,128)(2,1)S(1)}, bf16[192,1024]{1,0:T(8,128)(2,1)S(1)}, u32[]{:S(2)}, u32[]{:S(2)}) collective-permute-start(bf16[192,1024]{1,0:T(8,128)(2,1)S(1)} %slice_bitcast_fusion), channel_id=1, source_target_pairs={{8,24},{24,8},{9,25},{25,9},{10,26},{26,10},{11,27},{27,11},{12,28... | collective-permute-start | bytes 1179656 | tf_op jit(solution)/shard_map/ppermute | solution.py:306
  11.9 64.9 %copy-start = (bf16[8192,256]{1,0:T(8,128)(2,1)S(1)}, bf16[8192,256]{1,0:T(8,128)(2,1)}, u32[]{:S(2)}) copy-start(bf16[8192,256]{1,0:T(8,128)(2,1)} %head.5) | copy-start | bytes 12582916
  11.9 4.3 %collective-permute-start.6 = (f32[8,1024]{1,0:T(8,128)S(1)}, f32[8,1024]{1,0:T(8,128)S(1)}, u32[]{:S(2)}, u32[]{:S(2)}) collective-permute-start(f32[8,1024]{1,0:T(8,128)S(1)} %concatenate.9.near), channel_id=1, source_target_pairs={{0,1},{1,0},{2,3},{3,2},{4,5},{5,4},{6,7},{7,6},{8,9},{9,8},{10,11... | collective-permute-start | bytes 98312 | tf_op jit(solution)/shard_map/ppermute | solution.py:295
  16.2 1.1 copy-start.1
  17.4 0.7 copy-start.3
  19.6 13.1 %collective-permute-start.8 = (bf16[288,1024]{1,0:T(8,128)(2,1)S(1)}, bf16[288,1024]{1,0:T(8,128)(2,1)S(1)}, u32[]{:S(2)}, u32[]{:S(2)}) collective-permute-start(bf16[288,1024]{1,0:T(8,128)(2,1)S(1)} %get-tuple-element.20.z), channel_id=1, source_target_pairs={{0,16},{1,17},{2,18},{3,19},{4,20},{5,21},{6,22},{7,23},{8,9},{9,8... | collective-permute-start | bytes 1769480 | tf_op jit(solution)/shard_map/ppermute | solution.py:295
  20.9 15.3 %collective-permute-start.10 = (bf16[288,1024]{1,0:T(8,128)(2,1)S(1)}, bf16[288,1024]{1,0:T(8,128)(2,1)S(1)}, u32[]{:S(2)}, u32[]{:S(2)}) collective-permute-start(bf16[288,1024]{1,0:T(8,128)(2,1)S(1)} %get-tuple-element.20.z), channel_id=1, source_target_pairs={{0,2},{1,3},{2,0},{3,1},{4,6},{5,7},{6,4},{7,5},{8,10},{9,11},{10,... | collective-permute-start | bytes 1769480 | tf_op jit(solution)/shard_map/ppermute | solution.py:295
  20.9 18.0 %collective-permute-start.7 = (bf16[288,1024]{1,0:T(8,128)(2,1)S(1)}, bf16[288,1024]{1,0:T(8,128)(2,1)S(1)}, u32[]{:S(2)}, u32[]{:S(2)}) collective-permute-start(bf16[288,1024]{1,0:T(8,128)(2,1)S(1)} %get-tuple-element.20.z), channel_id=1, source_target_pairs={{0,1},{1,0},{2,3},{3,2},{4,5},{5,4},{6,7},{7,6},{8,24},{9,25},{10,... | collective-permute-start | bytes 1769480 | tf_op jit(solution)/shard_map/ppermute | solution.py:295
  22.3 27.5 %collective-permute-start.13 = (bf16[288,1024]{1,0:T(8,128)(2,1)S(1)}, bf16[288,1024]{1,0:T(8,128)(2,1)S(1)}, u32[]{:S(2)}, u32[]{:S(2)}) collective-permute-start(bf16[288,1024]{1,0:T(8,128)(2,1)S(1)} %get-tuple-element.20.z), channel_id=1, source_target_pairs={{0,6},{1,7},{2,4},{3,5},{4,2},{5,3},{6,0},{7,1},{8,14},{9,15},{10,... | collective-permute-start | bytes 1769480 | tf_op jit(solution)/shard_map/ppermute | solution.py:295
  36.2 16.0 %collective-permute-start.11 = (bf16[288,1024]{1,0:T(8,128)(2,1)S(1)}, bf16[288,1024]{1,0:T(8,128)(2,1)S(1)}, u32[]{:S(2)}, u32[]{:S(2)}) collective-permute-start(bf16[288,1024]{1,0:T(8,128)(2,1)S(1)} %shard_map.78.z1), channel_id=1, source_target_pairs={{0,1},{1,0},{2,3},{3,2},{4,5},{5,4},{6,7},{7,6},{8,24},{9,25},{10,... | collective-permute-start | bytes 1769480 | tf_op jit(solution)/shard_map/ppermute | solution.py:295
  38.5 14.1 %collective-permute-start.12 = (bf16[288,1024]{1,0:T(8,128)(2,1)S(1)}, bf16[288,1024]{1,0:T(8,128)(2,1)S(1)}, u32[]{:S(2)}, u32[]{:S(2)}) collective-permute-start(bf16[288,1024]{1,0:T(8,128)(2,1)S(1)} %shard_map.78.z1), channel_id=1, source_target_pairs={{0,16},{1,17},{2,18},{3,19},{4,20},{5,21},{6,22},{7,23},{8,9},{9,8... | collective-permute-start | bytes 1769480 | tf_op jit(solution)/shard_map/ppermute | solution.py:295
  38.9 20.0 %collective-permute-start.9 = (bf16[288,1024]{1,0:T(8,128)(2,1)S(1)}, bf16[288,1024]{1,0:T(8,128)(2,1)S(1)}, u32[]{:S(2)}, u32[]{:S(2)}) collective-permute-start(bf16[288,1024]{1,0:T(8,128)(2,1)S(1)} %collective-permute-done.7.a), channel_id=1, source_target_pairs={{0,16},{1,17},{2,18},{3,19},{4,20},{5,21},{6,22},{7,23},{8,9},{9,8... | collective-permute-start | bytes 1769480 | tf_op jit(solution)/shard_map/ppermute | solution.py:295
  58.9 15.9 %collective-permute-start.15 = (bf16[288,1024]{1,0:T(8,128)(2,1)S(1)}, bf16[288,1024]{1,0:T(8,128)(2,1)S(1)}, u32[]{:S(2)}, u32[]{:S(2)}) collective-permute-start(bf16[288,1024]{1,0:T(8,128)(2,1)S(1)} %shard_map.80.z), channel_id=1, source_target_pairs={{0,1},{1,0},{2,3},{3,2},{4,5},{5,4},{6,7},{7,6},{8,24},{9,25},{10,... | collective-permute-start | bytes 1769480 | tf_op jit(solution)/shard_map/ppermute | solution.py:295
  60.1 16.6 %collective-permute-start.14 = (bf16[288,1024]{1,0:T(8,128)(2,1)S(1)}, bf16[288,1024]{1,0:T(8,128)(2,1)S(1)}, u32[]{:S(2)}, u32[]{:S(2)}) collective-permute-start(bf16[288,1024]{1,0:T(8,128)(2,1)S(1)} %shard_map.80.z), channel_id=1, source_target_pairs={{0,2},{1,3},{2,0},{3,1},{4,6},{5,7},{6,4},{7,5},{8,10},{9,11},{10,... | collective-permute-start | bytes 1769480 | tf_op jit(solution)/shard_map/ppermute | solution.py:295
  61.7 25.2 %collective-permute-start.16 = (bf16[288,1024]{1,0:T(8,128)(2,1)S(1)}, bf16[288,1024]{1,0:T(8,128)(2,1)S(1)}, u32[]{:S(2)}, u32[]{:S(2)}) collective-permute-start(bf16[288,1024]{1,0:T(8,128)(2,1)S(1)} %shard_map.80.z), channel_id=1, source_target_pairs={{0,16},{1,17},{2,18},{3,19},{4,20},{5,21},{6,22},{7,23},{8,9},{9,8... | collective-permute-start | bytes 1769480 | tf_op jit(solution)/shard_map/ppermute | solution.py:295
  74.9 12.1 %collective-permute-start.17 = (bf16[288,1024]{1,0:T(8,128)(2,1)S(1)}, bf16[288,1024]{1,0:T(8,128)(2,1)S(1)}, u32[]{:S(2)}, u32[]{:S(2)}) collective-permute-start(bf16[288,1024]{1,0:T(8,128)(2,1)S(1)} %collective-permute-done.15.a), channel_id=1, source_target_pairs={{0,16},{1,17},{2,18},{3,19},{4,20},{5,21},{6,22},{7,23},{8,9},{9,8... | collective-permute-start | bytes 1769480 | tf_op jit(solution)/shard_map/ppermute | solution.py:295
  85.0 13.5 %collective-permute-start.18 = (bf16[288,1024]{1,0:T(8,128)(2,1)S(1)}, bf16[288,1024]{1,0:T(8,128)(2,1)S(1)}, u32[]{:S(2)}, u32[]{:S(2)}) collective-permute-start(bf16[288,1024]{1,0:T(8,128)(2,1)S(1)} %get-tuple-element.23.z), channel_id=1, source_target_pairs={{0,1},{1,0},{2,3},{3,2},{4,5},{5,4},{6,7},{7,6},{8,24},{9,25},{10,... | collective-permute-start | bytes 1769480 | tf_op jit(solution)/shard_map/ppermute | solution.py:295
  85.1 19.7 %collective-permute-start.20 = (bf16[288,1024]{1,0:T(8,128)(2,1)S(1)}, bf16[288,1024]{1,0:T(8,128)(2,1)S(1)}, u32[]{:S(2)}, u32[]{:S(2)}) collective-permute-start(bf16[288,1024]{1,0:T(8,128)(2,1)S(1)} %collective-permute-done.9.refs_2_.c), channel_id=1, source_target_pairs={{0,2},{1,3},{2,0},{3,1},{4,6},{5,7},{6,4},{7,5},{8,10},{9,11},{10,... | collective-permute-start | bytes 1769480 | tf_op jit(solution)/shard_map/ppermute | solution.py:295
  85.1 19.6 %collective-permute-start.19 = (bf16[288,1024]{1,0:T(8,128)(2,1)S(1)}, bf16[288,1024]{1,0:T(8,128)(2,1)S(1)}, u32[]{:S(2)}, u32[]{:S(2)}) collective-permute-start(bf16[288,1024]{1,0:T(8,128)(2,1)S(1)} %get-tuple-element.23.z), channel_id=1, source_target_pairs={{0,16},{1,17},{2,18},{3,19},{4,20},{5,21},{6,22},{7,23},{8,9},{9,8... | collective-permute-start | bytes 1769480 | tf_op jit(solution)/shard_map/ppermute | solution.py:295
  104.2 9.9 %collective-permute-start.21 = (bf16[288,1024]{1,0:T(8,128)(2,1)S(1)}, bf16[288,1024]{1,0:T(8,128)(2,1)S(1)}, u32[]{:S(2)}, u32[]{:S(2)}) collective-permute-start(bf16[288,1024]{1,0:T(8,128)(2,1)S(1)} %get-tuple-element.26.a), channel_id=1, source_target_pairs={{0,16},{1,17},{2,18},{3,19},{4,20},{5,21},{6,22},{7,23},{8,9},{9,8... | collective-permute-start | bytes 1769480 | tf_op jit(solution)/shard_map/ppermute | solution.py:295
  104.8 27.3 %copy-start.4 = (s32[4]{0:T(128)S(1)}, s32[4]{0:T(128)}, u32[]{:S(2)}) copy-start(s32[4]{0:T(128)} %lengths.5) | copy-start | bytes 52
  115.0 4.4 %collective-permute-start.22 = (f32[8,640]{1,0:T(8,128)S(1)}, f32[8,640]{1,0:T(8,128)S(1)}, u32[]{:S(2)}, u32[]{:S(2)}) collective-permute-start(f32[8,640]{1,0:T(8,128)S(1)} %shard_map.84), channel_id=1, source_target_pairs={{0,2},{1,3},{2,0},{3,1},{4,6},{5,7},{6,4},{7,5},{8,10},{9,11},{10,... | collective-permute-start | bytes 61448 | tf_op jit(solution)/shard_map/ppermute | solution.py:295
  116.6 4.8 %collective-permute-start.23 = (f32[8,640]{1,0:T(8,128)S(1)}, f32[8,640]{1,0:T(8,128)S(1)}, u32[]{:S(2)}, u32[]{:S(2)}) collective-permute-start(f32[8,640]{1,0:T(8,128)S(1)} %shard_map.84), channel_id=1, source_target_pairs={{0,4},{1,5},{2,6},{3,7},{4,0},{5,1},{6,2},{7,3},{8,12},{9,13},{10,... | collective-permute-start | bytes 61448 | tf_op jit(solution)/shard_map/ppermute | solution.py:295
  118.4 5.6 %collective-permute-start.24 = (f32[8,640]{1,0:T(8,128)S(1)}, f32[8,640]{1,0:T(8,128)S(1)}, u32[]{:S(2)}, u32[]{:S(2)}) collective-permute-start(f32[8,640]{1,0:T(8,128)S(1)} %shard_map.84), channel_id=1, source_target_pairs={{0,6},{1,7},{2,4},{3,5},{4,2},{5,3},{6,0},{7,1},{8,14},{9,15},{10,... | collective-permute-start | bytes 61448 | tf_op jit(solution)/shard_map/ppermute | solution.py:295
  124.1 3.8 %collective-permute-start.25 = (f32[8,640]{1,0:T(8,128)S(1)}, f32[8,640]{1,0:T(8,128)S(1)}, u32[]{:S(2)}, u32[]{:S(2)}) collective-permute-start(f32[8,640]{1,0:T(8,128)S(1)} %concatenate.10), channel_id=1, source_target_pairs={{0,1},{1,0},{2,3},{3,2},{4,5},{5,4},{6,7},{7,6},{8,9},{9,8},{10,11... | collective-permute-start | bytes 61448 | tf_op jit(solution)/shard_map/ppermute | solution.py:295
  124.8 3.8 %collective-permute-start.26 = (f32[8,640]{1,0:T(8,128)S(1)}, f32[8,640]{1,0:T(8,128)S(1)}, u32[]{:S(2)}, u32[]{:S(2)}) collective-permute-start(f32[8,640]{1,0:T(8,128)S(1)} %concatenate.10), channel_id=1, source_target_pairs={{0,16},{1,17},{2,18},{3,19},{4,20},{5,21},{6,22},{7,23},{8,24},{9,... | collective-permute-start | bytes 61448 | tf_op jit(solution)/shard_map/ppermute | solution.py:295
  126.0 4.7 %collective-permute-start.27 = (f32[8,640]{1,0:T(8,128)S(1)}, f32[8,640]{1,0:T(8,128)S(1)}, u32[]{:S(2)}, u32[]{:S(2)}) collective-permute-start(f32[8,640]{1,0:T(8,128)S(1)} %concatenate.10), channel_id=1, source_target_pairs={{0,17},{1,16},{2,19},{3,18},{4,21},{5,20},{6,23},{7,22},{8,25},{9,... | collective-permute-start | bytes 61448 | tf_op jit(solution)/shard_map/ppermute | solution.py:295
  130.8 1.2 collective-permute-start.28

commit v8 on v7

--- a/solution.py
+++ b/solution.py
@@ -43,7 +43,13 @@
     return jnp.transpose(full)[:, which : which + 1]
 
 
-def pick_kernel(count, lengths, rows, sibling, extra, near, far, full, near_out, far_out):
+def table_kernel(gain, reward, rows, lengths, table):
+    value = gain[...].astype(F32)
+    table[0:1, :] = 1.0 / (value * value)
+    table[1:2, :] = reward[...].astype(F32)
+
+
+def pick_kernel(count, lengths, rows, sibling, extra, gain, near, after, full, near_out):
     section = lax.axis_index("section")
     core, pair = lax.rem(section, 2), lax.div(section, 2)
     positions, half = rows.shape[0], extra.shape[0]
@@ -56,9 +62,8 @@
     picked = jnp.dot(pick[:, :positions], rows[...], preferred_element_type=F32)
     picked += jnp.dot(pick[:, positions : 2 * positions], sibling[...], preferred_element_type=F32)
     picked += jnp.dot(pick[:, 2 * positions :], extra[...], preferred_element_type=F32)
-    full[...] = (picked * near[0:1, :]).astype(BF16)
+    full[...] = (picked * gain[...].astype(F32)).astype(BF16)
     near_out[...] = near[...]
-    far_out[...] = far[...]
 
 
 def token_kernel(count, lengths, tokens, out):
@@ -102,21 +107,30 @@
     return jnp.concatenate(out, axis=1)
 
 
-def sides(terms):
-    square, reward = None, None
-    for value, table, k in terms:
-        value = value.astype(F32)
-        gain, weight = table[k : k + 1, :], table[k + 4 : k + 5, :]
-        s = value * value * (1.0 / (gain * gain))
-        r = value * weight
-        for i in range(value.shape[1] // LANES):
-            cols = slice(i * LANES, (i + 1) * LANES)
-            square = s[:, cols] if square is None else square + s[:, cols]
-            reward = r[:, cols] if reward is None else reward + r[:, cols]
-    return jnp.concatenate([square, reward], axis=1)
-
-
-def begin_kernel(head, sibling, near, far, z, a, b, c, z1, a1, b1, ids, z2, acc, side, ids_out, z2_out):
+def add_sides(terms, base, side_in, side):
+    step = 32
+    count, depth = terms[0][0].shape
+
+    def body(i, _):
+        rows = pl.ds(pl.multiple_of(i * step, step), step)
+        at = pl.ds(pl.multiple_of(base + i * step, step), step)
+        square, reward = jnp.zeros((step, LANES), F32), jnp.zeros((step, LANES), F32)
+        if side_in is not None:
+            square, reward = side_in[at, :LANES], side_in[at, LANES:]
+        for piece, table, k in terms:
+            for c in range(depth // LANES):
+                cols = slice(c * LANES, (c + 1) * LANES)
+                value = piece[rows, cols].astype(F32)
+                square += value * value * table[k : k + 1, cols]
+                reward += value * table[k + 4 : k + 5, cols]
+        side[at, :LANES] = square
+        side[at, LANES:] = reward
+        return 0
+
+    lax.fori_loop(0, count // step, body, 0)
+
+
+def begin_kernel(head, sibling, near, far, z, a, b, c, z1, a1, b1, ids, acc, side, ids_out):
     count, depth = z.shape
     _, core, _ = here()
     mine, others = blocks(count)
@@ -128,13 +142,12 @@
         def _():
             rows = pl.ds(mine, count)
             acc[rows, :] = products([(z[...], near0), (same[...], far0), (z1[...], near1), (same1[...], far1)])
-            side[rows, :] = sides([(z[...], near, 0), (same[...], far, 0), (z1[...], near, 1), (same1[...], far, 1)])
+            add_sides([(z, near, 0), (same, far, 0), (z1, near, 1), (same1, far, 1)], mine, None, side)
             rows = pl.ds(others, count)
             acc[rows, :] = products([(cross[...], near0), (c[...], far0), (cross1[...], near1)])
-            side[rows, :] = sides([(cross[...], near, 0), (c[...], far, 0), (cross1[...], near, 1)])
+            add_sides([(cross, near, 0), (c, far, 0), (cross1, near, 1)], others, None, side)
 
     ids_out[...] = ids[...]
-    z2_out[...] = z2[...]
 
 
 def middle_kernel(head, sibling, near, far, acc_in, side_in, z, a, b, c, a2, acc, side, a2_out):
@@ -148,10 +161,10 @@
         def _():
             rows = pl.ds(mine, count)
             acc[rows, :] = acc_in[rows, :] + products([(z[...], near3), (same[...], far3)])
-            side[rows, :] = side_in[rows, :] + sides([(z[...], near, 3), (same[...], far, 3)])
+            add_sides([(z, near, 3), (same, far, 3)], mine, side_in, side)
             rows = pl.ds(others, count)
             acc[rows, :] = acc_in[rows, :] + products([(cross[...], near3), (c[...], far3)])
-            side[rows, :] = side_in[rows, :] + sides([(cross[...], near, 3), (c[...], far, 3)])
+            add_sides([(cross, near, 3), (c, far, 3)], others, side_in, side)
 
     a2_out[...] = a2[...]
 
@@ -184,7 +197,7 @@
     return jnp.sum(side[:, :LANES], axis=1, keepdims=True), jnp.sum(side[:, LANES:], axis=1, keepdims=True)
 
 
-def own_kernel(width, head, sibling, near, far, acc_in, side_in, z, a, b, c1, token_ids, left, left_side, far_out, wide):
+def own_kernel(width, head, sibling, near, far, acc_in, side_in, z, a, b, c1, token_ids, left, left_side, far_out, wide, side):
     count, depth = z.shape
     _, core, _ = here()
     mine, others = blocks(count)
@@ -201,20 +214,23 @@
         def _():
             rows = pl.ds(mine, count)
             logits = acc_in[rows, :] + products([(z[...], near2), (same[...], far2)])
-            square, reward = added(side_in[rows, :] + sides([(z[...], near, 2), (same[...], far, 2)]))
+            add_sides([(z, near, 2), (same, far, 2)], mine, side_in, side)
+            square, reward = added(side[rows, :])
             wide[rows, :] = summary(logits, square, reward, token_ids[rows, :], ids, width)
             rows = pl.ds(others, count)
             left[...] = acc_in[rows, :] + products([(cross[...], near2), (c1[...], far1)])
-            left_side[...] = side_in[rows, :] + sides([(cross[...], near, 2), (c1[...], far, 1)])
-
-
-def last_kernel(width, far_weights, far, left, left_side, c, wide_in, token_ids, out, wide):
+            add_sides([(cross, near, 2), (c1, far, 1)], others, side_in, side)
+            left_side[...] = side[rows, :]
+
+
+def last_kernel(width, far_weights, far, left, left_side, c, wide_in, token_ids, out, wide, side):
     count = c.shape[0]
     _, others = blocks(count)
     ids = column_ids(far_weights.shape[1] // 2)
     wide[...] = wide_in[...]
     logits = left[...] + jnp.dot(c[...], far_weights[...], preferred_element_type=F32)
-    square, reward = added(left_side[...] + sides([(c[...], far, 2)]))
+    add_sides([(c, far, 2)], 0, left_side, side)
+    square, reward = added(side[...])
     rows = pl.ds(others, count)
     wide[rows, :] = summary(logits, square, reward, token_ids[rows, :], ids, width)
     out[...] = jnp.transpose(wide[...])[:8]
@@ -299,7 +315,10 @@
     ids_shape = jax.ShapeDtypeStruct((2 * count, 1), I32)
     perm_z = {k: mesh_perm(lambda s, d, k=k: (s, d ^ (2 * k))) for k in (1, 2, 3)}
     perm_x = mesh_perm(lambda s, d: (s, d ^ 1))
-    table = jnp.stack([norm_gain, reward_head]).astype(F32)
+    gain = norm_gain[None]
+    table = call(
+        table_kernel, jax.ShapeDtypeStruct((2, part), F32), [VMEM] * 3 + [SMEM], (gain, reward_head[None], rows, lengths)
+    )
 
     swap = [(s, s ^ 1) for s in range(sections)]
     over = [(s, s ^ 2) for s in range(sections)]
@@ -310,15 +329,13 @@
     if groups == 8:
         tables = [table] + [send(table, perm_z[k]) for k in (1, 2, 3)]
         near = jnp.concatenate([t[i : i + 1] for i in range(2) for t in tables])
-        far = send(near, perm_x)
     else:
         near = jnp.concatenate([jnp.broadcast_to(table[i : i + 1], (4, part)) for i in range(2)])
-        far = near
-    full, near, far = call(
+    full, near = call(
         functools.partial(pick_kernel, count),
-        [jax.ShapeDtypeStruct((count, part), BF16), like(near), like(far)],
-        [SMEM] + [VMEM] * 5,
-        (lengths, rows, sibling, extra, near, far),
+        [jax.ShapeDtypeStruct((count, part), BF16), like(near)],
+        [SMEM] + [VMEM] * 5 + [ANY],
+        (lengths, rows, sibling, extra, gain, near, head_sibling),
     )
     token_ids = call(functools.partial(token_kernel, count), ids_shape, [SMEM, VMEM], (lengths, tokens))
 
@@ -334,21 +351,23 @@
         z3 = send(full, perm_z[3])
         a0 = send(full, perm_a)
         b0 = send(full, perm_b)
-        c0 = send(a0, perm_b)
+        far = send(near, perm_x)
         z1 = gate(z1, b0)
         a1 = send(z1, perm_a)
         b1 = send(z1, perm_b)
-        z3 = gate(z3, a1, b1, c0)
+        c0 = send(a0, perm_b)
+        z3 = gate(z3, a1, b1, c0, far)
         a3 = send(z3, perm_a)
         b3 = send(z3, perm_b)
         z2 = send(z3, perm_z[1])
+        acc, side, token_ids = call(
+            begin_kernel,
+            [acc_shape, side_shape, ids_shape],
+            [VMEM] * 12,
+            (head, head_sibling, near, far, full, a0, b0, c0, z1, a1, b1, token_ids),
+        )
+        a3 = gate(a3, token_ids)
         c3 = send(a3, perm_b)
-        acc, side, token_ids, z2 = call(
-            begin_kernel,
-            [acc_shape, side_shape, ids_shape, like(z2)],
-            [VMEM] * 13,
-            (head, head_sibling, near, far, full, a0, b0, c0, z1, a1, b1, token_ids, z2),
-        )
         a2 = send(z2, perm_a)
         b2 = send(z2, perm_b)
         c1 = send(c0, perm_z[1])
@@ -369,13 +388,14 @@
             ],
             [VMEM] * 11,
             (head, head_sibling, near, far, acc, side, z2, a2, b2, c1, token_ids),
+            scratch=[pltpu.VMEM((2 * count, 2 * LANES), F32)],
         )
         stats = call(
             functools.partial(last_kernel, width),
             stats_shape,
             [VMEM] * 7,
             (far_weights, far, left, left_side, c2, wide, token_ids),
-            scratch=[pltpu.VMEM((up(2 * count), LANES), F32)],
+            scratch=[pltpu.VMEM((up(2 * count), LANES), F32), pltpu.VMEM((count, 2 * LANES), F32)],
         )
         stats = combine([stats] + [send(stats, perm_z[k]) for k in (1, 2, 3)])
         stats = combine(
@@ -391,7 +411,7 @@
         )
         gains, weights_all = (lax.all_gather(t, "dp", axis=0, tiled=True) for t in table)
         wide = everything.astype(F32)
-        square = jnp.sum((wide / gains) ** 2, axis=1, keepdims=True)
+        square = jnp.sum(wide * wide * gains, axis=1, keepdims=True)
         reward = jnp.sum(wide * weights_all, axis=1, keepdims=True)
         stats = call(
             functools.partial(whole_kernel, width), stats_shape, [VMEM] * 4, (acc, square, reward, token_ids)

time: 134 us -> 132 us (0.985)
  waiting for transfers between devices: 70.7 us -> 59 us
  starting transfers between devices: 33.3 us -> 42 us
    ppermute x25, waiting for transfers between devices: 69.5 us -> 58.1 us  [per_device(): send = lambda value, perm: lax.ppermute(value, AXES, perm)]
    ppermute x1, starting transfers between devices: 0.02 us -> 11.3 us  [per_device(): stats = both(lp, lax.ppermute(lp, 'section', swap))]
    ppermute x25, starting transfers between devices: 32.1 us -> 29.5 us  [per_device(): send = lambda value, perm: lax.ppermute(value, AXES, perm)]
    another operation x2 -> x0, local copies, waits for them, and re-layouts: 1.37 us -> none  [per_device(): table = jnp.stack([norm_gain, reward_head]).astype(F32)]
    broadcast_in_dim x0 -> x2, local copies, waits for them, and re-layouts: none -> 1.37 us  [the longest x1 0.69 us: per_device(): gain = norm_gain[None]]
    pallas_call x9 -> x11, Pallas kernels: 24.5 us -> 25.1 us  [call(): pl.pallas_call(body, out_shape=outs, in_specs=in_specs, out_specs=[VMEM]...]
  transfers between devices with their start and end apart: 29 -> 29, of which waited for: 17 -> 19; matrix products, arithmetic and copies ran while one was open for 2% -> 2% of each run, Pallas kernels for 16% -> 15%
where the time goes in v8:
time: 132 us; the launch traced here: 131 us
  waiting for transfers between devices  59 us (45%)
  starting transfers between devices  42 us (32%)
  Pallas kernels  25.1 us (19%)
  local copies, waits for them, and re-layouts  4.08 us (3%)
    ppermute x25, waiting for transfers between devices, per_device(): send = lambda value, perm: lax.ppermute(value, AXES, perm)  58.1 us
    ppermute x25, starting transfers between devices, per_device(): send = lambda value, perm: lax.ppermute(value, AXES, perm)  29.5 us
    pallas_call x11, Pallas kernels, call(): pl.pallas_call(body, out_shape=outs, in_specs=in_specs, out_specs=[VMEM]...  25.1 us
    ppermute x1, starting transfers between devices, per_device(): stats = both(lp, lax.ppermute(lp, 'section', swap))  11.3 us
  transfers between devices with their start and end apart: 29, of which 19 were waited for; matrix products, arithmetic and copies ran while one was open for 2% of the time, Pallas kernels for 15%

profile of v8, /device:TPU:0, one launch (start us, length us, event | category | flops | bytes accessed | tf_op | source)
XLA Modules:
  0.0 131.3 jit_solution(1524645270514184160)
XLA Ops:
  0.6 0.5 collective-permute-start
  1.1 0.7 broadcast_in_dim.12.gain
  1.8 0.7 broadcast_in_dim.13.reward
  2.5 0.7 copy-done.1
  3.2 1.2 shard_map.77
  4.3 4.7 %collective-permute-start.5 = (f32[2,1024]{1,0:T(2,128)S(1)}, f32[2,1024]{1,0:T(2,128)S(1)}, u32[]{:S(2)}, u32[]{:S(2)}) collective-permute-start(f32[2,1024]{1,0:T(2,128)S(1)} %shard_map.77), channel_id=1, source_target_pairs={{0,6},{1,7},{2,4},{3,5},{4,2},{5,3},{6,0},{7,1},{8,14},{9,15},{10,... | collective-permute-start | bytes 24584 | tf_op jit(solution)/shard_map/ppermute | solution.py:311
  9.0 0.6 collective-permute-start.3
  9.7 1.0 slice_bitcast_fusion
  10.7 0.7 collective-permute-start.2
  11.4 2.1 %collective-permute-done.4 = f32[2,1024]{1,0:T(2,128)S(1)} collective-permute-done((f32[2,1024]{1,0:T(2,128)S(1)}, f32[2,1024]{1,0:T(2,128)S(1)}, u32[]{:S(2)}, u32[]{:S(2)}) %collective-permute-start.4) | collective-permute-done | bytes 8224 | tf_op jit(solution)/shard_map/ppermute | solution.py:311
  13.7 0.8 copy-done.2
  14.5 2.4 %shard_map.78 = (bf16[288,1024]{1,0:T(8,128)(2,1)S(1)}, f32[8,1024]{1,0:T(8,128)S(1)}) custom-call(s32[4]{0:T(128)S(1)} %copy-done.2, bf16[384,1024]{1,0:T(8,128)(2,1)} %bitcast.rows, bf16[384,1024]{1,0:T(8,128)(2,1)S(1)} %collective-permute-done.1.sibling, bf16[192,1024]{1,0:T(8,128)(2,1)S(1)} %collective-permute-done.2.extra, ...), custom_call_target="tpu_custom_call" | custom-call | tf_op jit(solution)/shard_map/pallas_call | solution.py:279
  16.9 1.6 %collective-permute-start.8 = (bf16[288,1024]{1,0:T(8,128)(2,1)S(1)}, bf16[288,1024]{1,0:T(8,128)(2,1)S(1)}, u32[]{:S(2)}, u32[]{:S(2)}) collective-permute-start(bf16[288,1024]{1,0:T(8,128)(2,1)S(1)} %get-tuple-element.17.z), channel_id=1, source_target_pairs={{0,16},{1,17},{2,18},{3,19},{4,20},{5,21},{6,22},{7,23},{8,9},{9,8... | collective-permute-start | bytes 1769480 | tf_op jit(solution)/shard_map/ppermute | solution.py:311
  18.5 1.5 %collective-permute-start.7 = (bf16[288,1024]{1,0:T(8,128)(2,1)S(1)}, bf16[288,1024]{1,0:T(8,128)(2,1)S(1)}, u32[]{:S(2)}, u32[]{:S(2)}) collective-permute-start(bf16[288,1024]{1,0:T(8,128)(2,1)S(1)} %get-tuple-element.17.z), channel_id=1, source_target_pairs={{0,1},{1,0},{2,3},{3,2},{4,5},{5,4},{6,7},{7,6},{8,24},{9,25},{10,... | collective-permute-start | bytes 1769480 | tf_op jit(solution)/shard_map/ppermute | solution.py:311
  20.0 3.5 %collective-permute-start.13 = (bf16[288,1024]{1,0:T(8,128)(2,1)S(1)}, bf16[288,1024]{1,0:T(8,128)(2,1)S(1)}, u32[]{:S(2)}, u32[]{:S(2)}) collective-permute-start(bf16[288,1024]{1,0:T(8,128)(2,1)S(1)} %get-tuple-element.17.z), channel_id=1, source_target_pairs={{0,6},{1,7},{2,4},{3,5},{4,2},{5,3},{6,0},{7,1},{8,14},{9,15},{10,... | collective-permute-start | bytes 1769480 | tf_op jit(solution)/shard_map/ppermute | solution.py:311
  23.5 3.4 %collective-permute-done.8.refs_0_.b = bf16[288,1024]{1,0:T(8,128)(2,1)S(1)} collective-permute-done((bf16[288,1024]{1,0:T(8,128)(2,1)S(1)}, bf16[288,1024]{1,0:T(8,128)(2,1)S(1)}, u32[]{:S(2)}, u32[]{:S(2)}) %collective-permute-start.8) | collective-permute-done | bytes 589856 | tf_op jit(solution)/shard_map/ppermute | solution.py:311
  26.9 2.6 %collective-permute-done.10.value = bf16[288,1024]{1,0:T(8,128)(2,1)S(1)} collective-permute-done((bf16[288,1024]{1,0:T(8,128)(2,1)S(1)}, bf16[288,1024]{1,0:T(8,128)(2,1)S(1)}, u32[]{:S(2)}, u32[]{:S(2)}) %collective-permute-start.10) | collective-permute-done | bytes 589856 | tf_op jit(solution)/shard_map/ppermute | solution.py:311
  29.6 2.5 %collective-permute-start.11 = (bf16[288,1024]{1,0:T(8,128)(2,1)S(1)}, bf16[288,1024]{1,0:T(8,128)(2,1)S(1)}, u32[]{:S(2)}, u32[]{:S(2)}) collective-permute-start(bf16[288,1024]{1,0:T(8,128)(2,1)S(1)} %shard_map.79.z1), channel_id=1, source_target_pairs={{0,1},{1,0},{2,3},{3,2},{4,5},{5,4},{6,7},{7,6},{8,24},{9,25},{10,... | collective-permute-start | bytes 1769480 | tf_op jit(solution)/shard_map/ppermute | solution.py:311
  32.1 2.0 %collective-permute-start.9 = (bf16[288,1024]{1,0:T(8,128)(2,1)S(1)}, bf16[288,1024]{1,0:T(8,128)(2,1)S(1)}, u32[]{:S(2)}, u32[]{:S(2)}) collective-permute-start(bf16[288,1024]{1,0:T(8,128)(2,1)S(1)} %collective-permute-done.7.a), channel_id=1, source_target_pairs={{0,16},{1,17},{2,18},{3,19},{4,20},{5,21},{6,22},{7,23},{8,9},{9,8... | collective-permute-start | bytes 1769480 | tf_op jit(solution)/shard_map/ppermute | solution.py:311
  34.2 7.2 %collective-permute-done.6.far.refs_3_ = f32[8,1024]{1,0:T(8,128)S(1)} collective-permute-done((f32[8,1024]{1,0:T(8,128)S(1)}, f32[8,1024]{1,0:T(8,128)S(1)}, u32[]{:S(2)}, u32[]{:S(2)}) %collective-permute-start.6) | collective-permute-done | bytes 32800 | tf_op jit(solution)/shard_map/ppermute | solution.py:311
  41.4 1.3 collective-permute-done.13.value
  42.7 11.4 %collective-permute-done.9.c.refs_2_ = bf16[288,1024]{1,0:T(8,128)(2,1)S(1)} collective-permute-done((bf16[288,1024]{1,0:T(8,128)(2,1)S(1)}, bf16[288,1024]{1,0:T(8,128)(2,1)S(1)}, u32[]{:S(2)}, u32[]{:S(2)}) %collective-permute-start.9) | collective-permute-done | bytes 589856 | tf_op jit(solution)/shard_map/ppermute | solution.py:311
  54.3 1.0 shard_map.80.ids
  55.3 0.8 collective-permute-start.15
  56.1 6.8 %shard_map.81 = (f32[576,512]{1,0:T(8,128)S(1)}, f32[576,256]{1,0:T(8,128)S(1)}, s32[576,1]{1,0:T(8,128)S(1)}) custom-call(bf16[8192,256]{1,0:T(8,128)(2,1)S(1)} %copy-done, bf16[8192,256]{1,0:T(8,128)(2,1)} %collective-permute-done.after.sibling, f32[8,1024]{1,0:T(8,128)S(1)} %get-tuple-element.16.near, f32[8,1024]{1,0:T(8,128)S(1)} %collective-permute-done.6.far.refs_3_, ...), custom_call_target="tpu_custom_call" | custom-call | tf_op jit(solution)/shard_map/pallas_call | solution.py:279
  62.9 1.8 %collective-permute-done.14.value = bf16[288,1024]{1,0:T(8,128)(2,1)S(1)} collective-permute-done((bf16[288,1024]{1,0:T(8,128)(2,1)S(1)}, bf16[288,1024]{1,0:T(8,128)(2,1)S(1)}, u32[]{:S(2)}, u32[]{:S(2)}) %collective-permute-start.14) | collective-permute-done | bytes 589856 | tf_op jit(solution)/shard_map/ppermute | solution.py:311
  64.8 3.3 %collective-permute-done.17.z = bf16[288,1024]{1,0:T(8,128)(2,1)S(1)} collective-permute-done((bf16[288,1024]{1,0:T(8,128)(2,1)S(1)}, bf16[288,1024]{1,0:T(8,128)(2,1)S(1)}, u32[]{:S(2)}, u32[]{:S(2)}) %collective-permute-start.17) | collective-permute-done | bytes 589856 | tf_op jit(solution)/shard_map/ppermute | solution.py:311
  68.1 1.4 %collective-permute-start.18 = (bf16[288,1024]{1,0:T(8,128)(2,1)S(1)}, bf16[288,1024]{1,0:T(8,128)(2,1)S(1)}, u32[]{:S(2)}, u32[]{:S(2)}) collective-permute-start(bf16[288,1024]{1,0:T(8,128)(2,1)S(1)} %collective-permute-done.17.z), channel_id=1, source_target_pairs={{0,1},{1,0},{2,3},{3,2},{4,5},{5,4},{6,7},{7,6},{8,24},{9,25},{10,... | collective-permute-start | bytes 1769480 | tf_op jit(solution)/shard_map/ppermute | solution.py:311
  69.5 1.8 %collective-permute-done.15.b = bf16[288,1024]{1,0:T(8,128)(2,1)S(1)} collective-permute-done((bf16[288,1024]{1,0:T(8,128)(2,1)S(1)}, bf16[288,1024]{1,0:T(8,128)(2,1)S(1)}, u32[]{:S(2)}, u32[]{:S(2)}) %collective-permute-start.15) | collective-permute-done | bytes 589856 | tf_op jit(solution)/shard_map/ppermute | solution.py:311
  71.4 9.7 %collective-permute-done.16.c = bf16[288,1024]{1,0:T(8,128)(2,1)S(1)} collective-permute-done((bf16[288,1024]{1,0:T(8,128)(2,1)S(1)}, bf16[288,1024]{1,0:T(8,128)(2,1)S(1)}, u32[]{:S(2)}, u32[]{:S(2)}) %collective-permute-start.16) | collective-permute-done | bytes 589856 | tf_op jit(solution)/shard_map/ppermute | solution.py:311
  81.0 0.4 collective-permute-done.18.a2
  81.4 5.0 %shard_map.84 = (f32[576,512]{1,0:T(8,128)S(1)}, f32[576,256]{1,0:T(8,128)S(1)}, bf16[288,1024]{1,0:T(8,128)(2,1)S(1)}) custom-call(bf16[8192,256]{1,0:T(8,128)(2,1)S(1)} %copy-done, bf16[8192,256]{1,0:T(8,128)(2,1)} %collective-permute-done.after.sibling, f32[8,1024]{1,0:T(8,128)S(1)} %get-tuple-element.16.near, ...), custom_call_target="tpu_custom_call" | custom-call | tf_op jit(solution)/shard_map/pallas_call | solution.py:279
  86.4 0.6 collective-permute-start.21
  87.1 3.4 %collective-permute-done.19.b = bf16[288,1024]{1,0:T(8,128)(2,1)S(1)} collective-permute-done((bf16[288,1024]{1,0:T(8,128)(2,1)S(1)}, bf16[288,1024]{1,0:T(8,128)(2,1)S(1)}, u32[]{:S(2)}, u32[]{:S(2)}) %collective-permute-start.19) | collective-permute-done | bytes 589856 | tf_op jit(solution)/shard_map/ppermute | solution.py:311
  90.5 5.4 %shard_map.85 = (f32[288,512]{1,0:T(8,128)S(1)}, f32[288,256]{1,0:T(8,128)S(1)}, bf16[1024,512]{1,0:T(8,128)(2,1)S(1)}, f32[640,128]{1,0:T(8,128)S(1)}) custom-call(bf16[8192,256]{1,0:T(8,128)(2,1)S(1)} %copy-done, bf16[8192,256]{1,0:T(8,128)(2,1)} %collective-permute-done.after.sibling, f32[8,1024]{1,0:T(8,128)S(1)} %get-tuple-element.16.near, ...), custom_call_target="tpu_custom_call" | custom-call | tf_op jit(solution)/shard_map/pallas_call | solution.py:279
  95.9 0.9 collective-permute-done.21.c
  96.8 1.4 %shard_map.86 = f32[8,640]{1,0:T(8,128)S(1)} custom-call(bf16[1024,512]{1,0:T(8,128)(2,1)S(1)} %get-tuple-element.24.far_weights, f32[8,1024]{1,0:T(8,128)S(1)} %collective-permute-done.6.far.refs_3_, f32[288,512]{1,0:T(8,128)S(1)} %get-tuple-element.25.left, f32[288,256]{1,0:T(8,128)S(1)} %get-tuple-element.26.left_side, ...), custom_call_target="tpu_custom_call" | custom-call | tf_op jit(solution)/shard_map/pallas_call | solution.py:279
  98.2 2.0 %collective-permute-start.22 = (f32[8,640]{1,0:T(8,128)S(1)}, f32[8,640]{1,0:T(8,128)S(1)}, u32[]{:S(2)}, u32[]{:S(2)}) collective-permute-start(f32[8,640]{1,0:T(8,128)S(1)} %shard_map.86), channel_id=1, source_target_pairs={{0,2},{1,3},{2,0},{3,1},{4,6},{5,7},{6,4},{7,5},{8,10},{9,11},{10,... | collective-permute-start | bytes 61448 | tf_op jit(solution)/shard_map/ppermute | solution.py:311
  100.3 3.0 %collective-permute-start.23 = (f32[8,640]{1,0:T(8,128)S(1)}, f32[8,640]{1,0:T(8,128)S(1)}, u32[]{:S(2)}, u32[]{:S(2)}) collective-permute-start(f32[8,640]{1,0:T(8,128)S(1)} %shard_map.86), channel_id=1, source_target_pairs={{0,4},{1,5},{2,6},{3,7},{4,0},{5,1},{6,2},{7,3},{8,12},{9,13},{10,... | collective-permute-start | bytes 61448 | tf_op jit(solution)/shard_map/ppermute | solution.py:311
  103.3 1.8 %collective-permute-done.23 = f32[8,640]{1,0:T(8,128)S(1)} collective-permute-done((f32[8,640]{1,0:T(8,128)S(1)}, f32[8,640]{1,0:T(8,128)S(1)}, u32[]{:S(2)}, u32[]{:S(2)}) %collective-permute-start.23) | collective-permute-done | bytes 20512 | tf_op jit(solution)/shard_map/ppermute | solution.py:311
  105.0 3.9 %collective-permute-done.24 = f32[8,640]{1,0:T(8,128)S(1)} collective-permute-done((f32[8,640]{1,0:T(8,128)S(1)}, f32[8,640]{1,0:T(8,128)S(1)}, u32[]{:S(2)}, u32[]{:S(2)}) %collective-permute-start.24) | collective-permute-done | bytes 20512 | tf_op jit(solution)/shard_map/ppermute | solution.py:311
  109.0 3.4 %collective-permute-start.25 = (f32[8,640]{1,0:T(8,128)S(1)}, f32[8,640]{1,0:T(8,128)S(1)}, u32[]{:S(2)}, u32[]{:S(2)}) collective-permute-start(f32[8,640]{1,0:T(8,128)S(1)} %concatenate.10), channel_id=1, source_target_pairs={{0,1},{1,0},{2,3},{3,2},{4,5},{5,4},{6,7},{7,6},{8,9},{9,8},{10,11... | collective-permute-start | bytes 61448 | tf_op jit(solution)/shard_map/ppermute | solution.py:311
  112.4 1.5 %collective-permute-start.27 = (f32[8,640]{1,0:T(8,128)S(1)}, f32[8,640]{1,0:T(8,128)S(1)}, u32[]{:S(2)}, u32[]{:S(2)}) collective-permute-start(f32[8,640]{1,0:T(8,128)S(1)} %concatenate.10), channel_id=1, source_target_pairs={{0,17},{1,16},{2,19},{3,18},{4,21},{5,20},{6,23},{7,22},{8,25},{9,... | collective-permute-start | bytes 61448 | tf_op jit(solution)/shard_map/ppermute | solution.py:311
  114.2 2.0 %collective-permute-done.26 = f32[8,640]{1,0:T(8,128)S(1)} collective-permute-done((f32[8,640]{1,0:T(8,128)S(1)}, f32[8,640]{1,0:T(8,128)S(1)}, u32[]{:S(2)}, u32[]{:S(2)}) %collective-permute-start.26) | collective-permute-done | bytes 20512 | tf_op jit(solution)/shard_map/ppermute | solution.py:311
  116.2 0.9 collective-permute-done.27
  117.2 11.3 %collective-permute-start.28 = (f32[8,640]{1,0:T(8,128)S(1)}, f32[8,640]{1,0:T(8,128)S(1)}, u32[]{:S(2)}, u32[]{:S(2)}) collective-permute-start(f32[8,640]{1,0:T(8,128)S(1)} %maximum_maximum_fusion), channel_id=1, source_target_pairs={{0,8},{8,0},{16,24},{24,16},{1,9},{9,1},{17,25},{25,17},{2,10},{10... | collective-permute-start | bytes 61448 | tf_op jit(solution)/shard_map/ppermute | solution.py:425
  128.5 0.8 collective-permute-done.28
  129.4 1.9 %shard_map.87 = (f32[1,384]{1,0:T(1,128)}, f32[1,1]{1,0:T(1,128)}) custom-call(s32[4]{0:T(128)S(1)} %copy-done.3, f32[2,8,640]{2,1,0:T(8,128)S(1)} %pad_maximum_fusion.stats), custom_call_target="tpu_custom_call" | custom-call | tf_op jit(solution)/shard_map/pallas_call | solution.py:279
  (48 shorter events, 1.1 us)
Async XLA Ops:
  0.6 13.1 %collective-permute-start = (bf16[8192,256]{1,0:T(8,128)(2,1)}, bf16[8192,256]{1,0:T(8,128)(2,1)}, u32[]{:S(2)}, u32[]{:S(2)}) collective-permute-start(bf16[8192,256]{1,0:T(8,128)(2,1)} %head.5), channel_id=1, source_target_pairs={{0,8},{8,0},{16,24},{24,16},{1,9},{9,1},{17,25},{25,17},{2,10},{10... | collective-permute-start | bytes 12582920 | tf_op jit(solution)/shard_map/ppermute | solution.py:327
  2.5 0.7 copy-start.1
  4.3 6.4 %collective-permute-start.5 = (f32[2,1024]{1,0:T(2,128)S(1)}, f32[2,1024]{1,0:T(2,128)S(1)}, u32[]{:S(2)}, u32[]{:S(2)}) collective-permute-start(f32[2,1024]{1,0:T(2,128)S(1)} %shard_map.77), channel_id=1, source_target_pairs={{0,6},{1,7},{2,4},{3,5},{4,2},{5,3},{6,0},{7,1},{8,14},{9,15},{10,... | collective-permute-start | bytes 24584 | tf_op jit(solution)/shard_map/ppermute | solution.py:311
  9.0 4.5 %collective-permute-start.4 = (f32[2,1024]{1,0:T(2,128)S(1)}, f32[2,1024]{1,0:T(2,128)S(1)}, u32[]{:S(2)}, u32[]{:S(2)}) collective-permute-start(f32[2,1024]{1,0:T(2,128)S(1)} %shard_map.77), channel_id=1, source_target_pairs={{0,4},{1,5},{2,6},{3,7},{4,0},{5,1},{6,2},{7,3},{8,12},{9,13},{10,... | collective-permute-start | bytes 24584 | tf_op jit(solution)/shard_map/ppermute | solution.py:311
  9.0 4.6 %collective-permute-start.3 = (f32[2,1024]{1,0:T(2,128)S(1)}, f32[2,1024]{1,0:T(2,128)S(1)}, u32[]{:S(2)}, u32[]{:S(2)}) collective-permute-start(f32[2,1024]{1,0:T(2,128)S(1)} %shard_map.77), channel_id=1, source_target_pairs={{0,2},{1,3},{2,0},{3,1},{4,6},{5,7},{6,4},{7,5},{8,10},{9,11},{10,... | collective-permute-start | bytes 24584 | tf_op jit(solution)/shard_map/ppermute | solution.py:311
  9.7 4.1 %collective-permute-start.1 = (bf16[384,1024]{1,0:T(8,128)(2,1)}, bf16[384,1024]{1,0:T(8,128)(2,1)S(1)}, u32[]{:S(2)}, u32[]{:S(2)}) collective-permute-start(bf16[384,1024]{1,0:T(8,128)(2,1)} %bitcast.rows), channel_id=1, source_target_pairs={{0,8},{8,0},{16,24},{24,16},{1,9},{9,1},{17,25},{25,17},{2,10},{10... | collective-permute-start | bytes 2359304 | tf_op jit(solution)/shard_map/ppermute | solution.py:326
  10.7 3.0 %collective-permute-start.2 = (bf16[192,1024]{1,0:T(8,128)(2,1)S(1)}, bf16[192,1024]{1,0:T(8,128)(2,1)S(1)}, u32[]{:S(2)}, u32[]{:S(2)}) collective-permute-start(bf16[192,1024]{1,0:T(8,128)(2,1)S(1)} %slice_bitcast_fusion), channel_id=1, source_target_pairs={{8,24},{24,8},{9,25},{25,9},{10,26},{26,10},{11,27},{27,11},{12,28... | collective-permute-start | bytes 1179656 | tf_op jit(solution)/shard_map/ppermute | solution.py:325
  13.6 40.7 %copy-start.3 = (s32[4]{0:T(128)S(1)}, s32[4]{0:T(128)}, u32[]{:S(2)}) copy-start(s32[4]{0:T(128)} %lengths.7) | copy-start | bytes 52
  13.6 40.7 %copy-start.4 = (s32[4,384]{1,0:T(4,128)S(1)}, s32[4,384]{1,0:T(4,128)}, u32[]{:S(2)}) copy-start(s32[4,384]{1,0:T(4,128)} %tokens.1) | copy-start | bytes 18436
  13.7 42.4 %copy-start = (bf16[8192,256]{1,0:T(8,128)(2,1)S(1)}, bf16[8192,256]{1,0:T(8,128)(2,1)}, u32[]{:S(2)}) copy-start(bf16[8192,256]{1,0:T(8,128)(2,1)} %head.5) | copy-start | bytes 12582916
  13.7 0.8 copy-start.2
  16.9 9.9 %collective-permute-start.8 = (bf16[288,1024]{1,0:T(8,128)(2,1)S(1)}, bf16[288,1024]{1,0:T(8,128)(2,1)S(1)}, u32[]{:S(2)}, u32[]{:S(2)}) collective-permute-start(bf16[288,1024]{1,0:T(8,128)(2,1)S(1)} %get-tuple-element.17.z), channel_id=1, source_target_pairs={{0,16},{1,17},{2,18},{3,19},{4,20},{5,21},{6,22},{7,23},{8,9},{9,8... | collective-permute-start | bytes 1769480 | tf_op jit(solution)/shard_map/ppermute | solution.py:311
  18.5 11.0 %collective-permute-start.10 = (bf16[288,1024]{1,0:T(8,128)(2,1)S(1)}, bf16[288,1024]{1,0:T(8,128)(2,1)S(1)}, u32[]{:S(2)}, u32[]{:S(2)}) collective-permute-start(bf16[288,1024]{1,0:T(8,128)(2,1)S(1)} %get-tuple-element.17.z), channel_id=1, source_target_pairs={{0,2},{1,3},{2,0},{3,1},{4,6},{5,7},{6,4},{7,5},{8,10},{9,11},{10,... | collective-permute-start | bytes 1769480 | tf_op jit(solution)/shard_map/ppermute | solution.py:311
  18.5 13.5 %collective-permute-start.7 = (bf16[288,1024]{1,0:T(8,128)(2,1)S(1)}, bf16[288,1024]{1,0:T(8,128)(2,1)S(1)}, u32[]{:S(2)}, u32[]{:S(2)}) collective-permute-start(bf16[288,1024]{1,0:T(8,128)(2,1)S(1)} %get-tuple-element.17.z), channel_id=1, source_target_pairs={{0,1},{1,0},{2,3},{3,2},{4,5},{5,4},{6,7},{7,6},{8,24},{9,25},{10,... | collective-permute-start | bytes 1769480 | tf_op jit(solution)/shard_map/ppermute | solution.py:311
  20.0 22.6 %collective-permute-start.13 = (bf16[288,1024]{1,0:T(8,128)(2,1)S(1)}, bf16[288,1024]{1,0:T(8,128)(2,1)S(1)}, u32[]{:S(2)}, u32[]{:S(2)}) collective-permute-start(bf16[288,1024]{1,0:T(8,128)(2,1)S(1)} %get-tuple-element.17.z), channel_id=1, source_target_pairs={{0,6},{1,7},{2,4},{3,5},{4,2},{5,3},{6,0},{7,1},{8,14},{9,15},{10,... | collective-permute-start | bytes 1769480 | tf_op jit(solution)/shard_map/ppermute | solution.py:311
  29.6 13.1 %collective-permute-start.11 = (bf16[288,1024]{1,0:T(8,128)(2,1)S(1)}, bf16[288,1024]{1,0:T(8,128)(2,1)S(1)}, u32[]{:S(2)}, u32[]{:S(2)}) collective-permute-start(bf16[288,1024]{1,0:T(8,128)(2,1)S(1)} %shard_map.79.z1), channel_id=1, source_target_pairs={{0,1},{1,0},{2,3},{3,2},{4,5},{5,4},{6,7},{7,6},{8,24},{9,25},{10,... | collective-permute-start | bytes 1769480 | tf_op jit(solution)/shard_map/ppermute | solution.py:311
  32.1 10.6 %collective-permute-start.12 = (bf16[288,1024]{1,0:T(8,128)(2,1)S(1)}, bf16[288,1024]{1,0:T(8,128)(2,1)S(1)}, u32[]{:S(2)}, u32[]{:S(2)}) collective-permute-start(bf16[288,1024]{1,0:T(8,128)(2,1)S(1)} %shard_map.79.z1), channel_id=1, source_target_pairs={{0,16},{1,17},{2,18},{3,19},{4,20},{5,21},{6,22},{7,23},{8,9},{9,8... | collective-permute-start | bytes 1769480 | tf_op jit(solution)/shard_map/ppermute | solution.py:311
  32.1 22.0 %collective-permute-start.9 = (bf16[288,1024]{1,0:T(8,128)(2,1)S(1)}, bf16[288,1024]{1,0:T(8,128)(2,1)S(1)}, u32[]{:S(2)}, u32[]{:S(2)}) collective-permute-start(bf16[288,1024]{1,0:T(8,128)(2,1)S(1)} %collective-permute-done.7.a), channel_id=1, source_target_pairs={{0,16},{1,17},{2,18},{3,19},{4,20},{5,21},{6,22},{7,23},{8,9},{9,8... | collective-permute-start | bytes 1769480 | tf_op jit(solution)/shard_map/ppermute | solution.py:311
  34.1 7.3 %collective-permute-start.6 = (f32[8,1024]{1,0:T(8,128)S(1)}, f32[8,1024]{1,0:T(8,128)S(1)}, u32[]{:S(2)}, u32[]{:S(2)}) collective-permute-start(f32[8,1024]{1,0:T(8,128)S(1)} %get-tuple-element.16.near), channel_id=1, source_target_pairs={{0,1},{1,0},{2,3},{3,2},{4,5},{5,4},{6,7},{7,6},{8,9},{9,8},{10,11... | collective-permute-start | bytes 98312 | tf_op jit(solution)/shard_map/ppermute | solution.py:311
  54.1 10.6 %collective-permute-start.14 = (bf16[288,1024]{1,0:T(8,128)(2,1)S(1)}, bf16[288,1024]{1,0:T(8,128)(2,1)S(1)}, u32[]{:S(2)}, u32[]{:S(2)}) collective-permute-start(bf16[288,1024]{1,0:T(8,128)(2,1)S(1)} %shard_map.82.z), channel_id=1, source_target_pairs={{0,1},{1,0},{2,3},{3,2},{4,5},{5,4},{6,7},{7,6},{8,24},{9,25},{10,... | collective-permute-start | bytes 1769480 | tf_op jit(solution)/shard_map/ppermute | solution.py:311
  54.2 13.9 %collective-permute-start.17 = (bf16[288,1024]{1,0:T(8,128)(2,1)S(1)}, bf16[288,1024]{1,0:T(8,128)(2,1)S(1)}, u32[]{:S(2)}, u32[]{:S(2)}) collective-permute-start(bf16[288,1024]{1,0:T(8,128)(2,1)S(1)} %shard_map.82.z), channel_id=1, source_target_pairs={{0,2},{1,3},{2,0},{3,1},{4,6},{5,7},{6,4},{7,5},{8,10},{9,11},{10,... | collective-permute-start | bytes 1769480 | tf_op jit(solution)/shard_map/ppermute | solution.py:311
  55.3 16.1 %collective-permute-start.15 = (bf16[288,1024]{1,0:T(8,128)(2,1)S(1)}, bf16[288,1024]{1,0:T(8,128)(2,1)S(1)}, u32[]{:S(2)}, u32[]{:S(2)}) collective-permute-start(bf16[288,1024]{1,0:T(8,128)(2,1)S(1)} %shard_map.82.z), channel_id=1, source_target_pairs={{0,16},{1,17},{2,18},{3,19},{4,20},{5,21},{6,22},{7,23},{8,9},{9,8... | collective-permute-start | bytes 1769480 | tf_op jit(solution)/shard_map/ppermute | solution.py:311
  64.8 16.3 %collective-permute-start.16 = (bf16[288,1024]{1,0:T(8,128)(2,1)S(1)}, bf16[288,1024]{1,0:T(8,128)(2,1)S(1)}, u32[]{:S(2)}, u32[]{:S(2)}) collective-permute-start(bf16[288,1024]{1,0:T(8,128)(2,1)S(1)} %shard_map.83.a), channel_id=1, source_target_pairs={{0,16},{1,17},{2,18},{3,19},{4,20},{5,21},{6,22},{7,23},{8,9},{9,8... | collective-permute-start | bytes 1769480 | tf_op jit(solution)/shard_map/ppermute | solution.py:311
  68.1 13.3 %collective-permute-start.18 = (bf16[288,1024]{1,0:T(8,128)(2,1)S(1)}, bf16[288,1024]{1,0:T(8,128)(2,1)S(1)}, u32[]{:S(2)}, u32[]{:S(2)}) collective-permute-start(bf16[288,1024]{1,0:T(8,128)(2,1)S(1)} %collective-permute-done.17.z), channel_id=1, source_target_pairs={{0,1},{1,0},{2,3},{3,2},{4,5},{5,4},{6,7},{7,6},{8,24},{9,25},{10,... | collective-permute-start | bytes 1769480 | tf_op jit(solution)/shard_map/ppermute | solution.py:311
  69.5 17.6 %collective-permute-start.20 = (bf16[288,1024]{1,0:T(8,128)(2,1)S(1)}, bf16[288,1024]{1,0:T(8,128)(2,1)S(1)}, u32[]{:S(2)}, u32[]{:S(2)}) collective-permute-start(bf16[288,1024]{1,0:T(8,128)(2,1)S(1)} %collective-permute-done.9.c.refs_2_), channel_id=1, source_target_pairs={{0,2},{1,3},{2,0},{3,1},{4,6},{5,7},{6,4},{7,5},{8,10},{9,11},{10,... | collective-permute-start | bytes 1769480 | tf_op jit(solution)/shard_map/ppermute | solution.py:311
  69.5 21.0 %collective-permute-start.19 = (bf16[288,1024]{1,0:T(8,128)(2,1)S(1)}, bf16[288,1024]{1,0:T(8,128)(2,1)S(1)}, u32[]{:S(2)}, u32[]{:S(2)}) collective-permute-start(bf16[288,1024]{1,0:T(8,128)(2,1)S(1)} %collective-permute-done.17.z), channel_id=1, source_target_pairs={{0,16},{1,17},{2,18},{3,19},{4,20},{5,21},{6,22},{7,23},{8,9},{9,8... | collective-permute-start | bytes 1769480 | tf_op jit(solution)/shard_map/ppermute | solution.py:311
  86.4 10.4 %collective-permute-start.21 = (bf16[288,1024]{1,0:T(8,128)(2,1)S(1)}, bf16[288,1024]{1,0:T(8,128)(2,1)S(1)}, u32[]{:S(2)}, u32[]{:S(2)}) collective-permute-start(bf16[288,1024]{1,0:T(8,128)(2,1)S(1)} %get-tuple-element.23.a), channel_id=1, source_target_pairs={{0,16},{1,17},{2,18},{3,19},{4,20},{5,21},{6,22},{7,23},{8,9},{9,8... | collective-permute-start | bytes 1769480 | tf_op jit(solution)/shard_map/ppermute | solution.py:311
  98.2 5.1 %collective-permute-start.22 = (f32[8,640]{1,0:T(8,128)S(1)}, f32[8,640]{1,0:T(8,128)S(1)}, u32[]{:S(2)}, u32[]{:S(2)}) collective-permute-start(f32[8,640]{1,0:T(8,128)S(1)} %shard_map.86), channel_id=1, source_target_pairs={{0,2},{1,3},{2,0},{3,1},{4,6},{5,7},{6,4},{7,5},{8,10},{9,11},{10,... | collective-permute-start | bytes 61448 | tf_op jit(solution)/shard_map/ppermute | solution.py:311
  100.3 4.8 %collective-permute-start.23 = (f32[8,640]{1,0:T(8,128)S(1)}, f32[8,640]{1,0:T(8,128)S(1)}, u32[]{:S(2)}, u32[]{:S(2)}) collective-permute-start(f32[8,640]{1,0:T(8,128)S(1)} %shard_map.86), channel_id=1, source_target_pairs={{0,4},{1,5},{2,6},{3,7},{4,0},{5,1},{6,2},{7,3},{8,12},{9,13},{10,... | collective-permute-start | bytes 61448 | tf_op jit(solution)/shard_map/ppermute | solution.py:311
  103.3 5.6 %collective-permute-start.24 = (f32[8,640]{1,0:T(8,128)S(1)}, f32[8,640]{1,0:T(8,128)S(1)}, u32[]{:S(2)}, u32[]{:S(2)}) collective-permute-start(f32[8,640]{1,0:T(8,128)S(1)} %shard_map.86), channel_id=1, source_target_pairs={{0,6},{1,7},{2,4},{3,5},{4,2},{5,3},{6,0},{7,1},{8,14},{9,15},{10,... | collective-permute-start | bytes 61448 | tf_op jit(solution)/shard_map/ppermute | solution.py:311
  109.0 5.2 %collective-permute-start.25 = (f32[8,640]{1,0:T(8,128)S(1)}, f32[8,640]{1,0:T(8,128)S(1)}, u32[]{:S(2)}, u32[]{:S(2)}) collective-permute-start(f32[8,640]{1,0:T(8,128)S(1)} %concatenate.10), channel_id=1, source_target_pairs={{0,1},{1,0},{2,3},{3,2},{4,5},{5,4},{6,7},{7,6},{8,9},{9,8},{10,11... | collective-permute-start | bytes 61448 | tf_op jit(solution)/shard_map/ppermute | solution.py:311
  112.4 3.8 %collective-permute-start.26 = (f32[8,640]{1,0:T(8,128)S(1)}, f32[8,640]{1,0:T(8,128)S(1)}, u32[]{:S(2)}, u32[]{:S(2)}) collective-permute-start(f32[8,640]{1,0:T(8,128)S(1)} %concatenate.10), channel_id=1, source_target_pairs={{0,16},{1,17},{2,18},{3,19},{4,20},{5,21},{6,22},{7,23},{8,24},{9,... | collective-permute-start | bytes 61448 | tf_op jit(solution)/shard_map/ppermute | solution.py:311
  112.4 4.7 %collective-permute-start.27 = (f32[8,640]{1,0:T(8,128)S(1)}, f32[8,640]{1,0:T(8,128)S(1)}, u32[]{:S(2)}, u32[]{:S(2)}) collective-permute-start(f32[8,640]{1,0:T(8,128)S(1)} %concatenate.10), channel_id=1, source_target_pairs={{0,17},{1,16},{2,19},{3,18},{4,21},{5,20},{6,23},{7,22},{8,25},{9,... | collective-permute-start | bytes 61448 | tf_op jit(solution)/shard_map/ppermute | solution.py:311
  117.2 12.1 %collective-permute-start.28 = (f32[8,640]{1,0:T(8,128)S(1)}, f32[8,640]{1,0:T(8,128)S(1)}, u32[]{:S(2)}, u32[]{:S(2)}) collective-permute-start(f32[8,640]{1,0:T(8,128)S(1)} %maximum_maximum_fusion), channel_id=1, source_target_pairs={{0,8},{8,0},{16,24},{24,16},{1,9},{9,1},{17,25},{25,17},{2,10},{10... | collective-permute-start | bytes 61448 | tf_op jit(solution)/shard_map/ppermute | solution.py:425

commit v9 on v8

--- a/solution.py
+++ b/solution.py
@@ -43,7 +43,8 @@
     return jnp.transpose(full)[:, which : which + 1]
 
 
-def table_kernel(gain, reward, rows, lengths, table):
+def table_kernel(gain, reward, rows, table, rows_out):
+    rows_out[...] = rows[...]
     value = gain[...].astype(F32)
     table[0:1, :] = 1.0 / (value * value)
     table[1:2, :] = reward[...].astype(F32)
@@ -121,8 +122,8 @@
             for c in range(depth // LANES):
                 cols = slice(c * LANES, (c + 1) * LANES)
                 value = piece[rows, cols].astype(F32)
-                square += value * value * table[k : k + 1, cols]
-                reward += value * table[k + 4 : k + 5, cols]
+                square += value * value * table[2 * k : 2 * k + 1, cols]
+                reward += value * table[2 * k + 1 : 2 * k + 2, cols]
         side[at, :LANES] = square
         side[at, LANES:] = reward
         return 0
@@ -150,7 +151,7 @@
     ids_out[...] = ids[...]
 
 
-def middle_kernel(head, sibling, near, far, acc_in, side_in, z, a, b, c, a2, acc, side, a2_out):
+def middle_kernel(head, sibling, near, far, acc_in, side_in, z, a, b, c, acc, side):
     count, depth = z.shape
     _, core, _ = here()
     mine, others = blocks(count)
@@ -165,8 +166,6 @@
             rows = pl.ds(others, count)
             acc[rows, :] = acc_in[rows, :] + products([(cross[...], near3), (c[...], far3)])
             add_sides([(cross, near, 3), (c, far, 3)], others, side_in, side)
-
-    a2_out[...] = a2[...]
 
 
 def gate_kernel(value, *refs):
@@ -316,21 +315,21 @@
     perm_z = {k: mesh_perm(lambda s, d, k=k: (s, d ^ (2 * k))) for k in (1, 2, 3)}
     perm_x = mesh_perm(lambda s, d: (s, d ^ 1))
     gain = norm_gain[None]
-    table = call(
-        table_kernel, jax.ShapeDtypeStruct((2, part), F32), [VMEM] * 3 + [SMEM], (gain, reward_head[None], rows, lengths)
-    )
 
     swap = [(s, s ^ 1) for s in range(sections)]
     over = [(s, s ^ 2) for s in range(sections)]
     extra = lax.ppermute(rows[half:], "section", [(1, 3), (3, 1)])
     sibling = lax.ppermute(rows, "section", swap)
     head_sibling = lax.ppermute(head, "section", swap)
+    table, rows = call(
+        table_kernel, [jax.ShapeDtypeStruct((2, part), F32), like(rows)], [VMEM] * 3, (gain, reward_head[None], rows)
+    )
 
     if groups == 8:
-        tables = [table] + [send(table, perm_z[k]) for k in (1, 2, 3)]
-        near = jnp.concatenate([t[i : i + 1] for i in range(2) for t in tables])
+        near = jnp.concatenate([table, send(table, perm_z[1])])
+        near = jnp.concatenate([near, send(near, perm_z[2])])
     else:
-        near = jnp.concatenate([jnp.broadcast_to(table[i : i + 1], (4, part)) for i in range(2)])
+        near = jnp.concatenate([table] * 4)
     full, near = call(
         functools.partial(pick_kernel, count),
         [jax.ShapeDtypeStruct((count, part), BF16), like(near)],
@@ -371,12 +370,13 @@
         a2 = send(z2, perm_a)
         b2 = send(z2, perm_b)
         c1 = send(c0, perm_z[1])
-        acc, side, a2 = call(
+        acc, side = call(
             middle_kernel,
-            [acc_shape, side_shape, like(a2)],
-            [VMEM] * 11,
-            (head, head_sibling, near, far, acc, side, z3, a3, b3, c3, a2),
-        )
+            [acc_shape, side_shape],
+            [VMEM] * 10,
+            (head, head_sibling, near, far, acc, side, z3, a3, b3, c3),
+        )
+        a2 = gate(a2, side)
         c2 = send(a2, perm_b)
         left, left_side, far_weights, wide = call(
             functools.partial(own_kernel, width),

time: 132 us -> 127 us (0.962)
  Pallas kernels: 25.1 us -> 16.9 us
  starting transfers between devices: 42 us -> 46.2 us
    ppermute x25 -> x24, starting transfers between devices: 29.5 us -> 44.9 us  [per_device(): send = lambda value, perm: lax.ppermute(value, AXES, perm)]
    ppermute x1, starting transfers between devices: 11.3 us -> 0.02 us  [per_device(): stats = both(lp, lax.ppermute(lp, 'section', swap))]
    pallas_call x11 -> x12, Pallas kernels: 25.1 us -> 16.9 us  [call(): pl.pallas_call(body, out_shape=outs, in_specs=in_specs, out_specs=[VMEM]...]
    ppermute x25 -> x24, waiting for transfers between devices: 58.1 us -> 56.7 us  [per_device(): send = lambda value, perm: lax.ppermute(value, AXES, perm)]
  transfers between devices with their start and end apart: 29 -> 28, of which waited for: 19 -> 16; matrix products, arithmetic and copies ran while one was open for 2% -> 2% of each run, Pallas kernels for 15% -> 10%
where the time goes in v9:
time: 127 us; the launch traced here: 126 us
  waiting for transfers between devices  57.9 us (46%)
  starting transfers between devices  46.2 us (36%)
  Pallas kernels  16.9 us (13%)
  local copies, waits for them, and re-layouts  4.3 us (3%)
    ppermute x24, waiting for transfers between devices, per_device(): send = lambda value, perm: lax.ppermute(value, AXES, perm)  56.7 us
    ppermute x24, starting transfers between devices, per_device(): send = lambda value, perm: lax.ppermute(value, AXES, perm)  44.9 us
    pallas_call x12, Pallas kernels, call(): pl.pallas_call(body, out_shape=outs, in_specs=in_specs, out_specs=[VMEM]...  16.9 us
  transfers between devices with their start and end apart: 28, of which 16 were waited for; matrix products, arithmetic and copies ran while one was open for 2% of the time, Pallas kernels for 10%

profile of v9, /device:TPU:0, one launch (start us, length us, event | category | flops | bytes accessed | tf_op | source)
XLA Modules:
  0.0 126.4 jit_solution(6116219102803898767)
XLA Ops:
  1.2 1.0 slice_bitcast_fusion
  2.3 0.7 collective-permute-start.2
  2.9 0.7 broadcast_in_dim.12.gain
  3.6 0.7 broadcast_in_dim.13.reward
  4.3 1.1 copy-done.1
  5.5 3.1 %collective-permute-start.3 = (f32[2,1024]{1,0:T(2,128)S(1)}, f32[2,1024]{1,0:T(2,128)S(1)}, u32[]{:S(2)}, u32[]{:S(2)}) collective-permute-start(f32[2,1024]{1,0:T(2,128)S(1)} %get-tuple-element.18), channel_id=1, source_target_pairs={{0,2},{1,3},{2,0},{3,1},{4,6},{5,7},{6,4},{7,5},{8,10},{9,11},{10,... | collective-permute-start | bytes 24584 | tf_op jit(solution)/shard_map/ppermute | solution.py:310
  8.6 1.6 %collective-permute-done.3 = f32[2,1024]{1,0:T(2,128)S(1)} collective-permute-done((f32[2,1024]{1,0:T(2,128)S(1)}, f32[2,1024]{1,0:T(2,128)S(1)}, u32[]{:S(2)}, u32[]{:S(2)}) %collective-permute-start.3) | collective-permute-done | bytes 8224 | tf_op jit(solution)/shard_map/ppermute | solution.py:310
  10.2 3.1 %collective-permute-start.4 = (f32[4,1024]{1,0:T(4,128)S(1)}, f32[4,1024]{1,0:T(4,128)S(1)}, u32[]{:S(2)}, u32[]{:S(2)}) collective-permute-start(f32[4,1024]{1,0:T(4,128)S(1)} %pad_maximum_fusion.2), channel_id=1, source_target_pairs={{0,4},{1,5},{2,6},{3,7},{4,0},{5,1},{6,2},{7,3},{8,12},{9,13},{10,... | collective-permute-start | bytes 49160 | tf_op jit(solution)/shard_map/ppermute | solution.py:310
  13.3 1.7 %collective-permute-done.4 = f32[4,1024]{1,0:T(4,128)S(1)} collective-permute-done((f32[4,1024]{1,0:T(4,128)S(1)}, f32[4,1024]{1,0:T(4,128)S(1)}, u32[]{:S(2)}, u32[]{:S(2)}) %collective-permute-start.4) | collective-permute-done | bytes 16416 | tf_op jit(solution)/shard_map/ppermute | solution.py:310
  15.1 0.6 copy-done.3
  15.8 1.6 %shard_map.78 = (bf16[288,1024]{1,0:T(8,128)(2,1)S(1)}, f32[8,1024]{1,0:T(8,128)S(1)}) custom-call(s32[4]{0:T(128)S(1)} %copy-done.3, bf16[384,1024]{1,0:T(8,128)(2,1)S(1)} %get-tuple-element.17.rows, bf16[384,1024]{1,0:T(8,128)(2,1)S(1)} %collective-permute-done.1.sibling, bf16[192,1024]{1,0:T(8,128)(2,1)S(1)} %collective-permute-done.2.extra, ...), custom_call_target="tpu_custom_call" | custom-call | tf_op jit(solution)/shard_map/pallas_call | solution.py:278
  17.4 1.9 %collective-permute-start.6 = (bf16[288,1024]{1,0:T(8,128)(2,1)S(1)}, bf16[288,1024]{1,0:T(8,128)(2,1)S(1)}, u32[]{:S(2)}, u32[]{:S(2)}) collective-permute-start(bf16[288,1024]{1,0:T(8,128)(2,1)S(1)} %get-tuple-element.20.z), channel_id=1, source_target_pairs={{0,1},{1,0},{2,3},{3,2},{4,5},{5,4},{6,7},{7,6},{8,24},{9,25},{10,... | collective-permute-start | bytes 1769480 | tf_op jit(solution)/shard_map/ppermute | solution.py:310
  19.2 1.5 %collective-permute-start.7 = (bf16[288,1024]{1,0:T(8,128)(2,1)S(1)}, bf16[288,1024]{1,0:T(8,128)(2,1)S(1)}, u32[]{:S(2)}, u32[]{:S(2)}) collective-permute-start(bf16[288,1024]{1,0:T(8,128)(2,1)S(1)} %get-tuple-element.20.z), channel_id=1, source_target_pairs={{0,16},{1,17},{2,18},{3,19},{4,20},{5,21},{6,22},{7,23},{8,9},{9,8... | collective-permute-start | bytes 1769480 | tf_op jit(solution)/shard_map/ppermute | solution.py:310
  20.8 1.6 %collective-permute-start.9 = (bf16[288,1024]{1,0:T(8,128)(2,1)S(1)}, bf16[288,1024]{1,0:T(8,128)(2,1)S(1)}, u32[]{:S(2)}, u32[]{:S(2)}) collective-permute-start(bf16[288,1024]{1,0:T(8,128)(2,1)S(1)} %get-tuple-element.20.z), channel_id=1, source_target_pairs={{0,2},{1,3},{2,0},{3,1},{4,6},{5,7},{6,4},{7,5},{8,10},{9,11},{10,... | collective-permute-start | bytes 1769480 | tf_op jit(solution)/shard_map/ppermute | solution.py:310
  22.4 2.5 %collective-permute-start.12 = (bf16[288,1024]{1,0:T(8,128)(2,1)S(1)}, bf16[288,1024]{1,0:T(8,128)(2,1)S(1)}, u32[]{:S(2)}, u32[]{:S(2)}) collective-permute-start(bf16[288,1024]{1,0:T(8,128)(2,1)S(1)} %get-tuple-element.20.z), channel_id=1, source_target_pairs={{0,6},{1,7},{2,4},{3,5},{4,2},{5,3},{6,0},{7,1},{8,14},{9,15},{10,... | collective-permute-start | bytes 1769480 | tf_op jit(solution)/shard_map/ppermute | solution.py:310
  24.8 8.6 %collective-permute-done.6.a = bf16[288,1024]{1,0:T(8,128)(2,1)S(1)} collective-permute-done((bf16[288,1024]{1,0:T(8,128)(2,1)S(1)}, bf16[288,1024]{1,0:T(8,128)(2,1)S(1)}, u32[]{:S(2)}, u32[]{:S(2)}) %collective-permute-start.6) | collective-permute-done | bytes 589856 | tf_op jit(solution)/shard_map/ppermute | solution.py:310
  33.4 2.0 %collective-permute-start.8 = (bf16[288,1024]{1,0:T(8,128)(2,1)S(1)}, bf16[288,1024]{1,0:T(8,128)(2,1)S(1)}, u32[]{:S(2)}, u32[]{:S(2)}) collective-permute-start(bf16[288,1024]{1,0:T(8,128)(2,1)S(1)} %collective-permute-done.6.a), channel_id=1, source_target_pairs={{0,16},{1,17},{2,18},{3,19},{4,20},{5,21},{6,22},{7,23},{8,9},{9,8... | collective-permute-start | bytes 1769480 | tf_op jit(solution)/shard_map/ppermute | solution.py:310
  35.4 0.7 collective-permute-done.9.value
  36.2 0.7 collective-permute-start.10
  37.2 1.5 %collective-permute-start.5 = (f32[8,1024]{1,0:T(8,128)S(1)}, f32[8,1024]{1,0:T(8,128)S(1)}, u32[]{:S(2)}, u32[]{:S(2)}) collective-permute-start(f32[8,1024]{1,0:T(8,128)S(1)} %get-tuple-element.19.near), channel_id=1, source_target_pairs={{0,1},{1,0},{2,3},{3,2},{4,5},{5,4},{6,7},{7,6},{8,9},{9,8},{10,11... | collective-permute-start | bytes 98312 | tf_op jit(solution)/shard_map/ppermute | solution.py:310
  38.7 14.5 %collective-permute-done.5.far.refs_3_ = f32[8,1024]{1,0:T(8,128)S(1)} collective-permute-done((f32[8,1024]{1,0:T(8,128)S(1)}, f32[8,1024]{1,0:T(8,128)S(1)}, u32[]{:S(2)}, u32[]{:S(2)}) %collective-permute-start.5) | collective-permute-done | bytes 32800 | tf_op jit(solution)/shard_map/ppermute | solution.py:310
  53.2 2.1 %collective-permute-done.11.b1.refs_1_ = bf16[288,1024]{1,0:T(8,128)(2,1)S(1)} collective-permute-done((bf16[288,1024]{1,0:T(8,128)(2,1)S(1)}, bf16[288,1024]{1,0:T(8,128)(2,1)S(1)}, u32[]{:S(2)}, u32[]{:S(2)}) %collective-permute-start.11) | collective-permute-done | bytes 589856 | tf_op jit(solution)/shard_map/ppermute | solution.py:310
  55.4 1.1 collective-permute-start.13
  56.4 1.6 %collective-permute-start.16 = (bf16[288,1024]{1,0:T(8,128)(2,1)S(1)}, bf16[288,1024]{1,0:T(8,128)(2,1)S(1)}, u32[]{:S(2)}, u32[]{:S(2)}) collective-permute-start(bf16[288,1024]{1,0:T(8,128)(2,1)S(1)} %shard_map.82.z), channel_id=1, source_target_pairs={{0,2},{1,3},{2,0},{3,1},{4,6},{5,7},{6,4},{7,5},{8,10},{9,11},{10,... | collective-permute-start | bytes 1769480 | tf_op jit(solution)/shard_map/ppermute | solution.py:310
  58.0 1.0 shard_map.80.ids
  59.0 1.6 %collective-permute-start.14 = (bf16[288,1024]{1,0:T(8,128)(2,1)S(1)}, bf16[288,1024]{1,0:T(8,128)(2,1)S(1)}, u32[]{:S(2)}, u32[]{:S(2)}) collective-permute-start(bf16[288,1024]{1,0:T(8,128)(2,1)S(1)} %shard_map.82.z), channel_id=1, source_target_pairs={{0,16},{1,17},{2,18},{3,19},{4,20},{5,21},{6,22},{7,23},{8,9},{9,8... | collective-permute-start | bytes 1769480 | tf_op jit(solution)/shard_map/ppermute | solution.py:310
  60.5 4.7 %shard_map.81 = (f32[576,512]{1,0:T(8,128)S(1)}, f32[576,256]{1,0:T(8,128)S(1)}, s32[576,1]{1,0:T(8,128)S(1)}) custom-call(bf16[8192,256]{1,0:T(8,128)(2,1)S(1)} %copy-done, bf16[8192,256]{1,0:T(8,128)(2,1)S(1)} %collective-permute-done.after.sibling, f32[8,1024]{1,0:T(8,128)S(1)} %get-tuple-element.19.near, ...), custom_call_target="tpu_custom_call" | custom-call | tf_op jit(solution)/shard_map/pallas_call | solution.py:278
  65.3 5.9 %collective-permute-done.13.value = bf16[288,1024]{1,0:T(8,128)(2,1)S(1)} collective-permute-done((bf16[288,1024]{1,0:T(8,128)(2,1)S(1)}, bf16[288,1024]{1,0:T(8,128)(2,1)S(1)}, u32[]{:S(2)}, u32[]{:S(2)}) %collective-permute-start.13) | collective-permute-done | bytes 589856 | tf_op jit(solution)/shard_map/ppermute | solution.py:310
  71.2 1.3 collective-permute-start.15
  72.9 2.4 %collective-permute-start.19 = (bf16[288,1024]{1,0:T(8,128)(2,1)S(1)}, bf16[288,1024]{1,0:T(8,128)(2,1)S(1)}, u32[]{:S(2)}, u32[]{:S(2)}) collective-permute-start(bf16[288,1024]{1,0:T(8,128)(2,1)S(1)} %collective-permute-done.8.c.refs_2_), channel_id=1, source_target_pairs={{0,2},{1,3},{2,0},{3,1},{4,6},{5,7},{6,4},{7,5},{8,10},{9,11},{10,... | collective-permute-start | bytes 1769480 | tf_op jit(solution)/shard_map/ppermute | solution.py:310
  75.4 0.6 collective-permute-start.18
  76.0 6.8 %collective-permute-done.15.c = bf16[288,1024]{1,0:T(8,128)(2,1)S(1)} collective-permute-done((bf16[288,1024]{1,0:T(8,128)(2,1)S(1)}, bf16[288,1024]{1,0:T(8,128)(2,1)S(1)}, u32[]{:S(2)}, u32[]{:S(2)}) %collective-permute-start.15) | collective-permute-done | bytes 589856 | tf_op jit(solution)/shard_map/ppermute | solution.py:310
  82.8 2.9 %shard_map.84 = (f32[576,512]{1,0:T(8,128)S(1)}, f32[576,256]{1,0:T(8,128)S(1)}) custom-call(bf16[8192,256]{1,0:T(8,128)(2,1)S(1)} %copy-done, bf16[8192,256]{1,0:T(8,128)(2,1)S(1)} %collective-permute-done.after.sibling, f32[8,1024]{1,0:T(8,128)S(1)} %get-tuple-element.19.near, f32[8,1024]{1,0:T(8,128)S(1)} %collective-permute-done.5.far.refs_3_, ...), custom_call_target="tpu_custom_call" | custom-call | tf_op jit(solution)/shard_map/pallas_call | solution.py:278
  85.6 3.1 %collective-permute-done.17.value = bf16[288,1024]{1,0:T(8,128)(2,1)S(1)} collective-permute-done((bf16[288,1024]{1,0:T(8,128)(2,1)S(1)}, bf16[288,1024]{1,0:T(8,128)(2,1)S(1)}, u32[]{:S(2)}, u32[]{:S(2)}) %collective-permute-start.17) | collective-permute-done | bytes 589856 | tf_op jit(solution)/shard_map/ppermute | solution.py:310
  88.7 0.9 collective-permute-start.20
  89.7 3.3 %shard_map.86 = (f32[288,512]{1,0:T(8,128)S(1)}, f32[288,256]{1,0:T(8,128)S(1)}, bf16[1024,512]{1,0:T(8,128)(2,1)S(1)}, f32[640,128]{1,0:T(8,128)S(1)}) custom-call(bf16[8192,256]{1,0:T(8,128)(2,1)S(1)} %copy-done, bf16[8192,256]{1,0:T(8,128)(2,1)S(1)} %collective-permute-done.after.sibling, f32[8,1024]{1,0:T(8,128)S(1)} %get-tuple-element.19.near, ...), custom_call_target="tpu_custom_call" | custom-call | tf_op jit(solution)/shard_map/pallas_call | solution.py:278
  92.9 5.8 %collective-permute-done.20.c = bf16[288,1024]{1,0:T(8,128)(2,1)S(1)} collective-permute-done((bf16[288,1024]{1,0:T(8,128)(2,1)S(1)}, bf16[288,1024]{1,0:T(8,128)(2,1)S(1)}, u32[]{:S(2)}, u32[]{:S(2)}) %collective-permute-start.20) | collective-permute-done | bytes 589856 | tf_op jit(solution)/shard_map/ppermute | solution.py:310
  98.7 1.4 %shard_map.87 = f32[8,640]{1,0:T(8,128)S(1)} custom-call(bf16[1024,512]{1,0:T(8,128)(2,1)S(1)} %get-tuple-element.26.far_weights, f32[8,1024]{1,0:T(8,128)S(1)} %collective-permute-done.5.far.refs_3_, f32[288,512]{1,0:T(8,128)S(1)} %get-tuple-element.27.left, f32[288,256]{1,0:T(8,128)S(1)} %get-tuple-element.28.left_side, ...), custom_call_target="tpu_custom_call" | custom-call | tf_op jit(solution)/shard_map/pallas_call | solution.py:278
  100.1 12.7 %collective-permute-start.23 = (f32[8,640]{1,0:T(8,128)S(1)}, f32[8,640]{1,0:T(8,128)S(1)}, u32[]{:S(2)}, u32[]{:S(2)}) collective-permute-start(f32[8,640]{1,0:T(8,128)S(1)} %shard_map.87), channel_id=1, source_target_pairs={{0,6},{1,7},{2,4},{3,5},{4,2},{5,3},{6,0},{7,1},{8,14},{9,15},{10,... | collective-permute-start | bytes 61448 | tf_op jit(solution)/shard_map/ppermute | solution.py:310
  112.7 0.6 collective-permute-start.21
  113.4 1.1 collective-permute-done.23
  114.5 2.9 %collective-permute-done.22 = f32[8,640]{1,0:T(8,128)S(1)} collective-permute-done((f32[8,640]{1,0:T(8,128)S(1)}, f32[8,640]{1,0:T(8,128)S(1)}, u32[]{:S(2)}, u32[]{:S(2)}) %collective-permute-start.22) | collective-permute-done | bytes 20512 | tf_op jit(solution)/shard_map/ppermute | solution.py:310
  117.5 1.3 collective-permute-start.26
  118.8 0.6 collective-permute-start.25
  119.4 1.7 %collective-permute-start.24 = (f32[8,640]{1,0:T(8,128)S(1)}, f32[8,640]{1,0:T(8,128)S(1)}, u32[]{:S(2)}, u32[]{:S(2)}) collective-permute-start(f32[8,640]{1,0:T(8,128)S(1)} %concatenate.15), channel_id=1, source_target_pairs={{0,1},{1,0},{2,3},{3,2},{4,5},{5,4},{6,7},{7,6},{8,9},{9,8},{10,11... | collective-permute-start | bytes 61448 | tf_op jit(solution)/shard_map/ppermute | solution.py:310
  121.1 1.1 collective-permute-done.26
  123.3 1.2 collective-permute-done.27
  124.6 1.9 %shard_map.88 = (f32[1,384]{1,0:T(1,128)}, f32[1,1]{1,0:T(1,128)}) custom-call(s32[4]{0:T(128)S(1)} %copy-done.4, f32[2,8,640]{2,1,0:T(8,128)S(1)} %pad_maximum_fusion.stats), custom_call_target="tpu_custom_call" | custom-call | tf_op jit(solution)/shard_map/pallas_call | solution.py:278
  (44 shorter events, 3.0 us)
Async XLA Ops:
  0.6 14.5 %collective-permute-start = (bf16[8192,256]{1,0:T(8,128)(2,1)}, bf16[8192,256]{1,0:T(8,128)(2,1)S(1)}, u32[]{:S(2)}, u32[]{:S(2)}) collective-permute-start(bf16[8192,256]{1,0:T(8,128)(2,1)} %head.5), channel_id=1, source_target_pairs={{0,8},{8,0},{16,24},{24,16},{1,9},{9,1},{17,25},{25,17},{2,10},{10... | collective-permute-start | bytes 12582920 | tf_op jit(solution)/shard_map/ppermute | solution.py:323
  1.1 13.9 %collective-permute-start.1 = (bf16[384,1024]{1,0:T(8,128)(2,1)}, bf16[384,1024]{1,0:T(8,128)(2,1)S(1)}, u32[]{:S(2)}, u32[]{:S(2)}) collective-permute-start(bf16[384,1024]{1,0:T(8,128)(2,1)} %bitcast.8), channel_id=1, source_target_pairs={{0,8},{8,0},{16,24},{24,16},{1,9},{9,1},{17,25},{25,17},{2,10},{10... | collective-permute-start | bytes 2359304 | tf_op jit(solution)/shard_map/ppermute | solution.py:322
  2.3 12.8 %collective-permute-start.2 = (bf16[192,1024]{1,0:T(8,128)(2,1)S(1)}, bf16[192,1024]{1,0:T(8,128)(2,1)S(1)}, u32[]{:S(2)}, u32[]{:S(2)}) collective-permute-start(bf16[192,1024]{1,0:T(8,128)(2,1)S(1)} %slice_bitcast_fusion), channel_id=1, source_target_pairs={{8,24},{24,8},{9,25},{25,9},{10,26},{26,10},{11,27},{27,11},{12,28... | collective-permute-start | bytes 1179656 | tf_op jit(solution)/shard_map/ppermute | solution.py:321
  4.3 1.1 copy-start.1
  5.5 4.7 %collective-permute-start.3 = (f32[2,1024]{1,0:T(2,128)S(1)}, f32[2,1024]{1,0:T(2,128)S(1)}, u32[]{:S(2)}, u32[]{:S(2)}) collective-permute-start(f32[2,1024]{1,0:T(2,128)S(1)} %get-tuple-element.18), channel_id=1, source_target_pairs={{0,2},{1,3},{2,0},{3,1},{4,6},{5,7},{6,4},{7,5},{8,10},{9,11},{10,... | collective-permute-start | bytes 24584 | tf_op jit(solution)/shard_map/ppermute | solution.py:310
  10.2 4.8 %collective-permute-start.4 = (f32[4,1024]{1,0:T(4,128)S(1)}, f32[4,1024]{1,0:T(4,128)S(1)}, u32[]{:S(2)}, u32[]{:S(2)}) collective-permute-start(f32[4,1024]{1,0:T(4,128)S(1)} %pad_maximum_fusion.2), channel_id=1, source_target_pairs={{0,4},{1,5},{2,6},{3,7},{4,0},{5,1},{6,2},{7,3},{8,12},{9,13},{10,... | collective-permute-start | bytes 49160 | tf_op jit(solution)/shard_map/ppermute | solution.py:310
  15.1 0.7 copy-start.3
  15.8 42.2 %copy-start.2 = (s32[4,384]{1,0:T(4,128)S(1)}, s32[4,384]{1,0:T(4,128)}, u32[]{:S(2)}) copy-start(s32[4,384]{1,0:T(4,128)} %tokens.1) | copy-start | bytes 18436
  15.8 44.8 %copy-start = (bf16[8192,256]{1,0:T(8,128)(2,1)S(1)}, bf16[8192,256]{1,0:T(8,128)(2,1)}, u32[]{:S(2)}) copy-start(bf16[8192,256]{1,0:T(8,128)(2,1)} %head.5) | copy-start | bytes 12582916
  17.4 16.1 %collective-permute-start.6 = (bf16[288,1024]{1,0:T(8,128)(2,1)S(1)}, bf16[288,1024]{1,0:T(8,128)(2,1)S(1)}, u32[]{:S(2)}, u32[]{:S(2)}) collective-permute-start(bf16[288,1024]{1,0:T(8,128)(2,1)S(1)} %get-tuple-element.20.z), channel_id=1, source_target_pairs={{0,1},{1,0},{2,3},{3,2},{4,5},{5,4},{6,7},{7,6},{8,24},{9,25},{10,... | collective-permute-start | bytes 1769480 | tf_op jit(solution)/shard_map/ppermute | solution.py:310
  19.2 16.2 %collective-permute-start.7 = (bf16[288,1024]{1,0:T(8,128)(2,1)S(1)}, bf16[288,1024]{1,0:T(8,128)(2,1)S(1)}, u32[]{:S(2)}, u32[]{:S(2)}) collective-permute-start(bf16[288,1024]{1,0:T(8,128)(2,1)S(1)} %get-tuple-element.20.z), channel_id=1, source_target_pairs={{0,16},{1,17},{2,18},{3,19},{4,20},{5,21},{6,22},{7,23},{8,9},{9,8... | collective-permute-start | bytes 1769480 | tf_op jit(solution)/shard_map/ppermute | solution.py:310
  20.8 15.4 %collective-permute-start.9 = (bf16[288,1024]{1,0:T(8,128)(2,1)S(1)}, bf16[288,1024]{1,0:T(8,128)(2,1)S(1)}, u32[]{:S(2)}, u32[]{:S(2)}) collective-permute-start(bf16[288,1024]{1,0:T(8,128)(2,1)S(1)} %get-tuple-element.20.z), channel_id=1, source_target_pairs={{0,2},{1,3},{2,0},{3,1},{4,6},{5,7},{6,4},{7,5},{8,10},{9,11},{10,... | collective-permute-start | bytes 1769480 | tf_op jit(solution)/shard_map/ppermute | solution.py:310
  22.4 30.9 %collective-permute-start.12 = (bf16[288,1024]{1,0:T(8,128)(2,1)S(1)}, bf16[288,1024]{1,0:T(8,128)(2,1)S(1)}, u32[]{:S(2)}, u32[]{:S(2)}) collective-permute-start(bf16[288,1024]{1,0:T(8,128)(2,1)S(1)} %get-tuple-element.20.z), channel_id=1, source_target_pairs={{0,6},{1,7},{2,4},{3,5},{4,2},{5,3},{6,0},{7,1},{8,14},{9,15},{10,... | collective-permute-start | bytes 1769480 | tf_op jit(solution)/shard_map/ppermute | solution.py:310
  33.4 19.8 %collective-permute-start.8 = (bf16[288,1024]{1,0:T(8,128)(2,1)S(1)}, bf16[288,1024]{1,0:T(8,128)(2,1)S(1)}, u32[]{:S(2)}, u32[]{:S(2)}) collective-permute-start(bf16[288,1024]{1,0:T(8,128)(2,1)S(1)} %collective-permute-done.6.a), channel_id=1, source_target_pairs={{0,16},{1,17},{2,18},{3,19},{4,20},{5,21},{6,22},{7,23},{8,9},{9,8... | collective-permute-start | bytes 1769480 | tf_op jit(solution)/shard_map/ppermute | solution.py:310
  36.2 17.0 %collective-permute-start.10 = (bf16[288,1024]{1,0:T(8,128)(2,1)S(1)}, bf16[288,1024]{1,0:T(8,128)(2,1)S(1)}, u32[]{:S(2)}, u32[]{:S(2)}) collective-permute-start(bf16[288,1024]{1,0:T(8,128)(2,1)S(1)} %shard_map.79.z1), channel_id=1, source_target_pairs={{0,1},{1,0},{2,3},{3,2},{4,5},{5,4},{6,7},{7,6},{8,24},{9,25},{10,... | collective-permute-start | bytes 1769480 | tf_op jit(solution)/shard_map/ppermute | solution.py:310
  36.9 18.4 %collective-permute-start.11 = (bf16[288,1024]{1,0:T(8,128)(2,1)S(1)}, bf16[288,1024]{1,0:T(8,128)(2,1)S(1)}, u32[]{:S(2)}, u32[]{:S(2)}) collective-permute-start(bf16[288,1024]{1,0:T(8,128)(2,1)S(1)} %shard_map.79.z1), channel_id=1, source_target_pairs={{0,16},{1,17},{2,18},{3,19},{4,20},{5,21},{6,22},{7,23},{8,9},{9,8... | collective-permute-start | bytes 1769480 | tf_op jit(solution)/shard_map/ppermute | solution.py:310
  37.2 16.0 %collective-permute-start.5 = (f32[8,1024]{1,0:T(8,128)S(1)}, f32[8,1024]{1,0:T(8,128)S(1)}, u32[]{:S(2)}, u32[]{:S(2)}) collective-permute-start(f32[8,1024]{1,0:T(8,128)S(1)} %get-tuple-element.19.near), channel_id=1, source_target_pairs={{0,1},{1,0},{2,3},{3,2},{4,5},{5,4},{6,7},{7,6},{8,9},{9,8},{10,11... | collective-permute-start | bytes 98312 | tf_op jit(solution)/shard_map/ppermute | solution.py:310
  55.4 15.8 %collective-permute-start.13 = (bf16[288,1024]{1,0:T(8,128)(2,1)S(1)}, bf16[288,1024]{1,0:T(8,128)(2,1)S(1)}, u32[]{:S(2)}, u32[]{:S(2)}) collective-permute-start(bf16[288,1024]{1,0:T(8,128)(2,1)S(1)} %shard_map.82.z), channel_id=1, source_target_pairs={{0,1},{1,0},{2,3},{3,2},{4,5},{5,4},{6,7},{7,6},{8,24},{9,25},{10,... | collective-permute-start | bytes 1769480 | tf_op jit(solution)/shard_map/ppermute | solution.py:310
  56.4 16.0 %collective-permute-start.16 = (bf16[288,1024]{1,0:T(8,128)(2,1)S(1)}, bf16[288,1024]{1,0:T(8,128)(2,1)S(1)}, u32[]{:S(2)}, u32[]{:S(2)}) collective-permute-start(bf16[288,1024]{1,0:T(8,128)(2,1)S(1)} %shard_map.82.z), channel_id=1, source_target_pairs={{0,2},{1,3},{2,0},{3,1},{4,6},{5,7},{6,4},{7,5},{8,10},{9,11},{10,... | collective-permute-start | bytes 1769480 | tf_op jit(solution)/shard_map/ppermute | solution.py:310
  59.0 17.0 %collective-permute-start.14 = (bf16[288,1024]{1,0:T(8,128)(2,1)S(1)}, bf16[288,1024]{1,0:T(8,128)(2,1)S(1)}, u32[]{:S(2)}, u32[]{:S(2)}) collective-permute-start(bf16[288,1024]{1,0:T(8,128)(2,1)S(1)} %shard_map.82.z), channel_id=1, source_target_pairs={{0,16},{1,17},{2,18},{3,19},{4,20},{5,21},{6,22},{7,23},{8,9},{9,8... | collective-permute-start | bytes 1769480 | tf_op jit(solution)/shard_map/ppermute | solution.py:310
  71.2 11.6 %collective-permute-start.15 = (bf16[288,1024]{1,0:T(8,128)(2,1)S(1)}, bf16[288,1024]{1,0:T(8,128)(2,1)S(1)}, u32[]{:S(2)}, u32[]{:S(2)}) collective-permute-start(bf16[288,1024]{1,0:T(8,128)(2,1)S(1)} %shard_map.83.a), channel_id=1, source_target_pairs={{0,16},{1,17},{2,18},{3,19},{4,20},{5,21},{6,22},{7,23},{8,9},{9,8... | collective-permute-start | bytes 1769480 | tf_op jit(solution)/shard_map/ppermute | solution.py:310
  72.4 16.3 %collective-permute-start.17 = (bf16[288,1024]{1,0:T(8,128)(2,1)S(1)}, bf16[288,1024]{1,0:T(8,128)(2,1)S(1)}, u32[]{:S(2)}, u32[]{:S(2)}) collective-permute-start(bf16[288,1024]{1,0:T(8,128)(2,1)S(1)} %collective-permute-done.16.z), channel_id=1, source_target_pairs={{0,1},{1,0},{2,3},{3,2},{4,5},{5,4},{6,7},{7,6},{8,24},{9,25},{10,... | collective-permute-start | bytes 1769480 | tf_op jit(solution)/shard_map/ppermute | solution.py:310
  72.9 16.7 %collective-permute-start.19 = (bf16[288,1024]{1,0:T(8,128)(2,1)S(1)}, bf16[288,1024]{1,0:T(8,128)(2,1)S(1)}, u32[]{:S(2)}, u32[]{:S(2)}) collective-permute-start(bf16[288,1024]{1,0:T(8,128)(2,1)S(1)} %collective-permute-done.8.c.refs_2_), channel_id=1, source_target_pairs={{0,2},{1,3},{2,0},{3,1},{4,6},{5,7},{6,4},{7,5},{8,10},{9,11},{10,... | collective-permute-start | bytes 1769480 | tf_op jit(solution)/shard_map/ppermute | solution.py:310
  75.4 14.3 %collective-permute-start.18 = (bf16[288,1024]{1,0:T(8,128)(2,1)S(1)}, bf16[288,1024]{1,0:T(8,128)(2,1)S(1)}, u32[]{:S(2)}, u32[]{:S(2)}) collective-permute-start(bf16[288,1024]{1,0:T(8,128)(2,1)S(1)} %collective-permute-done.16.z), channel_id=1, source_target_pairs={{0,16},{1,17},{2,18},{3,19},{4,20},{5,21},{6,22},{7,23},{8,9},{9,8... | collective-permute-start | bytes 1769480 | tf_op jit(solution)/shard_map/ppermute | solution.py:310
  88.7 9.9 %collective-permute-start.20 = (bf16[288,1024]{1,0:T(8,128)(2,1)S(1)}, bf16[288,1024]{1,0:T(8,128)(2,1)S(1)}, u32[]{:S(2)}, u32[]{:S(2)}) collective-permute-start(bf16[288,1024]{1,0:T(8,128)(2,1)S(1)} %shard_map.85.a), channel_id=1, source_target_pairs={{0,16},{1,17},{2,18},{3,19},{4,20},{5,21},{6,22},{7,23},{8,9},{9,8... | collective-permute-start | bytes 1769480 | tf_op jit(solution)/shard_map/ppermute | solution.py:310
  89.7 34.9 %copy-start.4 = (s32[4]{0:T(128)S(1)}, s32[4]{0:T(128)}, u32[]{:S(2)}) copy-start(s32[4]{0:T(128)} %lengths.5) | copy-start | bytes 52
  100.1 14.4 %collective-permute-start.23 = (f32[8,640]{1,0:T(8,128)S(1)}, f32[8,640]{1,0:T(8,128)S(1)}, u32[]{:S(2)}, u32[]{:S(2)}) collective-permute-start(f32[8,640]{1,0:T(8,128)S(1)} %shard_map.87), channel_id=1, source_target_pairs={{0,6},{1,7},{2,4},{3,5},{4,2},{5,3},{6,0},{7,1},{8,14},{9,15},{10,... | collective-permute-start | bytes 61448 | tf_op jit(solution)/shard_map/ppermute | solution.py:310
  112.7 4.7 %collective-permute-start.22 = (f32[8,640]{1,0:T(8,128)S(1)}, f32[8,640]{1,0:T(8,128)S(1)}, u32[]{:S(2)}, u32[]{:S(2)}) collective-permute-start(f32[8,640]{1,0:T(8,128)S(1)} %shard_map.87), channel_id=1, source_target_pairs={{0,4},{1,5},{2,6},{3,7},{4,0},{5,1},{6,2},{7,3},{8,12},{9,13},{10,... | collective-permute-start | bytes 61448 | tf_op jit(solution)/shard_map/ppermute | solution.py:310
  112.7 4.7 %collective-permute-start.21 = (f32[8,640]{1,0:T(8,128)S(1)}, f32[8,640]{1,0:T(8,128)S(1)}, u32[]{:S(2)}, u32[]{:S(2)}) collective-permute-start(f32[8,640]{1,0:T(8,128)S(1)} %shard_map.87), channel_id=1, source_target_pairs={{0,2},{1,3},{2,0},{3,1},{4,6},{5,7},{6,4},{7,5},{8,10},{9,11},{10,... | collective-permute-start | bytes 61448 | tf_op jit(solution)/shard_map/ppermute | solution.py:310
  117.5 4.7 %collective-permute-start.26 = (f32[8,640]{1,0:T(8,128)S(1)}, f32[8,640]{1,0:T(8,128)S(1)}, u32[]{:S(2)}, u32[]{:S(2)}) collective-permute-start(f32[8,640]{1,0:T(8,128)S(1)} %concatenate.15), channel_id=1, source_target_pairs={{0,17},{1,16},{2,19},{3,18},{4,21},{5,20},{6,23},{7,22},{8,25},{9,... | collective-permute-start | bytes 61448 | tf_op jit(solution)/shard_map/ppermute | solution.py:310
  118.8 3.8 %collective-permute-start.25 = (f32[8,640]{1,0:T(8,128)S(1)}, f32[8,640]{1,0:T(8,128)S(1)}, u32[]{:S(2)}, u32[]{:S(2)}) collective-permute-start(f32[8,640]{1,0:T(8,128)S(1)} %concatenate.15), channel_id=1, source_target_pairs={{0,16},{1,17},{2,18},{3,19},{4,20},{5,21},{6,22},{7,23},{8,24},{9,... | collective-permute-start | bytes 61448 | tf_op jit(solution)/shard_map/ppermute | solution.py:310
  119.4 3.8 %collective-permute-start.24 = (f32[8,640]{1,0:T(8,128)S(1)}, f32[8,640]{1,0:T(8,128)S(1)}, u32[]{:S(2)}, u32[]{:S(2)}) collective-permute-start(f32[8,640]{1,0:T(8,128)S(1)} %concatenate.15), channel_id=1, source_target_pairs={{0,1},{1,0},{2,3},{3,2},{4,5},{5,4},{6,7},{7,6},{8,9},{9,8},{10,11... | collective-permute-start | bytes 61448 | tf_op jit(solution)/shard_map/ppermute | solution.py:310
  123.3 1.2 collective-permute-start.27

commit v10 on v9

--- a/solution.py
+++ b/solution.py
@@ -131,22 +131,26 @@
     lax.fori_loop(0, count // step, body, 0)
 
 
+def both_weights(head, sibling, depth, k):
+    return weights(head, sibling, depth, k, False), weights(head, sibling, depth, k, True)
+
+
 def begin_kernel(head, sibling, near, far, z, a, b, c, z1, a1, b1, ids, acc, side, ids_out):
     count, depth = z.shape
     _, core, _ = here()
     mine, others = blocks(count)
-    near0, far0 = weights(head, sibling, depth, 0, False), weights(head, sibling, depth, 0, True)
-    near1, far1 = weights(head, sibling, depth, 1, False), weights(head, sibling, depth, 1, True)
-    for which, same, cross, same1, cross1 in ((0, a, b, a1, b1), (1, b, a, b1, a1)):
+    near0, far0 = both_weights(head, sibling, depth, 0)
+    for which, k, same, cross, same1, cross1 in ((0, 1, a, b, a1, b1), (1, 3, b, a, b1, a1)):
 
         @pl.when(core == which)
         def _():
+            near1, far1 = both_weights(head, sibling, depth, k)
             rows = pl.ds(mine, count)
             acc[rows, :] = products([(z[...], near0), (same[...], far0), (z1[...], near1), (same1[...], far1)])
-            add_sides([(z, near, 0), (same, far, 0), (z1, near, 1), (same1, far, 1)], mine, None, side)
+            add_sides([(z, near, 0), (same, far, 0), (z1, near, k), (same1, far, k)], mine, None, side)
             rows = pl.ds(others, count)
             acc[rows, :] = products([(cross[...], near0), (c[...], far0), (cross1[...], near1)])
-            add_sides([(cross, near, 0), (c, far, 0), (cross1, near, 1)], others, None, side)
+            add_sides([(cross, near, 0), (c, far, 0), (cross1, near, k)], others, None, side)
 
     ids_out[...] = ids[...]
 
@@ -155,17 +159,17 @@
     count, depth = z.shape
     _, core, _ = here()
     mine, others = blocks(count)
-    near3, far3 = weights(head, sibling, depth, 3, False), weights(head, sibling, depth, 3, True)
-    for which, same, cross in ((0, a, b), (1, b, a)):
+    for which, k, same, cross in ((0, 3, a, b), (1, 1, b, a)):
 
         @pl.when(core == which)
         def _():
+            near3, far3 = both_weights(head, sibling, depth, k)
             rows = pl.ds(mine, count)
             acc[rows, :] = acc_in[rows, :] + products([(z[...], near3), (same[...], far3)])
-            add_sides([(z, near, 3), (same, far, 3)], mine, side_in, side)
+            add_sides([(z, near, k), (same, far, k)], mine, side_in, side)
             rows = pl.ds(others, count)
             acc[rows, :] = acc_in[rows, :] + products([(cross[...], near3), (c[...], far3)])
-            add_sides([(cross, near, 3), (c, far, 3)], others, side_in, side)
+            add_sides([(cross, near, k), (c, far, k)], others, side_in, side)
 
 
 def gate_kernel(value, *refs):
@@ -201,16 +205,16 @@
     _, core, _ = here()
     mine, others = blocks(count)
     near2, far2 = weights(head, sibling, depth, 2, False), weights(head, sibling, depth, 2, True)
-    far1 = weights(head, sibling, depth, 1, True)
     block = head.shape[1]
     far_out[:, :block] = far2[0]
     far_out[:, block:] = far2[1]
     ids = column_ids(block)
     wide[...] = jnp.zeros(wide.shape, F32)
-    for which, same, cross in ((0, a, b), (1, b, a)):
+    for which, k, same, cross in ((0, 1, a, b), (1, 3, b, a)):
 
         @pl.when(core == which)
         def _():
+            far1 = weights(head, sibling, depth, k, True)
             rows = pl.ds(mine, count)
             logits = acc_in[rows, :] + products([(z[...], near2), (same[...], far2)])
             add_sides([(z, near, 2), (same, far, 2)], mine, side_in, side)
@@ -218,7 +222,7 @@
             wide[rows, :] = summary(logits, square, reward, token_ids[rows, :], ids, width)
             rows = pl.ds(others, count)
             left[...] = acc_in[rows, :] + products([(cross[...], near2), (c1[...], far1)])
-            add_sides([(cross, near, 2), (c1, far, 1)], others, side_in, side)
+            add_sides([(cross, near, 2), (c1, far, k)], others, side_in, side)
             left_side[...] = side[rows, :]
 
 
@@ -346,11 +350,13 @@
             return call(gate_kernel, like(value), [VMEM] + [ANY] * len(after), (value,) + after)
 
         side_shape = jax.ShapeDtypeStruct((2 * count, 2 * LANES), F32)
-        z1 = send(full, perm_z[1])
-        z3 = send(full, perm_z[3])
+        perm_e = mesh_perm(lambda s, d: (s, d ^ (2 if s % 2 == 0 else 6)))
+        perm_f = mesh_perm(lambda s, d: (s, d ^ (6 if s % 2 == 0 else 2)))
+        z1 = send(full, perm_e)
         a0 = send(full, perm_a)
         b0 = send(full, perm_b)
         far = send(near, perm_x)
+        z3 = send(gate(full, z1), perm_f)
         z1 = gate(z1, b0)
         a1 = send(z1, perm_a)
         b1 = send(z1, perm_b)
@@ -358,7 +364,7 @@
         z3 = gate(z3, a1, b1, c0, far)
         a3 = send(z3, perm_a)
         b3 = send(z3, perm_b)
-        z2 = send(z3, perm_z[1])
+        z2 = send(z1, perm_f)
         acc, side, token_ids = call(
             begin_kernel,
             [acc_shape, side_shape, ids_shape],
@@ -369,7 +375,7 @@
         c3 = send(a3, perm_b)
         a2 = send(z2, perm_a)
         b2 = send(z2, perm_b)
-        c1 = send(c0, perm_z[1])
+        c1 = send(c0, perm_e)
         acc, side = call(
             middle_kernel,
             [acc_shape, side_shape],

time: 127 us -> 120 us (0.945)
  starting transfers between devices: 46.2 us -> 36 us
  waiting for transfers between devices: 57.9 us -> 62 us
    ppermute x24, starting transfers between devices: 44.9 us -> 34.7 us  [per_device(): send = lambda value, perm: lax.ppermute(value, AXES, perm)]
    ppermute x24, waiting for transfers between devices: 56.7 us -> 60.9 us  [per_device(): send = lambda value, perm: lax.ppermute(value, AXES, perm)]
    pallas_call x12 -> x13, Pallas kernels: 16.9 us -> 16.5 us  [call(): pl.pallas_call(body, out_shape=outs, in_specs=in_specs, out_specs=[VMEM]...]
  transfers between devices with their start and end apart: 28 -> 28, of which waited for: 16 -> 18; matrix products, arithmetic and copies ran while one was open for 2% -> 2% of each run, Pallas kernels for 10% -> 10%
where the time goes in v10:
time: 120 us
  waiting for transfers between devices  62 us (52%)
  starting transfers between devices  36 us (30%)
  Pallas kernels  16.5 us (14%)
  local copies, waits for them, and re-layouts  4.31 us (4%)
    ppermute x24, waiting for transfers between devices, per_device(): send = lambda value, perm: lax.ppermute(value, AXES, perm)  60.9 us
    ppermute x24, starting transfers between devices, per_device(): send = lambda value, perm: lax.ppermute(value, AXES, perm)  34.7 us
    pallas_call x13, Pallas kernels, call(): pl.pallas_call(body, out_shape=outs, in_specs=in_specs, out_specs=[VMEM]...  16.5 us
  transfers between devices with their start and end apart: 28, of which 18 were waited for; matrix products, arithmetic and copies ran while one was open for 2% of the time, Pallas kernels for 10%

profile of v10, /device:TPU:0, one launch (start us, length us, event | category | flops | bytes accessed | tf_op | source)
XLA Modules:
  0.0 119.9 jit_solution(15752478710575853464)
XLA Ops:
  0.6 0.5 collective-permute-start
  1.2 1.0 slice_bitcast_fusion
  2.3 0.7 collective-permute-start.2
  2.9 0.7 broadcast_in_dim.12.gain
  3.6 0.7 broadcast_in_dim.13.reward
  4.3 1.1 copy-done.1
  5.5 3.1 %collective-permute-start.3 = (f32[2,1024]{1,0:T(2,128)S(1)}, f32[2,1024]{1,0:T(2,128)S(1)}, u32[]{:S(2)}, u32[]{:S(2)}) collective-permute-start(f32[2,1024]{1,0:T(2,128)S(1)} %get-tuple-element.18), channel_id=1, source_target_pairs={{0,2},{1,3},{2,0},{3,1},{4,6},{5,7},{6,4},{7,5},{8,10},{9,11},{10,... | collective-permute-start | bytes 24584 | tf_op jit(solution)/shard_map/ppermute | solution.py:314
  8.6 1.6 %collective-permute-done.3 = f32[2,1024]{1,0:T(2,128)S(1)} collective-permute-done((f32[2,1024]{1,0:T(2,128)S(1)}, f32[2,1024]{1,0:T(2,128)S(1)}, u32[]{:S(2)}, u32[]{:S(2)}) %collective-permute-start.3) | collective-permute-done | bytes 8224 | tf_op jit(solution)/shard_map/ppermute | solution.py:314
  10.2 3.1 %collective-permute-start.4 = (f32[4,1024]{1,0:T(4,128)S(1)}, f32[4,1024]{1,0:T(4,128)S(1)}, u32[]{:S(2)}, u32[]{:S(2)}) collective-permute-start(f32[4,1024]{1,0:T(4,128)S(1)} %pad_maximum_fusion.2), channel_id=1, source_target_pairs={{0,4},{1,5},{2,6},{3,7},{4,0},{5,1},{6,2},{7,3},{8,12},{9,13},{10,... | collective-permute-start | bytes 49160 | tf_op jit(solution)/shard_map/ppermute | solution.py:314
  13.3 1.7 %collective-permute-done.4 = f32[4,1024]{1,0:T(4,128)S(1)} collective-permute-done((f32[4,1024]{1,0:T(4,128)S(1)}, f32[4,1024]{1,0:T(4,128)S(1)}, u32[]{:S(2)}, u32[]{:S(2)}) %collective-permute-start.4) | collective-permute-done | bytes 16416 | tf_op jit(solution)/shard_map/ppermute | solution.py:314
  15.1 0.6 copy-done.3
  15.8 1.6 %shard_map.78 = (bf16[288,1024]{1,0:T(8,128)(2,1)S(1)}, f32[8,1024]{1,0:T(8,128)S(1)}) custom-call(s32[4]{0:T(128)S(1)} %copy-done.3, bf16[384,1024]{1,0:T(8,128)(2,1)S(1)} %get-tuple-element.17.rows, bf16[384,1024]{1,0:T(8,128)(2,1)S(1)} %collective-permute-done.1.sibling, bf16[192,1024]{1,0:T(8,128)(2,1)S(1)} %collective-permute-done.2.extra, ...), custom_call_target="tpu_custom_call" | custom-call | tf_op jit(solution)/shard_map/pallas_call | solution.py:282
  17.4 1.9 %collective-permute-start.7 = (bf16[288,1024]{1,0:T(8,128)(2,1)S(1)}, bf16[288,1024]{1,0:T(8,128)(2,1)S(1)}, u32[]{:S(2)}, u32[]{:S(2)}) collective-permute-start(bf16[288,1024]{1,0:T(8,128)(2,1)S(1)} %get-tuple-element.20.z.value), channel_id=1, source_target_pairs={{0,16},{1,17},{2,18},{3,19},{4,20},{5,21},{6,22},{7,23},{8,9},{9,8... | collective-permute-start | bytes 1769480 | tf_op jit(solution)/shard_map/ppermute | solution.py:314
  19.3 1.6 %collective-permute-start.9 = (bf16[288,1024]{1,0:T(8,128)(2,1)S(1)}, bf16[288,1024]{1,0:T(8,128)(2,1)S(1)}, u32[]{:S(2)}, u32[]{:S(2)}) collective-permute-start(bf16[288,1024]{1,0:T(8,128)(2,1)S(1)} %get-tuple-element.20.z.value), channel_id=1, source_target_pairs={{0,2},{1,3},{2,0},{3,1},{4,6},{5,7},{6,4},{7,5},{8,14},{9,15},{10,... | collective-permute-start | bytes 1769480 | tf_op jit(solution)/shard_map/ppermute | solution.py:314
  20.9 1.5 %collective-permute-start.6 = (bf16[288,1024]{1,0:T(8,128)(2,1)S(1)}, bf16[288,1024]{1,0:T(8,128)(2,1)S(1)}, u32[]{:S(2)}, u32[]{:S(2)}) collective-permute-start(bf16[288,1024]{1,0:T(8,128)(2,1)S(1)} %get-tuple-element.20.z.value), channel_id=1, source_target_pairs={{0,1},{1,0},{2,3},{3,2},{4,5},{5,4},{6,7},{7,6},{8,24},{9,25},{10,... | collective-permute-start | bytes 1769480 | tf_op jit(solution)/shard_map/ppermute | solution.py:314
  22.4 7.7 %collective-permute-done.7.refs_0_.b = bf16[288,1024]{1,0:T(8,128)(2,1)S(1)} collective-permute-done((bf16[288,1024]{1,0:T(8,128)(2,1)S(1)}, bf16[288,1024]{1,0:T(8,128)(2,1)S(1)}, u32[]{:S(2)}, u32[]{:S(2)}) %collective-permute-start.7) | collective-permute-done | bytes 589856 | tf_op jit(solution)/shard_map/ppermute | solution.py:314
  30.1 5.4 %collective-permute-done.9.value.refs_0_ = bf16[288,1024]{1,0:T(8,128)(2,1)S(1)} collective-permute-done((bf16[288,1024]{1,0:T(8,128)(2,1)S(1)}, bf16[288,1024]{1,0:T(8,128)(2,1)S(1)}, u32[]{:S(2)}, u32[]{:S(2)}) %collective-permute-start.9) | collective-permute-done | bytes 589856 | tf_op jit(solution)/shard_map/ppermute | solution.py:314
  35.5 1.6 %collective-permute-start.10 = (bf16[288,1024]{1,0:T(8,128)(2,1)S(1)}, bf16[288,1024]{1,0:T(8,128)(2,1)S(1)}, u32[]{:S(2)}, u32[]{:S(2)}) collective-permute-start(bf16[288,1024]{1,0:T(8,128)(2,1)S(1)} %shard_map.79.z1), channel_id=1, source_target_pairs={{0,1},{1,0},{2,3},{3,2},{4,5},{5,4},{6,7},{7,6},{8,24},{9,25},{10,... | collective-permute-start | bytes 1769480 | tf_op jit(solution)/shard_map/ppermute | solution.py:314
  37.6 1.5 %collective-permute-start.11 = (bf16[288,1024]{1,0:T(8,128)(2,1)S(1)}, bf16[288,1024]{1,0:T(8,128)(2,1)S(1)}, u32[]{:S(2)}, u32[]{:S(2)}) collective-permute-start(bf16[288,1024]{1,0:T(8,128)(2,1)S(1)} %shard_map.79.z1), channel_id=1, source_target_pairs={{0,16},{1,17},{2,18},{3,19},{4,20},{5,21},{6,22},{7,23},{8,9},{9,8... | collective-permute-start | bytes 1769480 | tf_op jit(solution)/shard_map/ppermute | solution.py:314
  39.2 3.6 %collective-permute-start.12 = (bf16[288,1024]{1,0:T(8,128)(2,1)S(1)}, bf16[288,1024]{1,0:T(8,128)(2,1)S(1)}, u32[]{:S(2)}, u32[]{:S(2)}) collective-permute-start(bf16[288,1024]{1,0:T(8,128)(2,1)S(1)} %shard_map.82), channel_id=1, source_target_pairs={{0,6},{1,7},{2,4},{3,5},{4,2},{5,3},{6,0},{7,1},{8,10},{9,11},{10,... | collective-permute-start | bytes 1769480 | tf_op jit(solution)/shard_map/ppermute | solution.py:314
  42.8 0.6 collective-permute-start.5
  43.5 9.1 %collective-permute-done.5.far.refs_3_ = f32[8,1024]{1,0:T(8,128)S(1)} collective-permute-done((f32[8,1024]{1,0:T(8,128)S(1)}, f32[8,1024]{1,0:T(8,128)S(1)}, u32[]{:S(2)}, u32[]{:S(2)}) %collective-permute-start.5) | collective-permute-done | bytes 32800 | tf_op jit(solution)/shard_map/ppermute | solution.py:314
  52.5 4.2 %collective-permute-done.11.b1.refs_1_ = bf16[288,1024]{1,0:T(8,128)(2,1)S(1)} collective-permute-done((bf16[288,1024]{1,0:T(8,128)(2,1)S(1)}, bf16[288,1024]{1,0:T(8,128)(2,1)S(1)}, u32[]{:S(2)}, u32[]{:S(2)}) %collective-permute-start.11) | collective-permute-done | bytes 589856 | tf_op jit(solution)/shard_map/ppermute | solution.py:314
  56.8 1.2 %collective-permute-start.13 = (bf16[288,1024]{1,0:T(8,128)(2,1)S(1)}, bf16[288,1024]{1,0:T(8,128)(2,1)S(1)}, u32[]{:S(2)}, u32[]{:S(2)}) collective-permute-start(bf16[288,1024]{1,0:T(8,128)(2,1)S(1)} %shard_map.83.z), channel_id=1, source_target_pairs={{0,1},{1,0},{2,3},{3,2},{4,5},{5,4},{6,7},{7,6},{8,24},{9,25},{10,... | collective-permute-start | bytes 1769480 | tf_op jit(solution)/shard_map/ppermute | solution.py:314
  58.1 4.0 %collective-permute-start.16 = (bf16[288,1024]{1,0:T(8,128)(2,1)S(1)}, bf16[288,1024]{1,0:T(8,128)(2,1)S(1)}, u32[]{:S(2)}, u32[]{:S(2)}) collective-permute-start(bf16[288,1024]{1,0:T(8,128)(2,1)S(1)} %shard_map.79.z1), channel_id=1, source_target_pairs={{0,6},{1,7},{2,4},{3,5},{4,2},{5,3},{6,0},{7,1},{8,10},{9,11},{10,... | collective-permute-start | bytes 1769480 | tf_op jit(solution)/shard_map/ppermute | solution.py:314
  62.1 1.0 shard_map.80.ids
  63.1 0.6 collective-permute-start.14
  63.6 4.5 %shard_map.81 = (f32[576,512]{1,0:T(8,128)S(1)}, f32[576,256]{1,0:T(8,128)S(1)}, s32[576,1]{1,0:T(8,128)S(1)}) custom-call(bf16[8192,256]{1,0:T(8,128)(2,1)S(1)} %copy-done, bf16[8192,256]{1,0:T(8,128)(2,1)S(1)} %collective-permute-done.after.sibling, f32[8,1024]{1,0:T(8,128)S(1)} %get-tuple-element.19.near, ...), custom_call_target="tpu_custom_call" | custom-call | tf_op jit(solution)/shard_map/pallas_call | solution.py:282
  68.1 2.0 %collective-permute-done.13.value = bf16[288,1024]{1,0:T(8,128)(2,1)S(1)} collective-permute-done((bf16[288,1024]{1,0:T(8,128)(2,1)S(1)}, bf16[288,1024]{1,0:T(8,128)(2,1)S(1)}, u32[]{:S(2)}, u32[]{:S(2)}) %collective-permute-start.13) | collective-permute-done | bytes 589856 | tf_op jit(solution)/shard_map/ppermute | solution.py:314
  70.2 0.6 collective-permute-start.15
  70.8 5.3 %collective-permute-done.16.z = bf16[288,1024]{1,0:T(8,128)(2,1)S(1)} collective-permute-done((bf16[288,1024]{1,0:T(8,128)(2,1)S(1)}, bf16[288,1024]{1,0:T(8,128)(2,1)S(1)}, u32[]{:S(2)}, u32[]{:S(2)}) %collective-permute-start.16) | collective-permute-done | bytes 589856 | tf_op jit(solution)/shard_map/ppermute | solution.py:314
  76.3 0.5 collective-permute-start.18
  76.8 9.5 %collective-permute-done.15.c = bf16[288,1024]{1,0:T(8,128)(2,1)S(1)} collective-permute-done((bf16[288,1024]{1,0:T(8,128)(2,1)S(1)}, bf16[288,1024]{1,0:T(8,128)(2,1)S(1)}, u32[]{:S(2)}, u32[]{:S(2)}) %collective-permute-start.15) | collective-permute-done | bytes 589856 | tf_op jit(solution)/shard_map/ppermute | solution.py:314
  86.3 2.7 %shard_map.85 = (f32[576,512]{1,0:T(8,128)S(1)}, f32[576,256]{1,0:T(8,128)S(1)}) custom-call(bf16[8192,256]{1,0:T(8,128)(2,1)S(1)} %copy-done, bf16[8192,256]{1,0:T(8,128)(2,1)S(1)} %collective-permute-done.after.sibling, f32[8,1024]{1,0:T(8,128)S(1)} %get-tuple-element.19.near, f32[8,1024]{1,0:T(8,128)S(1)} %collective-permute-done.5.far.refs_3_, ...), custom_call_target="tpu_custom_call" | custom-call | tf_op jit(solution)/shard_map/pallas_call | solution.py:282
  89.0 3.4 %collective-permute-done.17.value = bf16[288,1024]{1,0:T(8,128)(2,1)S(1)} collective-permute-done((bf16[288,1024]{1,0:T(8,128)(2,1)S(1)}, bf16[288,1024]{1,0:T(8,128)(2,1)S(1)}, u32[]{:S(2)}, u32[]{:S(2)}) %collective-permute-start.17) | collective-permute-done | bytes 589856 | tf_op jit(solution)/shard_map/ppermute | solution.py:314
  92.9 3.2 %shard_map.87 = (f32[288,512]{1,0:T(8,128)S(1)}, f32[288,256]{1,0:T(8,128)S(1)}, bf16[1024,512]{1,0:T(8,128)(2,1)S(1)}, f32[640,128]{1,0:T(8,128)S(1)}) custom-call(bf16[8192,256]{1,0:T(8,128)(2,1)S(1)} %copy-done, bf16[8192,256]{1,0:T(8,128)(2,1)S(1)} %collective-permute-done.after.sibling, f32[8,1024]{1,0:T(8,128)S(1)} %get-tuple-element.19.near, ...), custom_call_target="tpu_custom_call" | custom-call | tf_op jit(solution)/shard_map/pallas_call | solution.py:282
  96.2 6.2 %collective-permute-done.20.c = bf16[288,1024]{1,0:T(8,128)(2,1)S(1)} collective-permute-done((bf16[288,1024]{1,0:T(8,128)(2,1)S(1)}, bf16[288,1024]{1,0:T(8,128)(2,1)S(1)}, u32[]{:S(2)}, u32[]{:S(2)}) %collective-permute-start.20) | collective-permute-done | bytes 589856 | tf_op jit(solution)/shard_map/ppermute | solution.py:314
  102.4 1.4 %shard_map.88 = f32[8,640]{1,0:T(8,128)S(1)} custom-call(bf16[1024,512]{1,0:T(8,128)(2,1)S(1)} %get-tuple-element.26.far_weights, f32[8,1024]{1,0:T(8,128)S(1)} %collective-permute-done.5.far.refs_3_, f32[288,512]{1,0:T(8,128)S(1)} %get-tuple-element.27.left, f32[288,256]{1,0:T(8,128)S(1)} %get-tuple-element.28.left_side, ...), custom_call_target="tpu_custom_call" | custom-call | tf_op jit(solution)/shard_map/pallas_call | solution.py:282
  103.8 1.3 %collective-permute-start.23 = (f32[8,640]{1,0:T(8,128)S(1)}, f32[8,640]{1,0:T(8,128)S(1)}, u32[]{:S(2)}, u32[]{:S(2)}) collective-permute-start(f32[8,640]{1,0:T(8,128)S(1)} %shard_map.88), channel_id=1, source_target_pairs={{0,6},{1,7},{2,4},{3,5},{4,2},{5,3},{6,0},{7,1},{8,14},{9,15},{10,... | collective-permute-start | bytes 61448 | tf_op jit(solution)/shard_map/ppermute | solution.py:314
  105.0 3.2 %collective-permute-start.21 = (f32[8,640]{1,0:T(8,128)S(1)}, f32[8,640]{1,0:T(8,128)S(1)}, u32[]{:S(2)}, u32[]{:S(2)}) collective-permute-start(f32[8,640]{1,0:T(8,128)S(1)} %shard_map.88), channel_id=1, source_target_pairs={{0,2},{1,3},{2,0},{3,1},{4,6},{5,7},{6,4},{7,5},{8,10},{9,11},{10,... | collective-permute-start | bytes 61448 | tf_op jit(solution)/shard_map/ppermute | solution.py:314
  108.2 1.2 collective-permute-done.23
  110.1 1.2 collective-permute-start.26
  111.3 1.6 %collective-permute-start.25 = (f32[8,640]{1,0:T(8,128)S(1)}, f32[8,640]{1,0:T(8,128)S(1)}, u32[]{:S(2)}, u32[]{:S(2)}) collective-permute-start(f32[8,640]{1,0:T(8,128)S(1)} %concatenate.15), channel_id=1, source_target_pairs={{0,16},{1,17},{2,18},{3,19},{4,20},{5,21},{6,22},{7,23},{8,24},{9,... | collective-permute-start | bytes 61448 | tf_op jit(solution)/shard_map/ppermute | solution.py:314
  112.8 0.8 collective-permute-start.24
  113.8 1.3 %collective-permute-done.26 = f32[8,640]{1,0:T(8,128)S(1)} collective-permute-done((f32[8,640]{1,0:T(8,128)S(1)}, f32[8,640]{1,0:T(8,128)S(1)}, u32[]{:S(2)}, u32[]{:S(2)}) %collective-permute-start.26) | collective-permute-done | bytes 20512 | tf_op jit(solution)/shard_map/ppermute | solution.py:314
  115.2 1.4 %collective-permute-done.24 = f32[8,640]{1,0:T(8,128)S(1)} collective-permute-done((f32[8,640]{1,0:T(8,128)S(1)}, f32[8,640]{1,0:T(8,128)S(1)}, u32[]{:S(2)}, u32[]{:S(2)}) %collective-permute-start.24) | collective-permute-done | bytes 20512 | tf_op jit(solution)/shard_map/ppermute | solution.py:314
  116.8 1.2 collective-permute-done.27
  118.0 1.9 %shard_map.89 = (f32[1,384]{1,0:T(1,128)}, f32[1,1]{1,0:T(1,128)}) custom-call(s32[4]{0:T(128)S(1)} %copy-done.4, f32[2,8,640]{2,1,0:T(8,128)S(1)} %pad_maximum_fusion.stats), custom_call_target="tpu_custom_call" | custom-call | tf_op jit(solution)/shard_map/pallas_call | solution.py:282
  (45 shorter events, 2.7 us)
Async XLA Ops:
  0.6 14.5 %collective-permute-start = (bf16[8192,256]{1,0:T(8,128)(2,1)}, bf16[8192,256]{1,0:T(8,128)(2,1)S(1)}, u32[]{:S(2)}, u32[]{:S(2)}) collective-permute-start(bf16[8192,256]{1,0:T(8,128)(2,1)} %head.5), channel_id=1, source_target_pairs={{0,8},{8,0},{16,24},{24,16},{1,9},{9,1},{17,25},{25,17},{2,10},{10... | collective-permute-start | bytes 12582920 | tf_op jit(solution)/shard_map/ppermute | solution.py:327
  1.1 13.9 %collective-permute-start.1 = (bf16[384,1024]{1,0:T(8,128)(2,1)}, bf16[384,1024]{1,0:T(8,128)(2,1)S(1)}, u32[]{:S(2)}, u32[]{:S(2)}) collective-permute-start(bf16[384,1024]{1,0:T(8,128)(2,1)} %bitcast.8), channel_id=1, source_target_pairs={{0,8},{8,0},{16,24},{24,16},{1,9},{9,1},{17,25},{25,17},{2,10},{10... | collective-permute-start | bytes 2359304 | tf_op jit(solution)/shard_map/ppermute | solution.py:326
  2.3 12.8 %collective-permute-start.2 = (bf16[192,1024]{1,0:T(8,128)(2,1)S(1)}, bf16[192,1024]{1,0:T(8,128)(2,1)S(1)}, u32[]{:S(2)}, u32[]{:S(2)}) collective-permute-start(bf16[192,1024]{1,0:T(8,128)(2,1)S(1)} %slice_bitcast_fusion), channel_id=1, source_target_pairs={{8,24},{24,8},{9,25},{25,9},{10,26},{26,10},{11,27},{27,11},{12,28... | collective-permute-start | bytes 1179656 | tf_op jit(solution)/shard_map/ppermute | solution.py:325
  4.3 1.1 copy-start.1
  5.5 4.7 %collective-permute-start.3 = (f32[2,1024]{1,0:T(2,128)S(1)}, f32[2,1024]{1,0:T(2,128)S(1)}, u32[]{:S(2)}, u32[]{:S(2)}) collective-permute-start(f32[2,1024]{1,0:T(2,128)S(1)} %get-tuple-element.18), channel_id=1, source_target_pairs={{0,2},{1,3},{2,0},{3,1},{4,6},{5,7},{6,4},{7,5},{8,10},{9,11},{10,... | collective-permute-start | bytes 24584 | tf_op jit(solution)/shard_map/ppermute | solution.py:314
  10.2 4.8 %collective-permute-start.4 = (f32[4,1024]{1,0:T(4,128)S(1)}, f32[4,1024]{1,0:T(4,128)S(1)}, u32[]{:S(2)}, u32[]{:S(2)}) collective-permute-start(f32[4,1024]{1,0:T(4,128)S(1)} %pad_maximum_fusion.2), channel_id=1, source_target_pairs={{0,4},{1,5},{2,6},{3,7},{4,0},{5,1},{6,2},{7,3},{8,12},{9,13},{10,... | collective-permute-start | bytes 49160 | tf_op jit(solution)/shard_map/ppermute | solution.py:314
  15.1 0.7 copy-start.3
  17.4 44.7 %copy-start.2 = (s32[4,384]{1,0:T(4,128)S(1)}, s32[4,384]{1,0:T(4,128)}, u32[]{:S(2)}) copy-start(s32[4,384]{1,0:T(4,128)} %tokens.1) | copy-start | bytes 18436
  17.4 46.3 %copy-start = (bf16[8192,256]{1,0:T(8,128)(2,1)S(1)}, bf16[8192,256]{1,0:T(8,128)(2,1)}, u32[]{:S(2)}) copy-start(bf16[8192,256]{1,0:T(8,128)(2,1)} %head.5) | copy-start | bytes 12582916
  17.4 12.7 %collective-permute-start.7 = (bf16[288,1024]{1,0:T(8,128)(2,1)S(1)}, bf16[288,1024]{1,0:T(8,128)(2,1)S(1)}, u32[]{:S(2)}, u32[]{:S(2)}) collective-permute-start(bf16[288,1024]{1,0:T(8,128)(2,1)S(1)} %get-tuple-element.20.z.value), channel_id=1, source_target_pairs={{0,16},{1,17},{2,18},{3,19},{4,20},{5,21},{6,22},{7,23},{8,9},{9,8... | collective-permute-start | bytes 1769480 | tf_op jit(solution)/shard_map/ppermute | solution.py:314
  19.3 16.2 %collective-permute-start.9 = (bf16[288,1024]{1,0:T(8,128)(2,1)S(1)}, bf16[288,1024]{1,0:T(8,128)(2,1)S(1)}, u32[]{:S(2)}, u32[]{:S(2)}) collective-permute-start(bf16[288,1024]{1,0:T(8,128)(2,1)S(1)} %get-tuple-element.20.z.value), channel_id=1, source_target_pairs={{0,2},{1,3},{2,0},{3,1},{4,6},{5,7},{6,4},{7,5},{8,14},{9,15},{10,... | collective-permute-start | bytes 1769480 | tf_op jit(solution)/shard_map/ppermute | solution.py:314
  20.9 16.2 %collective-permute-start.6 = (bf16[288,1024]{1,0:T(8,128)(2,1)S(1)}, bf16[288,1024]{1,0:T(8,128)(2,1)S(1)}, u32[]{:S(2)}, u32[]{:S(2)}) collective-permute-start(bf16[288,1024]{1,0:T(8,128)(2,1)S(1)} %get-tuple-element.20.z.value), channel_id=1, source_target_pairs={{0,1},{1,0},{2,3},{3,2},{4,5},{5,4},{6,7},{7,6},{8,24},{9,25},{10,... | collective-permute-start | bytes 1769480 | tf_op jit(solution)/shard_map/ppermute | solution.py:314
  35.5 17.0 %collective-permute-start.10 = (bf16[288,1024]{1,0:T(8,128)(2,1)S(1)}, bf16[288,1024]{1,0:T(8,128)(2,1)S(1)}, u32[]{:S(2)}, u32[]{:S(2)}) collective-permute-start(bf16[288,1024]{1,0:T(8,128)(2,1)S(1)} %shard_map.79.z1), channel_id=1, source_target_pairs={{0,1},{1,0},{2,3},{3,2},{4,5},{5,4},{6,7},{7,6},{8,24},{9,25},{10,... | collective-permute-start | bytes 1769480 | tf_op jit(solution)/shard_map/ppermute | solution.py:314
  37.1 15.4 %collective-permute-start.8 = (bf16[288,1024]{1,0:T(8,128)(2,1)S(1)}, bf16[288,1024]{1,0:T(8,128)(2,1)S(1)}, u32[]{:S(2)}, u32[]{:S(2)}) collective-permute-start(bf16[288,1024]{1,0:T(8,128)(2,1)S(1)} %collective-permute-done.6.a), channel_id=1, source_target_pairs={{0,16},{1,17},{2,18},{3,19},{4,20},{5,21},{6,22},{7,23},{8,9},{9,8... | collective-permute-start | bytes 1769480 | tf_op jit(solution)/shard_map/ppermute | solution.py:314
  37.6 19.2 %collective-permute-start.11 = (bf16[288,1024]{1,0:T(8,128)(2,1)S(1)}, bf16[288,1024]{1,0:T(8,128)(2,1)S(1)}, u32[]{:S(2)}, u32[]{:S(2)}) collective-permute-start(bf16[288,1024]{1,0:T(8,128)(2,1)S(1)} %shard_map.79.z1), channel_id=1, source_target_pairs={{0,16},{1,17},{2,18},{3,19},{4,20},{5,21},{6,22},{7,23},{8,9},{9,8... | collective-permute-start | bytes 1769480 | tf_op jit(solution)/shard_map/ppermute | solution.py:314
  39.2 17.6 %collective-permute-start.12 = (bf16[288,1024]{1,0:T(8,128)(2,1)S(1)}, bf16[288,1024]{1,0:T(8,128)(2,1)S(1)}, u32[]{:S(2)}, u32[]{:S(2)}) collective-permute-start(bf16[288,1024]{1,0:T(8,128)(2,1)S(1)} %shard_map.82), channel_id=1, source_target_pairs={{0,6},{1,7},{2,4},{3,5},{4,2},{5,3},{6,0},{7,1},{8,10},{9,11},{10,... | collective-permute-start | bytes 1769480 | tf_op jit(solution)/shard_map/ppermute | solution.py:314
  42.8 9.7 %collective-permute-start.5 = (f32[8,1024]{1,0:T(8,128)S(1)}, f32[8,1024]{1,0:T(8,128)S(1)}, u32[]{:S(2)}, u32[]{:S(2)}) collective-permute-start(f32[8,1024]{1,0:T(8,128)S(1)} %get-tuple-element.19.near), channel_id=1, source_target_pairs={{0,1},{1,0},{2,3},{3,2},{4,5},{5,4},{6,7},{7,6},{8,9},{9,8},{10,11... | collective-permute-start | bytes 98312 | tf_op jit(solution)/shard_map/ppermute | solution.py:314
  56.8 13.3 %collective-permute-start.13 = (bf16[288,1024]{1,0:T(8,128)(2,1)S(1)}, bf16[288,1024]{1,0:T(8,128)(2,1)S(1)}, u32[]{:S(2)}, u32[]{:S(2)}) collective-permute-start(bf16[288,1024]{1,0:T(8,128)(2,1)S(1)} %shard_map.83.z), channel_id=1, source_target_pairs={{0,1},{1,0},{2,3},{3,2},{4,5},{5,4},{6,7},{7,6},{8,24},{9,25},{10,... | collective-permute-start | bytes 1769480 | tf_op jit(solution)/shard_map/ppermute | solution.py:314
  58.1 18.0 %collective-permute-start.16 = (bf16[288,1024]{1,0:T(8,128)(2,1)S(1)}, bf16[288,1024]{1,0:T(8,128)(2,1)S(1)}, u32[]{:S(2)}, u32[]{:S(2)}) collective-permute-start(bf16[288,1024]{1,0:T(8,128)(2,1)S(1)} %shard_map.79.z1), channel_id=1, source_target_pairs={{0,6},{1,7},{2,4},{3,5},{4,2},{5,3},{6,0},{7,1},{8,10},{9,11},{10,... | collective-permute-start | bytes 1769480 | tf_op jit(solution)/shard_map/ppermute | solution.py:314
  63.1 13.8 %collective-permute-start.14 = (bf16[288,1024]{1,0:T(8,128)(2,1)S(1)}, bf16[288,1024]{1,0:T(8,128)(2,1)S(1)}, u32[]{:S(2)}, u32[]{:S(2)}) collective-permute-start(bf16[288,1024]{1,0:T(8,128)(2,1)S(1)} %shard_map.83.z), channel_id=1, source_target_pairs={{0,16},{1,17},{2,18},{3,19},{4,20},{5,21},{6,22},{7,23},{8,9},{9,8... | collective-permute-start | bytes 1769480 | tf_op jit(solution)/shard_map/ppermute | solution.py:314
  70.2 16.1 %collective-permute-start.15 = (bf16[288,1024]{1,0:T(8,128)(2,1)S(1)}, bf16[288,1024]{1,0:T(8,128)(2,1)S(1)}, u32[]{:S(2)}, u32[]{:S(2)}) collective-permute-start(bf16[288,1024]{1,0:T(8,128)(2,1)S(1)} %shard_map.84.a), channel_id=1, source_target_pairs={{0,16},{1,17},{2,18},{3,19},{4,20},{5,21},{6,22},{7,23},{8,9},{9,8... | collective-permute-start | bytes 1769480 | tf_op jit(solution)/shard_map/ppermute | solution.py:314
  76.1 16.3 %collective-permute-start.17 = (bf16[288,1024]{1,0:T(8,128)(2,1)S(1)}, bf16[288,1024]{1,0:T(8,128)(2,1)S(1)}, u32[]{:S(2)}, u32[]{:S(2)}) collective-permute-start(bf16[288,1024]{1,0:T(8,128)(2,1)S(1)} %collective-permute-done.16.z), channel_id=1, source_target_pairs={{0,1},{1,0},{2,3},{3,2},{4,5},{5,4},{6,7},{7,6},{8,24},{9,25},{10,... | collective-permute-start | bytes 1769480 | tf_op jit(solution)/shard_map/ppermute | solution.py:314
  76.3 16.6 %collective-permute-start.18 = (bf16[288,1024]{1,0:T(8,128)(2,1)S(1)}, bf16[288,1024]{1,0:T(8,128)(2,1)S(1)}, u32[]{:S(2)}, u32[]{:S(2)}) collective-permute-start(bf16[288,1024]{1,0:T(8,128)(2,1)S(1)} %collective-permute-done.16.z), channel_id=1, source_target_pairs={{0,16},{1,17},{2,18},{3,19},{4,20},{5,21},{6,22},{7,23},{8,9},{9,8... | collective-permute-start | bytes 1769480 | tf_op jit(solution)/shard_map/ppermute | solution.py:314
  76.8 16.1 %collective-permute-start.19 = (bf16[288,1024]{1,0:T(8,128)(2,1)S(1)}, bf16[288,1024]{1,0:T(8,128)(2,1)S(1)}, u32[]{:S(2)}, u32[]{:S(2)}) collective-permute-start(bf16[288,1024]{1,0:T(8,128)(2,1)S(1)} %collective-permute-done.8.c.refs_2_), channel_id=1, source_target_pairs={{0,2},{1,3},{2,0},{3,1},{4,6},{5,7},{6,4},{7,5},{8,14},{9,15},{10,... | collective-permute-start | bytes 1769480 | tf_op jit(solution)/shard_map/ppermute | solution.py:314
  92.4 9.9 %collective-permute-start.20 = (bf16[288,1024]{1,0:T(8,128)(2,1)S(1)}, bf16[288,1024]{1,0:T(8,128)(2,1)S(1)}, u32[]{:S(2)}, u32[]{:S(2)}) collective-permute-start(bf16[288,1024]{1,0:T(8,128)(2,1)S(1)} %shard_map.86.a), channel_id=1, source_target_pairs={{0,16},{1,17},{2,18},{3,19},{4,20},{5,21},{6,22},{7,23},{8,9},{9,8... | collective-permute-start | bytes 1769480 | tf_op jit(solution)/shard_map/ppermute | solution.py:314
  92.9 25.1 %copy-start.4 = (s32[4]{0:T(128)S(1)}, s32[4]{0:T(128)}, u32[]{:S(2)}) copy-start(s32[4]{0:T(128)} %lengths.5) | copy-start | bytes 52
  103.8 5.6 %collective-permute-start.23 = (f32[8,640]{1,0:T(8,128)S(1)}, f32[8,640]{1,0:T(8,128)S(1)}, u32[]{:S(2)}, u32[]{:S(2)}) collective-permute-start(f32[8,640]{1,0:T(8,128)S(1)} %shard_map.88), channel_id=1, source_target_pairs={{0,6},{1,7},{2,4},{3,5},{4,2},{5,3},{6,0},{7,1},{8,14},{9,15},{10,... | collective-permute-start | bytes 61448 | tf_op jit(solution)/shard_map/ppermute | solution.py:314
  105.0 4.8 %collective-permute-start.22 = (f32[8,640]{1,0:T(8,128)S(1)}, f32[8,640]{1,0:T(8,128)S(1)}, u32[]{:S(2)}, u32[]{:S(2)}) collective-permute-start(f32[8,640]{1,0:T(8,128)S(1)} %shard_map.88), channel_id=1, source_target_pairs={{0,4},{1,5},{2,6},{3,7},{4,0},{5,1},{6,2},{7,3},{8,12},{9,13},{10,... | collective-permute-start | bytes 61448 | tf_op jit(solution)/shard_map/ppermute | solution.py:314
  105.0 5.0 %collective-permute-start.21 = (f32[8,640]{1,0:T(8,128)S(1)}, f32[8,640]{1,0:T(8,128)S(1)}, u32[]{:S(2)}, u32[]{:S(2)}) collective-permute-start(f32[8,640]{1,0:T(8,128)S(1)} %shard_map.88), channel_id=1, source_target_pairs={{0,2},{1,3},{2,0},{3,1},{4,6},{5,7},{6,4},{7,5},{8,10},{9,11},{10,... | collective-permute-start | bytes 61448 | tf_op jit(solution)/shard_map/ppermute | solution.py:314
  110.1 4.9 %collective-permute-start.26 = (f32[8,640]{1,0:T(8,128)S(1)}, f32[8,640]{1,0:T(8,128)S(1)}, u32[]{:S(2)}, u32[]{:S(2)}) collective-permute-start(f32[8,640]{1,0:T(8,128)S(1)} %concatenate.15), channel_id=1, source_target_pairs={{0,17},{1,16},{2,19},{3,18},{4,21},{5,20},{6,23},{7,22},{8,25},{9,... | collective-permute-start | bytes 61448 | tf_op jit(solution)/shard_map/ppermute | solution.py:314
  111.3 3.9 %collective-permute-start.25 = (f32[8,640]{1,0:T(8,128)S(1)}, f32[8,640]{1,0:T(8,128)S(1)}, u32[]{:S(2)}, u32[]{:S(2)}) collective-permute-start(f32[8,640]{1,0:T(8,128)S(1)} %concatenate.15), channel_id=1, source_target_pairs={{0,16},{1,17},{2,18},{3,19},{4,20},{5,21},{6,22},{7,23},{8,24},{9,... | collective-permute-start | bytes 61448 | tf_op jit(solution)/shard_map/ppermute | solution.py:314
  112.8 3.8 %collective-permute-start.24 = (f32[8,640]{1,0:T(8,128)S(1)}, f32[8,640]{1,0:T(8,128)S(1)}, u32[]{:S(2)}, u32[]{:S(2)}) collective-permute-start(f32[8,640]{1,0:T(8,128)S(1)} %concatenate.15), channel_id=1, source_target_pairs={{0,1},{1,0},{2,3},{3,2},{4,5},{5,4},{6,7},{7,6},{8,9},{9,8},{10,11... | collective-permute-start | bytes 61448 | tf_op jit(solution)/shard_map/ppermute | solution.py:314
  116.7 1.2 %collective-permute-start.27 = (f32[8,640]{1,0:T(8,128)S(1)}, f32[8,640]{1,0:T(8,128)S(1)}, u32[]{:S(2)}, u32[]{:S(2)}) collective-permute-start(f32[8,640]{1,0:T(8,128)S(1)} %maximum_maximum_fusion), channel_id=1, source_target_pairs={{0,8},{8,0},{16,24},{24,16},{1,9},{9,1},{17,25},{25,17},{2,10},{10... | collective-permute-start | bytes 61448 | tf_op jit(solution)/shard_map/ppermute | solution.py:431

commit v11 on v10

--- a/solution.py
+++ b/solution.py
@@ -50,7 +50,7 @@
     table[1:2, :] = reward[...].astype(F32)
 
 
-def pick_kernel(count, lengths, rows, sibling, extra, gain, near, after, full, near_out):
+def pick_kernel(count, lengths, rows, sibling, extra, gain, table, after, full, table_out):
     section = lax.axis_index("section")
     core, pair = lax.rem(section, 2), lax.div(section, 2)
     positions, half = rows.shape[0], extra.shape[0]
@@ -64,21 +64,28 @@
     picked += jnp.dot(pick[:, positions : 2 * positions], sibling[...], preferred_element_type=F32)
     picked += jnp.dot(pick[:, 2 * positions :], extra[...], preferred_element_type=F32)
     full[...] = (picked * gain[...].astype(F32)).astype(BF16)
-    near_out[...] = near[...]
-
-
-def token_kernel(count, lengths, tokens, out):
-    core = lax.rem(lax.axis_index("section"), 2)
+    table_out[...] = table[...]
+
+
+def token_kernel(count, lengths, tokens, out, hit, per_row):
+    section, core, _ = here()
     spans, positions = tokens.shape
+    index = lax.broadcasted_iota(I32, (count, 1), 0)
+    lane = lax.broadcasted_iota(I32, (count, positions), 1)
+    hit[...] = jnp.zeros(hit.shape, F32)
     for pair in range(2):
-        index = lax.broadcasted_iota(I32, (count, 1), 0)
+        rows = slice(pair * count, pair * count + count)
         span, place = row_map(lengths, pair, core, index, count)
-        lane = lax.broadcasted_iota(I32, (count, positions), 1)
         found = jnp.zeros((count, positions), F32)
         for s in range(spans):
             found = jnp.where(span == s, tokens[s : s + 1, :].astype(F32), found)
-        found = jnp.sum(jnp.where(lane == place, found, F32(0.0)), axis=1, keepdims=True)
-        out[pair * count : pair * count + count, :] = found.astype(I32)
+        here_is = lane == place
+        found = jnp.sum(jnp.where(here_is, found, F32(0.0)), axis=1, keepdims=True)
+        out[rows, :] = found.astype(I32)
+        hit[0, rows, :] = jnp.where(here_is & (span == section), F32(1.0), F32(0.0))
+        span, place = row_map(lengths, pair, 1 - core, index, count)
+        hit[1, rows, :] = jnp.where((lane == place) & (span == section), F32(1.0), F32(0.0))
+    per_row[...] = jnp.zeros(per_row.shape, F32) + 1.0 / lengths[section].astype(F32)
 
 
 def here():
@@ -135,7 +142,7 @@
     return weights(head, sibling, depth, k, False), weights(head, sibling, depth, k, True)
 
 
-def begin_kernel(head, sibling, near, far, z, a, b, c, z1, a1, b1, ids, acc, side, ids_out):
+def begin_kernel(head, sibling, table, z, a, b, c, z1, a1, b1, ids, after, acc, side, ids_out):
     count, depth = z.shape
     _, core, _ = here()
     mine, others = blocks(count)
@@ -147,15 +154,16 @@
             near1, far1 = both_weights(head, sibling, depth, k)
             rows = pl.ds(mine, count)
             acc[rows, :] = products([(z[...], near0), (same[...], far0), (z1[...], near1), (same1[...], far1)])
-            add_sides([(z, near, 0), (same, far, 0), (z1, near, k), (same1, far, k)], mine, None, side)
+            terms = [(z, table, 0), (same, table, 1), (z1, table, 2 * k), (same1, table, 2 * k + 1)]
+            add_sides(terms, mine, None, side)
             rows = pl.ds(others, count)
             acc[rows, :] = products([(cross[...], near0), (c[...], far0), (cross1[...], near1)])
-            add_sides([(cross, near, 0), (c, far, 0), (cross1, near, k)], others, None, side)
+            add_sides([(cross, table, 0), (c, table, 1), (cross1, table, 2 * k)], others, None, side)
 
     ids_out[...] = ids[...]
 
 
-def middle_kernel(head, sibling, near, far, acc_in, side_in, z, a, b, c, acc, side):
+def middle_kernel(head, sibling, table, acc_in, side_in, z, a, b, c, acc, side):
     count, depth = z.shape
     _, core, _ = here()
     mine, others = blocks(count)
@@ -166,14 +174,19 @@
             near3, far3 = both_weights(head, sibling, depth, k)
             rows = pl.ds(mine, count)
             acc[rows, :] = acc_in[rows, :] + products([(z[...], near3), (same[...], far3)])
-            add_sides([(z, near, k), (same, far, k)], mine, side_in, side)
+            add_sides([(z, table, 2 * k), (same, table, 2 * k + 1)], mine, side_in, side)
             rows = pl.ds(others, count)
             acc[rows, :] = acc_in[rows, :] + products([(cross[...], near3), (c[...], far3)])
-            add_sides([(cross, near, k), (c, far, k)], others, side_in, side)
+            add_sides([(cross, table, 2 * k), (c, table, 2 * k + 1)], others, side_in, side)
 
 
 def gate_kernel(value, *refs):
-    refs[-1][...] = value[...]
+    refs[-1][...] = value[: refs[-1].shape[0], :]
+
+
+def padded_kernel(value, after, out):
+    out[: value.shape[0], :] = value[...]
+    out[value.shape[0] :, :] = jnp.zeros((out.shape[0] - value.shape[0], out.shape[1]), out.dtype)
 
 
 def column_ids(block):
@@ -200,7 +213,7 @@
     return jnp.sum(side[:, :LANES], axis=1, keepdims=True), jnp.sum(side[:, LANES:], axis=1, keepdims=True)
 
 
-def own_kernel(width, head, sibling, near, far, acc_in, side_in, z, a, b, c1, token_ids, left, left_side, far_out, wide, side):
+def own_kernel(width, head, sibling, table, acc_in, side_in, z, a, b, c1, token_ids, left, left_side, far_out, wide, side):
     count, depth = z.shape
     _, core, _ = here()
     mine, others = blocks(count)
@@ -217,22 +230,22 @@
             far1 = weights(head, sibling, depth, k, True)
             rows = pl.ds(mine, count)
             logits = acc_in[rows, :] + products([(z[...], near2), (same[...], far2)])
-            add_sides([(z, near, 2), (same, far, 2)], mine, side_in, side)
+            add_sides([(z, table, 4), (same, table, 5)], mine, side_in, side)
             square, reward = added(side[rows, :])
             wide[rows, :] = summary(logits, square, reward, token_ids[rows, :], ids, width)
             rows = pl.ds(others, count)
             left[...] = acc_in[rows, :] + products([(cross[...], near2), (c1[...], far1)])
-            add_sides([(cross, near, 2), (c1, far, k)], others, side_in, side)
+            add_sides([(cross, table, 4), (c1, table, 2 * k + 1)], others, side_in, side)
             left_side[...] = side[rows, :]
 
 
-def last_kernel(width, far_weights, far, left, left_side, c, wide_in, token_ids, out, wide, side):
+def last_kernel(width, far_weights, table, left, left_side, c, wide_in, token_ids, out, wide, side):
     count = c.shape[0]
     _, others = blocks(count)
     ids = column_ids(far_weights.shape[1] // 2)
     wide[...] = wide_in[...]
     logits = left[...] + jnp.dot(c[...], far_weights[...], preferred_element_type=F32)
-    add_sides([(c, far, 2)], 0, left_side, side)
+    add_sides([(c, table, 5)], 0, left_side, side)
     square, reward = added(side[...])
     rows = pl.ds(others, count)
     wide[rows, :] = summary(logits, square, reward, token_ids[rows, :], ids, width)
@@ -247,25 +260,11 @@
     out[...] = jnp.transpose(wide)[:8]
 
 
-def final_kernel(count, lengths, stats, out_ref, score_ref):
-    section = lax.axis_index("section")
-    positions = out_ref.shape[1]
-    where = lax.broadcasted_iota(I32, (1, positions), 1)
-    logprob = jnp.zeros((1, positions), F32)
-    score = jnp.zeros((1, 1), F32)
-    index = lax.broadcasted_iota(I32, (count, 1), 0)
-    for core in range(2):
-        columns = jnp.transpose(
-            jnp.concatenate([stats[core], jnp.zeros((LANES - 8, stats.shape[2]), F32)], axis=0)
-        )
-        for pair in range(2):
-            value = columns[pair * count : pair * count + count]
-            span, place = row_map(lengths, pair, core, index, count)
-            own = span == section
-            logprob += jnp.sum(jnp.where((place == where) & own, value[:, 0:1], F32(0.0)), axis=0, keepdims=True)
-            score += jnp.sum(jnp.where(own, value[:, 1:2], F32(0.0)), axis=0, keepdims=True)
-    out_ref[...] = logprob
-    score_ref[...] = score / lengths[section].astype(F32)
+def final_kernel(mine, sibling, hit, per_row, out_ref, score_ref):
+    exact = functools.partial(jnp.dot, precision=lax.Precision.HIGHEST, preferred_element_type=F32)
+    picked = exact(mine[...], hit[0]) + exact(sibling[...], hit[1])
+    out_ref[...] = picked[0:1, :]
+    score_ref[...] = jnp.sum(picked[1:2, :], axis=1, keepdims=True) * per_row[0:1, 0:1]
 
 
 def combine(parts):
@@ -330,17 +329,23 @@
     )
 
     if groups == 8:
-        near = jnp.concatenate([table, send(table, perm_z[1])])
-        near = jnp.concatenate([near, send(near, perm_z[2])])
-    else:
-        near = jnp.concatenate([table] * 4)
-    full, near = call(
+        table = jnp.concatenate([table, send(table, perm_x)])
+    full, table = call(
         functools.partial(pick_kernel, count),
-        [jax.ShapeDtypeStruct((count, part), BF16), like(near)],
+        [jax.ShapeDtypeStruct((count, part), BF16), like(table)],
         [SMEM] + [VMEM] * 5 + [ANY],
-        (lengths, rows, sibling, extra, gain, near, head_sibling),
-    )
-    token_ids = call(functools.partial(token_kernel, count), ids_shape, [SMEM, VMEM], (lengths, tokens))
+        (lengths, rows, sibling, extra, gain, table, head_sibling),
+    )
+    token_ids, hit, per_row = call(
+        functools.partial(token_kernel, count),
+        [
+            ids_shape,
+            jax.ShapeDtypeStruct((2, up(2 * count), positions), F32),
+            jax.ShapeDtypeStruct((8, LANES), F32),
+        ],
+        [SMEM, VMEM],
+        (lengths, tokens),
+    )
 
     if groups == 8:
         perm_a = mesh_perm(lambda s, d: (s, d ^ 1) if s % 2 == 0 else (s ^ 2, d))
@@ -355,21 +360,23 @@
         z1 = send(full, perm_e)
         a0 = send(full, perm_a)
         b0 = send(full, perm_b)
-        far = send(near, perm_x)
-        z3 = send(gate(full, z1), perm_f)
-        z1 = gate(z1, b0)
+        table = jnp.concatenate([table, send(table, perm_z[1])])
+        z3 = send(call(padded_kernel, jax.ShapeDtypeStruct((count + 16, part), BF16), [VMEM, ANY], (full, z1)), perm_f)
+        z1 = gate(z1, b0, table, token_ids)
         a1 = send(z1, perm_a)
         b1 = send(z1, perm_b)
         c0 = send(a0, perm_b)
-        z3 = gate(z3, a1, b1, c0, far)
+        table = jnp.concatenate([table, send(table, perm_z[2])])
+        z3 = call(gate_kernel, like(full), [VMEM] + [ANY] * 4, (z3, a1, b1, c0, table))
         a3 = send(z3, perm_a)
+        z3 = gate(z3)
         b3 = send(z3, perm_b)
         z2 = send(z1, perm_f)
         acc, side, token_ids = call(
             begin_kernel,
             [acc_shape, side_shape, ids_shape],
-            [VMEM] * 12,
-            (head, head_sibling, near, far, full, a0, b0, c0, z1, a1, b1, token_ids),
+            [VMEM] * 11 + [ANY],
+            (head, head_sibling, table, full, a0, b0, c0, z1, a1, b1, token_ids, z3),
         )
         a3 = gate(a3, token_ids)
         c3 = send(a3, perm_b)
@@ -379,8 +386,8 @@
         acc, side = call(
             middle_kernel,
             [acc_shape, side_shape],
-            [VMEM] * 10,
-            (head, head_sibling, near, far, acc, side, z3, a3, b3, c3),
+            [VMEM] * 9,
+            (head, head_sibling, table, acc, side, z3, a3, b3, c3),
         )
         a2 = gate(a2, side)
         c2 = send(a2, perm_b)
@@ -392,15 +399,15 @@
                 jax.ShapeDtypeStruct((part, 2 * block), BF16),
                 jax.ShapeDtypeStruct((up(2 * count), LANES), F32),
             ],
-            [VMEM] * 11,
-            (head, head_sibling, near, far, acc, side, z2, a2, b2, c1, token_ids),
+            [VMEM] * 10,
+            (head, head_sibling, table, acc, side, z2, a2, b2, c1, token_ids),
             scratch=[pltpu.VMEM((2 * count, 2 * LANES), F32)],
         )
         stats = call(
             functools.partial(last_kernel, width),
             stats_shape,
             [VMEM] * 7,
-            (far_weights, far, left, left_side, c2, wide, token_ids),
+            (far_weights, table, left, left_side, c2, wide, token_ids),
             scratch=[pltpu.VMEM((up(2 * count), LANES), F32), pltpu.VMEM((count, 2 * LANES), F32)],
         )
         stats = combine([stats] + [send(stats, perm_z[k]) for k in (1, 2, 3)])
@@ -415,7 +422,7 @@
         acc = jnp.concatenate(
             [jnp.dot(everything, h, preferred_element_type=F32) for h in (head, head_sibling)], axis=1
         )
-        gains, weights_all = (lax.all_gather(t, "dp", axis=0, tiled=True) for t in table)
+        gains, weights_all = (lax.all_gather(table[i], "dp", axis=0, tiled=True) for i in range(2))
         wide = everything.astype(F32)
         square = jnp.sum(wide * wide * gains, axis=1, keepdims=True)
         reward = jnp.sum(wide * weights_all, axis=1, keepdims=True)
@@ -425,15 +432,14 @@
         gathered = lax.all_gather(stats, "dp")
         stats = combine([gathered[i] for i in range(groups)])
         stats = combine([stats, lax.ppermute(stats, "section", over)])
-    lp = stats[2:3] - (stats[0:1] + jnp.log(stats[1:2]))
+    filled = jnp.arange(stats.shape[1], dtype=jnp.int32)[None, :] < 2 * count
+    lp = jnp.where(filled, stats[2:3] - (stats[0:1] + jnp.log(stats[1:2])), F32(0.0))
     lp = jnp.concatenate([lp, stats[3:4], jnp.zeros((6, lp.shape[1]), F32)])
-    both = lambda v, u: jnp.stack([jnp.where(core == 0, v, u), jnp.where(core == 0, u, v)])
-    stats = both(lp, lax.ppermute(lp, "section", swap))
     logprob, score = call(
-        functools.partial(final_kernel, count),
+        final_kernel,
         [jax.ShapeDtypeStruct((1, positions), F32), jax.ShapeDtypeStruct((1, 1), F32)],
-        [SMEM, VMEM],
-        (lengths, stats),
+        [VMEM] * 4,
+        (lp, lax.ppermute(lp, "section", swap), hit, per_row),
     )
     return (logprob, score[0])
 

time: 120 us -> 117 us (0.975)
  waiting for transfers between devices: 62 us -> 56.2 us
  starting transfers between devices: 36 us -> 39 us
    ppermute x24, waiting for transfers between devices: 60.9 us -> 55 us  [per_device(): send = lambda value, perm: lax.ppermute(value, AXES, perm)]
    ppermute x24, starting transfers between devices: 34.7 us -> 37.7 us  [per_device(): send = lambda value, perm: lax.ppermute(value, AXES, perm)]
    pallas_call x13 -> x14, Pallas kernels: 16.5 us -> 16.4 us  [call(): pl.pallas_call(body, out_shape=outs, in_specs=in_specs, out_specs=[VMEM]...]
  transfers between devices with their start and end apart: 28 -> 28, of which waited for: 18 -> 17; matrix products, arithmetic and copies ran while one was open for 2% -> 2% of each run, Pallas kernels for 10% -> 10%
where the time goes in v11:
time: 117 us
  waiting for transfers between devices  56.2 us (48%)
  starting transfers between devices  39 us (33%)
  Pallas kernels  16.4 us (14%)
  local copies, waits for them, and re-layouts  4.31 us (4%)
    ppermute x24, waiting for transfers between devices, per_device(): send = lambda value, perm: lax.ppermute(value, AXES, perm)  55 us
    ppermute x24, starting transfers between devices, per_device(): send = lambda value, perm: lax.ppermute(value, AXES, perm)  37.7 us
    pallas_call x14, Pallas kernels, call(): pl.pallas_call(body, out_shape=outs, in_specs=in_specs, out_specs=[VMEM]...  16.4 us
  transfers between devices with their start and end apart: 28, of which 17 were waited for; matrix products, arithmetic and copies ran while one was open for 2% of the time, Pallas kernels for 10%

profile of v11, /device:TPU:0, one launch (start us, length us, event | category | flops | bytes accessed | tf_op | source)
XLA Modules:
  0.0 117.0 jit_solution(9878788926357236770)
XLA Ops:
  1.2 1.0 slice_bitcast_fusion
  2.3 0.7 collective-permute-start.2
  2.9 0.7 broadcast_in_dim.17.gain
  3.6 0.7 broadcast_in_dim.18.reward
  4.3 1.1 copy-done.1
  5.5 3.0 %collective-permute-start.3 = (f32[2,1024]{1,0:T(2,128)S(1)}, f32[2,1024]{1,0:T(2,128)S(1)}, u32[]{:S(2)}, u32[]{:S(2)}) collective-permute-start(f32[2,1024]{1,0:T(2,128)S(1)} %get-tuple-element.21), channel_id=1, source_target_pairs={{0,1},{1,0},{2,3},{3,2},{4,5},{5,4},{6,7},{7,6},{8,9},{9,8},{10,11... | collective-permute-start | bytes 24584 | tf_op jit(solution)/shard_map/ppermute | solution.py:313
  8.5 1.6 %collective-permute-done.3 = f32[2,1024]{1,0:T(2,128)S(1)} collective-permute-done((f32[2,1024]{1,0:T(2,128)S(1)}, f32[2,1024]{1,0:T(2,128)S(1)}, u32[]{:S(2)}, u32[]{:S(2)}) %collective-permute-start.3) | collective-permute-done | bytes 8224 | tf_op jit(solution)/shard_map/ppermute | solution.py:313
  10.8 1.6 %shard_map.78 = (bf16[288,1024]{1,0:T(8,128)(2,1)S(1)}, f32[4,1024]{1,0:T(4,128)S(1)}) custom-call(s32[4]{0:T(128)S(1)} %copy-done.3, bf16[384,1024]{1,0:T(8,128)(2,1)S(1)} %get-tuple-element.20.rows, bf16[384,1024]{1,0:T(8,128)(2,1)S(1)} %collective-permute-done.1.sibling, bf16[192,1024]{1,0:T(8,128)(2,1)S(1)} %collective-permute-done.2.extra, ...), custom_call_target="tpu_custom_call" | custom-call | tf_op jit(solution)/shard_map/pallas_call | solution.py:281
  12.4 2.2 %collective-permute-start.9 = (bf16[288,1024]{1,0:T(8,128)(2,1)S(1)}, bf16[288,1024]{1,0:T(8,128)(2,1)S(1)}, u32[]{:S(2)}, u32[]{:S(2)}) collective-permute-start(bf16[288,1024]{1,0:T(8,128)(2,1)S(1)} %get-tuple-element.23.value.z), channel_id=1, source_target_pairs={{0,2},{1,3},{2,0},{3,1},{4,6},{5,7},{6,4},{7,5},{8,14},{9,15},{10,... | collective-permute-start | bytes 1769480 | tf_op jit(solution)/shard_map/ppermute | solution.py:313
  14.6 1.5 %collective-permute-start.7 = (bf16[288,1024]{1,0:T(8,128)(2,1)S(1)}, bf16[288,1024]{1,0:T(8,128)(2,1)S(1)}, u32[]{:S(2)}, u32[]{:S(2)}) collective-permute-start(bf16[288,1024]{1,0:T(8,128)(2,1)S(1)} %get-tuple-element.23.value.z), channel_id=1, source_target_pairs={{0,16},{1,17},{2,18},{3,19},{4,20},{5,21},{6,22},{7,23},{8,9},{9,8... | collective-permute-start | bytes 1769480 | tf_op jit(solution)/shard_map/ppermute | solution.py:313
  16.1 1.5 %collective-permute-start.6 = (bf16[288,1024]{1,0:T(8,128)(2,1)S(1)}, bf16[288,1024]{1,0:T(8,128)(2,1)S(1)}, u32[]{:S(2)}, u32[]{:S(2)}) collective-permute-start(bf16[288,1024]{1,0:T(8,128)(2,1)S(1)} %get-tuple-element.23.value.z), channel_id=1, source_target_pairs={{0,1},{1,0},{2,3},{3,2},{4,5},{5,4},{6,7},{7,6},{8,24},{9,25},{10,... | collective-permute-start | bytes 1769480 | tf_op jit(solution)/shard_map/ppermute | solution.py:313
  18.1 1.2 %shard_map.79 = (s32[576,1]{1,0:T(8,128)S(1)}, f32[2,640,384]{2,1,0:T(8,128)S(1)}, f32[8,128]{1,0:T(8,128)S(1)}) custom-call(s32[4]{0:T(128)S(1)} %copy-done.4, s32[4,384]{1,0:T(4,128)S(1)} %copy-done.2), custom_call_target="tpu_custom_call" | custom-call | tf_op jit(solution)/shard_map/pallas_call | solution.py:281
  19.3 7.0 %collective-permute-done.9.value.after = bf16[288,1024]{1,0:T(8,128)(2,1)S(1)} collective-permute-done((bf16[288,1024]{1,0:T(8,128)(2,1)S(1)}, bf16[288,1024]{1,0:T(8,128)(2,1)S(1)}, u32[]{:S(2)}, u32[]{:S(2)}) %collective-permute-start.9) | collective-permute-done | bytes 589856 | tf_op jit(solution)/shard_map/ppermute | solution.py:313
  26.3 6.8 %collective-permute-start.12 = (bf16[304,1024]{1,0:T(8,128)(2,1)S(1)}, bf16[304,1024]{1,0:T(8,128)(2,1)S(1)}, u32[]{:S(2)}, u32[]{:S(2)}) collective-permute-start(bf16[304,1024]{1,0:T(8,128)(2,1)S(1)} %shard_map.81), channel_id=1, source_target_pairs={{0,6},{1,7},{2,4},{3,5},{4,2},{5,3},{6,0},{7,1},{8,10},{9,11},{10,... | collective-permute-start | bytes 1867784 | tf_op jit(solution)/shard_map/ppermute | solution.py:313
  33.2 1.6 %collective-permute-start.10 = (bf16[288,1024]{1,0:T(8,128)(2,1)S(1)}, bf16[288,1024]{1,0:T(8,128)(2,1)S(1)}, u32[]{:S(2)}, u32[]{:S(2)}) collective-permute-start(bf16[288,1024]{1,0:T(8,128)(2,1)S(1)} %shard_map.80.z1), channel_id=1, source_target_pairs={{0,1},{1,0},{2,3},{3,2},{4,5},{5,4},{6,7},{7,6},{8,24},{9,25},{10,... | collective-permute-start | bytes 1769480 | tf_op jit(solution)/shard_map/ppermute | solution.py:313
  34.8 1.5 %collective-permute-start.11 = (bf16[288,1024]{1,0:T(8,128)(2,1)S(1)}, bf16[288,1024]{1,0:T(8,128)(2,1)S(1)}, u32[]{:S(2)}, u32[]{:S(2)}) collective-permute-start(bf16[288,1024]{1,0:T(8,128)(2,1)S(1)} %shard_map.80.z1), channel_id=1, source_target_pairs={{0,16},{1,17},{2,18},{3,19},{4,20},{5,21},{6,22},{7,23},{8,9},{9,8... | collective-permute-start | bytes 1769480 | tf_op jit(solution)/shard_map/ppermute | solution.py:313
  36.8 9.6 %collective-permute-done.5 = f32[8,1024]{1,0:T(8,128)S(1)} collective-permute-done((f32[8,1024]{1,0:T(8,128)S(1)}, f32[8,1024]{1,0:T(8,128)S(1)}, u32[]{:S(2)}, u32[]{:S(2)}) %collective-permute-start.5) | collective-permute-done | bytes 32800 | tf_op jit(solution)/shard_map/ppermute | solution.py:313
  46.4 3.1 %collective-permute-done.10.refs_0_.a1 = bf16[288,1024]{1,0:T(8,128)(2,1)S(1)} collective-permute-done((bf16[288,1024]{1,0:T(8,128)(2,1)S(1)}, bf16[288,1024]{1,0:T(8,128)(2,1)S(1)}, u32[]{:S(2)}, u32[]{:S(2)}) %collective-permute-start.10) | collective-permute-done | bytes 589856 | tf_op jit(solution)/shard_map/ppermute | solution.py:313
  49.5 4.3 %collective-permute-done.8.refs_2_.c = bf16[288,1024]{1,0:T(8,128)(2,1)S(1)} collective-permute-done((bf16[288,1024]{1,0:T(8,128)(2,1)S(1)}, bf16[288,1024]{1,0:T(8,128)(2,1)S(1)}, u32[]{:S(2)}, u32[]{:S(2)}) %collective-permute-start.8) | collective-permute-done | bytes 589856 | tf_op jit(solution)/shard_map/ppermute | solution.py:313
  53.9 1.6 %collective-permute-start.13 = (bf16[288,1024]{1,0:T(8,128)(2,1)S(1)}, bf16[288,1024]{1,0:T(8,128)(2,1)S(1)}, u32[]{:S(2)}, u32[]{:S(2)}) collective-permute-start(bf16[288,1024]{1,0:T(8,128)(2,1)S(1)} %shard_map.82.value), channel_id=1, source_target_pairs={{0,1},{1,0},{2,3},{3,2},{4,5},{5,4},{6,7},{7,6},{8,24},{9,25},{10,... | collective-permute-start | bytes 1769480 | tf_op jit(solution)/shard_map/ppermute | solution.py:313
  55.4 1.7 %collective-permute-start.16 = (bf16[288,1024]{1,0:T(8,128)(2,1)S(1)}, bf16[288,1024]{1,0:T(8,128)(2,1)S(1)}, u32[]{:S(2)}, u32[]{:S(2)}) collective-permute-start(bf16[288,1024]{1,0:T(8,128)(2,1)S(1)} %shard_map.80.z1), channel_id=1, source_target_pairs={{0,6},{1,7},{2,4},{3,5},{4,2},{5,3},{6,0},{7,1},{8,10},{9,11},{10,... | collective-permute-start | bytes 1769480 | tf_op jit(solution)/shard_map/ppermute | solution.py:313
  57.2 1.6 %collective-permute-start.14 = (bf16[288,1024]{1,0:T(8,128)(2,1)S(1)}, bf16[288,1024]{1,0:T(8,128)(2,1)S(1)}, u32[]{:S(2)}, u32[]{:S(2)}) collective-permute-start(bf16[288,1024]{1,0:T(8,128)(2,1)S(1)} %shard_map.83.after.z), channel_id=1, source_target_pairs={{0,16},{1,17},{2,18},{3,19},{4,20},{5,21},{6,22},{7,23},{8,9},{9,8... | collective-permute-start | bytes 1769480 | tf_op jit(solution)/shard_map/ppermute | solution.py:313
  58.8 4.5 %shard_map.84 = (f32[576,512]{1,0:T(8,128)S(1)}, f32[576,256]{1,0:T(8,128)S(1)}, s32[576,1]{1,0:T(8,128)S(1)}) custom-call(bf16[8192,256]{1,0:T(8,128)(2,1)S(1)} %copy-done, bf16[8192,256]{1,0:T(8,128)(2,1)S(1)} %collective-permute-done.after.sibling, f32[16,1024]{1,0:T(8,128)S(1)} %pad_maximum_fusion.refs_3_.table, ...), custom_call_target="tpu_custom_call" | custom-call | tf_op jit(solution)/shard_map/pallas_call | solution.py:281
  63.3 5.7 %collective-permute-done.13.value = bf16[288,1024]{1,0:T(8,128)(2,1)S(1)} collective-permute-done((bf16[288,1024]{1,0:T(8,128)(2,1)S(1)}, bf16[288,1024]{1,0:T(8,128)(2,1)S(1)}, u32[]{:S(2)}, u32[]{:S(2)}) %collective-permute-start.13) | collective-permute-done | bytes 589856 | tf_op jit(solution)/shard_map/ppermute | solution.py:313
  69.0 1.2 %collective-permute-start.15 = (bf16[288,1024]{1,0:T(8,128)(2,1)S(1)}, bf16[288,1024]{1,0:T(8,128)(2,1)S(1)}, u32[]{:S(2)}, u32[]{:S(2)}) collective-permute-start(bf16[288,1024]{1,0:T(8,128)(2,1)S(1)} %shard_map.85.a), channel_id=1, source_target_pairs={{0,16},{1,17},{2,18},{3,19},{4,20},{5,21},{6,22},{7,23},{8,9},{9,8... | collective-permute-start | bytes 1769480 | tf_op jit(solution)/shard_map/ppermute | solution.py:313
  70.1 0.9 collective-permute-done.16.z
  71.1 1.5 %collective-permute-start.17 = (bf16[288,1024]{1,0:T(8,128)(2,1)S(1)}, bf16[288,1024]{1,0:T(8,128)(2,1)S(1)}, u32[]{:S(2)}, u32[]{:S(2)}) collective-permute-start(bf16[288,1024]{1,0:T(8,128)(2,1)S(1)} %collective-permute-done.16.z), channel_id=1, source_target_pairs={{0,1},{1,0},{2,3},{3,2},{4,5},{5,4},{6,7},{7,6},{8,24},{9,25},{10,... | collective-permute-start | bytes 1769480 | tf_op jit(solution)/shard_map/ppermute | solution.py:313
  72.6 0.9 collective-permute-start.18
  73.5 1.2 %collective-permute-start.19 = (bf16[288,1024]{1,0:T(8,128)(2,1)S(1)}, bf16[288,1024]{1,0:T(8,128)(2,1)S(1)}, u32[]{:S(2)}, u32[]{:S(2)}) collective-permute-start(bf16[288,1024]{1,0:T(8,128)(2,1)S(1)} %collective-permute-done.8.refs_2_.c), channel_id=1, source_target_pairs={{0,2},{1,3},{2,0},{3,1},{4,6},{5,7},{6,4},{7,5},{8,14},{9,15},{10,... | collective-permute-start | bytes 1769480 | tf_op jit(solution)/shard_map/ppermute | solution.py:313
  74.7 8.4 %collective-permute-done.15.c = bf16[288,1024]{1,0:T(8,128)(2,1)S(1)} collective-permute-done((bf16[288,1024]{1,0:T(8,128)(2,1)S(1)}, bf16[288,1024]{1,0:T(8,128)(2,1)S(1)}, u32[]{:S(2)}, u32[]{:S(2)}) %collective-permute-start.15) | collective-permute-done | bytes 589856 | tf_op jit(solution)/shard_map/ppermute | solution.py:313
  83.1 2.7 %shard_map.86 = (f32[576,512]{1,0:T(8,128)S(1)}, f32[576,256]{1,0:T(8,128)S(1)}) custom-call(bf16[8192,256]{1,0:T(8,128)(2,1)S(1)} %copy-done, bf16[8192,256]{1,0:T(8,128)(2,1)S(1)} %collective-permute-done.after.sibling, f32[16,1024]{1,0:T(8,128)S(1)} %pad_maximum_fusion.refs_3_.table, f32[576,512]{1,0:T(8,128)S(1)} %get-tuple-element.25.acc_in, ...), custom_call_target="tpu_custom_call" | custom-call | tf_op jit(solution)/shard_map/pallas_call | solution.py:281
  85.8 1.6 %collective-permute-done.17.value = bf16[288,1024]{1,0:T(8,128)(2,1)S(1)} collective-permute-done((bf16[288,1024]{1,0:T(8,128)(2,1)S(1)}, bf16[288,1024]{1,0:T(8,128)(2,1)S(1)}, u32[]{:S(2)}, u32[]{:S(2)}) %collective-permute-start.17) | collective-permute-done | bytes 589856 | tf_op jit(solution)/shard_map/ppermute | solution.py:313
  87.4 1.1 collective-permute-start.20
  88.5 0.9 collective-permute-done.18.b
  89.4 3.2 %shard_map.88 = (f32[288,512]{1,0:T(8,128)S(1)}, f32[288,256]{1,0:T(8,128)S(1)}, bf16[1024,512]{1,0:T(8,128)(2,1)S(1)}, f32[640,128]{1,0:T(8,128)S(1)}) custom-call(bf16[8192,256]{1,0:T(8,128)(2,1)S(1)} %copy-done, bf16[8192,256]{1,0:T(8,128)(2,1)S(1)} %collective-permute-done.after.sibling, f32[16,1024]{1,0:T(8,128)S(1)} %pad_maximum_fusion.refs_3_.table, ...), custom_call_target="tpu_custom_call" | custom-call | tf_op jit(solution)/shard_map/pallas_call | solution.py:281
  92.6 4.7 %collective-permute-done.20.c = bf16[288,1024]{1,0:T(8,128)(2,1)S(1)} collective-permute-done((bf16[288,1024]{1,0:T(8,128)(2,1)S(1)}, bf16[288,1024]{1,0:T(8,128)(2,1)S(1)}, u32[]{:S(2)}, u32[]{:S(2)}) %collective-permute-start.20) | collective-permute-done | bytes 589856 | tf_op jit(solution)/shard_map/ppermute | solution.py:313
  97.4 1.4 %shard_map.89 = f32[8,640]{1,0:T(8,128)S(1)} custom-call(bf16[1024,512]{1,0:T(8,128)(2,1)S(1)} %get-tuple-element.30.far_weights, f32[16,1024]{1,0:T(8,128)S(1)} %pad_maximum_fusion.refs_3_.table, f32[288,512]{1,0:T(8,128)S(1)} %get-tuple-element.31.left, f32[288,256]{1,0:T(8,128)S(1)} %get-tuple-element.32.left_side, ...), custom_call_target="tpu_custom_call" | custom-call | tf_op jit(solution)/shard_map/pallas_call | solution.py:281
  98.7 1.6 %collective-permute-start.21 = (f32[8,640]{1,0:T(8,128)S(1)}, f32[8,640]{1,0:T(8,128)S(1)}, u32[]{:S(2)}, u32[]{:S(2)}) collective-permute-start(f32[8,640]{1,0:T(8,128)S(1)} %shard_map.89), channel_id=1, source_target_pairs={{0,2},{1,3},{2,0},{3,1},{4,6},{5,7},{6,4},{7,5},{8,10},{9,11},{10,... | collective-permute-start | bytes 61448 | tf_op jit(solution)/shard_map/ppermute | solution.py:313
  100.3 1.3 %collective-permute-start.22 = (f32[8,640]{1,0:T(8,128)S(1)}, f32[8,640]{1,0:T(8,128)S(1)}, u32[]{:S(2)}, u32[]{:S(2)}) collective-permute-start(f32[8,640]{1,0:T(8,128)S(1)} %shard_map.89), channel_id=1, source_target_pairs={{0,4},{1,5},{2,6},{3,7},{4,0},{5,1},{6,2},{7,3},{8,12},{9,13},{10,... | collective-permute-start | bytes 61448 | tf_op jit(solution)/shard_map/ppermute | solution.py:313
  101.6 1.5 %collective-permute-start.23 = (f32[8,640]{1,0:T(8,128)S(1)}, f32[8,640]{1,0:T(8,128)S(1)}, u32[]{:S(2)}, u32[]{:S(2)}) collective-permute-start(f32[8,640]{1,0:T(8,128)S(1)} %shard_map.89), channel_id=1, source_target_pairs={{0,6},{1,7},{2,4},{3,5},{4,2},{5,3},{6,0},{7,1},{8,14},{9,15},{10,... | collective-permute-start | bytes 61448 | tf_op jit(solution)/shard_map/ppermute | solution.py:313
  103.2 2.0 %collective-permute-done.22 = f32[8,640]{1,0:T(8,128)S(1)} collective-permute-done((f32[8,640]{1,0:T(8,128)S(1)}, f32[8,640]{1,0:T(8,128)S(1)}, u32[]{:S(2)}, u32[]{:S(2)}) %collective-permute-start.22) | collective-permute-done | bytes 20512 | tf_op jit(solution)/shard_map/ppermute | solution.py:313
  105.1 2.1 %collective-permute-done.23 = f32[8,640]{1,0:T(8,128)S(1)} collective-permute-done((f32[8,640]{1,0:T(8,128)S(1)}, f32[8,640]{1,0:T(8,128)S(1)}, u32[]{:S(2)}, u32[]{:S(2)}) %collective-permute-start.23) | collective-permute-done | bytes 20512 | tf_op jit(solution)/shard_map/ppermute | solution.py:313
  107.3 1.4 %collective-permute-start.24 = (f32[8,640]{1,0:T(8,128)S(1)}, f32[8,640]{1,0:T(8,128)S(1)}, u32[]{:S(2)}, u32[]{:S(2)}) collective-permute-start(f32[8,640]{1,0:T(8,128)S(1)} %concatenate.19), channel_id=1, source_target_pairs={{0,1},{1,0},{2,3},{3,2},{4,5},{5,4},{6,7},{7,6},{8,9},{9,8},{10,11... | collective-permute-start | bytes 61448 | tf_op jit(solution)/shard_map/ppermute | solution.py:313
  109.4 1.5 %collective-permute-start.26 = (f32[8,640]{1,0:T(8,128)S(1)}, f32[8,640]{1,0:T(8,128)S(1)}, u32[]{:S(2)}, u32[]{:S(2)}) collective-permute-start(f32[8,640]{1,0:T(8,128)S(1)} %concatenate.19), channel_id=1, source_target_pairs={{0,17},{1,16},{2,19},{3,18},{4,21},{5,20},{6,23},{7,22},{8,25},{9,... | collective-permute-start | bytes 61448 | tf_op jit(solution)/shard_map/ppermute | solution.py:313
  111.2 1.4 %collective-permute-done.25 = f32[8,640]{1,0:T(8,128)S(1)} collective-permute-done((f32[8,640]{1,0:T(8,128)S(1)}, f32[8,640]{1,0:T(8,128)S(1)}, u32[]{:S(2)}, u32[]{:S(2)}) %collective-permute-start.25) | collective-permute-done | bytes 20512 | tf_op jit(solution)/shard_map/ppermute | solution.py:313
  112.5 1.5 %collective-permute-done.26 = f32[8,640]{1,0:T(8,128)S(1)} collective-permute-done((f32[8,640]{1,0:T(8,128)S(1)}, f32[8,640]{1,0:T(8,128)S(1)}, u32[]{:S(2)}, u32[]{:S(2)}) %collective-permute-start.26) | collective-permute-done | bytes 20512 | tf_op jit(solution)/shard_map/ppermute | solution.py:313
  114.2 1.2 %collective-permute-done.27.sibling = f32[8,640]{1,0:T(8,128)S(1)} collective-permute-done((f32[8,640]{1,0:T(8,128)S(1)}, f32[8,640]{1,0:T(8,128)S(1)}, u32[]{:S(2)}, u32[]{:S(2)}) %collective-permute-start.27) | collective-permute-done | bytes 20512 | tf_op jit(solution)/shard_map/ppermute | solution.py:442
  115.4 1.6 %shard_map.90 = (f32[1,384]{1,0:T(1,128)}, f32[1,1]{1,0:T(1,128)}) custom-call(f32[8,640]{1,0:T(8,128)S(1)} %maximum_maximum_fusion.mine, f32[8,640]{1,0:T(8,128)S(1)} %collective-permute-done.27.sibling, f32[2,640,384]{2,1,0:T(8,128)S(1)} %get-tuple-element.34.hit, f32[8,128]{1,0:T(8,128)S(1)} %get-tuple-element.35.per_row), custom_call_target="tpu_custom_call" | custom-call | tf_op jit(solution)/shard_map/pallas_call | solution.py:281
  (45 shorter events, 3.7 us)
Async XLA Ops:
  0.6 9.5 %collective-permute-start = (bf16[8192,256]{1,0:T(8,128)(2,1)}, bf16[8192,256]{1,0:T(8,128)(2,1)S(1)}, u32[]{:S(2)}, u32[]{:S(2)}) collective-permute-start(bf16[8192,256]{1,0:T(8,128)(2,1)} %head.5), channel_id=1, source_target_pairs={{0,8},{8,0},{16,24},{24,16},{1,9},{9,1},{17,25},{25,17},{2,10},{10... | collective-permute-start | bytes 12582920 | tf_op jit(solution)/shard_map/ppermute | solution.py:326
  1.1 9.0 %collective-permute-start.1 = (bf16[384,1024]{1,0:T(8,128)(2,1)}, bf16[384,1024]{1,0:T(8,128)(2,1)S(1)}, u32[]{:S(2)}, u32[]{:S(2)}) collective-permute-start(bf16[384,1024]{1,0:T(8,128)(2,1)} %bitcast.4), channel_id=1, source_target_pairs={{0,8},{8,0},{16,24},{24,16},{1,9},{9,1},{17,25},{25,17},{2,10},{10... | collective-permute-start | bytes 2359304 | tf_op jit(solution)/shard_map/ppermute | solution.py:325
  2.3 7.9 %collective-permute-start.2 = (bf16[192,1024]{1,0:T(8,128)(2,1)S(1)}, bf16[192,1024]{1,0:T(8,128)(2,1)S(1)}, u32[]{:S(2)}, u32[]{:S(2)}) collective-permute-start(bf16[192,1024]{1,0:T(8,128)(2,1)S(1)} %slice_bitcast_fusion), channel_id=1, source_target_pairs={{8,24},{24,8},{9,25},{25,9},{10,26},{26,10},{11,27},{27,11},{12,28... | collective-permute-start | bytes 1179656 | tf_op jit(solution)/shard_map/ppermute | solution.py:324
  4.3 1.1 copy-start.1
  5.5 4.6 %collective-permute-start.3 = (f32[2,1024]{1,0:T(2,128)S(1)}, f32[2,1024]{1,0:T(2,128)S(1)}, u32[]{:S(2)}, u32[]{:S(2)}) collective-permute-start(f32[2,1024]{1,0:T(2,128)S(1)} %get-tuple-element.21), channel_id=1, source_target_pairs={{0,1},{1,0},{2,3},{3,2},{4,5},{5,4},{6,7},{7,6},{8,9},{9,8},{10,11... | collective-permute-start | bytes 24584 | tf_op jit(solution)/shard_map/ppermute | solution.py:313
  10.2 0.7 copy-start.3
  10.8 7.2 %copy-start.2 = (s32[4,384]{1,0:T(4,128)S(1)}, s32[4,384]{1,0:T(4,128)}, u32[]{:S(2)}) copy-start(s32[4,384]{1,0:T(4,128)} %tokens.1) | copy-start | bytes 18436
  10.8 7.2 %copy-start.4 = (s32[4]{0:T(128)S(1)}, s32[4]{0:T(128)}, u32[]{:S(2)}) copy-start(s32[4]{0:T(128)} %lengths.3) | copy-start | bytes 52
  12.4 13.9 %collective-permute-start.9 = (bf16[288,1024]{1,0:T(8,128)(2,1)S(1)}, bf16[288,1024]{1,0:T(8,128)(2,1)S(1)}, u32[]{:S(2)}, u32[]{:S(2)}) collective-permute-start(bf16[288,1024]{1,0:T(8,128)(2,1)S(1)} %get-tuple-element.23.value.z), channel_id=1, source_target_pairs={{0,2},{1,3},{2,0},{3,1},{4,6},{5,7},{6,4},{7,5},{8,14},{9,15},{10,... | collective-permute-start | bytes 1769480 | tf_op jit(solution)/shard_map/ppermute | solution.py:313
  14.6 18.5 %collective-permute-start.7 = (bf16[288,1024]{1,0:T(8,128)(2,1)S(1)}, bf16[288,1024]{1,0:T(8,128)(2,1)S(1)}, u32[]{:S(2)}, u32[]{:S(2)}) collective-permute-start(bf16[288,1024]{1,0:T(8,128)(2,1)S(1)} %get-tuple-element.23.value.z), channel_id=1, source_target_pairs={{0,16},{1,17},{2,18},{3,19},{4,20},{5,21},{6,22},{7,23},{8,9},{9,8... | collective-permute-start | bytes 1769480 | tf_op jit(solution)/shard_map/ppermute | solution.py:313
  16.1 20.2 %collective-permute-start.6 = (bf16[288,1024]{1,0:T(8,128)(2,1)S(1)}, bf16[288,1024]{1,0:T(8,128)(2,1)S(1)}, u32[]{:S(2)}, u32[]{:S(2)}) collective-permute-start(bf16[288,1024]{1,0:T(8,128)(2,1)S(1)} %get-tuple-element.23.value.z), channel_id=1, source_target_pairs={{0,1},{1,0},{2,3},{3,2},{4,5},{5,4},{6,7},{7,6},{8,24},{9,25},{10,... | collective-permute-start | bytes 1769480 | tf_op jit(solution)/shard_map/ppermute | solution.py:313
  17.6 15.5 %collective-permute-start.4 = (f32[4,1024]{1,0:T(4,128)S(1)}, f32[4,1024]{1,0:T(4,128)S(1)}, u32[]{:S(2)}, u32[]{:S(2)}) collective-permute-start(f32[4,1024]{1,0:T(4,128)S(1)} %get-tuple-element.22), channel_id=1, source_target_pairs={{0,2},{1,3},{2,0},{3,1},{4,6},{5,7},{6,4},{7,5},{8,10},{9,11},{10,... | collective-permute-start | bytes 49160 | tf_op jit(solution)/shard_map/ppermute | solution.py:313
  26.3 27.5 %collective-permute-start.12 = (bf16[304,1024]{1,0:T(8,128)(2,1)S(1)}, bf16[304,1024]{1,0:T(8,128)(2,1)S(1)}, u32[]{:S(2)}, u32[]{:S(2)}) collective-permute-start(bf16[304,1024]{1,0:T(8,128)(2,1)S(1)} %shard_map.81), channel_id=1, source_target_pairs={{0,6},{1,7},{2,4},{3,5},{4,2},{5,3},{6,0},{7,1},{8,10},{9,11},{10,... | collective-permute-start | bytes 1867784 | tf_op jit(solution)/shard_map/ppermute | solution.py:313
  33.2 16.3 %collective-permute-start.10 = (bf16[288,1024]{1,0:T(8,128)(2,1)S(1)}, bf16[288,1024]{1,0:T(8,128)(2,1)S(1)}, u32[]{:S(2)}, u32[]{:S(2)}) collective-permute-start(bf16[288,1024]{1,0:T(8,128)(2,1)S(1)} %shard_map.80.z1), channel_id=1, source_target_pairs={{0,1},{1,0},{2,3},{3,2},{4,5},{5,4},{6,7},{7,6},{8,24},{9,25},{10,... | collective-permute-start | bytes 1769480 | tf_op jit(solution)/shard_map/ppermute | solution.py:313
  34.8 14.8 %collective-permute-start.11 = (bf16[288,1024]{1,0:T(8,128)(2,1)S(1)}, bf16[288,1024]{1,0:T(8,128)(2,1)S(1)}, u32[]{:S(2)}, u32[]{:S(2)}) collective-permute-start(bf16[288,1024]{1,0:T(8,128)(2,1)S(1)} %shard_map.80.z1), channel_id=1, source_target_pairs={{0,16},{1,17},{2,18},{3,19},{4,20},{5,21},{6,22},{7,23},{8,9},{9,8... | collective-permute-start | bytes 1769480 | tf_op jit(solution)/shard_map/ppermute | solution.py:313
  36.3 17.5 %collective-permute-start.8 = (bf16[288,1024]{1,0:T(8,128)(2,1)S(1)}, bf16[288,1024]{1,0:T(8,128)(2,1)S(1)}, u32[]{:S(2)}, u32[]{:S(2)}) collective-permute-start(bf16[288,1024]{1,0:T(8,128)(2,1)S(1)} %collective-permute-done.6.a), channel_id=1, source_target_pairs={{0,16},{1,17},{2,18},{3,19},{4,20},{5,21},{6,22},{7,23},{8,9},{9,8... | collective-permute-start | bytes 1769480 | tf_op jit(solution)/shard_map/ppermute | solution.py:313
  36.8 9.6 %collective-permute-start.5 = (f32[8,1024]{1,0:T(8,128)S(1)}, f32[8,1024]{1,0:T(8,128)S(1)}, u32[]{:S(2)}, u32[]{:S(2)}) collective-permute-start(f32[8,1024]{1,0:T(8,128)S(1)} %pad_maximum_fusion.1.refs_1_), channel_id=1, source_target_pairs={{0,4},{1,5},{2,6},{3,7},{4,0},{5,1},{6,2},{7,3},{8,12},{9,13},{10,... | collective-permute-start | bytes 98312 | tf_op jit(solution)/shard_map/ppermute | solution.py:313
  46.4 12.4 %copy-start = (bf16[8192,256]{1,0:T(8,128)(2,1)S(1)}, bf16[8192,256]{1,0:T(8,128)(2,1)}, u32[]{:S(2)}) copy-start(bf16[8192,256]{1,0:T(8,128)(2,1)} %head.5) | copy-start | bytes 12582916
  53.9 15.1 %collective-permute-start.13 = (bf16[288,1024]{1,0:T(8,128)(2,1)S(1)}, bf16[288,1024]{1,0:T(8,128)(2,1)S(1)}, u32[]{:S(2)}, u32[]{:S(2)}) collective-permute-start(bf16[288,1024]{1,0:T(8,128)(2,1)S(1)} %shard_map.82.value), channel_id=1, source_target_pairs={{0,1},{1,0},{2,3},{3,2},{4,5},{5,4},{6,7},{7,6},{8,24},{9,25},{10,... | collective-permute-start | bytes 1769480 | tf_op jit(solution)/shard_map/ppermute | solution.py:313
  55.4 15.7 %collective-permute-start.16 = (bf16[288,1024]{1,0:T(8,128)(2,1)S(1)}, bf16[288,1024]{1,0:T(8,128)(2,1)S(1)}, u32[]{:S(2)}, u32[]{:S(2)}) collective-permute-start(bf16[288,1024]{1,0:T(8,128)(2,1)S(1)} %shard_map.80.z1), channel_id=1, source_target_pairs={{0,6},{1,7},{2,4},{3,5},{4,2},{5,3},{6,0},{7,1},{8,10},{9,11},{10,... | collective-permute-start | bytes 1769480 | tf_op jit(solution)/shard_map/ppermute | solution.py:313
  57.2 17.5 %collective-permute-start.14 = (bf16[288,1024]{1,0:T(8,128)(2,1)S(1)}, bf16[288,1024]{1,0:T(8,128)(2,1)S(1)}, u32[]{:S(2)}, u32[]{:S(2)}) collective-permute-start(bf16[288,1024]{1,0:T(8,128)(2,1)S(1)} %shard_map.83.after.z), channel_id=1, source_target_pairs={{0,16},{1,17},{2,18},{3,19},{4,20},{5,21},{6,22},{7,23},{8,9},{9,8... | collective-permute-start | bytes 1769480 | tf_op jit(solution)/shard_map/ppermute | solution.py:313
  69.0 14.1 %collective-permute-start.15 = (bf16[288,1024]{1,0:T(8,128)(2,1)S(1)}, bf16[288,1024]{1,0:T(8,128)(2,1)S(1)}, u32[]{:S(2)}, u32[]{:S(2)}) collective-permute-start(bf16[288,1024]{1,0:T(8,128)(2,1)S(1)} %shard_map.85.a), channel_id=1, source_target_pairs={{0,16},{1,17},{2,18},{3,19},{4,20},{5,21},{6,22},{7,23},{8,9},{9,8... | collective-permute-start | bytes 1769480 | tf_op jit(solution)/shard_map/ppermute | solution.py:313
  71.1 16.3 %collective-permute-start.17 = (bf16[288,1024]{1,0:T(8,128)(2,1)S(1)}, bf16[288,1024]{1,0:T(8,128)(2,1)S(1)}, u32[]{:S(2)}, u32[]{:S(2)}) collective-permute-start(bf16[288,1024]{1,0:T(8,128)(2,1)S(1)} %collective-permute-done.16.z), channel_id=1, source_target_pairs={{0,1},{1,0},{2,3},{3,2},{4,5},{5,4},{6,7},{7,6},{8,24},{9,25},{10,... | collective-permute-start | bytes 1769480 | tf_op jit(solution)/shard_map/ppermute | solution.py:313
  72.6 16.8 %collective-permute-start.18 = (bf16[288,1024]{1,0:T(8,128)(2,1)S(1)}, bf16[288,1024]{1,0:T(8,128)(2,1)S(1)}, u32[]{:S(2)}, u32[]{:S(2)}) collective-permute-start(bf16[288,1024]{1,0:T(8,128)(2,1)S(1)} %collective-permute-done.16.z), channel_id=1, source_target_pairs={{0,16},{1,17},{2,18},{3,19},{4,20},{5,21},{6,22},{7,23},{8,9},{9,8... | collective-permute-start | bytes 1769480 | tf_op jit(solution)/shard_map/ppermute | solution.py:313
  73.5 16.0 %collective-permute-start.19 = (bf16[288,1024]{1,0:T(8,128)(2,1)S(1)}, bf16[288,1024]{1,0:T(8,128)(2,1)S(1)}, u32[]{:S(2)}, u32[]{:S(2)}) collective-permute-start(bf16[288,1024]{1,0:T(8,128)(2,1)S(1)} %collective-permute-done.8.refs_2_.c), channel_id=1, source_target_pairs={{0,2},{1,3},{2,0},{3,1},{4,6},{5,7},{6,4},{7,5},{8,14},{9,15},{10,... | collective-permute-start | bytes 1769480 | tf_op jit(solution)/shard_map/ppermute | solution.py:313
  87.4 9.9 %collective-permute-start.20 = (bf16[288,1024]{1,0:T(8,128)(2,1)S(1)}, bf16[288,1024]{1,0:T(8,128)(2,1)S(1)}, u32[]{:S(2)}, u32[]{:S(2)}) collective-permute-start(bf16[288,1024]{1,0:T(8,128)(2,1)S(1)} %shard_map.87.a), channel_id=1, source_target_pairs={{0,16},{1,17},{2,18},{3,19},{4,20},{5,21},{6,22},{7,23},{8,9},{9,8... | collective-permute-start | bytes 1769480 | tf_op jit(solution)/shard_map/ppermute | solution.py:313
  98.7 4.4 %collective-permute-start.21 = (f32[8,640]{1,0:T(8,128)S(1)}, f32[8,640]{1,0:T(8,128)S(1)}, u32[]{:S(2)}, u32[]{:S(2)}) collective-permute-start(f32[8,640]{1,0:T(8,128)S(1)} %shard_map.89), channel_id=1, source_target_pairs={{0,2},{1,3},{2,0},{3,1},{4,6},{5,7},{6,4},{7,5},{8,10},{9,11},{10,... | collective-permute-start | bytes 61448 | tf_op jit(solution)/shard_map/ppermute | solution.py:313
  100.3 4.8 %collective-permute-start.22 = (f32[8,640]{1,0:T(8,128)S(1)}, f32[8,640]{1,0:T(8,128)S(1)}, u32[]{:S(2)}, u32[]{:S(2)}) collective-permute-start(f32[8,640]{1,0:T(8,128)S(1)} %shard_map.89), channel_id=1, source_target_pairs={{0,4},{1,5},{2,6},{3,7},{4,0},{5,1},{6,2},{7,3},{8,12},{9,13},{10,... | collective-permute-start | bytes 61448 | tf_op jit(solution)/shard_map/ppermute | solution.py:313
  101.6 5.6 %collective-permute-start.23 = (f32[8,640]{1,0:T(8,128)S(1)}, f32[8,640]{1,0:T(8,128)S(1)}, u32[]{:S(2)}, u32[]{:S(2)}) collective-permute-start(f32[8,640]{1,0:T(8,128)S(1)} %shard_map.89), channel_id=1, source_target_pairs={{0,6},{1,7},{2,4},{3,5},{4,2},{5,3},{6,0},{7,1},{8,14},{9,15},{10,... | collective-permute-start | bytes 61448 | tf_op jit(solution)/shard_map/ppermute | solution.py:313
  107.3 3.8 %collective-permute-start.24 = (f32[8,640]{1,0:T(8,128)S(1)}, f32[8,640]{1,0:T(8,128)S(1)}, u32[]{:S(2)}, u32[]{:S(2)}) collective-permute-start(f32[8,640]{1,0:T(8,128)S(1)} %concatenate.19), channel_id=1, source_target_pairs={{0,1},{1,0},{2,3},{3,2},{4,5},{5,4},{6,7},{7,6},{8,9},{9,8},{10,11... | collective-permute-start | bytes 61448 | tf_op jit(solution)/shard_map/ppermute | solution.py:313
  108.8 3.8 %collective-permute-start.25 = (f32[8,640]{1,0:T(8,128)S(1)}, f32[8,640]{1,0:T(8,128)S(1)}, u32[]{:S(2)}, u32[]{:S(2)}) collective-permute-start(f32[8,640]{1,0:T(8,128)S(1)} %concatenate.19), channel_id=1, source_target_pairs={{0,16},{1,17},{2,18},{3,19},{4,20},{5,21},{6,22},{7,23},{8,24},{9,... | collective-permute-start | bytes 61448 | tf_op jit(solution)/shard_map/ppermute | solution.py:313
  109.4 4.7 %collective-permute-start.26 = (f32[8,640]{1,0:T(8,128)S(1)}, f32[8,640]{1,0:T(8,128)S(1)}, u32[]{:S(2)}, u32[]{:S(2)}) collective-permute-start(f32[8,640]{1,0:T(8,128)S(1)} %concatenate.19), channel_id=1, source_target_pairs={{0,17},{1,16},{2,19},{3,18},{4,21},{5,20},{6,23},{7,22},{8,25},{9,... | collective-permute-start | bytes 61448 | tf_op jit(solution)/shard_map/ppermute | solution.py:313
  114.2 1.2 %collective-permute-start.27 = (f32[8,640]{1,0:T(8,128)S(1)}, f32[8,640]{1,0:T(8,128)S(1)}, u32[]{:S(2)}, u32[]{:S(2)}) collective-permute-start(f32[8,640]{1,0:T(8,128)S(1)} %maximum_maximum_fusion.mine), channel_id=1, source_target_pairs={{0,8},{8,0},{16,24},{24,16},{1,9},{9,1},{17,25},{25,17},{2,10},{10... | collective-permute-start | bytes 61448 | tf_op jit(solution)/shard_map/ppermute | solution.py:442

commit v12 on v11

--- a/solution.py
+++ b/solution.py
@@ -366,12 +366,12 @@
         a1 = send(z1, perm_a)
         b1 = send(z1, perm_b)
         c0 = send(a0, perm_b)
+        z3 = call(gate_kernel, like(full), [VMEM] + [ANY], (z3, a1))
+        a3 = send(z3, perm_a)
         table = jnp.concatenate([table, send(table, perm_z[2])])
-        z3 = call(gate_kernel, like(full), [VMEM] + [ANY] * 4, (z3, a1, b1, c0, table))
-        a3 = send(z3, perm_a)
-        z3 = gate(z3)
+        z3 = gate(z3, b1, c0, table)
         b3 = send(z3, perm_b)
-        z2 = send(z1, perm_f)
+        z2 = send(gate(z1, z3), perm_f)
         acc, side, token_ids = call(
             begin_kernel,
             [acc_shape, side_shape, ids_shape],

time: 117 us -> 124 us (1.060)
  starting transfers between devices: 39 us -> 53.8 us
  waiting for transfers between devices: 56.2 us -> 48 us
    ppermute x24, starting transfers between devices: 37.7 us -> 52.5 us  [per_device(): send = lambda value, perm: lax.ppermute(value, AXES, perm)]
    ppermute x24, waiting for transfers between devices: 55 us -> 46.8 us  [per_device(): send = lambda value, perm: lax.ppermute(value, AXES, perm)]
    pallas_call x14 -> x15, Pallas kernels: 16.4 us -> 16.5 us  [call(): pl.pallas_call(body, out_shape=outs, in_specs=in_specs, out_specs=[VMEM]...]
  transfers between devices with their start and end apart: 28 -> 28, of which waited for: 17 -> 14; matrix products, arithmetic and copies ran while one was open for 2% -> 2% of each run, Pallas kernels for 10% -> 10%
where the time goes in v12:
time: 124 us
  starting transfers between devices  53.8 us (43%)
  waiting for transfers between devices  48 us (39%)
  Pallas kernels  16.5 us (13%)
  local copies, waits for them, and re-layouts  4.3 us (3%)
    ppermute x24, starting transfers between devices, per_device(): send = lambda value, perm: lax.ppermute(value, AXES, perm)  52.5 us
    ppermute x24, waiting for transfers between devices, per_device(): send = lambda value, perm: lax.ppermute(value, AXES, perm)  46.8 us
    pallas_call x15, Pallas kernels, call(): pl.pallas_call(body, out_shape=outs, in_specs=in_specs, out_specs=[VMEM]...  16.5 us
  transfers between devices with their start and end apart: 28, of which 14 were waited for; matrix products, arithmetic and copies ran while one was open for 2% of the time, Pallas kernels for 10%

profile of v12, /device:TPU:0, one launch (start us, length us, event | category | flops | bytes accessed | tf_op | source)
XLA Modules:
  0.0 123.6 jit_solution(15872272708762721719)
XLA Ops:
  0.6 0.5 collective-permute-start
  1.2 1.0 slice_bitcast_fusion
  2.3 0.7 collective-permute-start.2
  2.9 0.7 broadcast_in_dim.17.gain
  3.6 0.7 broadcast_in_dim.18.reward
  4.3 1.1 copy-done.1
  5.5 3.0 %collective-permute-start.3 = (f32[2,1024]{1,0:T(2,128)S(1)}, f32[2,1024]{1,0:T(2,128)S(1)}, u32[]{:S(2)}, u32[]{:S(2)}) collective-permute-start(f32[2,1024]{1,0:T(2,128)S(1)} %get-tuple-element.21), channel_id=1, source_target_pairs={{0,1},{1,0},{2,3},{3,2},{4,5},{5,4},{6,7},{7,6},{8,9},{9,8},{10,11... | collective-permute-start | bytes 24584 | tf_op jit(solution)/shard_map/ppermute | solution.py:313
  8.5 1.6 %collective-permute-done.3 = f32[2,1024]{1,0:T(2,128)S(1)} collective-permute-done((f32[2,1024]{1,0:T(2,128)S(1)}, f32[2,1024]{1,0:T(2,128)S(1)}, u32[]{:S(2)}, u32[]{:S(2)}) %collective-permute-start.3) | collective-permute-done | bytes 8224 | tf_op jit(solution)/shard_map/ppermute | solution.py:313
  10.2 0.6 copy-done.3
  10.8 1.6 %shard_map.78 = (bf16[288,1024]{1,0:T(8,128)(2,1)S(1)}, f32[4,1024]{1,0:T(4,128)S(1)}) custom-call(s32[4]{0:T(128)S(1)} %copy-done.3, bf16[384,1024]{1,0:T(8,128)(2,1)S(1)} %get-tuple-element.20.rows, bf16[384,1024]{1,0:T(8,128)(2,1)S(1)} %collective-permute-done.1.sibling, bf16[192,1024]{1,0:T(8,128)(2,1)S(1)} %collective-permute-done.2.extra, ...), custom_call_target="tpu_custom_call" | custom-call | tf_op jit(solution)/shard_map/pallas_call | solution.py:281
  12.4 2.2 %collective-permute-start.9 = (bf16[288,1024]{1,0:T(8,128)(2,1)S(1)}, bf16[288,1024]{1,0:T(8,128)(2,1)S(1)}, u32[]{:S(2)}, u32[]{:S(2)}) collective-permute-start(bf16[288,1024]{1,0:T(8,128)(2,1)S(1)} %get-tuple-element.23.value.z), channel_id=1, source_target_pairs={{0,2},{1,3},{2,0},{3,1},{4,6},{5,7},{6,4},{7,5},{8,14},{9,15},{10,... | collective-permute-start | bytes 1769480 | tf_op jit(solution)/shard_map/ppermute | solution.py:313
  14.6 1.5 %collective-permute-start.7 = (bf16[288,1024]{1,0:T(8,128)(2,1)S(1)}, bf16[288,1024]{1,0:T(8,128)(2,1)S(1)}, u32[]{:S(2)}, u32[]{:S(2)}) collective-permute-start(bf16[288,1024]{1,0:T(8,128)(2,1)S(1)} %get-tuple-element.23.value.z), channel_id=1, source_target_pairs={{0,16},{1,17},{2,18},{3,19},{4,20},{5,21},{6,22},{7,23},{8,9},{9,8... | collective-permute-start | bytes 1769480 | tf_op jit(solution)/shard_map/ppermute | solution.py:313
  16.1 1.5 %collective-permute-start.6 = (bf16[288,1024]{1,0:T(8,128)(2,1)S(1)}, bf16[288,1024]{1,0:T(8,128)(2,1)S(1)}, u32[]{:S(2)}, u32[]{:S(2)}) collective-permute-start(bf16[288,1024]{1,0:T(8,128)(2,1)S(1)} %get-tuple-element.23.value.z), channel_id=1, source_target_pairs={{0,1},{1,0},{2,3},{3,2},{4,5},{5,4},{6,7},{7,6},{8,24},{9,25},{10,... | collective-permute-start | bytes 1769480 | tf_op jit(solution)/shard_map/ppermute | solution.py:313
  17.6 0.4 collective-permute-start.4
  18.1 1.2 shard_map.79
  19.3 7.0 %collective-permute-done.9.value.after = bf16[288,1024]{1,0:T(8,128)(2,1)S(1)} collective-permute-done((bf16[288,1024]{1,0:T(8,128)(2,1)S(1)}, bf16[288,1024]{1,0:T(8,128)(2,1)S(1)}, u32[]{:S(2)}, u32[]{:S(2)}) %collective-permute-start.9) | collective-permute-done | bytes 589856 | tf_op jit(solution)/shard_map/ppermute | solution.py:313
  26.3 6.8 %collective-permute-start.12 = (bf16[304,1024]{1,0:T(8,128)(2,1)S(1)}, bf16[304,1024]{1,0:T(8,128)(2,1)S(1)}, u32[]{:S(2)}, u32[]{:S(2)}) collective-permute-start(bf16[304,1024]{1,0:T(8,128)(2,1)S(1)} %shard_map.81), channel_id=1, source_target_pairs={{0,6},{1,7},{2,4},{3,5},{4,2},{5,3},{6,0},{7,1},{8,10},{9,11},{10,... | collective-permute-start | bytes 1867784 | tf_op jit(solution)/shard_map/ppermute | solution.py:313
  33.2 1.6 %collective-permute-start.10 = (bf16[288,1024]{1,0:T(8,128)(2,1)S(1)}, bf16[288,1024]{1,0:T(8,128)(2,1)S(1)}, u32[]{:S(2)}, u32[]{:S(2)}) collective-permute-start(bf16[288,1024]{1,0:T(8,128)(2,1)S(1)} %shard_map.80.z1.value), channel_id=1, source_target_pairs={{0,1},{1,0},{2,3},{3,2},{4,5},{5,4},{6,7},{7,6},{8,24},{9,25},{10,... | collective-permute-start | bytes 1769480 | tf_op jit(solution)/shard_map/ppermute | solution.py:313
  34.8 1.5 %collective-permute-start.8 = (bf16[288,1024]{1,0:T(8,128)(2,1)S(1)}, bf16[288,1024]{1,0:T(8,128)(2,1)S(1)}, u32[]{:S(2)}, u32[]{:S(2)}) collective-permute-start(bf16[288,1024]{1,0:T(8,128)(2,1)S(1)} %collective-permute-done.6.a), channel_id=1, source_target_pairs={{0,16},{1,17},{2,18},{3,19},{4,20},{5,21},{6,22},{7,23},{8,9},{9,8... | collective-permute-start | bytes 1769480 | tf_op jit(solution)/shard_map/ppermute | solution.py:313
  36.3 0.5 collective-permute-start.11
  36.8 12.7 %collective-permute-done.10.refs_0_.a1 = bf16[288,1024]{1,0:T(8,128)(2,1)S(1)} collective-permute-done((bf16[288,1024]{1,0:T(8,128)(2,1)S(1)}, bf16[288,1024]{1,0:T(8,128)(2,1)S(1)}, u32[]{:S(2)}, u32[]{:S(2)}) %collective-permute-start.10) | collective-permute-done | bytes 589856 | tf_op jit(solution)/shard_map/ppermute | solution.py:313
  49.6 1.6 %collective-permute-start.13 = (bf16[288,1024]{1,0:T(8,128)(2,1)S(1)}, bf16[288,1024]{1,0:T(8,128)(2,1)S(1)}, u32[]{:S(2)}, u32[]{:S(2)}) collective-permute-start(bf16[288,1024]{1,0:T(8,128)(2,1)S(1)} %shard_map.82.value), channel_id=1, source_target_pairs={{0,1},{1,0},{2,3},{3,2},{4,5},{5,4},{6,7},{7,6},{8,24},{9,25},{10,... | collective-permute-start | bytes 1769480 | tf_op jit(solution)/shard_map/ppermute | solution.py:313
  51.2 5.6 %collective-permute-done.11.refs_0_.b1 = bf16[288,1024]{1,0:T(8,128)(2,1)S(1)} collective-permute-done((bf16[288,1024]{1,0:T(8,128)(2,1)S(1)}, bf16[288,1024]{1,0:T(8,128)(2,1)S(1)}, u32[]{:S(2)}, u32[]{:S(2)}) %collective-permute-start.11) | collective-permute-done | bytes 589856 | tf_op jit(solution)/shard_map/ppermute | solution.py:313
  56.8 3.9 %collective-permute-start.16 = (bf16[288,1024]{1,0:T(8,128)(2,1)S(1)}, bf16[288,1024]{1,0:T(8,128)(2,1)S(1)}, u32[]{:S(2)}, u32[]{:S(2)}) collective-permute-start(bf16[288,1024]{1,0:T(8,128)(2,1)S(1)} %shard_map.87), channel_id=1, source_target_pairs={{0,6},{1,7},{2,4},{3,5},{4,2},{5,3},{6,0},{7,1},{8,10},{9,11},{10,... | collective-permute-start | bytes 1769480 | tf_op jit(solution)/shard_map/ppermute | solution.py:313
  60.8 1.5 %collective-permute-start.14 = (bf16[288,1024]{1,0:T(8,128)(2,1)S(1)}, bf16[288,1024]{1,0:T(8,128)(2,1)S(1)}, u32[]{:S(2)}, u32[]{:S(2)}) collective-permute-start(bf16[288,1024]{1,0:T(8,128)(2,1)S(1)} %shard_map.83.after.z.refs_0_), channel_id=1, source_target_pairs={{0,16},{1,17},{2,18},{3,19},{4,20},{5,21},{6,22},{7,23},{8,9},{9,8... | collective-permute-start | bytes 1769480 | tf_op jit(solution)/shard_map/ppermute | solution.py:313
  62.3 4.5 %shard_map.84 = (f32[576,512]{1,0:T(8,128)S(1)}, f32[576,256]{1,0:T(8,128)S(1)}, s32[576,1]{1,0:T(8,128)S(1)}) custom-call(bf16[8192,256]{1,0:T(8,128)(2,1)S(1)} %copy-done, bf16[8192,256]{1,0:T(8,128)(2,1)S(1)} %collective-permute-done.after.sibling, f32[16,1024]{1,0:T(8,128)S(1)} %pad_maximum_fusion.refs_2_.table, ...), custom_call_target="tpu_custom_call" | custom-call | tf_op jit(solution)/shard_map/pallas_call | solution.py:281
  66.8 0.6 collective-permute-start.15
  67.4 5.8 %collective-permute-done.16.z = bf16[288,1024]{1,0:T(8,128)(2,1)S(1)} collective-permute-done((bf16[288,1024]{1,0:T(8,128)(2,1)S(1)}, bf16[288,1024]{1,0:T(8,128)(2,1)S(1)}, u32[]{:S(2)}, u32[]{:S(2)}) %collective-permute-start.16) | collective-permute-done | bytes 589856 | tf_op jit(solution)/shard_map/ppermute | solution.py:313
  73.2 1.1 collective-permute-start.17
  74.3 9.6 %collective-permute-start.19 = (bf16[288,1024]{1,0:T(8,128)(2,1)S(1)}, bf16[288,1024]{1,0:T(8,128)(2,1)S(1)}, u32[]{:S(2)}, u32[]{:S(2)}) collective-permute-start(bf16[288,1024]{1,0:T(8,128)(2,1)S(1)} %collective-permute-done.8.refs_1_.c), channel_id=1, source_target_pairs={{0,2},{1,3},{2,0},{3,1},{4,6},{5,7},{6,4},{7,5},{8,14},{9,15},{10,... | collective-permute-start | bytes 1769480 | tf_op jit(solution)/shard_map/ppermute | solution.py:313
  83.9 1.7 %collective-permute-start.18 = (bf16[288,1024]{1,0:T(8,128)(2,1)S(1)}, bf16[288,1024]{1,0:T(8,128)(2,1)S(1)}, u32[]{:S(2)}, u32[]{:S(2)}) collective-permute-start(bf16[288,1024]{1,0:T(8,128)(2,1)S(1)} %collective-permute-done.16.z), channel_id=1, source_target_pairs={{0,16},{1,17},{2,18},{3,19},{4,20},{5,21},{6,22},{7,23},{8,9},{9,8... | collective-permute-start | bytes 1769480 | tf_op jit(solution)/shard_map/ppermute | solution.py:313
  85.6 2.7 %shard_map.86 = (f32[576,512]{1,0:T(8,128)S(1)}, f32[576,256]{1,0:T(8,128)S(1)}) custom-call(bf16[8192,256]{1,0:T(8,128)(2,1)S(1)} %copy-done, bf16[8192,256]{1,0:T(8,128)(2,1)S(1)} %collective-permute-done.after.sibling, f32[16,1024]{1,0:T(8,128)S(1)} %pad_maximum_fusion.refs_2_.table, f32[576,512]{1,0:T(8,128)S(1)} %get-tuple-element.25.acc_in, ...), custom_call_target="tpu_custom_call" | custom-call | tf_op jit(solution)/shard_map/pallas_call | solution.py:281
  88.7 3.0 %collective-permute-done.19.c1 = bf16[288,1024]{1,0:T(8,128)(2,1)S(1)} collective-permute-done((bf16[288,1024]{1,0:T(8,128)(2,1)S(1)}, bf16[288,1024]{1,0:T(8,128)(2,1)S(1)}, u32[]{:S(2)}, u32[]{:S(2)}) %collective-permute-start.19) | collective-permute-done | bytes 589856 | tf_op jit(solution)/shard_map/ppermute | solution.py:313
  91.7 2.0 %collective-permute-done.18.b = bf16[288,1024]{1,0:T(8,128)(2,1)S(1)} collective-permute-done((bf16[288,1024]{1,0:T(8,128)(2,1)S(1)}, bf16[288,1024]{1,0:T(8,128)(2,1)S(1)}, u32[]{:S(2)}, u32[]{:S(2)}) %collective-permute-start.18) | collective-permute-done | bytes 589856 | tf_op jit(solution)/shard_map/ppermute | solution.py:313
  93.8 3.2 %shard_map.89 = (f32[288,512]{1,0:T(8,128)S(1)}, f32[288,256]{1,0:T(8,128)S(1)}, bf16[1024,512]{1,0:T(8,128)(2,1)S(1)}, f32[640,128]{1,0:T(8,128)S(1)}) custom-call(bf16[8192,256]{1,0:T(8,128)(2,1)S(1)} %copy-done, bf16[8192,256]{1,0:T(8,128)(2,1)S(1)} %collective-permute-done.after.sibling, f32[16,1024]{1,0:T(8,128)S(1)} %pad_maximum_fusion.refs_2_.table, ...), custom_call_target="tpu_custom_call" | custom-call | tf_op jit(solution)/shard_map/pallas_call | solution.py:281
  97.0 3.1 %collective-permute-done.20.c = bf16[288,1024]{1,0:T(8,128)(2,1)S(1)} collective-permute-done((bf16[288,1024]{1,0:T(8,128)(2,1)S(1)}, bf16[288,1024]{1,0:T(8,128)(2,1)S(1)}, u32[]{:S(2)}, u32[]{:S(2)}) %collective-permute-start.20) | collective-permute-done | bytes 589856 | tf_op jit(solution)/shard_map/ppermute | solution.py:313
  100.1 1.4 %shard_map.90 = f32[8,640]{1,0:T(8,128)S(1)} custom-call(bf16[1024,512]{1,0:T(8,128)(2,1)S(1)} %get-tuple-element.30.far_weights, f32[16,1024]{1,0:T(8,128)S(1)} %pad_maximum_fusion.refs_2_.table, f32[288,512]{1,0:T(8,128)S(1)} %get-tuple-element.31.left, f32[288,256]{1,0:T(8,128)S(1)} %get-tuple-element.32.left_side, ...), custom_call_target="tpu_custom_call" | custom-call | tf_op jit(solution)/shard_map/pallas_call | solution.py:281
  101.5 0.6 collective-permute-start.23
  102.1 8.6 %collective-permute-start.22 = (f32[8,640]{1,0:T(8,128)S(1)}, f32[8,640]{1,0:T(8,128)S(1)}, u32[]{:S(2)}, u32[]{:S(2)}) collective-permute-start(f32[8,640]{1,0:T(8,128)S(1)} %shard_map.90), channel_id=1, source_target_pairs={{0,4},{1,5},{2,6},{3,7},{4,0},{5,1},{6,2},{7,3},{8,12},{9,13},{10,... | collective-permute-start | bytes 61448 | tf_op jit(solution)/shard_map/ppermute | solution.py:313
  110.6 0.4 collective-permute-start.21
  111.0 1.6 %collective-permute-done.22 = f32[8,640]{1,0:T(8,128)S(1)} collective-permute-done((f32[8,640]{1,0:T(8,128)S(1)}, f32[8,640]{1,0:T(8,128)S(1)}, u32[]{:S(2)}, u32[]{:S(2)}) %collective-permute-start.22) | collective-permute-done | bytes 20512 | tf_op jit(solution)/shard_map/ppermute | solution.py:313
  112.6 1.8 %collective-permute-done.21 = f32[8,640]{1,0:T(8,128)S(1)} collective-permute-done((f32[8,640]{1,0:T(8,128)S(1)}, f32[8,640]{1,0:T(8,128)S(1)}, u32[]{:S(2)}, u32[]{:S(2)}) %collective-permute-start.21) | collective-permute-done | bytes 20512 | tf_op jit(solution)/shard_map/ppermute | solution.py:313
  114.5 2.1 %collective-permute-start.26 = (f32[8,640]{1,0:T(8,128)S(1)}, f32[8,640]{1,0:T(8,128)S(1)}, u32[]{:S(2)}, u32[]{:S(2)}) collective-permute-start(f32[8,640]{1,0:T(8,128)S(1)} %concatenate.19), channel_id=1, source_target_pairs={{0,17},{1,16},{2,19},{3,18},{4,21},{5,20},{6,23},{7,22},{8,25},{9,... | collective-permute-start | bytes 61448 | tf_op jit(solution)/shard_map/ppermute | solution.py:313
  116.9 1.1 collective-permute-start.24
  118.1 1.1 collective-permute-done.26
  119.2 1.2 collective-permute-done.25
  120.8 1.2 collective-permute-done.27.sibling
  122.0 1.6 %shard_map.91 = (f32[1,384]{1,0:T(1,128)}, f32[1,1]{1,0:T(1,128)}) custom-call(f32[8,640]{1,0:T(8,128)S(1)} %maximum_maximum_fusion.mine, f32[8,640]{1,0:T(8,128)S(1)} %collective-permute-done.27.sibling, f32[2,640,384]{2,1,0:T(8,128)S(1)} %get-tuple-element.34.hit, f32[8,128]{1,0:T(8,128)S(1)} %get-tuple-element.35.per_row), custom_call_target="tpu_custom_call" | custom-call | tf_op jit(solution)/shard_map/pallas_call | solution.py:281
  (44 shorter events, 1.8 us)
Async XLA Ops:
  0.6 9.5 %collective-permute-start = (bf16[8192,256]{1,0:T(8,128)(2,1)}, bf16[8192,256]{1,0:T(8,128)(2,1)S(1)}, u32[]{:S(2)}, u32[]{:S(2)}) collective-permute-start(bf16[8192,256]{1,0:T(8,128)(2,1)} %head.5), channel_id=1, source_target_pairs={{0,8},{8,0},{16,24},{24,16},{1,9},{9,1},{17,25},{25,17},{2,10},{10... | collective-permute-start | bytes 12582920 | tf_op jit(solution)/shard_map/ppermute | solution.py:326
  1.1 9.0 %collective-permute-start.1 = (bf16[384,1024]{1,0:T(8,128)(2,1)}, bf16[384,1024]{1,0:T(8,128)(2,1)S(1)}, u32[]{:S(2)}, u32[]{:S(2)}) collective-permute-start(bf16[384,1024]{1,0:T(8,128)(2,1)} %bitcast.4), channel_id=1, source_target_pairs={{0,8},{8,0},{16,24},{24,16},{1,9},{9,1},{17,25},{25,17},{2,10},{10... | collective-permute-start | bytes 2359304 | tf_op jit(solution)/shard_map/ppermute | solution.py:325
  2.3 7.9 %collective-permute-start.2 = (bf16[192,1024]{1,0:T(8,128)(2,1)S(1)}, bf16[192,1024]{1,0:T(8,128)(2,1)S(1)}, u32[]{:S(2)}, u32[]{:S(2)}) collective-permute-start(bf16[192,1024]{1,0:T(8,128)(2,1)S(1)} %slice_bitcast_fusion), channel_id=1, source_target_pairs={{8,24},{24,8},{9,25},{25,9},{10,26},{26,10},{11,27},{27,11},{12,28... | collective-permute-start | bytes 1179656 | tf_op jit(solution)/shard_map/ppermute | solution.py:324
  4.3 1.1 copy-start.1
  5.5 4.6 %collective-permute-start.3 = (f32[2,1024]{1,0:T(2,128)S(1)}, f32[2,1024]{1,0:T(2,128)S(1)}, u32[]{:S(2)}, u32[]{:S(2)}) collective-permute-start(f32[2,1024]{1,0:T(2,128)S(1)} %get-tuple-element.21), channel_id=1, source_target_pairs={{0,1},{1,0},{2,3},{3,2},{4,5},{5,4},{6,7},{7,6},{8,9},{9,8},{10,11... | collective-permute-start | bytes 24584 | tf_op jit(solution)/shard_map/ppermute | solution.py:313
  10.2 0.7 copy-start.3
  10.8 7.2 %copy-start.2 = (s32[4,384]{1,0:T(4,128)S(1)}, s32[4,384]{1,0:T(4,128)}, u32[]{:S(2)}) copy-start(s32[4,384]{1,0:T(4,128)} %tokens.1) | copy-start | bytes 18436
  12.4 13.9 %collective-permute-start.9 = (bf16[288,1024]{1,0:T(8,128)(2,1)S(1)}, bf16[288,1024]{1,0:T(8,128)(2,1)S(1)}, u32[]{:S(2)}, u32[]{:S(2)}) collective-permute-start(bf16[288,1024]{1,0:T(8,128)(2,1)S(1)} %get-tuple-element.23.value.z), channel_id=1, source_target_pairs={{0,2},{1,3},{2,0},{3,1},{4,6},{5,7},{6,4},{7,5},{8,14},{9,15},{10,... | collective-permute-start | bytes 1769480 | tf_op jit(solution)/shard_map/ppermute | solution.py:313
  14.6 18.5 %collective-permute-start.7 = (bf16[288,1024]{1,0:T(8,128)(2,1)S(1)}, bf16[288,1024]{1,0:T(8,128)(2,1)S(1)}, u32[]{:S(2)}, u32[]{:S(2)}) collective-permute-start(bf16[288,1024]{1,0:T(8,128)(2,1)S(1)} %get-tuple-element.23.value.z), channel_id=1, source_target_pairs={{0,16},{1,17},{2,18},{3,19},{4,20},{5,21},{6,22},{7,23},{8,9},{9,8... | collective-permute-start | bytes 1769480 | tf_op jit(solution)/shard_map/ppermute | solution.py:313
  16.1 18.6 %collective-permute-start.6 = (bf16[288,1024]{1,0:T(8,128)(2,1)S(1)}, bf16[288,1024]{1,0:T(8,128)(2,1)S(1)}, u32[]{:S(2)}, u32[]{:S(2)}) collective-permute-start(bf16[288,1024]{1,0:T(8,128)(2,1)S(1)} %get-tuple-element.23.value.z), channel_id=1, source_target_pairs={{0,1},{1,0},{2,3},{3,2},{4,5},{5,4},{6,7},{7,6},{8,24},{9,25},{10,... | collective-permute-start | bytes 1769480 | tf_op jit(solution)/shard_map/ppermute | solution.py:313
  17.6 15.5 %collective-permute-start.4 = (f32[4,1024]{1,0:T(4,128)S(1)}, f32[4,1024]{1,0:T(4,128)S(1)}, u32[]{:S(2)}, u32[]{:S(2)}) collective-permute-start(f32[4,1024]{1,0:T(4,128)S(1)} %get-tuple-element.22), channel_id=1, source_target_pairs={{0,2},{1,3},{2,0},{3,1},{4,6},{5,7},{6,4},{7,5},{8,10},{9,11},{10,... | collective-permute-start | bytes 49160 | tf_op jit(solution)/shard_map/ppermute | solution.py:313
  26.3 23.2 %collective-permute-start.12 = (bf16[304,1024]{1,0:T(8,128)(2,1)S(1)}, bf16[304,1024]{1,0:T(8,128)(2,1)S(1)}, u32[]{:S(2)}, u32[]{:S(2)}) collective-permute-start(bf16[304,1024]{1,0:T(8,128)(2,1)S(1)} %shard_map.81), channel_id=1, source_target_pairs={{0,6},{1,7},{2,4},{3,5},{4,2},{5,3},{6,0},{7,1},{8,10},{9,11},{10,... | collective-permute-start | bytes 1867784 | tf_op jit(solution)/shard_map/ppermute | solution.py:313
  33.2 16.3 %collective-permute-start.10 = (bf16[288,1024]{1,0:T(8,128)(2,1)S(1)}, bf16[288,1024]{1,0:T(8,128)(2,1)S(1)}, u32[]{:S(2)}, u32[]{:S(2)}) collective-permute-start(bf16[288,1024]{1,0:T(8,128)(2,1)S(1)} %shard_map.80.z1.value), channel_id=1, source_target_pairs={{0,1},{1,0},{2,3},{3,2},{4,5},{5,4},{6,7},{7,6},{8,24},{9,25},{10,... | collective-permute-start | bytes 1769480 | tf_op jit(solution)/shard_map/ppermute | solution.py:313
  34.8 16.4 %collective-permute-start.8 = (bf16[288,1024]{1,0:T(8,128)(2,1)S(1)}, bf16[288,1024]{1,0:T(8,128)(2,1)S(1)}, u32[]{:S(2)}, u32[]{:S(2)}) collective-permute-start(bf16[288,1024]{1,0:T(8,128)(2,1)S(1)} %collective-permute-done.6.a), channel_id=1, source_target_pairs={{0,16},{1,17},{2,18},{3,19},{4,20},{5,21},{6,22},{7,23},{8,9},{9,8... | collective-permute-start | bytes 1769480 | tf_op jit(solution)/shard_map/ppermute | solution.py:313
  36.3 20.5 %collective-permute-start.11 = (bf16[288,1024]{1,0:T(8,128)(2,1)S(1)}, bf16[288,1024]{1,0:T(8,128)(2,1)S(1)}, u32[]{:S(2)}, u32[]{:S(2)}) collective-permute-start(bf16[288,1024]{1,0:T(8,128)(2,1)S(1)} %shard_map.80.z1.value), channel_id=1, source_target_pairs={{0,16},{1,17},{2,18},{3,19},{4,20},{5,21},{6,22},{7,23},{8,9},{9,8... | collective-permute-start | bytes 1769480 | tf_op jit(solution)/shard_map/ppermute | solution.py:313
  36.8 14.3 %collective-permute-start.5 = (f32[8,1024]{1,0:T(8,128)S(1)}, f32[8,1024]{1,0:T(8,128)S(1)}, u32[]{:S(2)}, u32[]{:S(2)}) collective-permute-start(f32[8,1024]{1,0:T(8,128)S(1)} %pad_maximum_fusion.1.refs_1_), channel_id=1, source_target_pairs={{0,4},{1,5},{2,6},{3,7},{4,0},{5,1},{6,2},{7,3},{8,12},{9,13},{10,... | collective-permute-start | bytes 98312 | tf_op jit(solution)/shard_map/ppermute | solution.py:313
  49.6 17.2 %collective-permute-start.13 = (bf16[288,1024]{1,0:T(8,128)(2,1)S(1)}, bf16[288,1024]{1,0:T(8,128)(2,1)S(1)}, u32[]{:S(2)}, u32[]{:S(2)}) collective-permute-start(bf16[288,1024]{1,0:T(8,128)(2,1)S(1)} %shard_map.82.value), channel_id=1, source_target_pairs={{0,1},{1,0},{2,3},{3,2},{4,5},{5,4},{6,7},{7,6},{8,24},{9,25},{10,... | collective-permute-start | bytes 1769480 | tf_op jit(solution)/shard_map/ppermute | solution.py:313
  51.1 11.2 %copy-start = (bf16[8192,256]{1,0:T(8,128)(2,1)S(1)}, bf16[8192,256]{1,0:T(8,128)(2,1)}, u32[]{:S(2)}) copy-start(bf16[8192,256]{1,0:T(8,128)(2,1)} %head.5) | copy-start | bytes 12582916
  56.8 16.4 %collective-permute-start.16 = (bf16[288,1024]{1,0:T(8,128)(2,1)S(1)}, bf16[288,1024]{1,0:T(8,128)(2,1)S(1)}, u32[]{:S(2)}, u32[]{:S(2)}) collective-permute-start(bf16[288,1024]{1,0:T(8,128)(2,1)S(1)} %shard_map.87), channel_id=1, source_target_pairs={{0,6},{1,7},{2,4},{3,5},{4,2},{5,3},{6,0},{7,1},{8,10},{9,11},{10,... | collective-permute-start | bytes 1769480 | tf_op jit(solution)/shard_map/ppermute | solution.py:313
  60.8 24.8 %collective-permute-start.14 = (bf16[288,1024]{1,0:T(8,128)(2,1)S(1)}, bf16[288,1024]{1,0:T(8,128)(2,1)S(1)}, u32[]{:S(2)}, u32[]{:S(2)}) collective-permute-start(bf16[288,1024]{1,0:T(8,128)(2,1)S(1)} %shard_map.83.after.z.refs_0_), channel_id=1, source_target_pairs={{0,16},{1,17},{2,18},{3,19},{4,20},{5,21},{6,22},{7,23},{8,9},{9,8... | collective-permute-start | bytes 1769480 | tf_op jit(solution)/shard_map/ppermute | solution.py:313
  66.8 18.7 %collective-permute-start.15 = (bf16[288,1024]{1,0:T(8,128)(2,1)S(1)}, bf16[288,1024]{1,0:T(8,128)(2,1)S(1)}, u32[]{:S(2)}, u32[]{:S(2)}) collective-permute-start(bf16[288,1024]{1,0:T(8,128)(2,1)S(1)} %shard_map.85.a), channel_id=1, source_target_pairs={{0,16},{1,17},{2,18},{3,19},{4,20},{5,21},{6,22},{7,23},{8,9},{9,8... | collective-permute-start | bytes 1769480 | tf_op jit(solution)/shard_map/ppermute | solution.py:313
  73.2 15.1 %collective-permute-start.17 = (bf16[288,1024]{1,0:T(8,128)(2,1)S(1)}, bf16[288,1024]{1,0:T(8,128)(2,1)S(1)}, u32[]{:S(2)}, u32[]{:S(2)}) collective-permute-start(bf16[288,1024]{1,0:T(8,128)(2,1)S(1)} %collective-permute-done.16.z), channel_id=1, source_target_pairs={{0,1},{1,0},{2,3},{3,2},{4,5},{5,4},{6,7},{7,6},{8,24},{9,25},{10,... | collective-permute-start | bytes 1769480 | tf_op jit(solution)/shard_map/ppermute | solution.py:313
  74.3 17.4 %collective-permute-start.19 = (bf16[288,1024]{1,0:T(8,128)(2,1)S(1)}, bf16[288,1024]{1,0:T(8,128)(2,1)S(1)}, u32[]{:S(2)}, u32[]{:S(2)}) collective-permute-start(bf16[288,1024]{1,0:T(8,128)(2,1)S(1)} %collective-permute-done.8.refs_1_.c), channel_id=1, source_target_pairs={{0,2},{1,3},{2,0},{3,1},{4,6},{5,7},{6,4},{7,5},{8,14},{9,15},{10,... | collective-permute-start | bytes 1769480 | tf_op jit(solution)/shard_map/ppermute | solution.py:313
  83.9 9.9 %collective-permute-start.18 = (bf16[288,1024]{1,0:T(8,128)(2,1)S(1)}, bf16[288,1024]{1,0:T(8,128)(2,1)S(1)}, u32[]{:S(2)}, u32[]{:S(2)}) collective-permute-start(bf16[288,1024]{1,0:T(8,128)(2,1)S(1)} %collective-permute-done.16.z), channel_id=1, source_target_pairs={{0,16},{1,17},{2,18},{3,19},{4,20},{5,21},{6,22},{7,23},{8,9},{9,8... | collective-permute-start | bytes 1769480 | tf_op jit(solution)/shard_map/ppermute | solution.py:313
  88.3 11.8 %collective-permute-start.20 = (bf16[288,1024]{1,0:T(8,128)(2,1)S(1)}, bf16[288,1024]{1,0:T(8,128)(2,1)S(1)}, u32[]{:S(2)}, u32[]{:S(2)}) collective-permute-start(bf16[288,1024]{1,0:T(8,128)(2,1)S(1)} %shard_map.88.a), channel_id=1, source_target_pairs={{0,16},{1,17},{2,18},{3,19},{4,20},{5,21},{6,22},{7,23},{8,9},{9,8... | collective-permute-start | bytes 1769480 | tf_op jit(solution)/shard_map/ppermute | solution.py:313
  101.5 9.6 %collective-permute-start.23 = (f32[8,640]{1,0:T(8,128)S(1)}, f32[8,640]{1,0:T(8,128)S(1)}, u32[]{:S(2)}, u32[]{:S(2)}) collective-permute-start(f32[8,640]{1,0:T(8,128)S(1)} %shard_map.90), channel_id=1, source_target_pairs={{0,6},{1,7},{2,4},{3,5},{4,2},{5,3},{6,0},{7,1},{8,14},{9,15},{10,... | collective-permute-start | bytes 61448 | tf_op jit(solution)/shard_map/ppermute | solution.py:313
  102.1 10.5 %collective-permute-start.22 = (f32[8,640]{1,0:T(8,128)S(1)}, f32[8,640]{1,0:T(8,128)S(1)}, u32[]{:S(2)}, u32[]{:S(2)}) collective-permute-start(f32[8,640]{1,0:T(8,128)S(1)} %shard_map.90), channel_id=1, source_target_pairs={{0,4},{1,5},{2,6},{3,7},{4,0},{5,1},{6,2},{7,3},{8,12},{9,13},{10,... | collective-permute-start | bytes 61448 | tf_op jit(solution)/shard_map/ppermute | solution.py:313
  110.6 3.8 %collective-permute-start.21 = (f32[8,640]{1,0:T(8,128)S(1)}, f32[8,640]{1,0:T(8,128)S(1)}, u32[]{:S(2)}, u32[]{:S(2)}) collective-permute-start(f32[8,640]{1,0:T(8,128)S(1)} %shard_map.90), channel_id=1, source_target_pairs={{0,2},{1,3},{2,0},{3,1},{4,6},{5,7},{6,4},{7,5},{8,10},{9,11},{10,... | collective-permute-start | bytes 61448 | tf_op jit(solution)/shard_map/ppermute | solution.py:313
  114.5 4.7 %collective-permute-start.26 = (f32[8,640]{1,0:T(8,128)S(1)}, f32[8,640]{1,0:T(8,128)S(1)}, u32[]{:S(2)}, u32[]{:S(2)}) collective-permute-start(f32[8,640]{1,0:T(8,128)S(1)} %concatenate.19), channel_id=1, source_target_pairs={{0,17},{1,16},{2,19},{3,18},{4,21},{5,20},{6,23},{7,22},{8,25},{9,... | collective-permute-start | bytes 61448 | tf_op jit(solution)/shard_map/ppermute | solution.py:313
  116.6 3.8 %collective-permute-start.25 = (f32[8,640]{1,0:T(8,128)S(1)}, f32[8,640]{1,0:T(8,128)S(1)}, u32[]{:S(2)}, u32[]{:S(2)}) collective-permute-start(f32[8,640]{1,0:T(8,128)S(1)} %concatenate.19), channel_id=1, source_target_pairs={{0,16},{1,17},{2,18},{3,19},{4,20},{5,21},{6,22},{7,23},{8,24},{9,... | collective-permute-start | bytes 61448 | tf_op jit(solution)/shard_map/ppermute | solution.py:313
  116.9 3.8 %collective-permute-start.24 = (f32[8,640]{1,0:T(8,128)S(1)}, f32[8,640]{1,0:T(8,128)S(1)}, u32[]{:S(2)}, u32[]{:S(2)}) collective-permute-start(f32[8,640]{1,0:T(8,128)S(1)} %concatenate.19), channel_id=1, source_target_pairs={{0,1},{1,0},{2,3},{3,2},{4,5},{5,4},{6,7},{7,6},{8,9},{9,8},{10,11... | collective-permute-start | bytes 61448 | tf_op jit(solution)/shard_map/ppermute | solution.py:313
  120.8 1.2 collective-permute-start.27

commit v13 on v12

--- a/solution.py
+++ b/solution.py
@@ -369,9 +369,9 @@
         z3 = call(gate_kernel, like(full), [VMEM] + [ANY], (z3, a1))
         a3 = send(z3, perm_a)
         table = jnp.concatenate([table, send(table, perm_z[2])])
-        z3 = gate(z3, b1, c0, table)
+        z2 = send(gate(z1, table), perm_f)
+        z3 = gate(z3, b1, c0)
         b3 = send(z3, perm_b)
-        z2 = send(gate(z1, z3), perm_f)
         acc, side, token_ids = call(
             begin_kernel,
             [acc_shape, side_shape, ids_shape],

time: 124 us -> 115 us (0.927)
  starting transfers between devices: 53.8 us -> 39.2 us
  waiting for transfers between devices: 48 us -> 53.3 us
    ppermute x24, starting transfers between devices: 52.5 us -> 37.9 us  [per_device(): send = lambda value, perm: lax.ppermute(value, AXES, perm)]
    ppermute x24, waiting for transfers between devices: 46.8 us -> 52.1 us  [per_device(): send = lambda value, perm: lax.ppermute(value, AXES, perm)]
where the time goes in v13:
time: 115 us; the launch traced here: 114 us
  waiting for transfers between devices  53.3 us (46%)
  starting transfers between devices  39.2 us (34%)
  Pallas kernels  16.4 us (14%)
  local copies, waits for them, and re-layouts  4.3 us (4%)
    ppermute x24, waiting for transfers between devices, per_device(): send = lambda value, perm: lax.ppermute(value, AXES, perm)  52.1 us
    ppermute x24, starting transfers between devices, per_device(): send = lambda value, perm: lax.ppermute(value, AXES, perm)  37.9 us
    pallas_call x15, Pallas kernels, call(): pl.pallas_call(body, out_shape=outs, in_specs=in_specs, out_specs=[VMEM]...  16.4 us
  transfers between devices with their start and end apart: 28, of which 14 were waited for; matrix products, arithmetic and copies ran while one was open for 2% of the time, Pallas kernels for 10%

profile of v13, /device:TPU:0, one launch (start us, length us, event | category | flops | bytes accessed | tf_op | source)
XLA Modules:
  0.0 114.2 jit_solution(13677567919807383133)
XLA Ops:
  0.6 0.5 collective-permute-start
  1.2 1.0 slice_bitcast_fusion
  2.3 0.7 collective-permute-start.2
  2.9 0.7 broadcast_in_dim.17.gain
  3.6 0.7 broadcast_in_dim.18.reward
  4.3 1.1 copy-done.1
  5.5 3.0 %collective-permute-start.3 = (f32[2,1024]{1,0:T(2,128)S(1)}, f32[2,1024]{1,0:T(2,128)S(1)}, u32[]{:S(2)}, u32[]{:S(2)}) collective-permute-start(f32[2,1024]{1,0:T(2,128)S(1)} %get-tuple-element.21), channel_id=1, source_target_pairs={{0,1},{1,0},{2,3},{3,2},{4,5},{5,4},{6,7},{7,6},{8,9},{9,8},{10,11... | collective-permute-start | bytes 24584 | tf_op jit(solution)/shard_map/ppermute | solution.py:313
  8.5 1.6 %collective-permute-done.3 = f32[2,1024]{1,0:T(2,128)S(1)} collective-permute-done((f32[2,1024]{1,0:T(2,128)S(1)}, f32[2,1024]{1,0:T(2,128)S(1)}, u32[]{:S(2)}, u32[]{:S(2)}) %collective-permute-start.3) | collective-permute-done | bytes 8224 | tf_op jit(solution)/shard_map/ppermute | solution.py:313
  10.2 0.6 copy-done.3
  10.8 1.6 %shard_map.78 = (bf16[288,1024]{1,0:T(8,128)(2,1)S(1)}, f32[4,1024]{1,0:T(4,128)S(1)}) custom-call(s32[4]{0:T(128)S(1)} %copy-done.3, bf16[384,1024]{1,0:T(8,128)(2,1)S(1)} %get-tuple-element.20.rows, bf16[384,1024]{1,0:T(8,128)(2,1)S(1)} %collective-permute-done.1.sibling, bf16[192,1024]{1,0:T(8,128)(2,1)S(1)} %collective-permute-done.2.extra, ...), custom_call_target="tpu_custom_call" | custom-call | tf_op jit(solution)/shard_map/pallas_call | solution.py:281
  12.4 2.2 %collective-permute-start.9 = (bf16[288,1024]{1,0:T(8,128)(2,1)S(1)}, bf16[288,1024]{1,0:T(8,128)(2,1)S(1)}, u32[]{:S(2)}, u32[]{:S(2)}) collective-permute-start(bf16[288,1024]{1,0:T(8,128)(2,1)S(1)} %get-tuple-element.23.value.z), channel_id=1, source_target_pairs={{0,2},{1,3},{2,0},{3,1},{4,6},{5,7},{6,4},{7,5},{8,14},{9,15},{10,... | collective-permute-start | bytes 1769480 | tf_op jit(solution)/shard_map/ppermute | solution.py:313
  14.6 1.5 %collective-permute-start.7 = (bf16[288,1024]{1,0:T(8,128)(2,1)S(1)}, bf16[288,1024]{1,0:T(8,128)(2,1)S(1)}, u32[]{:S(2)}, u32[]{:S(2)}) collective-permute-start(bf16[288,1024]{1,0:T(8,128)(2,1)S(1)} %get-tuple-element.23.value.z), channel_id=1, source_target_pairs={{0,16},{1,17},{2,18},{3,19},{4,20},{5,21},{6,22},{7,23},{8,9},{9,8... | collective-permute-start | bytes 1769480 | tf_op jit(solution)/shard_map/ppermute | solution.py:313
  16.6 1.2 %shard_map.79 = (s32[576,1]{1,0:T(8,128)S(1)}, f32[2,640,384]{2,1,0:T(8,128)S(1)}, f32[8,128]{1,0:T(8,128)S(1)}) custom-call(s32[4]{0:T(128)S(1)} %copy-done.3, s32[4,384]{1,0:T(4,128)S(1)} %copy-done.2), custom_call_target="tpu_custom_call" | custom-call | tf_op jit(solution)/shard_map/pallas_call | solution.py:281
  17.8 1.6 %collective-permute-start.6 = (bf16[288,1024]{1,0:T(8,128)(2,1)S(1)}, bf16[288,1024]{1,0:T(8,128)(2,1)S(1)}, u32[]{:S(2)}, u32[]{:S(2)}) collective-permute-start(bf16[288,1024]{1,0:T(8,128)(2,1)S(1)} %get-tuple-element.23.value.z), channel_id=1, source_target_pairs={{0,1},{1,0},{2,3},{3,2},{4,5},{5,4},{6,7},{7,6},{8,24},{9,25},{10,... | collective-permute-start | bytes 1769480 | tf_op jit(solution)/shard_map/ppermute | solution.py:313
  19.3 7.0 %collective-permute-done.9.value.after = bf16[288,1024]{1,0:T(8,128)(2,1)S(1)} collective-permute-done((bf16[288,1024]{1,0:T(8,128)(2,1)S(1)}, bf16[288,1024]{1,0:T(8,128)(2,1)S(1)}, u32[]{:S(2)}, u32[]{:S(2)}) %collective-permute-start.9) | collective-permute-done | bytes 589856 | tf_op jit(solution)/shard_map/ppermute | solution.py:313
  26.3 6.8 %collective-permute-start.12 = (bf16[304,1024]{1,0:T(8,128)(2,1)S(1)}, bf16[304,1024]{1,0:T(8,128)(2,1)S(1)}, u32[]{:S(2)}, u32[]{:S(2)}) collective-permute-start(bf16[304,1024]{1,0:T(8,128)(2,1)S(1)} %shard_map.81), channel_id=1, source_target_pairs={{0,6},{1,7},{2,4},{3,5},{4,2},{5,3},{6,0},{7,1},{8,10},{9,11},{10,... | collective-permute-start | bytes 1867784 | tf_op jit(solution)/shard_map/ppermute | solution.py:313
  33.2 1.6 %collective-permute-start.10 = (bf16[288,1024]{1,0:T(8,128)(2,1)S(1)}, bf16[288,1024]{1,0:T(8,128)(2,1)S(1)}, u32[]{:S(2)}, u32[]{:S(2)}) collective-permute-start(bf16[288,1024]{1,0:T(8,128)(2,1)S(1)} %shard_map.80.z1.value), channel_id=1, source_target_pairs={{0,1},{1,0},{2,3},{3,2},{4,5},{5,4},{6,7},{7,6},{8,24},{9,25},{10,... | collective-permute-start | bytes 1769480 | tf_op jit(solution)/shard_map/ppermute | solution.py:313
  34.8 1.5 %collective-permute-start.11 = (bf16[288,1024]{1,0:T(8,128)(2,1)S(1)}, bf16[288,1024]{1,0:T(8,128)(2,1)S(1)}, u32[]{:S(2)}, u32[]{:S(2)}) collective-permute-start(bf16[288,1024]{1,0:T(8,128)(2,1)S(1)} %shard_map.80.z1.value), channel_id=1, source_target_pairs={{0,16},{1,17},{2,18},{3,19},{4,20},{5,21},{6,22},{7,23},{8,9},{9,8... | collective-permute-start | bytes 1769480 | tf_op jit(solution)/shard_map/ppermute | solution.py:313
  36.3 0.5 collective-permute-start.8
  36.8 12.7 %collective-permute-done.10.refs_0_.a1 = bf16[288,1024]{1,0:T(8,128)(2,1)S(1)} collective-permute-done((bf16[288,1024]{1,0:T(8,128)(2,1)S(1)}, bf16[288,1024]{1,0:T(8,128)(2,1)S(1)}, u32[]{:S(2)}, u32[]{:S(2)}) %collective-permute-start.10) | collective-permute-done | bytes 589856 | tf_op jit(solution)/shard_map/ppermute | solution.py:313
  49.5 1.4 %collective-permute-start.13 = (bf16[288,1024]{1,0:T(8,128)(2,1)S(1)}, bf16[288,1024]{1,0:T(8,128)(2,1)S(1)}, u32[]{:S(2)}, u32[]{:S(2)}) collective-permute-start(bf16[288,1024]{1,0:T(8,128)(2,1)S(1)} %shard_map.82.value), channel_id=1, source_target_pairs={{0,1},{1,0},{2,3},{3,2},{4,5},{5,4},{6,7},{7,6},{8,24},{9,25},{10,... | collective-permute-start | bytes 1769480 | tf_op jit(solution)/shard_map/ppermute | solution.py:313
  51.0 0.6 collective-permute-start.16
  51.6 5.7 %collective-permute-done.8.refs_1_.c = bf16[288,1024]{1,0:T(8,128)(2,1)S(1)} collective-permute-done((bf16[288,1024]{1,0:T(8,128)(2,1)S(1)}, bf16[288,1024]{1,0:T(8,128)(2,1)S(1)}, u32[]{:S(2)}, u32[]{:S(2)}) %collective-permute-start.8) | collective-permute-done | bytes 589856 | tf_op jit(solution)/shard_map/ppermute | solution.py:313
  57.3 1.7 %collective-permute-start.14 = (bf16[288,1024]{1,0:T(8,128)(2,1)S(1)}, bf16[288,1024]{1,0:T(8,128)(2,1)S(1)}, u32[]{:S(2)}, u32[]{:S(2)}) collective-permute-start(bf16[288,1024]{1,0:T(8,128)(2,1)S(1)} %shard_map.83.after.z), channel_id=1, source_target_pairs={{0,16},{1,17},{2,18},{3,19},{4,20},{5,21},{6,22},{7,23},{8,9},{9,8... | collective-permute-start | bytes 1769480 | tf_op jit(solution)/shard_map/ppermute | solution.py:313
  59.0 4.5 %shard_map.84 = (f32[576,512]{1,0:T(8,128)S(1)}, f32[576,256]{1,0:T(8,128)S(1)}, s32[576,1]{1,0:T(8,128)S(1)}) custom-call(bf16[8192,256]{1,0:T(8,128)(2,1)S(1)} %copy-done, bf16[8192,256]{1,0:T(8,128)(2,1)S(1)} %collective-permute-done.after.sibling, f32[16,1024]{1,0:T(8,128)S(1)} %pad_maximum_fusion.table.refs_0_, ...), custom_call_target="tpu_custom_call" | custom-call | tf_op jit(solution)/shard_map/pallas_call | solution.py:281
  63.6 1.0 collective-permute-start.15
  65.0 1.5 %collective-permute-start.17 = (bf16[288,1024]{1,0:T(8,128)(2,1)S(1)}, bf16[288,1024]{1,0:T(8,128)(2,1)S(1)}, u32[]{:S(2)}, u32[]{:S(2)}) collective-permute-start(bf16[288,1024]{1,0:T(8,128)(2,1)S(1)} %collective-permute-done.16.z), channel_id=1, source_target_pairs={{0,1},{1,0},{2,3},{3,2},{4,5},{5,4},{6,7},{7,6},{8,24},{9,25},{10,... | collective-permute-start | bytes 1769480 | tf_op jit(solution)/shard_map/ppermute | solution.py:313
  66.5 1.8 %collective-permute-start.18 = (bf16[288,1024]{1,0:T(8,128)(2,1)S(1)}, bf16[288,1024]{1,0:T(8,128)(2,1)S(1)}, u32[]{:S(2)}, u32[]{:S(2)}) collective-permute-start(bf16[288,1024]{1,0:T(8,128)(2,1)S(1)} %collective-permute-done.16.z), channel_id=1, source_target_pairs={{0,16},{1,17},{2,18},{3,19},{4,20},{5,21},{6,22},{7,23},{8,9},{9,8... | collective-permute-start | bytes 1769480 | tf_op jit(solution)/shard_map/ppermute | solution.py:313
  68.2 0.8 collective-permute-start.19
  69.1 10.7 %collective-permute-done.15.c = bf16[288,1024]{1,0:T(8,128)(2,1)S(1)} collective-permute-done((bf16[288,1024]{1,0:T(8,128)(2,1)S(1)}, bf16[288,1024]{1,0:T(8,128)(2,1)S(1)}, u32[]{:S(2)}, u32[]{:S(2)}) %collective-permute-start.15) | collective-permute-done | bytes 589856 | tf_op jit(solution)/shard_map/ppermute | solution.py:313
  79.8 2.7 %shard_map.86 = (f32[576,512]{1,0:T(8,128)S(1)}, f32[576,256]{1,0:T(8,128)S(1)}) custom-call(bf16[8192,256]{1,0:T(8,128)(2,1)S(1)} %copy-done, bf16[8192,256]{1,0:T(8,128)(2,1)S(1)} %collective-permute-done.after.sibling, f32[16,1024]{1,0:T(8,128)S(1)} %pad_maximum_fusion.table.refs_0_, f32[576,512]{1,0:T(8,128)S(1)} %get-tuple-element.25.acc_in, ...), custom_call_target="tpu_custom_call" | custom-call | tf_op jit(solution)/shard_map/pallas_call | solution.py:281
  82.5 1.9 %collective-permute-start.20 = (bf16[288,1024]{1,0:T(8,128)(2,1)S(1)}, bf16[288,1024]{1,0:T(8,128)(2,1)S(1)}, u32[]{:S(2)}, u32[]{:S(2)}) collective-permute-start(bf16[288,1024]{1,0:T(8,128)(2,1)S(1)} %shard_map.88.a), channel_id=1, source_target_pairs={{0,16},{1,17},{2,18},{3,19},{4,20},{5,21},{6,22},{7,23},{8,9},{9,8... | collective-permute-start | bytes 1769480 | tf_op jit(solution)/shard_map/ppermute | solution.py:313
  84.4 1.8 %collective-permute-done.18.b = bf16[288,1024]{1,0:T(8,128)(2,1)S(1)} collective-permute-done((bf16[288,1024]{1,0:T(8,128)(2,1)S(1)}, bf16[288,1024]{1,0:T(8,128)(2,1)S(1)}, u32[]{:S(2)}, u32[]{:S(2)}) %collective-permute-start.18) | collective-permute-done | bytes 589856 | tf_op jit(solution)/shard_map/ppermute | solution.py:313
  86.2 3.2 %shard_map.89 = (f32[288,512]{1,0:T(8,128)S(1)}, f32[288,256]{1,0:T(8,128)S(1)}, bf16[1024,512]{1,0:T(8,128)(2,1)S(1)}, f32[640,128]{1,0:T(8,128)S(1)}) custom-call(bf16[8192,256]{1,0:T(8,128)(2,1)S(1)} %copy-done, bf16[8192,256]{1,0:T(8,128)(2,1)S(1)} %collective-permute-done.after.sibling, f32[16,1024]{1,0:T(8,128)S(1)} %pad_maximum_fusion.table.refs_0_, ...), custom_call_target="tpu_custom_call" | custom-call | tf_op jit(solution)/shard_map/pallas_call | solution.py:281
  89.4 3.1 %collective-permute-done.20.c = bf16[288,1024]{1,0:T(8,128)(2,1)S(1)} collective-permute-done((bf16[288,1024]{1,0:T(8,128)(2,1)S(1)}, bf16[288,1024]{1,0:T(8,128)(2,1)S(1)}, u32[]{:S(2)}, u32[]{:S(2)}) %collective-permute-start.20) | collective-permute-done | bytes 589856 | tf_op jit(solution)/shard_map/ppermute | solution.py:313
  92.5 1.4 %shard_map.90 = f32[8,640]{1,0:T(8,128)S(1)} custom-call(bf16[1024,512]{1,0:T(8,128)(2,1)S(1)} %get-tuple-element.30.far_weights, f32[16,1024]{1,0:T(8,128)S(1)} %pad_maximum_fusion.table.refs_0_, f32[288,512]{1,0:T(8,128)S(1)} %get-tuple-element.31.left, f32[288,256]{1,0:T(8,128)S(1)} %get-tuple-element.32.left_side, ...), custom_call_target="tpu_custom_call" | custom-call | tf_op jit(solution)/shard_map/pallas_call | solution.py:281
  93.9 2.1 %collective-permute-start.21 = (f32[8,640]{1,0:T(8,128)S(1)}, f32[8,640]{1,0:T(8,128)S(1)}, u32[]{:S(2)}, u32[]{:S(2)}) collective-permute-start(f32[8,640]{1,0:T(8,128)S(1)} %shard_map.90), channel_id=1, source_target_pairs={{0,2},{1,3},{2,0},{3,1},{4,6},{5,7},{6,4},{7,5},{8,10},{9,11},{10,... | collective-permute-start | bytes 61448 | tf_op jit(solution)/shard_map/ppermute | solution.py:313
  96.1 1.9 %collective-permute-start.22 = (f32[8,640]{1,0:T(8,128)S(1)}, f32[8,640]{1,0:T(8,128)S(1)}, u32[]{:S(2)}, u32[]{:S(2)}) collective-permute-start(f32[8,640]{1,0:T(8,128)S(1)} %shard_map.90), channel_id=1, source_target_pairs={{0,4},{1,5},{2,6},{3,7},{4,0},{5,1},{6,2},{7,3},{8,12},{9,13},{10,... | collective-permute-start | bytes 61448 | tf_op jit(solution)/shard_map/ppermute | solution.py:313
  97.9 0.6 collective-permute-start.23
  98.5 2.2 %collective-permute-done.22 = f32[8,640]{1,0:T(8,128)S(1)} collective-permute-done((f32[8,640]{1,0:T(8,128)S(1)}, f32[8,640]{1,0:T(8,128)S(1)}, u32[]{:S(2)}, u32[]{:S(2)}) %collective-permute-start.22) | collective-permute-done | bytes 20512 | tf_op jit(solution)/shard_map/ppermute | solution.py:313
  100.7 2.8 %collective-permute-done.23 = f32[8,640]{1,0:T(8,128)S(1)} collective-permute-done((f32[8,640]{1,0:T(8,128)S(1)}, f32[8,640]{1,0:T(8,128)S(1)}, u32[]{:S(2)}, u32[]{:S(2)}) %collective-permute-start.23) | collective-permute-done | bytes 20512 | tf_op jit(solution)/shard_map/ppermute | solution.py:313
  103.6 1.6 %collective-permute-start.24 = (f32[8,640]{1,0:T(8,128)S(1)}, f32[8,640]{1,0:T(8,128)S(1)}, u32[]{:S(2)}, u32[]{:S(2)}) collective-permute-start(f32[8,640]{1,0:T(8,128)S(1)} %concatenate.19), channel_id=1, source_target_pairs={{0,1},{1,0},{2,3},{3,2},{4,5},{5,4},{6,7},{7,6},{8,9},{9,8},{10,11... | collective-permute-start | bytes 61448 | tf_op jit(solution)/shard_map/ppermute | solution.py:313
  105.1 1.5 %collective-permute-start.25 = (f32[8,640]{1,0:T(8,128)S(1)}, f32[8,640]{1,0:T(8,128)S(1)}, u32[]{:S(2)}, u32[]{:S(2)}) collective-permute-start(f32[8,640]{1,0:T(8,128)S(1)} %concatenate.19), channel_id=1, source_target_pairs={{0,16},{1,17},{2,18},{3,19},{4,20},{5,21},{6,22},{7,23},{8,24},{9,... | collective-permute-start | bytes 61448 | tf_op jit(solution)/shard_map/ppermute | solution.py:313
  106.7 0.5 collective-permute-start.26
  107.4 1.5 %collective-permute-done.25 = f32[8,640]{1,0:T(8,128)S(1)} collective-permute-done((f32[8,640]{1,0:T(8,128)S(1)}, f32[8,640]{1,0:T(8,128)S(1)}, u32[]{:S(2)}, u32[]{:S(2)}) %collective-permute-start.25) | collective-permute-done | bytes 20512 | tf_op jit(solution)/shard_map/ppermute | solution.py:313
  108.9 2.4 %collective-permute-done.26 = f32[8,640]{1,0:T(8,128)S(1)} collective-permute-done((f32[8,640]{1,0:T(8,128)S(1)}, f32[8,640]{1,0:T(8,128)S(1)}, u32[]{:S(2)}, u32[]{:S(2)}) %collective-permute-start.26) | collective-permute-done | bytes 20512 | tf_op jit(solution)/shard_map/ppermute | solution.py:313
  111.5 1.2 %collective-permute-done.27.sibling = f32[8,640]{1,0:T(8,128)S(1)} collective-permute-done((f32[8,640]{1,0:T(8,128)S(1)}, f32[8,640]{1,0:T(8,128)S(1)}, u32[]{:S(2)}, u32[]{:S(2)}) %collective-permute-start.27) | collective-permute-done | bytes 20512 | tf_op jit(solution)/shard_map/ppermute | solution.py:442
  112.7 1.6 %shard_map.91 = (f32[1,384]{1,0:T(1,128)}, f32[1,1]{1,0:T(1,128)}) custom-call(f32[8,640]{1,0:T(8,128)S(1)} %maximum_maximum_fusion.mine, f32[8,640]{1,0:T(8,128)S(1)} %collective-permute-done.27.sibling, f32[2,640,384]{2,1,0:T(8,128)S(1)} %get-tuple-element.34.hit, f32[8,128]{1,0:T(8,128)S(1)} %get-tuple-element.35.per_row), custom_call_target="tpu_custom_call" | custom-call | tf_op jit(solution)/shard_map/pallas_call | solution.py:281
  (44 shorter events, 1.8 us)
Async XLA Ops:
  0.6 9.5 %collective-permute-start = (bf16[8192,256]{1,0:T(8,128)(2,1)}, bf16[8192,256]{1,0:T(8,128)(2,1)S(1)}, u32[]{:S(2)}, u32[]{:S(2)}) collective-permute-start(bf16[8192,256]{1,0:T(8,128)(2,1)} %head.5), channel_id=1, source_target_pairs={{0,8},{8,0},{16,24},{24,16},{1,9},{9,1},{17,25},{25,17},{2,10},{10... | collective-permute-start | bytes 12582920 | tf_op jit(solution)/shard_map/ppermute | solution.py:326
  1.1 9.0 %collective-permute-start.1 = (bf16[384,1024]{1,0:T(8,128)(2,1)}, bf16[384,1024]{1,0:T(8,128)(2,1)S(1)}, u32[]{:S(2)}, u32[]{:S(2)}) collective-permute-start(bf16[384,1024]{1,0:T(8,128)(2,1)} %bitcast.4), channel_id=1, source_target_pairs={{0,8},{8,0},{16,24},{24,16},{1,9},{9,1},{17,25},{25,17},{2,10},{10... | collective-permute-start | bytes 2359304 | tf_op jit(solution)/shard_map/ppermute | solution.py:325
  2.3 7.9 %collective-permute-start.2 = (bf16[192,1024]{1,0:T(8,128)(2,1)S(1)}, bf16[192,1024]{1,0:T(8,128)(2,1)S(1)}, u32[]{:S(2)}, u32[]{:S(2)}) collective-permute-start(bf16[192,1024]{1,0:T(8,128)(2,1)S(1)} %slice_bitcast_fusion), channel_id=1, source_target_pairs={{8,24},{24,8},{9,25},{25,9},{10,26},{26,10},{11,27},{27,11},{12,28... | collective-permute-start | bytes 1179656 | tf_op jit(solution)/shard_map/ppermute | solution.py:324
  4.3 1.1 copy-start.1
  5.5 4.6 %collective-permute-start.3 = (f32[2,1024]{1,0:T(2,128)S(1)}, f32[2,1024]{1,0:T(2,128)S(1)}, u32[]{:S(2)}, u32[]{:S(2)}) collective-permute-start(f32[2,1024]{1,0:T(2,128)S(1)} %get-tuple-element.21), channel_id=1, source_target_pairs={{0,1},{1,0},{2,3},{3,2},{4,5},{5,4},{6,7},{7,6},{8,9},{9,8},{10,11... | collective-permute-start | bytes 24584 | tf_op jit(solution)/shard_map/ppermute | solution.py:313
  10.2 0.7 copy-start.3
  10.8 5.7 %copy-start.2 = (s32[4,384]{1,0:T(4,128)S(1)}, s32[4,384]{1,0:T(4,128)}, u32[]{:S(2)}) copy-start(s32[4,384]{1,0:T(4,128)} %tokens.1) | copy-start | bytes 18436
  12.4 13.9 %collective-permute-start.9 = (bf16[288,1024]{1,0:T(8,128)(2,1)S(1)}, bf16[288,1024]{1,0:T(8,128)(2,1)S(1)}, u32[]{:S(2)}, u32[]{:S(2)}) collective-permute-start(bf16[288,1024]{1,0:T(8,128)(2,1)S(1)} %get-tuple-element.23.value.z), channel_id=1, source_target_pairs={{0,2},{1,3},{2,0},{3,1},{4,6},{5,7},{6,4},{7,5},{8,14},{9,15},{10,... | collective-permute-start | bytes 1769480 | tf_op jit(solution)/shard_map/ppermute | solution.py:313
  14.6 18.5 %collective-permute-start.7 = (bf16[288,1024]{1,0:T(8,128)(2,1)S(1)}, bf16[288,1024]{1,0:T(8,128)(2,1)S(1)}, u32[]{:S(2)}, u32[]{:S(2)}) collective-permute-start(bf16[288,1024]{1,0:T(8,128)(2,1)S(1)} %get-tuple-element.23.value.z), channel_id=1, source_target_pairs={{0,16},{1,17},{2,18},{3,19},{4,20},{5,21},{6,22},{7,23},{8,9},{9,8... | collective-permute-start | bytes 1769480 | tf_op jit(solution)/shard_map/ppermute | solution.py:313
  16.1 17.0 %collective-permute-start.4 = (f32[4,1024]{1,0:T(4,128)S(1)}, f32[4,1024]{1,0:T(4,128)S(1)}, u32[]{:S(2)}, u32[]{:S(2)}) collective-permute-start(f32[4,1024]{1,0:T(4,128)S(1)} %get-tuple-element.22), channel_id=1, source_target_pairs={{0,2},{1,3},{2,0},{3,1},{4,6},{5,7},{6,4},{7,5},{8,10},{9,11},{10,... | collective-permute-start | bytes 49160 | tf_op jit(solution)/shard_map/ppermute | solution.py:313
  17.8 18.5 %collective-permute-start.6 = (bf16[288,1024]{1,0:T(8,128)(2,1)S(1)}, bf16[288,1024]{1,0:T(8,128)(2,1)S(1)}, u32[]{:S(2)}, u32[]{:S(2)}) collective-permute-start(bf16[288,1024]{1,0:T(8,128)(2,1)S(1)} %get-tuple-element.23.value.z), channel_id=1, source_target_pairs={{0,1},{1,0},{2,3},{3,2},{4,5},{5,4},{6,7},{7,6},{8,24},{9,25},{10,... | collective-permute-start | bytes 1769480 | tf_op jit(solution)/shard_map/ppermute | solution.py:313
  26.3 23.1 %collective-permute-start.12 = (bf16[304,1024]{1,0:T(8,128)(2,1)S(1)}, bf16[304,1024]{1,0:T(8,128)(2,1)S(1)}, u32[]{:S(2)}, u32[]{:S(2)}) collective-permute-start(bf16[304,1024]{1,0:T(8,128)(2,1)S(1)} %shard_map.81), channel_id=1, source_target_pairs={{0,6},{1,7},{2,4},{3,5},{4,2},{5,3},{6,0},{7,1},{8,10},{9,11},{10,... | collective-permute-start | bytes 1867784 | tf_op jit(solution)/shard_map/ppermute | solution.py:313
  33.2 16.2 %collective-permute-start.10 = (bf16[288,1024]{1,0:T(8,128)(2,1)S(1)}, bf16[288,1024]{1,0:T(8,128)(2,1)S(1)}, u32[]{:S(2)}, u32[]{:S(2)}) collective-permute-start(bf16[288,1024]{1,0:T(8,128)(2,1)S(1)} %shard_map.80.z1.value), channel_id=1, source_target_pairs={{0,1},{1,0},{2,3},{3,2},{4,5},{5,4},{6,7},{7,6},{8,24},{9,25},{10,... | collective-permute-start | bytes 1769480 | tf_op jit(solution)/shard_map/ppermute | solution.py:313
  34.8 16.2 %collective-permute-start.5 = (f32[8,1024]{1,0:T(8,128)S(1)}, f32[8,1024]{1,0:T(8,128)S(1)}, u32[]{:S(2)}, u32[]{:S(2)}) collective-permute-start(f32[8,1024]{1,0:T(8,128)S(1)} %pad_maximum_fusion.1.refs_1_), channel_id=1, source_target_pairs={{0,4},{1,5},{2,6},{3,7},{4,0},{5,1},{6,2},{7,3},{8,12},{9,13},{10,... | collective-permute-start | bytes 98312 | tf_op jit(solution)/shard_map/ppermute | solution.py:313
  34.8 16.8 %collective-permute-start.11 = (bf16[288,1024]{1,0:T(8,128)(2,1)S(1)}, bf16[288,1024]{1,0:T(8,128)(2,1)S(1)}, u32[]{:S(2)}, u32[]{:S(2)}) collective-permute-start(bf16[288,1024]{1,0:T(8,128)(2,1)S(1)} %shard_map.80.z1.value), channel_id=1, source_target_pairs={{0,16},{1,17},{2,18},{3,19},{4,20},{5,21},{6,22},{7,23},{8,9},{9,8... | collective-permute-start | bytes 1769480 | tf_op jit(solution)/shard_map/ppermute | solution.py:313
  36.3 21.0 %collective-permute-start.8 = (bf16[288,1024]{1,0:T(8,128)(2,1)S(1)}, bf16[288,1024]{1,0:T(8,128)(2,1)S(1)}, u32[]{:S(2)}, u32[]{:S(2)}) collective-permute-start(bf16[288,1024]{1,0:T(8,128)(2,1)S(1)} %collective-permute-done.6.a), channel_id=1, source_target_pairs={{0,16},{1,17},{2,18},{3,19},{4,20},{5,21},{6,22},{7,23},{8,9},{9,8... | collective-permute-start | bytes 1769480 | tf_op jit(solution)/shard_map/ppermute | solution.py:313
  49.5 9.6 %copy-start = (bf16[8192,256]{1,0:T(8,128)(2,1)S(1)}, bf16[8192,256]{1,0:T(8,128)(2,1)}, u32[]{:S(2)}) copy-start(bf16[8192,256]{1,0:T(8,128)(2,1)} %head.5) | copy-start | bytes 12582916
  49.5 14.0 %collective-permute-start.13 = (bf16[288,1024]{1,0:T(8,128)(2,1)S(1)}, bf16[288,1024]{1,0:T(8,128)(2,1)S(1)}, u32[]{:S(2)}, u32[]{:S(2)}) collective-permute-start(bf16[288,1024]{1,0:T(8,128)(2,1)S(1)} %shard_map.82.value), channel_id=1, source_target_pairs={{0,1},{1,0},{2,3},{3,2},{4,5},{5,4},{6,7},{7,6},{8,24},{9,25},{10,... | collective-permute-start | bytes 1769480 | tf_op jit(solution)/shard_map/ppermute | solution.py:313
  51.0 14.0 %collective-permute-start.16 = (bf16[288,1024]{1,0:T(8,128)(2,1)S(1)}, bf16[288,1024]{1,0:T(8,128)(2,1)S(1)}, u32[]{:S(2)}, u32[]{:S(2)}) collective-permute-start(bf16[288,1024]{1,0:T(8,128)(2,1)S(1)} %shard_map.87), channel_id=1, source_target_pairs={{0,6},{1,7},{2,4},{3,5},{4,2},{5,3},{6,0},{7,1},{8,10},{9,11},{10,... | collective-permute-start | bytes 1769480 | tf_op jit(solution)/shard_map/ppermute | solution.py:313
  57.3 11.8 %collective-permute-start.14 = (bf16[288,1024]{1,0:T(8,128)(2,1)S(1)}, bf16[288,1024]{1,0:T(8,128)(2,1)S(1)}, u32[]{:S(2)}, u32[]{:S(2)}) collective-permute-start(bf16[288,1024]{1,0:T(8,128)(2,1)S(1)} %shard_map.83.after.z), channel_id=1, source_target_pairs={{0,16},{1,17},{2,18},{3,19},{4,20},{5,21},{6,22},{7,23},{8,9},{9,8... | collective-permute-start | bytes 1769480 | tf_op jit(solution)/shard_map/ppermute | solution.py:313
  63.6 16.2 %collective-permute-start.15 = (bf16[288,1024]{1,0:T(8,128)(2,1)S(1)}, bf16[288,1024]{1,0:T(8,128)(2,1)S(1)}, u32[]{:S(2)}, u32[]{:S(2)}) collective-permute-start(bf16[288,1024]{1,0:T(8,128)(2,1)S(1)} %shard_map.85.a), channel_id=1, source_target_pairs={{0,16},{1,17},{2,18},{3,19},{4,20},{5,21},{6,22},{7,23},{8,9},{9,8... | collective-permute-start | bytes 1769480 | tf_op jit(solution)/shard_map/ppermute | solution.py:313
  65.0 17.5 %collective-permute-start.17 = (bf16[288,1024]{1,0:T(8,128)(2,1)S(1)}, bf16[288,1024]{1,0:T(8,128)(2,1)S(1)}, u32[]{:S(2)}, u32[]{:S(2)}) collective-permute-start(bf16[288,1024]{1,0:T(8,128)(2,1)S(1)} %collective-permute-done.16.z), channel_id=1, source_target_pairs={{0,1},{1,0},{2,3},{3,2},{4,5},{5,4},{6,7},{7,6},{8,24},{9,25},{10,... | collective-permute-start | bytes 1769480 | tf_op jit(solution)/shard_map/ppermute | solution.py:313
  66.5 19.7 %collective-permute-start.18 = (bf16[288,1024]{1,0:T(8,128)(2,1)S(1)}, bf16[288,1024]{1,0:T(8,128)(2,1)S(1)}, u32[]{:S(2)}, u32[]{:S(2)}) collective-permute-start(bf16[288,1024]{1,0:T(8,128)(2,1)S(1)} %collective-permute-done.16.z), channel_id=1, source_target_pairs={{0,16},{1,17},{2,18},{3,19},{4,20},{5,21},{6,22},{7,23},{8,9},{9,8... | collective-permute-start | bytes 1769480 | tf_op jit(solution)/shard_map/ppermute | solution.py:313
  68.2 18.0 %collective-permute-start.19 = (bf16[288,1024]{1,0:T(8,128)(2,1)S(1)}, bf16[288,1024]{1,0:T(8,128)(2,1)S(1)}, u32[]{:S(2)}, u32[]{:S(2)}) collective-permute-start(bf16[288,1024]{1,0:T(8,128)(2,1)S(1)} %collective-permute-done.8.refs_1_.c), channel_id=1, source_target_pairs={{0,2},{1,3},{2,0},{3,1},{4,6},{5,7},{6,4},{7,5},{8,14},{9,15},{10,... | collective-permute-start | bytes 1769480 | tf_op jit(solution)/shard_map/ppermute | solution.py:313
  82.5 10.0 %collective-permute-start.20 = (bf16[288,1024]{1,0:T(8,128)(2,1)S(1)}, bf16[288,1024]{1,0:T(8,128)(2,1)S(1)}, u32[]{:S(2)}, u32[]{:S(2)}) collective-permute-start(bf16[288,1024]{1,0:T(8,128)(2,1)S(1)} %shard_map.88.a), channel_id=1, source_target_pairs={{0,16},{1,17},{2,18},{3,19},{4,20},{5,21},{6,22},{7,23},{8,9},{9,8... | collective-permute-start | bytes 1769480 | tf_op jit(solution)/shard_map/ppermute | solution.py:313
  93.9 4.6 %collective-permute-start.21 = (f32[8,640]{1,0:T(8,128)S(1)}, f32[8,640]{1,0:T(8,128)S(1)}, u32[]{:S(2)}, u32[]{:S(2)}) collective-permute-start(f32[8,640]{1,0:T(8,128)S(1)} %shard_map.90), channel_id=1, source_target_pairs={{0,2},{1,3},{2,0},{3,1},{4,6},{5,7},{6,4},{7,5},{8,10},{9,11},{10,... | collective-permute-start | bytes 61448 | tf_op jit(solution)/shard_map/ppermute | solution.py:313
  96.1 4.7 %collective-permute-start.22 = (f32[8,640]{1,0:T(8,128)S(1)}, f32[8,640]{1,0:T(8,128)S(1)}, u32[]{:S(2)}, u32[]{:S(2)}) collective-permute-start(f32[8,640]{1,0:T(8,128)S(1)} %shard_map.90), channel_id=1, source_target_pairs={{0,4},{1,5},{2,6},{3,7},{4,0},{5,1},{6,2},{7,3},{8,12},{9,13},{10,... | collective-permute-start | bytes 61448 | tf_op jit(solution)/shard_map/ppermute | solution.py:313
  97.9 5.6 %collective-permute-start.23 = (f32[8,640]{1,0:T(8,128)S(1)}, f32[8,640]{1,0:T(8,128)S(1)}, u32[]{:S(2)}, u32[]{:S(2)}) collective-permute-start(f32[8,640]{1,0:T(8,128)S(1)} %shard_map.90), channel_id=1, source_target_pairs={{0,6},{1,7},{2,4},{3,5},{4,2},{5,3},{6,0},{7,1},{8,14},{9,15},{10,... | collective-permute-start | bytes 61448 | tf_op jit(solution)/shard_map/ppermute | solution.py:313
  103.6 3.8 %collective-permute-start.24 = (f32[8,640]{1,0:T(8,128)S(1)}, f32[8,640]{1,0:T(8,128)S(1)}, u32[]{:S(2)}, u32[]{:S(2)}) collective-permute-start(f32[8,640]{1,0:T(8,128)S(1)} %concatenate.19), channel_id=1, source_target_pairs={{0,1},{1,0},{2,3},{3,2},{4,5},{5,4},{6,7},{7,6},{8,9},{9,8},{10,11... | collective-permute-start | bytes 61448 | tf_op jit(solution)/shard_map/ppermute | solution.py:313
  105.1 3.8 %collective-permute-start.25 = (f32[8,640]{1,0:T(8,128)S(1)}, f32[8,640]{1,0:T(8,128)S(1)}, u32[]{:S(2)}, u32[]{:S(2)}) collective-permute-start(f32[8,640]{1,0:T(8,128)S(1)} %concatenate.19), channel_id=1, source_target_pairs={{0,16},{1,17},{2,18},{3,19},{4,20},{5,21},{6,22},{7,23},{8,24},{9,... | collective-permute-start | bytes 61448 | tf_op jit(solution)/shard_map/ppermute | solution.py:313
  106.7 4.7 %collective-permute-start.26 = (f32[8,640]{1,0:T(8,128)S(1)}, f32[8,640]{1,0:T(8,128)S(1)}, u32[]{:S(2)}, u32[]{:S(2)}) collective-permute-start(f32[8,640]{1,0:T(8,128)S(1)} %concatenate.19), channel_id=1, source_target_pairs={{0,17},{1,16},{2,19},{3,18},{4,21},{5,20},{6,23},{7,22},{8,25},{9,... | collective-permute-start | bytes 61448 | tf_op jit(solution)/shard_map/ppermute | solution.py:313
  111.5 1.2 %collective-permute-start.27 = (f32[8,640]{1,0:T(8,128)S(1)}, f32[8,640]{1,0:T(8,128)S(1)}, u32[]{:S(2)}, u32[]{:S(2)}) collective-permute-start(f32[8,640]{1,0:T(8,128)S(1)} %maximum_maximum_fusion.mine), channel_id=1, source_target_pairs={{0,8},{8,0},{16,24},{24,16},{1,9},{9,1},{17,25},{25,17},{2,10},{10... | collective-permute-start | bytes 61448 | tf_op jit(solution)/shard_map/ppermute | solution.py:442

commit v14 on v13

--- a/solution.py
+++ b/solution.py
@@ -72,7 +72,7 @@
     spans, positions = tokens.shape
     index = lax.broadcasted_iota(I32, (count, 1), 0)
     lane = lax.broadcasted_iota(I32, (count, positions), 1)
-    hit[...] = jnp.zeros(hit.shape, F32)
+    hit[...] = jnp.zeros(hit.shape, BF16)
     for pair in range(2):
         rows = slice(pair * count, pair * count + count)
         span, place = row_map(lengths, pair, core, index, count)
@@ -82,9 +82,9 @@
         here_is = lane == place
         found = jnp.sum(jnp.where(here_is, found, F32(0.0)), axis=1, keepdims=True)
         out[rows, :] = found.astype(I32)
-        hit[0, rows, :] = jnp.where(here_is & (span == section), F32(1.0), F32(0.0))
+        hit[0, rows, :] = jnp.where(here_is & (span == section), F32(1.0), F32(0.0)).astype(BF16)
         span, place = row_map(lengths, pair, 1 - core, index, count)
-        hit[1, rows, :] = jnp.where((lane == place) & (span == section), F32(1.0), F32(0.0))
+        hit[1, rows, :] = jnp.where((lane == place) & (span == section), F32(1.0), F32(0.0)).astype(BF16)
     per_row[...] = jnp.zeros(per_row.shape, F32) + 1.0 / lengths[section].astype(F32)
 
 
@@ -261,8 +261,15 @@
 
 
 def final_kernel(mine, sibling, hit, per_row, out_ref, score_ref):
-    exact = functools.partial(jnp.dot, precision=lax.Precision.HIGHEST, preferred_element_type=F32)
-    picked = exact(mine[...], hit[0]) + exact(sibling[...], hit[1])
+    picked = jnp.zeros((8, hit.shape[2]), F32)
+    for core, values in enumerate((mine, sibling)):
+        rest, terms = values[0:2, :], []
+        for _ in range(3):
+            terms.append(rest.astype(BF16).astype(F32))
+            rest = rest - terms[-1]
+        stacked = jnp.concatenate(terms + [jnp.zeros_like(rest)], axis=0).astype(BF16)
+        picked += jnp.dot(stacked, hit[core], preferred_element_type=F32)
+    picked = picked[0:2, :] + (picked[2:4, :] + picked[4:6, :])
     out_ref[...] = picked[0:1, :]
     score_ref[...] = jnp.sum(picked[1:2, :], axis=1, keepdims=True) * per_row[0:1, 0:1]
 
@@ -340,7 +347,7 @@
         functools.partial(token_kernel, count),
         [
             ids_shape,
-            jax.ShapeDtypeStruct((2, up(2 * count), positions), F32),
+            jax.ShapeDtypeStruct((2, up(2 * count), positions), BF16),
             jax.ShapeDtypeStruct((8, LANES), F32),
         ],
         [SMEM, VMEM],

time: 115 us -> 114 us (level)
  transfers between devices with their start and end apart: 28 -> 28, of which waited for: 14 -> 14; matrix products, arithmetic and copies ran while one was open for 2% -> 2% of each run, Pallas kernels for 10% -> 11%
where the time goes in v14:
time: 114 us
  waiting for transfers between devices  53.3 us (47%)
  starting transfers between devices  39.1 us (34%)
  Pallas kernels  15.8 us (14%)
  local copies, waits for them, and re-layouts  4.3 us (4%)
    ppermute x24, waiting for transfers between devices, per_device(): send = lambda value, perm: lax.ppermute(value, AXES, perm)  52.1 us
    ppermute x24, starting transfers between devices, per_device(): send = lambda value, perm: lax.ppermute(value, AXES, perm)  37.8 us
    pallas_call x15, Pallas kernels, call(): pl.pallas_call(body, out_shape=outs, in_specs=in_specs, out_specs=[VMEM]...  15.8 us
  transfers between devices with their start and end apart: 28, of which 14 were waited for; matrix products, arithmetic and copies ran while one was open for 2% of the time, Pallas kernels for 11%

profile of v14, /device:TPU:0, one launch (start us, length us, event | category | flops | bytes accessed | tf_op | source)
XLA Modules:
  0.0 113.5 jit_solution(13789386687914846512)
XLA Ops:
  0.6 0.5 collective-permute-start
  1.2 1.0 slice_bitcast_fusion
  2.3 0.7 collective-permute-start.2
  3.0 0.7 broadcast_in_dim.17.gain
  3.6 0.7 broadcast_in_dim.18.reward
  4.3 1.1 copy-done.1
  5.5 3.0 %collective-permute-start.3 = (f32[2,1024]{1,0:T(2,128)S(1)}, f32[2,1024]{1,0:T(2,128)S(1)}, u32[]{:S(2)}, u32[]{:S(2)}) collective-permute-start(f32[2,1024]{1,0:T(2,128)S(1)} %get-tuple-element.21), channel_id=1, source_target_pairs={{0,1},{1,0},{2,3},{3,2},{4,5},{5,4},{6,7},{7,6},{8,9},{9,8},{10,11... | collective-permute-start | bytes 24584 | tf_op jit(solution)/shard_map/ppermute | solution.py:320
  8.5 1.6 %collective-permute-done.3 = f32[2,1024]{1,0:T(2,128)S(1)} collective-permute-done((f32[2,1024]{1,0:T(2,128)S(1)}, f32[2,1024]{1,0:T(2,128)S(1)}, u32[]{:S(2)}, u32[]{:S(2)}) %collective-permute-start.3) | collective-permute-done | bytes 8224 | tf_op jit(solution)/shard_map/ppermute | solution.py:320
  10.2 0.6 copy-done.3
  10.8 1.6 %shard_map.78 = (bf16[288,1024]{1,0:T(8,128)(2,1)S(1)}, f32[4,1024]{1,0:T(4,128)S(1)}) custom-call(s32[4]{0:T(128)S(1)} %copy-done.3, bf16[384,1024]{1,0:T(8,128)(2,1)S(1)} %get-tuple-element.20.rows, bf16[384,1024]{1,0:T(8,128)(2,1)S(1)} %collective-permute-done.1.sibling, bf16[192,1024]{1,0:T(8,128)(2,1)S(1)} %collective-permute-done.2.extra, ...), custom_call_target="tpu_custom_call" | custom-call | tf_op jit(solution)/shard_map/pallas_call | solution.py:288
  12.4 2.2 %collective-permute-start.9 = (bf16[288,1024]{1,0:T(8,128)(2,1)S(1)}, bf16[288,1024]{1,0:T(8,128)(2,1)S(1)}, u32[]{:S(2)}, u32[]{:S(2)}) collective-permute-start(bf16[288,1024]{1,0:T(8,128)(2,1)S(1)} %get-tuple-element.23.value.z), channel_id=1, source_target_pairs={{0,2},{1,3},{2,0},{3,1},{4,6},{5,7},{6,4},{7,5},{8,14},{9,15},{10,... | collective-permute-start | bytes 1769480 | tf_op jit(solution)/shard_map/ppermute | solution.py:320
  14.6 1.5 %collective-permute-start.7 = (bf16[288,1024]{1,0:T(8,128)(2,1)S(1)}, bf16[288,1024]{1,0:T(8,128)(2,1)S(1)}, u32[]{:S(2)}, u32[]{:S(2)}) collective-permute-start(bf16[288,1024]{1,0:T(8,128)(2,1)S(1)} %get-tuple-element.23.value.z), channel_id=1, source_target_pairs={{0,16},{1,17},{2,18},{3,19},{4,20},{5,21},{6,22},{7,23},{8,9},{9,8... | collective-permute-start | bytes 1769480 | tf_op jit(solution)/shard_map/ppermute | solution.py:320
  16.6 1.3 %shard_map.79 = (s32[576,1]{1,0:T(8,128)S(1)}, bf16[2,640,384]{2,1,0:T(8,128)(2,1)S(1)}, f32[8,128]{1,0:T(8,128)S(1)}) custom-call(s32[4]{0:T(128)S(1)} %copy-done.3, s32[4,384]{1,0:T(4,128)S(1)} %copy-done.2), custom_call_target="tpu_custom_call" | custom-call | tf_op jit(solution)/shard_map/pallas_call | solution.py:288
  17.9 1.6 %collective-permute-start.6 = (bf16[288,1024]{1,0:T(8,128)(2,1)S(1)}, bf16[288,1024]{1,0:T(8,128)(2,1)S(1)}, u32[]{:S(2)}, u32[]{:S(2)}) collective-permute-start(bf16[288,1024]{1,0:T(8,128)(2,1)S(1)} %get-tuple-element.23.value.z), channel_id=1, source_target_pairs={{0,1},{1,0},{2,3},{3,2},{4,5},{5,4},{6,7},{7,6},{8,24},{9,25},{10,... | collective-permute-start | bytes 1769480 | tf_op jit(solution)/shard_map/ppermute | solution.py:320
  19.4 6.9 %collective-permute-done.9.value.after = bf16[288,1024]{1,0:T(8,128)(2,1)S(1)} collective-permute-done((bf16[288,1024]{1,0:T(8,128)(2,1)S(1)}, bf16[288,1024]{1,0:T(8,128)(2,1)S(1)}, u32[]{:S(2)}, u32[]{:S(2)}) %collective-permute-start.9) | collective-permute-done | bytes 589856 | tf_op jit(solution)/shard_map/ppermute | solution.py:320
  26.4 6.8 %collective-permute-start.12 = (bf16[304,1024]{1,0:T(8,128)(2,1)S(1)}, bf16[304,1024]{1,0:T(8,128)(2,1)S(1)}, u32[]{:S(2)}, u32[]{:S(2)}) collective-permute-start(bf16[304,1024]{1,0:T(8,128)(2,1)S(1)} %shard_map.81), channel_id=1, source_target_pairs={{0,6},{1,7},{2,4},{3,5},{4,2},{5,3},{6,0},{7,1},{8,10},{9,11},{10,... | collective-permute-start | bytes 1867784 | tf_op jit(solution)/shard_map/ppermute | solution.py:320
  33.2 1.6 %collective-permute-start.10 = (bf16[288,1024]{1,0:T(8,128)(2,1)S(1)}, bf16[288,1024]{1,0:T(8,128)(2,1)S(1)}, u32[]{:S(2)}, u32[]{:S(2)}) collective-permute-start(bf16[288,1024]{1,0:T(8,128)(2,1)S(1)} %shard_map.80.z1.value), channel_id=1, source_target_pairs={{0,1},{1,0},{2,3},{3,2},{4,5},{5,4},{6,7},{7,6},{8,24},{9,25},{10,... | collective-permute-start | bytes 1769480 | tf_op jit(solution)/shard_map/ppermute | solution.py:320
  34.8 1.5 %collective-permute-start.11 = (bf16[288,1024]{1,0:T(8,128)(2,1)S(1)}, bf16[288,1024]{1,0:T(8,128)(2,1)S(1)}, u32[]{:S(2)}, u32[]{:S(2)}) collective-permute-start(bf16[288,1024]{1,0:T(8,128)(2,1)S(1)} %shard_map.80.z1.value), channel_id=1, source_target_pairs={{0,16},{1,17},{2,18},{3,19},{4,20},{5,21},{6,22},{7,23},{8,9},{9,8... | collective-permute-start | bytes 1769480 | tf_op jit(solution)/shard_map/ppermute | solution.py:320
  36.3 0.5 collective-permute-start.8
  36.8 12.7 %collective-permute-done.10.refs_0_.a1 = bf16[288,1024]{1,0:T(8,128)(2,1)S(1)} collective-permute-done((bf16[288,1024]{1,0:T(8,128)(2,1)S(1)}, bf16[288,1024]{1,0:T(8,128)(2,1)S(1)}, u32[]{:S(2)}, u32[]{:S(2)}) %collective-permute-start.10) | collective-permute-done | bytes 589856 | tf_op jit(solution)/shard_map/ppermute | solution.py:320
  49.5 1.3 %collective-permute-start.13 = (bf16[288,1024]{1,0:T(8,128)(2,1)S(1)}, bf16[288,1024]{1,0:T(8,128)(2,1)S(1)}, u32[]{:S(2)}, u32[]{:S(2)}) collective-permute-start(bf16[288,1024]{1,0:T(8,128)(2,1)S(1)} %shard_map.82.value), channel_id=1, source_target_pairs={{0,1},{1,0},{2,3},{3,2},{4,5},{5,4},{6,7},{7,6},{8,24},{9,25},{10,... | collective-permute-start | bytes 1769480 | tf_op jit(solution)/shard_map/ppermute | solution.py:320
  50.9 0.7 collective-permute-start.16
  51.6 5.5 %collective-permute-done.8.refs_1_.c = bf16[288,1024]{1,0:T(8,128)(2,1)S(1)} collective-permute-done((bf16[288,1024]{1,0:T(8,128)(2,1)S(1)}, bf16[288,1024]{1,0:T(8,128)(2,1)S(1)}, u32[]{:S(2)}, u32[]{:S(2)}) %collective-permute-start.8) | collective-permute-done | bytes 589856 | tf_op jit(solution)/shard_map/ppermute | solution.py:320
  57.1 2.0 %collective-permute-start.14 = (bf16[288,1024]{1,0:T(8,128)(2,1)S(1)}, bf16[288,1024]{1,0:T(8,128)(2,1)S(1)}, u32[]{:S(2)}, u32[]{:S(2)}) collective-permute-start(bf16[288,1024]{1,0:T(8,128)(2,1)S(1)} %shard_map.83.after.z), channel_id=1, source_target_pairs={{0,16},{1,17},{2,18},{3,19},{4,20},{5,21},{6,22},{7,23},{8,9},{9,8... | collective-permute-start | bytes 1769480 | tf_op jit(solution)/shard_map/ppermute | solution.py:320
  59.2 4.5 %shard_map.84 = (f32[576,512]{1,0:T(8,128)S(1)}, f32[576,256]{1,0:T(8,128)S(1)}, s32[576,1]{1,0:T(8,128)S(1)}) custom-call(bf16[8192,256]{1,0:T(8,128)(2,1)S(1)} %copy-done, bf16[8192,256]{1,0:T(8,128)(2,1)S(1)} %collective-permute-done.after.sibling, f32[16,1024]{1,0:T(8,128)S(1)} %pad_maximum_fusion.table.refs_0_, ...), custom_call_target="tpu_custom_call" | custom-call | tf_op jit(solution)/shard_map/pallas_call | solution.py:288
  63.7 0.8 collective-permute-start.15
  64.5 0.5 collective-permute-done.16.z
  65.0 1.6 %collective-permute-start.17 = (bf16[288,1024]{1,0:T(8,128)(2,1)S(1)}, bf16[288,1024]{1,0:T(8,128)(2,1)S(1)}, u32[]{:S(2)}, u32[]{:S(2)}) collective-permute-start(bf16[288,1024]{1,0:T(8,128)(2,1)S(1)} %collective-permute-done.16.z), channel_id=1, source_target_pairs={{0,1},{1,0},{2,3},{3,2},{4,5},{5,4},{6,7},{7,6},{8,24},{9,25},{10,... | collective-permute-start | bytes 1769480 | tf_op jit(solution)/shard_map/ppermute | solution.py:320
  66.6 1.9 %collective-permute-start.18 = (bf16[288,1024]{1,0:T(8,128)(2,1)S(1)}, bf16[288,1024]{1,0:T(8,128)(2,1)S(1)}, u32[]{:S(2)}, u32[]{:S(2)}) collective-permute-start(bf16[288,1024]{1,0:T(8,128)(2,1)S(1)} %collective-permute-done.16.z), channel_id=1, source_target_pairs={{0,16},{1,17},{2,18},{3,19},{4,20},{5,21},{6,22},{7,23},{8,9},{9,8... | collective-permute-start | bytes 1769480 | tf_op jit(solution)/shard_map/ppermute | solution.py:320
  68.5 0.6 collective-permute-start.19
  69.1 10.9 %collective-permute-done.15.c = bf16[288,1024]{1,0:T(8,128)(2,1)S(1)} collective-permute-done((bf16[288,1024]{1,0:T(8,128)(2,1)S(1)}, bf16[288,1024]{1,0:T(8,128)(2,1)S(1)}, u32[]{:S(2)}, u32[]{:S(2)}) %collective-permute-start.15) | collective-permute-done | bytes 589856 | tf_op jit(solution)/shard_map/ppermute | solution.py:320
  79.9 2.7 %shard_map.86 = (f32[576,512]{1,0:T(8,128)S(1)}, f32[576,256]{1,0:T(8,128)S(1)}) custom-call(bf16[8192,256]{1,0:T(8,128)(2,1)S(1)} %copy-done, bf16[8192,256]{1,0:T(8,128)(2,1)S(1)} %collective-permute-done.after.sibling, f32[16,1024]{1,0:T(8,128)S(1)} %pad_maximum_fusion.table.refs_0_, f32[576,512]{1,0:T(8,128)S(1)} %get-tuple-element.25.acc_in, ...), custom_call_target="tpu_custom_call" | custom-call | tf_op jit(solution)/shard_map/pallas_call | solution.py:288
  82.7 1.8 %collective-permute-start.20 = (bf16[288,1024]{1,0:T(8,128)(2,1)S(1)}, bf16[288,1024]{1,0:T(8,128)(2,1)S(1)}, u32[]{:S(2)}, u32[]{:S(2)}) collective-permute-start(bf16[288,1024]{1,0:T(8,128)(2,1)S(1)} %shard_map.88.a), channel_id=1, source_target_pairs={{0,16},{1,17},{2,18},{3,19},{4,20},{5,21},{6,22},{7,23},{8,9},{9,8... | collective-permute-start | bytes 1769480 | tf_op jit(solution)/shard_map/ppermute | solution.py:320
  84.5 1.8 %collective-permute-done.18.b = bf16[288,1024]{1,0:T(8,128)(2,1)S(1)} collective-permute-done((bf16[288,1024]{1,0:T(8,128)(2,1)S(1)}, bf16[288,1024]{1,0:T(8,128)(2,1)S(1)}, u32[]{:S(2)}, u32[]{:S(2)}) %collective-permute-start.18) | collective-permute-done | bytes 589856 | tf_op jit(solution)/shard_map/ppermute | solution.py:320
  86.3 3.2 %shard_map.89 = (f32[288,512]{1,0:T(8,128)S(1)}, f32[288,256]{1,0:T(8,128)S(1)}, bf16[1024,512]{1,0:T(8,128)(2,1)S(1)}, f32[640,128]{1,0:T(8,128)S(1)}) custom-call(bf16[8192,256]{1,0:T(8,128)(2,1)S(1)} %copy-done, bf16[8192,256]{1,0:T(8,128)(2,1)S(1)} %collective-permute-done.after.sibling, f32[16,1024]{1,0:T(8,128)S(1)} %pad_maximum_fusion.table.refs_0_, ...), custom_call_target="tpu_custom_call" | custom-call | tf_op jit(solution)/shard_map/pallas_call | solution.py:288
  89.5 3.1 %collective-permute-done.20.c = bf16[288,1024]{1,0:T(8,128)(2,1)S(1)} collective-permute-done((bf16[288,1024]{1,0:T(8,128)(2,1)S(1)}, bf16[288,1024]{1,0:T(8,128)(2,1)S(1)}, u32[]{:S(2)}, u32[]{:S(2)}) %collective-permute-start.20) | collective-permute-done | bytes 589856 | tf_op jit(solution)/shard_map/ppermute | solution.py:320
  92.6 1.4 %shard_map.90 = f32[8,640]{1,0:T(8,128)S(1)} custom-call(bf16[1024,512]{1,0:T(8,128)(2,1)S(1)} %get-tuple-element.30.far_weights, f32[16,1024]{1,0:T(8,128)S(1)} %pad_maximum_fusion.table.refs_0_, f32[288,512]{1,0:T(8,128)S(1)} %get-tuple-element.31.left, f32[288,256]{1,0:T(8,128)S(1)} %get-tuple-element.32.left_side, ...), custom_call_target="tpu_custom_call" | custom-call | tf_op jit(solution)/shard_map/pallas_call | solution.py:288
  94.0 2.1 %collective-permute-start.21 = (f32[8,640]{1,0:T(8,128)S(1)}, f32[8,640]{1,0:T(8,128)S(1)}, u32[]{:S(2)}, u32[]{:S(2)}) collective-permute-start(f32[8,640]{1,0:T(8,128)S(1)} %shard_map.90), channel_id=1, source_target_pairs={{0,2},{1,3},{2,0},{3,1},{4,6},{5,7},{6,4},{7,5},{8,10},{9,11},{10,... | collective-permute-start | bytes 61448 | tf_op jit(solution)/shard_map/ppermute | solution.py:320
  96.1 1.9 %collective-permute-start.22 = (f32[8,640]{1,0:T(8,128)S(1)}, f32[8,640]{1,0:T(8,128)S(1)}, u32[]{:S(2)}, u32[]{:S(2)}) collective-permute-start(f32[8,640]{1,0:T(8,128)S(1)} %shard_map.90), channel_id=1, source_target_pairs={{0,4},{1,5},{2,6},{3,7},{4,0},{5,1},{6,2},{7,3},{8,12},{9,13},{10,... | collective-permute-start | bytes 61448 | tf_op jit(solution)/shard_map/ppermute | solution.py:320
  97.9 0.6 collective-permute-start.23
  98.5 2.2 %collective-permute-done.22 = f32[8,640]{1,0:T(8,128)S(1)} collective-permute-done((f32[8,640]{1,0:T(8,128)S(1)}, f32[8,640]{1,0:T(8,128)S(1)}, u32[]{:S(2)}, u32[]{:S(2)}) %collective-permute-start.22) | collective-permute-done | bytes 20512 | tf_op jit(solution)/shard_map/ppermute | solution.py:320
  100.8 2.8 %collective-permute-done.23 = f32[8,640]{1,0:T(8,128)S(1)} collective-permute-done((f32[8,640]{1,0:T(8,128)S(1)}, f32[8,640]{1,0:T(8,128)S(1)}, u32[]{:S(2)}, u32[]{:S(2)}) %collective-permute-start.23) | collective-permute-done | bytes 20512 | tf_op jit(solution)/shard_map/ppermute | solution.py:320
  103.6 1.6 %collective-permute-start.24 = (f32[8,640]{1,0:T(8,128)S(1)}, f32[8,640]{1,0:T(8,128)S(1)}, u32[]{:S(2)}, u32[]{:S(2)}) collective-permute-start(f32[8,640]{1,0:T(8,128)S(1)} %concatenate.19), channel_id=1, source_target_pairs={{0,1},{1,0},{2,3},{3,2},{4,5},{5,4},{6,7},{7,6},{8,9},{9,8},{10,11... | collective-permute-start | bytes 61448 | tf_op jit(solution)/shard_map/ppermute | solution.py:320
  105.2 1.5 %collective-permute-start.25 = (f32[8,640]{1,0:T(8,128)S(1)}, f32[8,640]{1,0:T(8,128)S(1)}, u32[]{:S(2)}, u32[]{:S(2)}) collective-permute-start(f32[8,640]{1,0:T(8,128)S(1)} %concatenate.19), channel_id=1, source_target_pairs={{0,16},{1,17},{2,18},{3,19},{4,20},{5,21},{6,22},{7,23},{8,24},{9,... | collective-permute-start | bytes 61448 | tf_op jit(solution)/shard_map/ppermute | solution.py:320
  107.4 1.5 %collective-permute-done.25 = f32[8,640]{1,0:T(8,128)S(1)} collective-permute-done((f32[8,640]{1,0:T(8,128)S(1)}, f32[8,640]{1,0:T(8,128)S(1)}, u32[]{:S(2)}, u32[]{:S(2)}) %collective-permute-start.25) | collective-permute-done | bytes 20512 | tf_op jit(solution)/shard_map/ppermute | solution.py:320
  108.9 2.4 %collective-permute-done.26 = f32[8,640]{1,0:T(8,128)S(1)} collective-permute-done((f32[8,640]{1,0:T(8,128)S(1)}, f32[8,640]{1,0:T(8,128)S(1)}, u32[]{:S(2)}, u32[]{:S(2)}) %collective-permute-start.26) | collective-permute-done | bytes 20512 | tf_op jit(solution)/shard_map/ppermute | solution.py:320
  111.5 1.2 %collective-permute-done.27.sibling = f32[8,640]{1,0:T(8,128)S(1)} collective-permute-done((f32[8,640]{1,0:T(8,128)S(1)}, f32[8,640]{1,0:T(8,128)S(1)}, u32[]{:S(2)}, u32[]{:S(2)}) %collective-permute-start.27) | collective-permute-done | bytes 20512 | tf_op jit(solution)/shard_map/ppermute | solution.py:449
  112.7 0.8 shard_map.91
  (44 shorter events, 1.9 us)
Async XLA Ops:
  0.6 16.0 %copy-start.2 = (s32[4,384]{1,0:T(4,128)S(1)}, s32[4,384]{1,0:T(4,128)}, u32[]{:S(2)}) copy-start(s32[4,384]{1,0:T(4,128)} %tokens.1) | copy-start | bytes 18436
  0.6 9.5 %collective-permute-start = (bf16[8192,256]{1,0:T(8,128)(2,1)}, bf16[8192,256]{1,0:T(8,128)(2,1)S(1)}, u32[]{:S(2)}, u32[]{:S(2)}) collective-permute-start(bf16[8192,256]{1,0:T(8,128)(2,1)} %head.5), channel_id=1, source_target_pairs={{0,8},{8,0},{16,24},{24,16},{1,9},{9,1},{17,25},{25,17},{2,10},{10... | collective-permute-start | bytes 12582920 | tf_op jit(solution)/shard_map/ppermute | solution.py:333
  1.2 9.0 %collective-permute-start.1 = (bf16[384,1024]{1,0:T(8,128)(2,1)}, bf16[384,1024]{1,0:T(8,128)(2,1)S(1)}, u32[]{:S(2)}, u32[]{:S(2)}) collective-permute-start(bf16[384,1024]{1,0:T(8,128)(2,1)} %bitcast.4), channel_id=1, source_target_pairs={{0,8},{8,0},{16,24},{24,16},{1,9},{9,1},{17,25},{25,17},{2,10},{10... | collective-permute-start | bytes 2359304 | tf_op jit(solution)/shard_map/ppermute | solution.py:332
  2.3 7.9 %collective-permute-start.2 = (bf16[192,1024]{1,0:T(8,128)(2,1)S(1)}, bf16[192,1024]{1,0:T(8,128)(2,1)S(1)}, u32[]{:S(2)}, u32[]{:S(2)}) collective-permute-start(bf16[192,1024]{1,0:T(8,128)(2,1)S(1)} %slice_bitcast_fusion), channel_id=1, source_target_pairs={{8,24},{24,8},{9,25},{25,9},{10,26},{26,10},{11,27},{27,11},{12,28... | collective-permute-start | bytes 1179656 | tf_op jit(solution)/shard_map/ppermute | solution.py:331
  4.3 1.1 copy-start.1
  5.5 4.6 %collective-permute-start.3 = (f32[2,1024]{1,0:T(2,128)S(1)}, f32[2,1024]{1,0:T(2,128)S(1)}, u32[]{:S(2)}, u32[]{:S(2)}) collective-permute-start(f32[2,1024]{1,0:T(2,128)S(1)} %get-tuple-element.21), channel_id=1, source_target_pairs={{0,1},{1,0},{2,3},{3,2},{4,5},{5,4},{6,7},{7,6},{8,9},{9,8},{10,11... | collective-permute-start | bytes 24584 | tf_op jit(solution)/shard_map/ppermute | solution.py:320
  10.2 0.7 copy-start.3
  12.4 13.9 %collective-permute-start.9 = (bf16[288,1024]{1,0:T(8,128)(2,1)S(1)}, bf16[288,1024]{1,0:T(8,128)(2,1)S(1)}, u32[]{:S(2)}, u32[]{:S(2)}) collective-permute-start(bf16[288,1024]{1,0:T(8,128)(2,1)S(1)} %get-tuple-element.23.value.z), channel_id=1, source_target_pairs={{0,2},{1,3},{2,0},{3,1},{4,6},{5,7},{6,4},{7,5},{8,14},{9,15},{10,... | collective-permute-start | bytes 1769480 | tf_op jit(solution)/shard_map/ppermute | solution.py:320
  14.6 18.6 %collective-permute-start.7 = (bf16[288,1024]{1,0:T(8,128)(2,1)S(1)}, bf16[288,1024]{1,0:T(8,128)(2,1)S(1)}, u32[]{:S(2)}, u32[]{:S(2)}) collective-permute-start(bf16[288,1024]{1,0:T(8,128)(2,1)S(1)} %get-tuple-element.23.value.z), channel_id=1, source_target_pairs={{0,16},{1,17},{2,18},{3,19},{4,20},{5,21},{6,22},{7,23},{8,9},{9,8... | collective-permute-start | bytes 1769480 | tf_op jit(solution)/shard_map/ppermute | solution.py:320
  16.1 17.0 %collective-permute-start.4 = (f32[4,1024]{1,0:T(4,128)S(1)}, f32[4,1024]{1,0:T(4,128)S(1)}, u32[]{:S(2)}, u32[]{:S(2)}) collective-permute-start(f32[4,1024]{1,0:T(4,128)S(1)} %get-tuple-element.22), channel_id=1, source_target_pairs={{0,2},{1,3},{2,0},{3,1},{4,6},{5,7},{6,4},{7,5},{8,10},{9,11},{10,... | collective-permute-start | bytes 49160 | tf_op jit(solution)/shard_map/ppermute | solution.py:320
  17.9 18.4 %collective-permute-start.6 = (bf16[288,1024]{1,0:T(8,128)(2,1)S(1)}, bf16[288,1024]{1,0:T(8,128)(2,1)S(1)}, u32[]{:S(2)}, u32[]{:S(2)}) collective-permute-start(bf16[288,1024]{1,0:T(8,128)(2,1)S(1)} %get-tuple-element.23.value.z), channel_id=1, source_target_pairs={{0,1},{1,0},{2,3},{3,2},{4,5},{5,4},{6,7},{7,6},{8,24},{9,25},{10,... | collective-permute-start | bytes 1769480 | tf_op jit(solution)/shard_map/ppermute | solution.py:320
  26.4 32.8 %copy-start = (bf16[8192,256]{1,0:T(8,128)(2,1)S(1)}, bf16[8192,256]{1,0:T(8,128)(2,1)}, u32[]{:S(2)}) copy-start(bf16[8192,256]{1,0:T(8,128)(2,1)} %head.5) | copy-start | bytes 12582916
  26.4 23.1 %collective-permute-start.12 = (bf16[304,1024]{1,0:T(8,128)(2,1)S(1)}, bf16[304,1024]{1,0:T(8,128)(2,1)S(1)}, u32[]{:S(2)}, u32[]{:S(2)}) collective-permute-start(bf16[304,1024]{1,0:T(8,128)(2,1)S(1)} %shard_map.81), channel_id=1, source_target_pairs={{0,6},{1,7},{2,4},{3,5},{4,2},{5,3},{6,0},{7,1},{8,10},{9,11},{10,... | collective-permute-start | bytes 1867784 | tf_op jit(solution)/shard_map/ppermute | solution.py:320
  33.2 16.2 %collective-permute-start.10 = (bf16[288,1024]{1,0:T(8,128)(2,1)S(1)}, bf16[288,1024]{1,0:T(8,128)(2,1)S(1)}, u32[]{:S(2)}, u32[]{:S(2)}) collective-permute-start(bf16[288,1024]{1,0:T(8,128)(2,1)S(1)} %shard_map.80.z1.value), channel_id=1, source_target_pairs={{0,1},{1,0},{2,3},{3,2},{4,5},{5,4},{6,7},{7,6},{8,24},{9,25},{10,... | collective-permute-start | bytes 1769480 | tf_op jit(solution)/shard_map/ppermute | solution.py:320
  34.8 16.1 %collective-permute-start.5 = (f32[8,1024]{1,0:T(8,128)S(1)}, f32[8,1024]{1,0:T(8,128)S(1)}, u32[]{:S(2)}, u32[]{:S(2)}) collective-permute-start(f32[8,1024]{1,0:T(8,128)S(1)} %pad_maximum_fusion.1.refs_1_), channel_id=1, source_target_pairs={{0,4},{1,5},{2,6},{3,7},{4,0},{5,1},{6,2},{7,3},{8,12},{9,13},{10,... | collective-permute-start | bytes 98312 | tf_op jit(solution)/shard_map/ppermute | solution.py:320
  34.8 16.8 %collective-permute-start.11 = (bf16[288,1024]{1,0:T(8,128)(2,1)S(1)}, bf16[288,1024]{1,0:T(8,128)(2,1)S(1)}, u32[]{:S(2)}, u32[]{:S(2)}) collective-permute-start(bf16[288,1024]{1,0:T(8,128)(2,1)S(1)} %shard_map.80.z1.value), channel_id=1, source_target_pairs={{0,16},{1,17},{2,18},{3,19},{4,20},{5,21},{6,22},{7,23},{8,9},{9,8... | collective-permute-start | bytes 1769480 | tf_op jit(solution)/shard_map/ppermute | solution.py:320
  36.3 20.8 %collective-permute-start.8 = (bf16[288,1024]{1,0:T(8,128)(2,1)S(1)}, bf16[288,1024]{1,0:T(8,128)(2,1)S(1)}, u32[]{:S(2)}, u32[]{:S(2)}) collective-permute-start(bf16[288,1024]{1,0:T(8,128)(2,1)S(1)} %collective-permute-done.6.a), channel_id=1, source_target_pairs={{0,16},{1,17},{2,18},{3,19},{4,20},{5,21},{6,22},{7,23},{8,9},{9,8... | collective-permute-start | bytes 1769480 | tf_op jit(solution)/shard_map/ppermute | solution.py:320
  49.5 14.1 %collective-permute-start.13 = (bf16[288,1024]{1,0:T(8,128)(2,1)S(1)}, bf16[288,1024]{1,0:T(8,128)(2,1)S(1)}, u32[]{:S(2)}, u32[]{:S(2)}) collective-permute-start(bf16[288,1024]{1,0:T(8,128)(2,1)S(1)} %shard_map.82.value), channel_id=1, source_target_pairs={{0,1},{1,0},{2,3},{3,2},{4,5},{5,4},{6,7},{7,6},{8,24},{9,25},{10,... | collective-permute-start | bytes 1769480 | tf_op jit(solution)/shard_map/ppermute | solution.py:320
  50.9 14.1 %collective-permute-start.16 = (bf16[288,1024]{1,0:T(8,128)(2,1)S(1)}, bf16[288,1024]{1,0:T(8,128)(2,1)S(1)}, u32[]{:S(2)}, u32[]{:S(2)}) collective-permute-start(bf16[288,1024]{1,0:T(8,128)(2,1)S(1)} %shard_map.87), channel_id=1, source_target_pairs={{0,6},{1,7},{2,4},{3,5},{4,2},{5,3},{6,0},{7,1},{8,10},{9,11},{10,... | collective-permute-start | bytes 1769480 | tf_op jit(solution)/shard_map/ppermute | solution.py:320
  57.1 11.9 %collective-permute-start.14 = (bf16[288,1024]{1,0:T(8,128)(2,1)S(1)}, bf16[288,1024]{1,0:T(8,128)(2,1)S(1)}, u32[]{:S(2)}, u32[]{:S(2)}) collective-permute-start(bf16[288,1024]{1,0:T(8,128)(2,1)S(1)} %shard_map.83.after.z), channel_id=1, source_target_pairs={{0,16},{1,17},{2,18},{3,19},{4,20},{5,21},{6,22},{7,23},{8,9},{9,8... | collective-permute-start | bytes 1769480 | tf_op jit(solution)/shard_map/ppermute | solution.py:320
  63.7 16.2 %collective-permute-start.15 = (bf16[288,1024]{1,0:T(8,128)(2,1)S(1)}, bf16[288,1024]{1,0:T(8,128)(2,1)S(1)}, u32[]{:S(2)}, u32[]{:S(2)}) collective-permute-start(bf16[288,1024]{1,0:T(8,128)(2,1)S(1)} %shard_map.85.a), channel_id=1, source_target_pairs={{0,16},{1,17},{2,18},{3,19},{4,20},{5,21},{6,22},{7,23},{8,9},{9,8... | collective-permute-start | bytes 1769480 | tf_op jit(solution)/shard_map/ppermute | solution.py:320
  65.0 17.6 %collective-permute-start.17 = (bf16[288,1024]{1,0:T(8,128)(2,1)S(1)}, bf16[288,1024]{1,0:T(8,128)(2,1)S(1)}, u32[]{:S(2)}, u32[]{:S(2)}) collective-permute-start(bf16[288,1024]{1,0:T(8,128)(2,1)S(1)} %collective-permute-done.16.z), channel_id=1, source_target_pairs={{0,1},{1,0},{2,3},{3,2},{4,5},{5,4},{6,7},{7,6},{8,24},{9,25},{10,... | collective-permute-start | bytes 1769480 | tf_op jit(solution)/shard_map/ppermute | solution.py:320
  66.6 19.7 %collective-permute-start.18 = (bf16[288,1024]{1,0:T(8,128)(2,1)S(1)}, bf16[288,1024]{1,0:T(8,128)(2,1)S(1)}, u32[]{:S(2)}, u32[]{:S(2)}) collective-permute-start(bf16[288,1024]{1,0:T(8,128)(2,1)S(1)} %collective-permute-done.16.z), channel_id=1, source_target_pairs={{0,16},{1,17},{2,18},{3,19},{4,20},{5,21},{6,22},{7,23},{8,9},{9,8... | collective-permute-start | bytes 1769480 | tf_op jit(solution)/shard_map/ppermute | solution.py:320
  68.5 17.8 %collective-permute-start.19 = (bf16[288,1024]{1,0:T(8,128)(2,1)S(1)}, bf16[288,1024]{1,0:T(8,128)(2,1)S(1)}, u32[]{:S(2)}, u32[]{:S(2)}) collective-permute-start(bf16[288,1024]{1,0:T(8,128)(2,1)S(1)} %collective-permute-done.8.refs_1_.c), channel_id=1, source_target_pairs={{0,2},{1,3},{2,0},{3,1},{4,6},{5,7},{6,4},{7,5},{8,14},{9,15},{10,... | collective-permute-start | bytes 1769480 | tf_op jit(solution)/shard_map/ppermute | solution.py:320
  82.7 9.9 %collective-permute-start.20 = (bf16[288,1024]{1,0:T(8,128)(2,1)S(1)}, bf16[288,1024]{1,0:T(8,128)(2,1)S(1)}, u32[]{:S(2)}, u32[]{:S(2)}) collective-permute-start(bf16[288,1024]{1,0:T(8,128)(2,1)S(1)} %shard_map.88.a), channel_id=1, source_target_pairs={{0,16},{1,17},{2,18},{3,19},{4,20},{5,21},{6,22},{7,23},{8,9},{9,8... | collective-permute-start | bytes 1769480 | tf_op jit(solution)/shard_map/ppermute | solution.py:320
  94.0 4.5 %collective-permute-start.21 = (f32[8,640]{1,0:T(8,128)S(1)}, f32[8,640]{1,0:T(8,128)S(1)}, u32[]{:S(2)}, u32[]{:S(2)}) collective-permute-start(f32[8,640]{1,0:T(8,128)S(1)} %shard_map.90), channel_id=1, source_target_pairs={{0,2},{1,3},{2,0},{3,1},{4,6},{5,7},{6,4},{7,5},{8,10},{9,11},{10,... | collective-permute-start | bytes 61448 | tf_op jit(solution)/shard_map/ppermute | solution.py:320
  96.1 4.7 %collective-permute-start.22 = (f32[8,640]{1,0:T(8,128)S(1)}, f32[8,640]{1,0:T(8,128)S(1)}, u32[]{:S(2)}, u32[]{:S(2)}) collective-permute-start(f32[8,640]{1,0:T(8,128)S(1)} %shard_map.90), channel_id=1, source_target_pairs={{0,4},{1,5},{2,6},{3,7},{4,0},{5,1},{6,2},{7,3},{8,12},{9,13},{10,... | collective-permute-start | bytes 61448 | tf_op jit(solution)/shard_map/ppermute | solution.py:320
  97.9 5.6 %collective-permute-start.23 = (f32[8,640]{1,0:T(8,128)S(1)}, f32[8,640]{1,0:T(8,128)S(1)}, u32[]{:S(2)}, u32[]{:S(2)}) collective-permute-start(f32[8,640]{1,0:T(8,128)S(1)} %shard_map.90), channel_id=1, source_target_pairs={{0,6},{1,7},{2,4},{3,5},{4,2},{5,3},{6,0},{7,1},{8,14},{9,15},{10,... | collective-permute-start | bytes 61448 | tf_op jit(solution)/shard_map/ppermute | solution.py:320
  103.6 3.8 %collective-permute-start.24 = (f32[8,640]{1,0:T(8,128)S(1)}, f32[8,640]{1,0:T(8,128)S(1)}, u32[]{:S(2)}, u32[]{:S(2)}) collective-permute-start(f32[8,640]{1,0:T(8,128)S(1)} %concatenate.19), channel_id=1, source_target_pairs={{0,1},{1,0},{2,3},{3,2},{4,5},{5,4},{6,7},{7,6},{8,9},{9,8},{10,11... | collective-permute-start | bytes 61448 | tf_op jit(solution)/shard_map/ppermute | solution.py:320
  105.2 3.8 %collective-permute-start.25 = (f32[8,640]{1,0:T(8,128)S(1)}, f32[8,640]{1,0:T(8,128)S(1)}, u32[]{:S(2)}, u32[]{:S(2)}) collective-permute-start(f32[8,640]{1,0:T(8,128)S(1)} %concatenate.19), channel_id=1, source_target_pairs={{0,16},{1,17},{2,18},{3,19},{4,20},{5,21},{6,22},{7,23},{8,24},{9,... | collective-permute-start | bytes 61448 | tf_op jit(solution)/shard_map/ppermute | solution.py:320
  106.7 4.7 %collective-permute-start.26 = (f32[8,640]{1,0:T(8,128)S(1)}, f32[8,640]{1,0:T(8,128)S(1)}, u32[]{:S(2)}, u32[]{:S(2)}) collective-permute-start(f32[8,640]{1,0:T(8,128)S(1)} %concatenate.19), channel_id=1, source_target_pairs={{0,17},{1,16},{2,19},{3,18},{4,21},{5,20},{6,23},{7,22},{8,25},{9,... | collective-permute-start | bytes 61448 | tf_op jit(solution)/shard_map/ppermute | solution.py:320
  111.5 1.2 %collective-permute-start.27 = (f32[8,640]{1,0:T(8,128)S(1)}, f32[8,640]{1,0:T(8,128)S(1)}, u32[]{:S(2)}, u32[]{:S(2)}) collective-permute-start(f32[8,640]{1,0:T(8,128)S(1)} %maximum_maximum_fusion.mine), channel_id=1, source_target_pairs={{0,8},{8,0},{16,24},{24,16},{1,9},{9,1},{17,25},{25,17},{2,10},{10... | collective-permute-start | bytes 61448 | tf_op jit(solution)/shard_map/ppermute | solution.py:449

commit v15 on v14

--- a/solution.py
+++ b/solution.py
@@ -50,7 +50,7 @@
     table[1:2, :] = reward[...].astype(F32)
 
 
-def pick_kernel(count, lengths, rows, sibling, extra, gain, table, after, full, table_out):
+def pick_kernel(count, lengths, rows, sibling, extra, gain, table, after, ids, full, table_out):
     section = lax.axis_index("section")
     core, pair = lax.rem(section, 2), lax.div(section, 2)
     positions, half = rows.shape[0], extra.shape[0]
@@ -337,12 +337,6 @@
 
     if groups == 8:
         table = jnp.concatenate([table, send(table, perm_x)])
-    full, table = call(
-        functools.partial(pick_kernel, count),
-        [jax.ShapeDtypeStruct((count, part), BF16), like(table)],
-        [SMEM] + [VMEM] * 5 + [ANY],
-        (lengths, rows, sibling, extra, gain, table, head_sibling),
-    )
     token_ids, hit, per_row = call(
         functools.partial(token_kernel, count),
         [
@@ -353,6 +347,12 @@
         [SMEM, VMEM],
         (lengths, tokens),
     )
+    full, table = call(
+        functools.partial(pick_kernel, count),
+        [jax.ShapeDtypeStruct((count, part), BF16), like(table)],
+        [SMEM] + [VMEM] * 5 + [ANY] * 2,
+        (lengths, rows, sibling, extra, gain, table, head_sibling, token_ids),
+    )
 
     if groups == 8:
         perm_a = mesh_perm(lambda s, d: (s, d ^ 1) if s % 2 == 0 else (s ^ 2, d))
@@ -369,7 +369,7 @@
         b0 = send(full, perm_b)
         table = jnp.concatenate([table, send(table, perm_z[1])])
         z3 = send(call(padded_kernel, jax.ShapeDtypeStruct((count + 16, part), BF16), [VMEM, ANY], (full, z1)), perm_f)
-        z1 = gate(z1, b0, table, token_ids)
+        z1 = gate(z1, b0, table)
         a1 = send(z1, perm_a)
         b1 = send(z1, perm_b)
         c0 = send(a0, perm_b)

time: 114 us -> 111 us (0.974)
  starting transfers between devices: 39.1 us -> 34.3 us
  waiting for transfers between devices: 53.3 us -> 54.5 us
    ppermute x24, starting transfers between devices: 37.8 us -> 33 us  [per_device(): send = lambda value, perm: lax.ppermute(value, AXES, perm)]
    ppermute x24, waiting for transfers between devices: 52.1 us -> 53.3 us  [per_device(): send = lambda value, perm: lax.ppermute(value, AXES, perm)]
  transfers between devices with their start and end apart: 28 -> 28, of which waited for: 14 -> 13; matrix products, arithmetic and copies ran while one was open for 2% -> 2% of each run, Pallas kernels for 11% -> 11%
where the time goes in v15:
time: 111 us
  waiting for transfers between devices  54.5 us (49%)
  starting transfers between devices  34.3 us (31%)
  Pallas kernels  15.8 us (14%)
  local copies, waits for them, and re-layouts  4.99 us (4%)
    ppermute x24, waiting for transfers between devices, per_device(): send = lambda value, perm: lax.ppermute(value, AXES, perm)  53.3 us
    ppermute x24, starting transfers between devices, per_device(): send = lambda value, perm: lax.ppermute(value, AXES, perm)  33 us
    pallas_call x15, Pallas kernels, call(): pl.pallas_call(body, out_shape=outs, in_specs=in_specs, out_specs=[VMEM]...  15.8 us
    unnamed x8, local copies, waits for them, and re-layouts  2.48 us
  transfers between devices with their start and end apart: 28, of which 13 were waited for; matrix products, arithmetic and copies ran while one was open for 2% of the time, Pallas kernels for 11%

profile of v15, /device:TPU:0, one launch (start us, length us, event | category | flops | bytes accessed | tf_op | source)
XLA Modules:
  0.0 110.6 jit_solution(1980319458100971465)
XLA Ops:
  0.6 0.5 collective-permute-start
  1.2 1.0 slice_bitcast_fusion
  2.3 0.7 collective-permute-start.2
  2.9 0.7 broadcast_in_dim.17.gain
  3.6 0.7 broadcast_in_dim.18.reward
  4.3 1.1 %copy-done.1 = bf16[1,384,1024]{2,1,0:T(8,128)(2,1)S(1)} copy-done((bf16[1,384,1024]{2,1,0:T(8,128)(2,1)S(1)}, bf16[1,384,1024]{2,1,0:T(8,128)(2,1)}, u32[]{:S(2)}) %copy-start.1) | copy-done | bytes 786456
  5.5 3.0 %collective-permute-start.3 = (f32[2,1024]{1,0:T(2,128)S(1)}, f32[2,1024]{1,0:T(2,128)S(1)}, u32[]{:S(2)}, u32[]{:S(2)}) collective-permute-start(f32[2,1024]{1,0:T(2,128)S(1)} %get-tuple-element.21), channel_id=1, source_target_pairs={{0,1},{1,0},{2,3},{3,2},{4,5},{5,4},{6,7},{7,6},{8,9},{9,8},{10,11... | collective-permute-start | bytes 24584 | tf_op jit(solution)/shard_map/ppermute | solution.py:320
  8.5 0.7 copy-done.2
  9.2 0.7 copy-done.3
  9.8 1.3 %shard_map.78 = (s32[576,1]{1,0:T(8,128)S(1)}, bf16[2,640,384]{2,1,0:T(8,128)(2,1)S(1)}, f32[8,128]{1,0:T(8,128)S(1)}) custom-call(s32[4]{0:T(128)S(1)} %copy-done.3, s32[4,384]{1,0:T(4,128)S(1)} %copy-done.2), custom_call_target="tpu_custom_call" | custom-call | tf_op jit(solution)/shard_map/pallas_call | solution.py:288
  11.2 1.6 %shard_map.79 = (bf16[288,1024]{1,0:T(8,128)(2,1)S(1)}, f32[4,1024]{1,0:T(4,128)S(1)}) custom-call(s32[4]{0:T(128)S(1)} %copy-done.3, bf16[384,1024]{1,0:T(8,128)(2,1)S(1)} %get-tuple-element.20.rows, bf16[384,1024]{1,0:T(8,128)(2,1)S(1)} %collective-permute-done.1.sibling, bf16[192,1024]{1,0:T(8,128)(2,1)S(1)} %collective-permute-done.2.extra, ...), custom_call_target="tpu_custom_call" | custom-call | tf_op jit(solution)/shard_map/pallas_call | solution.py:288
  12.8 1.6 %collective-permute-start.9 = (bf16[288,1024]{1,0:T(8,128)(2,1)S(1)}, bf16[288,1024]{1,0:T(8,128)(2,1)S(1)}, u32[]{:S(2)}, u32[]{:S(2)}) collective-permute-start(bf16[288,1024]{1,0:T(8,128)(2,1)S(1)} %get-tuple-element.24.value.z), channel_id=1, source_target_pairs={{0,2},{1,3},{2,0},{3,1},{4,6},{5,7},{6,4},{7,5},{8,14},{9,15},{10,... | collective-permute-start | bytes 1769480 | tf_op jit(solution)/shard_map/ppermute | solution.py:320
  14.4 1.5 %collective-permute-start.7 = (bf16[288,1024]{1,0:T(8,128)(2,1)S(1)}, bf16[288,1024]{1,0:T(8,128)(2,1)S(1)}, u32[]{:S(2)}, u32[]{:S(2)}) collective-permute-start(bf16[288,1024]{1,0:T(8,128)(2,1)S(1)} %get-tuple-element.24.value.z), channel_id=1, source_target_pairs={{0,16},{1,17},{2,18},{3,19},{4,20},{5,21},{6,22},{7,23},{8,9},{9,8... | collective-permute-start | bytes 1769480 | tf_op jit(solution)/shard_map/ppermute | solution.py:320
  15.9 0.4 collective-permute-start.4
  16.4 1.0 collective-permute-start.6
  17.4 8.8 %collective-permute-done.9.value.after = bf16[288,1024]{1,0:T(8,128)(2,1)S(1)} collective-permute-done((bf16[288,1024]{1,0:T(8,128)(2,1)S(1)}, bf16[288,1024]{1,0:T(8,128)(2,1)S(1)}, u32[]{:S(2)}, u32[]{:S(2)}) %collective-permute-start.9) | collective-permute-done | bytes 589856 | tf_op jit(solution)/shard_map/ppermute | solution.py:320
  26.3 6.7 %collective-permute-start.12 = (bf16[304,1024]{1,0:T(8,128)(2,1)S(1)}, bf16[304,1024]{1,0:T(8,128)(2,1)S(1)}, u32[]{:S(2)}, u32[]{:S(2)}) collective-permute-start(bf16[304,1024]{1,0:T(8,128)(2,1)S(1)} %shard_map.81), channel_id=1, source_target_pairs={{0,6},{1,7},{2,4},{3,5},{4,2},{5,3},{6,0},{7,1},{8,10},{9,11},{10,... | collective-permute-start | bytes 1867784 | tf_op jit(solution)/shard_map/ppermute | solution.py:320
  33.0 1.1 collective-permute-start.10
  34.1 1.5 %collective-permute-start.11 = (bf16[288,1024]{1,0:T(8,128)(2,1)S(1)}, bf16[288,1024]{1,0:T(8,128)(2,1)S(1)}, u32[]{:S(2)}, u32[]{:S(2)}) collective-permute-start(bf16[288,1024]{1,0:T(8,128)(2,1)S(1)} %shard_map.80.z1.value), channel_id=1, source_target_pairs={{0,16},{1,17},{2,18},{3,19},{4,20},{5,21},{6,22},{7,23},{8,9},{9,8... | collective-permute-start | bytes 1769480 | tf_op jit(solution)/shard_map/ppermute | solution.py:320
  35.6 0.5 collective-permute-start.8
  36.1 13.1 %collective-permute-done.10.refs_0_.a1 = bf16[288,1024]{1,0:T(8,128)(2,1)S(1)} collective-permute-done((bf16[288,1024]{1,0:T(8,128)(2,1)S(1)}, bf16[288,1024]{1,0:T(8,128)(2,1)S(1)}, u32[]{:S(2)}, u32[]{:S(2)}) %collective-permute-start.10) | collective-permute-done | bytes 589856 | tf_op jit(solution)/shard_map/ppermute | solution.py:320
  49.3 1.1 collective-permute-start.13
  50.5 0.4 collective-permute-start.16
  50.9 6.4 %collective-permute-done.8.refs_1_.c = bf16[288,1024]{1,0:T(8,128)(2,1)S(1)} collective-permute-done((bf16[288,1024]{1,0:T(8,128)(2,1)S(1)}, bf16[288,1024]{1,0:T(8,128)(2,1)S(1)}, u32[]{:S(2)}, u32[]{:S(2)}) %collective-permute-start.8) | collective-permute-done | bytes 589856 | tf_op jit(solution)/shard_map/ppermute | solution.py:320
  57.5 4.5 %shard_map.84 = (f32[576,512]{1,0:T(8,128)S(1)}, f32[576,256]{1,0:T(8,128)S(1)}, s32[576,1]{1,0:T(8,128)S(1)}) custom-call(bf16[8192,256]{1,0:T(8,128)(2,1)S(1)} %copy-done, bf16[8192,256]{1,0:T(8,128)(2,1)S(1)} %collective-permute-done.after.sibling, f32[16,1024]{1,0:T(8,128)S(1)} %pad_maximum_fusion.table.refs_0_, ...), custom_call_target="tpu_custom_call" | custom-call | tf_op jit(solution)/shard_map/pallas_call | solution.py:288
  62.0 0.8 collective-permute-done.13.value
  62.8 1.6 %collective-permute-start.15 = (bf16[288,1024]{1,0:T(8,128)(2,1)S(1)}, bf16[288,1024]{1,0:T(8,128)(2,1)S(1)}, u32[]{:S(2)}, u32[]{:S(2)}) collective-permute-start(bf16[288,1024]{1,0:T(8,128)(2,1)S(1)} %shard_map.85.a), channel_id=1, source_target_pairs={{0,16},{1,17},{2,18},{3,19},{4,20},{5,21},{6,22},{7,23},{8,9},{9,8... | collective-permute-start | bytes 1769480 | tf_op jit(solution)/shard_map/ppermute | solution.py:320
  64.4 1.3 %collective-permute-start.17 = (bf16[288,1024]{1,0:T(8,128)(2,1)S(1)}, bf16[288,1024]{1,0:T(8,128)(2,1)S(1)}, u32[]{:S(2)}, u32[]{:S(2)}) collective-permute-start(bf16[288,1024]{1,0:T(8,128)(2,1)S(1)} %collective-permute-done.16.z), channel_id=1, source_target_pairs={{0,1},{1,0},{2,3},{3,2},{4,5},{5,4},{6,7},{7,6},{8,24},{9,25},{10,... | collective-permute-start | bytes 1769480 | tf_op jit(solution)/shard_map/ppermute | solution.py:320
  65.7 0.8 collective-permute-start.18
  66.5 1.9 %collective-permute-start.19 = (bf16[288,1024]{1,0:T(8,128)(2,1)S(1)}, bf16[288,1024]{1,0:T(8,128)(2,1)S(1)}, u32[]{:S(2)}, u32[]{:S(2)}) collective-permute-start(bf16[288,1024]{1,0:T(8,128)(2,1)S(1)} %collective-permute-done.8.refs_1_.c), channel_id=1, source_target_pairs={{0,2},{1,3},{2,0},{3,1},{4,6},{5,7},{6,4},{7,5},{8,14},{9,15},{10,... | collective-permute-start | bytes 1769480 | tf_op jit(solution)/shard_map/ppermute | solution.py:320
  68.4 11.6 %collective-permute-done.15.c = bf16[288,1024]{1,0:T(8,128)(2,1)S(1)} collective-permute-done((bf16[288,1024]{1,0:T(8,128)(2,1)S(1)}, bf16[288,1024]{1,0:T(8,128)(2,1)S(1)}, u32[]{:S(2)}, u32[]{:S(2)}) %collective-permute-start.15) | collective-permute-done | bytes 589856 | tf_op jit(solution)/shard_map/ppermute | solution.py:320
  80.0 2.7 %shard_map.86 = (f32[576,512]{1,0:T(8,128)S(1)}, f32[576,256]{1,0:T(8,128)S(1)}) custom-call(bf16[8192,256]{1,0:T(8,128)(2,1)S(1)} %copy-done, bf16[8192,256]{1,0:T(8,128)(2,1)S(1)} %collective-permute-done.after.sibling, f32[16,1024]{1,0:T(8,128)S(1)} %pad_maximum_fusion.table.refs_0_, f32[576,512]{1,0:T(8,128)S(1)} %get-tuple-element.25.acc_in, ...), custom_call_target="tpu_custom_call" | custom-call | tf_op jit(solution)/shard_map/pallas_call | solution.py:288
  82.9 3.4 %collective-permute-done.18.b = bf16[288,1024]{1,0:T(8,128)(2,1)S(1)} collective-permute-done((bf16[288,1024]{1,0:T(8,128)(2,1)S(1)}, bf16[288,1024]{1,0:T(8,128)(2,1)S(1)}, u32[]{:S(2)}, u32[]{:S(2)}) %collective-permute-start.18) | collective-permute-done | bytes 589856 | tf_op jit(solution)/shard_map/ppermute | solution.py:320
  86.3 3.2 %shard_map.89 = (f32[288,512]{1,0:T(8,128)S(1)}, f32[288,256]{1,0:T(8,128)S(1)}, bf16[1024,512]{1,0:T(8,128)(2,1)S(1)}, f32[640,128]{1,0:T(8,128)S(1)}) custom-call(bf16[8192,256]{1,0:T(8,128)(2,1)S(1)} %copy-done, bf16[8192,256]{1,0:T(8,128)(2,1)S(1)} %collective-permute-done.after.sibling, f32[16,1024]{1,0:T(8,128)S(1)} %pad_maximum_fusion.table.refs_0_, ...), custom_call_target="tpu_custom_call" | custom-call | tf_op jit(solution)/shard_map/pallas_call | solution.py:288
  89.5 3.1 %collective-permute-done.20.c = bf16[288,1024]{1,0:T(8,128)(2,1)S(1)} collective-permute-done((bf16[288,1024]{1,0:T(8,128)(2,1)S(1)}, bf16[288,1024]{1,0:T(8,128)(2,1)S(1)}, u32[]{:S(2)}, u32[]{:S(2)}) %collective-permute-start.20) | collective-permute-done | bytes 589856 | tf_op jit(solution)/shard_map/ppermute | solution.py:320
  92.7 1.4 %shard_map.90 = f32[8,640]{1,0:T(8,128)S(1)} custom-call(bf16[1024,512]{1,0:T(8,128)(2,1)S(1)} %get-tuple-element.30.far_weights, f32[16,1024]{1,0:T(8,128)S(1)} %pad_maximum_fusion.table.refs_0_, f32[288,512]{1,0:T(8,128)S(1)} %get-tuple-element.31.left, f32[288,256]{1,0:T(8,128)S(1)} %get-tuple-element.32.left_side, ...), custom_call_target="tpu_custom_call" | custom-call | tf_op jit(solution)/shard_map/pallas_call | solution.py:288
  94.0 3.9 %collective-permute-start.23 = (f32[8,640]{1,0:T(8,128)S(1)}, f32[8,640]{1,0:T(8,128)S(1)}, u32[]{:S(2)}, u32[]{:S(2)}) collective-permute-start(f32[8,640]{1,0:T(8,128)S(1)} %shard_map.90), channel_id=1, source_target_pairs={{0,6},{1,7},{2,4},{3,5},{4,2},{5,3},{6,0},{7,1},{8,14},{9,15},{10,... | collective-permute-start | bytes 61448 | tf_op jit(solution)/shard_map/ppermute | solution.py:320
  98.0 0.6 collective-permute-start.21
  98.6 1.2 %collective-permute-done.23 = f32[8,640]{1,0:T(8,128)S(1)} collective-permute-done((f32[8,640]{1,0:T(8,128)S(1)}, f32[8,640]{1,0:T(8,128)S(1)}, u32[]{:S(2)}, u32[]{:S(2)}) %collective-permute-start.23) | collective-permute-done | bytes 20512 | tf_op jit(solution)/shard_map/ppermute | solution.py:320
  99.9 2.8 %collective-permute-done.22 = f32[8,640]{1,0:T(8,128)S(1)} collective-permute-done((f32[8,640]{1,0:T(8,128)S(1)}, f32[8,640]{1,0:T(8,128)S(1)}, u32[]{:S(2)}, u32[]{:S(2)}) %collective-permute-start.22) | collective-permute-done | bytes 20512 | tf_op jit(solution)/shard_map/ppermute | solution.py:320
  102.8 1.2 %collective-permute-start.26 = (f32[8,640]{1,0:T(8,128)S(1)}, f32[8,640]{1,0:T(8,128)S(1)}, u32[]{:S(2)}, u32[]{:S(2)}) collective-permute-start(f32[8,640]{1,0:T(8,128)S(1)} %concatenate.19), channel_id=1, source_target_pairs={{0,17},{1,16},{2,19},{3,18},{4,21},{5,20},{6,23},{7,22},{8,25},{9,... | collective-permute-start | bytes 61448 | tf_op jit(solution)/shard_map/ppermute | solution.py:320
  104.0 0.7 collective-permute-start.25
  104.7 1.6 %collective-permute-start.24 = (f32[8,640]{1,0:T(8,128)S(1)}, f32[8,640]{1,0:T(8,128)S(1)}, u32[]{:S(2)}, u32[]{:S(2)}) collective-permute-start(f32[8,640]{1,0:T(8,128)S(1)} %concatenate.19), channel_id=1, source_target_pairs={{0,1},{1,0},{2,3},{3,2},{4,5},{5,4},{6,7},{7,6},{8,9},{9,8},{10,11... | collective-permute-start | bytes 61448 | tf_op jit(solution)/shard_map/ppermute | solution.py:320
  106.4 1.1 %collective-permute-done.26 = f32[8,640]{1,0:T(8,128)S(1)} collective-permute-done((f32[8,640]{1,0:T(8,128)S(1)}, f32[8,640]{1,0:T(8,128)S(1)}, u32[]{:S(2)}, u32[]{:S(2)}) %collective-permute-start.26) | collective-permute-done | bytes 20512 | tf_op jit(solution)/shard_map/ppermute | solution.py:320
  107.5 0.3 collective-permute-done.25
  107.8 0.7 collective-permute-done.24
  108.6 1.2 %collective-permute-done.27.sibling = f32[8,640]{1,0:T(8,128)S(1)} collective-permute-done((f32[8,640]{1,0:T(8,128)S(1)}, f32[8,640]{1,0:T(8,128)S(1)}, u32[]{:S(2)}, u32[]{:S(2)}) %collective-permute-start.27) | collective-permute-done | bytes 20512 | tf_op jit(solution)/shard_map/ppermute | solution.py:449
  109.8 0.8 shard_map.91
  (44 shorter events, 1.1 us)
Async XLA Ops:
  0.6 10.5 %collective-permute-start = (bf16[8192,256]{1,0:T(8,128)(2,1)}, bf16[8192,256]{1,0:T(8,128)(2,1)S(1)}, u32[]{:S(2)}, u32[]{:S(2)}) collective-permute-start(bf16[8192,256]{1,0:T(8,128)(2,1)} %head.5), channel_id=1, source_target_pairs={{0,8},{8,0},{16,24},{24,16},{1,9},{9,1},{17,25},{25,17},{2,10},{10... | collective-permute-start | bytes 12582920 | tf_op jit(solution)/shard_map/ppermute | solution.py:333
  1.1 10.0 %collective-permute-start.1 = (bf16[384,1024]{1,0:T(8,128)(2,1)}, bf16[384,1024]{1,0:T(8,128)(2,1)S(1)}, u32[]{:S(2)}, u32[]{:S(2)}) collective-permute-start(bf16[384,1024]{1,0:T(8,128)(2,1)} %bitcast.4), channel_id=1, source_target_pairs={{0,8},{8,0},{16,24},{24,16},{1,9},{9,1},{17,25},{25,17},{2,10},{10... | collective-permute-start | bytes 2359304 | tf_op jit(solution)/shard_map/ppermute | solution.py:332
  2.3 8.9 %collective-permute-start.2 = (bf16[192,1024]{1,0:T(8,128)(2,1)S(1)}, bf16[192,1024]{1,0:T(8,128)(2,1)S(1)}, u32[]{:S(2)}, u32[]{:S(2)}) collective-permute-start(bf16[192,1024]{1,0:T(8,128)(2,1)S(1)} %slice_bitcast_fusion), channel_id=1, source_target_pairs={{8,24},{24,8},{9,25},{25,9},{10,26},{26,10},{11,27},{27,11},{12,28... | collective-permute-start | bytes 1179656 | tf_op jit(solution)/shard_map/ppermute | solution.py:331
  4.3 1.1 %copy-start.1 = (bf16[1,384,1024]{2,1,0:T(8,128)(2,1)S(1)}, bf16[1,384,1024]{2,1,0:T(8,128)(2,1)}, u32[]{:S(2)}) copy-start(bf16[1,384,1024]{2,1,0:T(8,128)(2,1)} %param.6) | copy-start | bytes 2359300
  5.5 5.6 %collective-permute-start.3 = (f32[2,1024]{1,0:T(2,128)S(1)}, f32[2,1024]{1,0:T(2,128)S(1)}, u32[]{:S(2)}, u32[]{:S(2)}) collective-permute-start(f32[2,1024]{1,0:T(2,128)S(1)} %get-tuple-element.21), channel_id=1, source_target_pairs={{0,1},{1,0},{2,3},{3,2},{4,5},{5,4},{6,7},{7,6},{8,9},{9,8},{10,11... | collective-permute-start | bytes 24584 | tf_op jit(solution)/shard_map/ppermute | solution.py:320
  8.5 0.7 copy-start.2
  9.2 0.7 copy-start.3
  12.8 13.4 %collective-permute-start.9 = (bf16[288,1024]{1,0:T(8,128)(2,1)S(1)}, bf16[288,1024]{1,0:T(8,128)(2,1)S(1)}, u32[]{:S(2)}, u32[]{:S(2)}) collective-permute-start(bf16[288,1024]{1,0:T(8,128)(2,1)S(1)} %get-tuple-element.24.value.z), channel_id=1, source_target_pairs={{0,2},{1,3},{2,0},{3,1},{4,6},{5,7},{6,4},{7,5},{8,14},{9,15},{10,... | collective-permute-start | bytes 1769480 | tf_op jit(solution)/shard_map/ppermute | solution.py:320
  14.4 18.5 %collective-permute-start.7 = (bf16[288,1024]{1,0:T(8,128)(2,1)S(1)}, bf16[288,1024]{1,0:T(8,128)(2,1)S(1)}, u32[]{:S(2)}, u32[]{:S(2)}) collective-permute-start(bf16[288,1024]{1,0:T(8,128)(2,1)S(1)} %get-tuple-element.24.value.z), channel_id=1, source_target_pairs={{0,16},{1,17},{2,18},{3,19},{4,20},{5,21},{6,22},{7,23},{8,9},{9,8... | collective-permute-start | bytes 1769480 | tf_op jit(solution)/shard_map/ppermute | solution.py:320
  15.9 41.5 %copy-start = (bf16[8192,256]{1,0:T(8,128)(2,1)S(1)}, bf16[8192,256]{1,0:T(8,128)(2,1)}, u32[]{:S(2)}) copy-start(bf16[8192,256]{1,0:T(8,128)(2,1)} %head.5) | copy-start | bytes 12582916
  15.9 17.0 %collective-permute-start.4 = (f32[4,1024]{1,0:T(4,128)S(1)}, f32[4,1024]{1,0:T(4,128)S(1)}, u32[]{:S(2)}, u32[]{:S(2)}) collective-permute-start(f32[4,1024]{1,0:T(4,128)S(1)} %get-tuple-element.23), channel_id=1, source_target_pairs={{0,2},{1,3},{2,0},{3,1},{4,6},{5,7},{6,4},{7,5},{8,10},{9,11},{10,... | collective-permute-start | bytes 49160 | tf_op jit(solution)/shard_map/ppermute | solution.py:320
  16.4 19.2 %collective-permute-start.6 = (bf16[288,1024]{1,0:T(8,128)(2,1)S(1)}, bf16[288,1024]{1,0:T(8,128)(2,1)S(1)}, u32[]{:S(2)}, u32[]{:S(2)}) collective-permute-start(bf16[288,1024]{1,0:T(8,128)(2,1)S(1)} %get-tuple-element.24.value.z), channel_id=1, source_target_pairs={{0,1},{1,0},{2,3},{3,2},{4,5},{5,4},{6,7},{7,6},{8,24},{9,25},{10,... | collective-permute-start | bytes 1769480 | tf_op jit(solution)/shard_map/ppermute | solution.py:320
  26.3 23.0 %collective-permute-start.12 = (bf16[304,1024]{1,0:T(8,128)(2,1)S(1)}, bf16[304,1024]{1,0:T(8,128)(2,1)S(1)}, u32[]{:S(2)}, u32[]{:S(2)}) collective-permute-start(bf16[304,1024]{1,0:T(8,128)(2,1)S(1)} %shard_map.81), channel_id=1, source_target_pairs={{0,6},{1,7},{2,4},{3,5},{4,2},{5,3},{6,0},{7,1},{8,10},{9,11},{10,... | collective-permute-start | bytes 1867784 | tf_op jit(solution)/shard_map/ppermute | solution.py:320
  33.0 16.2 %collective-permute-start.10 = (bf16[288,1024]{1,0:T(8,128)(2,1)S(1)}, bf16[288,1024]{1,0:T(8,128)(2,1)S(1)}, u32[]{:S(2)}, u32[]{:S(2)}) collective-permute-start(bf16[288,1024]{1,0:T(8,128)(2,1)S(1)} %shard_map.80.z1.value), channel_id=1, source_target_pairs={{0,1},{1,0},{2,3},{3,2},{4,5},{5,4},{6,7},{7,6},{8,24},{9,25},{10,... | collective-permute-start | bytes 1769480 | tf_op jit(solution)/shard_map/ppermute | solution.py:320
  34.1 16.3 %collective-permute-start.5 = (f32[8,1024]{1,0:T(8,128)S(1)}, f32[8,1024]{1,0:T(8,128)S(1)}, u32[]{:S(2)}, u32[]{:S(2)}) collective-permute-start(f32[8,1024]{1,0:T(8,128)S(1)} %pad_maximum_fusion.1.refs_1_), channel_id=1, source_target_pairs={{0,4},{1,5},{2,6},{3,7},{4,0},{5,1},{6,2},{7,3},{8,12},{9,13},{10,... | collective-permute-start | bytes 98312 | tf_op jit(solution)/shard_map/ppermute | solution.py:320
  34.1 23.2 %collective-permute-start.11 = (bf16[288,1024]{1,0:T(8,128)(2,1)S(1)}, bf16[288,1024]{1,0:T(8,128)(2,1)S(1)}, u32[]{:S(2)}, u32[]{:S(2)}) collective-permute-start(bf16[288,1024]{1,0:T(8,128)(2,1)S(1)} %shard_map.80.z1.value), channel_id=1, source_target_pairs={{0,16},{1,17},{2,18},{3,19},{4,20},{5,21},{6,22},{7,23},{8,9},{9,8... | collective-permute-start | bytes 1769480 | tf_op jit(solution)/shard_map/ppermute | solution.py:320
  35.6 21.7 %collective-permute-start.8 = (bf16[288,1024]{1,0:T(8,128)(2,1)S(1)}, bf16[288,1024]{1,0:T(8,128)(2,1)S(1)}, u32[]{:S(2)}, u32[]{:S(2)}) collective-permute-start(bf16[288,1024]{1,0:T(8,128)(2,1)S(1)} %collective-permute-done.6.a), channel_id=1, source_target_pairs={{0,16},{1,17},{2,18},{3,19},{4,20},{5,21},{6,22},{7,23},{8,9},{9,8... | collective-permute-start | bytes 1769480 | tf_op jit(solution)/shard_map/ppermute | solution.py:320
  49.3 13.4 %collective-permute-start.13 = (bf16[288,1024]{1,0:T(8,128)(2,1)S(1)}, bf16[288,1024]{1,0:T(8,128)(2,1)S(1)}, u32[]{:S(2)}, u32[]{:S(2)}) collective-permute-start(bf16[288,1024]{1,0:T(8,128)(2,1)S(1)} %shard_map.82.value), channel_id=1, source_target_pairs={{0,1},{1,0},{2,3},{3,2},{4,5},{5,4},{6,7},{7,6},{8,24},{9,25},{10,... | collective-permute-start | bytes 1769480 | tf_op jit(solution)/shard_map/ppermute | solution.py:320
  50.5 13.9 %collective-permute-start.16 = (bf16[288,1024]{1,0:T(8,128)(2,1)S(1)}, bf16[288,1024]{1,0:T(8,128)(2,1)S(1)}, u32[]{:S(2)}, u32[]{:S(2)}) collective-permute-start(bf16[288,1024]{1,0:T(8,128)(2,1)S(1)} %shard_map.87), channel_id=1, source_target_pairs={{0,6},{1,7},{2,4},{3,5},{4,2},{5,3},{6,0},{7,1},{8,10},{9,11},{10,... | collective-permute-start | bytes 1769480 | tf_op jit(solution)/shard_map/ppermute | solution.py:320
  57.4 11.0 %collective-permute-start.14 = (bf16[288,1024]{1,0:T(8,128)(2,1)S(1)}, bf16[288,1024]{1,0:T(8,128)(2,1)S(1)}, u32[]{:S(2)}, u32[]{:S(2)}) collective-permute-start(bf16[288,1024]{1,0:T(8,128)(2,1)S(1)} %shard_map.83.after.z), channel_id=1, source_target_pairs={{0,16},{1,17},{2,18},{3,19},{4,20},{5,21},{6,22},{7,23},{8,9},{9,8... | collective-permute-start | bytes 1769480 | tf_op jit(solution)/shard_map/ppermute | solution.py:320
  62.8 17.2 %collective-permute-start.15 = (bf16[288,1024]{1,0:T(8,128)(2,1)S(1)}, bf16[288,1024]{1,0:T(8,128)(2,1)S(1)}, u32[]{:S(2)}, u32[]{:S(2)}) collective-permute-start(bf16[288,1024]{1,0:T(8,128)(2,1)S(1)} %shard_map.85.a), channel_id=1, source_target_pairs={{0,16},{1,17},{2,18},{3,19},{4,20},{5,21},{6,22},{7,23},{8,9},{9,8... | collective-permute-start | bytes 1769480 | tf_op jit(solution)/shard_map/ppermute | solution.py:320
  64.4 18.3 %collective-permute-start.17 = (bf16[288,1024]{1,0:T(8,128)(2,1)S(1)}, bf16[288,1024]{1,0:T(8,128)(2,1)S(1)}, u32[]{:S(2)}, u32[]{:S(2)}) collective-permute-start(bf16[288,1024]{1,0:T(8,128)(2,1)S(1)} %collective-permute-done.16.z), channel_id=1, source_target_pairs={{0,1},{1,0},{2,3},{3,2},{4,5},{5,4},{6,7},{7,6},{8,24},{9,25},{10,... | collective-permute-start | bytes 1769480 | tf_op jit(solution)/shard_map/ppermute | solution.py:320
  65.7 20.6 %collective-permute-start.18 = (bf16[288,1024]{1,0:T(8,128)(2,1)S(1)}, bf16[288,1024]{1,0:T(8,128)(2,1)S(1)}, u32[]{:S(2)}, u32[]{:S(2)}) collective-permute-start(bf16[288,1024]{1,0:T(8,128)(2,1)S(1)} %collective-permute-done.16.z), channel_id=1, source_target_pairs={{0,16},{1,17},{2,18},{3,19},{4,20},{5,21},{6,22},{7,23},{8,9},{9,8... | collective-permute-start | bytes 1769480 | tf_op jit(solution)/shard_map/ppermute | solution.py:320
  66.5 19.8 %collective-permute-start.19 = (bf16[288,1024]{1,0:T(8,128)(2,1)S(1)}, bf16[288,1024]{1,0:T(8,128)(2,1)S(1)}, u32[]{:S(2)}, u32[]{:S(2)}) collective-permute-start(bf16[288,1024]{1,0:T(8,128)(2,1)S(1)} %collective-permute-done.8.refs_1_.c), channel_id=1, source_target_pairs={{0,2},{1,3},{2,0},{3,1},{4,6},{5,7},{6,4},{7,5},{8,14},{9,15},{10,... | collective-permute-start | bytes 1769480 | tf_op jit(solution)/shard_map/ppermute | solution.py:320
  82.7 9.9 %collective-permute-start.20 = (bf16[288,1024]{1,0:T(8,128)(2,1)S(1)}, bf16[288,1024]{1,0:T(8,128)(2,1)S(1)}, u32[]{:S(2)}, u32[]{:S(2)}) collective-permute-start(bf16[288,1024]{1,0:T(8,128)(2,1)S(1)} %shard_map.88.a), channel_id=1, source_target_pairs={{0,16},{1,17},{2,18},{3,19},{4,20},{5,21},{6,22},{7,23},{8,9},{9,8... | collective-permute-start | bytes 1769480 | tf_op jit(solution)/shard_map/ppermute | solution.py:320
  94.0 5.8 %collective-permute-start.23 = (f32[8,640]{1,0:T(8,128)S(1)}, f32[8,640]{1,0:T(8,128)S(1)}, u32[]{:S(2)}, u32[]{:S(2)}) collective-permute-start(f32[8,640]{1,0:T(8,128)S(1)} %shard_map.90), channel_id=1, source_target_pairs={{0,6},{1,7},{2,4},{3,5},{4,2},{5,3},{6,0},{7,1},{8,14},{9,15},{10,... | collective-permute-start | bytes 61448 | tf_op jit(solution)/shard_map/ppermute | solution.py:320
  98.0 4.7 %collective-permute-start.22 = (f32[8,640]{1,0:T(8,128)S(1)}, f32[8,640]{1,0:T(8,128)S(1)}, u32[]{:S(2)}, u32[]{:S(2)}) collective-permute-start(f32[8,640]{1,0:T(8,128)S(1)} %shard_map.90), channel_id=1, source_target_pairs={{0,4},{1,5},{2,6},{3,7},{4,0},{5,1},{6,2},{7,3},{8,12},{9,13},{10,... | collective-permute-start | bytes 61448 | tf_op jit(solution)/shard_map/ppermute | solution.py:320
  98.0 4.7 %collective-permute-start.21 = (f32[8,640]{1,0:T(8,128)S(1)}, f32[8,640]{1,0:T(8,128)S(1)}, u32[]{:S(2)}, u32[]{:S(2)}) collective-permute-start(f32[8,640]{1,0:T(8,128)S(1)} %shard_map.90), channel_id=1, source_target_pairs={{0,2},{1,3},{2,0},{3,1},{4,6},{5,7},{6,4},{7,5},{8,10},{9,11},{10,... | collective-permute-start | bytes 61448 | tf_op jit(solution)/shard_map/ppermute | solution.py:320
  102.8 4.7 %collective-permute-start.26 = (f32[8,640]{1,0:T(8,128)S(1)}, f32[8,640]{1,0:T(8,128)S(1)}, u32[]{:S(2)}, u32[]{:S(2)}) collective-permute-start(f32[8,640]{1,0:T(8,128)S(1)} %concatenate.19), channel_id=1, source_target_pairs={{0,17},{1,16},{2,19},{3,18},{4,21},{5,20},{6,23},{7,22},{8,25},{9,... | collective-permute-start | bytes 61448 | tf_op jit(solution)/shard_map/ppermute | solution.py:320
  104.0 3.8 %collective-permute-start.25 = (f32[8,640]{1,0:T(8,128)S(1)}, f32[8,640]{1,0:T(8,128)S(1)}, u32[]{:S(2)}, u32[]{:S(2)}) collective-permute-start(f32[8,640]{1,0:T(8,128)S(1)} %concatenate.19), channel_id=1, source_target_pairs={{0,16},{1,17},{2,18},{3,19},{4,20},{5,21},{6,22},{7,23},{8,24},{9,... | collective-permute-start | bytes 61448 | tf_op jit(solution)/shard_map/ppermute | solution.py:320
  104.7 3.8 %collective-permute-start.24 = (f32[8,640]{1,0:T(8,128)S(1)}, f32[8,640]{1,0:T(8,128)S(1)}, u32[]{:S(2)}, u32[]{:S(2)}) collective-permute-start(f32[8,640]{1,0:T(8,128)S(1)} %concatenate.19), channel_id=1, source_target_pairs={{0,1},{1,0},{2,3},{3,2},{4,5},{5,4},{6,7},{7,6},{8,9},{9,8},{10,11... | collective-permute-start | bytes 61448 | tf_op jit(solution)/shard_map/ppermute | solution.py:320
  108.6 1.2 %collective-permute-start.27 = (f32[8,640]{1,0:T(8,128)S(1)}, f32[8,640]{1,0:T(8,128)S(1)}, u32[]{:S(2)}, u32[]{:S(2)}) collective-permute-start(f32[8,640]{1,0:T(8,128)S(1)} %maximum_maximum_fusion.mine), channel_id=1, source_target_pairs={{0,8},{8,0},{16,24},{24,16},{1,9},{9,1},{17,25},{25,17},{2,10},{10... | collective-permute-start | bytes 61448 | tf_op jit(solution)/shard_map/ppermute | solution.py:449

commit v16 on v15

--- a/solution.py
+++ b/solution.py
@@ -67,24 +67,32 @@
     table_out[...] = table[...]
 
 
-def token_kernel(count, lengths, tokens, out, hit, per_row):
+def token_kernel(count, lengths, tokens, out):
+    _, core, _ = here()
+    spans, positions = tokens.shape
+    index = lax.broadcasted_iota(I32, (count, 1), 0)
+    lane = lax.broadcasted_iota(I32, (count, positions), 1)
+    for pair in range(2):
+        span, place = row_map(lengths, pair, core, index, count)
+        found = jnp.zeros((count, positions), F32)
+        for s in range(spans):
+            found = jnp.where(span == s, tokens[s : s + 1, :].astype(F32), found)
+        found = jnp.sum(jnp.where(lane == place, found, F32(0.0)), axis=1, keepdims=True)
+        out[pair * count : pair * count + count, :] = found.astype(I32)
+
+
+def mask_kernel(count, lengths, hit, per_row):
     section, core, _ = here()
-    spans, positions = tokens.shape
+    positions = hit.shape[2]
     index = lax.broadcasted_iota(I32, (count, 1), 0)
     lane = lax.broadcasted_iota(I32, (count, positions), 1)
     hit[...] = jnp.zeros(hit.shape, BF16)
     for pair in range(2):
         rows = slice(pair * count, pair * count + count)
-        span, place = row_map(lengths, pair, core, index, count)
-        found = jnp.zeros((count, positions), F32)
-        for s in range(spans):
-            found = jnp.where(span == s, tokens[s : s + 1, :].astype(F32), found)
-        here_is = lane == place
-        found = jnp.sum(jnp.where(here_is, found, F32(0.0)), axis=1, keepdims=True)
-        out[rows, :] = found.astype(I32)
-        hit[0, rows, :] = jnp.where(here_is & (span == section), F32(1.0), F32(0.0)).astype(BF16)
-        span, place = row_map(lengths, pair, 1 - core, index, count)
-        hit[1, rows, :] = jnp.where((lane == place) & (span == section), F32(1.0), F32(0.0)).astype(BF16)
+        for which in range(2):
+            span, place = row_map(lengths, pair, core + which - 2 * core * which, index, count)
+            here_is = (lane == place) & (span == section)
+            hit[which, rows, :] = jnp.where(here_is, F32(1.0), F32(0.0)).astype(BF16)
     per_row[...] = jnp.zeros(per_row.shape, F32) + 1.0 / lengths[section].astype(F32)
 
 
@@ -337,21 +345,21 @@
 
     if groups == 8:
         table = jnp.concatenate([table, send(table, perm_x)])
-    token_ids, hit, per_row = call(
-        functools.partial(token_kernel, count),
+    token_ids = call(functools.partial(token_kernel, count), ids_shape, [SMEM, VMEM], (lengths, tokens))
+    hit, per_row = call(
+        functools.partial(mask_kernel, count),
         [
-            ids_shape,
             jax.ShapeDtypeStruct((2, up(2 * count), positions), BF16),
             jax.ShapeDtypeStruct((8, LANES), F32),
         ],
-        [SMEM, VMEM],
-        (lengths, tokens),
+        [SMEM],
+        (lengths,),
     )
     full, table = call(
         functools.partial(pick_kernel, count),
         [jax.ShapeDtypeStruct((count, part), BF16), like(table)],
         [SMEM] + [VMEM] * 5 + [ANY] * 2,
-        (lengths, rows, sibling, extra, gain, table, head_sibling, token_ids),
+        (lengths, rows, sibling, extra, gain, table, head_sibling, per_row),
     )
 
     if groups == 8:

time: 111 us -> 111 us (level)
  waiting for transfers between devices: 54.5 us -> 52.4 us
  starting transfers between devices: 34.3 us -> 36 us
    ppermute x24, waiting for transfers between devices: 53.3 us -> 51.2 us  [per_device(): send = lambda value, perm: lax.ppermute(value, AXES, perm)]
    ppermute x24, starting transfers between devices: 33 us -> 34.7 us  [per_device(): send = lambda value, perm: lax.ppermute(value, AXES, perm)]
    pallas_call x15 -> x16, Pallas kernels: 15.8 us -> 16.7 us  [call(): pl.pallas_call(body, out_shape=outs, in_specs=in_specs, out_specs=[VMEM]...]
  transfers between devices with their start and end apart: 28 -> 28, of which waited for: 13 -> 14; matrix products, arithmetic and copies ran while one was open for 2% -> 2% of each run, Pallas kernels for 11% -> 12%
where the time goes in v16:
time: 111 us; the launch traced here: 110 us
  waiting for transfers between devices  52.4 us (47%)
  starting transfers between devices  36 us (32%)
  Pallas kernels  16.7 us (15%)
  local copies, waits for them, and re-layouts  4.31 us (4%)
    ppermute x24, waiting for transfers between devices, per_device(): send = lambda value, perm: lax.ppermute(value, AXES, perm)  51.2 us
    ppermute x24, starting transfers between devices, per_device(): send = lambda value, perm: lax.ppermute(value, AXES, perm)  34.7 us
    pallas_call x16, Pallas kernels, call(): pl.pallas_call(body, out_shape=outs, in_specs=in_specs, out_specs=[VMEM]...  16.7 us
  transfers between devices with their start and end apart: 28, of which 14 were waited for; matrix products, arithmetic and copies ran while one was open for 2% of the time, Pallas kernels for 12%

profile of v16, /device:TPU:0, one launch (start us, length us, event | category | flops | bytes accessed | tf_op | source)
XLA Modules:
  0.0 110.5 jit_solution(4830448378636555949)
XLA Ops:
  0.6 0.5 collective-permute-start
  1.2 1.0 slice_bitcast_fusion
  2.3 0.7 collective-permute-start.2
  2.9 0.7 broadcast_in_dim.17.gain
  3.6 0.7 broadcast_in_dim.18.reward
  4.3 1.1 %copy-done.1 = bf16[1,384,1024]{2,1,0:T(8,128)(2,1)S(1)} copy-done((bf16[1,384,1024]{2,1,0:T(8,128)(2,1)S(1)}, bf16[1,384,1024]{2,1,0:T(8,128)(2,1)}, u32[]{:S(2)}) %copy-start.1) | copy-done | bytes 786456
  5.5 3.0 %collective-permute-start.3 = (f32[2,1024]{1,0:T(2,128)S(1)}, f32[2,1024]{1,0:T(2,128)S(1)}, u32[]{:S(2)}, u32[]{:S(2)}) collective-permute-start(f32[2,1024]{1,0:T(2,128)S(1)} %get-tuple-element.20), channel_id=1, source_target_pairs={{0,1},{1,0},{2,3},{3,2},{4,5},{5,4},{6,7},{7,6},{8,9},{9,8},{10,11... | collective-permute-start | bytes 24584 | tf_op jit(solution)/shard_map/ppermute | solution.py:328
  8.5 0.7 copy-done.3
  9.2 1.2 %shard_map.78 = (bf16[2,640,384]{2,1,0:T(8,128)(2,1)S(1)}, f32[8,128]{1,0:T(8,128)S(1)}) custom-call(s32[4]{0:T(128)S(1)} %copy-done.3), custom_call_target="tpu_custom_call" | custom-call | tf_op jit(solution)/shard_map/pallas_call | solution.py:296
  10.4 1.6 %shard_map.79 = (bf16[288,1024]{1,0:T(8,128)(2,1)S(1)}, f32[4,1024]{1,0:T(4,128)S(1)}) custom-call(s32[4]{0:T(128)S(1)} %copy-done.3, bf16[384,1024]{1,0:T(8,128)(2,1)S(1)} %get-tuple-element.19.rows, bf16[384,1024]{1,0:T(8,128)(2,1)S(1)} %collective-permute-done.1.sibling, bf16[192,1024]{1,0:T(8,128)(2,1)S(1)} %collective-permute-done.2.extra, ...), custom_call_target="tpu_custom_call" | custom-call | tf_op jit(solution)/shard_map/pallas_call | solution.py:296
  12.0 1.9 %collective-permute-start.9 = (bf16[288,1024]{1,0:T(8,128)(2,1)S(1)}, bf16[288,1024]{1,0:T(8,128)(2,1)S(1)}, u32[]{:S(2)}, u32[]{:S(2)}) collective-permute-start(bf16[288,1024]{1,0:T(8,128)(2,1)S(1)} %get-tuple-element.23.value.z), channel_id=1, source_target_pairs={{0,2},{1,3},{2,0},{3,1},{4,6},{5,7},{6,4},{7,5},{8,14},{9,15},{10,... | collective-permute-start | bytes 1769480 | tf_op jit(solution)/shard_map/ppermute | solution.py:328
  14.0 1.5 %collective-permute-start.7 = (bf16[288,1024]{1,0:T(8,128)(2,1)S(1)}, bf16[288,1024]{1,0:T(8,128)(2,1)S(1)}, u32[]{:S(2)}, u32[]{:S(2)}) collective-permute-start(bf16[288,1024]{1,0:T(8,128)(2,1)S(1)} %get-tuple-element.23.value.z), channel_id=1, source_target_pairs={{0,16},{1,17},{2,18},{3,19},{4,20},{5,21},{6,22},{7,23},{8,9},{9,8... | collective-permute-start | bytes 1769480 | tf_op jit(solution)/shard_map/ppermute | solution.py:328
  15.5 0.4 collective-permute-start.4
  15.9 1.5 %collective-permute-start.6 = (bf16[288,1024]{1,0:T(8,128)(2,1)S(1)}, bf16[288,1024]{1,0:T(8,128)(2,1)S(1)}, u32[]{:S(2)}, u32[]{:S(2)}) collective-permute-start(bf16[288,1024]{1,0:T(8,128)(2,1)S(1)} %get-tuple-element.23.value.z), channel_id=1, source_target_pairs={{0,1},{1,0},{2,3},{3,2},{4,5},{5,4},{6,7},{7,6},{8,24},{9,25},{10,... | collective-permute-start | bytes 1769480 | tf_op jit(solution)/shard_map/ppermute | solution.py:328
  17.4 8.1 %collective-permute-done.9.value.after = bf16[288,1024]{1,0:T(8,128)(2,1)S(1)} collective-permute-done((bf16[288,1024]{1,0:T(8,128)(2,1)S(1)}, bf16[288,1024]{1,0:T(8,128)(2,1)S(1)}, u32[]{:S(2)}, u32[]{:S(2)}) %collective-permute-start.9) | collective-permute-done | bytes 589856 | tf_op jit(solution)/shard_map/ppermute | solution.py:328
  25.6 6.9 %collective-permute-start.12 = (bf16[304,1024]{1,0:T(8,128)(2,1)S(1)}, bf16[304,1024]{1,0:T(8,128)(2,1)S(1)}, u32[]{:S(2)}, u32[]{:S(2)}) collective-permute-start(bf16[304,1024]{1,0:T(8,128)(2,1)S(1)} %shard_map.82), channel_id=1, source_target_pairs={{0,6},{1,7},{2,4},{3,5},{4,2},{5,3},{6,0},{7,1},{8,10},{9,11},{10,... | collective-permute-start | bytes 1867784 | tf_op jit(solution)/shard_map/ppermute | solution.py:328
  32.6 1.6 %collective-permute-start.10 = (bf16[288,1024]{1,0:T(8,128)(2,1)S(1)}, bf16[288,1024]{1,0:T(8,128)(2,1)S(1)}, u32[]{:S(2)}, u32[]{:S(2)}) collective-permute-start(bf16[288,1024]{1,0:T(8,128)(2,1)S(1)} %shard_map.80.z1.value), channel_id=1, source_target_pairs={{0,1},{1,0},{2,3},{3,2},{4,5},{5,4},{6,7},{7,6},{8,24},{9,25},{10,... | collective-permute-start | bytes 1769480 | tf_op jit(solution)/shard_map/ppermute | solution.py:328
  34.1 1.5 %collective-permute-start.11 = (bf16[288,1024]{1,0:T(8,128)(2,1)S(1)}, bf16[288,1024]{1,0:T(8,128)(2,1)S(1)}, u32[]{:S(2)}, u32[]{:S(2)}) collective-permute-start(bf16[288,1024]{1,0:T(8,128)(2,1)S(1)} %shard_map.80.z1.value), channel_id=1, source_target_pairs={{0,16},{1,17},{2,18},{3,19},{4,20},{5,21},{6,22},{7,23},{8,9},{9,8... | collective-permute-start | bytes 1769480 | tf_op jit(solution)/shard_map/ppermute | solution.py:328
  35.6 0.5 collective-permute-start.8
  36.2 12.7 %collective-permute-done.10.refs_0_.a1 = bf16[288,1024]{1,0:T(8,128)(2,1)S(1)} collective-permute-done((bf16[288,1024]{1,0:T(8,128)(2,1)S(1)}, bf16[288,1024]{1,0:T(8,128)(2,1)S(1)}, u32[]{:S(2)}, u32[]{:S(2)}) %collective-permute-start.10) | collective-permute-done | bytes 589856 | tf_op jit(solution)/shard_map/ppermute | solution.py:328
  48.9 1.6 %collective-permute-start.13 = (bf16[288,1024]{1,0:T(8,128)(2,1)S(1)}, bf16[288,1024]{1,0:T(8,128)(2,1)S(1)}, u32[]{:S(2)}, u32[]{:S(2)}) collective-permute-start(bf16[288,1024]{1,0:T(8,128)(2,1)S(1)} %shard_map.83.value), channel_id=1, source_target_pairs={{0,1},{1,0},{2,3},{3,2},{4,5},{5,4},{6,7},{7,6},{8,24},{9,25},{10,... | collective-permute-start | bytes 1769480 | tf_op jit(solution)/shard_map/ppermute | solution.py:328
  50.5 0.4 collective-permute-start.16
  50.9 1.0 shard_map.81.ids
  51.9 5.0 %collective-permute-done.8.refs_1_.c = bf16[288,1024]{1,0:T(8,128)(2,1)S(1)} collective-permute-done((bf16[288,1024]{1,0:T(8,128)(2,1)S(1)}, bf16[288,1024]{1,0:T(8,128)(2,1)S(1)}, u32[]{:S(2)}, u32[]{:S(2)}) %collective-permute-start.8) | collective-permute-done | bytes 589856 | tf_op jit(solution)/shard_map/ppermute | solution.py:328
  57.1 4.5 %shard_map.85 = (f32[576,512]{1,0:T(8,128)S(1)}, f32[576,256]{1,0:T(8,128)S(1)}, s32[576,1]{1,0:T(8,128)S(1)}) custom-call(bf16[8192,256]{1,0:T(8,128)(2,1)S(1)} %copy-done, bf16[8192,256]{1,0:T(8,128)(2,1)S(1)} %collective-permute-done.after.sibling, f32[16,1024]{1,0:T(8,128)S(1)} %pad_maximum_fusion.table.refs_0_, ...), custom_call_target="tpu_custom_call" | custom-call | tf_op jit(solution)/shard_map/pallas_call | solution.py:296
  61.6 0.7 collective-permute-done.13.value
  62.4 1.6 %collective-permute-start.15 = (bf16[288,1024]{1,0:T(8,128)(2,1)S(1)}, bf16[288,1024]{1,0:T(8,128)(2,1)S(1)}, u32[]{:S(2)}, u32[]{:S(2)}) collective-permute-start(bf16[288,1024]{1,0:T(8,128)(2,1)S(1)} %shard_map.86.a), channel_id=1, source_target_pairs={{0,16},{1,17},{2,18},{3,19},{4,20},{5,21},{6,22},{7,23},{8,9},{9,8... | collective-permute-start | bytes 1769480 | tf_op jit(solution)/shard_map/ppermute | solution.py:328
  64.3 1.5 %collective-permute-start.17 = (bf16[288,1024]{1,0:T(8,128)(2,1)S(1)}, bf16[288,1024]{1,0:T(8,128)(2,1)S(1)}, u32[]{:S(2)}, u32[]{:S(2)}) collective-permute-start(bf16[288,1024]{1,0:T(8,128)(2,1)S(1)} %collective-permute-done.16.z), channel_id=1, source_target_pairs={{0,1},{1,0},{2,3},{3,2},{4,5},{5,4},{6,7},{7,6},{8,24},{9,25},{10,... | collective-permute-start | bytes 1769480 | tf_op jit(solution)/shard_map/ppermute | solution.py:328
  65.8 0.5 collective-permute-start.18
  66.3 2.1 %collective-permute-start.19 = (bf16[288,1024]{1,0:T(8,128)(2,1)S(1)}, bf16[288,1024]{1,0:T(8,128)(2,1)S(1)}, u32[]{:S(2)}, u32[]{:S(2)}) collective-permute-start(bf16[288,1024]{1,0:T(8,128)(2,1)S(1)} %collective-permute-done.8.refs_1_.c), channel_id=1, source_target_pairs={{0,2},{1,3},{2,0},{3,1},{4,6},{5,7},{6,4},{7,5},{8,14},{9,15},{10,... | collective-permute-start | bytes 1769480 | tf_op jit(solution)/shard_map/ppermute | solution.py:328
  68.4 11.2 %collective-permute-done.15.c = bf16[288,1024]{1,0:T(8,128)(2,1)S(1)} collective-permute-done((bf16[288,1024]{1,0:T(8,128)(2,1)S(1)}, bf16[288,1024]{1,0:T(8,128)(2,1)S(1)}, u32[]{:S(2)}, u32[]{:S(2)}) %collective-permute-start.15) | collective-permute-done | bytes 589856 | tf_op jit(solution)/shard_map/ppermute | solution.py:328
  79.6 2.7 %shard_map.87 = (f32[576,512]{1,0:T(8,128)S(1)}, f32[576,256]{1,0:T(8,128)S(1)}) custom-call(bf16[8192,256]{1,0:T(8,128)(2,1)S(1)} %copy-done, bf16[8192,256]{1,0:T(8,128)(2,1)S(1)} %collective-permute-done.after.sibling, f32[16,1024]{1,0:T(8,128)S(1)} %pad_maximum_fusion.table.refs_0_, f32[576,512]{1,0:T(8,128)S(1)} %get-tuple-element.24.acc_in, ...), custom_call_target="tpu_custom_call" | custom-call | tf_op jit(solution)/shard_map/pallas_call | solution.py:296
  82.4 3.5 %collective-permute-done.18.b = bf16[288,1024]{1,0:T(8,128)(2,1)S(1)} collective-permute-done((bf16[288,1024]{1,0:T(8,128)(2,1)S(1)}, bf16[288,1024]{1,0:T(8,128)(2,1)S(1)}, u32[]{:S(2)}, u32[]{:S(2)}) %collective-permute-start.18) | collective-permute-done | bytes 589856 | tf_op jit(solution)/shard_map/ppermute | solution.py:328
  85.9 3.2 %shard_map.90 = (f32[288,512]{1,0:T(8,128)S(1)}, f32[288,256]{1,0:T(8,128)S(1)}, bf16[1024,512]{1,0:T(8,128)(2,1)S(1)}, f32[640,128]{1,0:T(8,128)S(1)}) custom-call(bf16[8192,256]{1,0:T(8,128)(2,1)S(1)} %copy-done, bf16[8192,256]{1,0:T(8,128)(2,1)S(1)} %collective-permute-done.after.sibling, f32[16,1024]{1,0:T(8,128)S(1)} %pad_maximum_fusion.table.refs_0_, ...), custom_call_target="tpu_custom_call" | custom-call | tf_op jit(solution)/shard_map/pallas_call | solution.py:296
  89.1 3.1 %collective-permute-done.20.c = bf16[288,1024]{1,0:T(8,128)(2,1)S(1)} collective-permute-done((bf16[288,1024]{1,0:T(8,128)(2,1)S(1)}, bf16[288,1024]{1,0:T(8,128)(2,1)S(1)}, u32[]{:S(2)}, u32[]{:S(2)}) %collective-permute-start.20) | collective-permute-done | bytes 589856 | tf_op jit(solution)/shard_map/ppermute | solution.py:328
  92.3 1.4 %shard_map.91 = f32[8,640]{1,0:T(8,128)S(1)} custom-call(bf16[1024,512]{1,0:T(8,128)(2,1)S(1)} %get-tuple-element.29.far_weights, f32[16,1024]{1,0:T(8,128)S(1)} %pad_maximum_fusion.table.refs_0_, f32[288,512]{1,0:T(8,128)S(1)} %get-tuple-element.30.left, f32[288,256]{1,0:T(8,128)S(1)} %get-tuple-element.31.left_side, ...), custom_call_target="tpu_custom_call" | custom-call | tf_op jit(solution)/shard_map/pallas_call | solution.py:296
  93.7 3.5 %collective-permute-start.23 = (f32[8,640]{1,0:T(8,128)S(1)}, f32[8,640]{1,0:T(8,128)S(1)}, u32[]{:S(2)}, u32[]{:S(2)}) collective-permute-start(f32[8,640]{1,0:T(8,128)S(1)} %shard_map.91), channel_id=1, source_target_pairs={{0,6},{1,7},{2,4},{3,5},{4,2},{5,3},{6,0},{7,1},{8,14},{9,15},{10,... | collective-permute-start | bytes 61448 | tf_op jit(solution)/shard_map/ppermute | solution.py:328
  97.2 0.9 collective-permute-start.21
  98.1 1.3 %collective-permute-done.23 = f32[8,640]{1,0:T(8,128)S(1)} collective-permute-done((f32[8,640]{1,0:T(8,128)S(1)}, f32[8,640]{1,0:T(8,128)S(1)}, u32[]{:S(2)}, u32[]{:S(2)}) %collective-permute-start.23) | collective-permute-done | bytes 20512 | tf_op jit(solution)/shard_map/ppermute | solution.py:328
  99.4 2.5 %collective-permute-done.22 = f32[8,640]{1,0:T(8,128)S(1)} collective-permute-done((f32[8,640]{1,0:T(8,128)S(1)}, f32[8,640]{1,0:T(8,128)S(1)}, u32[]{:S(2)}, u32[]{:S(2)}) %collective-permute-start.22) | collective-permute-done | bytes 20512 | tf_op jit(solution)/shard_map/ppermute | solution.py:328
  102.0 2.0 %collective-permute-start.26 = (f32[8,640]{1,0:T(8,128)S(1)}, f32[8,640]{1,0:T(8,128)S(1)}, u32[]{:S(2)}, u32[]{:S(2)}) collective-permute-start(f32[8,640]{1,0:T(8,128)S(1)} %concatenate.19), channel_id=1, source_target_pairs={{0,17},{1,16},{2,19},{3,18},{4,21},{5,20},{6,23},{7,22},{8,25},{9,... | collective-permute-start | bytes 61448 | tf_op jit(solution)/shard_map/ppermute | solution.py:328
  104.0 0.5 collective-permute-start.25
  104.5 1.0 collective-permute-start.24
  105.6 1.1 %collective-permute-done.26 = f32[8,640]{1,0:T(8,128)S(1)} collective-permute-done((f32[8,640]{1,0:T(8,128)S(1)}, f32[8,640]{1,0:T(8,128)S(1)}, u32[]{:S(2)}, u32[]{:S(2)}) %collective-permute-start.26) | collective-permute-done | bytes 20512 | tf_op jit(solution)/shard_map/ppermute | solution.py:328
  106.7 1.1 collective-permute-done.25
  107.8 0.5 collective-permute-done.24
  108.4 1.2 %collective-permute-done.27.sibling = f32[8,640]{1,0:T(8,128)S(1)} collective-permute-done((f32[8,640]{1,0:T(8,128)S(1)}, f32[8,640]{1,0:T(8,128)S(1)}, u32[]{:S(2)}, u32[]{:S(2)}) %collective-permute-start.27) | collective-permute-done | bytes 20512 | tf_op jit(solution)/shard_map/ppermute | solution.py:457
  109.6 0.8 shard_map.92
  (45 shorter events, 1.3 us)
Async XLA Ops:
  0.6 9.8 %collective-permute-start = (bf16[8192,256]{1,0:T(8,128)(2,1)}, bf16[8192,256]{1,0:T(8,128)(2,1)S(1)}, u32[]{:S(2)}, u32[]{:S(2)}) collective-permute-start(bf16[8192,256]{1,0:T(8,128)(2,1)} %head.5), channel_id=1, source_target_pairs={{0,8},{8,0},{16,24},{24,16},{1,9},{9,1},{17,25},{25,17},{2,10},{10... | collective-permute-start | bytes 12582920 | tf_op jit(solution)/shard_map/ppermute | solution.py:341
  1.1 9.2 %collective-permute-start.1 = (bf16[384,1024]{1,0:T(8,128)(2,1)}, bf16[384,1024]{1,0:T(8,128)(2,1)S(1)}, u32[]{:S(2)}, u32[]{:S(2)}) collective-permute-start(bf16[384,1024]{1,0:T(8,128)(2,1)} %bitcast.4), channel_id=1, source_target_pairs={{0,8},{8,0},{16,24},{24,16},{1,9},{9,1},{17,25},{25,17},{2,10},{10... | collective-permute-start | bytes 2359304 | tf_op jit(solution)/shard_map/ppermute | solution.py:340
  2.3 8.1 %collective-permute-start.2 = (bf16[192,1024]{1,0:T(8,128)(2,1)S(1)}, bf16[192,1024]{1,0:T(8,128)(2,1)S(1)}, u32[]{:S(2)}, u32[]{:S(2)}) collective-permute-start(bf16[192,1024]{1,0:T(8,128)(2,1)S(1)} %slice_bitcast_fusion), channel_id=1, source_target_pairs={{8,24},{24,8},{9,25},{25,9},{10,26},{26,10},{11,27},{27,11},{12,28... | collective-permute-start | bytes 1179656 | tf_op jit(solution)/shard_map/ppermute | solution.py:339
  4.3 1.1 %copy-start.1 = (bf16[1,384,1024]{2,1,0:T(8,128)(2,1)S(1)}, bf16[1,384,1024]{2,1,0:T(8,128)(2,1)}, u32[]{:S(2)}) copy-start(bf16[1,384,1024]{2,1,0:T(8,128)(2,1)} %param.6) | copy-start | bytes 2359300
  5.5 4.8 %collective-permute-start.3 = (f32[2,1024]{1,0:T(2,128)S(1)}, f32[2,1024]{1,0:T(2,128)S(1)}, u32[]{:S(2)}, u32[]{:S(2)}) collective-permute-start(f32[2,1024]{1,0:T(2,128)S(1)} %get-tuple-element.20), channel_id=1, source_target_pairs={{0,1},{1,0},{2,3},{3,2},{4,5},{5,4},{6,7},{7,6},{8,9},{9,8},{10,11... | collective-permute-start | bytes 24584 | tf_op jit(solution)/shard_map/ppermute | solution.py:328
  8.5 0.7 copy-start.3
  12.0 38.9 %copy-start.2 = (s32[4,384]{1,0:T(4,128)S(1)}, s32[4,384]{1,0:T(4,128)}, u32[]{:S(2)}) copy-start(s32[4,384]{1,0:T(4,128)} %tokens.1) | copy-start | bytes 18436
  12.0 13.5 %collective-permute-start.9 = (bf16[288,1024]{1,0:T(8,128)(2,1)S(1)}, bf16[288,1024]{1,0:T(8,128)(2,1)S(1)}, u32[]{:S(2)}, u32[]{:S(2)}) collective-permute-start(bf16[288,1024]{1,0:T(8,128)(2,1)S(1)} %get-tuple-element.23.value.z), channel_id=1, source_target_pairs={{0,2},{1,3},{2,0},{3,1},{4,6},{5,7},{6,4},{7,5},{8,14},{9,15},{10,... | collective-permute-start | bytes 1769480 | tf_op jit(solution)/shard_map/ppermute | solution.py:328
  14.0 18.5 %collective-permute-start.7 = (bf16[288,1024]{1,0:T(8,128)(2,1)S(1)}, bf16[288,1024]{1,0:T(8,128)(2,1)S(1)}, u32[]{:S(2)}, u32[]{:S(2)}) collective-permute-start(bf16[288,1024]{1,0:T(8,128)(2,1)S(1)} %get-tuple-element.23.value.z), channel_id=1, source_target_pairs={{0,16},{1,17},{2,18},{3,19},{4,20},{5,21},{6,22},{7,23},{8,9},{9,8... | collective-permute-start | bytes 1769480 | tf_op jit(solution)/shard_map/ppermute | solution.py:328
  15.5 17.0 %collective-permute-start.4 = (f32[4,1024]{1,0:T(4,128)S(1)}, f32[4,1024]{1,0:T(4,128)S(1)}, u32[]{:S(2)}, u32[]{:S(2)}) collective-permute-start(f32[4,1024]{1,0:T(4,128)S(1)} %get-tuple-element.22), channel_id=1, source_target_pairs={{0,2},{1,3},{2,0},{3,1},{4,6},{5,7},{6,4},{7,5},{8,10},{9,11},{10,... | collective-permute-start | bytes 49160 | tf_op jit(solution)/shard_map/ppermute | solution.py:328
  15.9 19.7 %collective-permute-start.6 = (bf16[288,1024]{1,0:T(8,128)(2,1)S(1)}, bf16[288,1024]{1,0:T(8,128)(2,1)S(1)}, u32[]{:S(2)}, u32[]{:S(2)}) collective-permute-start(bf16[288,1024]{1,0:T(8,128)(2,1)S(1)} %get-tuple-element.23.value.z), channel_id=1, source_target_pairs={{0,1},{1,0},{2,3},{3,2},{4,5},{5,4},{6,7},{7,6},{8,24},{9,25},{10,... | collective-permute-start | bytes 1769480 | tf_op jit(solution)/shard_map/ppermute | solution.py:328
  25.6 31.5 %copy-start = (bf16[8192,256]{1,0:T(8,128)(2,1)S(1)}, bf16[8192,256]{1,0:T(8,128)(2,1)}, u32[]{:S(2)}) copy-start(bf16[8192,256]{1,0:T(8,128)(2,1)} %head.5) | copy-start | bytes 12582916
  25.6 23.2 %collective-permute-start.12 = (bf16[304,1024]{1,0:T(8,128)(2,1)S(1)}, bf16[304,1024]{1,0:T(8,128)(2,1)S(1)}, u32[]{:S(2)}, u32[]{:S(2)}) collective-permute-start(bf16[304,1024]{1,0:T(8,128)(2,1)S(1)} %shard_map.82), channel_id=1, source_target_pairs={{0,6},{1,7},{2,4},{3,5},{4,2},{5,3},{6,0},{7,1},{8,10},{9,11},{10,... | collective-permute-start | bytes 1867784 | tf_op jit(solution)/shard_map/ppermute | solution.py:328
  32.6 16.2 %collective-permute-start.10 = (bf16[288,1024]{1,0:T(8,128)(2,1)S(1)}, bf16[288,1024]{1,0:T(8,128)(2,1)S(1)}, u32[]{:S(2)}, u32[]{:S(2)}) collective-permute-start(bf16[288,1024]{1,0:T(8,128)(2,1)S(1)} %shard_map.80.z1.value), channel_id=1, source_target_pairs={{0,1},{1,0},{2,3},{3,2},{4,5},{5,4},{6,7},{7,6},{8,24},{9,25},{10,... | collective-permute-start | bytes 1769480 | tf_op jit(solution)/shard_map/ppermute | solution.py:328
  34.1 16.3 %collective-permute-start.5 = (f32[8,1024]{1,0:T(8,128)S(1)}, f32[8,1024]{1,0:T(8,128)S(1)}, u32[]{:S(2)}, u32[]{:S(2)}) collective-permute-start(f32[8,1024]{1,0:T(8,128)S(1)} %pad_maximum_fusion.1.refs_1_), channel_id=1, source_target_pairs={{0,4},{1,5},{2,6},{3,7},{4,0},{5,1},{6,2},{7,3},{8,12},{9,13},{10,... | collective-permute-start | bytes 98312 | tf_op jit(solution)/shard_map/ppermute | solution.py:328
  34.1 22.8 %collective-permute-start.11 = (bf16[288,1024]{1,0:T(8,128)(2,1)S(1)}, bf16[288,1024]{1,0:T(8,128)(2,1)S(1)}, u32[]{:S(2)}, u32[]{:S(2)}) collective-permute-start(bf16[288,1024]{1,0:T(8,128)(2,1)S(1)} %shard_map.80.z1.value), channel_id=1, source_target_pairs={{0,16},{1,17},{2,18},{3,19},{4,20},{5,21},{6,22},{7,23},{8,9},{9,8... | collective-permute-start | bytes 1769480 | tf_op jit(solution)/shard_map/ppermute | solution.py:328
  35.6 21.3 %collective-permute-start.8 = (bf16[288,1024]{1,0:T(8,128)(2,1)S(1)}, bf16[288,1024]{1,0:T(8,128)(2,1)S(1)}, u32[]{:S(2)}, u32[]{:S(2)}) collective-permute-start(bf16[288,1024]{1,0:T(8,128)(2,1)S(1)} %collective-permute-done.6.a), channel_id=1, source_target_pairs={{0,16},{1,17},{2,18},{3,19},{4,20},{5,21},{6,22},{7,23},{8,9},{9,8... | collective-permute-start | bytes 1769480 | tf_op jit(solution)/shard_map/ppermute | solution.py:328
  48.9 13.4 %collective-permute-start.13 = (bf16[288,1024]{1,0:T(8,128)(2,1)S(1)}, bf16[288,1024]{1,0:T(8,128)(2,1)S(1)}, u32[]{:S(2)}, u32[]{:S(2)}) collective-permute-start(bf16[288,1024]{1,0:T(8,128)(2,1)S(1)} %shard_map.83.value), channel_id=1, source_target_pairs={{0,1},{1,0},{2,3},{3,2},{4,5},{5,4},{6,7},{7,6},{8,24},{9,25},{10,... | collective-permute-start | bytes 1769480 | tf_op jit(solution)/shard_map/ppermute | solution.py:328
  50.5 13.8 %collective-permute-start.16 = (bf16[288,1024]{1,0:T(8,128)(2,1)S(1)}, bf16[288,1024]{1,0:T(8,128)(2,1)S(1)}, u32[]{:S(2)}, u32[]{:S(2)}) collective-permute-start(bf16[288,1024]{1,0:T(8,128)(2,1)S(1)} %shard_map.88), channel_id=1, source_target_pairs={{0,6},{1,7},{2,4},{3,5},{4,2},{5,3},{6,0},{7,1},{8,10},{9,11},{10,... | collective-permute-start | bytes 1769480 | tf_op jit(solution)/shard_map/ppermute | solution.py:328
  57.0 11.4 %collective-permute-start.14 = (bf16[288,1024]{1,0:T(8,128)(2,1)S(1)}, bf16[288,1024]{1,0:T(8,128)(2,1)S(1)}, u32[]{:S(2)}, u32[]{:S(2)}) collective-permute-start(bf16[288,1024]{1,0:T(8,128)(2,1)S(1)} %shard_map.84.after.z), channel_id=1, source_target_pairs={{0,16},{1,17},{2,18},{3,19},{4,20},{5,21},{6,22},{7,23},{8,9},{9,8... | collective-permute-start | bytes 1769480 | tf_op jit(solution)/shard_map/ppermute | solution.py:328
  62.4 17.2 %collective-permute-start.15 = (bf16[288,1024]{1,0:T(8,128)(2,1)S(1)}, bf16[288,1024]{1,0:T(8,128)(2,1)S(1)}, u32[]{:S(2)}, u32[]{:S(2)}) collective-permute-start(bf16[288,1024]{1,0:T(8,128)(2,1)S(1)} %shard_map.86.a), channel_id=1, source_target_pairs={{0,16},{1,17},{2,18},{3,19},{4,20},{5,21},{6,22},{7,23},{8,9},{9,8... | collective-permute-start | bytes 1769480 | tf_op jit(solution)/shard_map/ppermute | solution.py:328
  64.3 17.9 %collective-permute-start.17 = (bf16[288,1024]{1,0:T(8,128)(2,1)S(1)}, bf16[288,1024]{1,0:T(8,128)(2,1)S(1)}, u32[]{:S(2)}, u32[]{:S(2)}) collective-permute-start(bf16[288,1024]{1,0:T(8,128)(2,1)S(1)} %collective-permute-done.16.z), channel_id=1, source_target_pairs={{0,1},{1,0},{2,3},{3,2},{4,5},{5,4},{6,7},{7,6},{8,24},{9,25},{10,... | collective-permute-start | bytes 1769480 | tf_op jit(solution)/shard_map/ppermute | solution.py:328
  65.8 20.1 %collective-permute-start.18 = (bf16[288,1024]{1,0:T(8,128)(2,1)S(1)}, bf16[288,1024]{1,0:T(8,128)(2,1)S(1)}, u32[]{:S(2)}, u32[]{:S(2)}) collective-permute-start(bf16[288,1024]{1,0:T(8,128)(2,1)S(1)} %collective-permute-done.16.z), channel_id=1, source_target_pairs={{0,16},{1,17},{2,18},{3,19},{4,20},{5,21},{6,22},{7,23},{8,9},{9,8... | collective-permute-start | bytes 1769480 | tf_op jit(solution)/shard_map/ppermute | solution.py:328
  66.3 19.6 %collective-permute-start.19 = (bf16[288,1024]{1,0:T(8,128)(2,1)S(1)}, bf16[288,1024]{1,0:T(8,128)(2,1)S(1)}, u32[]{:S(2)}, u32[]{:S(2)}) collective-permute-start(bf16[288,1024]{1,0:T(8,128)(2,1)S(1)} %collective-permute-done.8.refs_1_.c), channel_id=1, source_target_pairs={{0,2},{1,3},{2,0},{3,1},{4,6},{5,7},{6,4},{7,5},{8,14},{9,15},{10,... | collective-permute-start | bytes 1769480 | tf_op jit(solution)/shard_map/ppermute | solution.py:328
  82.3 9.9 %collective-permute-start.20 = (bf16[288,1024]{1,0:T(8,128)(2,1)S(1)}, bf16[288,1024]{1,0:T(8,128)(2,1)S(1)}, u32[]{:S(2)}, u32[]{:S(2)}) collective-permute-start(bf16[288,1024]{1,0:T(8,128)(2,1)S(1)} %shard_map.89.a), channel_id=1, source_target_pairs={{0,16},{1,17},{2,18},{3,19},{4,20},{5,21},{6,22},{7,23},{8,9},{9,8... | collective-permute-start | bytes 1769480 | tf_op jit(solution)/shard_map/ppermute | solution.py:328
  93.7 5.8 %collective-permute-start.23 = (f32[8,640]{1,0:T(8,128)S(1)}, f32[8,640]{1,0:T(8,128)S(1)}, u32[]{:S(2)}, u32[]{:S(2)}) collective-permute-start(f32[8,640]{1,0:T(8,128)S(1)} %shard_map.91), channel_id=1, source_target_pairs={{0,6},{1,7},{2,4},{3,5},{4,2},{5,3},{6,0},{7,1},{8,14},{9,15},{10,... | collective-permute-start | bytes 61448 | tf_op jit(solution)/shard_map/ppermute | solution.py:328
  97.2 4.7 %collective-permute-start.22 = (f32[8,640]{1,0:T(8,128)S(1)}, f32[8,640]{1,0:T(8,128)S(1)}, u32[]{:S(2)}, u32[]{:S(2)}) collective-permute-start(f32[8,640]{1,0:T(8,128)S(1)} %shard_map.91), channel_id=1, source_target_pairs={{0,4},{1,5},{2,6},{3,7},{4,0},{5,1},{6,2},{7,3},{8,12},{9,13},{10,... | collective-permute-start | bytes 61448 | tf_op jit(solution)/shard_map/ppermute | solution.py:328
  97.2 4.7 %collective-permute-start.21 = (f32[8,640]{1,0:T(8,128)S(1)}, f32[8,640]{1,0:T(8,128)S(1)}, u32[]{:S(2)}, u32[]{:S(2)}) collective-permute-start(f32[8,640]{1,0:T(8,128)S(1)} %shard_map.91), channel_id=1, source_target_pairs={{0,2},{1,3},{2,0},{3,1},{4,6},{5,7},{6,4},{7,5},{8,10},{9,11},{10,... | collective-permute-start | bytes 61448 | tf_op jit(solution)/shard_map/ppermute | solution.py:328
  102.0 4.7 %collective-permute-start.26 = (f32[8,640]{1,0:T(8,128)S(1)}, f32[8,640]{1,0:T(8,128)S(1)}, u32[]{:S(2)}, u32[]{:S(2)}) collective-permute-start(f32[8,640]{1,0:T(8,128)S(1)} %concatenate.19), channel_id=1, source_target_pairs={{0,17},{1,16},{2,19},{3,18},{4,21},{5,20},{6,23},{7,22},{8,25},{9,... | collective-permute-start | bytes 61448 | tf_op jit(solution)/shard_map/ppermute | solution.py:328
  104.0 3.8 %collective-permute-start.25 = (f32[8,640]{1,0:T(8,128)S(1)}, f32[8,640]{1,0:T(8,128)S(1)}, u32[]{:S(2)}, u32[]{:S(2)}) collective-permute-start(f32[8,640]{1,0:T(8,128)S(1)} %concatenate.19), channel_id=1, source_target_pairs={{0,16},{1,17},{2,18},{3,19},{4,20},{5,21},{6,22},{7,23},{8,24},{9,... | collective-permute-start | bytes 61448 | tf_op jit(solution)/shard_map/ppermute | solution.py:328
  104.5 3.8 %collective-permute-start.24 = (f32[8,640]{1,0:T(8,128)S(1)}, f32[8,640]{1,0:T(8,128)S(1)}, u32[]{:S(2)}, u32[]{:S(2)}) collective-permute-start(f32[8,640]{1,0:T(8,128)S(1)} %concatenate.19), channel_id=1, source_target_pairs={{0,1},{1,0},{2,3},{3,2},{4,5},{5,4},{6,7},{7,6},{8,9},{9,8},{10,11... | collective-permute-start | bytes 61448 | tf_op jit(solution)/shard_map/ppermute | solution.py:328
  108.4 1.2 %collective-permute-start.27 = (f32[8,640]{1,0:T(8,128)S(1)}, f32[8,640]{1,0:T(8,128)S(1)}, u32[]{:S(2)}, u32[]{:S(2)}) collective-permute-start(f32[8,640]{1,0:T(8,128)S(1)} %maximum_maximum_fusion.mine), channel_id=1, source_target_pairs={{0,8},{8,0},{16,24},{24,16},{1,9},{9,1},{17,25},{25,17},{2,10},{10... | collective-permute-start | bytes 61448 | tf_op jit(solution)/shard_map/ppermute | solution.py:457

commit v17 on v16

--- a/solution.py
+++ b/solution.py
@@ -143,7 +143,7 @@
         side[at, LANES:] = reward
         return 0
 
-    lax.fori_loop(0, count // step, body, 0)
+    lax.fori_loop(0, count // step, body, 0, unroll=3)
 
 
 def both_weights(head, sibling, depth, k):

time: 111 us -> 111 us (level)
  transfers between devices with their start and end apart: 28 -> 28, of which waited for: 14 -> 14; matrix products, arithmetic and copies ran while one was open for 2% -> 2% of each run, Pallas kernels for 12% -> 11%
where the time goes in v17:
time: 111 us; the launch traced here: 110 us
  waiting for transfers between devices  53 us (48%)
  starting transfers between devices  35.8 us (32%)
  Pallas kernels  16.2 us (15%)
  local copies, waits for them, and re-layouts  4.31 us (4%)
    ppermute x24, waiting for transfers between devices, per_device(): send = lambda value, perm: lax.ppermute(value, AXES, perm)  51.8 us
    ppermute x24, starting transfers between devices, per_device(): send = lambda value, perm: lax.ppermute(value, AXES, perm)  34.5 us
    pallas_call x16, Pallas kernels, call(): pl.pallas_call(body, out_shape=outs, in_specs=in_specs, out_specs=[VMEM]...  16.2 us
  transfers between devices with their start and end apart: 28, of which 14 were waited for; matrix products, arithmetic and copies ran while one was open for 2% of the time, Pallas kernels for 11%

profile of v17, /device:TPU:0, one launch (start us, length us, event | category | flops | bytes accessed | tf_op | source)
XLA Modules:
  0.0 110.4 jit_solution(7090611842526118312)
XLA Ops:
  0.6 0.5 collective-permute-start
  1.2 1.0 slice_bitcast_fusion
  2.3 0.7 collective-permute-start.2
  2.9 0.7 broadcast_in_dim.17.gain
  3.6 0.7 broadcast_in_dim.18.reward
  4.3 1.1 %copy-done.1 = bf16[1,384,1024]{2,1,0:T(8,128)(2,1)S(1)} copy-done((bf16[1,384,1024]{2,1,0:T(8,128)(2,1)S(1)}, bf16[1,384,1024]{2,1,0:T(8,128)(2,1)}, u32[]{:S(2)}) %copy-start.1) | copy-done | bytes 786456
  5.5 3.0 %collective-permute-start.3 = (f32[2,1024]{1,0:T(2,128)S(1)}, f32[2,1024]{1,0:T(2,128)S(1)}, u32[]{:S(2)}, u32[]{:S(2)}) collective-permute-start(f32[2,1024]{1,0:T(2,128)S(1)} %get-tuple-element.20), channel_id=1, source_target_pairs={{0,1},{1,0},{2,3},{3,2},{4,5},{5,4},{6,7},{7,6},{8,9},{9,8},{10,11... | collective-permute-start | bytes 24584 | tf_op jit(solution)/shard_map/ppermute | solution.py:328
  8.5 0.7 copy-done.3
  9.2 1.2 %shard_map.78 = (bf16[2,640,384]{2,1,0:T(8,128)(2,1)S(1)}, f32[8,128]{1,0:T(8,128)S(1)}) custom-call(s32[4]{0:T(128)S(1)} %copy-done.3), custom_call_target="tpu_custom_call" | custom-call | tf_op jit(solution)/shard_map/pallas_call | solution.py:296
  10.4 1.6 %shard_map.79 = (bf16[288,1024]{1,0:T(8,128)(2,1)S(1)}, f32[4,1024]{1,0:T(4,128)S(1)}) custom-call(s32[4]{0:T(128)S(1)} %copy-done.3, bf16[384,1024]{1,0:T(8,128)(2,1)S(1)} %get-tuple-element.19.rows, bf16[384,1024]{1,0:T(8,128)(2,1)S(1)} %collective-permute-done.1.sibling, bf16[192,1024]{1,0:T(8,128)(2,1)S(1)} %collective-permute-done.2.extra, ...), custom_call_target="tpu_custom_call" | custom-call | tf_op jit(solution)/shard_map/pallas_call | solution.py:296
  12.0 1.9 %collective-permute-start.9 = (bf16[288,1024]{1,0:T(8,128)(2,1)S(1)}, bf16[288,1024]{1,0:T(8,128)(2,1)S(1)}, u32[]{:S(2)}, u32[]{:S(2)}) collective-permute-start(bf16[288,1024]{1,0:T(8,128)(2,1)S(1)} %get-tuple-element.23.value.z), channel_id=1, source_target_pairs={{0,2},{1,3},{2,0},{3,1},{4,6},{5,7},{6,4},{7,5},{8,14},{9,15},{10,... | collective-permute-start | bytes 1769480 | tf_op jit(solution)/shard_map/ppermute | solution.py:328
  14.0 1.5 %collective-permute-start.7 = (bf16[288,1024]{1,0:T(8,128)(2,1)S(1)}, bf16[288,1024]{1,0:T(8,128)(2,1)S(1)}, u32[]{:S(2)}, u32[]{:S(2)}) collective-permute-start(bf16[288,1024]{1,0:T(8,128)(2,1)S(1)} %get-tuple-element.23.value.z), channel_id=1, source_target_pairs={{0,16},{1,17},{2,18},{3,19},{4,20},{5,21},{6,22},{7,23},{8,9},{9,8... | collective-permute-start | bytes 1769480 | tf_op jit(solution)/shard_map/ppermute | solution.py:328
  15.5 0.4 collective-permute-start.4
  15.9 1.5 %collective-permute-start.6 = (bf16[288,1024]{1,0:T(8,128)(2,1)S(1)}, bf16[288,1024]{1,0:T(8,128)(2,1)S(1)}, u32[]{:S(2)}, u32[]{:S(2)}) collective-permute-start(bf16[288,1024]{1,0:T(8,128)(2,1)S(1)} %get-tuple-element.23.value.z), channel_id=1, source_target_pairs={{0,1},{1,0},{2,3},{3,2},{4,5},{5,4},{6,7},{7,6},{8,24},{9,25},{10,... | collective-permute-start | bytes 1769480 | tf_op jit(solution)/shard_map/ppermute | solution.py:328
  17.4 8.1 %collective-permute-done.9.value.after = bf16[288,1024]{1,0:T(8,128)(2,1)S(1)} collective-permute-done((bf16[288,1024]{1,0:T(8,128)(2,1)S(1)}, bf16[288,1024]{1,0:T(8,128)(2,1)S(1)}, u32[]{:S(2)}, u32[]{:S(2)}) %collective-permute-start.9) | collective-permute-done | bytes 589856 | tf_op jit(solution)/shard_map/ppermute | solution.py:328
  25.6 6.9 %collective-permute-start.12 = (bf16[304,1024]{1,0:T(8,128)(2,1)S(1)}, bf16[304,1024]{1,0:T(8,128)(2,1)S(1)}, u32[]{:S(2)}, u32[]{:S(2)}) collective-permute-start(bf16[304,1024]{1,0:T(8,128)(2,1)S(1)} %shard_map.82), channel_id=1, source_target_pairs={{0,6},{1,7},{2,4},{3,5},{4,2},{5,3},{6,0},{7,1},{8,10},{9,11},{10,... | collective-permute-start | bytes 1867784 | tf_op jit(solution)/shard_map/ppermute | solution.py:328
  32.6 1.6 %collective-permute-start.10 = (bf16[288,1024]{1,0:T(8,128)(2,1)S(1)}, bf16[288,1024]{1,0:T(8,128)(2,1)S(1)}, u32[]{:S(2)}, u32[]{:S(2)}) collective-permute-start(bf16[288,1024]{1,0:T(8,128)(2,1)S(1)} %shard_map.80.z1.value), channel_id=1, source_target_pairs={{0,1},{1,0},{2,3},{3,2},{4,5},{5,4},{6,7},{7,6},{8,24},{9,25},{10,... | collective-permute-start | bytes 1769480 | tf_op jit(solution)/shard_map/ppermute | solution.py:328
  34.1 1.5 %collective-permute-start.11 = (bf16[288,1024]{1,0:T(8,128)(2,1)S(1)}, bf16[288,1024]{1,0:T(8,128)(2,1)S(1)}, u32[]{:S(2)}, u32[]{:S(2)}) collective-permute-start(bf16[288,1024]{1,0:T(8,128)(2,1)S(1)} %shard_map.80.z1.value), channel_id=1, source_target_pairs={{0,16},{1,17},{2,18},{3,19},{4,20},{5,21},{6,22},{7,23},{8,9},{9,8... | collective-permute-start | bytes 1769480 | tf_op jit(solution)/shard_map/ppermute | solution.py:328
  35.6 0.5 collective-permute-start.8
  36.2 12.7 %collective-permute-done.10.refs_0_.a1 = bf16[288,1024]{1,0:T(8,128)(2,1)S(1)} collective-permute-done((bf16[288,1024]{1,0:T(8,128)(2,1)S(1)}, bf16[288,1024]{1,0:T(8,128)(2,1)S(1)}, u32[]{:S(2)}, u32[]{:S(2)}) %collective-permute-start.10) | collective-permute-done | bytes 589856 | tf_op jit(solution)/shard_map/ppermute | solution.py:328
  48.9 1.6 %collective-permute-start.13 = (bf16[288,1024]{1,0:T(8,128)(2,1)S(1)}, bf16[288,1024]{1,0:T(8,128)(2,1)S(1)}, u32[]{:S(2)}, u32[]{:S(2)}) collective-permute-start(bf16[288,1024]{1,0:T(8,128)(2,1)S(1)} %shard_map.83.value), channel_id=1, source_target_pairs={{0,1},{1,0},{2,3},{3,2},{4,5},{5,4},{6,7},{7,6},{8,24},{9,25},{10,... | collective-permute-start | bytes 1769480 | tf_op jit(solution)/shard_map/ppermute | solution.py:328
  50.5 0.4 collective-permute-start.16
  50.9 1.0 shard_map.81.ids
  51.9 5.0 %collective-permute-done.8.refs_1_.c = bf16[288,1024]{1,0:T(8,128)(2,1)S(1)} collective-permute-done((bf16[288,1024]{1,0:T(8,128)(2,1)S(1)}, bf16[288,1024]{1,0:T(8,128)(2,1)S(1)}, u32[]{:S(2)}, u32[]{:S(2)}) %collective-permute-start.8) | collective-permute-done | bytes 589856 | tf_op jit(solution)/shard_map/ppermute | solution.py:328
  57.1 4.3 %shard_map.85 = (f32[576,512]{1,0:T(8,128)S(1)}, f32[576,256]{1,0:T(8,128)S(1)}, s32[576,1]{1,0:T(8,128)S(1)}) custom-call(bf16[8192,256]{1,0:T(8,128)(2,1)S(1)} %copy-done, bf16[8192,256]{1,0:T(8,128)(2,1)S(1)} %collective-permute-done.after.sibling, f32[16,1024]{1,0:T(8,128)S(1)} %pad_maximum_fusion.table.refs_0_, ...), custom_call_target="tpu_custom_call" | custom-call | tf_op jit(solution)/shard_map/pallas_call | solution.py:296
  61.4 0.9 collective-permute-done.13.value
  62.4 1.6 %collective-permute-start.15 = (bf16[288,1024]{1,0:T(8,128)(2,1)S(1)}, bf16[288,1024]{1,0:T(8,128)(2,1)S(1)}, u32[]{:S(2)}, u32[]{:S(2)}) collective-permute-start(bf16[288,1024]{1,0:T(8,128)(2,1)S(1)} %shard_map.86.a), channel_id=1, source_target_pairs={{0,16},{1,17},{2,18},{3,19},{4,20},{5,21},{6,22},{7,23},{8,9},{9,8... | collective-permute-start | bytes 1769480 | tf_op jit(solution)/shard_map/ppermute | solution.py:328
  64.3 1.5 %collective-permute-start.17 = (bf16[288,1024]{1,0:T(8,128)(2,1)S(1)}, bf16[288,1024]{1,0:T(8,128)(2,1)S(1)}, u32[]{:S(2)}, u32[]{:S(2)}) collective-permute-start(bf16[288,1024]{1,0:T(8,128)(2,1)S(1)} %collective-permute-done.16.z), channel_id=1, source_target_pairs={{0,1},{1,0},{2,3},{3,2},{4,5},{5,4},{6,7},{7,6},{8,24},{9,25},{10,... | collective-permute-start | bytes 1769480 | tf_op jit(solution)/shard_map/ppermute | solution.py:328
  65.8 0.5 collective-permute-start.18
  66.3 1.9 %collective-permute-start.19 = (bf16[288,1024]{1,0:T(8,128)(2,1)S(1)}, bf16[288,1024]{1,0:T(8,128)(2,1)S(1)}, u32[]{:S(2)}, u32[]{:S(2)}) collective-permute-start(bf16[288,1024]{1,0:T(8,128)(2,1)S(1)} %collective-permute-done.8.refs_1_.c), channel_id=1, source_target_pairs={{0,2},{1,3},{2,0},{3,1},{4,6},{5,7},{6,4},{7,5},{8,14},{9,15},{10,... | collective-permute-start | bytes 1769480 | tf_op jit(solution)/shard_map/ppermute | solution.py:328
  68.3 11.3 %collective-permute-done.15.c = bf16[288,1024]{1,0:T(8,128)(2,1)S(1)} collective-permute-done((bf16[288,1024]{1,0:T(8,128)(2,1)S(1)}, bf16[288,1024]{1,0:T(8,128)(2,1)S(1)}, u32[]{:S(2)}, u32[]{:S(2)}) %collective-permute-start.15) | collective-permute-done | bytes 589856 | tf_op jit(solution)/shard_map/ppermute | solution.py:328
  79.6 2.5 %shard_map.87 = (f32[576,512]{1,0:T(8,128)S(1)}, f32[576,256]{1,0:T(8,128)S(1)}) custom-call(bf16[8192,256]{1,0:T(8,128)(2,1)S(1)} %copy-done, bf16[8192,256]{1,0:T(8,128)(2,1)S(1)} %collective-permute-done.after.sibling, f32[16,1024]{1,0:T(8,128)S(1)} %pad_maximum_fusion.table.refs_0_, f32[576,512]{1,0:T(8,128)S(1)} %get-tuple-element.24.acc_in, ...), custom_call_target="tpu_custom_call" | custom-call | tf_op jit(solution)/shard_map/pallas_call | solution.py:296
  82.3 3.7 %collective-permute-done.18.b = bf16[288,1024]{1,0:T(8,128)(2,1)S(1)} collective-permute-done((bf16[288,1024]{1,0:T(8,128)(2,1)S(1)}, bf16[288,1024]{1,0:T(8,128)(2,1)S(1)}, u32[]{:S(2)}, u32[]{:S(2)}) %collective-permute-start.18) | collective-permute-done | bytes 589856 | tf_op jit(solution)/shard_map/ppermute | solution.py:328
  85.9 3.0 %shard_map.90 = (f32[288,512]{1,0:T(8,128)S(1)}, f32[288,256]{1,0:T(8,128)S(1)}, bf16[1024,512]{1,0:T(8,128)(2,1)S(1)}, f32[640,128]{1,0:T(8,128)S(1)}) custom-call(bf16[8192,256]{1,0:T(8,128)(2,1)S(1)} %copy-done, bf16[8192,256]{1,0:T(8,128)(2,1)S(1)} %collective-permute-done.after.sibling, f32[16,1024]{1,0:T(8,128)S(1)} %pad_maximum_fusion.table.refs_0_, ...), custom_call_target="tpu_custom_call" | custom-call | tf_op jit(solution)/shard_map/pallas_call | solution.py:296
  89.0 3.3 %collective-permute-done.20.c = bf16[288,1024]{1,0:T(8,128)(2,1)S(1)} collective-permute-done((bf16[288,1024]{1,0:T(8,128)(2,1)S(1)}, bf16[288,1024]{1,0:T(8,128)(2,1)S(1)}, u32[]{:S(2)}, u32[]{:S(2)}) %collective-permute-start.20) | collective-permute-done | bytes 589856 | tf_op jit(solution)/shard_map/ppermute | solution.py:328
  92.2 1.3 %shard_map.91 = f32[8,640]{1,0:T(8,128)S(1)} custom-call(bf16[1024,512]{1,0:T(8,128)(2,1)S(1)} %get-tuple-element.29.far_weights, f32[16,1024]{1,0:T(8,128)S(1)} %pad_maximum_fusion.table.refs_0_, f32[288,512]{1,0:T(8,128)S(1)} %get-tuple-element.30.left, f32[288,256]{1,0:T(8,128)S(1)} %get-tuple-element.31.left_side, ...), custom_call_target="tpu_custom_call" | custom-call | tf_op jit(solution)/shard_map/pallas_call | solution.py:296
  93.6 3.5 %collective-permute-start.23 = (f32[8,640]{1,0:T(8,128)S(1)}, f32[8,640]{1,0:T(8,128)S(1)}, u32[]{:S(2)}, u32[]{:S(2)}) collective-permute-start(f32[8,640]{1,0:T(8,128)S(1)} %shard_map.91), channel_id=1, source_target_pairs={{0,6},{1,7},{2,4},{3,5},{4,2},{5,3},{6,0},{7,1},{8,14},{9,15},{10,... | collective-permute-start | bytes 61448 | tf_op jit(solution)/shard_map/ppermute | solution.py:328
  97.1 0.9 collective-permute-start.21
  98.0 1.4 %collective-permute-done.23 = f32[8,640]{1,0:T(8,128)S(1)} collective-permute-done((f32[8,640]{1,0:T(8,128)S(1)}, f32[8,640]{1,0:T(8,128)S(1)}, u32[]{:S(2)}, u32[]{:S(2)}) %collective-permute-start.23) | collective-permute-done | bytes 20512 | tf_op jit(solution)/shard_map/ppermute | solution.py:328
  99.4 2.4 %collective-permute-done.22 = f32[8,640]{1,0:T(8,128)S(1)} collective-permute-done((f32[8,640]{1,0:T(8,128)S(1)}, f32[8,640]{1,0:T(8,128)S(1)}, u32[]{:S(2)}, u32[]{:S(2)}) %collective-permute-start.22) | collective-permute-done | bytes 20512 | tf_op jit(solution)/shard_map/ppermute | solution.py:328
  101.9 2.0 %collective-permute-start.26 = (f32[8,640]{1,0:T(8,128)S(1)}, f32[8,640]{1,0:T(8,128)S(1)}, u32[]{:S(2)}, u32[]{:S(2)}) collective-permute-start(f32[8,640]{1,0:T(8,128)S(1)} %concatenate.19), channel_id=1, source_target_pairs={{0,17},{1,16},{2,19},{3,18},{4,21},{5,20},{6,23},{7,22},{8,25},{9,... | collective-permute-start | bytes 61448 | tf_op jit(solution)/shard_map/ppermute | solution.py:328
  103.9 0.5 collective-permute-start.25
  104.4 1.0 collective-permute-start.24
  105.5 1.1 %collective-permute-done.26 = f32[8,640]{1,0:T(8,128)S(1)} collective-permute-done((f32[8,640]{1,0:T(8,128)S(1)}, f32[8,640]{1,0:T(8,128)S(1)}, u32[]{:S(2)}, u32[]{:S(2)}) %collective-permute-start.26) | collective-permute-done | bytes 20512 | tf_op jit(solution)/shard_map/ppermute | solution.py:328
  106.6 1.1 collective-permute-done.25
  107.7 0.5 collective-permute-done.24
  108.4 1.2 %collective-permute-done.27.sibling = f32[8,640]{1,0:T(8,128)S(1)} collective-permute-done((f32[8,640]{1,0:T(8,128)S(1)}, f32[8,640]{1,0:T(8,128)S(1)}, u32[]{:S(2)}, u32[]{:S(2)}) %collective-permute-start.27) | collective-permute-done | bytes 20512 | tf_op jit(solution)/shard_map/ppermute | solution.py:457
  109.5 0.8 shard_map.92
  (45 shorter events, 1.3 us)
Async XLA Ops:
  0.6 9.8 %collective-permute-start = (bf16[8192,256]{1,0:T(8,128)(2,1)}, bf16[8192,256]{1,0:T(8,128)(2,1)S(1)}, u32[]{:S(2)}, u32[]{:S(2)}) collective-permute-start(bf16[8192,256]{1,0:T(8,128)(2,1)} %head.5), channel_id=1, source_target_pairs={{0,8},{8,0},{16,24},{24,16},{1,9},{9,1},{17,25},{25,17},{2,10},{10... | collective-permute-start | bytes 12582920 | tf_op jit(solution)/shard_map/ppermute | solution.py:341
  1.1 9.2 %collective-permute-start.1 = (bf16[384,1024]{1,0:T(8,128)(2,1)}, bf16[384,1024]{1,0:T(8,128)(2,1)S(1)}, u32[]{:S(2)}, u32[]{:S(2)}) collective-permute-start(bf16[384,1024]{1,0:T(8,128)(2,1)} %bitcast.4), channel_id=1, source_target_pairs={{0,8},{8,0},{16,24},{24,16},{1,9},{9,1},{17,25},{25,17},{2,10},{10... | collective-permute-start | bytes 2359304 | tf_op jit(solution)/shard_map/ppermute | solution.py:340
  2.3 8.1 %collective-permute-start.2 = (bf16[192,1024]{1,0:T(8,128)(2,1)S(1)}, bf16[192,1024]{1,0:T(8,128)(2,1)S(1)}, u32[]{:S(2)}, u32[]{:S(2)}) collective-permute-start(bf16[192,1024]{1,0:T(8,128)(2,1)S(1)} %slice_bitcast_fusion), channel_id=1, source_target_pairs={{8,24},{24,8},{9,25},{25,9},{10,26},{26,10},{11,27},{27,11},{12,28... | collective-permute-start | bytes 1179656 | tf_op jit(solution)/shard_map/ppermute | solution.py:339
  4.3 1.1 %copy-start.1 = (bf16[1,384,1024]{2,1,0:T(8,128)(2,1)S(1)}, bf16[1,384,1024]{2,1,0:T(8,128)(2,1)}, u32[]{:S(2)}) copy-start(bf16[1,384,1024]{2,1,0:T(8,128)(2,1)} %param.6) | copy-start | bytes 2359300
  5.5 4.8 %collective-permute-start.3 = (f32[2,1024]{1,0:T(2,128)S(1)}, f32[2,1024]{1,0:T(2,128)S(1)}, u32[]{:S(2)}, u32[]{:S(2)}) collective-permute-start(f32[2,1024]{1,0:T(2,128)S(1)} %get-tuple-element.20), channel_id=1, source_target_pairs={{0,1},{1,0},{2,3},{3,2},{4,5},{5,4},{6,7},{7,6},{8,9},{9,8},{10,11... | collective-permute-start | bytes 24584 | tf_op jit(solution)/shard_map/ppermute | solution.py:328
  8.5 0.7 copy-start.3
  12.0 38.9 %copy-start.2 = (s32[4,384]{1,0:T(4,128)S(1)}, s32[4,384]{1,0:T(4,128)}, u32[]{:S(2)}) copy-start(s32[4,384]{1,0:T(4,128)} %tokens.1) | copy-start | bytes 18436
  12.0 13.5 %collective-permute-start.9 = (bf16[288,1024]{1,0:T(8,128)(2,1)S(1)}, bf16[288,1024]{1,0:T(8,128)(2,1)S(1)}, u32[]{:S(2)}, u32[]{:S(2)}) collective-permute-start(bf16[288,1024]{1,0:T(8,128)(2,1)S(1)} %get-tuple-element.23.value.z), channel_id=1, source_target_pairs={{0,2},{1,3},{2,0},{3,1},{4,6},{5,7},{6,4},{7,5},{8,14},{9,15},{10,... | collective-permute-start | bytes 1769480 | tf_op jit(solution)/shard_map/ppermute | solution.py:328
  14.0 18.5 %collective-permute-start.7 = (bf16[288,1024]{1,0:T(8,128)(2,1)S(1)}, bf16[288,1024]{1,0:T(8,128)(2,1)S(1)}, u32[]{:S(2)}, u32[]{:S(2)}) collective-permute-start(bf16[288,1024]{1,0:T(8,128)(2,1)S(1)} %get-tuple-element.23.value.z), channel_id=1, source_target_pairs={{0,16},{1,17},{2,18},{3,19},{4,20},{5,21},{6,22},{7,23},{8,9},{9,8... | collective-permute-start | bytes 1769480 | tf_op jit(solution)/shard_map/ppermute | solution.py:328
  15.5 17.0 %collective-permute-start.4 = (f32[4,1024]{1,0:T(4,128)S(1)}, f32[4,1024]{1,0:T(4,128)S(1)}, u32[]{:S(2)}, u32[]{:S(2)}) collective-permute-start(f32[4,1024]{1,0:T(4,128)S(1)} %get-tuple-element.22), channel_id=1, source_target_pairs={{0,2},{1,3},{2,0},{3,1},{4,6},{5,7},{6,4},{7,5},{8,10},{9,11},{10,... | collective-permute-start | bytes 49160 | tf_op jit(solution)/shard_map/ppermute | solution.py:328
  15.9 19.7 %collective-permute-start.6 = (bf16[288,1024]{1,0:T(8,128)(2,1)S(1)}, bf16[288,1024]{1,0:T(8,128)(2,1)S(1)}, u32[]{:S(2)}, u32[]{:S(2)}) collective-permute-start(bf16[288,1024]{1,0:T(8,128)(2,1)S(1)} %get-tuple-element.23.value.z), channel_id=1, source_target_pairs={{0,1},{1,0},{2,3},{3,2},{4,5},{5,4},{6,7},{7,6},{8,24},{9,25},{10,... | collective-permute-start | bytes 1769480 | tf_op jit(solution)/shard_map/ppermute | solution.py:328
  25.6 31.5 %copy-start = (bf16[8192,256]{1,0:T(8,128)(2,1)S(1)}, bf16[8192,256]{1,0:T(8,128)(2,1)}, u32[]{:S(2)}) copy-start(bf16[8192,256]{1,0:T(8,128)(2,1)} %head.5) | copy-start | bytes 12582916
  25.6 23.2 %collective-permute-start.12 = (bf16[304,1024]{1,0:T(8,128)(2,1)S(1)}, bf16[304,1024]{1,0:T(8,128)(2,1)S(1)}, u32[]{:S(2)}, u32[]{:S(2)}) collective-permute-start(bf16[304,1024]{1,0:T(8,128)(2,1)S(1)} %shard_map.82), channel_id=1, source_target_pairs={{0,6},{1,7},{2,4},{3,5},{4,2},{5,3},{6,0},{7,1},{8,10},{9,11},{10,... | collective-permute-start | bytes 1867784 | tf_op jit(solution)/shard_map/ppermute | solution.py:328
  32.6 16.2 %collective-permute-start.10 = (bf16[288,1024]{1,0:T(8,128)(2,1)S(1)}, bf16[288,1024]{1,0:T(8,128)(2,1)S(1)}, u32[]{:S(2)}, u32[]{:S(2)}) collective-permute-start(bf16[288,1024]{1,0:T(8,128)(2,1)S(1)} %shard_map.80.z1.value), channel_id=1, source_target_pairs={{0,1},{1,0},{2,3},{3,2},{4,5},{5,4},{6,7},{7,6},{8,24},{9,25},{10,... | collective-permute-start | bytes 1769480 | tf_op jit(solution)/shard_map/ppermute | solution.py:328
  34.1 16.3 %collective-permute-start.5 = (f32[8,1024]{1,0:T(8,128)S(1)}, f32[8,1024]{1,0:T(8,128)S(1)}, u32[]{:S(2)}, u32[]{:S(2)}) collective-permute-start(f32[8,1024]{1,0:T(8,128)S(1)} %pad_maximum_fusion.1.refs_1_), channel_id=1, source_target_pairs={{0,4},{1,5},{2,6},{3,7},{4,0},{5,1},{6,2},{7,3},{8,12},{9,13},{10,... | collective-permute-start | bytes 98312 | tf_op jit(solution)/shard_map/ppermute | solution.py:328
  34.1 22.8 %collective-permute-start.11 = (bf16[288,1024]{1,0:T(8,128)(2,1)S(1)}, bf16[288,1024]{1,0:T(8,128)(2,1)S(1)}, u32[]{:S(2)}, u32[]{:S(2)}) collective-permute-start(bf16[288,1024]{1,0:T(8,128)(2,1)S(1)} %shard_map.80.z1.value), channel_id=1, source_target_pairs={{0,16},{1,17},{2,18},{3,19},{4,20},{5,21},{6,22},{7,23},{8,9},{9,8... | collective-permute-start | bytes 1769480 | tf_op jit(solution)/shard_map/ppermute | solution.py:328
  35.6 21.3 %collective-permute-start.8 = (bf16[288,1024]{1,0:T(8,128)(2,1)S(1)}, bf16[288,1024]{1,0:T(8,128)(2,1)S(1)}, u32[]{:S(2)}, u32[]{:S(2)}) collective-permute-start(bf16[288,1024]{1,0:T(8,128)(2,1)S(1)} %collective-permute-done.6.a), channel_id=1, source_target_pairs={{0,16},{1,17},{2,18},{3,19},{4,20},{5,21},{6,22},{7,23},{8,9},{9,8... | collective-permute-start | bytes 1769480 | tf_op jit(solution)/shard_map/ppermute | solution.py:328
  48.9 13.4 %collective-permute-start.13 = (bf16[288,1024]{1,0:T(8,128)(2,1)S(1)}, bf16[288,1024]{1,0:T(8,128)(2,1)S(1)}, u32[]{:S(2)}, u32[]{:S(2)}) collective-permute-start(bf16[288,1024]{1,0:T(8,128)(2,1)S(1)} %shard_map.83.value), channel_id=1, source_target_pairs={{0,1},{1,0},{2,3},{3,2},{4,5},{5,4},{6,7},{7,6},{8,24},{9,25},{10,... | collective-permute-start | bytes 1769480 | tf_op jit(solution)/shard_map/ppermute | solution.py:328
  50.5 13.8 %collective-permute-start.16 = (bf16[288,1024]{1,0:T(8,128)(2,1)S(1)}, bf16[288,1024]{1,0:T(8,128)(2,1)S(1)}, u32[]{:S(2)}, u32[]{:S(2)}) collective-permute-start(bf16[288,1024]{1,0:T(8,128)(2,1)S(1)} %shard_map.88), channel_id=1, source_target_pairs={{0,6},{1,7},{2,4},{3,5},{4,2},{5,3},{6,0},{7,1},{8,10},{9,11},{10,... | collective-permute-start | bytes 1769480 | tf_op jit(solution)/shard_map/ppermute | solution.py:328
  57.0 11.2 %collective-permute-start.14 = (bf16[288,1024]{1,0:T(8,128)(2,1)S(1)}, bf16[288,1024]{1,0:T(8,128)(2,1)S(1)}, u32[]{:S(2)}, u32[]{:S(2)}) collective-permute-start(bf16[288,1024]{1,0:T(8,128)(2,1)S(1)} %shard_map.84.after.z), channel_id=1, source_target_pairs={{0,16},{1,17},{2,18},{3,19},{4,20},{5,21},{6,22},{7,23},{8,9},{9,8... | collective-permute-start | bytes 1769480 | tf_op jit(solution)/shard_map/ppermute | solution.py:328
  62.4 17.2 %collective-permute-start.15 = (bf16[288,1024]{1,0:T(8,128)(2,1)S(1)}, bf16[288,1024]{1,0:T(8,128)(2,1)S(1)}, u32[]{:S(2)}, u32[]{:S(2)}) collective-permute-start(bf16[288,1024]{1,0:T(8,128)(2,1)S(1)} %shard_map.86.a), channel_id=1, source_target_pairs={{0,16},{1,17},{2,18},{3,19},{4,20},{5,21},{6,22},{7,23},{8,9},{9,8... | collective-permute-start | bytes 1769480 | tf_op jit(solution)/shard_map/ppermute | solution.py:328
  64.3 17.8 %collective-permute-start.17 = (bf16[288,1024]{1,0:T(8,128)(2,1)S(1)}, bf16[288,1024]{1,0:T(8,128)(2,1)S(1)}, u32[]{:S(2)}, u32[]{:S(2)}) collective-permute-start(bf16[288,1024]{1,0:T(8,128)(2,1)S(1)} %collective-permute-done.16.z), channel_id=1, source_target_pairs={{0,1},{1,0},{2,3},{3,2},{4,5},{5,4},{6,7},{7,6},{8,24},{9,25},{10,... | collective-permute-start | bytes 1769480 | tf_op jit(solution)/shard_map/ppermute | solution.py:328
  65.8 20.1 %collective-permute-start.18 = (bf16[288,1024]{1,0:T(8,128)(2,1)S(1)}, bf16[288,1024]{1,0:T(8,128)(2,1)S(1)}, u32[]{:S(2)}, u32[]{:S(2)}) collective-permute-start(bf16[288,1024]{1,0:T(8,128)(2,1)S(1)} %collective-permute-done.16.z), channel_id=1, source_target_pairs={{0,16},{1,17},{2,18},{3,19},{4,20},{5,21},{6,22},{7,23},{8,9},{9,8... | collective-permute-start | bytes 1769480 | tf_op jit(solution)/shard_map/ppermute | solution.py:328
  66.3 19.6 %collective-permute-start.19 = (bf16[288,1024]{1,0:T(8,128)(2,1)S(1)}, bf16[288,1024]{1,0:T(8,128)(2,1)S(1)}, u32[]{:S(2)}, u32[]{:S(2)}) collective-permute-start(bf16[288,1024]{1,0:T(8,128)(2,1)S(1)} %collective-permute-done.8.refs_1_.c), channel_id=1, source_target_pairs={{0,2},{1,3},{2,0},{3,1},{4,6},{5,7},{6,4},{7,5},{8,14},{9,15},{10,... | collective-permute-start | bytes 1769480 | tf_op jit(solution)/shard_map/ppermute | solution.py:328
  82.2 10.1 %collective-permute-start.20 = (bf16[288,1024]{1,0:T(8,128)(2,1)S(1)}, bf16[288,1024]{1,0:T(8,128)(2,1)S(1)}, u32[]{:S(2)}, u32[]{:S(2)}) collective-permute-start(bf16[288,1024]{1,0:T(8,128)(2,1)S(1)} %shard_map.89.a), channel_id=1, source_target_pairs={{0,16},{1,17},{2,18},{3,19},{4,20},{5,21},{6,22},{7,23},{8,9},{9,8... | collective-permute-start | bytes 1769480 | tf_op jit(solution)/shard_map/ppermute | solution.py:328
  93.6 5.8 %collective-permute-start.23 = (f32[8,640]{1,0:T(8,128)S(1)}, f32[8,640]{1,0:T(8,128)S(1)}, u32[]{:S(2)}, u32[]{:S(2)}) collective-permute-start(f32[8,640]{1,0:T(8,128)S(1)} %shard_map.91), channel_id=1, source_target_pairs={{0,6},{1,7},{2,4},{3,5},{4,2},{5,3},{6,0},{7,1},{8,14},{9,15},{10,... | collective-permute-start | bytes 61448 | tf_op jit(solution)/shard_map/ppermute | solution.py:328
  97.1 4.7 %collective-permute-start.22 = (f32[8,640]{1,0:T(8,128)S(1)}, f32[8,640]{1,0:T(8,128)S(1)}, u32[]{:S(2)}, u32[]{:S(2)}) collective-permute-start(f32[8,640]{1,0:T(8,128)S(1)} %shard_map.91), channel_id=1, source_target_pairs={{0,4},{1,5},{2,6},{3,7},{4,0},{5,1},{6,2},{7,3},{8,12},{9,13},{10,... | collective-permute-start | bytes 61448 | tf_op jit(solution)/shard_map/ppermute | solution.py:328
  97.1 4.7 %collective-permute-start.21 = (f32[8,640]{1,0:T(8,128)S(1)}, f32[8,640]{1,0:T(8,128)S(1)}, u32[]{:S(2)}, u32[]{:S(2)}) collective-permute-start(f32[8,640]{1,0:T(8,128)S(1)} %shard_map.91), channel_id=1, source_target_pairs={{0,2},{1,3},{2,0},{3,1},{4,6},{5,7},{6,4},{7,5},{8,10},{9,11},{10,... | collective-permute-start | bytes 61448 | tf_op jit(solution)/shard_map/ppermute | solution.py:328
  101.9 4.7 %collective-permute-start.26 = (f32[8,640]{1,0:T(8,128)S(1)}, f32[8,640]{1,0:T(8,128)S(1)}, u32[]{:S(2)}, u32[]{:S(2)}) collective-permute-start(f32[8,640]{1,0:T(8,128)S(1)} %concatenate.19), channel_id=1, source_target_pairs={{0,17},{1,16},{2,19},{3,18},{4,21},{5,20},{6,23},{7,22},{8,25},{9,... | collective-permute-start | bytes 61448 | tf_op jit(solution)/shard_map/ppermute | solution.py:328
  103.9 3.8 %collective-permute-start.25 = (f32[8,640]{1,0:T(8,128)S(1)}, f32[8,640]{1,0:T(8,128)S(1)}, u32[]{:S(2)}, u32[]{:S(2)}) collective-permute-start(f32[8,640]{1,0:T(8,128)S(1)} %concatenate.19), channel_id=1, source_target_pairs={{0,16},{1,17},{2,18},{3,19},{4,20},{5,21},{6,22},{7,23},{8,24},{9,... | collective-permute-start | bytes 61448 | tf_op jit(solution)/shard_map/ppermute | solution.py:328
  104.4 3.8 %collective-permute-start.24 = (f32[8,640]{1,0:T(8,128)S(1)}, f32[8,640]{1,0:T(8,128)S(1)}, u32[]{:S(2)}, u32[]{:S(2)}) collective-permute-start(f32[8,640]{1,0:T(8,128)S(1)} %concatenate.19), channel_id=1, source_target_pairs={{0,1},{1,0},{2,3},{3,2},{4,5},{5,4},{6,7},{7,6},{8,9},{9,8},{10,11... | collective-permute-start | bytes 61448 | tf_op jit(solution)/shard_map/ppermute | solution.py:328
  108.3 1.2 %collective-permute-start.27 = (f32[8,640]{1,0:T(8,128)S(1)}, f32[8,640]{1,0:T(8,128)S(1)}, u32[]{:S(2)}, u32[]{:S(2)}) collective-permute-start(f32[8,640]{1,0:T(8,128)S(1)} %maximum_maximum_fusion.mine), channel_id=1, source_target_pairs={{0,8},{8,0},{16,24},{24,16},{1,9},{9,1},{17,25},{25,17},{2,10},{10... | collective-permute-start | bytes 61448 | tf_op jit(solution)/shard_map/ppermute | solution.py:457
